TPU v7x, 32 devices: a whole 2x2x4 slice. The times are simulated.
32 devices in a mesh: grp: 2 (over y), ctx: 4 (over z), tp: 4 (over x, core).
Axes of the slice: x: 2, y: 2, z: 4, core: 2. Of those that a mesh axis runs over, the one named last changes fastest.
Arguments:
- residual: bfloat16 [1024, 7168], P(('grp', 'ctx'), 'tp'), parts along dimension 0, may hold values from -20 to 20
- latent: bfloat16 [576, 1024], P(None, ('grp', 'ctx')), parts along dimension 1, may hold values from -4 to 4
- queries: bfloat16 [1024, 36864], P(('grp', 'ctx'), 'tp'), parts along dimension 0, may hold values from -32 to 32
- lengths: int32 [8], P('grp'), parts along dimension 0, may hold values from 1 to 384, 512 in all
- value_weight: bfloat16 [512, 8192], P(None, 'tp'), may hold values from -1 to 1
- output_weight: bfloat16 [8192, 7168], P('ctx', 'tp'), may hold values from -0.0625 to 0.0625
- norm_gain: float32 [7168], P('tp'), may hold values from 0.1 to 1.9
- gate_weight: bfloat16 [7168, 10240], P('tp', 'ctx'), may hold values from -0.0625 to 0.0625
- up_weight: bfloat16 [7168, 10240], P('tp', 'ctx'), may hold values from -0.0625 to 0.0625
- down_weight: bfloat16 [10240, 7168], P('ctx', 'tp'), may hold values from -0.0625 to 0.0625
Outputs:
- attended: bfloat16 [1024, 7168], P(('grp', 'ctx'), 'tp'), parts along dimension 0
- layer_out: bfloat16 [1024, 7168], P(('grp', 'ctx'), 'tp'), parts along dimension 0
There are 2 independent parts, one for each index of `grp`. A program takes and returns all parts, laid end to end along the dimension named above; an argument that names none is the same for every part. Nothing has to cross between parts.
Inputs may be any that keep to these rules, and one draw needn't show every extreme that they name: The 4 traces fill the sequence in order and their lengths sum to 512.
All inputs are finite; a program needn't handle non-finite values.
Results may differ from a plain program's by a relative error of at most 0.02.
Values may be sent and summed in bfloat16 or wider, within the bound.
No kernel may reach another device: no remote copies, remote signals or barrier semaphores. Data moves between devices by JAX's collectives and lax.ppermute only.
A program may use at most 128 MiB of HBM per device.

v0:
```python
import jax
import jax.numpy as jnp
from jax import lax
from jax.sharding import PartitionSpec as P

D = 7168
LAT = 512
ROPE = 64
VHEAD = 128


score_scale = 192.0 ** (-0.5)
rope_base = 10000.0
norm_eps = 1e-06
masked_score = -1e30


def rope_freqs(half_width):
    return rope_base ** (-jnp.arange(half_width, dtype=jnp.float32) / half_width)


def trace_info(token_index, lengths):
    trace_ends = jnp.cumsum(lengths)
    starts = trace_ends - lengths
    trace_ids = jnp.sum((token_index[:, None] >= trace_ends[None, :]).astype(jnp.int32), axis=1)
    member = trace_ids[:, None] == jnp.arange(lengths.shape[0], dtype=jnp.int32)[None, :]
    pos_shift = jnp.sum(jnp.where(member, (0 - starts)[None, :], 0), axis=1)
    return (trace_ids, token_index + pos_shift)


def rope_keys(latent, positions, latent_width):
    values = latent.astype(jnp.float32)
    half_width = (values.shape[0] - latent_width) // 2
    angles = rope_freqs(half_width)[:, None] * positions.astype(jnp.float32)[None, :]
    first_half = values[latent_width : latent_width + half_width]
    second_half = values[latent_width + half_width :]
    cosine = jnp.cos(angles)
    sine_value = jnp.sin(angles)
    return jnp.concatenate(
        [
            values[:latent_width],
            first_half * cosine - second_half * sine_value,
            first_half * sine_value + second_half * cosine,
        ],
        axis=0,
    ).astype(jnp.bfloat16)


def rope_queries(queries, positions, latent_width):
    values = queries.astype(jnp.float32)
    half_width = (values.shape[2] - latent_width) // 2
    angles = positions.astype(jnp.float32)[:, None] * rope_freqs(half_width)[None, :]
    cosine = jnp.cos(angles)[:, None, :]
    sine_value = jnp.sin(angles)[:, None, :]
    first_half = values[:, :, latent_width : latent_width + half_width]
    second_half = values[:, :, latent_width + half_width :]
    return jnp.concatenate(
        [
            values[:, :, :latent_width],
            first_half * cosine - second_half * sine_value,
            first_half * sine_value + second_half * cosine,
        ],
        axis=2,
    ).astype(jnp.bfloat16)


def score_rows(state_carry, query_block, block_index, block_trace, key_piece, key_index, key_trace):
    row_top, row_total, mixed_sum = state_carry
    allowed = (key_trace[None, :] == block_trace[:, None]) & (
        key_index[None, :] <= block_index[:, None]
    )
    scores = (
        jnp.einsum("qhe,ek->hqk", query_block, key_piece, preferred_element_type=jnp.float32)
        * score_scale
    )
    scores = jnp.where(allowed[None], scores, masked_score)
    new_top = jnp.maximum(row_top, jnp.max(scores, axis=2))
    exponent = jnp.where(allowed[None], jnp.exp(scores - new_top[:, :, None]), 0.0)
    row_total = jnp.sum(exponent, axis=2)
    mixed_sum = jnp.einsum(
        "hqk,lk->hql",
        exponent.astype(jnp.bfloat16),
        key_piece[:LAT],
        preferred_element_type=jnp.float32,
    )
    return (new_top, row_total, mixed_sum)


def on_device(
    residual,
    latent,
    queries,
    lengths,
    value_weight,
    output_weight,
    norm_gain,
    gate_weight,
    up_weight,
    down_weight,
):
    row_count = residual.shape[0]
    ctx_place = lax.axis_index("ctx")
    local_heads = value_weight.shape[1] // VHEAD
    own_index = ctx_place * row_count + jnp.arange(row_count, dtype=jnp.int32)
    own_trace, own_position = trace_info(own_index, lengths)
    rotated_keys = rope_keys(latent, own_position, LAT)
    rotated_queries = rope_queries(
        queries.reshape(row_count, local_heads, LAT + ROPE), own_position, LAT
    )
    last_query = ctx_place * row_count + row_count - 1
    start_state = (
        jnp.full((local_heads, row_count), masked_score, jnp.float32),
        jnp.zeros((local_heads, row_count), jnp.float32),
        jnp.zeros((local_heads, row_count, LAT), jnp.float32),
    )
    key_piece = lax.all_gather(rotated_keys, "ctx", axis=1, tiled=True)
    key_index = jnp.arange(key_piece.shape[1], dtype=jnp.int32)
    key_trace, _ = trace_info(key_index, lengths)
    folded = lax.cond(
        jnp.int32(0) <= last_query,
        lambda held: score_rows(
            held, rotated_queries, own_index, own_trace, key_piece, key_index, key_trace
        ),
        lambda held: held,
        start_state,
    )
    row_top, row_total, mixed_sum = folded
    mixed_latent = (mixed_sum / row_total[:, :, None]).astype(jnp.bfloat16)
    heads_out = (
        jnp.einsum(
            "hql,lhd->qhd",
            mixed_latent,
            value_weight.reshape(LAT, local_heads, VHEAD),
            preferred_element_type=jnp.float32,
        )
        .astype(jnp.bfloat16)
        .reshape(row_count, local_heads * VHEAD)
    )
    all_heads = lax.all_gather(heads_out, "tp", axis=1, tiled=True)
    head_block = lax.all_to_all(all_heads, "ctx", split_axis=1, concat_axis=0, tiled=True)
    head_sum = lax.psum_scatter(
        jnp.dot(head_block, output_weight, preferred_element_type=jnp.float32).astype(jnp.bfloat16),
        "ctx",
        scatter_dimension=0,
        tiled=True,
    ).astype(jnp.float32)
    attended = (residual.astype(jnp.float32) + head_sum).astype(jnp.bfloat16)
    attended_float = attended.astype(jnp.float32)
    squares = lax.psum(jnp.sum(attended_float * attended_float, axis=1), "tp")
    inverse_rms = lax.rsqrt(squares / D + norm_eps)
    scaled = (attended_float * inverse_rms[:, None] * norm_gain[None, :]).astype(jnp.bfloat16)
    scaled_all = lax.all_gather(scaled, "ctx", axis=0, tiled=True)
    unit_count = gate_weight.shape[1]
    gate_up = jnp.concatenate([gate_weight, up_weight], axis=1)
    summed = lax.psum_scatter(
        jnp.dot(scaled_all, gate_up, preferred_element_type=jnp.float32).astype(jnp.bfloat16),
        "tp",
        scatter_dimension=0,
        tiled=True,
    ).astype(jnp.float32)
    hidden_share = (jax.nn.silu(summed[:, :unit_count]) * summed[:, unit_count:]).astype(
        jnp.bfloat16
    )
    hidden_all = lax.all_gather(hidden_share, "tp", axis=0, tiled=True)
    down_sum = lax.psum_scatter(
        jnp.dot(hidden_all, down_weight, preferred_element_type=jnp.float32).astype(jnp.bfloat16),
        "ctx",
        scatter_dimension=0,
        tiled=True,
    ).astype(jnp.float32)
    layer_out = (attended_float + down_sum).astype(jnp.bfloat16)
    return (attended, layer_out)


def solution(mesh):
    in_specs = (
        P(("grp", "ctx"), "tp"),
        P(None, ("grp", "ctx")),
        P(("grp", "ctx"), "tp"),
        P("grp"),
        P(None, "tp"),
        P("ctx", "tp"),
        P("tp"),
        P("tp", "ctx"),
        P("tp", "ctx"),
        P("ctx", "tp"),
    )
    out_specs = (P(("grp", "ctx"), "tp"), P(("grp", "ctx"), "tp"))
    return jax.shard_map(
        on_device, mesh=mesh, in_specs=in_specs, out_specs=out_specs, check_vma=False
    )
```

profile of v0, /device:TPU:0, one launch (start us, length us, event | category | flops | bytes accessed | tf_op | source)
XLA Modules:
  0.0 379.5 jit_solution(6798058642352320378)
XLA Ops:
  7.2 0.0 all-gather.4.cloned.1.call-start
  7.2 3.0 copy.23
  10.3 0.0 copy-start.3
  10.3 2.6 convert_element_type.87
  12.9 0.0 copy-start.6
  12.9 0.0 slice-start
  12.9 1.5 slice.39
  14.5 0.0 copy-done.3
  14.5 0.0 copy-start
  14.5 0.0 copy-done.6
  14.5 0.2 reduce-window.8
  14.7 0.1 fusion.39
  14.8 0.1 convert_reduce_fusion
  14.9 0.1 select_reduce_fusion
  15.0 0.1 multiply_cosine_fusion
  15.1 0.1 fusion.36
  15.3 0.0 slice-done
  15.3 18.0 %all_gather.12 = bf16[576,512]{1,0:T(8,128)(2,1)S(1)} all-gather(bf16[576,128]{1,0:T(8,128)(2,1)S(1)} %pad_maximum_fusion.1), channel_id=1, replica_groups=mesh['grp'=2,'ctx'=4,'tp'=4] {'ctx'}, dimensions={1}, use_global_device_ids=true | all-gather | bytes 737280 | tf_op jit(solution)/shard_map/all_gather | solution.py:116
  33.3 3.9 %copy.27 = bf16[512,2048]{0,1:T(8,128)(2,1)} copy(bf16[512,2048]{1,0:T(8,128)(2,1)} %param.16) | data formatting | bytes 4194304 | tf_op jit(solution)/shard_map/reshape | solution.py:133
  37.2 1.1 subtract_convert_fusion
  38.3 0.0 copy-done
  38.3 1.6 pad_maximum_fusion
  39.9 0.0 copy-start.2
  40.0 8.6 %conditional.1 = (f32[16,128]{1,0:T(8,128)S(1)}, f32[16,128,512]{2,1,0:T(8,128)}) conditional(s32[]{:T(128)} %convert_element_type.81, () %tuple.16, (s32[512,4]{0,1:T(4,128)S(1)}, s32[128]{0:T(128)S(1)}, s32[512]{0:T(512)S(1)}, s32[]{:T(128)}, s32[128]{0:T(128)S(1)}, /*index=5*/bf16[576,512]{1,0:T(8,128)(2,1)S(1)}, ...), branch_computations={%region_3.4_spmd, %region_4.0_spmd} | conditional | flops 2295528960 | bytes 20578328 | solution.py:119
  40.0 0.2 compare_and_fusion
  40.2 3.8 %fusion = (f32[16,128]{1,0:T(8,128)S(1)}, f32[512,128,16]{1,0,2:T(8,128)S(1)}) fusion(pred[128,512]{0,1:T(8,128)(4,1)S(1)} %compare_and_fusion, bf16[128,16,576]{0,2,1:T(8,128)(2,1)} %get-tuple-element.24, bf16[576,512]{1,0:T(8,128)(2,1)S(1)} %get-tuple-element.23), kind=kOutput, calls=%fused_computation.2 | convolution fusion | flops 1211103232 | bytes 7217152 | tf_op jit(solution)/shard_map/cond/branch_1_fun/qhe,ek->hqk/dot_general | solution.py:73
  44.0 3.5 fusion.3
  47.5 1.0 fusion.2
  48.5 0.0 copy-done.2
  48.5 3.8 fusion.26
  52.3 0.0 all-gather.4.cloned.1.call-update
  52.3 0.0 reduce-scatter.4.cloned.1.call-start
  52.4 22.1 %all-gather.4.cloned.1.call-done = bf16[128,8192]{0,1:T(8,128)(2,1)} async-done(((bf16[128,2048]{0,1:T(8,128)(2,1)}), bf16[128,8192]{0,1:T(8,128)(2,1)}) %all-gather.4.cloned.1.call-update) | async-done | bytes 2097168 | tf_op jit(solution)/shard_map/all_gather | solution.py:139
  74.5 53.2 %all_to_all.19 = bf16[128,4,2048]{0,2,1:T(8,128)(2,1)S(1)} all-to-all(bf16[128,4,2048]{0,2,1:T(8,128)(2,1)} %bitcast.41), channel_id=1, replica_groups=mesh['grp'=2,'ctx'=4,'tp'=4] {'ctx'}, dimensions={1} | all-to-all | bytes 4194304 | tf_op jit(solution)/shard_map/all_to_all | solution.py:140
  127.7 2.7 copy.25
  130.4 0.0 copy-start.4
  130.4 0.0 copy-start.5
  130.4 9.0 %convolution_convert_fusion = bf16[512,1792]{1,0:T(8,128)(2,1)} fusion(bf16[512,2048]{1,0:T(8,128)(2,1)} %bitcast.42, bf16[2048,1792]{1,0:T(8,128)(2,1)} %param.17), kind=kOutput, calls=%fused_computation.27 | convolution fusion | flops 3759013888 | bytes 11272192 | tf_op jit(solution)/shard_map/dot_general | solution.py:142
  139.4 0.0 reduce-scatter.4.cloned.1.call-update
  139.4 0.0 all-gather.6.cloned.1.call-start
  139.4 37.6 %reduce-scatter.4.cloned.1.call-done = bf16[128,1792]{1,0:T(8,128)(2,1)} async-done(((bf16[512,1792]{1,0:T(8,128)(2,1)}), bf16[128,1792]{1,0:T(8,128)(2,1)}) %reduce-scatter.4.cloned.1.call-update) | async-done | bytes 458768 | tf_op jit(solution)/shard_map/reduce_scatter | solution.py:141
  177.1 0.0 copy-done.4
  177.1 1.3 fusion.27
  178.3 0.0 copy-start.1
  178.4 6.4 %psum.7 = f32[128]{0:T(128)S(1)} all-reduce(f32[128]{0:T(128)S(1)} %get-tuple-element.31), channel_id=1, replica_groups=mesh['grp'=2,'ctx'=4,'tp'=4] {'tp'}, use_global_device_ids=true, to_apply=%region_10.11 | all-reduce | flops 128 | bytes 1024 | tf_op jit(solution)/shard_map/psum | solution.py:149
  184.8 0.0 copy-done.5
  184.8 0.9 fusion.29
  185.7 0.0 all-gather.6.cloned.1.call-update
  185.8 0.2 reduce-scatter.6.cloned.1.call-start
  186.0 40.0 %all-gather.6.cloned.1.call-done = bf16[512,1792]{1,0:T(8,128)(2,1)} async-done(((bf16[128,1792]{1,0:T(8,128)(2,1)}), bf16[512,1792]{1,0:T(8,128)(2,1)}) %all-gather.6.cloned.1.call-update) | async-done | bytes 1835024 | tf_op jit(solution)/shard_map/all_gather | solution.py:152
  226.0 15.6 %fusion.21 = bf16[512,5120]{1,0:T(8,128)(2,1)} fusion(bf16[512,1792]{1,0:T(8,128)(2,1)} %all-gather.6.cloned.1.call-done, bf16[1792,2560]{1,0:T(8,128)(2,1)} %param.20, bf16[1792,2560]{1,0:T(8,128)(2,1)} %param.19), kind=kOutput, calls=%fused_computation.25 | convolution fusion | flops 9434562560 | bytes 25427968 | tf_op jit(solution)/shard_map/dot_general | solution.py:156
  241.6 0.0 reduce-scatter.6.cloned.1.call-update
  241.7 0.0 all-gather.8.cloned.1.call-start
  241.7 50.4 %reduce-scatter.6.cloned.1.call-done = bf16[128,5120]{1,0:T(8,128)(2,1)} async-done(((bf16[512,5120]{1,0:T(8,128)(2,1)}), bf16[128,5120]{1,0:T(8,128)(2,1)}) %reduce-scatter.6.cloned.1.call-update) | async-done | bytes 1310736 | tf_op jit(solution)/shard_map/reduce_scatter | solution.py:155
  292.1 1.6 convert_element_type.97
  293.6 1.2 fusion.25
  294.8 0.0 all-gather.8.cloned.1.call-update
  294.9 0.0 reduce-scatter.8.cloned.1.call-start
  294.9 25.7 %all-gather.8.cloned.1.call-done = bf16[512,2560]{1,0:T(8,128)(2,1)} async-done(((bf16[128,2560]{1,0:T(8,128)(2,1)}), bf16[512,2560]{1,0:T(8,128)(2,1)}) %all-gather.8.cloned.1.call-update) | async-done | bytes 2621456 | tf_op jit(solution)/shard_map/all_gather | solution.py:164
  320.6 10.5 %convolution_convert_fusion.1 = bf16[512,1792]{1,0:T(8,128)(2,1)} fusion(bf16[512,2560]{1,0:T(8,128)(2,1)} %all-gather.8.cloned.1.call-done, bf16[2560,1792]{1,0:T(8,128)(2,1)} %param.21), kind=kOutput, calls=%fused_computation.28 | convolution fusion | flops 4698537984 | bytes 13631488 | tf_op jit(solution)/shard_map/dot_general | solution.py:166
  331.1 0.0 reduce-scatter.8.cloned.1.call-update
  331.2 39.6 %reduce-scatter.8.cloned.1.call-done = bf16[128,1792]{1,0:T(8,128)(2,1)} async-done(((bf16[512,1792]{1,0:T(8,128)(2,1)}), bf16[128,1792]{1,0:T(8,128)(2,1)}) %reduce-scatter.8.cloned.1.call-update) | async-done | bytes 458768 | tf_op jit(solution)/shard_map/reduce_scatter | solution.py:165
  370.7 0.0 copy-done.1
  370.7 1.9 fusion.30
  (12 shorter events, 0.1 us)
Async XLA Ops:
  7.2 67.3 %all-gather.4.cloned.1.call-start = ((), (), s32[]{:S(2)}) async-start(), calls=%async_computation.4 | async-start | bytes 2621440 | tf_op jit(solution)/shard_map/all_gather | solution.py:139
  10.3 4.2 %copy-start.3 = (bf16[576,128]{1,0:T(8,128)(2,1)S(1)}, bf16[576,128]{1,0:T(8,128)(2,1)}, u32[]{:S(2)}) copy-start(bf16[576,128]{1,0:T(8,128)(2,1)} %param.13) | copy-start | bytes 442372
  12.9 1.6 copy-start.6
  12.9 2.3 slice-start
  14.5 23.8 %copy-start = (bf16[128,16,512]{0,2,1:T(8,128)(2,1)S(1)}, bf16[128,16,512]{0,2,1:T(8,128)(2,1)}, u32[]{:S(2)}) copy-start(bf16[128,16,512]{0,2,1:T(8,128)(2,1)} %slice.39) | copy-start | bytes 6291460
  39.9 8.6 %copy-start.2 = (bf16[512,2048]{0,1:T(8,128)(2,1)S(1)}, bf16[512,2048]{0,1:T(8,128)(2,1)}, u32[]{:S(2)}) copy-start(bf16[512,2048]{0,1:T(8,128)(2,1)} %copy.27) | copy-start | bytes 6291460
  52.3 124.7 %reduce-scatter.4.cloned.1.call-start = ((), (), s32[]{:S(2)}) async-start(), calls=%async_computation.5 | async-start | bytes 2293760 | tf_op jit(solution)/shard_map/reduce_scatter | solution.py:141
  130.4 46.7 %copy-start.4 = (bf16[128,1792]{1,0:T(8,128)(2,1)S(1)}, bf16[128,1792]{1,0:T(8,128)(2,1)}, u32[]{:S(2)}) copy-start(bf16[128,1792]{1,0:T(8,128)(2,1)} %param.12) | copy-start | bytes 1376260
  130.4 54.4 %copy-start.5 = (f32[1792]{0:T(1024)S(1)}, f32[1792]{0:T(1024)}, u32[]{:S(2)}) copy-start(f32[1792]{0:T(1024)} %param.18) | copy-start | bytes 21508
  139.4 86.6 %all-gather.6.cloned.1.call-start = ((), (), s32[]{:S(2)}) async-start(), calls=%async_computation.6 | async-start | bytes 2293760 | tf_op jit(solution)/shard_map/all_gather | solution.py:152
  178.3 192.4 %copy-start.1 = (bf16[128,1792]{1,0:T(8,128)(2,1)}, bf16[128,1792]{1,0:T(8,128)(2,1)S(1)}, u32[]{:S(2)}) copy-start(bf16[128,1792]{1,0:T(8,128)(2,1)S(1)} %get-tuple-element.32) | copy-start | bytes 1376260
  185.8 106.3 %reduce-scatter.6.cloned.1.call-start = ((), (), s32[]{:S(2)}) async-start(), calls=%async_computation.7 | async-start | bytes 6553600 | tf_op jit(solution)/shard_map/reduce_scatter | solution.py:155
  241.7 78.9 %all-gather.8.cloned.1.call-start = ((), (), s32[]{:S(2)}) async-start(), calls=%async_computation.8 | async-start | bytes 3276800 | tf_op jit(solution)/shard_map/all_gather | solution.py:164
  294.9 75.9 %reduce-scatter.8.cloned.1.call-start = ((), (), s32[]{:S(2)}) async-start(), calls=%async_computation.9 | async-start | bytes 2293760 | tf_op jit(solution)/shard_map/reduce_scatter | solution.py:165
Sparse Core Ops, SparseCore 0:
  52.5 21.9 all-gather.3
  139.5 37.5 reduce-scatter.3
  185.9 40.0 all-gather.5
  241.8 50.2 reduce-scatter.5
  295.0 25.5 all-gather.7
  331.3 39.3 reduce-scatter.7
where the time goes:
time: 380 us; the launch traced here: 379 us
  waiting for transfers between devices  215 us (57%)
  blocking collectives  77.6 us (20%)
  matrix products  46.3 us (12%)
  other arithmetic  14.2 us (4%)
  between operations  14.2 us (4%)
  local copies, waits for them, and re-layouts  11.2 us (3%)
    all_to_all x1, blocking collectives, on_device(): lax.all_to_all(all_heads, 'ctx', split_axis=1, concat_axis=0, tiled=True)  53.2 us
    reduce_scatter x1, waiting for transfers between devices, on_device(): lax.psum_scatter(jnp.dot(scaled_all, gate_up, preferred_element_type=jnp....  50.4 us
    all_gather x1, waiting for transfers between devices, on_device(): scaled_all = lax.all_gather(scaled, 'ctx', axis=0, tiled=True)  40 us
    reduce_scatter x1, waiting for transfers between devices, on_device(): lax.psum_scatter(jnp.dot(hidden_all, down_weight, preferred_element_type=...  39.6 us
    reduce_scatter x1, waiting for transfers between devices, on_device(): lax.psum_scatter(jnp.dot(head_block, output_weight, preferred_element_typ...  37.6 us
    all_gather x1, waiting for transfers between devices, on_device(): hidden_all = lax.all_gather(hidden_share, 'tp', axis=0, tiled=True)  25.7 us
    all_gather x1, waiting for transfers between devices, on_device(): all_heads = lax.all_gather(heads_out, 'tp', axis=1, tiled=True)  22.1 us
    all_gather x1, blocking collectives, on_device(): key_piece = lax.all_gather(rotated_keys, 'ctx', axis=1, tiled=True)  18 us
  transfers between devices with their start and end apart: 6, of which 6 were waited for; matrix products, arithmetic and copies ran while one was open for 0% of the time, Pallas kernels for 0%

commit v1 on v0

--- a/solution.py
+++ b/solution.py
@@ -84,6 +84,125 @@
         preferred_element_type=jnp.float32,
     )
     return (new_top, row_total, mixed_sum)
+
+
+def swap(value, axis_name, bit):
+    width = lax.axis_size(axis_name)
+    return lax.ppermute(value, axis_name, [(i, i ^ bit) for i in range(width)])
+
+
+def pick(value, index):
+    return lax.dynamic_index_in_dim(value, index, 0, keepdims=False)
+
+
+def wide(value):
+    return value.astype(jnp.float32)
+
+
+def matmul(a, b):
+    return jnp.dot(a, b, preferred_element_type=jnp.float32).astype(jnp.bfloat16)
+
+
+def spread_heads(heads_out, n_ctx, n_tp):
+    pieces = heads_out.reshape(n_ctx, heads_out.shape[0] // n_ctx, heads_out.shape[1])
+    return [
+        lax.ppermute(
+            pieces[s],
+            ("ctx", "tp"),
+            [(c * n_tp + t, t * n_tp + (c ^ s)) for c in range(n_ctx) for t in range(n_tp)],
+        )
+        for s in range(n_ctx)
+    ]
+
+
+def pair_rows(first, second):
+    return jnp.concatenate(
+        [first[0], second[1], second[0], first[1], first[2], second[3], second[2], first[3]], axis=0
+    )
+
+
+def reduce_ctx(kept, sent):
+    came = swap(sent, "ctx", 1)
+    mine = wide(kept[0]) + wide(came[0])
+    other = (wide(kept[1]) + wide(came[1])).astype(jnp.bfloat16)
+    return mine + wide(swap(other, "ctx", 2))
+
+
+def gather_ctx(rows):
+    pair = jnp.concatenate([rows, swap(rows, "ctx", 2)], axis=0)
+    return jnp.concatenate([pair, swap(pair, "ctx", 1)], axis=0)
+
+
+def paired_tail(
+    heads_out, residual, output_weight, norm_gain, gate_weight, up_weight, down_weight, n_ctx, n_tp
+):
+    row_count, width = residual.shape
+    half = row_count // 2
+    model_width = width * n_tp
+    c = lax.axis_index("ctx")
+    t = lax.axis_index("tp")
+    core = t & 1
+    first_half = (t >> 1) ^ (c >> 1)
+    own = spread_heads(heads_out, n_ctx, n_tp)
+    own_all = jnp.stack(own)
+    far = swap(own_all, "tp", 2)
+    near = swap(own_all, "tp", 1)
+    far_near = swap(far, "tp", 1)
+    rows_a = pair_rows(own_all, near)
+    order = [2, 3, 0, 1]
+    rows_b = pair_rows([far[i] for i in order], [far_near[i] for i in order])
+    residual_halves = residual.reshape(2, half, width)
+
+    def project(rows, which):
+        blocks = matmul(rows, output_weight).reshape(n_ctx, half, width)
+        place = t ^ c
+        head_sum = reduce_ctx(
+            (pick(blocks, place), pick(blocks, place ^ 2)),
+            jnp.stack([pick(blocks, place ^ 1), pick(blocks, place ^ 3)]),
+        )
+        attended = (wide(pick(residual_halves, which)) + head_sum).astype(jnp.bfloat16)
+        return attended, gather_ctx(attended)
+
+    attended_a, all_a = project(rows_a, first_half)
+    attended_b, all_b = project(rows_b, 1 - first_half)
+
+    def gate_up(all_rows):
+        values = wide(all_rows)
+        squares = jnp.sum(values * values, axis=1).reshape(2, 2 * half)
+        scaled = (values * norm_gain[None, :]).astype(jnp.bfloat16)
+        sums = [matmul(scaled, w).reshape(2, 2 * half, -1) for w in (gate_weight, up_weight)]
+        kept, came = [], []
+        for term in sums + [squares]:
+            came.append(swap(pick(term, 1 - core), "tp", 1))
+            kept.append(pick(term, core))
+        return kept, came
+
+    kept_a, came_a = gate_up(all_a)
+    across = [
+        swap((wide(k) + wide(r)).astype(k.dtype), "tp", 2) for k, r in zip(kept_a, came_a)
+    ]
+    kept_b, came_b = gate_up(all_b)
+    gate, up, squares = [wide(k) + wide(r) + wide(x) for k, r, x in zip(kept_b, came_b, across)]
+    inverse_rms = lax.rsqrt(squares / model_width + norm_eps)[:, None]
+    hidden = (jax.nn.silu(gate * inverse_rms) * (up * inverse_rms)).astype(jnp.bfloat16)
+    hidden_far = swap(hidden, "tp", 2)
+    hidden_near = swap(hidden, "tp", 1)
+    hidden_far_near = swap(hidden_far, "tp", 1)
+
+    def down(mine, other, attended):
+        blocks = matmul(jnp.concatenate([mine, other], axis=0), down_weight)
+        blocks = blocks.reshape(2, 2, half, width)
+        total = reduce_ctx(pick(blocks, core), pick(blocks, 1 - core))
+        return (wide(attended) + total).astype(jnp.bfloat16)
+
+    out_b = down(hidden, hidden_near, attended_b)
+    out_a = down(hidden_far, hidden_far_near, attended_a)
+
+    def in_order(a, b):
+        first = first_half == 0
+        return jnp.concatenate([jnp.where(first, a, b), jnp.where(first, b, a)], axis=0)
+
+    return in_order(attended_a, attended_b), in_order(out_a, out_b)
 
 
 def on_device(
@@ -136,6 +255,19 @@
         .astype(jnp.bfloat16)
         .reshape(row_count, local_heads * VHEAD)
     )
+    n_ctx, n_tp = lax.axis_size("ctx"), lax.axis_size("tp")
+    if n_ctx == 4 and n_tp == 4 and row_count % 64 == 0:
+        return paired_tail(
+            heads_out,
+            residual,
+            output_weight,
+            norm_gain,
+            gate_weight,
+            up_weight,
+            down_weight,
+            n_ctx,
+            n_tp,
+        )
     all_heads = lax.all_gather(heads_out, "tp", axis=1, tiled=True)
     head_block = lax.all_to_all(all_heads, "ctx", split_axis=1, concat_axis=0, tiled=True)
     head_sum = lax.psum_scatter(

time: 380 us -> 283 us (0.74)
  blocking collectives: 77.6 us -> 18 us
  waiting for transfers between devices: 215 us -> 168 us
  starting transfers between devices: 0.43 us -> 28 us
  between operations: 14.2 us -> 1.38 us
  local copies, waits for them, and re-layouts: 11.2 us -> 6.69 us
    ppermute x0 -> x31, waiting for transfers between devices: none -> 168 us  [the longest x27 154 us: swap(): return lax.ppermute(value, axis_name, [(i, i ^ bit) for i in range(width)])]
    reduce_scatter x3 -> x0, waiting for transfers between devices: 128 us -> none  [the longest x1 50.4 us: on_device(): lax.psum_scatter(jnp.dot(scaled_all, gate_up, preferred_element_type=jnp....]
    all_gather x3 -> x0, waiting for transfers between devices: 87.8 us -> none  [the longest x1 40 us: on_device(): scaled_all = lax.all_gather(scaled, 'ctx', axis=0, tiled=True)]
    all_to_all x1 -> x0, blocking collectives: 53.2 us -> none  [on_device(): lax.all_to_all(all_heads, 'ctx', split_axis=1, concat_axis=0, tiled=True)]
    ppermute x0 -> x31, starting transfers between devices: none -> 28 us  [the longest x27 23.5 us: swap(): return lax.ppermute(value, axis_name, [(i, i ^ bit) for i in range(width)])]
    psum x1 -> x0, blocking collectives: 6.42 us -> none  [on_device(): squares = lax.psum(jnp.sum(attended_float * attended_float, axis=1), 'tp')]
    convert_element_type x4 -> x7, other arithmetic: 5.61 us -> 1.36 us  [the longest x1 0.82 us: paired_tail(): (jax.nn.silu(gate * inverse_rms) * (up * inverse_rms)).astype(jnp.bfloat16)]
    reshape x1 -> x0, local copies, waits for them, and re-layouts: 3.93 us -> none  [on_device(): value_weight.reshape(LAT, local_heads, VHEAD)]
  transfers between devices with their start and end apart: 6 -> 31, of which waited for: 6 -> 18; matrix products, arithmetic and copies ran while one was open for 0% -> 12% of each run, Pallas kernels for 0% -> 0%
where the time goes in v1:
time: 283 us; the launch traced here: 282 us
  waiting for transfers between devices  168 us (59%)
  matrix products  43.7 us (15%)
  starting transfers between devices  28 us (10%)
  blocking collectives  18 us (6%)
  other arithmetic  16.2 us (6%)
  local copies, waits for them, and re-layouts  6.69 us (2%)
    ppermute x27, waiting for transfers between devices, swap(): return lax.ppermute(value, axis_name, [(i, i ^ bit) for i in range(width)])  154 us
    dot_general x8, matrix products, matmul(): jnp.dot(a, b, preferred_element_type=jnp.float32).astype(jnp.bfloat16)  33.5 us
    ppermute x27, starting transfers between devices, swap(): return lax.ppermute(value, axis_name, [(i, i ^ bit) for i in range(width)])  23.5 us
    all_gather x1, blocking collectives, on_device(): key_piece = lax.all_gather(rotated_keys, 'ctx', axis=1, tiled=True)  18 us
    ppermute x4, waiting for transfers between devices, spread_heads(): lax.ppermute(pieces[s], ('ctx', 'tp'), [(c * n_tp + t, t * n_tp + (c ^ s)...  14 us
  transfers between devices with their start and end apart: 31, of which 18 were waited for; matrix products, arithmetic and copies ran while one was open for 12% of the time, Pallas kernels for 0%

profile of v1, /device:TPU:0, one launch (start us, length us, event | category | flops | bytes accessed | tf_op | source)
XLA Modules:
  0.0 282.1 jit_solution(12022651935021631955)
XLA Ops:
  0.7 4.4 %copy.23 = bf16[128,9216]{0,1:T(8,128)(2,1)} copy(bf16[128,9216]{1,0:T(8,128)(2,1)} %param.14) | data formatting | bytes 4718592 | tf_op args[2]
  5.1 4.4 %convert_element_type.279 = f32[128,16,576]{0,2,1:T(8,128)} convert(bf16[128,16,576]{0,2,1:T(8,128)(2,1)} %bitcast.236) | non-fusion elementwise | flops 1179648 | bytes 7077888 | tf_op jit(solution)/shard_map/convert_element_type | solution.py:50
  9.5 1.5 slice.151
  11.1 0.2 reduce-window.8
  11.8 18.0 %all_gather.3 = bf16[576,512]{1,0:T(8,128)(2,1)S(1)} all-gather(bf16[576,128]{1,0:T(8,128)(2,1)S(1)} %pad_maximum_fusion.10), channel_id=1, replica_groups=mesh['grp'=2,'ctx'=4,'tp'=4] {'ctx'}, dimensions={1}, use_global_device_ids=true | all-gather | bytes 737280 | tf_op jit(solution)/shard_map/all_gather | solution.py:235
  29.8 1.1 subtract_convert_fusion
  30.9 3.2 %pad_maximum_fusion = bf16[128,16,576]{0,2,1:T(8,128)(2,1)} fusion(bf16[128,16,32]{0,2,1:T(8,128)(2,1)S(1)} %get-tuple-element.40, bf16[128,16,32]{0,2,1:T(8,128)(2,1)S(1)} %get-tuple-element.39, bf16[128,16,512]{0,2,1:T(8,128)(2,1)} %slice.151), kind=kLoop, calls=%fused_computation.30 | loop fusion | flops 7077888 | bytes 4718592 | tf_op jit(solution)/shard_map/concatenate | solution.py:57
  34.2 8.4 %conditional.1 = (f32[16,128]{1,0:T(8,128)S(1)}, f32[16,128,512]{2,1,0:T(8,128)}) conditional(s32[]{:T(128)} %convert_element_type.273, () %tuple.16, (s32[512,4]{0,1:T(4,128)S(1)}, s32[128]{0:T(128)S(1)}, s32[512]{0:T(512)S(1)}, s32[]{:T(128)}, s32[128]{0:T(128)S(1)}, /*index=5*/bf16[576,512]{1,0:T(8,128)(2,1)S(1)}, ...), branch_computations={%region_3.4_spmd, %region_4.0_spmd} | conditional | flops 2295528960 | bytes 20578328 | solution.py:238
  34.2 0.2 compare_and_fusion
  34.4 3.7 %fusion = (f32[16,128]{1,0:T(8,128)S(1)}, f32[512,128,16]{1,0,2:T(8,128)S(1)}) fusion(pred[128,512]{0,1:T(8,128)(4,1)S(1)} %compare_and_fusion, bf16[128,16,576]{0,2,1:T(8,128)(2,1)} %get-tuple-element.24, bf16[576,512]{1,0:T(8,128)(2,1)S(1)} %get-tuple-element.23), kind=kOutput, calls=%fused_computation.2 | convolution fusion | flops 1211103232 | bytes 7217152 | tf_op jit(solution)/shard_map/cond/branch_1_fun/qhe,ek->hqk/dot_general | solution.py:73
  38.1 3.5 %fusion.3 = f32[16,128,512]{2,1,0:T(8,128)} fusion(f32[512,128,16]{1,0,2:T(8,128)S(1)} %get-tuple-element.38, f32[16,128]{1,0:T(8,128)S(1)} %broadcast_maximum_fusion, pred[128,512]{0,1:T(8,128)(4,1)S(1)} %compare_and_fusion, bf16[576,512]{1,0:T(8,128)(2,1)S(1)} %get-tuple-element.23), kind=kOutput, calls=%fused_computation.5 | convolution fusion | flops 1078984704 | bytes 8986624 | tf_op jit(solution)/shard_map/cond/branch_1_fun/hqk,lk->hql/dot_general | solution.py:80
  41.6 1.0 fusion.2
  42.6 3.0 %fusion.41 = bf16[128,16,128]{2,0,1:T(8,128)(2,1)S(1)} fusion(f32[16,128,512]{2,1,0:T(8,128)} %get-tuple-element.29, f32[16,128]{1,0:T(8,128)S(1)} %get-tuple-element.30, bf16[512,2048]{1,0:T(8,128)(2,1)S(1)} %copy-done), kind=kOutput, calls=%fused_computation.61 | convolution fusion | flops 270794752 | bytes 6823936 | tf_op jit(solution)/shard_map/hql,lhd->qhd/dot_general | solution.py:249
  45.9 1.5 collective-permute-start.2
  47.4 2.1 collective-permute-start.3
  49.5 0.8 collective-permute-start
  50.4 1.7 collective-permute-done.1
  52.0 12.4 %collective-permute-done.2 = bf16[32,2048]{1,0:T(8,128)(2,1)S(1)} collective-permute-done((bf16[32,2048]{1,0:T(8,128)(2,1)S(1)}, bf16[32,2048]{1,0:T(8,128)(2,1)S(1)}, u32[]{:S(2)}, u32[]{:S(2)}) %collective-permute-start.2) | collective-permute-done | bytes 131104 | tf_op jit(solution)/shard_map/ppermute | solution.py:109
  64.5 2.7 collective-permute-start.4
  67.2 4.5 %collective-permute-start.7 = (bf16[4,32,2048]{2,1,0:T(8,128)(2,1)S(1)}, bf16[4,32,2048]{2,1,0:T(8,128)(2,1)S(1)}, u32[]{:S(2)}, u32[]{:S(2)}) collective-permute-start(bf16[4,32,2048]{2,1,0:T(8,128)(2,1)S(1)} %pad_maximum_fusion.3), channel_id=1, source_target_pairs={{0,2},{1,3},{2,0},{3,1},{4,6},{5,7},{6,4},{7,5},{8,10},{9,11},{10,... | collective-permute-start | bytes 1572872 | tf_op jit(solution)/shard_map/ppermute | solution.py:91
  71.9 12.3 %collective-permute-done.7 = bf16[4,32,2048]{2,1,0:T(8,128)(2,1)S(1)} collective-permute-done((bf16[4,32,2048]{2,1,0:T(8,128)(2,1)S(1)}, bf16[4,32,2048]{2,1,0:T(8,128)(2,1)S(1)}, u32[]{:S(2)}, u32[]{:S(2)}) %collective-permute-start.7) | collective-permute-done | bytes 524320 | tf_op jit(solution)/shard_map/ppermute | solution.py:91
  84.2 5.1 %convolution_convert_fusion.5 = bf16[256,1792]{1,0:T(8,128)(2,1)S(1)} fusion(bf16[256,2048]{1,0:T(8,128)(2,1)S(1)} %constant_dynamic-update-slice_fusion, bf16[2048,1792]{1,0:T(8,128)(2,1)} %param.17), kind=kOutput, calls=%fused_computation.27 | convolution fusion | flops 1879506944 | bytes 9306112 | tf_op jit(solution)/shard_map/dot_general | solution.py:103
  89.6 2.1 convolution_convert_fusion.4
  91.8 0.6 collective-permute-start.9
  92.4 1.6 collective-permute-start.5
  94.0 11.2 %collective-permute-done.9 = bf16[2,64,1792]{2,1,0:T(8,128)(2,1)S(1)} collective-permute-done((bf16[2,64,1792]{2,1,0:T(8,128)(2,1)S(1)}, bf16[2,64,1792]{2,1,0:T(8,128)(2,1)S(1)}, u32[]{:S(2)}, u32[]{:S(2)}) %collective-permute-start.9) | collective-permute-done | bytes 458784 | tf_op jit(solution)/shard_map/ppermute | solution.py:91
  105.2 1.8 collective-permute-start.10
  107.1 12.4 %collective-permute-done.5 = bf16[2,64,1792]{2,1,0:T(8,128)(2,1)S(1)} collective-permute-done((bf16[2,64,1792]{2,1,0:T(8,128)(2,1)S(1)}, bf16[2,64,1792]{2,1,0:T(8,128)(2,1)S(1)}, u32[]{:S(2)}, u32[]{:S(2)}) %collective-permute-start.5) | collective-permute-done | bytes 458784 | tf_op jit(solution)/shard_map/ppermute | solution.py:91
  119.6 1.0 collective-permute-start.6
  120.6 12.1 %collective-permute-done.6 = bf16[64,1792]{1,0:T(8,128)(2,1)S(1)} collective-permute-done((bf16[64,1792]{1,0:T(8,128)(2,1)S(1)}, bf16[64,1792]{1,0:T(8,128)(2,1)S(1)}, u32[]{:S(2)}, u32[]{:S(2)}) %collective-permute-start.6) | collective-permute-done | bytes 229408 | tf_op jit(solution)/shard_map/ppermute | solution.py:91
  132.7 1.4 broadcast_select_fusion.3
  134.2 2.9 %collective-permute-start.14 = (bf16[64,1792]{1,0:T(8,128)(2,1)S(1)}, bf16[64,1792]{1,0:T(8,128)(2,1)S(1)}, u32[]{:S(2)}, u32[]{:S(2)}) collective-permute-start(bf16[64,1792]{1,0:T(8,128)(2,1)S(1)} %get-tuple-element.35), channel_id=1, source_target_pairs={{0,8},{4,12},{8,0},{12,4},{1,9},{5,13},{9,1},{13,5},{2,10},{6,14},... | collective-permute-start | bytes 688136 | tf_op jit(solution)/shard_map/ppermute | solution.py:91
  137.1 14.6 %collective-permute-done.11 = bf16[64,1792]{1,0:T(8,128)(2,1)S(1)} collective-permute-done((bf16[64,1792]{1,0:T(8,128)(2,1)S(1)}, bf16[64,1792]{1,0:T(8,128)(2,1)S(1)}, u32[]{:S(2)}, u32[]{:S(2)}) %collective-permute-start.11) | collective-permute-done | bytes 229408 | tf_op jit(solution)/shard_map/ppermute | solution.py:91
  151.9 4.8 %collective-permute-done.14 = bf16[64,1792]{1,0:T(8,128)(2,1)S(1)} collective-permute-done((bf16[64,1792]{1,0:T(8,128)(2,1)S(1)}, bf16[64,1792]{1,0:T(8,128)(2,1)S(1)}, u32[]{:S(2)}, u32[]{:S(2)}) %collective-permute-start.14) | collective-permute-done | bytes 229408 | tf_op jit(solution)/shard_map/ppermute | solution.py:91
  156.8 9.7 %collective-permute-done.12 = bf16[128,1792]{1,0:T(8,128)(2,1)S(1)} collective-permute-done((bf16[128,1792]{1,0:T(8,128)(2,1)S(1)}, bf16[128,1792]{1,0:T(8,128)(2,1)S(1)}, u32[]{:S(2)}, u32[]{:S(2)}) %collective-permute-start.12) | collective-permute-done | bytes 458784 | tf_op jit(solution)/shard_map/ppermute | solution.py:91
  166.5 6.1 %convolution_convert_fusion.3 = bf16[256,2560]{1,0:T(8,128)(2,1)S(1)} fusion(bf16[1792,2560]{1,0:T(8,128)(2,1)} %param.19, f32[1792]{0:T(1024)S(1)} %copy-done.5, bf16[128,1792]{1,0:T(8,128)(2,1)S(1)} %collective-permute-done.12, bf16[64,1792]{1,0:T(8,128)(2,1)S(1)} %collective-permute-done.11, bf16[64,1792]{1,0:T(8,128)(2,1)S(1)} %get-tuple-element.36), kind=kOutput, calls=%fused_computation.25 | convolution fusion | flops 2353135616 | bytes 11410432 | tf_op jit(solution)/shard_map/dot_general | solution.py:103
  172.8 3.4 %collective-permute-done.15 = bf16[128,1792]{1,0:T(8,128)(2,1)S(1)} collective-permute-done((bf16[128,1792]{1,0:T(8,128)(2,1)S(1)}, bf16[128,1792]{1,0:T(8,128)(2,1)S(1)}, u32[]{:S(2)}, u32[]{:S(2)}) %collective-permute-start.15) | collective-permute-done | bytes 458784 | tf_op jit(solution)/shard_map/ppermute | solution.py:91
  176.2 2.5 convolution_convert_fusion.2
  179.0 2.5 convolution_convert_fusion.1
  181.6 0.5 collective-permute-start.21
  182.1 2.8 convolution_convert_fusion
  185.0 0.3 fusion.23
  185.5 1.2 collective-permute-start.17
  186.7 0.4 collective-permute-done.22
  187.2 1.2 collective-permute-start.23
  188.4 0.3 fusion.21
  188.7 0.8 collective-permute-done.19
  189.6 0.2 collective-permute-start.18
  189.8 0.9 collective-permute-done.18
  190.7 0.9 collective-permute-start.20
  191.6 25.2 %collective-permute-done.20 = f32[128]{0:T(128)S(1)} collective-permute-done((f32[128]{0:T(128)S(1)}, f32[128]{0:T(128)S(1)}, u32[]{:S(2)}, u32[]{:S(2)}) %collective-permute-start.20) | collective-permute-done | bytes 544 | tf_op jit(solution)/shard_map/ppermute | solution.py:91
  216.8 0.8 fusion.34
  217.6 1.2 collective-permute-start.24
  218.8 15.1 %collective-permute-done.24 = bf16[128,2560]{1,0:T(8,128)(2,1)S(1)} collective-permute-done((bf16[128,2560]{1,0:T(8,128)(2,1)S(1)}, bf16[128,2560]{1,0:T(8,128)(2,1)S(1)}, u32[]{:S(2)}, u32[]{:S(2)}) %collective-permute-start.24) | collective-permute-done | bytes 655392 | tf_op jit(solution)/shard_map/ppermute | solution.py:91
  233.9 6.1 %convolution_convert_fusion.6 = bf16[256,1792]{1,0:T(8,128)(2,1)S(1)} fusion(bf16[2560,1792]{1,0:T(8,128)(2,1)} %param.21, bf16[128,2560]{1,0:T(8,128)(2,1)S(1)} %collective-permute-done.28, bf16[128,2560]{1,0:T(8,128)(2,1)S(1)} %fusion.34), kind=kOutput, calls=%fused_computation.28 | convolution fusion | flops 2351890432 | bytes 11403264 | tf_op jit(solution)/shard_map/dot_general | solution.py:103
  240.2 6.1 %convolution_convert_fusion.7 = bf16[256,1792]{1,0:T(8,128)(2,1)S(1)} fusion(bf16[2560,1792]{1,0:T(8,128)(2,1)} %param.21, bf16[128,2560]{1,0:T(8,128)(2,1)S(1)} %collective-permute-done.25, bf16[128,2560]{1,0:T(8,128)(2,1)S(1)} %collective-permute-done.24), kind=kOutput, calls=%fused_computation.29 | convolution fusion | flops 2351890432 | bytes 11403264 | tf_op jit(solution)/shard_map/dot_general | solution.py:103
  246.4 2.1 collective-permute-start.26
  248.5 5.0 %collective-permute-done.29 = bf16[2,64,1792]{2,1,0:T(8,128)(2,1)S(1)} collective-permute-done((bf16[2,64,1792]{2,1,0:T(8,128)(2,1)S(1)}, bf16[2,64,1792]{2,1,0:T(8,128)(2,1)S(1)}, u32[]{:S(2)}, u32[]{:S(2)}) %collective-permute-start.29) | collective-permute-done | bytes 458784 | tf_op jit(solution)/shard_map/ppermute | solution.py:91
  253.6 0.5 collective-permute-start.30
  254.1 13.8 %collective-permute-done.26 = bf16[2,64,1792]{2,1,0:T(8,128)(2,1)S(1)} collective-permute-done((bf16[2,64,1792]{2,1,0:T(8,128)(2,1)S(1)}, bf16[2,64,1792]{2,1,0:T(8,128)(2,1)S(1)}, u32[]{:S(2)}, u32[]{:S(2)}) %collective-permute-start.26) | collective-permute-done | bytes 458784 | tf_op jit(solution)/shard_map/ppermute | solution.py:91
  268.0 12.2 %collective-permute-done.27 = bf16[64,1792]{1,0:T(8,128)(2,1)S(1)} collective-permute-done((bf16[64,1792]{1,0:T(8,128)(2,1)S(1)}, bf16[64,1792]{1,0:T(8,128)(2,1)S(1)}, u32[]{:S(2)}, u32[]{:S(2)}) %collective-permute-start.27) | collective-permute-done | bytes 229408 | tf_op jit(solution)/shard_map/ppermute | solution.py:91
  280.2 0.3 broadcast_select_fusion.1
  280.5 0.8 pad_maximum_fusion.9
  281.3 0.8 pad_maximum_fusion.6
  (121 shorter events, 2.9 us)
Async XLA Ops:
  0.6 42.0 %copy-start = (bf16[512,2048]{1,0:T(8,128)(2,1)S(1)}, bf16[512,2048]{1,0:T(8,128)(2,1)}, u32[]{:S(2)}) copy-start(bf16[512,2048]{1,0:T(8,128)(2,1)} %param.16) | copy-start | bytes 6291460
  5.1 4.4 %copy-start.2 = (bf16[128,9216]{0,1:T(8,128)(2,1)S(1)}, bf16[128,9216]{0,1:T(8,128)(2,1)}, u32[]{:S(2)}) copy-start(bf16[128,9216]{0,1:T(8,128)(2,1)} %copy.23) | copy-start | bytes 7077892
  9.5 1.5 copy-start.4
  9.5 1.6 copy-start.6
  9.5 2.3 slice-start
  45.8 6.3 %collective-permute-start.1 = (bf16[32,2048]{1,0:T(8,128)(2,1)S(1)}, bf16[32,2048]{1,0:T(8,128)(2,1)S(1)}, u32[]{:S(2)}, u32[]{:S(2)}) collective-permute-start(bf16[32,2048]{1,0:T(8,128)(2,1)S(1)} %bitcast.263), channel_id=1, source_target_pairs={{0,1},{1,5},{2,9},{3,13},{4,0},{5,4},{6,8},{7,12},{8,3},{9,7},{10,... | collective-permute-start | bytes 393224 | tf_op jit(solution)/shard_map/ppermute | solution.py:109
  45.9 18.6 %collective-permute-start.2 = (bf16[32,2048]{1,0:T(8,128)(2,1)S(1)}, bf16[32,2048]{1,0:T(8,128)(2,1)S(1)}, u32[]{:S(2)}, u32[]{:S(2)}) collective-permute-start(bf16[32,2048]{1,0:T(8,128)(2,1)S(1)} %bitcast.264), channel_id=1, source_target_pairs={{0,2},{1,6},{2,10},{3,14},{4,3},{5,7},{6,11},{7,15},{8,0},{9,4},{1... | collective-permute-start | bytes 393224 | tf_op jit(solution)/shard_map/ppermute | solution.py:109
  47.4 17.0 %collective-permute-start.3 = (bf16[32,2048]{1,0:T(8,128)(2,1)S(1)}, bf16[32,2048]{1,0:T(8,128)(2,1)S(1)}, u32[]{:S(2)}, u32[]{:S(2)}) collective-permute-start(bf16[32,2048]{1,0:T(8,128)(2,1)S(1)} %bitcast.265), channel_id=1, source_target_pairs={{0,3},{1,7},{2,11},{3,15},{4,2},{5,6},{6,10},{7,14},{8,1},{9,5},{1... | collective-permute-start | bytes 393224 | tf_op jit(solution)/shard_map/ppermute | solution.py:109
  49.5 14.9 %collective-permute-start = (bf16[32,2048]{1,0:T(8,128)(2,1)S(1)}, bf16[32,2048]{1,0:T(8,128)(2,1)S(1)}, u32[]{:S(2)}, u32[]{:S(2)}) collective-permute-start(bf16[32,2048]{1,0:T(8,128)(2,1)S(1)} %bitcast.266), channel_id=1, source_target_pairs={{0,0},{1,4},{2,8},{3,12},{4,1},{5,5},{6,9},{7,13},{8,2},{9,6},{10,... | collective-permute-start | bytes 393224 | tf_op jit(solution)/shard_map/ppermute | solution.py:109
  64.5 7.2 %collective-permute-start.4 = (bf16[4,32,2048]{2,1,0:T(8,128)(2,1)S(1)}, bf16[4,32,2048]{2,1,0:T(8,128)(2,1)S(1)}, u32[]{:S(2)}, u32[]{:S(2)}) collective-permute-start(bf16[4,32,2048]{2,1,0:T(8,128)(2,1)S(1)} %pad_maximum_fusion.3), channel_id=1, source_target_pairs={{0,1},{1,0},{2,3},{3,2},{4,5},{5,4},{6,7},{7,6},{8,9},{9,8},{10,11... | collective-permute-start | bytes 1572872 | tf_op jit(solution)/shard_map/ppermute | solution.py:91
  67.2 17.0 %collective-permute-start.7 = (bf16[4,32,2048]{2,1,0:T(8,128)(2,1)S(1)}, bf16[4,32,2048]{2,1,0:T(8,128)(2,1)S(1)}, u32[]{:S(2)}, u32[]{:S(2)}) collective-permute-start(bf16[4,32,2048]{2,1,0:T(8,128)(2,1)S(1)} %pad_maximum_fusion.3), channel_id=1, source_target_pairs={{0,2},{1,3},{2,0},{3,1},{4,6},{5,7},{6,4},{7,5},{8,10},{9,11},{10,... | collective-permute-start | bytes 1572872 | tf_op jit(solution)/shard_map/ppermute | solution.py:91
  71.8 17.7 %slice-start.7 = ((s8[7340032]{0:T(1024)(128)(4,1)}), s8[4194304]{0:T(1024)(128)(4,1)S(1)}, s32[]{:S(2)}) async-start(s8[7340032]{0:T(1024)(128)(4,1)} %bitcast.277), calls=%async_computation.7 | async-start | bytes 8388608
  71.9 17.7 %slice-start.8 = ((s8[7340032]{0:T(1024)(128)(4,1)}), s8[3145728]{0:T(1024)(128)(4,1)S(1)}, s32[]{:S(2)}) async-start(s8[7340032]{0:T(1024)(128)(4,1)} %bitcast.277), calls=%async_computation.8 | async-start | bytes 6291456
  84.2 5.2 %collective-permute-start.8 = (bf16[4,32,2048]{2,1,0:T(8,128)(2,1)S(1)}, bf16[4,32,2048]{2,1,0:T(8,128)(2,1)S(1)}, u32[]{:S(2)}, u32[]{:S(2)}) collective-permute-start(bf16[4,32,2048]{2,1,0:T(8,128)(2,1)S(1)} %collective-permute-done.7), channel_id=1, source_target_pairs={{0,1},{1,0},{2,3},{3,2},{4,5},{5,4},{6,7},{7,6},{8,9},{9,8},{10,11... | collective-permute-start | bytes 1572872 | tf_op jit(solution)/shard_map/ppermute | solution.py:91
  91.7 13.6 %copy-start.3 = (bf16[256,1792]{1,0:T(8,128)(2,1)}, bf16[256,1792]{1,0:T(8,128)(2,1)S(1)}, u32[]{:S(2)}) copy-start(bf16[256,1792]{1,0:T(8,128)(2,1)S(1)} %convolution_convert_fusion.4) | copy-start | bytes 2752516
  91.8 13.4 %collective-permute-start.9 = (bf16[2,64,1792]{2,1,0:T(8,128)(2,1)S(1)}, bf16[2,64,1792]{2,1,0:T(8,128)(2,1)S(1)}, u32[]{:S(2)}, u32[]{:S(2)}) collective-permute-start(bf16[2,64,1792]{2,1,0:T(8,128)(2,1)S(1)} %pad_maximum_fusion.5), channel_id=1, source_target_pairs={{0,4},{4,0},{8,12},{12,8},{1,5},{5,1},{9,13},{13,9},{2,6},{6,2},{1... | collective-permute-start | bytes 1376264 | tf_op jit(solution)/shard_map/ppermute | solution.py:91
  92.4 27.1 %collective-permute-start.5 = (bf16[2,64,1792]{2,1,0:T(8,128)(2,1)S(1)}, bf16[2,64,1792]{2,1,0:T(8,128)(2,1)S(1)}, u32[]{:S(2)}, u32[]{:S(2)}) collective-permute-start(bf16[2,64,1792]{2,1,0:T(8,128)(2,1)S(1)} %pad_maximum_fusion.4), channel_id=1, source_target_pairs={{0,4},{4,0},{8,12},{12,8},{1,5},{5,1},{9,13},{13,9},{2,6},{6,2},{1... | collective-permute-start | bytes 1376264 | tf_op jit(solution)/shard_map/ppermute | solution.py:91
  105.2 15.4 %collective-permute-start.10 = (bf16[64,1792]{1,0:T(8,128)(2,1)S(1)}, bf16[64,1792]{1,0:T(8,128)(2,1)S(1)}, u32[]{:S(2)}, u32[]{:S(2)}) collective-permute-start(bf16[64,1792]{1,0:T(8,128)(2,1)S(1)} %fusion.59), channel_id=1, source_target_pairs={{0,8},{4,12},{8,0},{12,4},{1,9},{5,13},{9,1},{13,5},{2,10},{6,14},... | collective-permute-start | bytes 688136 | tf_op jit(solution)/shard_map/ppermute | solution.py:91
  119.6 13.1 %collective-permute-start.6 = (bf16[64,1792]{1,0:T(8,128)(2,1)S(1)}, bf16[64,1792]{1,0:T(8,128)(2,1)S(1)}, u32[]{:S(2)}, u32[]{:S(2)}) collective-permute-start(bf16[64,1792]{1,0:T(8,128)(2,1)S(1)} %fusion.58), channel_id=1, source_target_pairs={{0,8},{4,12},{8,0},{12,4},{1,9},{5,13},{9,1},{13,5},{2,10},{6,14},... | collective-permute-start | bytes 688136 | tf_op jit(solution)/shard_map/ppermute | solution.py:91
  132.7 33.8 %copy-start.5 = (f32[1792]{0:T(1024)S(1)}, f32[1792]{0:T(1024)}, u32[]{:S(2)}) copy-start(f32[1792]{0:T(1024)} %param.18) | copy-start | bytes 21508
  134.1 17.6 %collective-permute-start.11 = (bf16[64,1792]{1,0:T(8,128)(2,1)S(1)}, bf16[64,1792]{1,0:T(8,128)(2,1)S(1)}, u32[]{:S(2)}, u32[]{:S(2)}) collective-permute-start(bf16[64,1792]{1,0:T(8,128)(2,1)S(1)} %get-tuple-element.36), channel_id=1, source_target_pairs={{0,8},{4,12},{8,0},{12,4},{1,9},{5,13},{9,1},{13,5},{2,10},{6,14},... | collective-permute-start | bytes 688136 | tf_op jit(solution)/shard_map/ppermute | solution.py:91
  134.2 22.4 %collective-permute-start.14 = (bf16[64,1792]{1,0:T(8,128)(2,1)S(1)}, bf16[64,1792]{1,0:T(8,128)(2,1)S(1)}, u32[]{:S(2)}, u32[]{:S(2)}) collective-permute-start(bf16[64,1792]{1,0:T(8,128)(2,1)S(1)} %get-tuple-element.35), channel_id=1, source_target_pairs={{0,8},{4,12},{8,0},{12,4},{1,9},{5,13},{9,1},{13,5},{2,10},{6,14},... | collective-permute-start | bytes 688136 | tf_op jit(solution)/shard_map/ppermute | solution.py:91
  151.8 14.7 %collective-permute-start.12 = (bf16[128,1792]{1,0:T(8,128)(2,1)S(1)}, bf16[128,1792]{1,0:T(8,128)(2,1)S(1)}, u32[]{:S(2)}, u32[]{:S(2)}) collective-permute-start(bf16[128,1792]{1,0:T(8,128)(2,1)S(1)} %pad_maximum_fusion.7), channel_id=1, source_target_pairs={{0,4},{4,0},{8,12},{12,8},{1,5},{5,1},{9,13},{13,9},{2,6},{6,2},{1... | collective-permute-start | bytes 1376264 | tf_op jit(solution)/shard_map/ppermute | solution.py:91
  156.7 19.6 %slice-start.1 = ((s8[9175040]{0:T(1024)(128)(4,1)}), s8[4194304]{0:T(1024)(128)(4,1)S(1)}, s32[]{:S(2)}) async-start(s8[9175040]{0:T(1024)(128)(4,1)} %bitcast.273), calls=%async_computation.1 | async-start | bytes 8388608
  156.7 19.5 %slice-start.2 = ((s8[9175040]{0:T(1024)(128)(4,1)}), s8[4194304]{0:T(1024)(128)(4,1)S(1)}, s32[]{:S(2)}) async-start(s8[9175040]{0:T(1024)(128)(4,1)} %bitcast.273), calls=%async_computation.2 | async-start | bytes 8388608
  156.7 19.5 %slice-start.3 = ((s8[9175040]{0:T(1024)(128)(4,1)}), s8[786432]{0:T(1024)(128)(4,1)S(1)}, s32[]{:S(2)}) async-start(s8[9175040]{0:T(1024)(128)(4,1)} %bitcast.273), calls=%async_computation.3 | async-start | bytes 1572864
  156.7 19.5 %collective-permute-start.15 = (bf16[128,1792]{1,0:T(8,128)(2,1)S(1)}, bf16[128,1792]{1,0:T(8,128)(2,1)S(1)}, u32[]{:S(2)}, u32[]{:S(2)}) collective-permute-start(bf16[128,1792]{1,0:T(8,128)(2,1)S(1)} %pad_maximum_fusion.8), channel_id=1, source_target_pairs={{0,4},{4,0},{8,12},{12,8},{1,5},{5,1},{9,13},{13,9},{2,6},{6,2},{1... | collective-permute-start | bytes 1376264 | tf_op jit(solution)/shard_map/ppermute | solution.py:91
  172.6 6.3 %slice-start.4 = ((s8[9175040]{0:T(1024)(128)(4,1)}), s8[4194304]{0:T(1024)(128)(4,1)S(1)}, s32[]{:S(2)}) async-start(s8[9175040]{0:T(1024)(128)(4,1)} %bitcast.275), calls=%async_computation.4 | async-start | bytes 8388608
  172.7 6.2 %slice-start.5 = ((s8[9175040]{0:T(1024)(128)(4,1)}), s8[4194304]{0:T(1024)(128)(4,1)S(1)}, s32[]{:S(2)}) async-start(s8[9175040]{0:T(1024)(128)(4,1)} %bitcast.275), calls=%async_computation.5 | async-start | bytes 8388608
  172.7 6.2 %slice-start.6 = ((s8[9175040]{0:T(1024)(128)(4,1)}), s8[786432]{0:T(1024)(128)(4,1)S(1)}, s32[]{:S(2)}) async-start(s8[9175040]{0:T(1024)(128)(4,1)} %bitcast.275), calls=%async_computation.6 | async-start | bytes 1572864
  172.7 44.0 %collective-permute-start.13 = (bf16[128,2560]{1,0:T(8,128)(2,1)S(1)}, bf16[128,2560]{1,0:T(8,128)(2,1)S(1)}, u32[]{:S(2)}, u32[]{:S(2)}) collective-permute-start(bf16[128,2560]{1,0:T(8,128)(2,1)S(1)} %dynamic-slice_bitcast_fusion.3), channel_id=1, source_target_pairs={{0,1},{1,0},{2,3},{3,2},{4,5},{5,4},{6,7},{7,6},{8,9},{9,8},{10,11... | collective-permute-start | bytes 1966088 | tf_op jit(solution)/shard_map/ppermute | solution.py:91
  178.8 6.5 %collective-permute-start.16 = (bf16[128,2560]{1,0:T(8,128)(2,1)S(1)}, bf16[128,2560]{1,0:T(8,128)(2,1)S(1)}, u32[]{:S(2)}, u32[]{:S(2)}) collective-permute-start(bf16[128,2560]{1,0:T(8,128)(2,1)S(1)} %dynamic-slice_bitcast_fusion.2), channel_id=1, source_target_pairs={{0,1},{1,0},{2,3},{3,2},{4,5},{5,4},{6,7},{7,6},{8,9},{9,8},{10,11... | collective-permute-start | bytes 1966088 | tf_op jit(solution)/shard_map/ppermute | solution.py:91
  181.6 35.2 %collective-permute-start.21 = (bf16[128,2560]{1,0:T(8,128)(2,1)S(1)}, bf16[128,2560]{1,0:T(8,128)(2,1)S(1)}, u32[]{:S(2)}, u32[]{:S(2)}) collective-permute-start(bf16[128,2560]{1,0:T(8,128)(2,1)S(1)} %dynamic-slice_bitcast_fusion.1), channel_id=1, source_target_pairs={{0,1},{1,0},{2,3},{3,2},{4,5},{5,4},{6,7},{7,6},{8,9},{9,8},{10,11... | collective-permute-start | bytes 1966088 | tf_op jit(solution)/shard_map/ppermute | solution.py:91
  184.9 2.2 collective-permute-start.22
  185.5 31.3 %collective-permute-start.17 = (bf16[128,2560]{1,0:T(8,128)(2,1)S(1)}, bf16[128,2560]{1,0:T(8,128)(2,1)S(1)}, u32[]{:S(2)}, u32[]{:S(2)}) collective-permute-start(bf16[128,2560]{1,0:T(8,128)(2,1)S(1)} %fusion.35), channel_id=1, source_target_pairs={{0,2},{1,3},{2,0},{3,1},{4,6},{5,7},{6,4},{7,5},{8,10},{9,11},{10,... | collective-permute-start | bytes 1966088 | tf_op jit(solution)/shard_map/ppermute | solution.py:91
  187.2 29.5 %collective-permute-start.23 = (bf16[128,2560]{1,0:T(8,128)(2,1)S(1)}, bf16[128,2560]{1,0:T(8,128)(2,1)S(1)}, u32[]{:S(2)}, u32[]{:S(2)}) collective-permute-start(bf16[128,2560]{1,0:T(8,128)(2,1)S(1)} %fusion.30), channel_id=1, source_target_pairs={{0,2},{1,3},{2,0},{3,1},{4,6},{5,7},{6,4},{7,5},{8,10},{9,11},{10,... | collective-permute-start | bytes 1966088 | tf_op jit(solution)/shard_map/ppermute | solution.py:91
  188.4 1.1 collective-permute-start.19
  189.6 1.1 collective-permute-start.18
  190.7 26.1 %collective-permute-start.20 = (f32[128]{0:T(128)S(1)}, f32[128]{0:T(128)S(1)}, u32[]{:S(2)}, u32[]{:S(2)}) collective-permute-start(f32[128]{0:T(128)S(1)} %fusion.86), channel_id=1, source_target_pairs={{0,2},{1,3},{2,0},{3,1},{4,6},{5,7},{6,4},{7,5},{8,10},{9,11},{10,... | collective-permute-start | bytes 1544 | tf_op jit(solution)/shard_map/ppermute | solution.py:91
  217.6 16.3 %collective-permute-start.24 = (bf16[128,2560]{1,0:T(8,128)(2,1)S(1)}, bf16[128,2560]{1,0:T(8,128)(2,1)S(1)}, u32[]{:S(2)}, u32[]{:S(2)}) collective-permute-start(bf16[128,2560]{1,0:T(8,128)(2,1)S(1)} %fusion.34), channel_id=1, source_target_pairs={{0,2},{1,3},{2,0},{3,1},{4,6},{5,7},{6,4},{7,5},{8,10},{9,11},{10,... | collective-permute-start | bytes 1966088 | tf_op jit(solution)/shard_map/ppermute | solution.py:91
  218.8 15.1 %collective-permute-start.28 = (bf16[128,2560]{1,0:T(8,128)(2,1)S(1)}, bf16[128,2560]{1,0:T(8,128)(2,1)S(1)}, u32[]{:S(2)}, u32[]{:S(2)}) collective-permute-start(bf16[128,2560]{1,0:T(8,128)(2,1)S(1)} %fusion.34), channel_id=1, source_target_pairs={{0,1},{1,0},{2,3},{3,2},{4,5},{5,4},{6,7},{7,6},{8,9},{9,8},{10,11... | collective-permute-start | bytes 1966088 | tf_op jit(solution)/shard_map/ppermute | solution.py:91
  233.9 6.3 %collective-permute-start.25 = (bf16[128,2560]{1,0:T(8,128)(2,1)S(1)}, bf16[128,2560]{1,0:T(8,128)(2,1)S(1)}, u32[]{:S(2)}, u32[]{:S(2)}) collective-permute-start(bf16[128,2560]{1,0:T(8,128)(2,1)S(1)} %collective-permute-done.24), channel_id=1, source_target_pairs={{0,1},{1,0},{2,3},{3,2},{4,5},{5,4},{6,7},{7,6},{8,9},{9,8},{10,11... | collective-permute-start | bytes 1966088 | tf_op jit(solution)/shard_map/ppermute | solution.py:91
  240.1 13.4 %collective-permute-start.29 = (bf16[2,64,1792]{2,1,0:T(8,128)(2,1)S(1)}, bf16[2,64,1792]{2,1,0:T(8,128)(2,1)S(1)}, u32[]{:S(2)}, u32[]{:S(2)}) collective-permute-start(bf16[2,64,1792]{2,1,0:T(8,128)(2,1)S(1)} %dynamic-slice_bitcast_fusion.4), channel_id=1, source_target_pairs={{0,4},{4,0},{8,12},{12,8},{1,5},{5,1},{9,13},{13,9},{2,6},{6,2},{1... | collective-permute-start | bytes 1376264 | tf_op jit(solution)/shard_map/ppermute | solution.py:91
  246.4 21.5 %collective-permute-start.26 = (bf16[2,64,1792]{2,1,0:T(8,128)(2,1)S(1)}, bf16[2,64,1792]{2,1,0:T(8,128)(2,1)S(1)}, u32[]{:S(2)}, u32[]{:S(2)}) collective-permute-start(bf16[2,64,1792]{2,1,0:T(8,128)(2,1)S(1)} %dynamic-slice_bitcast_fusion.5), channel_id=1, source_target_pairs={{0,4},{4,0},{8,12},{12,8},{1,5},{5,1},{9,13},{13,9},{2,6},{6,2},{1... | collective-permute-start | bytes 1376264 | tf_op jit(solution)/shard_map/ppermute | solution.py:91
  253.6 14.4 %collective-permute-start.30 = (bf16[64,1792]{1,0:T(8,128)(2,1)S(1)}, bf16[64,1792]{1,0:T(8,128)(2,1)S(1)}, u32[]{:S(2)}, u32[]{:S(2)}) collective-permute-start(bf16[64,1792]{1,0:T(8,128)(2,1)S(1)} %fusion.48), channel_id=1, source_target_pairs={{0,8},{4,12},{8,0},{12,4},{1,9},{5,13},{9,1},{13,5},{2,10},{6,14},... | collective-permute-start | bytes 688136 | tf_op jit(solution)/shard_map/ppermute | solution.py:91
  267.9 14.3 %copy-start.1 = (bf16[512,2048]{1,0:T(8,128)(2,1)S(1)}, bf16[512,2048]{1,0:T(8,128)(2,1)}, u32[]{:S(2)}) copy-start(bf16[512,2048]{1,0:T(8,128)(2,1)} %param.16) | copy-start | bytes 6291460
  267.9 12.3 %collective-permute-start.27 = (bf16[64,1792]{1,0:T(8,128)(2,1)S(1)}, bf16[64,1792]{1,0:T(8,128)(2,1)S(1)}, u32[]{:S(2)}, u32[]{:S(2)}) collective-permute-start(bf16[64,1792]{1,0:T(8,128)(2,1)S(1)} %fusion.52), channel_id=1, source_target_pairs={{0,8},{4,12},{8,0},{12,4},{1,9},{5,13},{9,1},{13,5},{2,10},{6,14},... | collective-permute-start | bytes 688136 | tf_op jit(solution)/shard_map/ppermute | solution.py:91

commit v2 on v1

--- a/solution.py
+++ b/solution.py
@@ -1,6 +1,10 @@
+import functools
+
 import jax
 import jax.numpy as jnp
 from jax import lax
+from jax.experimental import pallas as pl
+from jax.experimental.pallas import tpu as pltpu
 from jax.sharding import PartitionSpec as P
 
 D = 7168
@@ -46,44 +50,131 @@
     ).astype(jnp.bfloat16)
 
 
-def rope_queries(queries, positions, latent_width):
-    values = queries.astype(jnp.float32)
-    half_width = (values.shape[2] - latent_width) // 2
+def rope_tables(positions, half_width, lanes):
     angles = positions.astype(jnp.float32)[:, None] * rope_freqs(half_width)[None, :]
-    cosine = jnp.cos(angles)[:, None, :]
-    sine_value = jnp.sin(angles)[:, None, :]
-    first_half = values[:, :, latent_width : latent_width + half_width]
-    second_half = values[:, :, latent_width + half_width :]
-    return jnp.concatenate(
+    cosine, sine_value = jnp.cos(angles), jnp.sin(angles)
+    cos_part = jnp.concatenate([cosine, cosine], axis=1)
+    sin_part = jnp.concatenate([-sine_value, sine_value], axis=1)
+    rest = lanes - 2 * half_width
+    ones = jnp.ones((angles.shape[0], rest), jnp.float32)
+    zeros = jnp.zeros((angles.shape[0], rest), jnp.float32)
+    return jnp.stack(
         [
-            values[:, :, :latent_width],
-            first_half * cosine - second_half * sine_value,
-            first_half * sine_value + second_half * cosine,
+            jnp.concatenate([cos_part, ones], axis=1),
+            jnp.concatenate([sin_part, zeros], axis=1),
+            jnp.concatenate([ones, cos_part], axis=1),
+            jnp.concatenate([zeros, sin_part], axis=1),
+        ]
+    )
+
+
+def attention_kernel(
+    group, tables, starts, own_index, key_index, keys, queries, value_weight, out, even, odd, values, bias
+):
+    row_count = queries.shape[0]
+    width = queries.shape[1] // group
+    half_width = (width - LAT) // 2
+    lanes = 2 * (width - LAT)
+
+    @pl.when(pl.program_id(0) == 0)
+    def prepare():
+        all_keys = keys[...]
+        pad = jnp.zeros((width - LAT, all_keys.shape[1]), jnp.bfloat16)
+        even[:width] = all_keys
+        even[width:] = pad
+        odd[: width - LAT] = pad
+        odd[width - LAT :] = all_keys
+        values[...] = keys[:LAT].astype(jnp.float32).T.astype(jnp.bfloat16)
+        allowed = (key_index[...] >= starts[...]) & (key_index[...] <= own_index[...])
+        bias[...] = jnp.where(allowed, 0.0, masked_score)
+
+    lane = lax.broadcasted_iota(jnp.int32, (row_count, lanes), 1)
+    low = (lane & (2 * half_width - 1)) < half_width
+
+    def turned(start, which):
+        entry = queries[:, start : start + lanes].astype(jnp.float32)
+        partner = jnp.where(
+            low, pltpu.roll(entry, lanes - half_width, 1), pltpu.roll(entry, half_width, 1)
+        )
+        return (entry * tables[2 * which] + partner * tables[2 * which + 1]).astype(jnp.bfloat16)
+
+    for which, key_rows in ((0, even), (1, odd)):
+        rows = []
+        for head in range(which, group, 2):
+            base = (head - which) * width
+            if which == 0:
+                rows.append(
+                    jnp.concatenate([queries[:, base : base + LAT], turned(base + LAT, 0)], axis=1)
+                )
+            else:
+                first = base + LAT
+                rows.append(
+                    jnp.concatenate(
+                        [queries[:, first : first + LAT], turned(first + LAT, 1)], axis=1
+                    )
+                )
+        stacked = jnp.concatenate(rows, axis=0)
+        scores = jnp.dot(stacked, key_rows[...], preferred_element_type=jnp.float32)
+        scores = scores.reshape(len(rows), row_count, -1) + bias[...][None]
+        top = jnp.max(scores, axis=2, keepdims=True)
+        exponent = jnp.exp((scores - top) * score_scale)
+        total = jnp.sum(exponent, axis=2, keepdims=True).reshape(len(rows) * row_count, 1)
+        weights = exponent.astype(jnp.bfloat16).reshape(len(rows) * row_count, -1)
+        mixed = jnp.dot(weights, values[...], preferred_element_type=jnp.float32)
+        mixed = (mixed / total).astype(jnp.bfloat16)
+        for i in range(len(rows)):
+            head = 2 * i + which
+            out[:, head * VHEAD : (head + 1) * VHEAD] = jnp.dot(
+                mixed[i * row_count : (i + 1) * row_count],
+                value_weight[:, head * VHEAD : (head + 1) * VHEAD],
+                preferred_element_type=jnp.float32,
+            ).astype(jnp.bfloat16)
+
+
+def attention(queries, keys, key_index, own_index, own_position, value_weight):
+    row_count, query_width = queries.shape
+    local_heads = value_weight.shape[1] // VHEAD
+    width = query_width // local_heads
+    group = 4 if local_heads % 4 == 0 else 2
+    key_count = keys.shape[1]
+    tables = rope_tables(own_position, (width - LAT) // 2, 2 * (width - LAT))
+    whole = lambda shape: pl.BlockSpec(shape, lambda i: (0,) * len(shape))
+    deep = 2 * width - LAT
+    return pl.pallas_call(
+        functools.partial(attention_kernel, group),
+        grid=(local_heads // group,),
+        in_specs=[
+            whole(tables.shape),
+            whole((row_count, 1)),
+            whole((row_count, 1)),
+            whole((1, key_count)),
+            whole(keys.shape),
+            pl.BlockSpec((row_count, group * width), lambda i: (0, i)),
+            pl.BlockSpec((LAT, group * VHEAD), lambda i: (0, i)),
         ],
-        axis=2,
-    ).astype(jnp.bfloat16)
-
-
-def score_rows(state_carry, query_block, block_index, block_trace, key_piece, key_index, key_trace):
-    row_top, row_total, mixed_sum = state_carry
-    allowed = (key_trace[None, :] == block_trace[:, None]) & (
-        key_index[None, :] <= block_index[:, None]
-    )
-    scores = (
-        jnp.einsum("qhe,ek->hqk", query_block, key_piece, preferred_element_type=jnp.float32)
-        * score_scale
-    )
-    scores = jnp.where(allowed[None], scores, masked_score)
-    new_top = jnp.maximum(row_top, jnp.max(scores, axis=2))
-    exponent = jnp.where(allowed[None], jnp.exp(scores - new_top[:, :, None]), 0.0)
-    row_total = jnp.sum(exponent, axis=2)
-    mixed_sum = jnp.einsum(
-        "hqk,lk->hql",
-        exponent.astype(jnp.bfloat16),
-        key_piece[:LAT],
-        preferred_element_type=jnp.float32,
-    )
-    return (new_top, row_total, mixed_sum)
+        out_specs=pl.BlockSpec((row_count, group * VHEAD), lambda i: (0, i)),
+        out_shape=jax.ShapeDtypeStruct((row_count, local_heads * VHEAD), jnp.bfloat16),
+        scratch_shapes=[
+            pltpu.VMEM((deep, key_count), jnp.bfloat16),
+            pltpu.VMEM((deep, key_count), jnp.bfloat16),
+            pltpu.VMEM((key_count, LAT), jnp.bfloat16),
+            pltpu.VMEM((row_count, key_count), jnp.float32),
+        ],
+        compiler_params=pltpu.CompilerParams(vmem_limit_bytes=40 * 1024 * 1024),
+        cost_estimate=pl.CostEstimate(
+            flops=2 * row_count * local_heads * (key_count * (deep + LAT) + LAT * VHEAD),
+            bytes_accessed=2 * (queries.size + keys.size + value_weight.size),
+            transcendentals=row_count * local_heads * key_count,
+        ),
+    )(
+        tables,
+        (own_index - own_position)[:, None],
+        own_index[:, None],
+        key_index[None, :],
+        keys,
+        queries,
+        value_weight,
+    )
 
 
 def swap(value, axis_name, bit):
@@ -101,6 +192,22 @@
 
 def matmul(a, b):
     return jnp.dot(a, b, preferred_element_type=jnp.float32).astype(jnp.bfloat16)
+
+
+def gather_keys(rotated_keys, n_ctx):
+    rows = rotated_keys.shape[0] // 2
+    core = lax.axis_index("tp") & 1
+    half = lax.dynamic_slice_in_dim(rotated_keys, core * rows, rows, 0)
+    came = [
+        lax.ppermute(half, "ctx", [(c, c + d) for c in range(n_ctx - d)])
+        for d in range(n_ctx - 1, 0, -1)
+    ]
+    mine = jnp.concatenate(came, axis=1)
+    other = swap(mine, "tp", 1)
+    before = jnp.concatenate(
+        [jnp.where(core == 0, mine, other), jnp.where(core == 0, other, mine)], axis=0
+    )
+    return jnp.concatenate([before, rotated_keys], axis=1)
 
 
 def spread_heads(heads_out, n_ctx, n_tp):
@@ -219,44 +326,20 @@
 ):
     row_count = residual.shape[0]
     ctx_place = lax.axis_index("ctx")
-    local_heads = value_weight.shape[1] // VHEAD
+    n_ctx, n_tp = lax.axis_size("ctx"), lax.axis_size("tp")
+    paired = n_ctx == 4 and n_tp == 4 and row_count % 64 == 0
     own_index = ctx_place * row_count + jnp.arange(row_count, dtype=jnp.int32)
-    own_trace, own_position = trace_info(own_index, lengths)
+    _, own_position = trace_info(own_index, lengths)
     rotated_keys = rope_keys(latent, own_position, LAT)
-    rotated_queries = rope_queries(
-        queries.reshape(row_count, local_heads, LAT + ROPE), own_position, LAT
-    )
-    last_query = ctx_place * row_count + row_count - 1
-    start_state = (
-        jnp.full((local_heads, row_count), masked_score, jnp.float32),
-        jnp.zeros((local_heads, row_count), jnp.float32),
-        jnp.zeros((local_heads, row_count, LAT), jnp.float32),
-    )
-    key_piece = lax.all_gather(rotated_keys, "ctx", axis=1, tiled=True)
-    key_index = jnp.arange(key_piece.shape[1], dtype=jnp.int32)
-    key_trace, _ = trace_info(key_index, lengths)
-    folded = lax.cond(
-        jnp.int32(0) <= last_query,
-        lambda held: score_rows(
-            held, rotated_queries, own_index, own_trace, key_piece, key_index, key_trace
-        ),
-        lambda held: held,
-        start_state,
-    )
-    row_top, row_total, mixed_sum = folded
-    mixed_latent = (mixed_sum / row_total[:, :, None]).astype(jnp.bfloat16)
-    heads_out = (
-        jnp.einsum(
-            "hql,lhd->qhd",
-            mixed_latent,
-            value_weight.reshape(LAT, local_heads, VHEAD),
-            preferred_element_type=jnp.float32,
-        )
-        .astype(jnp.bfloat16)
-        .reshape(row_count, local_heads * VHEAD)
-    )
-    n_ctx, n_tp = lax.axis_size("ctx"), lax.axis_size("tp")
-    if n_ctx == 4 and n_tp == 4 and row_count % 64 == 0:
+    key_order = jnp.arange(n_ctx * row_count, dtype=jnp.int32)
+    if paired:
+        keys = gather_keys(rotated_keys, n_ctx)
+        key_index = key_order + (ctx_place - (n_ctx - 1)) * row_count
+    else:
+        keys = lax.all_gather(rotated_keys, "ctx", axis=1, tiled=True)
+        key_index = key_order
+    heads_out = attention(queries, keys, key_index, own_index, own_position, value_weight)
+    if paired:
         return paired_tail(
             heads_out,
             residual,

time: 283 us -> 259 us (0.915)
  blocking collectives: 18 us -> 0 us
  starting transfers between devices: 28 us -> 38.9 us
  matrix products: 43.7 us -> 33.6 us
  Pallas kernels: 0 us -> 6.63 us
  other arithmetic: 16.2 us -> 9.98 us
  local copies, waits for them, and re-layouts: 6.69 us -> 2.6 us
    all_gather x1 -> x0, blocking collectives: 18 us -> none  [on_device(): key_piece = lax.all_gather(rotated_keys, 'ctx', axis=1, tiled=True)]
    ppermute x0 -> x3, starting transfers between devices: none -> 10.7 us  [gather_keys(): lax.ppermute(half, 'ctx', [(c, c + d) for c in range(n_ctx - d)])]
    dot_general x3 -> x0, matrix products: 10.2 us -> none  [the longest x1 3.7 us: score_rows(): jnp.einsum('qhe,ek->hqk', query_block, key_piece, preferred_element_type=...]
    pallas_call x0 -> x1, Pallas kernels: none -> 6.63 us  [attention(): pl.pallas_call(functools.partial(attention_kernel, group), grid=(local_he...]
    convert_element_type x3 -> x0, other arithmetic: 4.5 us -> none  [the longest x1 4.42 us: rope_queries(): values = queries.astype(jnp.float32)]
    ppermute x27 -> x28, waiting for transfers between devices: 154 us -> 150 us  [swap(): return lax.ppermute(value, axis_name, [(i, i ^ bit) for i in range(width)])]
    unnamed x46 -> x42, local copies, waits for them, and re-layouts: 4.68 us -> 0.95 us
    concatenate x1, other arithmetic: 3.24 us -> 0.06 us  [gather_keys(): return jnp.concatenate([before, rotated_keys], axis=1)]
  transfers between devices with their start and end apart: 31 -> 35, of which waited for: 18 -> 20; matrix products, arithmetic and copies ran while one was open for 12% -> 14% of each run, Pallas kernels for 0% -> 0%
where the time goes in v2:
time: 259 us
  waiting for transfers between devices  166 us (64%)
  starting transfers between devices  38.9 us (15%)
  matrix products  33.6 us (13%)
  other arithmetic  9.98 us (4%)
  Pallas kernels  6.63 us (3%)
  local copies, waits for them, and re-layouts  2.6 us (1%)
    ppermute x28, waiting for transfers between devices, swap(): return lax.ppermute(value, axis_name, [(i, i ^ bit) for i in range(width)])  150 us
    dot_general x8, matrix products, matmul(): jnp.dot(a, b, preferred_element_type=jnp.float32).astype(jnp.bfloat16)  33.6 us
    ppermute x28, starting transfers between devices, swap(): return lax.ppermute(value, axis_name, [(i, i ^ bit) for i in range(width)])  20.7 us
    ppermute x4, waiting for transfers between devices, spread_heads(): lax.ppermute(pieces[s], ('ctx', 'tp'), [(c * n_tp + t, t * n_tp + (c ^ s)...  14.8 us
    ppermute x3, starting transfers between devices, gather_keys(): lax.ppermute(half, 'ctx', [(c, c + d) for c in range(n_ctx - d)])  10.7 us
    ppermute x4, starting transfers between devices, spread_heads(): lax.ppermute(pieces[s], ('ctx', 'tp'), [(c * n_tp + t, t * n_tp + (c ^ s)...  7.45 us
    pallas_call x1, Pallas kernels, attention(): pl.pallas_call(functools.partial(attention_kernel, group), grid=(local_he...  6.63 us
  transfers between devices with their start and end apart: 35, of which 20 were waited for; matrix products, arithmetic and copies ran while one was open for 14% of the time, Pallas kernels for 0%

profile of v2, /device:TPU:0, one launch (start us, length us, event | category | flops | bytes accessed | tf_op | source)
XLA Modules:
  0.0 258.7 jit_solution(2453094467089379805)
XLA Ops:
  0.6 0.9 convert_element_type.250
  1.6 1.1 slice.102
  2.7 0.8 reduce-window.8
  3.5 0.7 subtract_subtract_fusion
  4.5 0.3 fusion.47
  4.8 7.0 %collective-permute-start = (bf16[288,128]{1,0:T(8,128)(2,1)S(1)}, bf16[288,128]{1,0:T(8,128)(2,1)S(1)}, u32[]{:S(2)}, u32[]{:S(2)}) collective-permute-start(bf16[288,128]{1,0:T(8,128)(2,1)S(1)} %fusion.47), channel_id=1, source_target_pairs={{0,12},{1,13},{2,14},{3,15},{16,28},{17,29},{18,30},{19,31}} | collective-permute-start | bytes 221192 | tf_op jit(solution)/shard_map/ppermute | solution.py:202
  11.8 1.3 collective-permute-start.1
  13.1 2.5 collective-permute-start.2
  15.6 0.3 multiply_cosine_fusion
  16.3 1.2 collective-permute-done.2
  17.7 1.4 collective-permute-done.3
  19.2 6.6 %shard_map.113 = bf16[128,2048]{1,0:T(8,128)(2,1)S(1)} custom-call(f32[4,128,128]{2,1,0:T(8,128)S(1)} %pad_maximum_fusion.9.tables, s32[128,1]{1,0:T(8,128)S(1)} %copy.13.starts, s32[128,1]{1,0:T(8,128)S(1)} %iota_add_fusion.own_index, s32[1,512]{1,0:T(1,128)S(1)} %iota_add_fusion.1.key_index, bf16[576,512]{1,0:T(8,128)(2,1)S(1)} %maximum_maximum_fusion.keys, ...), custom_call_target="tpu_custom_call" | custom-call | flops 2684354560 | bytes 5046272 | tf_op jit(solution)/shard_map/pallas_call | solution.py:143
  26.1 5.0 %collective-permute-start.6 = (bf16[32,2048]{1,0:T(8,128)(2,1)S(1)}, bf16[32,2048]{1,0:T(8,128)(2,1)S(1)}, u32[]{:S(2)}, u32[]{:S(2)}) collective-permute-start(bf16[32,2048]{1,0:T(8,128)(2,1)S(1)} %get-tuple-element.14), channel_id=1, source_target_pairs={{0,2},{1,6},{2,10},{3,14},{4,3},{5,7},{6,11},{7,15},{8,0},{9,4},{1... | collective-permute-start | bytes 393224 | tf_op jit(solution)/shard_map/ppermute | solution.py:216
  31.1 1.5 collective-permute-start.7
  32.5 0.8 collective-permute-start.4
  33.4 14.8 %collective-permute-done.6 = bf16[32,2048]{1,0:T(8,128)(2,1)S(1)} collective-permute-done((bf16[32,2048]{1,0:T(8,128)(2,1)S(1)}, bf16[32,2048]{1,0:T(8,128)(2,1)S(1)}, u32[]{:S(2)}, u32[]{:S(2)}) %collective-permute-start.6) | collective-permute-done | bytes 131104 | tf_op jit(solution)/shard_map/ppermute | solution.py:216
  48.3 2.7 %collective-permute-start.8 = (bf16[4,32,2048]{2,1,0:T(8,128)(2,1)S(1)}, bf16[4,32,2048]{2,1,0:T(8,128)(2,1)S(1)}, u32[]{:S(2)}, u32[]{:S(2)}) collective-permute-start(bf16[4,32,2048]{2,1,0:T(8,128)(2,1)S(1)} %pad_maximum_fusion.2), channel_id=1, source_target_pairs={{0,1},{1,0},{2,3},{3,2},{4,5},{5,4},{6,7},{7,6},{8,9},{9,8},{10,11... | collective-permute-start | bytes 1572872 | tf_op jit(solution)/shard_map/ppermute | solution.py:182
  51.0 4.5 %collective-permute-start.11 = (bf16[4,32,2048]{2,1,0:T(8,128)(2,1)S(1)}, bf16[4,32,2048]{2,1,0:T(8,128)(2,1)S(1)}, u32[]{:S(2)}, u32[]{:S(2)}) collective-permute-start(bf16[4,32,2048]{2,1,0:T(8,128)(2,1)S(1)} %pad_maximum_fusion.2), channel_id=1, source_target_pairs={{0,2},{1,3},{2,0},{3,1},{4,6},{5,7},{6,4},{7,5},{8,10},{9,11},{10,... | collective-permute-start | bytes 1572872 | tf_op jit(solution)/shard_map/ppermute | solution.py:182
  55.7 5.3 %convolution_convert_fusion.5 = bf16[256,1792]{1,0:T(8,128)(2,1)S(1)} fusion(bf16[256,2048]{1,0:T(8,128)(2,1)S(1)} %constant_dynamic-update-slice_fusion.3, bf16[2048,1792]{1,0:T(8,128)(2,1)} %param.15), kind=kOutput, calls=%fused_computation.5 | convolution fusion | flops 1879506944 | bytes 9306112 | tf_op jit(solution)/shard_map/dot_general | solution.py:194
  61.0 7.0 %collective-permute-done.11 = bf16[4,32,2048]{2,1,0:T(8,128)(2,1)S(1)} collective-permute-done((bf16[4,32,2048]{2,1,0:T(8,128)(2,1)S(1)}, bf16[4,32,2048]{2,1,0:T(8,128)(2,1)S(1)}, u32[]{:S(2)}, u32[]{:S(2)}) %collective-permute-start.11) | collective-permute-done | bytes 524320 | tf_op jit(solution)/shard_map/ppermute | solution.py:182
  68.0 0.7 collective-permute-start.9
  68.8 1.2 collective-permute-done.12
  70.1 2.1 convolution_convert_fusion.4
  72.3 0.7 collective-permute-start.13
  73.0 8.5 %collective-permute-done.9 = bf16[2,64,1792]{2,1,0:T(8,128)(2,1)S(1)} collective-permute-done((bf16[2,64,1792]{2,1,0:T(8,128)(2,1)S(1)}, bf16[2,64,1792]{2,1,0:T(8,128)(2,1)S(1)}, u32[]{:S(2)}, u32[]{:S(2)}) %collective-permute-start.9) | collective-permute-done | bytes 458784 | tf_op jit(solution)/shard_map/ppermute | solution.py:182
  81.4 0.7 fusion.32
  82.2 1.8 collective-permute-start.10
  84.0 11.8 %collective-permute-done.13 = bf16[2,64,1792]{2,1,0:T(8,128)(2,1)S(1)} collective-permute-done((bf16[2,64,1792]{2,1,0:T(8,128)(2,1)S(1)}, bf16[2,64,1792]{2,1,0:T(8,128)(2,1)S(1)}, u32[]{:S(2)}, u32[]{:S(2)}) %collective-permute-start.13) | collective-permute-done | bytes 458784 | tf_op jit(solution)/shard_map/ppermute | solution.py:182
  96.0 12.3 %collective-permute-done.14 = bf16[64,1792]{1,0:T(8,128)(2,1)S(1)} collective-permute-done((bf16[64,1792]{1,0:T(8,128)(2,1)S(1)}, bf16[64,1792]{1,0:T(8,128)(2,1)S(1)}, u32[]{:S(2)}, u32[]{:S(2)}) %collective-permute-start.14) | collective-permute-done | bytes 229408 | tf_op jit(solution)/shard_map/ppermute | solution.py:182
  108.3 0.7 copy-done.3
  109.0 1.5 broadcast_select_fusion.3
  110.6 2.9 %collective-permute-start.18 = (bf16[64,1792]{1,0:T(8,128)(2,1)S(1)}, bf16[64,1792]{1,0:T(8,128)(2,1)S(1)}, u32[]{:S(2)}, u32[]{:S(2)}) collective-permute-start(bf16[64,1792]{1,0:T(8,128)(2,1)S(1)} %get-tuple-element.6), channel_id=1, source_target_pairs={{0,8},{4,12},{8,0},{12,4},{1,9},{5,13},{9,1},{13,5},{2,10},{6,14},... | collective-permute-start | bytes 688136 | tf_op jit(solution)/shard_map/ppermute | solution.py:182
  113.5 14.6 %collective-permute-done.15 = bf16[64,1792]{1,0:T(8,128)(2,1)S(1)} collective-permute-done((bf16[64,1792]{1,0:T(8,128)(2,1)S(1)}, bf16[64,1792]{1,0:T(8,128)(2,1)S(1)}, u32[]{:S(2)}, u32[]{:S(2)}) %collective-permute-start.15) | collective-permute-done | bytes 229408 | tf_op jit(solution)/shard_map/ppermute | solution.py:182
  128.3 4.8 %collective-permute-done.18 = bf16[64,1792]{1,0:T(8,128)(2,1)S(1)} collective-permute-done((bf16[64,1792]{1,0:T(8,128)(2,1)S(1)}, bf16[64,1792]{1,0:T(8,128)(2,1)S(1)}, u32[]{:S(2)}, u32[]{:S(2)}) %collective-permute-start.18) | collective-permute-done | bytes 229408 | tf_op jit(solution)/shard_map/ppermute | solution.py:182
  133.2 9.7 %collective-permute-done.16 = bf16[128,1792]{1,0:T(8,128)(2,1)S(1)} collective-permute-done((bf16[128,1792]{1,0:T(8,128)(2,1)S(1)}, bf16[128,1792]{1,0:T(8,128)(2,1)S(1)}, u32[]{:S(2)}, u32[]{:S(2)}) %collective-permute-start.16) | collective-permute-done | bytes 458784 | tf_op jit(solution)/shard_map/ppermute | solution.py:182
  142.9 6.1 %convolution_convert_fusion.3 = bf16[256,2560]{1,0:T(8,128)(2,1)S(1)} fusion(bf16[1792,2560]{1,0:T(8,128)(2,1)} %param.17, f32[1792]{0:T(1024)S(1)} %copy-done.4, bf16[128,1792]{1,0:T(8,128)(2,1)S(1)} %collective-permute-done.16, bf16[64,1792]{1,0:T(8,128)(2,1)S(1)} %collective-permute-done.15, bf16[64,1792]{1,0:T(8,128)(2,1)S(1)} %get-tuple-element.7), kind=kOutput, calls=%fused_computation.3 | convolution fusion | flops 2353135616 | bytes 11410432 | tf_op jit(solution)/shard_map/dot_general | solution.py:194
  149.2 3.4 %collective-permute-done.19 = bf16[128,1792]{1,0:T(8,128)(2,1)S(1)} collective-permute-done((bf16[128,1792]{1,0:T(8,128)(2,1)S(1)}, bf16[128,1792]{1,0:T(8,128)(2,1)S(1)}, u32[]{:S(2)}, u32[]{:S(2)}) %collective-permute-start.19) | collective-permute-done | bytes 458784 | tf_op jit(solution)/shard_map/ppermute | solution.py:182
  152.7 2.5 convolution_convert_fusion.2
  155.4 2.5 convolution_convert_fusion.1
  158.0 0.5 collective-permute-start.25
  158.5 2.7 %convolution_convert_fusion = bf16[256,2560]{1,0:T(8,128)(2,1)S(1)} fusion(bf16[1792,2560]{1,0:T(8,128)(2,1)S(1)} %bitcast.224, f32[1792]{0:T(1024)S(1)} %copy-done.4, bf16[128,1792]{1,0:T(8,128)(2,1)S(1)} %collective-permute-done.19, bf16[64,1792]{1,0:T(8,128)(2,1)S(1)} %collective-permute-done.18, bf16[64,1792]{1,0:T(8,128)(2,1)S(1)} %get-tuple-element.6), kind=kOutput, calls=%fused_computation | convolution fusion | flops 2353135616 | bytes 11410432 | tf_op jit(solution)/shard_map/dot_general | solution.py:194
  161.4 0.3 fusion.3
  161.9 0.5 collective-permute-start.21
  162.3 1.2 collective-permute-done.26
  163.6 0.5 collective-permute-start.27
  164.2 0.3 fusion.1
  164.5 0.8 collective-permute-done.23
  165.3 0.2 collective-permute-start.22
  165.5 0.9 collective-permute-done.22
  166.4 1.6 collective-permute-start.24
  168.0 25.2 %collective-permute-done.24 = f32[128]{0:T(128)S(1)} collective-permute-done((f32[128]{0:T(128)S(1)}, f32[128]{0:T(128)S(1)}, u32[]{:S(2)}, u32[]{:S(2)}) %collective-permute-start.24) | collective-permute-done | bytes 544 | tf_op jit(solution)/shard_map/ppermute | solution.py:182
  193.2 0.8 fusion.14
  194.0 0.5 collective-permute-start.28
  194.5 15.9 %collective-permute-done.28 = bf16[128,2560]{1,0:T(8,128)(2,1)S(1)} collective-permute-done((bf16[128,2560]{1,0:T(8,128)(2,1)S(1)}, bf16[128,2560]{1,0:T(8,128)(2,1)S(1)}, u32[]{:S(2)}, u32[]{:S(2)}) %collective-permute-start.28) | collective-permute-done | bytes 655392 | tf_op jit(solution)/shard_map/ppermute | solution.py:182
  210.3 6.1 %convolution_convert_fusion.6 = bf16[256,1792]{1,0:T(8,128)(2,1)S(1)} fusion(bf16[2560,1792]{1,0:T(8,128)(2,1)} %param.19, bf16[128,2560]{1,0:T(8,128)(2,1)S(1)} %collective-permute-done.32, bf16[128,2560]{1,0:T(8,128)(2,1)S(1)} %fusion.14), kind=kOutput, calls=%fused_computation.6 | convolution fusion | flops 2351890432 | bytes 11403264 | tf_op jit(solution)/shard_map/dot_general | solution.py:194
  216.6 6.1 %convolution_convert_fusion.7 = bf16[256,1792]{1,0:T(8,128)(2,1)S(1)} fusion(bf16[2560,1792]{1,0:T(8,128)(2,1)} %param.19, bf16[128,2560]{1,0:T(8,128)(2,1)S(1)} %collective-permute-done.29, bf16[128,2560]{1,0:T(8,128)(2,1)S(1)} %collective-permute-done.28), kind=kOutput, calls=%fused_computation.7 | convolution fusion | flops 2351890432 | bytes 11403264 | tf_op jit(solution)/shard_map/dot_general | solution.py:194
  222.8 2.1 collective-permute-start.30
  224.9 5.0 %collective-permute-done.33 = bf16[2,64,1792]{2,1,0:T(8,128)(2,1)S(1)} collective-permute-done((bf16[2,64,1792]{2,1,0:T(8,128)(2,1)S(1)}, bf16[2,64,1792]{2,1,0:T(8,128)(2,1)S(1)}, u32[]{:S(2)}, u32[]{:S(2)}) %collective-permute-start.33) | collective-permute-done | bytes 458784 | tf_op jit(solution)/shard_map/ppermute | solution.py:182
  230.0 0.7 collective-permute-start.34
  230.6 13.6 %collective-permute-done.30 = bf16[2,64,1792]{2,1,0:T(8,128)(2,1)S(1)} collective-permute-done((bf16[2,64,1792]{2,1,0:T(8,128)(2,1)S(1)}, bf16[2,64,1792]{2,1,0:T(8,128)(2,1)S(1)}, u32[]{:S(2)}, u32[]{:S(2)}) %collective-permute-start.30) | collective-permute-done | bytes 458784 | tf_op jit(solution)/shard_map/ppermute | solution.py:182
  244.5 12.3 %collective-permute-done.31 = bf16[64,1792]{1,0:T(8,128)(2,1)S(1)} collective-permute-done((bf16[64,1792]{1,0:T(8,128)(2,1)S(1)}, bf16[64,1792]{1,0:T(8,128)(2,1)S(1)}, u32[]{:S(2)}, u32[]{:S(2)}) %collective-permute-start.31) | collective-permute-done | bytes 229408 | tf_op jit(solution)/shard_map/ppermute | solution.py:182
  256.8 0.3 broadcast_select_fusion.1
  257.1 0.8 pad_maximum_fusion.8
  257.9 0.8 pad_maximum_fusion.5
  (116 shorter events, 3.4 us)
Async XLA Ops:
  1.6 17.6 %copy-start.1 = (bf16[512,2048]{1,0:T(8,128)(2,1)S(1)}, bf16[512,2048]{1,0:T(8,128)(2,1)}, u32[]{:S(2)}) copy-start(bf16[512,2048]{1,0:T(8,128)(2,1)} %value_weight.1) | copy-start | bytes 6291460
  4.8 11.4 %collective-permute-start = (bf16[288,128]{1,0:T(8,128)(2,1)S(1)}, bf16[288,128]{1,0:T(8,128)(2,1)S(1)}, u32[]{:S(2)}, u32[]{:S(2)}) collective-permute-start(bf16[288,128]{1,0:T(8,128)(2,1)S(1)} %fusion.47), channel_id=1, source_target_pairs={{0,12},{1,13},{2,14},{3,15},{16,28},{17,29},{18,30},{19,31}} | collective-permute-start | bytes 221192 | tf_op jit(solution)/shard_map/ppermute | solution.py:202
  11.8 4.5 %collective-permute-start.1 = (bf16[288,128]{1,0:T(8,128)(2,1)S(1)}, bf16[288,128]{1,0:T(8,128)(2,1)S(1)}, u32[]{:S(2)}, u32[]{:S(2)}) collective-permute-start(bf16[288,128]{1,0:T(8,128)(2,1)S(1)} %fusion.47), channel_id=1, source_target_pairs={{0,8},{4,12},{1,9},{5,13},{2,10},{6,14},{3,11},{7,15},{16,24},{20,... | collective-permute-start | bytes 221192 | tf_op jit(solution)/shard_map/ppermute | solution.py:202
  13.1 4.4 %collective-permute-start.2 = (bf16[288,128]{1,0:T(8,128)(2,1)S(1)}, bf16[288,128]{1,0:T(8,128)(2,1)S(1)}, u32[]{:S(2)}, u32[]{:S(2)}) collective-permute-start(bf16[288,128]{1,0:T(8,128)(2,1)S(1)} %fusion.47), channel_id=1, source_target_pairs={{0,4},{4,8},{8,12},{1,5},{5,9},{9,13},{2,6},{6,10},{10,14},{3,7},{... | collective-permute-start | bytes 221192 | tf_op jit(solution)/shard_map/ppermute | solution.py:202
  16.0 3.2 %copy-start = (bf16[128,9216]{1,0:T(8,128)(2,1)S(1)}, bf16[128,9216]{1,0:T(8,128)(2,1)}, u32[]{:S(2)}) copy-start(bf16[128,9216]{1,0:T(8,128)(2,1)} %queries.1) | copy-start | bytes 7077892
  17.6 1.5 collective-permute-start.3
  25.9 7.5 %collective-permute-start.5 = (bf16[32,2048]{1,0:T(8,128)(2,1)S(1)}, bf16[32,2048]{1,0:T(8,128)(2,1)S(1)}, u32[]{:S(2)}, u32[]{:S(2)}) collective-permute-start(bf16[32,2048]{1,0:T(8,128)(2,1)S(1)} %get-tuple-element.12), channel_id=1, source_target_pairs={{0,1},{1,5},{2,9},{3,13},{4,0},{5,4},{6,8},{7,12},{8,3},{9,7},{10,... | collective-permute-start | bytes 393224 | tf_op jit(solution)/shard_map/ppermute | solution.py:216
  26.1 22.1 %collective-permute-start.6 = (bf16[32,2048]{1,0:T(8,128)(2,1)S(1)}, bf16[32,2048]{1,0:T(8,128)(2,1)S(1)}, u32[]{:S(2)}, u32[]{:S(2)}) collective-permute-start(bf16[32,2048]{1,0:T(8,128)(2,1)S(1)} %get-tuple-element.14), channel_id=1, source_target_pairs={{0,2},{1,6},{2,10},{3,14},{4,3},{5,7},{6,11},{7,15},{8,0},{9,4},{1... | collective-permute-start | bytes 393224 | tf_op jit(solution)/shard_map/ppermute | solution.py:216
  31.1 17.1 %collective-permute-start.7 = (bf16[32,2048]{1,0:T(8,128)(2,1)S(1)}, bf16[32,2048]{1,0:T(8,128)(2,1)S(1)}, u32[]{:S(2)}, u32[]{:S(2)}) collective-permute-start(bf16[32,2048]{1,0:T(8,128)(2,1)S(1)} %get-tuple-element.13), channel_id=1, source_target_pairs={{0,3},{1,7},{2,11},{3,15},{4,2},{5,6},{6,10},{7,14},{8,1},{9,5},{1... | collective-permute-start | bytes 393224 | tf_op jit(solution)/shard_map/ppermute | solution.py:216
  32.5 15.7 %collective-permute-start.4 = (bf16[32,2048]{1,0:T(8,128)(2,1)S(1)}, bf16[32,2048]{1,0:T(8,128)(2,1)S(1)}, u32[]{:S(2)}, u32[]{:S(2)}) collective-permute-start(bf16[32,2048]{1,0:T(8,128)(2,1)S(1)} %get-tuple-element.15), channel_id=1, source_target_pairs={{0,0},{1,4},{2,8},{3,12},{4,1},{5,5},{6,9},{7,13},{8,2},{9,6},{10,... | collective-permute-start | bytes 393224 | tf_op jit(solution)/shard_map/ppermute | solution.py:216
  48.3 7.3 %collective-permute-start.8 = (bf16[4,32,2048]{2,1,0:T(8,128)(2,1)S(1)}, bf16[4,32,2048]{2,1,0:T(8,128)(2,1)S(1)}, u32[]{:S(2)}, u32[]{:S(2)}) collective-permute-start(bf16[4,32,2048]{2,1,0:T(8,128)(2,1)S(1)} %pad_maximum_fusion.2), channel_id=1, source_target_pairs={{0,1},{1,0},{2,3},{3,2},{4,5},{5,4},{6,7},{7,6},{8,9},{9,8},{10,11... | collective-permute-start | bytes 1572872 | tf_op jit(solution)/shard_map/ppermute | solution.py:182
  51.0 17.0 %collective-permute-start.11 = (bf16[4,32,2048]{2,1,0:T(8,128)(2,1)S(1)}, bf16[4,32,2048]{2,1,0:T(8,128)(2,1)S(1)}, u32[]{:S(2)}, u32[]{:S(2)}) collective-permute-start(bf16[4,32,2048]{2,1,0:T(8,128)(2,1)S(1)} %pad_maximum_fusion.2), channel_id=1, source_target_pairs={{0,2},{1,3},{2,0},{3,1},{4,6},{5,7},{6,4},{7,5},{8,10},{9,11},{10,... | collective-permute-start | bytes 1572872 | tf_op jit(solution)/shard_map/ppermute | solution.py:182
  55.6 14.4 %slice-start.6 = ((s8[7340032]{0:T(1024)(128)(4,1)}), s8[4194304]{0:T(1024)(128)(4,1)S(1)}, s32[]{:S(2)}) async-start(s8[7340032]{0:T(1024)(128)(4,1)} %bitcast.225), calls=%async_computation.6 | async-start | bytes 8388608
  55.7 14.4 %slice-start.7 = ((s8[7340032]{0:T(1024)(128)(4,1)}), s8[3145728]{0:T(1024)(128)(4,1)S(1)}, s32[]{:S(2)}) async-start(s8[7340032]{0:T(1024)(128)(4,1)} %bitcast.225), calls=%async_computation.7 | async-start | bytes 6291456
  68.0 1.9 collective-permute-start.12
  68.0 13.4 %collective-permute-start.9 = (bf16[2,64,1792]{2,1,0:T(8,128)(2,1)S(1)}, bf16[2,64,1792]{2,1,0:T(8,128)(2,1)S(1)}, u32[]{:S(2)}, u32[]{:S(2)}) collective-permute-start(bf16[2,64,1792]{2,1,0:T(8,128)(2,1)S(1)} %pad_maximum_fusion.3), channel_id=1, source_target_pairs={{0,4},{4,0},{8,12},{12,8},{1,5},{5,1},{9,13},{13,9},{2,6},{6,2},{1... | collective-permute-start | bytes 1376264 | tf_op jit(solution)/shard_map/ppermute | solution.py:182
  72.3 23.5 %collective-permute-start.13 = (bf16[2,64,1792]{2,1,0:T(8,128)(2,1)S(1)}, bf16[2,64,1792]{2,1,0:T(8,128)(2,1)S(1)}, u32[]{:S(2)}, u32[]{:S(2)}) collective-permute-start(bf16[2,64,1792]{2,1,0:T(8,128)(2,1)S(1)} %pad_maximum_fusion.4), channel_id=1, source_target_pairs={{0,4},{4,0},{8,12},{12,8},{1,5},{5,1},{9,13},{13,9},{2,6},{6,2},{1... | collective-permute-start | bytes 1376264 | tf_op jit(solution)/shard_map/ppermute | solution.py:182
  82.2 13.8 %collective-permute-start.10 = (bf16[64,1792]{1,0:T(8,128)(2,1)}, bf16[64,1792]{1,0:T(8,128)(2,1)S(1)}, u32[]{:S(2)}, u32[]{:S(2)}) collective-permute-start(bf16[64,1792]{1,0:T(8,128)(2,1)} %fusion.32), channel_id=1, source_target_pairs={{0,8},{4,12},{8,0},{12,4},{1,9},{5,13},{9,1},{13,5},{2,10},{6,14},... | collective-permute-start | bytes 688136 | tf_op jit(solution)/shard_map/ppermute | solution.py:182
  95.9 12.5 %collective-permute-start.14 = (bf16[64,1792]{1,0:T(8,128)(2,1)S(1)}, bf16[64,1792]{1,0:T(8,128)(2,1)S(1)}, u32[]{:S(2)}, u32[]{:S(2)}) collective-permute-start(bf16[64,1792]{1,0:T(8,128)(2,1)S(1)} %fusion.33), channel_id=1, source_target_pairs={{0,8},{4,12},{8,0},{12,4},{1,9},{5,13},{9,1},{13,5},{2,10},{6,14},... | collective-permute-start | bytes 688136 | tf_op jit(solution)/shard_map/ppermute | solution.py:182
  96.0 12.3 %copy-start.2 = (bf16[64,1792]{1,0:T(8,128)(2,1)}, bf16[64,1792]{1,0:T(8,128)(2,1)S(1)}, u32[]{:S(2)}) copy-start(bf16[64,1792]{1,0:T(8,128)(2,1)S(1)} %collective-permute-done.10) | copy-start | bytes 688132
  108.3 0.7 copy-start.3
  109.0 33.9 %copy-start.4 = (f32[1792]{0:T(1024)S(1)}, f32[1792]{0:T(1024)}, u32[]{:S(2)}) copy-start(f32[1792]{0:T(1024)} %param.16) | copy-start | bytes 21508
  110.6 17.6 %collective-permute-start.15 = (bf16[64,1792]{1,0:T(8,128)(2,1)S(1)}, bf16[64,1792]{1,0:T(8,128)(2,1)S(1)}, u32[]{:S(2)}, u32[]{:S(2)}) collective-permute-start(bf16[64,1792]{1,0:T(8,128)(2,1)S(1)} %get-tuple-element.7), channel_id=1, source_target_pairs={{0,8},{4,12},{8,0},{12,4},{1,9},{5,13},{9,1},{13,5},{2,10},{6,14},... | collective-permute-start | bytes 688136 | tf_op jit(solution)/shard_map/ppermute | solution.py:182
  110.6 22.5 %collective-permute-start.18 = (bf16[64,1792]{1,0:T(8,128)(2,1)S(1)}, bf16[64,1792]{1,0:T(8,128)(2,1)S(1)}, u32[]{:S(2)}, u32[]{:S(2)}) collective-permute-start(bf16[64,1792]{1,0:T(8,128)(2,1)S(1)} %get-tuple-element.6), channel_id=1, source_target_pairs={{0,8},{4,12},{8,0},{12,4},{1,9},{5,13},{9,1},{13,5},{2,10},{6,14},... | collective-permute-start | bytes 688136 | tf_op jit(solution)/shard_map/ppermute | solution.py:182
  128.2 14.7 %collective-permute-start.16 = (bf16[128,1792]{1,0:T(8,128)(2,1)S(1)}, bf16[128,1792]{1,0:T(8,128)(2,1)S(1)}, u32[]{:S(2)}, u32[]{:S(2)}) collective-permute-start(bf16[128,1792]{1,0:T(8,128)(2,1)S(1)} %pad_maximum_fusion.6), channel_id=1, source_target_pairs={{0,4},{4,0},{8,12},{12,8},{1,5},{5,1},{9,13},{13,9},{2,6},{6,2},{1... | collective-permute-start | bytes 1376264 | tf_op jit(solution)/shard_map/ppermute | solution.py:182
  133.1 19.6 %slice-start = ((s8[9175040]{0:T(1024)(128)(4,1)}), s8[4194304]{0:T(1024)(128)(4,1)S(1)}, s32[]{:S(2)}) async-start(s8[9175040]{0:T(1024)(128)(4,1)} %bitcast.221), calls=%async_computation | async-start | bytes 8388608
  133.1 19.5 %slice-start.1 = ((s8[9175040]{0:T(1024)(128)(4,1)}), s8[4194304]{0:T(1024)(128)(4,1)S(1)}, s32[]{:S(2)}) async-start(s8[9175040]{0:T(1024)(128)(4,1)} %bitcast.221), calls=%async_computation.1 | async-start | bytes 8388608
  133.1 19.5 %slice-start.2 = ((s8[9175040]{0:T(1024)(128)(4,1)}), s8[786432]{0:T(1024)(128)(4,1)S(1)}, s32[]{:S(2)}) async-start(s8[9175040]{0:T(1024)(128)(4,1)} %bitcast.221), calls=%async_computation.2 | async-start | bytes 1572864
  133.1 19.5 %collective-permute-start.19 = (bf16[128,1792]{1,0:T(8,128)(2,1)S(1)}, bf16[128,1792]{1,0:T(8,128)(2,1)S(1)}, u32[]{:S(2)}, u32[]{:S(2)}) collective-permute-start(bf16[128,1792]{1,0:T(8,128)(2,1)S(1)} %pad_maximum_fusion.7), channel_id=1, source_target_pairs={{0,4},{4,0},{8,12},{12,8},{1,5},{5,1},{9,13},{13,9},{2,6},{6,2},{1... | collective-permute-start | bytes 1376264 | tf_op jit(solution)/shard_map/ppermute | solution.py:182
  149.0 6.3 %slice-start.3 = ((s8[9175040]{0:T(1024)(128)(4,1)}), s8[4194304]{0:T(1024)(128)(4,1)S(1)}, s32[]{:S(2)}) async-start(s8[9175040]{0:T(1024)(128)(4,1)} %bitcast.223), calls=%async_computation.3 | async-start | bytes 8388608
  149.1 6.2 %slice-start.4 = ((s8[9175040]{0:T(1024)(128)(4,1)}), s8[4194304]{0:T(1024)(128)(4,1)S(1)}, s32[]{:S(2)}) async-start(s8[9175040]{0:T(1024)(128)(4,1)} %bitcast.223), calls=%async_computation.4 | async-start | bytes 8388608
  149.1 6.2 %slice-start.5 = ((s8[9175040]{0:T(1024)(128)(4,1)}), s8[786432]{0:T(1024)(128)(4,1)S(1)}, s32[]{:S(2)}) async-start(s8[9175040]{0:T(1024)(128)(4,1)} %bitcast.223), calls=%async_computation.5 | async-start | bytes 1572864
  149.1 44.0 %collective-permute-start.17 = (bf16[128,2560]{1,0:T(8,128)(2,1)S(1)}, bf16[128,2560]{1,0:T(8,128)(2,1)S(1)}, u32[]{:S(2)}, u32[]{:S(2)}) collective-permute-start(bf16[128,2560]{1,0:T(8,128)(2,1)S(1)} %dynamic-slice_bitcast_fusion.3), channel_id=1, source_target_pairs={{0,1},{1,0},{2,3},{3,2},{4,5},{5,4},{6,7},{7,6},{8,9},{9,8},{10,11... | collective-permute-start | bytes 1966088 | tf_op jit(solution)/shard_map/ppermute | solution.py:182
  155.3 6.4 %collective-permute-start.20 = (bf16[128,2560]{1,0:T(8,128)(2,1)S(1)}, bf16[128,2560]{1,0:T(8,128)(2,1)S(1)}, u32[]{:S(2)}, u32[]{:S(2)}) collective-permute-start(bf16[128,2560]{1,0:T(8,128)(2,1)S(1)} %dynamic-slice_bitcast_fusion.2), channel_id=1, source_target_pairs={{0,1},{1,0},{2,3},{3,2},{4,5},{5,4},{6,7},{7,6},{8,9},{9,8},{10,11... | collective-permute-start | bytes 1966088 | tf_op jit(solution)/shard_map/ppermute | solution.py:182
  158.0 35.2 %collective-permute-start.25 = (bf16[128,2560]{1,0:T(8,128)(2,1)S(1)}, bf16[128,2560]{1,0:T(8,128)(2,1)S(1)}, u32[]{:S(2)}, u32[]{:S(2)}) collective-permute-start(bf16[128,2560]{1,0:T(8,128)(2,1)S(1)} %dynamic-slice_bitcast_fusion.1), channel_id=1, source_target_pairs={{0,1},{1,0},{2,3},{3,2},{4,5},{5,4},{6,7},{7,6},{8,9},{9,8},{10,11... | collective-permute-start | bytes 1966088 | tf_op jit(solution)/shard_map/ppermute | solution.py:182
  161.3 2.2 collective-permute-start.26
  161.9 31.3 %collective-permute-start.21 = (bf16[128,2560]{1,0:T(8,128)(2,1)S(1)}, bf16[128,2560]{1,0:T(8,128)(2,1)S(1)}, u32[]{:S(2)}, u32[]{:S(2)}) collective-permute-start(bf16[128,2560]{1,0:T(8,128)(2,1)S(1)} %fusion.15), channel_id=1, source_target_pairs={{0,2},{1,3},{2,0},{3,1},{4,6},{5,7},{6,4},{7,5},{8,10},{9,11},{10,... | collective-permute-start | bytes 1966088 | tf_op jit(solution)/shard_map/ppermute | solution.py:182
  163.6 29.5 %collective-permute-start.27 = (bf16[128,2560]{1,0:T(8,128)(2,1)S(1)}, bf16[128,2560]{1,0:T(8,128)(2,1)S(1)}, u32[]{:S(2)}, u32[]{:S(2)}) collective-permute-start(bf16[128,2560]{1,0:T(8,128)(2,1)S(1)} %fusion.10), channel_id=1, source_target_pairs={{0,2},{1,3},{2,0},{3,1},{4,6},{5,7},{6,4},{7,5},{8,10},{9,11},{10,... | collective-permute-start | bytes 1966088 | tf_op jit(solution)/shard_map/ppermute | solution.py:182
  164.2 1.1 collective-permute-start.23
  165.3 1.1 collective-permute-start.22
  166.4 26.7 %collective-permute-start.24 = (f32[128]{0:T(128)S(1)}, f32[128]{0:T(128)S(1)}, u32[]{:S(2)}, u32[]{:S(2)}) collective-permute-start(f32[128]{0:T(128)S(1)} %fusion.62), channel_id=1, source_target_pairs={{0,2},{1,3},{2,0},{3,1},{4,6},{5,7},{6,4},{7,5},{8,10},{9,11},{10,... | collective-permute-start | bytes 1544 | tf_op jit(solution)/shard_map/ppermute | solution.py:182
  194.0 16.3 %collective-permute-start.28 = (bf16[128,2560]{1,0:T(8,128)(2,1)S(1)}, bf16[128,2560]{1,0:T(8,128)(2,1)S(1)}, u32[]{:S(2)}, u32[]{:S(2)}) collective-permute-start(bf16[128,2560]{1,0:T(8,128)(2,1)S(1)} %fusion.14), channel_id=1, source_target_pairs={{0,2},{1,3},{2,0},{3,1},{4,6},{5,7},{6,4},{7,5},{8,10},{9,11},{10,... | collective-permute-start | bytes 1966088 | tf_op jit(solution)/shard_map/ppermute | solution.py:182
  194.5 15.9 %collective-permute-start.32 = (bf16[128,2560]{1,0:T(8,128)(2,1)S(1)}, bf16[128,2560]{1,0:T(8,128)(2,1)S(1)}, u32[]{:S(2)}, u32[]{:S(2)}) collective-permute-start(bf16[128,2560]{1,0:T(8,128)(2,1)S(1)} %fusion.14), channel_id=1, source_target_pairs={{0,1},{1,0},{2,3},{3,2},{4,5},{5,4},{6,7},{7,6},{8,9},{9,8},{10,11... | collective-permute-start | bytes 1966088 | tf_op jit(solution)/shard_map/ppermute | solution.py:182
  210.3 6.3 %collective-permute-start.29 = (bf16[128,2560]{1,0:T(8,128)(2,1)S(1)}, bf16[128,2560]{1,0:T(8,128)(2,1)S(1)}, u32[]{:S(2)}, u32[]{:S(2)}) collective-permute-start(bf16[128,2560]{1,0:T(8,128)(2,1)S(1)} %collective-permute-done.28), channel_id=1, source_target_pairs={{0,1},{1,0},{2,3},{3,2},{4,5},{5,4},{6,7},{7,6},{8,9},{9,8},{10,11... | collective-permute-start | bytes 1966088 | tf_op jit(solution)/shard_map/ppermute | solution.py:182
  216.5 13.4 %collective-permute-start.33 = (bf16[2,64,1792]{2,1,0:T(8,128)(2,1)S(1)}, bf16[2,64,1792]{2,1,0:T(8,128)(2,1)S(1)}, u32[]{:S(2)}, u32[]{:S(2)}) collective-permute-start(bf16[2,64,1792]{2,1,0:T(8,128)(2,1)S(1)} %dynamic-slice_bitcast_fusion.4), channel_id=1, source_target_pairs={{0,4},{4,0},{8,12},{12,8},{1,5},{5,1},{9,13},{13,9},{2,6},{6,2},{1... | collective-permute-start | bytes 1376264 | tf_op jit(solution)/shard_map/ppermute | solution.py:182
  222.8 21.5 %collective-permute-start.30 = (bf16[2,64,1792]{2,1,0:T(8,128)(2,1)S(1)}, bf16[2,64,1792]{2,1,0:T(8,128)(2,1)S(1)}, u32[]{:S(2)}, u32[]{:S(2)}) collective-permute-start(bf16[2,64,1792]{2,1,0:T(8,128)(2,1)S(1)} %dynamic-slice_bitcast_fusion.5), channel_id=1, source_target_pairs={{0,4},{4,0},{8,12},{12,8},{1,5},{5,1},{9,13},{13,9},{2,6},{6,2},{1... | collective-permute-start | bytes 1376264 | tf_op jit(solution)/shard_map/ppermute | solution.py:182
  230.0 14.5 %collective-permute-start.34 = (bf16[64,1792]{1,0:T(8,128)(2,1)S(1)}, bf16[64,1792]{1,0:T(8,128)(2,1)S(1)}, u32[]{:S(2)}, u32[]{:S(2)}) collective-permute-start(bf16[64,1792]{1,0:T(8,128)(2,1)S(1)} %fusion.22), channel_id=1, source_target_pairs={{0,8},{4,12},{8,0},{12,4},{1,9},{5,13},{9,1},{13,5},{2,10},{6,14},... | collective-permute-start | bytes 688136 | tf_op jit(solution)/shard_map/ppermute | solution.py:182
  244.3 12.5 %collective-permute-start.31 = (bf16[64,1792]{1,0:T(8,128)(2,1)S(1)}, bf16[64,1792]{1,0:T(8,128)(2,1)S(1)}, u32[]{:S(2)}, u32[]{:S(2)}) collective-permute-start(bf16[64,1792]{1,0:T(8,128)(2,1)S(1)} %fusion.26), channel_id=1, source_target_pairs={{0,8},{4,12},{8,0},{12,4},{1,9},{5,13},{9,1},{13,5},{2,10},{6,14},... | collective-permute-start | bytes 688136 | tf_op jit(solution)/shard_map/ppermute | solution.py:182

commit v3 on v2

--- a/solution.py
+++ b/solution.py
@@ -228,16 +228,46 @@
     )
 
 
-def reduce_ctx(kept, sent):
-    came = swap(sent, "ctx", 1)
-    mine = wide(kept[0]) + wide(came[0])
-    other = (wide(kept[1]) + wide(came[1])).astype(jnp.bfloat16)
-    return mine + wide(swap(other, "ctx", 2))
-
-
-def gather_ctx(rows):
-    pair = jnp.concatenate([rows, swap(rows, "ctx", 2)], axis=0)
-    return jnp.concatenate([pair, swap(pair, "ctx", 1)], axis=0)
+def after(value, earlier):
+    return lax.optimization_barrier((value, earlier))[0]
+
+
+def reduce_ctx(block_of, n_ctx):
+    c = lax.axis_index("ctx")
+    right = left = None
+    hops = []
+    for s in range(1, n_ctx):
+        to_right = block_of(jnp.minimum(n_ctx + c - s, n_ctx - 1))
+        to_left = block_of(jnp.maximum(c + s - n_ctx, 0))
+        if s > 1:
+            to_right = (wide(to_right) + wide(right)).astype(jnp.bfloat16)
+            to_left = (wide(to_left) + wide(left)).astype(jnp.bfloat16)
+        right = lax.ppermute(to_right, "ctx", [(i, i + 1) for i in range(s)])
+        left = lax.ppermute(to_left, "ctx", [(i, i - 1) for i in range(n_ctx - s, n_ctx)])
+        hops.append(right)
+    return wide(block_of(c)) + wide(right) + wide(left), hops
+
+
+def gather_ctx(rows, n_ctx):
+    c = lax.axis_index("ctx")
+    right = left = rows
+    from_left, from_right = [], []
+    for s in range(1, n_ctx):
+        right = lax.ppermute(right, "ctx", [(i, i + 1) for i in range(s - 1, n_ctx - 1)])
+        left = lax.ppermute(left, "ctx", [(i, i - 1) for i in range(1, n_ctx - s + 1)])
+        from_left.append(right)
+        from_right.append(left)
+
+    def block(place):
+        return lax.select_n(
+            c,
+            *[
+                rows if i == place else from_left[i - place - 1] if i > place else from_right[place - i - 1]
+                for i in range(n_ctx)
+            ],
+        )
+
+    return jnp.concatenate([block(i) for i in range(n_ctx)], axis=0)
 
 
 def paired_tail(
@@ -252,26 +282,23 @@
     first_half = (t >> 1) ^ (c >> 1)
     own = spread_heads(heads_out, n_ctx, n_tp)
     own_all = jnp.stack(own)
+    near = swap(own_all, "tp", 1)
     far = swap(own_all, "tp", 2)
-    near = swap(own_all, "tp", 1)
+    residual_halves = residual.reshape(2, half, width)
+
+    def sum_heads(blocks, which):
+        head_sum, hops = reduce_ctx(lambda i: pick(blocks, t ^ i), n_ctx)
+        return (wide(pick(residual_halves, which)) + head_sum).astype(jnp.bfloat16), hops
+
+    blocks_a = matmul(pair_rows(own_all, near), output_weight).reshape(n_ctx, half, width)
+    attended_a, hops_a = sum_heads(blocks_a, first_half)
+    far = after(far, hops_a[0])
     far_near = swap(far, "tp", 1)
-    rows_a = pair_rows(own_all, near)
     order = [2, 3, 0, 1]
     rows_b = pair_rows([far[i] for i in order], [far_near[i] for i in order])
-    residual_halves = residual.reshape(2, half, width)
-
-    def project(rows, which):
-        blocks = matmul(rows, output_weight).reshape(n_ctx, half, width)
-        place = t ^ c
-        head_sum = reduce_ctx(
-            (pick(blocks, place), pick(blocks, place ^ 2)),
-            jnp.stack([pick(blocks, place ^ 1), pick(blocks, place ^ 3)]),
-        )
-        attended = (wide(pick(residual_halves, which)) + head_sum).astype(jnp.bfloat16)
-        return attended, gather_ctx(attended)
-
-    attended_a, all_a = project(rows_a, first_half)
-    attended_b, all_b = project(rows_b, 1 - first_half)
+    blocks_b = matmul(rows_b, output_weight).reshape(n_ctx, half, width)
+    all_a = gather_ctx(attended_a, n_ctx)
+    attended_b, _ = sum_heads(after(blocks_b, attended_a), 1 - first_half)
 
     def gate_up(all_rows):
         values = wide(all_rows)
@@ -288,22 +315,26 @@
     across = [
         swap((wide(k) + wide(r)).astype(k.dtype), "tp", 2) for k, r in zip(kept_a, came_a)
     ]
+    all_b = gather_ctx(attended_b, n_ctx)
     kept_b, came_b = gate_up(all_b)
     gate, up, squares = [wide(k) + wide(r) + wide(x) for k, r, x in zip(kept_b, came_b, across)]
     inverse_rms = lax.rsqrt(squares / model_width + norm_eps)[:, None]
     hidden = (jax.nn.silu(gate * inverse_rms) * (up * inverse_rms)).astype(jnp.bfloat16)
+    hidden_near = swap(hidden, "tp", 1)
     hidden_far = swap(hidden, "tp", 2)
-    hidden_near = swap(hidden, "tp", 1)
+
+    def down(mine, other):
+        return matmul(jnp.concatenate([mine, other], axis=0), down_weight).reshape(n_ctx, half, width)
+
+    def finish(blocks, attended):
+        total, hops = reduce_ctx(lambda i: pick(blocks, i ^ (2 * core)), n_ctx)
+        return (wide(attended) + total).astype(jnp.bfloat16), hops
+
+    down_b = down(hidden, hidden_near)
+    out_b, hops_b = finish(down_b, attended_b)
+    hidden_far = after(hidden_far, hops_b[0])
     hidden_far_near = swap(hidden_far, "tp", 1)
-
-    def down(mine, other, attended):
-        blocks = matmul(jnp.concatenate([mine, other], axis=0), down_weight)
-        blocks = blocks.reshape(2, 2, half, width)
-        total = reduce_ctx(pick(blocks, core), pick(blocks, 1 - core))
-        return (wide(attended) + total).astype(jnp.bfloat16)
-
-    out_b = down(hidden, hidden_near, attended_b)
-    out_a = down(hidden_far, hidden_far_near, attended_a)
+    out_a, _ = finish(down(hidden_far, hidden_far_near), attended_a)
 
     def in_order(a, b):
         first = first_half == 0

time: 259 us -> 265 us (1.023)
  starting transfers between devices: 38.9 us -> 104 us
  waiting for transfers between devices: 166 us -> 101 us
  matrix products: 33.6 us -> 36.9 us
    ppermute x28 -> x16, waiting for transfers between devices: 150 us -> 35.4 us  [swap(): return lax.ppermute(value, axis_name, [(i, i ^ bit) for i in range(width)])]
    ppermute x0 -> x36, starting transfers between devices: none -> 74 us  [the longest x12 48 us: reduce_ctx(): right = lax.ppermute(to_right, 'ctx', [(i, i + 1) for i in range(s)])]
    ppermute x0 -> x36, waiting for transfers between devices: none -> 49 us  [the longest x6 21.8 us: gather_ctx(): lax.ppermute(left, 'ctx', [(i, i - 1) for i in range(1, n_ctx - s + 1)])]
    ppermute x28 -> x16, starting transfers between devices: 20.7 us -> 11.7 us  [swap(): return lax.ppermute(value, axis_name, [(i, i ^ bit) for i in range(width)])]
    dot_general x8, matrix products: 33.6 us -> 36.9 us  [matmul(): jnp.dot(a, b, preferred_element_type=jnp.float32).astype(jnp.bfloat16)]
    convert_element_type x4 -> x13, other arithmetic: 0.92 us -> 3.8 us  [the longest x8 2.07 us: reduce_ctx(): to_right = (wide(to_right) + wide(right)).astype(jnp.bfloat16)]
  transfers between devices with their start and end apart: 35 -> 59, of which waited for: 20 -> 25; matrix products, arithmetic and copies ran while one was open for 14% -> 14% of each run, Pallas kernels for 0% -> 0%
where the time goes in v3:
time: 265 us; the launch traced here: 264 us
  starting transfers between devices  104 us (39%)
  waiting for transfers between devices  101 us (38%)
  matrix products  36.9 us (14%)
  other arithmetic  12.6 us (5%)
  Pallas kernels  6.63 us (3%)
    ppermute x12, starting transfers between devices, reduce_ctx(): right = lax.ppermute(to_right, 'ctx', [(i, i + 1) for i in range(s)])  48 us
    dot_general x8, matrix products, matmul(): jnp.dot(a, b, preferred_element_type=jnp.float32).astype(jnp.bfloat16)  36.9 us
    ppermute x16, waiting for transfers between devices, swap(): return lax.ppermute(value, axis_name, [(i, i ^ bit) for i in range(width)])  35.4 us
    ppermute x6, waiting for transfers between devices, gather_ctx(): lax.ppermute(left, 'ctx', [(i, i - 1) for i in range(1, n_ctx - s + 1)])  21.8 us
    ppermute x12, waiting for transfers between devices, reduce_ctx(): lax.ppermute(to_left, 'ctx', [(i, i - 1) for i in range(n_ctx - s, n_ctx)])  16.5 us
    ppermute x4, waiting for transfers between devices, spread_heads(): lax.ppermute(pieces[s], ('ctx', 'tp'), [(c * n_tp + t, t * n_tp + (c ^ s)...  15 us
    ppermute x16, starting transfers between devices, swap(): return lax.ppermute(value, axis_name, [(i, i ^ bit) for i in range(width)])  11.7 us
    ppermute x3, starting transfers between devices, gather_keys(): lax.ppermute(half, 'ctx', [(c, c + d) for c in range(n_ctx - d)])  10.7 us
  transfers between devices with their start and end apart: 59, of which 25 were waited for; matrix products, arithmetic and copies ran while one was open for 14% of the time, Pallas kernels for 0%

profile of v3, /device:TPU:0, one launch (start us, length us, event | category | flops | bytes accessed | tf_op | source)
XLA Modules:
  0.0 264.2 jit_solution(8625047845832413815)
XLA Ops:
  0.6 0.9 convert_element_type.380
  1.6 1.1 slice.62
  4.8 7.0 %collective-permute-start = (bf16[288,128]{1,0:T(8,128)(2,1)S(1)}, bf16[288,128]{1,0:T(8,128)(2,1)S(1)}, u32[]{:S(2)}, u32[]{:S(2)}) collective-permute-start(bf16[288,128]{1,0:T(8,128)(2,1)S(1)} %fusion.59), channel_id=1, source_target_pairs={{0,12},{1,13},{2,14},{3,15},{16,28},{17,29},{18,30},{19,31}} | collective-permute-start | bytes 221192 | tf_op jit(solution)/shard_map/ppermute | solution.py:202
  11.8 1.3 collective-permute-start.1
  13.1 2.5 collective-permute-start.2
  16.3 1.2 collective-permute-done.2
  17.7 1.4 collective-permute-done.3
  19.2 6.6 %shard_map.113 = bf16[128,2048]{1,0:T(8,128)(2,1)S(1)} custom-call(f32[4,128,128]{2,1,0:T(8,128)S(1)} %pad_maximum_fusion.5.tables, s32[128,1]{1,0:T(8,128)S(1)} %copy.13.starts, s32[128,1]{1,0:T(8,128)S(1)} %iota_add_fusion.own_index, s32[1,512]{1,0:T(1,128)S(1)} %iota_add_fusion.1.key_index, bf16[576,512]{1,0:T(8,128)(2,1)S(1)} %maximum_maximum_fusion.keys, ...), custom_call_target="tpu_custom_call" | custom-call | flops 2684354560 | bytes 5046272 | tf_op jit(solution)/shard_map/pallas_call | solution.py:143
  26.1 5.0 %collective-permute-start.6 = (bf16[32,2048]{1,0:T(8,128)(2,1)S(1)}, bf16[32,2048]{1,0:T(8,128)(2,1)S(1)}, u32[]{:S(2)}, u32[]{:S(2)}) collective-permute-start(bf16[32,2048]{1,0:T(8,128)(2,1)S(1)} %get-tuple-element.39), channel_id=1, source_target_pairs={{0,2},{1,6},{2,10},{3,14},{4,3},{5,7},{6,11},{7,15},{8,0},{9,4},{1... | collective-permute-start | bytes 393224 | tf_op jit(solution)/shard_map/ppermute | solution.py:216
  31.1 1.5 collective-permute-start.7
  33.2 15.0 %collective-permute-done.6 = bf16[32,2048]{1,0:T(8,128)(2,1)S(1)} collective-permute-done((bf16[32,2048]{1,0:T(8,128)(2,1)S(1)}, bf16[32,2048]{1,0:T(8,128)(2,1)S(1)}, u32[]{:S(2)}, u32[]{:S(2)}) %collective-permute-start.6) | collective-permute-done | bytes 131104 | tf_op jit(solution)/shard_map/ppermute | solution.py:216
  48.3 2.7 %collective-permute-start.8 = (bf16[4,32,2048]{2,1,0:T(8,128)(2,1)S(1)}, bf16[4,32,2048]{2,1,0:T(8,128)(2,1)S(1)}, u32[]{:S(2)}, u32[]{:S(2)}) collective-permute-start(bf16[4,32,2048]{2,1,0:T(8,128)(2,1)S(1)} %pad_maximum_fusion.2), channel_id=1, source_target_pairs={{0,1},{1,0},{2,3},{3,2},{4,5},{5,4},{6,7},{7,6},{8,9},{9,8},{10,11... | collective-permute-start | bytes 1572872 | tf_op jit(solution)/shard_map/ppermute | solution.py:182
  51.0 1.5 collective-permute-done.8
  52.6 5.2 %convolution_convert_fusion.5 = bf16[256,1792]{1,0:T(8,128)(2,1)S(1)} fusion(bf16[256,2048]{1,0:T(8,128)(2,1)S(1)} %constant_dynamic-update-slice_fusion.3, bf16[2048,1792]{1,0:T(8,128)(2,1)} %param.15), kind=kOutput, calls=%fused_computation.5 | convolution fusion | flops 1879506944 | bytes 9306112 | tf_op jit(solution)/shard_map/dot_general | solution.py:194
  57.8 2.6 collective-permute-start.9
  60.5 4.8 %collective-permute-start.15 = (bf16[4,32,2048]{2,1,0:T(8,128)(2,1)S(1)}, bf16[4,32,2048]{2,1,0:T(8,128)(2,1)S(1)}, u32[]{:S(2)}, u32[]{:S(2)}) collective-permute-start(bf16[4,32,2048]{2,1,0:T(8,128)(2,1)S(1)} %pad_maximum_fusion.2), channel_id=1, source_target_pairs={{0,2},{1,3},{2,0},{3,1},{4,6},{5,7},{6,4},{7,5},{8,10},{9,11},{10,... | collective-permute-start | bytes 1572872 | tf_op jit(solution)/shard_map/ppermute | solution.py:182
  66.0 4.2 %collective-permute-start.10 = (bf16[64,1792]{1,0:T(8,128)(2,1)S(1)}, bf16[64,1792]{1,0:T(8,128)(2,1)S(1)}, u32[]{:S(2)}, u32[]{:S(2)}) collective-permute-start(bf16[64,1792]{1,0:T(8,128)(2,1)S(1)} %fusion.45), channel_id=1, source_target_pairs={{0,4},{4,8},{1,5},{5,9},{2,6},{6,10},{3,7},{7,11},{16,20},{20,24},... | collective-permute-start | bytes 688136 | tf_op jit(solution)/shard_map/ppermute | solution.py:245
  70.3 6.9 %collective-permute-done.15 = bf16[4,32,2048]{2,1,0:T(8,128)(2,1)S(1)} collective-permute-done((bf16[4,32,2048]{2,1,0:T(8,128)(2,1)S(1)}, bf16[4,32,2048]{2,1,0:T(8,128)(2,1)S(1)}, u32[]{:S(2)}, u32[]{:S(2)}) %collective-permute-start.15) | collective-permute-done | bytes 524320 | tf_op jit(solution)/shard_map/ppermute | solution.py:182
  78.1 2.6 collective-permute-start.11
  80.7 1.3 collective-permute-start.14
  82.2 5.2 %convolution_convert_fusion.4 = bf16[256,1792]{1,0:T(8,128)(2,1)S(1)} fusion(bf16[256,2048]{1,0:T(8,128)(2,1)S(1)} %bitcast_dynamic-update-slice_fusion, bf16[2048,1792]{1,0:T(8,128)(2,1)} %param.15), kind=kOutput, calls=%fused_computation.4 | convolution fusion | flops 1879506944 | bytes 9306112 | tf_op jit(solution)/shard_map/dot_general | solution.py:194
  87.4 6.5 %collective-permute-done.14 = bf16[64,1792]{1,0:T(8,128)(2,1)S(1)} collective-permute-done((bf16[64,1792]{1,0:T(8,128)(2,1)S(1)}, bf16[64,1792]{1,0:T(8,128)(2,1)S(1)}, u32[]{:S(2)}, u32[]{:S(2)}) %collective-permute-start.14) | collective-permute-done | bytes 229408 | tf_op jit(solution)/shard_map/ppermute | solution.py:246
  94.1 3.8 %collective-permute-start.17 = (bf16[64,1792]{1,0:T(8,128)(2,1)S(1)}, bf16[64,1792]{1,0:T(8,128)(2,1)S(1)}, u32[]{:S(2)}, u32[]{:S(2)}) collective-permute-start(bf16[64,1792]{1,0:T(8,128)(2,1)S(1)} %get-tuple-element.23), channel_id=1, source_target_pairs={{0,4},{1,5},{2,6},{3,7},{16,20},{17,21},{18,22},{19,23}} | collective-permute-start | bytes 688136 | tf_op jit(solution)/shard_map/ppermute | solution.py:245
  97.9 1.3 collective-permute-start.30
  99.2 1.3 collective-permute-start.33
  101.2 2.6 collective-permute-done.17
  103.9 4.4 %collective-permute-start.18 = (bf16[64,1792]{1,0:T(8,128)(2,1)S(1)}, bf16[64,1792]{1,0:T(8,128)(2,1)S(1)}, u32[]{:S(2)}, u32[]{:S(2)}) collective-permute-start(bf16[64,1792]{1,0:T(8,128)(2,1)S(1)} %fusion.38), channel_id=1, source_target_pairs={{0,4},{4,8},{1,5},{5,9},{2,6},{6,10},{3,7},{7,11},{16,20},{20,24},... | collective-permute-start | bytes 688136 | tf_op jit(solution)/shard_map/ppermute | solution.py:245
  109.3 1.3 collective-permute-start.34
  110.6 1.1 collective-permute-done.18
  112.6 5.1 %collective-permute-start.19 = (bf16[64,1792]{1,0:T(8,128)(2,1)S(1)}, bf16[64,1792]{1,0:T(8,128)(2,1)S(1)}, u32[]{:S(2)}, u32[]{:S(2)}) collective-permute-start(bf16[64,1792]{1,0:T(8,128)(2,1)S(1)} %get-tuple-element.21), channel_id=1, source_target_pairs={{0,4},{4,8},{8,12},{1,5},{5,9},{9,13},{2,6},{6,10},{10,14},{3,7},{... | collective-permute-start | bytes 688136 | tf_op jit(solution)/shard_map/ppermute | solution.py:245
  118.4 1.3 collective-permute-start.35
  119.8 1.3 collective-permute-start.22
  121.2 6.0 %collective-permute-done.35 = bf16[64,1792]{1,0:T(8,128)(2,1)} collective-permute-done((bf16[64,1792]{1,0:T(8,128)(2,1)S(1)}, bf16[64,1792]{1,0:T(8,128)(2,1)}, u32[]{:S(2)}, u32[]{:S(2)}) %collective-permute-start.35) | collective-permute-done | bytes 229408 | tf_op jit(solution)/shard_map/ppermute | solution.py:257
  127.2 2.5 collective-permute-done.22
  129.7 1.3 select_select_fusion.3
  130.9 3.4 %collective-permute-start.23 = (bf16[64,1792]{1,0:T(8,128)(2,1)S(1)}, bf16[64,1792]{1,0:T(8,128)(2,1)S(1)}, u32[]{:S(2)}, u32[]{:S(2)}) collective-permute-start(bf16[64,1792]{1,0:T(8,128)(2,1)S(1)} %get-tuple-element.47), channel_id=1, source_target_pairs={{0,4},{4,8},{8,12},{1,5},{5,9},{9,13},{2,6},{6,10},{10,14},{3,7},{... | collective-permute-start | bytes 688136 | tf_op jit(solution)/shard_map/ppermute | solution.py:256
  134.4 1.5 collective-permute-start.26
  136.3 6.3 %convolution_convert_fusion.2 = bf16[256,2560]{1,0:T(8,128)(2,1)S(1)} fusion(bf16[1792,2560]{1,0:T(8,128)(2,1)} %param.17, f32[1792]{0:T(1024)S(1)} %copy-done.3, bf16[64,1792]{1,0:T(8,128)(2,1)S(1)} %get-tuple-element.36, bf16[64,1792]{1,0:T(8,128)(2,1)S(1)} %get-tuple-element.35, bf16[64,1792]{1,0:T(8,128)(2,1)S(1)} %get-tuple-element.34, ...), kind=kOutput, calls=%fused_computation.2 | convolution fusion | flops 2354053120 | bytes 11410432 | tf_op jit(solution)/shard_map/dot_general | solution.py:194
  143.2 2.5 convolution_convert_fusion
  146.4 1.3 collective-permute-start.27
  148.6 11.1 %collective-permute-done.27 = bf16[64,1792]{1,0:T(8,128)(2,1)S(1)} collective-permute-done((bf16[64,1792]{1,0:T(8,128)(2,1)S(1)}, bf16[64,1792]{1,0:T(8,128)(2,1)S(1)}, u32[]{:S(2)}, u32[]{:S(2)}) %collective-permute-start.27) | collective-permute-done | bytes 229408 | tf_op jit(solution)/shard_map/ppermute | solution.py:257
  159.6 1.3 collective-permute-start.28
  161.3 2.1 collective-permute-start.43
  163.4 4.8 %collective-permute-done.28 = bf16[64,1792]{1,0:T(8,128)(2,1)S(1)} collective-permute-done((bf16[64,1792]{1,0:T(8,128)(2,1)S(1)}, bf16[64,1792]{1,0:T(8,128)(2,1)S(1)}, u32[]{:S(2)}, u32[]{:S(2)}) %collective-permute-start.28) | collective-permute-done | bytes 229408 | tf_op jit(solution)/shard_map/ppermute | solution.py:257
  168.4 2.5 convolution_convert_fusion.3
  170.9 2.5 convolution_convert_fusion.1
  174.6 16.5 %collective-permute-done.40 = f32[128]{0:T(128)S(1)} collective-permute-done((f32[128]{0:T(128)S(1)}, f32[128]{0:T(128)S(1)}, u32[]{:S(2)}, u32[]{:S(2)}) %collective-permute-start.40) | collective-permute-done | bytes 544 | tf_op jit(solution)/shard_map/ppermute | solution.py:182
  191.1 1.1 collective-permute-done.38
  193.7 1.6 collective-permute-done.45
  195.3 6.1 %convolution_convert_fusion.7 = bf16[256,1792]{1,0:T(8,128)(2,1)S(1)} fusion(bf16[2560,1792]{1,0:T(8,128)(2,1)} %param.19, bf16[128,2560]{1,0:T(8,128)(2,1)S(1)} %collective-permute-done.45, bf16[128,2560]{1,0:T(8,128)(2,1)S(1)} %fusion.14), kind=kOutput, calls=%fused_computation.7 | convolution fusion | flops 2351890432 | bytes 11403264 | tf_op jit(solution)/shard_map/dot_general | solution.py:194
  201.4 4.3 %collective-permute-start.46 = (bf16[64,1792]{1,0:T(8,128)(2,1)S(1)}, bf16[64,1792]{1,0:T(8,128)(2,1)S(1)}, u32[]{:S(2)}, u32[]{:S(2)}) collective-permute-start(bf16[64,1792]{1,0:T(8,128)(2,1)S(1)} %get-tuple-element.16), channel_id=1, source_target_pairs={{0,4},{1,5},{2,6},{3,7},{16,20},{17,21},{18,22},{19,23}} | collective-permute-start | bytes 688136 | tf_op jit(solution)/shard_map/ppermute | solution.py:245
  205.7 4.7 %collective-permute-done.44 = bf16[128,2560]{1,0:T(8,128)(2,1)} collective-permute-done((bf16[128,2560]{1,0:T(8,128)(2,1)S(1)}, bf16[128,2560]{1,0:T(8,128)(2,1)}, u32[]{:S(2)}, u32[]{:S(2)}) %collective-permute-start.44) | collective-permute-done | bytes 655392 | tf_op jit(solution)/shard_map/ppermute | solution.py:182
  211.8 1.5 collective-permute-done.47
  213.4 6.6 %convolution_convert_fusion.6 = bf16[256,1792]{1,0:T(8,128)(2,1)S(1)} fusion(bf16[2560,1792]{1,0:T(8,128)(2,1)} %param.19, bf16[128,2560]{1,0:T(8,128)(2,1)} %collective-permute-done.47, bf16[128,2560]{1,0:T(8,128)(2,1)} %collective-permute-done.44), kind=kOutput, calls=%fused_computation.6 | convolution fusion | flops 2351890432 | bytes 11403264 | tf_op jit(solution)/shard_map/dot_general | solution.py:194
  220.0 4.4 %collective-permute-start.48 = (bf16[64,1792]{1,0:T(8,128)(2,1)S(1)}, bf16[64,1792]{1,0:T(8,128)(2,1)S(1)}, u32[]{:S(2)}, u32[]{:S(2)}) collective-permute-start(bf16[64,1792]{1,0:T(8,128)(2,1)S(1)} %get-tuple-element.19), channel_id=1, source_target_pairs={{0,4},{1,5},{2,6},{3,7},{16,20},{17,21},{18,22},{19,23}} | collective-permute-start | bytes 688136 | tf_op jit(solution)/shard_map/ppermute | solution.py:245
  224.5 1.3 collective-permute-start.54
  226.5 3.9 %collective-permute-done.48 = bf16[64,1792]{1,0:T(8,128)(2,1)S(1)} collective-permute-done((bf16[64,1792]{1,0:T(8,128)(2,1)S(1)}, bf16[64,1792]{1,0:T(8,128)(2,1)S(1)}, u32[]{:S(2)}, u32[]{:S(2)}) %collective-permute-start.48) | collective-permute-done | bytes 229408 | tf_op jit(solution)/shard_map/ppermute | solution.py:245
  230.4 4.4 %collective-permute-start.49 = (bf16[64,1792]{1,0:T(8,128)(2,1)S(1)}, bf16[64,1792]{1,0:T(8,128)(2,1)S(1)}, u32[]{:S(2)}, u32[]{:S(2)}) collective-permute-start(bf16[64,1792]{1,0:T(8,128)(2,1)S(1)} %fusion.31), channel_id=1, source_target_pairs={{0,4},{4,8},{1,5},{5,9},{2,6},{6,10},{3,7},{7,11},{16,20},{20,24},... | collective-permute-start | bytes 688136 | tf_op jit(solution)/shard_map/ppermute | solution.py:245
  236.7 5.0 %collective-permute-start.55 = (bf16[64,1792]{1,0:T(8,128)(2,1)}, bf16[64,1792]{1,0:T(8,128)(2,1)S(1)}, u32[]{:S(2)}, u32[]{:S(2)}) collective-permute-start(bf16[64,1792]{1,0:T(8,128)(2,1)} %get-tuple-element.13), channel_id=1, source_target_pairs={{0,4},{4,8},{8,12},{1,5},{5,9},{9,13},{2,6},{6,10},{10,14},{3,7},{... | collective-permute-start | bytes 688136 | tf_op jit(solution)/shard_map/ppermute | solution.py:245
  244.0 1.3 collective-permute-start.58
  245.3 5.8 %collective-permute-start.50 = (bf16[64,1792]{1,0:T(8,128)(2,1)}, bf16[64,1792]{1,0:T(8,128)(2,1)S(1)}, u32[]{:S(2)}, u32[]{:S(2)}) collective-permute-start(bf16[64,1792]{1,0:T(8,128)(2,1)} %get-tuple-element.17), channel_id=1, source_target_pairs={{0,4},{4,8},{8,12},{1,5},{5,9},{9,13},{2,6},{6,10},{10,14},{3,7},{... | collective-permute-start | bytes 688136 | tf_op jit(solution)/shard_map/ppermute | solution.py:245
  251.9 1.3 collective-permute-start.53
  253.3 1.6 collective-permute-done.50
  254.9 7.4 %collective-permute-done.53 = bf16[64,1792]{1,0:T(8,128)(2,1)S(1)} collective-permute-done((bf16[64,1792]{1,0:T(8,128)(2,1)}, bf16[64,1792]{1,0:T(8,128)(2,1)S(1)}, u32[]{:S(2)}, u32[]{:S(2)}) %collective-permute-start.53) | collective-permute-done | bytes 229408 | tf_op jit(solution)/shard_map/ppermute | solution.py:246
  (163 shorter events, 24.1 us)
Async XLA Ops:
  1.6 17.6 %copy-start.1 = (bf16[512,2048]{1,0:T(8,128)(2,1)S(1)}, bf16[512,2048]{1,0:T(8,128)(2,1)}, u32[]{:S(2)}) copy-start(bf16[512,2048]{1,0:T(8,128)(2,1)} %value_weight.1) | copy-start | bytes 6291460
  4.8 11.4 %collective-permute-start = (bf16[288,128]{1,0:T(8,128)(2,1)S(1)}, bf16[288,128]{1,0:T(8,128)(2,1)S(1)}, u32[]{:S(2)}, u32[]{:S(2)}) collective-permute-start(bf16[288,128]{1,0:T(8,128)(2,1)S(1)} %fusion.59), channel_id=1, source_target_pairs={{0,12},{1,13},{2,14},{3,15},{16,28},{17,29},{18,30},{19,31}} | collective-permute-start | bytes 221192 | tf_op jit(solution)/shard_map/ppermute | solution.py:202
  11.8 4.5 %collective-permute-start.1 = (bf16[288,128]{1,0:T(8,128)(2,1)S(1)}, bf16[288,128]{1,0:T(8,128)(2,1)S(1)}, u32[]{:S(2)}, u32[]{:S(2)}) collective-permute-start(bf16[288,128]{1,0:T(8,128)(2,1)S(1)} %fusion.59), channel_id=1, source_target_pairs={{0,8},{4,12},{1,9},{5,13},{2,10},{6,14},{3,11},{7,15},{16,24},{20,... | collective-permute-start | bytes 221192 | tf_op jit(solution)/shard_map/ppermute | solution.py:202
  13.1 4.4 %collective-permute-start.2 = (bf16[288,128]{1,0:T(8,128)(2,1)S(1)}, bf16[288,128]{1,0:T(8,128)(2,1)S(1)}, u32[]{:S(2)}, u32[]{:S(2)}) collective-permute-start(bf16[288,128]{1,0:T(8,128)(2,1)S(1)} %fusion.59), channel_id=1, source_target_pairs={{0,4},{4,8},{8,12},{1,5},{5,9},{9,13},{2,6},{6,10},{10,14},{3,7},{... | collective-permute-start | bytes 221192 | tf_op jit(solution)/shard_map/ppermute | solution.py:202
  17.6 1.5 collective-permute-start.3
  25.9 7.3 %collective-permute-start.5 = (bf16[32,2048]{1,0:T(8,128)(2,1)S(1)}, bf16[32,2048]{1,0:T(8,128)(2,1)S(1)}, u32[]{:S(2)}, u32[]{:S(2)}) collective-permute-start(bf16[32,2048]{1,0:T(8,128)(2,1)S(1)} %get-tuple-element.37), channel_id=1, source_target_pairs={{0,1},{1,5},{2,9},{3,13},{4,0},{5,4},{6,8},{7,12},{8,3},{9,7},{10,... | collective-permute-start | bytes 393224 | tf_op jit(solution)/shard_map/ppermute | solution.py:216
  26.1 22.1 %collective-permute-start.6 = (bf16[32,2048]{1,0:T(8,128)(2,1)S(1)}, bf16[32,2048]{1,0:T(8,128)(2,1)S(1)}, u32[]{:S(2)}, u32[]{:S(2)}) collective-permute-start(bf16[32,2048]{1,0:T(8,128)(2,1)S(1)} %get-tuple-element.39), channel_id=1, source_target_pairs={{0,2},{1,6},{2,10},{3,14},{4,3},{5,7},{6,11},{7,15},{8,0},{9,4},{1... | collective-permute-start | bytes 393224 | tf_op jit(solution)/shard_map/ppermute | solution.py:216
  31.1 17.1 %collective-permute-start.7 = (bf16[32,2048]{1,0:T(8,128)(2,1)S(1)}, bf16[32,2048]{1,0:T(8,128)(2,1)S(1)}, u32[]{:S(2)}, u32[]{:S(2)}) collective-permute-start(bf16[32,2048]{1,0:T(8,128)(2,1)S(1)} %get-tuple-element.38), channel_id=1, source_target_pairs={{0,3},{1,7},{2,11},{3,15},{4,2},{5,6},{6,10},{7,14},{8,1},{9,5},{1... | collective-permute-start | bytes 393224 | tf_op jit(solution)/shard_map/ppermute | solution.py:216
  32.5 15.7 %collective-permute-start.4 = (bf16[32,2048]{1,0:T(8,128)(2,1)S(1)}, bf16[32,2048]{1,0:T(8,128)(2,1)S(1)}, u32[]{:S(2)}, u32[]{:S(2)}) collective-permute-start(bf16[32,2048]{1,0:T(8,128)(2,1)S(1)} %get-tuple-element.40), channel_id=1, source_target_pairs={{0,0},{1,4},{2,8},{3,12},{4,1},{5,5},{6,9},{7,13},{8,2},{9,6},{10,... | collective-permute-start | bytes 393224 | tf_op jit(solution)/shard_map/ppermute | solution.py:216
  48.3 4.2 %collective-permute-start.8 = (bf16[4,32,2048]{2,1,0:T(8,128)(2,1)S(1)}, bf16[4,32,2048]{2,1,0:T(8,128)(2,1)S(1)}, u32[]{:S(2)}, u32[]{:S(2)}) collective-permute-start(bf16[4,32,2048]{2,1,0:T(8,128)(2,1)S(1)} %pad_maximum_fusion.2), channel_id=1, source_target_pairs={{0,1},{1,0},{2,3},{3,2},{4,5},{5,4},{6,7},{7,6},{8,9},{9,8},{10,11... | collective-permute-start | bytes 1572872 | tf_op jit(solution)/shard_map/ppermute | solution.py:182
  57.8 8.1 %collective-permute-start.9 = (bf16[64,1792]{1,0:T(8,128)(2,1)S(1)}, bf16[64,1792]{1,0:T(8,128)(2,1)S(1)}, u32[]{:S(2)}, u32[]{:S(2)}) collective-permute-start(bf16[64,1792]{1,0:T(8,128)(2,1)S(1)} %get-tuple-element.27), channel_id=1, source_target_pairs={{0,4},{1,5},{2,6},{3,7},{16,20},{17,21},{18,22},{19,23}} | collective-permute-start | bytes 688136 | tf_op jit(solution)/shard_map/ppermute | solution.py:245
  60.5 16.8 %collective-permute-start.15 = (bf16[4,32,2048]{2,1,0:T(8,128)(2,1)S(1)}, bf16[4,32,2048]{2,1,0:T(8,128)(2,1)S(1)}, u32[]{:S(2)}, u32[]{:S(2)}) collective-permute-start(bf16[4,32,2048]{2,1,0:T(8,128)(2,1)S(1)} %pad_maximum_fusion.2), channel_id=1, source_target_pairs={{0,2},{1,3},{2,0},{3,1},{4,6},{5,7},{6,4},{7,5},{8,10},{9,11},{10,... | collective-permute-start | bytes 1572872 | tf_op jit(solution)/shard_map/ppermute | solution.py:182
  65.3 11.9 %collective-permute-start.12 = (bf16[64,1792]{1,0:T(8,128)(2,1)S(1)}, bf16[64,1792]{1,0:T(8,128)(2,1)S(1)}, u32[]{:S(2)}, u32[]{:S(2)}) collective-permute-start(bf16[64,1792]{1,0:T(8,128)(2,1)S(1)} %get-tuple-element.28), channel_id=1, source_target_pairs={{12,8},{13,9},{14,10},{15,11},{28,24},{29,25},{30,26},{31,27}} | collective-permute-start | bytes 688136 | tf_op jit(solution)/shard_map/ppermute | solution.py:246
  66.0 11.2 %collective-permute-start.10 = (bf16[64,1792]{1,0:T(8,128)(2,1)S(1)}, bf16[64,1792]{1,0:T(8,128)(2,1)S(1)}, u32[]{:S(2)}, u32[]{:S(2)}) collective-permute-start(bf16[64,1792]{1,0:T(8,128)(2,1)S(1)} %fusion.45), channel_id=1, source_target_pairs={{0,4},{4,8},{1,5},{5,9},{2,6},{6,10},{3,7},{7,11},{16,20},{20,24},... | collective-permute-start | bytes 688136 | tf_op jit(solution)/shard_map/ppermute | solution.py:245
  77.2 4.8 %collective-permute-start.16 = (bf16[4,32,2048]{2,1,0:T(8,128)(2,1)S(1)}, bf16[4,32,2048]{2,1,0:T(8,128)(2,1)S(1)}, u32[]{:S(2)}, u32[]{:S(2)}) collective-permute-start(bf16[4,32,2048]{2,1,0:T(8,128)(2,1)S(1)} %collective-permute-done.15), channel_id=1, source_target_pairs={{0,1},{1,0},{2,3},{3,2},{4,5},{5,4},{6,7},{7,6},{8,9},{9,8},{10,11... | collective-permute-start | bytes 1572872 | tf_op jit(solution)/shard_map/ppermute | solution.py:182
  77.4 3.3 %collective-permute-start.13 = (bf16[64,1792]{1,0:T(8,128)(2,1)S(1)}, bf16[64,1792]{1,0:T(8,128)(2,1)S(1)}, u32[]{:S(2)}, u32[]{:S(2)}) collective-permute-start(bf16[64,1792]{1,0:T(8,128)(2,1)S(1)} %get-tuple-element.26), channel_id=1, source_target_pairs={{8,4},{12,8},{9,5},{13,9},{10,6},{14,10},{11,7},{15,11},{24,20},{2... | collective-permute-start | bytes 688136 | tf_op jit(solution)/shard_map/ppermute | solution.py:246
  78.1 9.3 %collective-permute-start.11 = (bf16[64,1792]{1,0:T(8,128)(2,1)S(1)}, bf16[64,1792]{1,0:T(8,128)(2,1)S(1)}, u32[]{:S(2)}, u32[]{:S(2)}) collective-permute-start(bf16[64,1792]{1,0:T(8,128)(2,1)S(1)} %get-tuple-element.25), channel_id=1, source_target_pairs={{0,4},{4,8},{8,12},{1,5},{5,9},{9,13},{2,6},{6,10},{10,14},{3,7},{... | collective-permute-start | bytes 688136 | tf_op jit(solution)/shard_map/ppermute | solution.py:245
  80.7 13.2 %collective-permute-start.14 = (bf16[64,1792]{1,0:T(8,128)(2,1)S(1)}, bf16[64,1792]{1,0:T(8,128)(2,1)S(1)}, u32[]{:S(2)}, u32[]{:S(2)}) collective-permute-start(bf16[64,1792]{1,0:T(8,128)(2,1)S(1)} %fusion.44), channel_id=1, source_target_pairs={{4,0},{8,4},{12,8},{5,1},{9,5},{13,9},{6,2},{10,6},{14,10},{7,3},{... | collective-permute-start | bytes 688136 | tf_op jit(solution)/shard_map/ppermute | solution.py:246
  94.1 9.7 %collective-permute-start.17 = (bf16[64,1792]{1,0:T(8,128)(2,1)S(1)}, bf16[64,1792]{1,0:T(8,128)(2,1)S(1)}, u32[]{:S(2)}, u32[]{:S(2)}) collective-permute-start(bf16[64,1792]{1,0:T(8,128)(2,1)S(1)} %get-tuple-element.23), channel_id=1, source_target_pairs={{0,4},{1,5},{2,6},{3,7},{16,20},{17,21},{18,22},{19,23}} | collective-permute-start | bytes 688136 | tf_op jit(solution)/shard_map/ppermute | solution.py:245
  97.9 10.8 %collective-permute-start.30 = (bf16[64,1792]{1,0:T(8,128)(2,1)S(1)}, bf16[64,1792]{1,0:T(8,128)(2,1)S(1)}, u32[]{:S(2)}, u32[]{:S(2)}) collective-permute-start(bf16[64,1792]{1,0:T(8,128)(2,1)S(1)} %fusion.49), channel_id=1, source_target_pairs={{0,4},{4,8},{8,12},{1,5},{5,9},{9,13},{2,6},{6,10},{10,14},{3,7},{... | collective-permute-start | bytes 688136 | tf_op jit(solution)/shard_map/ppermute | solution.py:256
  99.2 10.1 %collective-permute-start.33 = (bf16[64,1792]{1,0:T(8,128)(2,1)S(1)}, bf16[64,1792]{1,0:T(8,128)(2,1)S(1)}, u32[]{:S(2)}, u32[]{:S(2)}) collective-permute-start(bf16[64,1792]{1,0:T(8,128)(2,1)S(1)} %fusion.49), channel_id=1, source_target_pairs={{4,0},{8,4},{12,8},{5,1},{9,5},{13,9},{6,2},{10,6},{14,10},{7,3},{... | collective-permute-start | bytes 688136 | tf_op jit(solution)/shard_map/ppermute | solution.py:257
  100.5 10.1 %collective-permute-start.20 = (bf16[64,1792]{1,0:T(8,128)(2,1)S(1)}, bf16[64,1792]{1,0:T(8,128)(2,1)S(1)}, u32[]{:S(2)}, u32[]{:S(2)}) collective-permute-start(bf16[64,1792]{1,0:T(8,128)(2,1)S(1)} %get-tuple-element.24), channel_id=1, source_target_pairs={{12,8},{13,9},{14,10},{15,11},{28,24},{29,25},{30,26},{31,27}} | collective-permute-start | bytes 688136 | tf_op jit(solution)/shard_map/ppermute | solution.py:246
  103.9 7.9 %collective-permute-start.18 = (bf16[64,1792]{1,0:T(8,128)(2,1)S(1)}, bf16[64,1792]{1,0:T(8,128)(2,1)S(1)}, u32[]{:S(2)}, u32[]{:S(2)}) collective-permute-start(bf16[64,1792]{1,0:T(8,128)(2,1)S(1)} %fusion.38), channel_id=1, source_target_pairs={{0,4},{4,8},{1,5},{5,9},{2,6},{6,10},{3,7},{7,11},{16,20},{20,24},... | collective-permute-start | bytes 688136 | tf_op jit(solution)/shard_map/ppermute | solution.py:245
  108.6 9.1 %collective-permute-start.31 = (bf16[64,1792]{1,0:T(8,128)(2,1)S(1)}, bf16[64,1792]{1,0:T(8,128)(2,1)S(1)}, u32[]{:S(2)}, u32[]{:S(2)}) collective-permute-start(bf16[64,1792]{1,0:T(8,128)(2,1)S(1)} %collective-permute-done.30), channel_id=1, source_target_pairs={{4,8},{8,12},{5,9},{9,13},{6,10},{10,14},{7,11},{11,15},{20,24},{2... | collective-permute-start | bytes 688136 | tf_op jit(solution)/shard_map/ppermute | solution.py:256
  109.3 9.1 %collective-permute-start.34 = (bf16[64,1792]{1,0:T(8,128)(2,1)S(1)}, bf16[64,1792]{1,0:T(8,128)(2,1)S(1)}, u32[]{:S(2)}, u32[]{:S(2)}) collective-permute-start(bf16[64,1792]{1,0:T(8,128)(2,1)S(1)} %collective-permute-done.33), channel_id=1, source_target_pairs={{4,0},{8,4},{5,1},{9,5},{6,2},{10,6},{7,3},{11,7},{20,16},{24,20},... | collective-permute-start | bytes 688136 | tf_op jit(solution)/shard_map/ppermute | solution.py:257
  111.9 7.8 %collective-permute-start.21 = (bf16[64,1792]{1,0:T(8,128)(2,1)S(1)}, bf16[64,1792]{1,0:T(8,128)(2,1)S(1)}, u32[]{:S(2)}, u32[]{:S(2)}) collective-permute-start(bf16[64,1792]{1,0:T(8,128)(2,1)S(1)} %get-tuple-element.22), channel_id=1, source_target_pairs={{8,4},{12,8},{9,5},{13,9},{10,6},{14,10},{11,7},{15,11},{24,20},{2... | collective-permute-start | bytes 688136 | tf_op jit(solution)/shard_map/ppermute | solution.py:246
  112.6 8.7 %collective-permute-start.19 = (bf16[64,1792]{1,0:T(8,128)(2,1)S(1)}, bf16[64,1792]{1,0:T(8,128)(2,1)S(1)}, u32[]{:S(2)}, u32[]{:S(2)}) collective-permute-start(bf16[64,1792]{1,0:T(8,128)(2,1)S(1)} %get-tuple-element.21), channel_id=1, source_target_pairs={{0,4},{4,8},{8,12},{1,5},{5,9},{9,13},{2,6},{6,10},{10,14},{3,7},{... | collective-permute-start | bytes 688136 | tf_op jit(solution)/shard_map/ppermute | solution.py:245
  117.7 3.5 %collective-permute-start.32 = (bf16[64,1792]{1,0:T(8,128)(2,1)S(1)}, bf16[64,1792]{1,0:T(8,128)(2,1)S(1)}, u32[]{:S(2)}, u32[]{:S(2)}) collective-permute-start(bf16[64,1792]{1,0:T(8,128)(2,1)S(1)} %collective-permute-done.31), channel_id=1, source_target_pairs={{8,12},{9,13},{10,14},{11,15},{24,28},{25,29},{26,30},{27,31}} | collective-permute-start | bytes 688136 | tf_op jit(solution)/shard_map/ppermute | solution.py:256
  118.4 8.8 %collective-permute-start.35 = (bf16[64,1792]{1,0:T(8,128)(2,1)S(1)}, bf16[64,1792]{1,0:T(8,128)(2,1)}, u32[]{:S(2)}, u32[]{:S(2)}) collective-permute-start(bf16[64,1792]{1,0:T(8,128)(2,1)S(1)} %collective-permute-done.34), channel_id=1, source_target_pairs={{4,0},{5,1},{6,2},{7,3},{20,16},{21,17},{22,18},{23,19}} | collective-permute-start | bytes 688136 | tf_op jit(solution)/shard_map/ppermute | solution.py:257
  119.8 9.8 %collective-permute-start.22 = (bf16[64,1792]{1,0:T(8,128)(2,1)S(1)}, bf16[64,1792]{1,0:T(8,128)(2,1)}, u32[]{:S(2)}, u32[]{:S(2)}) collective-permute-start(bf16[64,1792]{1,0:T(8,128)(2,1)S(1)} %fusion.37), channel_id=1, source_target_pairs={{4,0},{8,4},{12,8},{5,1},{9,5},{13,9},{6,2},{10,6},{14,10},{7,3},{... | collective-permute-start | bytes 688136 | tf_op jit(solution)/shard_map/ppermute | solution.py:246
  121.1 15.1 %copy-start.3 = (f32[1792]{0:T(1024)S(1)}, f32[1792]{0:T(1024)}, u32[]{:S(2)}) copy-start(f32[1792]{0:T(1024)} %param.16) | copy-start | bytes 21508
  130.9 14.8 %collective-permute-start.23 = (bf16[64,1792]{1,0:T(8,128)(2,1)S(1)}, bf16[64,1792]{1,0:T(8,128)(2,1)S(1)}, u32[]{:S(2)}, u32[]{:S(2)}) collective-permute-start(bf16[64,1792]{1,0:T(8,128)(2,1)S(1)} %get-tuple-element.47), channel_id=1, source_target_pairs={{0,4},{4,8},{8,12},{1,5},{5,9},{9,13},{2,6},{6,10},{10,14},{3,7},{... | collective-permute-start | bytes 688136 | tf_op jit(solution)/shard_map/ppermute | solution.py:256
  134.4 12.0 %collective-permute-start.26 = (bf16[64,1792]{1,0:T(8,128)(2,1)S(1)}, bf16[64,1792]{1,0:T(8,128)(2,1)S(1)}, u32[]{:S(2)}, u32[]{:S(2)}) collective-permute-start(bf16[64,1792]{1,0:T(8,128)(2,1)S(1)} %get-tuple-element.47), channel_id=1, source_target_pairs={{4,0},{8,4},{12,8},{5,1},{9,5},{13,9},{6,2},{10,6},{14,10},{7,3},{... | collective-permute-start | bytes 688136 | tf_op jit(solution)/shard_map/ppermute | solution.py:257
  136.2 38.0 %collective-permute-start.39 = (f32[128]{0:T(128)S(1)}, f32[128]{0:T(128)S(1)}, u32[]{:S(2)}, u32[]{:S(2)}) collective-permute-start(f32[128]{0:T(128)S(1)} %fusion.75), channel_id=1, source_target_pairs={{0,1},{1,0},{2,3},{3,2},{4,5},{5,4},{6,7},{7,6},{8,9},{9,8},{10,11... | collective-permute-start | bytes 1544 | tf_op jit(solution)/shard_map/ppermute | solution.py:182
  136.3 32.1 %slice-start = ((s8[9175040]{0:T(1024)(128)(4,1)}), s8[4194304]{0:T(1024)(128)(4,1)S(1)}, s32[]{:S(2)}) async-start(s8[9175040]{0:T(1024)(128)(4,1)} %bitcast.238), calls=%async_computation | async-start | bytes 8388608
  136.3 32.1 %slice-start.1 = ((s8[9175040]{0:T(1024)(128)(4,1)}), s8[4194304]{0:T(1024)(128)(4,1)S(1)}, s32[]{:S(2)}) async-start(s8[9175040]{0:T(1024)(128)(4,1)} %bitcast.238), calls=%async_computation.1 | async-start | bytes 8388608
  142.6 25.7 %slice-start.2 = ((s8[9175040]{0:T(1024)(128)(4,1)}), s8[786432]{0:T(1024)(128)(4,1)S(1)}, s32[]{:S(2)}) async-start(s8[9175040]{0:T(1024)(128)(4,1)} %bitcast.238), calls=%async_computation.2 | async-start | bytes 1572864
  142.6 18.3 %collective-permute-start.36 = (bf16[128,2560]{1,0:T(8,128)(2,1)S(1)}, bf16[128,2560]{1,0:T(8,128)(2,1)S(1)}, u32[]{:S(2)}, u32[]{:S(2)}) collective-permute-start(bf16[128,2560]{1,0:T(8,128)(2,1)S(1)} %dynamic-slice_bitcast_fusion.2), channel_id=1, source_target_pairs={{0,1},{1,0},{2,3},{3,2},{4,5},{5,4},{6,7},{7,6},{8,9},{9,8},{10,11... | collective-permute-start | bytes 1966088 | tf_op jit(solution)/shard_map/ppermute | solution.py:182
  145.7 2.2 collective-permute-start.24
  146.4 13.2 %collective-permute-start.27 = (bf16[64,1792]{1,0:T(8,128)(2,1)S(1)}, bf16[64,1792]{1,0:T(8,128)(2,1)S(1)}, u32[]{:S(2)}, u32[]{:S(2)}) collective-permute-start(bf16[64,1792]{1,0:T(8,128)(2,1)S(1)} %collective-permute-done.26), channel_id=1, source_target_pairs={{4,0},{8,4},{5,1},{9,5},{6,2},{10,6},{7,3},{11,7},{20,16},{24,20},... | collective-permute-start | bytes 688136 | tf_op jit(solution)/shard_map/ppermute | solution.py:257
  147.8 13.4 %collective-permute-start.42 = (bf16[128,2560]{1,0:T(8,128)(2,1)S(1)}, bf16[128,2560]{1,0:T(8,128)(2,1)S(1)}, u32[]{:S(2)}, u32[]{:S(2)}) collective-permute-start(bf16[128,2560]{1,0:T(8,128)(2,1)S(1)} %dynamic-slice_bitcast_fusion), channel_id=1, source_target_pairs={{0,1},{1,0},{2,3},{3,2},{4,5},{5,4},{6,7},{7,6},{8,9},{9,8},{10,11... | collective-permute-start | bytes 1966088 | tf_op jit(solution)/shard_map/ppermute | solution.py:182
  147.9 15.5 %collective-permute-start.25 = (bf16[64,1792]{1,0:T(8,128)(2,1)S(1)}, bf16[64,1792]{1,0:T(8,128)(2,1)S(1)}, u32[]{:S(2)}, u32[]{:S(2)}) collective-permute-start(bf16[64,1792]{1,0:T(8,128)(2,1)S(1)} %collective-permute-done.24), channel_id=1, source_target_pairs={{8,12},{9,13},{10,14},{11,15},{24,28},{25,29},{26,30},{27,31}} | collective-permute-start | bytes 688136 | tf_op jit(solution)/shard_map/ppermute | solution.py:256
  159.6 8.6 %collective-permute-start.28 = (bf16[64,1792]{1,0:T(8,128)(2,1)S(1)}, bf16[64,1792]{1,0:T(8,128)(2,1)S(1)}, u32[]{:S(2)}, u32[]{:S(2)}) collective-permute-start(bf16[64,1792]{1,0:T(8,128)(2,1)S(1)} %collective-permute-done.27), channel_id=1, source_target_pairs={{4,0},{5,1},{6,2},{7,3},{20,16},{21,17},{22,18},{23,19}} | collective-permute-start | bytes 688136 | tf_op jit(solution)/shard_map/ppermute | solution.py:257
  161.1 31.1 %collective-permute-start.37 = (bf16[128,2560]{1,0:T(8,128)(2,1)S(1)}, bf16[128,2560]{1,0:T(8,128)(2,1)S(1)}, u32[]{:S(2)}, u32[]{:S(2)}) collective-permute-start(bf16[128,2560]{1,0:T(8,128)(2,1)S(1)} %fusion.15), channel_id=1, source_target_pairs={{0,2},{1,3},{2,0},{3,1},{4,6},{5,7},{6,4},{7,5},{8,10},{9,11},{10,... | collective-permute-start | bytes 1966088 | tf_op jit(solution)/shard_map/ppermute | solution.py:182
  161.3 30.9 %collective-permute-start.43 = (bf16[128,2560]{1,0:T(8,128)(2,1)S(1)}, bf16[128,2560]{1,0:T(8,128)(2,1)S(1)}, u32[]{:S(2)}, u32[]{:S(2)}) collective-permute-start(bf16[128,2560]{1,0:T(8,128)(2,1)S(1)} %fusion.10), channel_id=1, source_target_pairs={{0,2},{1,3},{2,0},{3,1},{4,6},{5,7},{6,4},{7,5},{8,10},{9,11},{10,... | collective-permute-start | bytes 1966088 | tf_op jit(solution)/shard_map/ppermute | solution.py:182
  173.5 18.8 %collective-permute-start.29 = (bf16[128,2560]{1,0:T(8,128)(2,1)S(1)}, bf16[128,2560]{1,0:T(8,128)(2,1)S(1)}, u32[]{:S(2)}, u32[]{:S(2)}) collective-permute-start(bf16[128,2560]{1,0:T(8,128)(2,1)S(1)} %dynamic-slice_bitcast_fusion.3), channel_id=1, source_target_pairs={{0,1},{1,0},{2,3},{3,2},{4,5},{5,4},{6,7},{7,6},{8,9},{9,8},{10,11... | collective-permute-start | bytes 1966088 | tf_op jit(solution)/shard_map/ppermute | solution.py:182
  173.6 18.6 %collective-permute-start.41 = (bf16[128,2560]{1,0:T(8,128)(2,1)S(1)}, bf16[128,2560]{1,0:T(8,128)(2,1)S(1)}, u32[]{:S(2)}, u32[]{:S(2)}) collective-permute-start(bf16[128,2560]{1,0:T(8,128)(2,1)S(1)} %dynamic-slice_bitcast_fusion.1), channel_id=1, source_target_pairs={{0,1},{1,0},{2,3},{3,2},{4,5},{5,4},{6,7},{7,6},{8,9},{9,8},{10,11... | collective-permute-start | bytes 1966088 | tf_op jit(solution)/shard_map/ppermute | solution.py:182
  174.2 16.9 %collective-permute-start.40 = (f32[128]{0:T(128)S(1)}, f32[128]{0:T(128)S(1)}, u32[]{:S(2)}, u32[]{:S(2)}) collective-permute-start(f32[128]{0:T(128)S(1)} %fusion.74), channel_id=1, source_target_pairs={{0,2},{1,3},{2,0},{3,1},{4,6},{5,7},{6,4},{7,5},{8,10},{9,11},{10,... | collective-permute-start | bytes 1544 | tf_op jit(solution)/shard_map/ppermute | solution.py:182
  191.1 1.1 collective-permute-start.38
  193.1 2.2 collective-permute-start.45
  193.4 17.0 %collective-permute-start.44 = (bf16[128,2560]{1,0:T(8,128)(2,1)S(1)}, bf16[128,2560]{1,0:T(8,128)(2,1)}, u32[]{:S(2)}, u32[]{:S(2)}) collective-permute-start(bf16[128,2560]{1,0:T(8,128)(2,1)S(1)} %fusion.14), channel_id=1, source_target_pairs={{0,2},{1,3},{2,0},{3,1},{4,6},{5,7},{6,4},{7,5},{8,10},{9,11},{10,... | collective-permute-start | bytes 1966088 | tf_op jit(solution)/shard_map/ppermute | solution.py:182
  201.4 9.5 %collective-permute-start.46 = (bf16[64,1792]{1,0:T(8,128)(2,1)S(1)}, bf16[64,1792]{1,0:T(8,128)(2,1)S(1)}, u32[]{:S(2)}, u32[]{:S(2)}) collective-permute-start(bf16[64,1792]{1,0:T(8,128)(2,1)S(1)} %get-tuple-element.16), channel_id=1, source_target_pairs={{0,4},{1,5},{2,6},{3,7},{16,20},{17,21},{18,22},{19,23}} | collective-permute-start | bytes 688136 | tf_op jit(solution)/shard_map/ppermute | solution.py:245
  210.9 2.4 collective-permute-start.47
  211.0 23.9 %collective-permute-start.56 = (bf16[64,1792]{1,0:T(8,128)(2,1)S(1)}, bf16[64,1792]{1,0:T(8,128)(2,1)S(1)}, u32[]{:S(2)}, u32[]{:S(2)}) collective-permute-start(bf16[64,1792]{1,0:T(8,128)(2,1)S(1)} %get-tuple-element.15), channel_id=1, source_target_pairs={{12,8},{13,9},{14,10},{15,11},{28,24},{29,25},{30,26},{31,27}} | collective-permute-start | bytes 688136 | tf_op jit(solution)/shard_map/ppermute | solution.py:246
  220.0 10.3 %collective-permute-start.48 = (bf16[64,1792]{1,0:T(8,128)(2,1)S(1)}, bf16[64,1792]{1,0:T(8,128)(2,1)S(1)}, u32[]{:S(2)}, u32[]{:S(2)}) collective-permute-start(bf16[64,1792]{1,0:T(8,128)(2,1)S(1)} %get-tuple-element.19), channel_id=1, source_target_pairs={{0,4},{1,5},{2,6},{3,7},{16,20},{17,21},{18,22},{19,23}} | collective-permute-start | bytes 688136 | tf_op jit(solution)/shard_map/ppermute | solution.py:245
  224.5 10.8 %collective-permute-start.54 = (bf16[64,1792]{1,0:T(8,128)(2,1)S(1)}, bf16[64,1792]{1,0:T(8,128)(2,1)S(1)}, u32[]{:S(2)}, u32[]{:S(2)}) collective-permute-start(bf16[64,1792]{1,0:T(8,128)(2,1)S(1)} %fusion.24), channel_id=1, source_target_pairs={{0,4},{4,8},{1,5},{5,9},{2,6},{6,10},{3,7},{7,11},{16,20},{20,24},... | collective-permute-start | bytes 688136 | tf_op jit(solution)/shard_map/ppermute | solution.py:245
  225.8 16.0 %collective-permute-start.51 = (bf16[64,1792]{1,0:T(8,128)(2,1)S(1)}, bf16[64,1792]{1,0:T(8,128)(2,1)S(1)}, u32[]{:S(2)}, u32[]{:S(2)}) collective-permute-start(bf16[64,1792]{1,0:T(8,128)(2,1)S(1)} %get-tuple-element.20), channel_id=1, source_target_pairs={{12,8},{13,9},{14,10},{15,11},{28,24},{29,25},{30,26},{31,27}} | collective-permute-start | bytes 688136 | tf_op jit(solution)/shard_map/ppermute | solution.py:246
  230.4 11.4 %collective-permute-start.49 = (bf16[64,1792]{1,0:T(8,128)(2,1)S(1)}, bf16[64,1792]{1,0:T(8,128)(2,1)S(1)}, u32[]{:S(2)}, u32[]{:S(2)}) collective-permute-start(bf16[64,1792]{1,0:T(8,128)(2,1)S(1)} %fusion.31), channel_id=1, source_target_pairs={{0,4},{4,8},{1,5},{5,9},{2,6},{6,10},{3,7},{7,11},{16,20},{20,24},... | collective-permute-start | bytes 688136 | tf_op jit(solution)/shard_map/ppermute | solution.py:245
  236.1 7.2 %collective-permute-start.57 = (bf16[64,1792]{1,0:T(8,128)(2,1)S(1)}, bf16[64,1792]{1,0:T(8,128)(2,1)S(1)}, u32[]{:S(2)}, u32[]{:S(2)}) collective-permute-start(bf16[64,1792]{1,0:T(8,128)(2,1)S(1)} %get-tuple-element.14), channel_id=1, source_target_pairs={{8,4},{12,8},{9,5},{13,9},{10,6},{14,10},{11,7},{15,11},{24,20},{2... | collective-permute-start | bytes 688136 | tf_op jit(solution)/shard_map/ppermute | solution.py:246
  236.7 16.4 %collective-permute-start.55 = (bf16[64,1792]{1,0:T(8,128)(2,1)}, bf16[64,1792]{1,0:T(8,128)(2,1)S(1)}, u32[]{:S(2)}, u32[]{:S(2)}) collective-permute-start(bf16[64,1792]{1,0:T(8,128)(2,1)} %get-tuple-element.13), channel_id=1, source_target_pairs={{0,4},{4,8},{8,12},{1,5},{5,9},{9,13},{2,6},{6,10},{10,14},{3,7},{... | collective-permute-start | bytes 688136 | tf_op jit(solution)/shard_map/ppermute | solution.py:245
  242.6 8.5 %collective-permute-start.52 = (bf16[64,1792]{1,0:T(8,128)(2,1)S(1)}, bf16[64,1792]{1,0:T(8,128)(2,1)S(1)}, u32[]{:S(2)}, u32[]{:S(2)}) collective-permute-start(bf16[64,1792]{1,0:T(8,128)(2,1)S(1)} %get-tuple-element.18), channel_id=1, source_target_pairs={{8,4},{12,8},{9,5},{13,9},{10,6},{14,10},{11,7},{15,11},{24,20},{2... | collective-permute-start | bytes 688136 | tf_op jit(solution)/shard_map/ppermute | solution.py:246
  244.0 9.3 %collective-permute-start.58 = (bf16[64,1792]{1,0:T(8,128)(2,1)}, bf16[64,1792]{1,0:T(8,128)(2,1)S(1)}, u32[]{:S(2)}, u32[]{:S(2)}) collective-permute-start(bf16[64,1792]{1,0:T(8,128)(2,1)} %fusion.23), channel_id=1, source_target_pairs={{4,0},{8,4},{12,8},{5,1},{9,5},{13,9},{6,2},{10,6},{14,10},{7,3},{... | collective-permute-start | bytes 688136 | tf_op jit(solution)/shard_map/ppermute | solution.py:246
  245.3 9.6 %collective-permute-start.50 = (bf16[64,1792]{1,0:T(8,128)(2,1)}, bf16[64,1792]{1,0:T(8,128)(2,1)S(1)}, u32[]{:S(2)}, u32[]{:S(2)}) collective-permute-start(bf16[64,1792]{1,0:T(8,128)(2,1)} %get-tuple-element.17), channel_id=1, source_target_pairs={{0,4},{4,8},{8,12},{1,5},{5,9},{9,13},{2,6},{6,10},{10,14},{3,7},{... | collective-permute-start | bytes 688136 | tf_op jit(solution)/shard_map/ppermute | solution.py:245
  251.9 10.4 %collective-permute-start.53 = (bf16[64,1792]{1,0:T(8,128)(2,1)}, bf16[64,1792]{1,0:T(8,128)(2,1)S(1)}, u32[]{:S(2)}, u32[]{:S(2)}) collective-permute-start(bf16[64,1792]{1,0:T(8,128)(2,1)} %fusion.30), channel_id=1, source_target_pairs={{4,0},{8,4},{12,8},{5,1},{9,5},{13,9},{6,2},{10,6},{14,10},{7,3},{... | collective-permute-start | bytes 688136 | tf_op jit(solution)/shard_map/ppermute | solution.py:246
  (5 other events, 36.1 us)

commit v4 on v2

--- a/solution.py
+++ b/solution.py
@@ -228,16 +228,17 @@
     )
 
 
-def reduce_ctx(kept, sent):
-    came = swap(sent, "ctx", 1)
-    mine = wide(kept[0]) + wide(came[0])
-    other = (wide(kept[1]) + wide(came[1])).astype(jnp.bfloat16)
-    return mine + wide(swap(other, "ctx", 2))
+def after(value, earlier):
+    return lax.optimization_barrier((value, earlier))[0]
+
+
+def reduce_ctx(blocks):
+    flat = blocks.reshape(-1, blocks.shape[-1])
+    return wide(lax.psum_scatter(flat, "ctx", scatter_dimension=0, tiled=True))
 
 
 def gather_ctx(rows):
-    pair = jnp.concatenate([rows, swap(rows, "ctx", 2)], axis=0)
-    return jnp.concatenate([pair, swap(pair, "ctx", 1)], axis=0)
+    return lax.all_gather(rows, "ctx", axis=0, tiled=True)
 
 
 def paired_tail(
@@ -252,26 +253,23 @@
     first_half = (t >> 1) ^ (c >> 1)
     own = spread_heads(heads_out, n_ctx, n_tp)
     own_all = jnp.stack(own)
+    near = swap(own_all, "tp", 1)
     far = swap(own_all, "tp", 2)
-    near = swap(own_all, "tp", 1)
+    residual_halves = residual.reshape(2, half, width)
+
+    def sum_heads(blocks, which):
+        head_sum = reduce_ctx(jnp.stack([pick(blocks, t ^ i) for i in range(n_ctx)]))
+        return (wide(pick(residual_halves, which)) + head_sum).astype(jnp.bfloat16)
+
+    blocks_a = matmul(pair_rows(own_all, near), output_weight).reshape(n_ctx, half, width)
+    far = after(far, blocks_a)
     far_near = swap(far, "tp", 1)
-    rows_a = pair_rows(own_all, near)
     order = [2, 3, 0, 1]
     rows_b = pair_rows([far[i] for i in order], [far_near[i] for i in order])
-    residual_halves = residual.reshape(2, half, width)
-
-    def project(rows, which):
-        blocks = matmul(rows, output_weight).reshape(n_ctx, half, width)
-        place = t ^ c
-        head_sum = reduce_ctx(
-            (pick(blocks, place), pick(blocks, place ^ 2)),
-            jnp.stack([pick(blocks, place ^ 1), pick(blocks, place ^ 3)]),
-        )
-        attended = (wide(pick(residual_halves, which)) + head_sum).astype(jnp.bfloat16)
-        return attended, gather_ctx(attended)
-
-    attended_a, all_a = project(rows_a, first_half)
-    attended_b, all_b = project(rows_b, 1 - first_half)
+    blocks_b = matmul(rows_b, output_weight).reshape(n_ctx, half, width)
+    attended_a = sum_heads(blocks_a, first_half)
+    all_a = gather_ctx(attended_a)
+    attended_b = sum_heads(after(blocks_b, attended_a), 1 - first_half)
 
     def gate_up(all_rows):
         values = wide(all_rows)
@@ -285,25 +283,27 @@
         return kept, came
 
     kept_a, came_a = gate_up(all_a)
-    across = [
-        swap((wide(k) + wide(r)).astype(k.dtype), "tp", 2) for k, r in zip(kept_a, came_a)
-    ]
+    chip_a = [(wide(k) + wide(r)).astype(k.dtype) for k, r in zip(kept_a, came_a)]
+    across = [swap(term, "tp", 2) for term in chip_a]
+    all_b = after(gather_ctx(attended_b), chip_a)
     kept_b, came_b = gate_up(all_b)
     gate, up, squares = [wide(k) + wide(r) + wide(x) for k, r, x in zip(kept_b, came_b, across)]
     inverse_rms = lax.rsqrt(squares / model_width + norm_eps)[:, None]
     hidden = (jax.nn.silu(gate * inverse_rms) * (up * inverse_rms)).astype(jnp.bfloat16)
+    hidden_near = swap(hidden, "tp", 1)
     hidden_far = swap(hidden, "tp", 2)
-    hidden_near = swap(hidden, "tp", 1)
+
+    def down(mine, other):
+        blocks = matmul(jnp.concatenate([mine, other], axis=0), down_weight)
+        blocks = blocks.reshape(n_ctx, half, width)
+        return jnp.stack([pick(blocks, i ^ (2 * core)) for i in range(n_ctx)])
+
+    down_b = down(hidden, hidden_near)
+    out_b = (wide(attended_b) + reduce_ctx(down_b)).astype(jnp.bfloat16)
+    hidden_far = after(hidden_far, down_b)
     hidden_far_near = swap(hidden_far, "tp", 1)
-
-    def down(mine, other, attended):
-        blocks = matmul(jnp.concatenate([mine, other], axis=0), down_weight)
-        blocks = blocks.reshape(2, 2, half, width)
-        total = reduce_ctx(pick(blocks, core), pick(blocks, 1 - core))
-        return (wide(attended) + total).astype(jnp.bfloat16)
-
-    out_b = down(hidden, hidden_near, attended_b)
-    out_a = down(hidden_far, hidden_far_near, attended_a)
+    down_a = down(hidden_far, hidden_far_near)
+    out_a = (wide(attended_a) + reduce_ctx(down_a)).astype(jnp.bfloat16)
 
     def in_order(a, b):
         first = first_half == 0

time: 259 us -> 268 us (1.035)
  waiting for transfers between devices: 166 us -> 112 us
  blocking collectives: 0 us -> 38.4 us
  between operations: 1.42 us -> 14.4 us
  matrix products: 33.6 us -> 43.7 us
  other arithmetic: 9.98 us -> 16.6 us
  starting transfers between devices: 38.9 us -> 32.5 us
    ppermute x28 -> x16, waiting for transfers between devices: 150 us -> 22.1 us  [swap(): return lax.ppermute(value, axis_name, [(i, i ^ bit) for i in range(width)])]
    reduce_scatter x0 -> x4, waiting for transfers between devices: none -> 73.9 us  [reduce_ctx(): return wide(lax.psum_scatter(flat, 'ctx', scatter_dimension=0, tiled=True))]
    all_gather x0 -> x2, blocking collectives: none -> 38.4 us  [gather_ctx(): return lax.all_gather(rows, 'ctx', axis=0, tiled=True)]
    dot_general x8, matrix products: 33.6 us -> 43.7 us  [matmul(): jnp.dot(a, b, preferred_element_type=jnp.float32).astype(jnp.bfloat16)]
    ppermute x28 -> x16, starting transfers between devices: 20.7 us -> 14 us  [swap(): return lax.ppermute(value, axis_name, [(i, i ^ bit) for i in range(width)])]
    another operation x4 -> x6, other arithmetic: 1.07 us -> 5.19 us  [the longest x2 2.11 us: sum_heads(): jnp.stack([pick(blocks, t ^ i) for i in range(n_ctx)])]
  transfers between devices with their start and end apart: 35 -> 27, of which waited for: 20 -> 14; matrix products, arithmetic and copies ran while one was open for 14% -> 18% of each run, Pallas kernels for 0% -> 0%
where the time goes in v4:
time: 268 us; the launch traced here: 267 us
  waiting for transfers between devices  112 us (42%)
  matrix products  43.7 us (16%)
  blocking collectives  38.4 us (14%)
  starting transfers between devices  32.5 us (12%)
  other arithmetic  16.6 us (6%)
  between operations  14.4 us (5%)
  Pallas kernels  6.62 us (2%)
  local copies, waits for them, and re-layouts  2.84 us (1%)
    reduce_scatter x4, waiting for transfers between devices, reduce_ctx(): return wide(lax.psum_scatter(flat, 'ctx', scatter_dimension=0, tiled=True))  73.9 us
    dot_general x8, matrix products, matmul(): jnp.dot(a, b, preferred_element_type=jnp.float32).astype(jnp.bfloat16)  43.7 us
    all_gather x2, blocking collectives, gather_ctx(): return lax.all_gather(rows, 'ctx', axis=0, tiled=True)  38.4 us
    ppermute x16, waiting for transfers between devices, swap(): return lax.ppermute(value, axis_name, [(i, i ^ bit) for i in range(width)])  22.1 us
    ppermute x4, waiting for transfers between devices, spread_heads(): lax.ppermute(pieces[s], ('ctx', 'tp'), [(c * n_tp + t, t * n_tp + (c ^ s)...  15 us
    ppermute x16, starting transfers between devices, swap(): return lax.ppermute(value, axis_name, [(i, i ^ bit) for i in range(width)])  14 us
    ppermute x3, starting transfers between devices, gather_keys(): lax.ppermute(half, 'ctx', [(c, c + d) for c in range(n_ctx - d)])  10.7 us
    ppermute x4, starting transfers between devices, spread_heads(): lax.ppermute(pieces[s], ('ctx', 'tp'), [(c * n_tp + t, t * n_tp + (c ^ s)...  7.29 us
  transfers between devices with their start and end apart: 27, of which 14 were waited for; matrix products, arithmetic and copies ran while one was open for 18% of the time, Pallas kernels for 0%

profile of v4, /device:TPU:0, one launch (start us, length us, event | category | flops | bytes accessed | tf_op | source)
XLA Modules:
  0.0 267.4 jit_solution(13242442465711668523)
XLA Ops:
  7.2 0.9 convert_element_type.152
  8.2 1.1 slice.62
  9.3 0.8 reduce-window.8
  10.1 0.7 subtract_subtract_fusion
  11.1 0.3 fusion.33
  11.4 7.0 %collective-permute-start = (bf16[288,128]{1,0:T(8,128)(2,1)S(1)}, bf16[288,128]{1,0:T(8,128)(2,1)S(1)}, u32[]{:S(2)}, u32[]{:S(2)}) collective-permute-start(bf16[288,128]{1,0:T(8,128)(2,1)S(1)} %fusion.33), channel_id=1, source_target_pairs={{0,12},{1,13},{2,14},{3,15},{16,28},{17,29},{18,30},{19,31}} | collective-permute-start | bytes 221192 | tf_op jit(solution)/shard_map/ppermute | solution.py:202
  18.4 1.3 collective-permute-start.1
  19.7 2.5 collective-permute-start.2
  22.2 0.3 multiply_cosine_fusion
  22.6 0.2 maximum_bitcast_fusion
  22.9 1.2 collective-permute-done.2
  24.3 1.4 collective-permute-done.3
  25.8 6.6 %shard_map.113 = bf16[128,2048]{1,0:T(8,128)(2,1)S(1)} custom-call(f32[4,128,128]{2,1,0:T(8,128)S(1)} %pad_maximum_fusion.7.tables, s32[128,1]{1,0:T(8,128)S(1)} %copy.13.starts, s32[128,1]{1,0:T(8,128)S(1)} %iota_add_fusion.own_index, s32[1,512]{1,0:T(1,128)S(1)} %iota_add_fusion.1.key_index, bf16[576,512]{1,0:T(8,128)(2,1)S(1)} %maximum_maximum_fusion.keys, ...), custom_call_target="tpu_custom_call" | custom-call | flops 2684354560 | bytes 5046272 | tf_op jit(solution)/shard_map/pallas_call | solution.py:143
  32.5 0.2 collective-permute-start.5
  32.7 5.0 %collective-permute-start.6 = (bf16[32,2048]{1,0:T(8,128)(2,1)S(1)}, bf16[32,2048]{1,0:T(8,128)(2,1)S(1)}, u32[]{:S(2)}, u32[]{:S(2)}) collective-permute-start(bf16[32,2048]{1,0:T(8,128)(2,1)S(1)} %get-tuple-element.32), channel_id=1, source_target_pairs={{0,2},{1,6},{2,10},{3,14},{4,3},{5,7},{6,11},{7,15},{8,0},{9,4},{1... | collective-permute-start | bytes 393224 | tf_op jit(solution)/shard_map/ppermute | solution.py:216
  37.6 1.5 collective-permute-start.7
  39.1 0.7 collective-permute-start.4
  39.8 15.0 %collective-permute-done.6 = bf16[32,2048]{1,0:T(8,128)(2,1)S(1)} collective-permute-done((bf16[32,2048]{1,0:T(8,128)(2,1)S(1)}, bf16[32,2048]{1,0:T(8,128)(2,1)S(1)}, u32[]{:S(2)}, u32[]{:S(2)}) %collective-permute-start.6) | collective-permute-done | bytes 131104 | tf_op jit(solution)/shard_map/ppermute | solution.py:216
  54.9 2.7 %collective-permute-start.8 = (bf16[4,32,2048]{2,1,0:T(8,128)(2,1)S(1)}, bf16[4,32,2048]{2,1,0:T(8,128)(2,1)S(1)}, u32[]{:S(2)}, u32[]{:S(2)}) collective-permute-start(bf16[4,32,2048]{2,1,0:T(8,128)(2,1)S(1)} %pad_maximum_fusion.4), channel_id=1, source_target_pairs={{0,1},{1,0},{2,3},{3,2},{4,5},{5,4},{6,7},{7,6},{8,9},{9,8},{10,11... | collective-permute-start | bytes 1572872 | tf_op jit(solution)/shard_map/ppermute | solution.py:182
  57.5 4.6 %collective-permute-start.9 = (bf16[4,32,2048]{2,1,0:T(8,128)(2,1)S(1)}, bf16[4,32,2048]{2,1,0:T(8,128)(2,1)S(1)}, u32[]{:S(2)}, u32[]{:S(2)}) collective-permute-start(bf16[4,32,2048]{2,1,0:T(8,128)(2,1)S(1)} %pad_maximum_fusion.4), channel_id=1, source_target_pairs={{0,2},{1,3},{2,0},{3,1},{4,6},{5,7},{6,4},{7,5},{8,10},{9,11},{10,... | collective-permute-start | bytes 1572872 | tf_op jit(solution)/shard_map/ppermute | solution.py:182
  62.3 5.2 %convolution_convert_fusion.5 = bf16[256,1792]{1,0:T(8,128)(2,1)S(1)} fusion(bf16[256,2048]{1,0:T(8,128)(2,1)S(1)} %constant_dynamic-update-slice_fusion.3, bf16[2048,1792]{1,0:T(8,128)(2,1)} %param.15), kind=kOutput, calls=%fused_computation.5 | convolution fusion | flops 1879506944 | bytes 9306112 | tf_op jit(solution)/shard_map/dot_general | solution.py:194
  67.5 7.1 %collective-permute-done.9 = bf16[4,32,2048]{2,1,0:T(8,128)(2,1)S(1)} collective-permute-done((bf16[4,32,2048]{2,1,0:T(8,128)(2,1)S(1)}, bf16[4,32,2048]{2,1,0:T(8,128)(2,1)S(1)}, u32[]{:S(2)}, u32[]{:S(2)}) %collective-permute-start.9) | collective-permute-done | bytes 524320 | tf_op jit(solution)/shard_map/ppermute | solution.py:182
  74.7 1.1 pad_maximum_fusion
  75.8 0.7 collective-permute-done.10
  76.6 5.2 %convolution_convert_fusion.4 = bf16[256,1792]{1,0:T(8,128)(2,1)S(1)} fusion(bf16[256,2048]{1,0:T(8,128)(2,1)S(1)} %bitcast_dynamic-update-slice_fusion, bf16[2048,1792]{1,0:T(8,128)(2,1)} %param.15), kind=kOutput, calls=%fused_computation.4 | convolution fusion | flops 1879506944 | bytes 9306112 | tf_op jit(solution)/shard_map/dot_general | solution.py:194
  81.9 18.0 %reduce-scatter.5.cloned.1.call-done = bf16[64,1792]{1,0:T(8,128)(2,1)} async-done(((bf16[256,1792]{1,0:T(8,128)(2,1)}), bf16[64,1792]{1,0:T(8,128)(2,1)}) %reduce-scatter.5.cloned.1.call-update) | async-done | bytes 229392 | tf_op jit(solution)/shard_map/reduce_scatter | solution.py:237
  99.9 1.0 fusion.23
  100.9 19.2 %all_gather.7 = bf16[256,1792]{1,0:T(8,128)(2,1)S(1)} all-gather(bf16[64,1792]{1,0:T(8,128)(2,1)S(1)} %fusion.23), channel_id=1, replica_groups=mesh['grp'=2,'ctx'=4,'tp'=4] {'ctx'}, dimensions={0}, use_global_device_ids=true | all-gather | bytes 1146880 | tf_op jit(solution)/shard_map/all_gather | solution.py:241
  120.0 0.3 fusion.1
  120.3 6.1 %convolution_convert_fusion.3 = bf16[256,2560]{1,0:T(8,128)(2,1)S(1)} fusion(bf16[1792,2560]{1,0:T(8,128)(2,1)} %param.17, bf16[256,1792]{1,0:T(8,128)(2,1)S(1)} %all_gather.7, f32[1792]{0:T(1024)S(1)} %copy-done.4), kind=kOutput, calls=%fused_computation.3 | convolution fusion | flops 2350841856 | bytes 11410432 | tf_op jit(solution)/shard_map/dot_general | solution.py:194
  126.4 0.9 dynamic-slice_bitcast_fusion.3
  127.3 0.5 collective-permute-start.13
  127.9 1.1 pad_maximum_fusion.1
  129.0 0.2 reduce-scatter.11.cloned.1.call-start
  129.2 6.1 %convolution_convert_fusion.2 = bf16[256,2560]{1,0:T(8,128)(2,1)S(1)} fusion(bf16[1792,2560]{1,0:T(8,128)(2,1)} %param.18, bf16[256,1792]{1,0:T(8,128)(2,1)S(1)} %all_gather.7, f32[1792]{0:T(1024)S(1)} %copy-done.4), kind=kOutput, calls=%fused_computation.2 | convolution fusion | flops 2350841856 | bytes 11410432 | tf_op jit(solution)/shard_map/dot_general | solution.py:194
  135.6 2.1 fusion.17
  137.7 1.5 collective-permute-start.15
  139.4 0.6 collective-permute-start.19
  140.0 13.9 %reduce-scatter.7.cloned.1.call-done = bf16[64,1792]{1,0:T(8,128)(2,1)} async-done(((bf16[256,1792]{1,0:T(8,128)(2,1)}), bf16[64,1792]{1,0:T(8,128)(2,1)}) %reduce-scatter.7.cloned.1.call-update) | async-done | bytes 229392 | tf_op jit(solution)/shard_map/reduce_scatter | solution.py:237
  153.9 1.2 broadcast_select_fusion.3
  155.1 19.3 %all_gather.6 = bf16[256,1792]{1,0:T(8,128)(2,1)S(1)} all-gather(bf16[64,1792]{1,0:T(8,128)(2,1)S(1)} %get-tuple-element.11), channel_id=1, replica_groups=mesh['grp'=2,'ctx'=4,'tp'=4] {'ctx'}, dimensions={0}, use_global_device_ids=true | all-gather | bytes 1146880 | tf_op jit(solution)/shard_map/all_gather | solution.py:241
  174.4 6.3 %convolution_convert_fusion.1 = bf16[256,2560]{1,0:T(8,128)(2,1)S(1)} fusion(bf16[1792,2560]{1,0:T(8,128)(2,1)} %param.17, bf16[256,1792]{1,0:T(8,128)(2,1)S(1)} %all_gather.6, f32[1792]{0:T(1024)S(1)} %copy-done.4), kind=kOutput, calls=%fused_computation.1 | convolution fusion | flops 2350841856 | bytes 11410432 | tf_op jit(solution)/shard_map/dot_general | solution.py:194
  180.7 2.5 convolution_convert_fusion
  183.5 0.5 collective-permute-start.18
  184.0 1.5 collective-permute-start.17
  185.5 0.3 fusion.3
  185.8 1.8 collective-permute-done.17
  187.5 1.1 collective-permute-done.16
  188.7 0.8 fusion.13
  189.5 0.3 collective-permute-start.21
  189.8 1.5 collective-permute-start.20
  191.3 0.4 collective-permute-done.21
  191.7 6.1 %convolution_convert_fusion.7 = bf16[256,1792]{1,0:T(8,128)(2,1)S(1)} fusion(bf16[2560,1792]{1,0:T(8,128)(2,1)} %param.19, bf16[128,2560]{1,0:T(8,128)(2,1)S(1)} %collective-permute-done.21, bf16[128,2560]{1,0:T(8,128)(2,1)S(1)} %fusion.13), kind=kOutput, calls=%fused_computation.7 | convolution fusion | flops 2351890432 | bytes 11403264 | tf_op jit(solution)/shard_map/dot_general | solution.py:194
  197.9 1.1 pad_maximum_fusion.2
  199.0 7.8 %collective-permute-done.20 = bf16[128,2560]{1,0:T(8,128)(2,1)S(1)} collective-permute-done((bf16[128,2560]{1,0:T(8,128)(2,1)S(1)}, bf16[128,2560]{1,0:T(8,128)(2,1)S(1)}, u32[]{:S(2)}, u32[]{:S(2)}) %collective-permute-start.20) | collective-permute-done | bytes 655392 | tf_op jit(solution)/shard_map/ppermute | solution.py:182
  206.8 0.3 reduce-scatter.9.cloned.1.call-start
  207.1 1.8 collective-permute-done.22
  208.9 6.1 %convolution_convert_fusion.6 = bf16[256,1792]{1,0:T(8,128)(2,1)S(1)} fusion(bf16[2560,1792]{1,0:T(8,128)(2,1)} %param.19, bf16[128,2560]{1,0:T(8,128)(2,1)S(1)} %collective-permute-done.22, bf16[128,2560]{1,0:T(8,128)(2,1)S(1)} %collective-permute-done.20), kind=kOutput, calls=%fused_computation.6 | convolution fusion | flops 2351890432 | bytes 11403264 | tf_op jit(solution)/shard_map/dot_general | solution.py:194
  215.1 1.0 pad_maximum_fusion.3
  216.1 15.7 %reduce-scatter.11.cloned.1.call-done = bf16[64,1792]{1,0:T(8,128)(2,1)} async-done(((bf16[256,1792]{1,0:T(8,128)(2,1)}), bf16[64,1792]{1,0:T(8,128)(2,1)}) %reduce-scatter.11.cloned.1.call-update) | async-done | bytes 229392 | tf_op jit(solution)/shard_map/reduce_scatter | solution.py:237
  231.9 26.2 %reduce-scatter.9.cloned.1.call-done = bf16[64,1792]{1,0:T(8,128)(2,1)} async-done(((bf16[256,1792]{1,0:T(8,128)(2,1)}), bf16[64,1792]{1,0:T(8,128)(2,1)}) %reduce-scatter.9.cloned.1.call-update) | async-done | bytes 229392 | tf_op jit(solution)/shard_map/reduce_scatter | solution.py:237
  258.1 1.2 broadcast_select_fusion.1
  259.3 0.8 pad_maximum_fusion.6
  260.1 0.8 pad_maximum_fusion.5
  (90 shorter events, 2.1 us)
Async XLA Ops:
  7.2 92.7 %reduce-scatter.5.cloned.1.call-start = ((), (), s32[]{:S(2)}) async-start(), calls=%async_computation.4 | async-start | bytes 1146880 | tf_op jit(solution)/shard_map/reduce_scatter | solution.py:237
  8.2 17.6 %copy-start.1 = (bf16[512,2048]{1,0:T(8,128)(2,1)S(1)}, bf16[512,2048]{1,0:T(8,128)(2,1)}, u32[]{:S(2)}) copy-start(bf16[512,2048]{1,0:T(8,128)(2,1)} %value_weight.1) | copy-start | bytes 6291460
  11.4 11.4 %collective-permute-start = (bf16[288,128]{1,0:T(8,128)(2,1)S(1)}, bf16[288,128]{1,0:T(8,128)(2,1)S(1)}, u32[]{:S(2)}, u32[]{:S(2)}) collective-permute-start(bf16[288,128]{1,0:T(8,128)(2,1)S(1)} %fusion.33), channel_id=1, source_target_pairs={{0,12},{1,13},{2,14},{3,15},{16,28},{17,29},{18,30},{19,31}} | collective-permute-start | bytes 221192 | tf_op jit(solution)/shard_map/ppermute | solution.py:202
  18.4 4.5 %collective-permute-start.1 = (bf16[288,128]{1,0:T(8,128)(2,1)S(1)}, bf16[288,128]{1,0:T(8,128)(2,1)S(1)}, u32[]{:S(2)}, u32[]{:S(2)}) collective-permute-start(bf16[288,128]{1,0:T(8,128)(2,1)S(1)} %fusion.33), channel_id=1, source_target_pairs={{0,8},{4,12},{1,9},{5,13},{2,10},{6,14},{3,11},{7,15},{16,24},{20,... | collective-permute-start | bytes 221192 | tf_op jit(solution)/shard_map/ppermute | solution.py:202
  19.7 4.4 %collective-permute-start.2 = (bf16[288,128]{1,0:T(8,128)(2,1)S(1)}, bf16[288,128]{1,0:T(8,128)(2,1)S(1)}, u32[]{:S(2)}, u32[]{:S(2)}) collective-permute-start(bf16[288,128]{1,0:T(8,128)(2,1)S(1)} %fusion.33), channel_id=1, source_target_pairs={{0,4},{4,8},{8,12},{1,5},{5,9},{9,13},{2,6},{6,10},{10,14},{3,7},{... | collective-permute-start | bytes 221192 | tf_op jit(solution)/shard_map/ppermute | solution.py:202
  22.6 3.2 %copy-start = (bf16[128,9216]{1,0:T(8,128)(2,1)S(1)}, bf16[128,9216]{1,0:T(8,128)(2,1)}, u32[]{:S(2)}) copy-start(bf16[128,9216]{1,0:T(8,128)(2,1)} %queries.1) | copy-start | bytes 7077892
  24.1 1.5 collective-permute-start.3
  32.5 7.3 %collective-permute-start.5 = (bf16[32,2048]{1,0:T(8,128)(2,1)S(1)}, bf16[32,2048]{1,0:T(8,128)(2,1)S(1)}, u32[]{:S(2)}, u32[]{:S(2)}) collective-permute-start(bf16[32,2048]{1,0:T(8,128)(2,1)S(1)} %get-tuple-element.30), channel_id=1, source_target_pairs={{0,1},{1,5},{2,9},{3,13},{4,0},{5,4},{6,8},{7,12},{8,3},{9,7},{10,... | collective-permute-start | bytes 393224 | tf_op jit(solution)/shard_map/ppermute | solution.py:216
  32.7 22.1 %collective-permute-start.6 = (bf16[32,2048]{1,0:T(8,128)(2,1)S(1)}, bf16[32,2048]{1,0:T(8,128)(2,1)S(1)}, u32[]{:S(2)}, u32[]{:S(2)}) collective-permute-start(bf16[32,2048]{1,0:T(8,128)(2,1)S(1)} %get-tuple-element.32), channel_id=1, source_target_pairs={{0,2},{1,6},{2,10},{3,14},{4,3},{5,7},{6,11},{7,15},{8,0},{9,4},{1... | collective-permute-start | bytes 393224 | tf_op jit(solution)/shard_map/ppermute | solution.py:216
  37.6 17.1 %collective-permute-start.7 = (bf16[32,2048]{1,0:T(8,128)(2,1)S(1)}, bf16[32,2048]{1,0:T(8,128)(2,1)S(1)}, u32[]{:S(2)}, u32[]{:S(2)}) collective-permute-start(bf16[32,2048]{1,0:T(8,128)(2,1)S(1)} %get-tuple-element.31), channel_id=1, source_target_pairs={{0,3},{1,7},{2,11},{3,15},{4,2},{5,6},{6,10},{7,14},{8,1},{9,5},{1... | collective-permute-start | bytes 393224 | tf_op jit(solution)/shard_map/ppermute | solution.py:216
  39.1 15.7 %collective-permute-start.4 = (bf16[32,2048]{1,0:T(8,128)(2,1)S(1)}, bf16[32,2048]{1,0:T(8,128)(2,1)S(1)}, u32[]{:S(2)}, u32[]{:S(2)}) collective-permute-start(bf16[32,2048]{1,0:T(8,128)(2,1)S(1)} %get-tuple-element.33), channel_id=1, source_target_pairs={{0,0},{1,4},{2,8},{3,12},{4,1},{5,5},{6,9},{7,13},{8,2},{9,6},{10,... | collective-permute-start | bytes 393224 | tf_op jit(solution)/shard_map/ppermute | solution.py:216
  54.9 7.3 %collective-permute-start.8 = (bf16[4,32,2048]{2,1,0:T(8,128)(2,1)S(1)}, bf16[4,32,2048]{2,1,0:T(8,128)(2,1)S(1)}, u32[]{:S(2)}, u32[]{:S(2)}) collective-permute-start(bf16[4,32,2048]{2,1,0:T(8,128)(2,1)S(1)} %pad_maximum_fusion.4), channel_id=1, source_target_pairs={{0,1},{1,0},{2,3},{3,2},{4,5},{5,4},{6,7},{7,6},{8,9},{9,8},{10,11... | collective-permute-start | bytes 1572872 | tf_op jit(solution)/shard_map/ppermute | solution.py:182
  57.5 17.0 %collective-permute-start.9 = (bf16[4,32,2048]{2,1,0:T(8,128)(2,1)S(1)}, bf16[4,32,2048]{2,1,0:T(8,128)(2,1)S(1)}, u32[]{:S(2)}, u32[]{:S(2)}) collective-permute-start(bf16[4,32,2048]{2,1,0:T(8,128)(2,1)S(1)} %pad_maximum_fusion.4), channel_id=1, source_target_pairs={{0,2},{1,3},{2,0},{3,1},{4,6},{5,7},{6,4},{7,5},{8,10},{9,11},{10,... | collective-permute-start | bytes 1572872 | tf_op jit(solution)/shard_map/ppermute | solution.py:182
  74.6 1.9 collective-permute-start.10
  75.7 78.2 %reduce-scatter.7.cloned.1.call-start = ((), (), s32[]{:S(2)}) async-start(), calls=%async_computation.5 | async-start | bytes 1146880 | tf_op jit(solution)/shard_map/reduce_scatter | solution.py:237
  76.6 23.2 %copy-start.2 = (bf16[128,1792]{1,0:T(8,128)(2,1)S(1)}, bf16[128,1792]{1,0:T(8,128)(2,1)}, u32[]{:S(2)}) copy-start(bf16[128,1792]{1,0:T(8,128)(2,1)} %param.10) | copy-start | bytes 1376260
  81.8 38.4 %copy-start.4 = (f32[1792]{0:T(1024)S(1)}, f32[1792]{0:T(1024)}, u32[]{:S(2)}) copy-start(f32[1792]{0:T(1024)} %param.16) | copy-start | bytes 21508
  127.3 8.3 %collective-permute-start.11 = (bf16[128,2560]{1,0:T(8,128)(2,1)}, bf16[128,2560]{1,0:T(8,128)(2,1)}, u32[]{:S(2)}, u32[]{:S(2)}) collective-permute-start(bf16[128,2560]{1,0:T(8,128)(2,1)} %dynamic-slice_bitcast_fusion.3), channel_id=1, source_target_pairs={{0,1},{1,0},{2,3},{3,2},{4,5},{5,4},{6,7},{7,6},{8,9},{9,8},{10,11... | collective-permute-start | bytes 1966088 | tf_op jit(solution)/shard_map/ppermute | solution.py:182
  127.3 8.2 %collective-permute-start.13 = (f32[128]{0:T(128)S(1)}, f32[128]{0:T(128)S(1)}, u32[]{:S(2)}, u32[]{:S(2)}) collective-permute-start(f32[128]{0:T(128)S(1)} %fusion.45), channel_id=1, source_target_pairs={{0,1},{1,0},{2,3},{3,2},{4,5},{5,4},{6,7},{7,6},{8,9},{9,8},{10,11... | collective-permute-start | bytes 1544 | tf_op jit(solution)/shard_map/ppermute | solution.py:182
  129.0 102.9 %reduce-scatter.11.cloned.1.call-start = ((), (), s32[]{:S(2)}) async-start(), calls=%async_computation.7 | async-start | bytes 1146880 | tf_op jit(solution)/shard_map/reduce_scatter | solution.py:237
  135.4 3.8 %collective-permute-start.12 = (bf16[128,2560]{1,0:T(8,128)(2,1)S(1)}, bf16[128,2560]{1,0:T(8,128)(2,1)S(1)}, u32[]{:S(2)}, u32[]{:S(2)}) collective-permute-start(bf16[128,2560]{1,0:T(8,128)(2,1)S(1)} %dynamic-slice_bitcast_fusion.2), channel_id=1, source_target_pairs={{0,1},{1,0},{2,3},{3,2},{4,5},{5,4},{6,7},{7,6},{8,9},{9,8},{10,11... | collective-permute-start | bytes 1966088 | tf_op jit(solution)/shard_map/ppermute | solution.py:182
  135.6 18.3 %copy-start.3 = (bf16[128,1792]{1,0:T(8,128)(2,1)S(1)}, bf16[128,1792]{1,0:T(8,128)(2,1)}, u32[]{:S(2)}) copy-start(bf16[128,1792]{1,0:T(8,128)(2,1)} %param.10) | copy-start | bytes 1376260
  137.7 50.9 %collective-permute-start.15 = (bf16[128,2560]{1,0:T(8,128)(2,1)}, bf16[128,2560]{1,0:T(8,128)(2,1)S(1)}, u32[]{:S(2)}, u32[]{:S(2)}) collective-permute-start(bf16[128,2560]{1,0:T(8,128)(2,1)} %fusion.17), channel_id=1, source_target_pairs={{0,2},{1,3},{2,0},{3,1},{4,6},{5,7},{6,4},{7,5},{8,10},{9,11},{10,... | collective-permute-start | bytes 1966088 | tf_op jit(solution)/shard_map/ppermute | solution.py:182
  139.4 49.3 %collective-permute-start.19 = (bf16[128,2560]{1,0:T(8,128)(2,1)S(1)}, bf16[128,2560]{1,0:T(8,128)(2,1)S(1)}, u32[]{:S(2)}, u32[]{:S(2)}) collective-permute-start(bf16[128,2560]{1,0:T(8,128)(2,1)S(1)} %fusion.16), channel_id=1, source_target_pairs={{0,2},{1,3},{2,0},{3,1},{4,6},{5,7},{6,4},{7,5},{8,10},{9,11},{10,... | collective-permute-start | bytes 1966088 | tf_op jit(solution)/shard_map/ppermute | solution.py:182
  153.9 26.8 %slice-start = ((s8[9175040]{0:T(1024)(128)(4,1)}), s8[4194304]{0:T(1024)(128)(4,1)S(1)}, s32[]{:S(2)}) async-start(s8[9175040]{0:T(1024)(128)(4,1)} %bitcast.151), calls=%async_computation.8 | async-start | bytes 8388608
  174.4 6.3 %slice-start.1 = ((s8[9175040]{0:T(1024)(128)(4,1)}), s8[4194304]{0:T(1024)(128)(4,1)S(1)}, s32[]{:S(2)}) async-start(s8[9175040]{0:T(1024)(128)(4,1)} %bitcast.151), calls=%async_computation.9 | async-start | bytes 8388608
  174.4 6.3 %slice-start.2 = ((s8[9175040]{0:T(1024)(128)(4,1)}), s8[786432]{0:T(1024)(128)(4,1)S(1)}, s32[]{:S(2)}) async-start(s8[9175040]{0:T(1024)(128)(4,1)} %bitcast.151), calls=%async_computation.10 | async-start | bytes 1572864
  183.3 5.4 %collective-permute-start.14 = (bf16[128,2560]{1,0:T(8,128)(2,1)S(1)}, bf16[128,2560]{1,0:T(8,128)(2,1)S(1)}, u32[]{:S(2)}, u32[]{:S(2)}) collective-permute-start(bf16[128,2560]{1,0:T(8,128)(2,1)S(1)} %dynamic-slice_bitcast_fusion.1), channel_id=1, source_target_pairs={{0,1},{1,0},{2,3},{3,2},{4,5},{5,4},{6,7},{7,6},{8,9},{9,8},{10,11... | collective-permute-start | bytes 1966088 | tf_op jit(solution)/shard_map/ppermute | solution.py:182
  183.5 5.3 %collective-permute-start.18 = (bf16[128,2560]{1,0:T(8,128)(2,1)S(1)}, bf16[128,2560]{1,0:T(8,128)(2,1)S(1)}, u32[]{:S(2)}, u32[]{:S(2)}) collective-permute-start(bf16[128,2560]{1,0:T(8,128)(2,1)S(1)} %dynamic-slice_bitcast_fusion), channel_id=1, source_target_pairs={{0,1},{1,0},{2,3},{3,2},{4,5},{5,4},{6,7},{7,6},{8,9},{9,8},{10,11... | collective-permute-start | bytes 1966088 | tf_op jit(solution)/shard_map/ppermute | solution.py:182
  184.0 3.5 %collective-permute-start.17 = (f32[128]{0:T(128)S(1)}, f32[128]{0:T(128)S(1)}, u32[]{:S(2)}, u32[]{:S(2)}) collective-permute-start(f32[128]{0:T(128)S(1)} %fusion.44), channel_id=1, source_target_pairs={{0,2},{1,3},{2,0},{3,1},{4,6},{5,7},{6,4},{7,5},{8,10},{9,11},{10,... | collective-permute-start | bytes 1544 | tf_op jit(solution)/shard_map/ppermute | solution.py:182
  187.5 1.1 collective-permute-start.16
  189.5 2.2 collective-permute-start.21
  189.8 16.9 %collective-permute-start.20 = (bf16[128,2560]{1,0:T(8,128)(2,1)S(1)}, bf16[128,2560]{1,0:T(8,128)(2,1)S(1)}, u32[]{:S(2)}, u32[]{:S(2)}) collective-permute-start(bf16[128,2560]{1,0:T(8,128)(2,1)S(1)} %fusion.13), channel_id=1, source_target_pairs={{0,2},{1,3},{2,0},{3,1},{4,6},{5,7},{6,4},{7,5},{8,10},{9,11},{10,... | collective-permute-start | bytes 1966088 | tf_op jit(solution)/shard_map/ppermute | solution.py:182
  206.8 2.1 collective-permute-start.22
  206.8 51.3 %reduce-scatter.9.cloned.1.call-start = ((), (), s32[]{:S(2)}) async-start(), calls=%async_computation.6 | async-start | bytes 1146880 | tf_op jit(solution)/shard_map/reduce_scatter | solution.py:237
Sparse Core Ops, SparseCore 0:
  75.9 23.9 reduce-scatter.4
  129.1 24.7 reduce-scatter.6
  206.9 24.9 reduce-scatter.10
  234.0 24.0 reduce-scatter.8

commit v5 on v4

--- a/solution.py
+++ b/solution.py
@@ -190,8 +190,30 @@
     return value.astype(jnp.float32)
 
 
-def matmul(a, b):
-    return jnp.dot(a, b, preferred_element_type=jnp.float32).astype(jnp.bfloat16)
+def matmul_kernel(rows, weight, out):
+    out[...] = jnp.dot(rows[...], weight[...], preferred_element_type=jnp.float32).astype(out.dtype)
+
+
+def matmul(rows, weight):
+    row_count, depth = rows.shape
+    columns = weight.shape[1]
+    block = 256
+    return pl.pallas_call(
+        matmul_kernel,
+        grid=(columns // block,),
+        in_specs=[
+            pl.BlockSpec((row_count, depth), lambda i: (0, 0)),
+            pl.BlockSpec((depth, block), lambda i: (0, i)),
+        ],
+        out_specs=pl.BlockSpec((row_count, block), lambda i: (0, i)),
+        out_shape=jax.ShapeDtypeStruct((row_count, columns), jnp.bfloat16),
+        compiler_params=pltpu.CompilerParams(vmem_limit_bytes=16 * 1024 * 1024),
+        cost_estimate=pl.CostEstimate(
+            flops=2 * row_count * depth * columns,
+            bytes_accessed=2 * weight.size,
+            transcendentals=0,
+        ),
+    )(rows, weight)
 
 
 def gather_keys(rotated_keys, n_ctx):
@@ -230,15 +252,6 @@
 
 def after(value, earlier):
     return lax.optimization_barrier((value, earlier))[0]
-
-
-def reduce_ctx(blocks):
-    flat = blocks.reshape(-1, blocks.shape[-1])
-    return wide(lax.psum_scatter(flat, "ctx", scatter_dimension=0, tiled=True))
-
-
-def gather_ctx(rows):
-    return lax.all_gather(rows, "ctx", axis=0, tiled=True)
 
 
 def paired_tail(
@@ -254,56 +267,77 @@
     own = spread_heads(heads_out, n_ctx, n_tp)
     own_all = jnp.stack(own)
     near = swap(own_all, "tp", 1)
-    far = swap(own_all, "tp", 2)
     residual_halves = residual.reshape(2, half, width)
 
     def sum_heads(blocks, which):
-        head_sum = reduce_ctx(jnp.stack([pick(blocks, t ^ i) for i in range(n_ctx)]))
-        return (wide(pick(residual_halves, which)) + head_sum).astype(jnp.bfloat16)
+        place = t ^ c
+        sent = jnp.stack([pick(blocks, place ^ 1), pick(blocks, place ^ 3)])
+        came = swap(sent, "ctx", 1)
+        mine = wide(pick(blocks, place)) + wide(came[0])
+        other = (wide(pick(blocks, place ^ 2)) + wide(came[1])).astype(jnp.bfloat16)
+        total = wide(pick(residual_halves, which)) + mine + wide(swap(other, "ctx", 2))
+        return total.astype(jnp.bfloat16), sent, came
+
+    def gather_ctx(rows):
+        pair = jnp.concatenate([rows, swap(rows, "ctx", 2)], axis=0)
+        return pair, swap(pair, "ctx", 1)
 
     blocks_a = matmul(pair_rows(own_all, near), output_weight).reshape(n_ctx, half, width)
-    far = after(far, blocks_a)
+    attended_a, sent_a, came_a = sum_heads(blocks_a, first_half)
+    far = after(swap(after(own_all, sent_a), "tp", 2), came_a)
     far_near = swap(far, "tp", 1)
     order = [2, 3, 0, 1]
     rows_b = pair_rows([far[i] for i in order], [far_near[i] for i in order])
     blocks_b = matmul(rows_b, output_weight).reshape(n_ctx, half, width)
-    attended_a = sum_heads(blocks_a, first_half)
-    all_a = gather_ctx(attended_a)
-    attended_b = sum_heads(after(blocks_b, attended_a), 1 - first_half)
-
-    def gate_up(all_rows):
-        values = wide(all_rows)
-        squares = jnp.sum(values * values, axis=1).reshape(2, 2 * half)
+    near_a, far_a = gather_ctx(attended_a)
+    attended_b, _, _ = sum_heads(after(blocks_b, attended_a), 1 - first_half)
+
+    def gate_up(rows):
+        values = wide(rows)
+        squares = jnp.sum(values * values, axis=1).reshape(-1, 2, half)
         scaled = (values * norm_gain[None, :]).astype(jnp.bfloat16)
-        sums = [matmul(scaled, w).reshape(2, 2 * half, -1) for w in (gate_weight, up_weight)]
-        kept, came = [], []
-        for term in sums + [squares]:
-            came.append(swap(pick(term, 1 - core), "tp", 1))
-            kept.append(pick(term, core))
-        return kept, came
-
-    kept_a, came_a = gate_up(all_a)
-    chip_a = [(wide(k) + wide(r)).astype(k.dtype) for k, r in zip(kept_a, came_a)]
-    across = [swap(term, "tp", 2) for term in chip_a]
-    all_b = after(gather_ctx(attended_b), chip_a)
-    kept_b, came_b = gate_up(all_b)
-    gate, up, squares = [wide(k) + wide(r) + wide(x) for k, r, x in zip(kept_b, came_b, across)]
-    inverse_rms = lax.rsqrt(squares / model_width + norm_eps)[:, None]
-    hidden = (jax.nn.silu(gate * inverse_rms) * (up * inverse_rms)).astype(jnp.bfloat16)
+        terms = [
+            matmul(scaled, weight).reshape(-1, 2, half, weight.shape[1])
+            for weight in (gate_weight, up_weight)
+        ]
+
+        def side(value, which):
+            return lax.dynamic_index_in_dim(value, which, 1, keepdims=False)
+
+        kept = jnp.stack([side(term, core) for term in terms])
+        came = swap(jnp.stack([side(term, 1 - core) for term in terms]), "tp", 1)
+        total = wide(kept) + wide(came)
+        came_squares = swap(side(squares, 1 - core), "tp", 1)
+        return total, side(squares, core) + came_squares
+
+    sums_a, squares_a = [], []
+    for rows in (near_a, far_a):
+        total, squares = gate_up(rows)
+        sums_a.append(total.astype(jnp.bfloat16))
+        squares_a.append(squares)
+    across = [swap(total, "tp", 2) for total in sums_a]
+    across_squares = swap(jnp.concatenate(squares_a, axis=0), "tp", 2)
+    all_b = jnp.concatenate(gather_ctx(attended_b), axis=0)
+    sums_b, squares_b = gate_up(after(all_b, sums_a))
+    inverse_rms = lax.rsqrt((squares_b + across_squares) / model_width + norm_eps)[:, :, None]
+    gate, up = (sums_b + wide(jnp.concatenate(across, axis=1))) * inverse_rms[None]
+    hidden = (jax.nn.silu(gate) * up).astype(jnp.bfloat16).reshape(2 * half, -1)
     hidden_near = swap(hidden, "tp", 1)
     hidden_far = swap(hidden, "tp", 2)
 
-    def down(mine, other):
+    def sum_down(mine, other):
         blocks = matmul(jnp.concatenate([mine, other], axis=0), down_weight)
-        blocks = blocks.reshape(n_ctx, half, width)
-        return jnp.stack([pick(blocks, i ^ (2 * core)) for i in range(n_ctx)])
-
-    down_b = down(hidden, hidden_near)
-    out_b = (wide(attended_b) + reduce_ctx(down_b)).astype(jnp.bfloat16)
-    hidden_far = after(hidden_far, down_b)
-    hidden_far_near = swap(hidden_far, "tp", 1)
-    down_a = down(hidden_far, hidden_far_near)
-    out_a = (wide(attended_a) + reduce_ctx(down_a)).astype(jnp.bfloat16)
+        blocks = blocks.reshape(2, 2, half, width)
+        came = swap(blocks[:, 1], "ctx", 1)
+        pair = wide(blocks[:, 0]) + wide(came)
+        other_place = pick(pair, 1 - core).astype(jnp.bfloat16)
+        return pick(pair, core) + wide(swap(other_place, "ctx", 2)), came
+
+    down_b, came_b = sum_down(hidden, hidden_near)
+    hidden_far = after(hidden_far, came_b)
+    down_a, _ = sum_down(hidden_far, swap(hidden_far, "tp", 1))
+    out_a = (wide(attended_a) + down_a).astype(jnp.bfloat16)
+    out_b = (wide(attended_b) + down_b).astype(jnp.bfloat16)
 
     def in_order(a, b):
         first = first_half == 0
@@ -327,7 +361,7 @@
     row_count = residual.shape[0]
     ctx_place = lax.axis_index("ctx")
     n_ctx, n_tp = lax.axis_size("ctx"), lax.axis_size("tp")
-    paired = n_ctx == 4 and n_tp == 4 and row_count % 64 == 0
+    paired = n_ctx == 4 and n_tp == 4 and row_count % 64 == 0 and residual.shape[1] % 256 == 0
     own_index = ctx_place * row_count + jnp.arange(row_count, dtype=jnp.int32)
     _, own_position = trace_info(own_index, lengths)
     rotated_keys = rope_keys(latent, own_position, LAT)

time: 268 us -> 279 us (1.041)
  waiting for transfers between devices: 112 us -> 161 us
  matrix products: 43.7 us -> 0 us
  Pallas kernels: 6.62 us -> 47.7 us
  blocking collectives: 38.4 us -> 0 us
  between operations: 14.4 us -> 1.64 us
  local copies, waits for them, and re-layouts: 2.84 us -> 12.8 us
  starting transfers between devices: 32.5 us -> 40 us
    ppermute x16 -> x28, waiting for transfers between devices: 22.1 us -> 142 us  [swap(): return lax.ppermute(value, axis_name, [(i, i ^ bit) for i in range(width)])]
    reduce_scatter x4 -> x0, waiting for transfers between devices: 73.9 us -> none  [reduce_ctx(): return wide(lax.psum_scatter(flat, 'ctx', scatter_dimension=0, tiled=True))]
    dot_general x8 -> x0, matrix products: 43.7 us -> none  [matmul(): jnp.dot(a, b, preferred_element_type=jnp.float32).astype(jnp.bfloat16)]
    pallas_call x0 -> x10, Pallas kernels: none -> 41.1 us  [matmul(): pl.pallas_call(matmul_kernel, grid=(columns // block,), in_specs=[pl.Bloc...]
    all_gather x2 -> x0, blocking collectives: 38.4 us -> none  [gather_ctx(): return lax.all_gather(rows, 'ctx', axis=0, tiled=True)]
    unnamed x32 -> x52, local copies, waits for them, and re-layouts: 0.23 us -> 10.6 us
    ppermute x16 -> x28, starting transfers between devices: 14 us -> 23.2 us  [swap(): return lax.ppermute(value, axis_name, [(i, i ^ bit) for i in range(width)])]
    ppermute x4, waiting for transfers between devices: 15 us -> 17.8 us  [spread_heads(): lax.ppermute(pieces[s], ('ctx', 'tp'), [(c * n_tp + t, t * n_tp + (c ^ s)...]
  transfers between devices with their start and end apart: 27 -> 35, of which waited for: 14 -> 20; matrix products, arithmetic and copies ran while one was open for 18% -> 2% of each run, Pallas kernels for 0% -> 8%
where the time goes in v5:
time: 279 us; the launch traced here: 278 us
  waiting for transfers between devices  161 us (58%)
  Pallas kernels  47.7 us (17%)
  starting transfers between devices  40 us (14%)
  other arithmetic  15.5 us (6%)
  local copies, waits for them, and re-layouts  12.8 us (5%)
    ppermute x28, waiting for transfers between devices, swap(): return lax.ppermute(value, axis_name, [(i, i ^ bit) for i in range(width)])  142 us
    pallas_call x10, Pallas kernels, matmul(): pl.pallas_call(matmul_kernel, grid=(columns // block,), in_specs=[pl.Bloc...  41.1 us
    ppermute x28, starting transfers between devices, swap(): return lax.ppermute(value, axis_name, [(i, i ^ bit) for i in range(width)])  23.2 us
    ppermute x4, waiting for transfers between devices, spread_heads(): lax.ppermute(pieces[s], ('ctx', 'tp'), [(c * n_tp + t, t * n_tp + (c ^ s)...  17.8 us
    unnamed x52, local copies, waits for them, and re-layouts  10.6 us
    ppermute x3, starting transfers between devices, gather_keys(): lax.ppermute(half, 'ctx', [(c, c + d) for c in range(n_ctx - d)])  10.1 us
    ppermute x4, starting transfers between devices, spread_heads(): lax.ppermute(pieces[s], ('ctx', 'tp'), [(c * n_tp + t, t * n_tp + (c ^ s)...  6.7 us
    pallas_call x1, Pallas kernels, attention(): pl.pallas_call(functools.partial(attention_kernel, group), grid=(local_he...  6.62 us
  transfers between devices with their start and end apart: 35, of which 20 were waited for; matrix products, arithmetic and copies ran while one was open for 2% of the time, Pallas kernels for 8%

profile of v5, /device:TPU:0, one launch (start us, length us, event | category | flops | bytes accessed | tf_op | source)
XLA Modules:
  0.0 278.4 jit_solution(12658296744966610230)
XLA Ops:
  0.6 0.9 slice.86
  1.6 1.1 convert_element_type.199
  2.7 0.8 reduce-window.8
  3.5 0.7 subtract_subtract_fusion
  4.8 5.9 %collective-permute-start.1 = (bf16[288,128]{1,0:T(8,128)(2,1)S(1)}, bf16[288,128]{1,0:T(8,128)(2,1)S(1)}, u32[]{:S(2)}, u32[]{:S(2)}) collective-permute-start(bf16[288,128]{1,0:T(8,128)(2,1)S(1)} %fusion.29), channel_id=1, source_target_pairs={{0,8},{4,12},{1,9},{5,13},{2,10},{6,14},{3,11},{7,15},{16,24},{20,... | collective-permute-start | bytes 221192 | tf_op jit(solution)/shard_map/ppermute | solution.py:224
  10.8 2.3 collective-permute-start
  13.1 1.8 collective-permute-start.2
  15.7 1.2 collective-permute-done.2
  17.1 1.4 collective-permute-done.3
  18.6 6.6 %shard_map.113 = bf16[128,2048]{1,0:T(8,128)(2,1)S(1)} custom-call(f32[4,128,128]{2,1,0:T(8,128)S(1)} %pad_maximum_fusion.13.tables, s32[128,1]{1,0:T(8,128)S(1)} %copy.22.starts, s32[128,1]{1,0:T(8,128)S(1)} %iota_add_fusion.own_index, s32[1,512]{1,0:T(1,128)S(1)} %iota_add_fusion.1.key_index, bf16[576,512]{1,0:T(8,128)(2,1)S(1)} %maximum_maximum_fusion.keys, ...), custom_call_target="tpu_custom_call" | custom-call | flops 2684354560 | bytes 5046272 | tf_op jit(solution)/shard_map/pallas_call | solution.py:143
  25.5 5.1 %collective-permute-start.7 = (bf16[32,2048]{1,0:T(8,128)(2,1)S(1)}, bf16[32,2048]{1,0:T(8,128)(2,1)S(1)}, u32[]{:S(2)}, u32[]{:S(2)}) collective-permute-start(bf16[32,2048]{1,0:T(8,128)(2,1)S(1)} %get-tuple-element.38), channel_id=1, source_target_pairs={{0,3},{1,7},{2,11},{3,15},{4,2},{5,6},{6,10},{7,14},{8,1},{9,5},{1... | collective-permute-start | bytes 393224 | tf_op jit(solution)/shard_map/ppermute | solution.py:238
  30.6 0.6 collective-permute-start.6
  31.2 0.8 collective-permute-start.4
  32.0 5.0 %collective-permute-done.7 = bf16[32,2048]{1,0:T(8,128)(2,1)S(1)} collective-permute-done((bf16[32,2048]{1,0:T(8,128)(2,1)S(1)}, bf16[32,2048]{1,0:T(8,128)(2,1)S(1)}, u32[]{:S(2)}, u32[]{:S(2)}) %collective-permute-start.7) | collective-permute-done | bytes 131104 | tf_op jit(solution)/shard_map/ppermute | solution.py:238
  37.0 12.8 %collective-permute-done.6 = bf16[32,2048]{1,0:T(8,128)(2,1)S(1)} collective-permute-done((bf16[32,2048]{1,0:T(8,128)(2,1)S(1)}, bf16[32,2048]{1,0:T(8,128)(2,1)S(1)}, u32[]{:S(2)}, u32[]{:S(2)}) %collective-permute-start.6) | collective-permute-done | bytes 131104 | tf_op jit(solution)/shard_map/ppermute | solution.py:238
  50.0 1.9 collective-permute-done.8
  52.0 3.1 %copy-done.2 = bf16[2048,1792]{1,0:T(8,128)(2,1)S(1)} copy-done((bf16[2048,1792]{1,0:T(8,128)(2,1)S(1)}, bf16[2048,1792]{1,0:T(8,128)(2,1)}, u32[]{:S(2)}) %copy-start.2) | copy-done | bytes 7340056
  55.1 3.8 %shard_map.114 = bf16[256,1792]{1,0:T(8,128)(2,1)S(1)} custom-call(bf16[256,2048]{1,0:T(8,128)(2,1)S(1)} %constant_dynamic-update-slice_fusion.3.rows, bf16[2048,1792]{1,0:T(8,128)(2,1)S(1)} %copy-done.2), custom_call_target="tpu_custom_call" | custom-call | flops 1879048192 | bytes 7340032 | tf_op jit(solution)/shard_map/pallas_call | solution.py:201
  59.0 1.2 collective-permute-start.9
  60.2 3.9 %collective-permute-start.11 = (bf16[4,32,2048]{2,1,0:T(8,128)(2,1)S(1)}, bf16[4,32,2048]{2,1,0:T(8,128)(2,1)S(1)}, u32[]{:S(2)}, u32[]{:S(2)}) collective-permute-start(bf16[4,32,2048]{2,1,0:T(8,128)(2,1)S(1)} %pad_maximum_fusion.6), channel_id=1, source_target_pairs={{0,2},{1,3},{2,0},{3,1},{4,6},{5,7},{6,4},{7,5},{8,10},{9,11},{10,... | collective-permute-start | bytes 1572872 | tf_op jit(solution)/shard_map/ppermute | solution.py:182
  64.1 7.6 %collective-permute-done.9 = bf16[2,64,1792]{2,1,0:T(8,128)(2,1)} collective-permute-done((bf16[2,64,1792]{2,1,0:T(8,128)(2,1)S(1)}, bf16[2,64,1792]{2,1,0:T(8,128)(2,1)}, u32[]{:S(2)}, u32[]{:S(2)}) %collective-permute-start.9) | collective-permute-done | bytes 458784 | tf_op jit(solution)/shard_map/ppermute | solution.py:182
  71.7 1.0 fusion.16
  72.7 5.6 %collective-permute-start.10 = (bf16[64,1792]{1,0:T(8,128)(2,1)S(1)}, bf16[64,1792]{1,0:T(8,128)(2,1)S(1)}, u32[]{:S(2)}, u32[]{:S(2)}) collective-permute-start(bf16[64,1792]{1,0:T(8,128)(2,1)S(1)} %fusion.16), channel_id=1, source_target_pairs={{0,8},{4,12},{8,0},{12,4},{1,9},{5,13},{9,1},{13,5},{2,10},{6,14},... | collective-permute-start | bytes 688136 | tf_op jit(solution)/shard_map/ppermute | solution.py:182
  78.3 10.2 %collective-permute-done.10 = bf16[64,1792]{1,0:T(8,128)(2,1)S(1)} collective-permute-done((bf16[64,1792]{1,0:T(8,128)(2,1)S(1)}, bf16[64,1792]{1,0:T(8,128)(2,1)S(1)}, u32[]{:S(2)}, u32[]{:S(2)}) %collective-permute-start.10) | collective-permute-done | bytes 229408 | tf_op jit(solution)/shard_map/ppermute | solution.py:182
  88.5 1.1 fusion.15
  89.6 12.2 %collective-permute-done.17 = bf16[64,1792]{1,0:T(8,128)(2,1)S(1)} collective-permute-done((bf16[64,1792]{1,0:T(8,128)(2,1)S(1)}, bf16[64,1792]{1,0:T(8,128)(2,1)S(1)}, u32[]{:S(2)}, u32[]{:S(2)}) %collective-permute-start.17) | collective-permute-done | bytes 229408 | tf_op jit(solution)/shard_map/ppermute | solution.py:182
  102.2 3.6 %copy-done = bf16[1792,2560]{1,0:T(8,128)(2,1)S(1)} copy-done((bf16[1792,2560]{1,0:T(8,128)(2,1)S(1)}, bf16[1792,2560]{1,0:T(8,128)(2,1)}, u32[]{:S(2)}) %copy-start) | copy-done | bytes 9175064
  105.8 3.7 %shard_map.117 = bf16[128,2560]{1,0:T(8,128)(2,1)S(1)} custom-call(bf16[128,1792]{1,0:T(8,128)(2,1)S(1)} %get-tuple-element.43.rows, bf16[1792,2560]{1,0:T(8,128)(2,1)S(1)} %copy-done), custom_call_target="tpu_custom_call" | custom-call | flops 1174405120 | bytes 9175040 | tf_op jit(solution)/shard_map/pallas_call | solution.py:201
  109.6 3.6 %copy-done.1 = bf16[1792,2560]{1,0:T(8,128)(2,1)S(1)} copy-done((bf16[1792,2560]{1,0:T(8,128)(2,1)S(1)}, bf16[1792,2560]{1,0:T(8,128)(2,1)}, u32[]{:S(2)}) %copy-start.1) | copy-done | bytes 9175064
  113.2 3.8 %shard_map.116 = bf16[128,2560]{1,0:T(8,128)(2,1)S(1)} custom-call(bf16[128,1792]{1,0:T(8,128)(2,1)S(1)} %get-tuple-element.43.rows, bf16[1792,2560]{1,0:T(8,128)(2,1)S(1)} %copy-done.1), custom_call_target="tpu_custom_call" | custom-call | flops 1174405120 | bytes 9175040 | tf_op jit(solution)/shard_map/pallas_call | solution.py:201
  117.4 3.8 %shard_map.115 = bf16[256,1792]{1,0:T(8,128)(2,1)S(1)} custom-call(bf16[256,2048]{1,0:T(8,128)(2,1)S(1)} %bitcast_dynamic-update-slice_fusion.rows, bf16[2048,1792]{1,0:T(8,128)(2,1)S(1)} %bitcast.167), custom_call_target="tpu_custom_call" | custom-call | flops 1879048192 | bytes 7340032 | tf_op jit(solution)/shard_map/pallas_call | solution.py:201
  121.3 2.1 collective-permute-start.13
  123.7 3.8 %shard_map.119 = bf16[128,2560]{1,0:T(8,128)(2,1)S(1)} custom-call(bf16[128,1792]{1,0:T(8,128)(2,1)S(1)} %get-tuple-element.45.rows, bf16[1792,2560]{1,0:T(8,128)(2,1)S(1)} %bitcast.161), custom_call_target="tpu_custom_call" | custom-call | flops 1174405120 | bytes 9175040 | tf_op jit(solution)/shard_map/pallas_call | solution.py:201
  127.6 3.7 %shard_map.118 = bf16[128,2560]{1,0:T(8,128)(2,1)S(1)} custom-call(bf16[128,1792]{1,0:T(8,128)(2,1)S(1)} %get-tuple-element.45.rows, bf16[1792,2560]{1,0:T(8,128)(2,1)S(1)} %bitcast.163), custom_call_target="tpu_custom_call" | custom-call | flops 1174405120 | bytes 9175040 | tf_op jit(solution)/shard_map/pallas_call | solution.py:201
  131.4 3.2 %collective-permute-done.13 = bf16[2,64,1792]{2,1,0:T(8,128)(2,1)S(1)} collective-permute-done((bf16[2,64,1792]{2,1,0:T(8,128)(2,1)S(1)}, bf16[2,64,1792]{2,1,0:T(8,128)(2,1)S(1)}, u32[]{:S(2)}, u32[]{:S(2)}) %collective-permute-start.13) | collective-permute-done | bytes 458784 | tf_op jit(solution)/shard_map/ppermute | solution.py:182
  134.7 1.5 collective-permute-start.14
  136.3 11.6 %collective-permute-done.14 = bf16[64,1792]{1,0:T(8,128)(2,1)S(1)} collective-permute-done((bf16[64,1792]{1,0:T(8,128)(2,1)S(1)}, bf16[64,1792]{1,0:T(8,128)(2,1)S(1)}, u32[]{:S(2)}, u32[]{:S(2)}) %collective-permute-start.14) | collective-permute-done | bytes 229408 | tf_op jit(solution)/shard_map/ppermute | solution.py:182
  148.2 1.0 add_convert_fusion.1
  149.2 10.1 %collective-permute-done.15 = bf16[64,1792]{1,0:T(8,128)(2,1)S(1)} collective-permute-done((bf16[64,1792]{1,0:T(8,128)(2,1)S(1)}, bf16[64,1792]{1,0:T(8,128)(2,1)S(1)}, u32[]{:S(2)}, u32[]{:S(2)}) %collective-permute-start.15) | collective-permute-done | bytes 229408 | tf_op jit(solution)/shard_map/ppermute | solution.py:182
  159.4 1.0 add_convert_fusion
  160.4 11.4 %collective-permute-done.16 = bf16[128,1792]{1,0:T(8,128)(2,1)S(1)} collective-permute-done((bf16[128,1792]{1,0:T(8,128)(2,1)S(1)}, bf16[128,1792]{1,0:T(8,128)(2,1)S(1)}, u32[]{:S(2)}, u32[]{:S(2)}) %collective-permute-start.16) | collective-permute-done | bytes 458784 | tf_op jit(solution)/shard_map/ppermute | solution.py:182
  172.2 4.9 %shard_map.121 = bf16[256,2560]{1,0:T(8,128)(2,1)S(1)} custom-call(bf16[256,1792]{1,0:T(8,128)(2,1)S(1)} %get-tuple-element.24.rows, bf16[1792,2560]{1,0:T(8,128)(2,1)S(1)} %bitcast.161), custom_call_target="tpu_custom_call" | custom-call | flops 2348810240 | bytes 9175040 | tf_op jit(solution)/shard_map/pallas_call | solution.py:201
  177.2 4.9 %shard_map.120 = bf16[256,2560]{1,0:T(8,128)(2,1)S(1)} custom-call(bf16[256,1792]{1,0:T(8,128)(2,1)S(1)} %get-tuple-element.24.rows, bf16[1792,2560]{1,0:T(8,128)(2,1)S(1)} %bitcast.163), custom_call_target="tpu_custom_call" | custom-call | flops 2348810240 | bytes 9175040 | tf_op jit(solution)/shard_map/pallas_call | solution.py:201
  182.3 1.2 pad_maximum_fusion
  183.6 0.5 collective-permute-start.25
  184.2 2.0 collective-permute-done.25
  186.2 0.7 collective-permute-start.22
  186.9 1.3 collective-permute-start.23
  188.3 0.8 collective-permute-start.27
  189.2 28.4 %collective-permute-done.27 = f32[2,64]{1,0:T(2,128)S(1)} collective-permute-done((f32[2,64]{1,0:T(2,128)S(1)}, f32[2,64]{1,0:T(2,128)S(1)}, u32[]{:S(2)}, u32[]{:S(2)}) %collective-permute-start.27) | collective-permute-done | bytes 544 | tf_op jit(solution)/shard_map/ppermute | solution.py:182
  217.6 2.4 add_multiply_fusion
  220.7 0.8 collective-permute-start.28
  221.4 1.3 collective-permute-done.29
  222.9 4.3 %shard_map.122 = bf16[256,1792]{1,0:T(8,128)(2,1)S(1)} custom-call(bf16[256,2560]{1,0:T(8,128)(2,1)S(1)} %pad_maximum_fusion.1.rows, bf16[2560,1792]{1,0:T(8,128)(2,1)S(1)} %bitcast.165), custom_call_target="tpu_custom_call" | custom-call | flops 2348810240 | bytes 9175040 | tf_op jit(solution)/shard_map/pallas_call | solution.py:201
  227.6 10.2 %collective-permute-done.28 = bf16[128,2560]{1,0:T(8,128)(2,1)S(1)} collective-permute-done((bf16[128,2560]{1,0:T(8,128)(2,1)S(1)}, bf16[128,2560]{1,0:T(8,128)(2,1)S(1)}, u32[]{:S(2)}, u32[]{:S(2)}) %collective-permute-start.28) | collective-permute-done | bytes 655392 | tf_op jit(solution)/shard_map/ppermute | solution.py:182
  237.8 2.0 collective-permute-done.30
  239.8 2.1 collective-permute-done.31
  242.0 4.3 %shard_map.123 = bf16[256,1792]{1,0:T(8,128)(2,1)S(1)} custom-call(bf16[256,2560]{1,0:T(8,128)(2,1)S(1)} %pad_maximum_fusion.2.rows, bf16[2560,1792]{1,0:T(8,128)(2,1)S(1)} %bitcast.165), custom_call_target="tpu_custom_call" | custom-call | flops 2348810240 | bytes 9175040 | tf_op jit(solution)/shard_map/pallas_call | solution.py:201
  246.9 2.8 %collective-permute-start.34 = (bf16[64,1792]{1,0:T(8,128)(2,1)S(1)}, bf16[64,1792]{1,0:T(8,128)(2,1)S(1)}, u32[]{:S(2)}, u32[]{:S(2)}) collective-permute-start(bf16[64,1792]{1,0:T(8,128)(2,1)S(1)} %fusion.19), channel_id=1, source_target_pairs={{0,8},{4,12},{8,0},{12,4},{1,9},{5,13},{9,1},{13,5},{2,10},{6,14},... | collective-permute-start | bytes 688136 | tf_op jit(solution)/shard_map/ppermute | solution.py:182
  249.7 14.2 %collective-permute-done.32 = bf16[2,64,1792]{2,1,0:T(8,128)(2,1)S(1)} collective-permute-done((bf16[2,64,1792]{2,1,0:T(8,128)(2,1)S(1)}, bf16[2,64,1792]{2,1,0:T(8,128)(2,1)S(1)}, u32[]{:S(2)}, u32[]{:S(2)}) %collective-permute-start.32) | collective-permute-done | bytes 458784 | tf_op jit(solution)/shard_map/ppermute | solution.py:182
  264.1 0.6 collective-permute-start.33
  264.7 11.9 %collective-permute-done.33 = bf16[64,1792]{1,0:T(8,128)(2,1)S(1)} collective-permute-done((bf16[64,1792]{1,0:T(8,128)(2,1)S(1)}, bf16[64,1792]{1,0:T(8,128)(2,1)S(1)}, u32[]{:S(2)}, u32[]{:S(2)}) %collective-permute-start.33) | collective-permute-done | bytes 229408 | tf_op jit(solution)/shard_map/ppermute | solution.py:182
  276.8 0.8 pad_maximum_fusion.12
  277.6 0.8 pad_maximum_fusion.9
  (149 shorter events, 6.9 us)
Async XLA Ops:
  1.6 17.0 %copy-start.4 = (bf16[512,2048]{1,0:T(8,128)(2,1)S(1)}, bf16[512,2048]{1,0:T(8,128)(2,1)}, u32[]{:S(2)}) copy-start(bf16[512,2048]{1,0:T(8,128)(2,1)} %value_weight.1) | copy-start | bytes 6291460
  4.8 10.8 %collective-permute-start.1 = (bf16[288,128]{1,0:T(8,128)(2,1)S(1)}, bf16[288,128]{1,0:T(8,128)(2,1)S(1)}, u32[]{:S(2)}, u32[]{:S(2)}) collective-permute-start(bf16[288,128]{1,0:T(8,128)(2,1)S(1)} %fusion.29), channel_id=1, source_target_pairs={{0,8},{4,12},{1,9},{5,13},{2,10},{6,14},{3,11},{7,15},{16,24},{20,... | collective-permute-start | bytes 221192 | tf_op jit(solution)/shard_map/ppermute | solution.py:224
  10.8 4.9 %collective-permute-start = (bf16[288,128]{1,0:T(8,128)(2,1)S(1)}, bf16[288,128]{1,0:T(8,128)(2,1)S(1)}, u32[]{:S(2)}, u32[]{:S(2)}) collective-permute-start(bf16[288,128]{1,0:T(8,128)(2,1)S(1)} %fusion.29), channel_id=1, source_target_pairs={{0,12},{1,13},{2,14},{3,15},{16,28},{17,29},{18,30},{19,31}} | collective-permute-start | bytes 221192 | tf_op jit(solution)/shard_map/ppermute | solution.py:224
  13.1 3.8 %collective-permute-start.2 = (bf16[288,128]{1,0:T(8,128)(2,1)S(1)}, bf16[288,128]{1,0:T(8,128)(2,1)S(1)}, u32[]{:S(2)}, u32[]{:S(2)}) collective-permute-start(bf16[288,128]{1,0:T(8,128)(2,1)S(1)} %fusion.29), channel_id=1, source_target_pairs={{0,4},{4,8},{8,12},{1,5},{5,9},{9,13},{2,6},{6,10},{10,14},{3,7},{... | collective-permute-start | bytes 221192 | tf_op jit(solution)/shard_map/ppermute | solution.py:224
  16.9 1.7 copy-start.3
  16.9 1.5 collective-permute-start.3
  25.3 6.7 %collective-permute-start.5 = (bf16[32,2048]{1,0:T(8,128)(2,1)S(1)}, bf16[32,2048]{1,0:T(8,128)(2,1)S(1)}, u32[]{:S(2)}, u32[]{:S(2)}) collective-permute-start(bf16[32,2048]{1,0:T(8,128)(2,1)S(1)} %get-tuple-element.37), channel_id=1, source_target_pairs={{0,1},{1,5},{2,9},{3,13},{4,0},{5,4},{6,8},{7,12},{8,3},{9,7},{10,... | collective-permute-start | bytes 393224 | tf_op jit(solution)/shard_map/ppermute | solution.py:238
  25.5 11.5 %collective-permute-start.7 = (bf16[32,2048]{1,0:T(8,128)(2,1)S(1)}, bf16[32,2048]{1,0:T(8,128)(2,1)S(1)}, u32[]{:S(2)}, u32[]{:S(2)}) collective-permute-start(bf16[32,2048]{1,0:T(8,128)(2,1)S(1)} %get-tuple-element.38), channel_id=1, source_target_pairs={{0,3},{1,7},{2,11},{3,15},{4,2},{5,6},{6,10},{7,14},{8,1},{9,5},{1... | collective-permute-start | bytes 393224 | tf_op jit(solution)/shard_map/ppermute | solution.py:238
  30.6 19.2 %collective-permute-start.6 = (bf16[32,2048]{1,0:T(8,128)(2,1)S(1)}, bf16[32,2048]{1,0:T(8,128)(2,1)S(1)}, u32[]{:S(2)}, u32[]{:S(2)}) collective-permute-start(bf16[32,2048]{1,0:T(8,128)(2,1)S(1)} %get-tuple-element.39), channel_id=1, source_target_pairs={{0,2},{1,6},{2,10},{3,14},{4,3},{5,7},{6,11},{7,15},{8,0},{9,4},{1... | collective-permute-start | bytes 393224 | tf_op jit(solution)/shard_map/ppermute | solution.py:238
  31.2 18.7 %collective-permute-start.4 = (bf16[32,2048]{1,0:T(8,128)(2,1)S(1)}, bf16[32,2048]{1,0:T(8,128)(2,1)S(1)}, u32[]{:S(2)}, u32[]{:S(2)}) collective-permute-start(bf16[32,2048]{1,0:T(8,128)(2,1)S(1)} %get-tuple-element.40), channel_id=1, source_target_pairs={{0,0},{1,4},{2,8},{3,12},{4,1},{5,5},{6,9},{7,13},{8,2},{9,6},{10,... | collective-permute-start | bytes 393224 | tf_op jit(solution)/shard_map/ppermute | solution.py:238
  49.9 2.0 collective-permute-start.8
  52.0 3.1 %copy-start.2 = (bf16[2048,1792]{1,0:T(8,128)(2,1)S(1)}, bf16[2048,1792]{1,0:T(8,128)(2,1)}, u32[]{:S(2)}) copy-start(bf16[2048,1792]{1,0:T(8,128)(2,1)} %weight.11) | copy-start | bytes 22020100
  58.9 29.6 %copy-start.5 = (bf16[128,1792]{1,0:T(8,128)(2,1)S(1)}, bf16[128,1792]{1,0:T(8,128)(2,1)}, u32[]{:S(2)}) copy-start(bf16[128,1792]{1,0:T(8,128)(2,1)} %param.10) | copy-start | bytes 1376260
  59.0 12.7 %collective-permute-start.9 = (bf16[2,64,1792]{2,1,0:T(8,128)(2,1)S(1)}, bf16[2,64,1792]{2,1,0:T(8,128)(2,1)}, u32[]{:S(2)}, u32[]{:S(2)}) collective-permute-start(bf16[2,64,1792]{2,1,0:T(8,128)(2,1)S(1)} %pad_maximum_fusion.7), channel_id=1, source_target_pairs={{0,4},{4,0},{8,12},{12,8},{1,5},{5,1},{9,13},{13,9},{2,6},{6,2},{1... | collective-permute-start | bytes 1376264 | tf_op jit(solution)/shard_map/ppermute | solution.py:182
  60.2 18.1 %collective-permute-start.11 = (bf16[4,32,2048]{2,1,0:T(8,128)(2,1)S(1)}, bf16[4,32,2048]{2,1,0:T(8,128)(2,1)S(1)}, u32[]{:S(2)}, u32[]{:S(2)}) collective-permute-start(bf16[4,32,2048]{2,1,0:T(8,128)(2,1)S(1)} %pad_maximum_fusion.6), channel_id=1, source_target_pairs={{0,2},{1,3},{2,0},{3,1},{4,6},{5,7},{6,4},{7,5},{8,10},{9,11},{10,... | collective-permute-start | bytes 1572872 | tf_op jit(solution)/shard_map/ppermute | solution.py:182
  72.7 29.3 %copy-start.6 = (f32[1792]{0:T(1024)S(1)}, f32[1792]{0:T(1024)}, u32[]{:S(2)}) copy-start(f32[1792]{0:T(1024)} %param.16) | copy-start | bytes 21508
  72.7 15.7 %collective-permute-start.10 = (bf16[64,1792]{1,0:T(8,128)(2,1)S(1)}, bf16[64,1792]{1,0:T(8,128)(2,1)S(1)}, u32[]{:S(2)}, u32[]{:S(2)}) collective-permute-start(bf16[64,1792]{1,0:T(8,128)(2,1)S(1)} %fusion.16), channel_id=1, source_target_pairs={{0,8},{4,12},{8,0},{12,4},{1,9},{5,13},{9,1},{13,5},{2,10},{6,14},... | collective-permute-start | bytes 688136 | tf_op jit(solution)/shard_map/ppermute | solution.py:182
  78.3 39.0 %collective-permute-start.12 = (bf16[4,32,2048]{2,1,0:T(8,128)(2,1)S(1)}, bf16[4,32,2048]{2,1,0:T(8,128)(2,1)S(1)}, u32[]{:S(2)}, u32[]{:S(2)}) collective-permute-start(bf16[4,32,2048]{2,1,0:T(8,128)(2,1)S(1)} %collective-permute-done.11), channel_id=1, source_target_pairs={{0,1},{1,0},{2,3},{3,2},{4,5},{5,4},{6,7},{7,6},{8,9},{9,8},{10,11... | collective-permute-start | bytes 1572872 | tf_op jit(solution)/shard_map/ppermute | solution.py:182
  89.5 12.3 %collective-permute-start.17 = (bf16[64,1792]{1,0:T(8,128)(2,1)S(1)}, bf16[64,1792]{1,0:T(8,128)(2,1)S(1)}, u32[]{:S(2)}, u32[]{:S(2)}) collective-permute-start(bf16[64,1792]{1,0:T(8,128)(2,1)S(1)} %fusion.15), channel_id=1, source_target_pairs={{0,8},{4,12},{8,0},{12,4},{1,9},{5,13},{9,1},{13,5},{2,10},{6,14},... | collective-permute-start | bytes 688136 | tf_op jit(solution)/shard_map/ppermute | solution.py:182
  101.9 21.5 %collective-permute-start.19 = (bf16[128,1792]{1,0:T(8,128)(2,1)S(1)}, bf16[128,1792]{1,0:T(8,128)(2,1)S(1)}, u32[]{:S(2)}, u32[]{:S(2)}) collective-permute-start(bf16[128,1792]{1,0:T(8,128)(2,1)S(1)} %pad_maximum_fusion.11), channel_id=1, source_target_pairs={{0,4},{4,0},{8,12},{12,8},{1,5},{5,1},{9,13},{13,9},{2,6},{6,2},{1... | collective-permute-start | bytes 1376264 | tf_op jit(solution)/shard_map/ppermute | solution.py:182
  102.2 3.6 %copy-start = (bf16[1792,2560]{1,0:T(8,128)(2,1)S(1)}, bf16[1792,2560]{1,0:T(8,128)(2,1)}, u32[]{:S(2)}) copy-start(bf16[1792,2560]{1,0:T(8,128)(2,1)} %weight.17) | copy-start | bytes 27525124
  105.8 11.6 %slice-start.9 = ((s8[7340032]{0:T(1024)(128)(4,1)}), s8[4194304]{0:T(1024)(128)(4,1)S(1)}, s32[]{:S(2)}) async-start(s8[7340032]{0:T(1024)(128)(4,1)} %bitcast.166), calls=%async_computation.9 | async-start | bytes 8388608
  109.6 3.6 %copy-start.1 = (bf16[1792,2560]{1,0:T(8,128)(2,1)S(1)}, bf16[1792,2560]{1,0:T(8,128)(2,1)}, u32[]{:S(2)}) copy-start(bf16[1792,2560]{1,0:T(8,128)(2,1)} %weight.16) | copy-start | bytes 27525124
  113.2 4.2 %slice-start.10 = ((s8[7340032]{0:T(1024)(128)(4,1)}), s8[3145728]{0:T(1024)(128)(4,1)S(1)}, s32[]{:S(2)}) async-start(s8[7340032]{0:T(1024)(128)(4,1)} %bitcast.166), calls=%async_computation.10 | async-start | bytes 6291456
  113.2 10.5 %slice-start = ((s8[9175040]{0:T(1024)(128)(4,1)}), s8[4194304]{0:T(1024)(128)(4,1)S(1)}, s32[]{:S(2)}) async-start(s8[9175040]{0:T(1024)(128)(4,1)} %bitcast.160), calls=%async_computation | async-start | bytes 8388608
  113.2 10.5 %slice-start.1 = ((s8[9175040]{0:T(1024)(128)(4,1)}), s8[4194304]{0:T(1024)(128)(4,1)S(1)}, s32[]{:S(2)}) async-start(s8[9175040]{0:T(1024)(128)(4,1)} %bitcast.160), calls=%async_computation.1 | async-start | bytes 8388608
  117.1 31.0 %collective-permute-start.18 = (bf16[2,1,64,2560]{3,2,1,0:T(8,128)(2,1)S(1)}, bf16[2,1,64,2560]{3,2,1,0:T(8,128)(2,1)S(1)}, u32[]{:S(2)}, u32[]{:S(2)}) collective-permute-start(bf16[2,1,64,2560]{3,2,1,0:T(8,128)(2,1)S(1)} %pad_maximum_fusion.4), channel_id=1, source_target_pairs={{0,1},{1,0},{2,3},{3,2},{4,5},{5,4},{6,7},{7,6},{8,9},{9,8},{10,11... | collective-permute-start | bytes 1966088 | tf_op jit(solution)/shard_map/ppermute | solution.py:182
  117.4 6.3 %slice-start.2 = ((s8[9175040]{0:T(1024)(128)(4,1)}), s8[786432]{0:T(1024)(128)(4,1)S(1)}, s32[]{:S(2)}) async-start(s8[9175040]{0:T(1024)(128)(4,1)} %bitcast.160), calls=%async_computation.2 | async-start | bytes 1572864
  117.4 10.1 %slice-start.3 = ((s8[9175040]{0:T(1024)(128)(4,1)}), s8[4194304]{0:T(1024)(128)(4,1)S(1)}, s32[]{:S(2)}) async-start(s8[9175040]{0:T(1024)(128)(4,1)} %bitcast.162), calls=%async_computation.3 | async-start | bytes 8388608
  117.4 10.1 %slice-start.4 = ((s8[9175040]{0:T(1024)(128)(4,1)}), s8[4194304]{0:T(1024)(128)(4,1)S(1)}, s32[]{:S(2)}) async-start(s8[9175040]{0:T(1024)(128)(4,1)} %bitcast.162), calls=%async_computation.4 | async-start | bytes 8388608
  121.3 13.3 %collective-permute-start.13 = (bf16[2,64,1792]{2,1,0:T(8,128)(2,1)S(1)}, bf16[2,64,1792]{2,1,0:T(8,128)(2,1)S(1)}, u32[]{:S(2)}, u32[]{:S(2)}) collective-permute-start(bf16[2,64,1792]{2,1,0:T(8,128)(2,1)S(1)} %pad_maximum_fusion.8), channel_id=1, source_target_pairs={{0,4},{4,0},{8,12},{12,8},{1,5},{5,1},{9,13},{13,9},{2,6},{6,2},{1... | collective-permute-start | bytes 1376264 | tf_op jit(solution)/shard_map/ppermute | solution.py:182
  123.7 3.9 %slice-start.5 = ((s8[9175040]{0:T(1024)(128)(4,1)}), s8[786432]{0:T(1024)(128)(4,1)S(1)}, s32[]{:S(2)}) async-start(s8[9175040]{0:T(1024)(128)(4,1)} %bitcast.162), calls=%async_computation.5 | async-start | bytes 1572864
  134.7 13.3 %collective-permute-start.14 = (bf16[64,1792]{1,0:T(8,128)(2,1)S(1)}, bf16[64,1792]{1,0:T(8,128)(2,1)S(1)}, u32[]{:S(2)}, u32[]{:S(2)}) collective-permute-start(bf16[64,1792]{1,0:T(8,128)(2,1)S(1)} %fusion.17), channel_id=1, source_target_pairs={{0,8},{4,12},{8,0},{12,4},{1,9},{5,13},{9,1},{13,5},{2,10},{6,14},... | collective-permute-start | bytes 688136 | tf_op jit(solution)/shard_map/ppermute | solution.py:182
  136.3 23.1 %collective-permute-start.20 = (bf16[2,1,64,2560]{3,2,1,0:T(8,128)(2,1)S(1)}, bf16[2,1,64,2560]{3,2,1,0:T(8,128)(2,1)S(1)}, u32[]{:S(2)}, u32[]{:S(2)}) collective-permute-start(bf16[2,1,64,2560]{3,2,1,0:T(8,128)(2,1)S(1)} %pad_maximum_fusion.5), channel_id=1, source_target_pairs={{0,1},{1,0},{2,3},{3,2},{4,5},{5,4},{6,7},{7,6},{8,9},{9,8},{10,11... | collective-permute-start | bytes 1966088 | tf_op jit(solution)/shard_map/ppermute | solution.py:182
  148.1 11.2 %collective-permute-start.15 = (bf16[64,1792]{1,0:T(8,128)(2,1)S(1)}, bf16[64,1792]{1,0:T(8,128)(2,1)S(1)}, u32[]{:S(2)}, u32[]{:S(2)}) collective-permute-start(bf16[64,1792]{1,0:T(8,128)(2,1)S(1)} %get-tuple-element.16), channel_id=1, source_target_pairs={{0,8},{4,12},{8,0},{12,4},{1,9},{5,13},{9,1},{13,5},{2,10},{6,14},... | collective-permute-start | bytes 688136 | tf_op jit(solution)/shard_map/ppermute | solution.py:182
  159.3 12.5 %collective-permute-start.16 = (bf16[128,1792]{1,0:T(8,128)(2,1)S(1)}, bf16[128,1792]{1,0:T(8,128)(2,1)S(1)}, u32[]{:S(2)}, u32[]{:S(2)}) collective-permute-start(bf16[128,1792]{1,0:T(8,128)(2,1)S(1)} %pad_maximum_fusion.10), channel_id=1, source_target_pairs={{0,4},{4,0},{8,12},{12,8},{1,5},{5,1},{9,13},{13,9},{2,6},{6,2},{1... | collective-permute-start | bytes 1376264 | tf_op jit(solution)/shard_map/ppermute | solution.py:182
  182.3 40.5 %slice-start.6 = ((s8[9175040]{0:T(1024)(128)(4,1)}), s8[786432]{0:T(1024)(128)(4,1)S(1)}, s32[]{:S(2)}) async-start(s8[9175040]{0:T(1024)(128)(4,1)} %bitcast.164), calls=%async_computation.6 | async-start | bytes 1572864
  183.5 34.1 %collective-permute-start.21 = (bf16[2,2,64,2560]{3,2,1,0:T(8,128)(2,1)}, bf16[2,2,64,2560]{3,2,1,0:T(8,128)(2,1)}, u32[]{:S(2)}, u32[]{:S(2)}) collective-permute-start(bf16[2,2,64,2560]{3,2,1,0:T(8,128)(2,1)} %pad_maximum_fusion), channel_id=1, source_target_pairs={{0,1},{1,0},{2,3},{3,2},{4,5},{5,4},{6,7},{7,6},{8,9},{9,8},{10,11... | collective-permute-start | bytes 3932168 | tf_op jit(solution)/shard_map/ppermute | solution.py:182
  183.6 2.6 collective-permute-start.25
  184.2 4.0 %collective-permute-start.26 = (f32[1,64]{1,0:T(1,128)S(1)}, f32[1,64]{1,0:T(1,128)S(1)}, u32[]{:S(2)}, u32[]{:S(2)}) collective-permute-start(f32[1,64]{1,0:T(1,128)S(1)} %fusion.44), channel_id=1, source_target_pairs={{0,1},{1,0},{2,3},{3,2},{4,5},{5,4},{6,7},{7,6},{8,9},{9,8},{10,11... | collective-permute-start | bytes 776 | tf_op jit(solution)/shard_map/ppermute | solution.py:182
  186.2 31.4 %collective-permute-start.22 = (bf16[2,1,64,2560]{3,2,1,0:T(8,128)(2,1)}, bf16[2,1,64,2560]{3,2,1,0:T(8,128)(2,1)}, u32[]{:S(2)}, u32[]{:S(2)}) collective-permute-start(bf16[2,1,64,2560]{3,2,1,0:T(8,128)(2,1)} %add_convert_fusion.1), channel_id=1, source_target_pairs={{0,2},{1,3},{2,0},{3,1},{4,6},{5,7},{6,4},{7,5},{8,10},{9,11},{10,... | collective-permute-start | bytes 1966088 | tf_op jit(solution)/shard_map/ppermute | solution.py:182
  186.9 30.7 %collective-permute-start.23 = (bf16[2,1,64,2560]{3,2,1,0:T(8,128)(2,1)}, bf16[2,1,64,2560]{3,2,1,0:T(8,128)(2,1)}, u32[]{:S(2)}, u32[]{:S(2)}) collective-permute-start(bf16[2,1,64,2560]{3,2,1,0:T(8,128)(2,1)} %add_convert_fusion), channel_id=1, source_target_pairs={{0,2},{1,3},{2,0},{3,1},{4,6},{5,7},{6,4},{7,5},{8,10},{9,11},{10,... | collective-permute-start | bytes 1966088 | tf_op jit(solution)/shard_map/ppermute | solution.py:182
  188.3 29.3 %collective-permute-start.27 = (f32[2,64]{1,0:T(2,128)S(1)}, f32[2,64]{1,0:T(2,128)S(1)}, u32[]{:S(2)}, u32[]{:S(2)}) collective-permute-start(f32[2,64]{1,0:T(2,128)S(1)} %pad_maximum_fusion.14), channel_id=1, source_target_pairs={{0,2},{1,3},{2,0},{3,1},{4,6},{5,7},{6,4},{7,5},{8,10},{9,11},{10,... | collective-permute-start | bytes 1544 | tf_op jit(solution)/shard_map/ppermute | solution.py:182
  189.1 28.4 %collective-permute-start.24 = (f32[2,64]{1,0:T(2,128)S(1)}, f32[2,64]{1,0:T(2,128)S(1)}, u32[]{:S(2)}, u32[]{:S(2)}) collective-permute-start(f32[2,64]{1,0:T(2,128)S(1)} %bitcast.191), channel_id=1, source_target_pairs={{0,1},{1,0},{2,3},{3,2},{4,5},{5,4},{6,7},{7,6},{8,9},{9,8},{10,11... | collective-permute-start | bytes 1544 | tf_op jit(solution)/shard_map/ppermute | solution.py:182
  217.6 5.3 %slice-start.7 = ((s8[9175040]{0:T(1024)(128)(4,1)}), s8[4194304]{0:T(1024)(128)(4,1)S(1)}, s32[]{:S(2)}) async-start(s8[9175040]{0:T(1024)(128)(4,1)} %bitcast.164), calls=%async_computation.7 | async-start | bytes 8388608
  220.0 2.9 %slice-start.8 = ((s8[9175040]{0:T(1024)(128)(4,1)}), s8[4194304]{0:T(1024)(128)(4,1)S(1)}, s32[]{:S(2)}) async-start(s8[9175040]{0:T(1024)(128)(4,1)} %bitcast.164), calls=%async_computation.8 | async-start | bytes 8388608
  220.6 2.2 collective-permute-start.29
  220.7 17.1 %collective-permute-start.28 = (bf16[128,2560]{1,0:T(8,128)(2,1)S(1)}, bf16[128,2560]{1,0:T(8,128)(2,1)S(1)}, u32[]{:S(2)}, u32[]{:S(2)}) collective-permute-start(bf16[128,2560]{1,0:T(8,128)(2,1)S(1)} %fusion.2), channel_id=1, source_target_pairs={{0,2},{1,3},{2,0},{3,1},{4,6},{5,7},{6,4},{7,5},{8,10},{9,11},{10,... | collective-permute-start | bytes 1966088 | tf_op jit(solution)/shard_map/ppermute | solution.py:182
  227.2 12.6 %collective-permute-start.30 = (bf16[2,64,1792]{2,1,0:T(8,128)(2,1)S(1)}, bf16[2,64,1792]{2,1,0:T(8,128)(2,1)S(1)}, u32[]{:S(2)}, u32[]{:S(2)}) collective-permute-start(bf16[2,64,1792]{2,1,0:T(8,128)(2,1)S(1)} %slice_bitcast_fusion.3), channel_id=1, source_target_pairs={{0,4},{4,0},{8,12},{12,8},{1,5},{5,1},{9,13},{13,9},{2,6},{6,2},{1... | collective-permute-start | bytes 1376264 | tf_op jit(solution)/shard_map/ppermute | solution.py:182
  239.8 2.1 collective-permute-start.31
  246.4 17.5 %collective-permute-start.32 = (bf16[2,64,1792]{2,1,0:T(8,128)(2,1)S(1)}, bf16[2,64,1792]{2,1,0:T(8,128)(2,1)S(1)}, u32[]{:S(2)}, u32[]{:S(2)}) collective-permute-start(bf16[2,64,1792]{2,1,0:T(8,128)(2,1)S(1)} %slice_bitcast_fusion.1), channel_id=1, source_target_pairs={{0,4},{4,0},{8,12},{12,8},{1,5},{5,1},{9,13},{13,9},{2,6},{6,2},{1... | collective-permute-start | bytes 1376264 | tf_op jit(solution)/shard_map/ppermute | solution.py:182
  246.9 17.8 %collective-permute-start.34 = (bf16[64,1792]{1,0:T(8,128)(2,1)S(1)}, bf16[64,1792]{1,0:T(8,128)(2,1)S(1)}, u32[]{:S(2)}, u32[]{:S(2)}) collective-permute-start(bf16[64,1792]{1,0:T(8,128)(2,1)S(1)} %fusion.19), channel_id=1, source_target_pairs={{0,8},{4,12},{8,0},{12,4},{1,9},{5,13},{9,1},{13,5},{2,10},{6,14},... | collective-permute-start | bytes 688136 | tf_op jit(solution)/shard_map/ppermute | solution.py:182
  264.1 12.5 %collective-permute-start.33 = (bf16[64,1792]{1,0:T(8,128)(2,1)S(1)}, bf16[64,1792]{1,0:T(8,128)(2,1)S(1)}, u32[]{:S(2)}, u32[]{:S(2)}) collective-permute-start(bf16[64,1792]{1,0:T(8,128)(2,1)S(1)} %fusion.18), channel_id=1, source_target_pairs={{0,8},{4,12},{8,0},{12,4},{1,9},{5,13},{9,1},{13,5},{2,10},{6,14},... | collective-permute-start | bytes 688136 | tf_op jit(solution)/shard_map/ppermute | solution.py:182

commit v6 on v4

--- a/solution.py
+++ b/solution.py
@@ -190,8 +190,26 @@
     return value.astype(jnp.float32)
 
 
-def matmul(a, b):
-    return jnp.dot(a, b, preferred_element_type=jnp.float32).astype(jnp.bfloat16)
+def streamed_kernel(count, *refs):
+    rows, weights, outs = refs[0], refs[1 : 1 + count], refs[1 + count :]
+    for weight, out in zip(weights, outs):
+        out[...] = jnp.dot(rows[...], weight[...], preferred_element_type=jnp.float32).astype(out.dtype)
+
+
+def matmuls(rows, weights):
+    row_count, depth = rows.shape
+    columns = weights[0].shape[1]
+    block = 256
+    return pl.pallas_call(
+        functools.partial(streamed_kernel, len(weights)),
+        grid=(columns // block,),
+        in_specs=[pl.BlockSpec((row_count, depth), lambda i: (0, 0))]
+        + [pl.BlockSpec((depth, block), lambda i: (0, i)) for _ in weights],
+        out_specs=[pl.BlockSpec((row_count, block), lambda i: (0, i)) for _ in weights],
+        out_shape=[jax.ShapeDtypeStruct((row_count, columns), jnp.bfloat16) for _ in weights],
+        compiler_params=pltpu.CompilerParams(vmem_limit_bytes=50 * 1024 * 1024),
+        cost_estimate=pl.CostEstimate(flops=1024, bytes_accessed=1024, transcendentals=0),
+    )(rows, *weights)
 
 
 def gather_keys(rotated_keys, n_ctx):
@@ -230,15 +248,6 @@
 
 def after(value, earlier):
     return lax.optimization_barrier((value, earlier))[0]
-
-
-def reduce_ctx(blocks):
-    flat = blocks.reshape(-1, blocks.shape[-1])
-    return wide(lax.psum_scatter(flat, "ctx", scatter_dimension=0, tiled=True))
-
-
-def gather_ctx(rows):
-    return lax.all_gather(rows, "ctx", axis=0, tiled=True)
 
 
 def paired_tail(
@@ -254,56 +263,94 @@
     own = spread_heads(heads_out, n_ctx, n_tp)
     own_all = jnp.stack(own)
     near = swap(own_all, "tp", 1)
-    far = swap(own_all, "tp", 2)
     residual_halves = residual.reshape(2, half, width)
 
-    def sum_heads(blocks, which):
-        head_sum = reduce_ctx(jnp.stack([pick(blocks, t ^ i) for i in range(n_ctx)]))
-        return (wide(pick(residual_halves, which)) + head_sum).astype(jnp.bfloat16)
-
-    blocks_a = matmul(pair_rows(own_all, near), output_weight).reshape(n_ctx, half, width)
-    far = after(far, blocks_a)
+    def first_hop(rows):
+        blocks = matmuls(rows, [output_weight])[0].reshape(n_ctx, half, width)
+        place = t ^ c
+        sent = jnp.stack([pick(blocks, place ^ 1), pick(blocks, place ^ 3)])
+        kept = [pick(blocks, place), pick(blocks, place ^ 2)]
+        return kept, sent, swap(sent, "ctx", 1)
+
+    def second_hop(kept, came):
+        other = (wide(kept[1]) + wide(came[1])).astype(jnp.bfloat16)
+        return wide(kept[0]) + wide(came[0]), other, swap(other, "ctx", 2)
+
+    def attend(mine, came, which):
+        return (wide(pick(residual_halves, which)) + mine + wide(came)).astype(jnp.bfloat16)
+
+    def side(value, which):
+        return lax.dynamic_index_in_dim(value, which, 1, keepdims=False)
+
+    def gate_up(rows):
+        values = wide(rows)
+        squares = jnp.sum(values * values, axis=1).reshape(-1, 2, half)
+        scaled = (values * norm_gain[None, :]).astype(jnp.bfloat16)
+        terms = [
+            term.reshape(-1, 2, half, term.shape[1])
+            for term in matmuls(scaled, [gate_weight, up_weight])
+        ]
+        sent = jnp.stack([side(term, 1 - core) for term in terms])
+        kept = jnp.stack([side(term, core) for term in terms])
+        return kept, sent, squares
+
+    kept_a, sent_a, came_a = first_hop(pair_rows(own_all, near))
+    far = swap(after(own_all, sent_a), "tp", 2)
+    mine_a, other_a, last_a = second_hop(kept_a, came_a)
+    far = after(far, other_a)
     far_near = swap(far, "tp", 1)
+    attended_a = attend(mine_a, last_a, first_half)
+    twin_a = swap(attended_a, "ctx", 2)
     order = [2, 3, 0, 1]
     rows_b = pair_rows([far[i] for i in order], [far_near[i] for i in order])
-    blocks_b = matmul(rows_b, output_weight).reshape(n_ctx, half, width)
-    attended_a = sum_heads(blocks_a, first_half)
-    all_a = gather_ctx(attended_a)
-    attended_b = sum_heads(after(blocks_b, attended_a), 1 - first_half)
-
-    def gate_up(all_rows):
-        values = wide(all_rows)
-        squares = jnp.sum(values * values, axis=1).reshape(2, 2 * half)
-        scaled = (values * norm_gain[None, :]).astype(jnp.bfloat16)
-        sums = [matmul(scaled, w).reshape(2, 2 * half, -1) for w in (gate_weight, up_weight)]
-        kept, came = [], []
-        for term in sums + [squares]:
-            came.append(swap(pick(term, 1 - core), "tp", 1))
-            kept.append(pick(term, core))
-        return kept, came
-
-    kept_a, came_a = gate_up(all_a)
-    chip_a = [(wide(k) + wide(r)).astype(k.dtype) for k, r in zip(kept_a, came_a)]
-    across = [swap(term, "tp", 2) for term in chip_a]
-    all_b = after(gather_ctx(attended_b), chip_a)
-    kept_b, came_b = gate_up(all_b)
-    gate, up, squares = [wide(k) + wide(r) + wide(x) for k, r, x in zip(kept_b, came_b, across)]
-    inverse_rms = lax.rsqrt(squares / model_width + norm_eps)[:, None]
-    hidden = (jax.nn.silu(gate * inverse_rms) * (up * inverse_rms)).astype(jnp.bfloat16)
+    kept_b, sent_b, came_b = first_hop(after(rows_b, attended_a))
+    pair_a = jnp.concatenate([attended_a, after(twin_a, sent_b)], axis=0)
+    rest_a = swap(pair_a, "ctx", 1)
+    kept_p, sent_p, squares_p = gate_up(pair_a)
+    came_p = swap(sent_p, "tp", 1)
+    mine_b, other_b, last_b = second_hop(kept_b, after(came_b, sent_p))
+    sums_p = (wide(kept_p) + wide(after(came_p, other_b))).astype(jnp.bfloat16)
+    across_p = swap(sums_p, "tp", 2)
+    kept_q, sent_q, squares_q = gate_up(after(rest_a, sums_p))
+    across_p, last_b, sent_q = lax.optimization_barrier((across_p, last_b, sent_q))
+    attended_b = attend(mine_b, last_b, 1 - first_half)
+    sums_q = (wide(kept_q) + wide(swap(sent_q, "tp", 1))).astype(jnp.bfloat16)
+    across_q = swap(sums_q, "tp", 2)
+    pair_b = jnp.concatenate([attended_b, swap(attended_b, "ctx", 2)], axis=0)
+    all_b = jnp.concatenate([pair_b, swap(pair_b, "ctx", 1)], axis=0)
+    all_b, across_q = lax.optimization_barrier((all_b, across_q))
+    kept, sent, squares_b = gate_up(all_b)
+    came = swap(sent, "tp", 1)
+    squares = jnp.stack([jnp.concatenate([squares_p, squares_q], axis=0), squares_b])
+    chip_squares = lax.dynamic_index_in_dim(squares, core, 2, keepdims=False) + swap(
+        lax.dynamic_index_in_dim(squares, 1 - core, 2, keepdims=False), "tp", 1
+    )
+    total_squares = chip_squares[1] + swap(chip_squares[0], "tp", 2)
+    inverse_rms = lax.rsqrt(total_squares / model_width + norm_eps)[:, :, None]
+    across = jnp.concatenate([across_p, across_q], axis=1)
+    gate = (wide(kept[0]) + wide(came[0]) + wide(across[0])) * inverse_rms
+    up = (wide(kept[1]) + wide(came[1]) + wide(across[1])) * inverse_rms
+    hidden = (jax.nn.silu(gate) * up).astype(jnp.bfloat16).reshape(2 * half, -1)
     hidden_near = swap(hidden, "tp", 1)
     hidden_far = swap(hidden, "tp", 2)
 
-    def down(mine, other):
-        blocks = matmul(jnp.concatenate([mine, other], axis=0), down_weight)
-        blocks = blocks.reshape(n_ctx, half, width)
-        return jnp.stack([pick(blocks, i ^ (2 * core)) for i in range(n_ctx)])
-
-    down_b = down(hidden, hidden_near)
-    out_b = (wide(attended_b) + reduce_ctx(down_b)).astype(jnp.bfloat16)
-    hidden_far = after(hidden_far, down_b)
+    def down_hop(mine, other):
+        blocks = matmuls(jnp.concatenate([mine, other], axis=0), [down_weight])[0]
+        blocks = blocks.reshape(2, 2, half, width)
+        return blocks[:, 0], swap(blocks[:, 1], "ctx", 1)
+
+    def down_second(kept, came):
+        pair = wide(kept) + wide(came)
+        other = pick(pair, 1 - core).astype(jnp.bfloat16)
+        return pick(pair, core), other, swap(other, "ctx", 2)
+
+    kept_b, came_b = down_hop(hidden, hidden_near)
+    hidden_far = after(hidden_far, kept_b)
     hidden_far_near = swap(hidden_far, "tp", 1)
-    down_a = down(hidden_far, hidden_far_near)
-    out_a = (wide(attended_a) + reduce_ctx(down_a)).astype(jnp.bfloat16)
+    down_b, other_b, last_b = down_second(kept_b, after(came_b, hidden_far))
+    down_a, _, last_a = down_second(*down_hop(hidden_far, after(hidden_far_near, other_b)))
+    out_b = (wide(attended_b) + down_b + wide(last_b)).astype(jnp.bfloat16)
+    out_a = (wide(attended_a) + down_a + wide(last_a)).astype(jnp.bfloat16)
 
     def in_order(a, b):
         first = first_half == 0
@@ -327,7 +374,7 @@
     row_count = residual.shape[0]
     ctx_place = lax.axis_index("ctx")
     n_ctx, n_tp = lax.axis_size("ctx"), lax.axis_size("tp")
-    paired = n_ctx == 4 and n_tp == 4 and row_count % 64 == 0
+    paired = n_ctx == 4 and n_tp == 4 and row_count % 64 == 0 and residual.shape[1] % 256 == 0
     own_index = ctx_place * row_count + jnp.arange(row_count, dtype=jnp.int32)
     _, own_position = trace_info(own_index, lengths)
     rotated_keys = rope_keys(latent, own_position, LAT)

time: 268 us -> 256 us (0.955)
  Pallas kernels: 6.62 us -> 68.3 us
  matrix products: 43.7 us -> 0 us
  blocking collectives: 38.4 us -> 0 us
  between operations: 14.4 us -> 1.46 us
  waiting for transfers between devices: 112 us -> 124 us
  starting transfers between devices: 32.5 us -> 42.5 us
  other arithmetic: 16.6 us -> 10.9 us
  local copies, waits for them, and re-layouts: 2.84 us -> 7.26 us
    ppermute x16 -> x26, waiting for transfers between devices: 22.1 us -> 105 us  [swap(): return lax.ppermute(value, axis_name, [(i, i ^ bit) for i in range(width)])]
    reduce_scatter x4 -> x0, waiting for transfers between devices: 73.9 us -> none  [reduce_ctx(): return wide(lax.psum_scatter(flat, 'ctx', scatter_dimension=0, tiled=True))]
    pallas_call x0 -> x7, Pallas kernels: none -> 61.7 us  [matmuls(): pl.pallas_call(functools.partial(streamed_kernel, len(weights)), grid=(co...]
    dot_general x8 -> x0, matrix products: 43.7 us -> none  [matmul(): jnp.dot(a, b, preferred_element_type=jnp.float32).astype(jnp.bfloat16)]
    all_gather x2 -> x0, blocking collectives: 38.4 us -> none  [gather_ctx(): return lax.all_gather(rows, 'ctx', axis=0, tiled=True)]
    ppermute x16 -> x26, starting transfers between devices: 14 us -> 25.7 us  [swap(): return lax.ppermute(value, axis_name, [(i, i ^ bit) for i in range(width)])]
    ppermute x4, waiting for transfers between devices: 15 us -> 17.8 us  [spread_heads(): lax.ppermute(pieces[s], ('ctx', 'tp'), [(c * n_tp + t, t * n_tp + (c ^ s)...]
    another operation x6 -> x9, other arithmetic: 5.19 us -> 2.43 us  [the longest x3 1.34 us: gate_up(): sent = jnp.stack([side(term, 1 - core) for term in terms])]
  transfers between devices with their start and end apart: 27 -> 33, of which waited for: 14 -> 19; matrix products, arithmetic and copies ran while one was open for 18% -> 3% of each run, Pallas kernels for 0% -> 19%
where the time goes in v6:
time: 256 us; the launch traced here: 254 us
  waiting for transfers between devices  124 us (48%)
  Pallas kernels  68.3 us (27%)
  starting transfers between devices  42.5 us (17%)
  other arithmetic  10.9 us (4%)
  local copies, waits for them, and re-layouts  7.26 us (3%)
    ppermute x26, waiting for transfers between devices, swap(): return lax.ppermute(value, axis_name, [(i, i ^ bit) for i in range(width)])  105 us
    pallas_call x7, Pallas kernels, matmuls(): pl.pallas_call(functools.partial(streamed_kernel, len(weights)), grid=(co...  61.7 us
    ppermute x26, starting transfers between devices, swap(): return lax.ppermute(value, axis_name, [(i, i ^ bit) for i in range(width)])  25.7 us
    ppermute x4, waiting for transfers between devices, spread_heads(): lax.ppermute(pieces[s], ('ctx', 'tp'), [(c * n_tp + t, t * n_tp + (c ^ s)...  17.8 us
    ppermute x3, starting transfers between devices, gather_keys(): lax.ppermute(half, 'ctx', [(c, c + d) for c in range(n_ctx - d)])  10.1 us
    ppermute x4, starting transfers between devices, spread_heads(): lax.ppermute(pieces[s], ('ctx', 'tp'), [(c * n_tp + t, t * n_tp + (c ^ s)...  6.7 us
    pallas_call x1, Pallas kernels, attention(): pl.pallas_call(functools.partial(attention_kernel, group), grid=(local_he...  6.62 us
  transfers between devices with their start and end apart: 33, of which 19 were waited for; matrix products, arithmetic and copies ran while one was open for 3% of the time, Pallas kernels for 19%

profile of v6, /device:TPU:0, one launch (start us, length us, event | category | flops | bytes accessed | tf_op | source)
XLA Modules:
  0.0 254.4 jit_solution(4479248492232476114)
XLA Ops:
  0.6 0.9 slice.104
  1.6 1.1 convert_element_type.229
  2.7 0.8 reduce-window.8
  3.5 0.7 subtract_subtract_fusion
  4.5 0.3 fusion.29
  4.8 5.9 %collective-permute-start.1 = (bf16[288,128]{1,0:T(8,128)(2,1)S(1)}, bf16[288,128]{1,0:T(8,128)(2,1)S(1)}, u32[]{:S(2)}, u32[]{:S(2)}) collective-permute-start(bf16[288,128]{1,0:T(8,128)(2,1)S(1)} %fusion.29), channel_id=1, source_target_pairs={{0,8},{4,12},{1,9},{5,13},{2,10},{6,14},{3,11},{7,15},{16,24},{20,... | collective-permute-start | bytes 221192 | tf_op jit(solution)/shard_map/ppermute | solution.py:220
  10.8 2.3 collective-permute-start
  13.1 1.8 collective-permute-start.2
  14.9 0.3 multiply_cosine_fusion
  15.7 1.2 collective-permute-done.2
  17.1 1.4 collective-permute-done.3
  18.6 6.6 %shard_map.113 = bf16[128,2048]{1,0:T(8,128)(2,1)S(1)} custom-call(f32[4,128,128]{2,1,0:T(8,128)S(1)} %pad_maximum_fusion.13.tables, s32[128,1]{1,0:T(8,128)S(1)} %copy.19.starts, s32[128,1]{1,0:T(8,128)S(1)} %iota_add_fusion.own_index, s32[1,512]{1,0:T(1,128)S(1)} %iota_add_fusion.1.key_index, bf16[576,512]{1,0:T(8,128)(2,1)S(1)} %maximum_maximum_fusion.keys, ...), custom_call_target="tpu_custom_call" | custom-call | flops 2684354560 | bytes 5046272 | tf_op jit(solution)/shard_map/pallas_call | solution.py:143
  25.5 5.1 %collective-permute-start.7 = (bf16[32,2048]{1,0:T(8,128)(2,1)S(1)}, bf16[32,2048]{1,0:T(8,128)(2,1)S(1)}, u32[]{:S(2)}, u32[]{:S(2)}) collective-permute-start(bf16[32,2048]{1,0:T(8,128)(2,1)S(1)} %get-tuple-element.72), channel_id=1, source_target_pairs={{0,3},{1,7},{2,11},{3,15},{4,2},{5,6},{6,10},{7,14},{8,1},{9,5},{1... | collective-permute-start | bytes 393224 | tf_op jit(solution)/shard_map/ppermute | solution.py:234
  30.6 0.6 collective-permute-start.6
  31.2 0.8 collective-permute-start.4
  32.0 5.0 %collective-permute-done.7 = bf16[32,2048]{1,0:T(8,128)(2,1)S(1)} collective-permute-done((bf16[32,2048]{1,0:T(8,128)(2,1)S(1)}, bf16[32,2048]{1,0:T(8,128)(2,1)S(1)}, u32[]{:S(2)}, u32[]{:S(2)}) %collective-permute-start.7) | collective-permute-done | bytes 131104 | tf_op jit(solution)/shard_map/ppermute | solution.py:234
  37.0 12.8 %collective-permute-done.6 = bf16[32,2048]{1,0:T(8,128)(2,1)S(1)} collective-permute-done((bf16[32,2048]{1,0:T(8,128)(2,1)S(1)}, bf16[32,2048]{1,0:T(8,128)(2,1)S(1)}, u32[]{:S(2)}, u32[]{:S(2)}) %collective-permute-start.6) | collective-permute-done | bytes 131104 | tf_op jit(solution)/shard_map/ppermute | solution.py:234
  50.0 1.9 collective-permute-done.8
  52.0 6.8 %shard_map.114 = bf16[256,1792]{1,0:T(8,128)(2,1)S(1)} custom-call(bf16[256,2048]{1,0:T(8,128)(2,1)S(1)} %constant_dynamic-update-slice_fusion.3.refs_0_, bf16[2048,1792]{1,0:T(8,128)(2,1)} %refs_1_.8), custom_call_target="tpu_custom_call" | custom-call | flops 1024 | bytes 1024 | tf_op jit(solution)/shard_map/pallas_call | solution.py:203
  58.9 1.3 collective-permute-start.9
  60.2 3.9 %collective-permute-start.11 = (bf16[4,32,2048]{2,1,0:T(8,128)(2,1)S(1)}, bf16[4,32,2048]{2,1,0:T(8,128)(2,1)S(1)}, u32[]{:S(2)}, u32[]{:S(2)}) collective-permute-start(bf16[4,32,2048]{2,1,0:T(8,128)(2,1)S(1)} %pad_maximum_fusion.6), channel_id=1, source_target_pairs={{0,2},{1,3},{2,0},{3,1},{4,6},{5,7},{6,4},{7,5},{8,10},{9,11},{10,... | collective-permute-start | bytes 1572872 | tf_op jit(solution)/shard_map/ppermute | solution.py:182
  64.1 7.4 %collective-permute-done.9 = bf16[2,64,1792]{2,1,0:T(8,128)(2,1)S(1)} collective-permute-done((bf16[2,64,1792]{2,1,0:T(8,128)(2,1)S(1)}, bf16[2,64,1792]{2,1,0:T(8,128)(2,1)S(1)}, u32[]{:S(2)}, u32[]{:S(2)}) %collective-permute-start.9) | collective-permute-done | bytes 458784 | tf_op jit(solution)/shard_map/ppermute | solution.py:182
  71.6 5.6 %collective-permute-start.10 = (bf16[64,1792]{1,0:T(8,128)(2,1)S(1)}, bf16[64,1792]{1,0:T(8,128)(2,1)S(1)}, u32[]{:S(2)}, u32[]{:S(2)}) collective-permute-start(bf16[64,1792]{1,0:T(8,128)(2,1)S(1)} %fusion.16), channel_id=1, source_target_pairs={{0,8},{4,12},{8,0},{12,4},{1,9},{5,13},{9,1},{13,5},{2,10},{6,14},... | collective-permute-start | bytes 688136 | tf_op jit(solution)/shard_map/ppermute | solution.py:182
  77.2 10.2 %collective-permute-done.10 = bf16[64,1792]{1,0:T(8,128)(2,1)S(1)} collective-permute-done((bf16[64,1792]{1,0:T(8,128)(2,1)S(1)}, bf16[64,1792]{1,0:T(8,128)(2,1)S(1)}, u32[]{:S(2)}, u32[]{:S(2)}) %collective-permute-start.10) | collective-permute-done | bytes 229408 | tf_op jit(solution)/shard_map/ppermute | solution.py:182
  87.8 6.8 %shard_map.115 = bf16[256,1792]{1,0:T(8,128)(2,1)S(1)} custom-call(bf16[256,2048]{1,0:T(8,128)(2,1)S(1)} %bitcast_dynamic-update-slice_fusion.refs_0_, bf16[2048,1792]{1,0:T(8,128)(2,1)} %refs_1_.8), custom_call_target="tpu_custom_call" | custom-call | flops 1024 | bytes 1024 | tf_op jit(solution)/shard_map/pallas_call | solution.py:203
  94.7 4.1 %collective-permute-start.13 = (bf16[2,64,1792]{2,1,0:T(8,128)(2,1)S(1)}, bf16[2,64,1792]{2,1,0:T(8,128)(2,1)S(1)}, u32[]{:S(2)}, u32[]{:S(2)}) collective-permute-start(bf16[2,64,1792]{2,1,0:T(8,128)(2,1)S(1)} %pad_maximum_fusion.8), channel_id=1, source_target_pairs={{0,4},{4,0},{8,12},{12,8},{1,5},{5,1},{9,13},{13,9},{2,6},{6,2},{1... | collective-permute-start | bytes 1376264 | tf_op jit(solution)/shard_map/ppermute | solution.py:182
  98.8 1.1 collective-permute-done.14
  100.0 0.2 fusion.7
  100.2 10.6 %shard_map.116 = (bf16[128,2560]{1,0:T(8,128)(2,1)S(1)}, bf16[128,2560]{1,0:T(8,128)(2,1)S(1)}) custom-call(bf16[128,1792]{1,0:T(8,128)(2,1)S(1)} %get-tuple-element.77.refs_0_, bf16[1792,2560]{1,0:T(8,128)(2,1)} %refs_1_.11, bf16[1792,2560]{1,0:T(8,128)(2,1)} %refs_2_.5), custom_call_target="tpu_custom_call" | custom-call | flops 1024 | bytes 1024 | tf_op jit(solution)/shard_map/pallas_call | solution.py:203
  111.3 1.8 collective-permute-start.17
  113.3 1.0 collective-permute-start.16
  114.3 14.7 %collective-permute-done.18 = bf16[128,1792]{1,0:T(8,128)(2,1)S(1)} collective-permute-done((bf16[128,1792]{1,0:T(8,128)(2,1)S(1)}, bf16[128,1792]{1,0:T(8,128)(2,1)S(1)}, u32[]{:S(2)}, u32[]{:S(2)}) %collective-permute-start.18) | collective-permute-done | bytes 458784 | tf_op jit(solution)/shard_map/ppermute | solution.py:182
  129.3 10.6 %shard_map.117 = (bf16[128,2560]{1,0:T(8,128)(2,1)S(1)}, bf16[128,2560]{1,0:T(8,128)(2,1)S(1)}) custom-call(bf16[128,1792]{1,0:T(8,128)(2,1)S(1)} %get-tuple-element.79.refs_0_, bf16[1792,2560]{1,0:T(8,128)(2,1)} %refs_1_.11, bf16[1792,2560]{1,0:T(8,128)(2,1)} %refs_2_.5), custom_call_target="tpu_custom_call" | custom-call | flops 1024 | bytes 1024 | tf_op jit(solution)/shard_map/pallas_call | solution.py:203
  140.2 0.8 copy-done.8
  141.0 0.8 broadcast_select_fusion.3
  142.0 11.9 %collective-permute-done.19 = bf16[64,1792]{1,0:T(8,128)(2,1)S(1)} collective-permute-done((bf16[64,1792]{1,0:T(8,128)(2,1)S(1)}, bf16[64,1792]{1,0:T(8,128)(2,1)S(1)}, u32[]{:S(2)}, u32[]{:S(2)}) %collective-permute-start.19) | collective-permute-done | bytes 229408 | tf_op jit(solution)/shard_map/ppermute | solution.py:182
  154.2 0.7 collective-permute-start.22
  154.9 11.5 %collective-permute-done.20 = bf16[128,1792]{1,0:T(8,128)(2,1)S(1)} collective-permute-done((bf16[128,1792]{1,0:T(8,128)(2,1)S(1)}, bf16[128,1792]{1,0:T(8,128)(2,1)S(1)}, u32[]{:S(2)}, u32[]{:S(2)}) %collective-permute-start.20) | collective-permute-done | bytes 458784 | tf_op jit(solution)/shard_map/ppermute | solution.py:182
  166.5 4.4 %collective-permute-done.22 = bf16[2,1,64,2560]{3,2,1,0:T(8,128)(2,1)S(1)} collective-permute-done((bf16[2,1,64,2560]{3,2,1,0:T(8,128)(2,1)S(1)}, bf16[2,1,64,2560]{3,2,1,0:T(8,128)(2,1)S(1)}, u32[]{:S(2)}, u32[]{:S(2)}) %collective-permute-start.22) | collective-permute-done | bytes 655392 | tf_op jit(solution)/shard_map/ppermute | solution.py:182
  170.9 0.3 fusion.1
  171.2 0.5 copy-done.5
  171.9 11.9 %shard_map.118 = (bf16[256,2560]{1,0:T(8,128)(2,1)S(1)}, bf16[256,2560]{1,0:T(8,128)(2,1)S(1)}) custom-call(bf16[256,1792]{1,0:T(8,128)(2,1)S(1)} %get-tuple-element.58.refs_0_, bf16[1792,2560]{1,0:T(8,128)(2,1)} %refs_1_.11, bf16[1792,2560]{1,0:T(8,128)(2,1)} %refs_2_.5), custom_call_target="tpu_custom_call" | custom-call | flops 1024 | bytes 1024 | tf_op jit(solution)/shard_map/pallas_call | solution.py:203
  183.8 1.0 dynamic-slice_bitcast_fusion
  184.8 0.9 dynamic-slice_bitcast_fusion.1
  185.7 1.2 pad_maximum_fusion
  187.0 0.5 collective-permute-start.23
  187.5 0.7 collective-permute-start.25
  188.3 2.9 %collective-permute-done.25 = f32[2,64]{1,0:T(2,128)S(1)} collective-permute-done((f32[2,64]{1,0:T(2,128)S(1)}, f32[2,64]{1,0:T(2,128)S(1)}, u32[]{:S(2)}, u32[]{:S(2)}) %collective-permute-start.25) | collective-permute-done | bytes 544 | tf_op jit(solution)/shard_map/ppermute | solution.py:182
  191.3 1.5 fusion.48
  192.9 1.0 fusion.4
  194.1 0.7 collective-permute-start.26
  194.7 1.4 collective-permute-done.27
  196.2 7.4 %shard_map.119 = bf16[256,1792]{1,0:T(8,128)(2,1)S(1)} custom-call(bf16[256,2560]{1,0:T(8,128)(2,1)S(1)} %pad_maximum_fusion.1.refs_0_, bf16[2560,1792]{1,0:T(8,128)(2,1)} %refs_1_.13), custom_call_target="tpu_custom_call" | custom-call | flops 1024 | bytes 1024 | tf_op jit(solution)/shard_map/pallas_call | solution.py:203
  203.7 1.8 collective-permute-start.29
  205.5 5.7 %collective-permute-done.26 = bf16[128,2560]{1,0:T(8,128)(2,1)S(1)} collective-permute-done((bf16[128,2560]{1,0:T(8,128)(2,1)S(1)}, bf16[128,2560]{1,0:T(8,128)(2,1)S(1)}, u32[]{:S(2)}, u32[]{:S(2)}) %collective-permute-start.26) | collective-permute-done | bytes 655392 | tf_op jit(solution)/shard_map/ppermute | solution.py:182
  211.2 5.1 %collective-permute-done.29 = bf16[2,64,1792]{2,1,0:T(8,128)(2,1)S(1)} collective-permute-done((bf16[2,64,1792]{2,1,0:T(8,128)(2,1)S(1)}, bf16[2,64,1792]{2,1,0:T(8,128)(2,1)S(1)}, u32[]{:S(2)}, u32[]{:S(2)}) %collective-permute-start.29) | collective-permute-done | bytes 458784 | tf_op jit(solution)/shard_map/ppermute | solution.py:182
  216.6 7.4 %shard_map.120 = bf16[256,1792]{1,0:T(8,128)(2,1)S(1)} custom-call(bf16[256,2560]{1,0:T(8,128)(2,1)S(1)} %pad_maximum_fusion.2.refs_0_, bf16[2560,1792]{1,0:T(8,128)(2,1)} %refs_1_.13), custom_call_target="tpu_custom_call" | custom-call | flops 1024 | bytes 1024 | tf_op jit(solution)/shard_map/pallas_call | solution.py:203
  224.0 1.8 collective-permute-start.30
  225.8 1.0 collective-permute-start.32
  226.8 13.9 %collective-permute-done.30 = bf16[2,64,1792]{2,1,0:T(8,128)(2,1)S(1)} collective-permute-done((bf16[2,64,1792]{2,1,0:T(8,128)(2,1)S(1)}, bf16[2,64,1792]{2,1,0:T(8,128)(2,1)S(1)}, u32[]{:S(2)}, u32[]{:S(2)}) %collective-permute-start.30) | collective-permute-done | bytes 458784 | tf_op jit(solution)/shard_map/ppermute | solution.py:182
  240.9 0.3 collective-permute-start.31
  241.2 11.2 %collective-permute-done.31 = bf16[64,1792]{1,0:T(8,128)(2,1)S(1)} collective-permute-done((bf16[64,1792]{1,0:T(8,128)(2,1)S(1)}, bf16[64,1792]{1,0:T(8,128)(2,1)S(1)}, u32[]{:S(2)}, u32[]{:S(2)}) %collective-permute-start.31) | collective-permute-done | bytes 229408 | tf_op jit(solution)/shard_map/ppermute | solution.py:182
  252.7 0.8 pad_maximum_fusion.12
  253.6 0.8 pad_maximum_fusion.10
  (123 shorter events, 5.2 us)
Async XLA Ops:
  1.6 17.0 %copy-start.1 = (bf16[512,2048]{1,0:T(8,128)(2,1)S(1)}, bf16[512,2048]{1,0:T(8,128)(2,1)}, u32[]{:S(2)}) copy-start(bf16[512,2048]{1,0:T(8,128)(2,1)} %value_weight.1) | copy-start | bytes 6291460
  4.8 10.8 %collective-permute-start.1 = (bf16[288,128]{1,0:T(8,128)(2,1)S(1)}, bf16[288,128]{1,0:T(8,128)(2,1)S(1)}, u32[]{:S(2)}, u32[]{:S(2)}) collective-permute-start(bf16[288,128]{1,0:T(8,128)(2,1)S(1)} %fusion.29), channel_id=1, source_target_pairs={{0,8},{4,12},{1,9},{5,13},{2,10},{6,14},{3,11},{7,15},{16,24},{20,... | collective-permute-start | bytes 221192 | tf_op jit(solution)/shard_map/ppermute | solution.py:220
  10.8 4.9 %collective-permute-start = (bf16[288,128]{1,0:T(8,128)(2,1)S(1)}, bf16[288,128]{1,0:T(8,128)(2,1)S(1)}, u32[]{:S(2)}, u32[]{:S(2)}) collective-permute-start(bf16[288,128]{1,0:T(8,128)(2,1)S(1)} %fusion.29), channel_id=1, source_target_pairs={{0,12},{1,13},{2,14},{3,15},{16,28},{17,29},{18,30},{19,31}} | collective-permute-start | bytes 221192 | tf_op jit(solution)/shard_map/ppermute | solution.py:220
  13.1 3.8 %collective-permute-start.2 = (bf16[288,128]{1,0:T(8,128)(2,1)S(1)}, bf16[288,128]{1,0:T(8,128)(2,1)S(1)}, u32[]{:S(2)}, u32[]{:S(2)}) collective-permute-start(bf16[288,128]{1,0:T(8,128)(2,1)S(1)} %fusion.29), channel_id=1, source_target_pairs={{0,4},{4,8},{8,12},{1,5},{5,9},{9,13},{2,6},{6,10},{10,14},{3,7},{... | collective-permute-start | bytes 221192 | tf_op jit(solution)/shard_map/ppermute | solution.py:220
  16.9 1.7 copy-start
  16.9 1.5 collective-permute-start.3
  25.3 6.7 %collective-permute-start.5 = (bf16[32,2048]{1,0:T(8,128)(2,1)S(1)}, bf16[32,2048]{1,0:T(8,128)(2,1)S(1)}, u32[]{:S(2)}, u32[]{:S(2)}) collective-permute-start(bf16[32,2048]{1,0:T(8,128)(2,1)S(1)} %get-tuple-element.71), channel_id=1, source_target_pairs={{0,1},{1,5},{2,9},{3,13},{4,0},{5,4},{6,8},{7,12},{8,3},{9,7},{10,... | collective-permute-start | bytes 393224 | tf_op jit(solution)/shard_map/ppermute | solution.py:234
  25.5 11.5 %collective-permute-start.7 = (bf16[32,2048]{1,0:T(8,128)(2,1)S(1)}, bf16[32,2048]{1,0:T(8,128)(2,1)S(1)}, u32[]{:S(2)}, u32[]{:S(2)}) collective-permute-start(bf16[32,2048]{1,0:T(8,128)(2,1)S(1)} %get-tuple-element.72), channel_id=1, source_target_pairs={{0,3},{1,7},{2,11},{3,15},{4,2},{5,6},{6,10},{7,14},{8,1},{9,5},{1... | collective-permute-start | bytes 393224 | tf_op jit(solution)/shard_map/ppermute | solution.py:234
  30.6 19.2 %collective-permute-start.6 = (bf16[32,2048]{1,0:T(8,128)(2,1)S(1)}, bf16[32,2048]{1,0:T(8,128)(2,1)S(1)}, u32[]{:S(2)}, u32[]{:S(2)}) collective-permute-start(bf16[32,2048]{1,0:T(8,128)(2,1)S(1)} %get-tuple-element.73), channel_id=1, source_target_pairs={{0,2},{1,6},{2,10},{3,14},{4,3},{5,7},{6,11},{7,15},{8,0},{9,4},{1... | collective-permute-start | bytes 393224 | tf_op jit(solution)/shard_map/ppermute | solution.py:234
  31.2 18.7 %collective-permute-start.4 = (bf16[32,2048]{1,0:T(8,128)(2,1)S(1)}, bf16[32,2048]{1,0:T(8,128)(2,1)S(1)}, u32[]{:S(2)}, u32[]{:S(2)}) collective-permute-start(bf16[32,2048]{1,0:T(8,128)(2,1)S(1)} %get-tuple-element.74), channel_id=1, source_target_pairs={{0,0},{1,4},{2,8},{3,12},{4,1},{5,5},{6,9},{7,13},{8,2},{9,6},{10,... | collective-permute-start | bytes 393224 | tf_op jit(solution)/shard_map/ppermute | solution.py:234
  49.9 2.0 collective-permute-start.8
  58.8 28.6 %copy-start.7 = (bf16[128,1792]{1,0:T(8,128)(2,1)S(1)}, bf16[128,1792]{1,0:T(8,128)(2,1)}, u32[]{:S(2)}) copy-start(bf16[128,1792]{1,0:T(8,128)(2,1)} %param.10) | copy-start | bytes 1376260
  58.9 12.6 %collective-permute-start.9 = (bf16[2,64,1792]{2,1,0:T(8,128)(2,1)S(1)}, bf16[2,64,1792]{2,1,0:T(8,128)(2,1)S(1)}, u32[]{:S(2)}, u32[]{:S(2)}) collective-permute-start(bf16[2,64,1792]{2,1,0:T(8,128)(2,1)S(1)} %pad_maximum_fusion.7), channel_id=1, source_target_pairs={{0,4},{4,0},{8,12},{12,8},{1,5},{5,1},{9,13},{13,9},{2,6},{6,2},{1... | collective-permute-start | bytes 1376264 | tf_op jit(solution)/shard_map/ppermute | solution.py:182
  60.2 17.0 %collective-permute-start.11 = (bf16[4,32,2048]{2,1,0:T(8,128)(2,1)S(1)}, bf16[4,32,2048]{2,1,0:T(8,128)(2,1)S(1)}, u32[]{:S(2)}, u32[]{:S(2)}) collective-permute-start(bf16[4,32,2048]{2,1,0:T(8,128)(2,1)S(1)} %pad_maximum_fusion.6), channel_id=1, source_target_pairs={{0,2},{1,3},{2,0},{3,1},{4,6},{5,7},{6,4},{7,5},{8,10},{9,11},{10,... | collective-permute-start | bytes 1572872 | tf_op jit(solution)/shard_map/ppermute | solution.py:182
  71.6 15.8 %collective-permute-start.10 = (bf16[64,1792]{1,0:T(8,128)(2,1)S(1)}, bf16[64,1792]{1,0:T(8,128)(2,1)S(1)}, u32[]{:S(2)}, u32[]{:S(2)}) collective-permute-start(bf16[64,1792]{1,0:T(8,128)(2,1)S(1)} %fusion.16), channel_id=1, source_target_pairs={{0,8},{4,12},{8,0},{12,4},{1,9},{5,13},{9,1},{13,5},{2,10},{6,14},... | collective-permute-start | bytes 688136 | tf_op jit(solution)/shard_map/ppermute | solution.py:182
  77.2 10.4 %collective-permute-start.12 = (bf16[4,32,2048]{2,1,0:T(8,128)(2,1)S(1)}, bf16[4,32,2048]{2,1,0:T(8,128)(2,1)S(1)}, u32[]{:S(2)}, u32[]{:S(2)}) collective-permute-start(bf16[4,32,2048]{2,1,0:T(8,128)(2,1)S(1)} %collective-permute-done.11), channel_id=1, source_target_pairs={{0,1},{1,0},{2,3},{3,2},{4,5},{5,4},{6,7},{7,6},{8,9},{9,8},{10,11... | collective-permute-start | bytes 1572872 | tf_op jit(solution)/shard_map/ppermute | solution.py:182
  87.5 12.4 %collective-permute-start.14 = (bf16[64,1792]{1,0:T(8,128)(2,1)S(1)}, bf16[64,1792]{1,0:T(8,128)(2,1)S(1)}, u32[]{:S(2)}, u32[]{:S(2)}) collective-permute-start(bf16[64,1792]{1,0:T(8,128)(2,1)S(1)} %fusion.15), channel_id=1, source_target_pairs={{0,8},{4,12},{8,0},{12,4},{1,9},{5,13},{9,1},{13,5},{2,10},{6,14},... | collective-permute-start | bytes 688136 | tf_op jit(solution)/shard_map/ppermute | solution.py:182
  94.6 5.4 %copy-start.9 = (f32[1792]{0:T(1024)S(1)}, f32[1792]{0:T(1024)}, u32[]{:S(2)}) copy-start(f32[1792]{0:T(1024)} %param.16) | copy-start | bytes 21508
  94.7 16.6 %collective-permute-start.13 = (bf16[2,64,1792]{2,1,0:T(8,128)(2,1)S(1)}, bf16[2,64,1792]{2,1,0:T(8,128)(2,1)S(1)}, u32[]{:S(2)}, u32[]{:S(2)}) collective-permute-start(bf16[2,64,1792]{2,1,0:T(8,128)(2,1)S(1)} %pad_maximum_fusion.8), channel_id=1, source_target_pairs={{0,4},{4,0},{8,12},{12,8},{1,5},{5,1},{9,13},{13,9},{2,6},{6,2},{1... | collective-permute-start | bytes 1376264 | tf_op jit(solution)/shard_map/ppermute | solution.py:182
  111.0 2.2 collective-permute-start.15
  111.1 17.9 %collective-permute-start.18 = (bf16[128,1792]{1,0:T(8,128)(2,1)S(1)}, bf16[128,1792]{1,0:T(8,128)(2,1)S(1)}, u32[]{:S(2)}, u32[]{:S(2)}) collective-permute-start(bf16[128,1792]{1,0:T(8,128)(2,1)S(1)} %pad_maximum_fusion.9), channel_id=1, source_target_pairs={{0,4},{4,0},{8,12},{12,8},{1,5},{5,1},{9,13},{13,9},{2,6},{6,2},{1... | collective-permute-start | bytes 1376264 | tf_op jit(solution)/shard_map/ppermute | solution.py:182
  111.3 28.8 %collective-permute-start.17 = (bf16[64,1792]{1,0:T(8,128)(2,1)S(1)}, bf16[64,1792]{1,0:T(8,128)(2,1)S(1)}, u32[]{:S(2)}, u32[]{:S(2)}) collective-permute-start(bf16[64,1792]{1,0:T(8,128)(2,1)S(1)} %fusion.17), channel_id=1, source_target_pairs={{0,8},{4,12},{8,0},{12,4},{1,9},{5,13},{9,1},{13,5},{2,10},{6,14},... | collective-permute-start | bytes 688136 | tf_op jit(solution)/shard_map/ppermute | solution.py:182
  113.3 26.8 %collective-permute-start.16 = (bf16[2,1,64,2560]{3,2,1,0:T(8,128)(2,1)S(1)}, bf16[2,1,64,2560]{3,2,1,0:T(8,128)(2,1)S(1)}, u32[]{:S(2)}, u32[]{:S(2)}) collective-permute-start(bf16[2,1,64,2560]{3,2,1,0:T(8,128)(2,1)S(1)} %add_convert_fusion.1), channel_id=1, source_target_pairs={{0,2},{1,3},{2,0},{3,1},{4,6},{5,7},{6,4},{7,5},{8,10},{9,11},{10,... | collective-permute-start | bytes 1966088 | tf_op jit(solution)/shard_map/ppermute | solution.py:182
  140.0 1.0 copy-start.8
  140.1 13.8 %collective-permute-start.21 = (bf16[2,1,64,2560]{3,2,1,0:T(8,128)(2,1)S(1)}, bf16[2,1,64,2560]{3,2,1,0:T(8,128)(2,1)S(1)}, u32[]{:S(2)}, u32[]{:S(2)}) collective-permute-start(bf16[2,1,64,2560]{3,2,1,0:T(8,128)(2,1)S(1)} %pad_maximum_fusion.5), channel_id=1, source_target_pairs={{0,1},{1,0},{2,3},{3,2},{4,5},{5,4},{6,7},{7,6},{8,9},{9,8},{10,11... | collective-permute-start | bytes 1966088 | tf_op jit(solution)/shard_map/ppermute | solution.py:182
  141.8 12.0 %collective-permute-start.19 = (bf16[64,1792]{1,0:T(8,128)(2,1)S(1)}, bf16[64,1792]{1,0:T(8,128)(2,1)S(1)}, u32[]{:S(2)}, u32[]{:S(2)}) collective-permute-start(bf16[64,1792]{1,0:T(8,128)(2,1)S(1)} %get-tuple-element.48), channel_id=1, source_target_pairs={{0,8},{4,12},{8,0},{12,4},{1,9},{5,13},{9,1},{13,5},{2,10},{6,14},... | collective-permute-start | bytes 688136 | tf_op jit(solution)/shard_map/ppermute | solution.py:182
  153.9 12.5 %collective-permute-start.20 = (bf16[128,1792]{1,0:T(8,128)(2,1)S(1)}, bf16[128,1792]{1,0:T(8,128)(2,1)S(1)}, u32[]{:S(2)}, u32[]{:S(2)}) collective-permute-start(bf16[128,1792]{1,0:T(8,128)(2,1)S(1)} %pad_maximum_fusion.11), channel_id=1, source_target_pairs={{0,4},{4,0},{8,12},{12,8},{1,5},{5,1},{9,13},{13,9},{2,6},{6,2},{1... | collective-permute-start | bytes 1376264 | tf_op jit(solution)/shard_map/ppermute | solution.py:182
  154.2 16.7 %collective-permute-start.22 = (bf16[2,1,64,2560]{3,2,1,0:T(8,128)(2,1)S(1)}, bf16[2,1,64,2560]{3,2,1,0:T(8,128)(2,1)S(1)}, u32[]{:S(2)}, u32[]{:S(2)}) collective-permute-start(bf16[2,1,64,2560]{3,2,1,0:T(8,128)(2,1)S(1)} %add_convert_fusion), channel_id=1, source_target_pairs={{0,2},{1,3},{2,0},{3,1},{4,6},{5,7},{6,4},{7,5},{8,10},{9,11},{10,... | collective-permute-start | bytes 1966088 | tf_op jit(solution)/shard_map/ppermute | solution.py:182
  170.9 0.8 copy-start.5
  171.8 15.7 %collective-permute-start.24 = (f32[2,2,64]{2,1,0:T(2,128)S(1)}, f32[2,2,64]{2,1,0:T(2,128)S(1)}, u32[]{:S(2)}, u32[]{:S(2)}) collective-permute-start(f32[2,2,64]{2,1,0:T(2,128)S(1)} %bitcast.185), channel_id=1, source_target_pairs={{0,1},{1,0},{2,3},{3,2},{4,5},{5,4},{6,7},{7,6},{8,9},{9,8},{10,11... | collective-permute-start | bytes 3080 | tf_op jit(solution)/shard_map/ppermute | solution.py:182
  185.7 1.7 copy-start.6
  187.0 4.3 %collective-permute-start.23 = (bf16[2,2,64,2560]{3,2,1,0:T(8,128)(2,1)}, bf16[2,2,64,2560]{3,2,1,0:T(8,128)(2,1)}, u32[]{:S(2)}, u32[]{:S(2)}) collective-permute-start(bf16[2,2,64,2560]{3,2,1,0:T(8,128)(2,1)} %pad_maximum_fusion), channel_id=1, source_target_pairs={{0,1},{1,0},{2,3},{3,2},{4,5},{5,4},{6,7},{7,6},{8,9},{9,8},{10,11... | collective-permute-start | bytes 3932168 | tf_op jit(solution)/shard_map/ppermute | solution.py:182
  187.5 3.6 %collective-permute-start.25 = (f32[2,64]{1,0:T(2,128)S(1)}, f32[2,64]{1,0:T(2,128)S(1)}, u32[]{:S(2)}, u32[]{:S(2)}) collective-permute-start(f32[2,64]{1,0:T(2,128)S(1)} %slice_bitcast_fusion.12), channel_id=1, source_target_pairs={{0,2},{1,3},{2,0},{3,1},{4,6},{5,7},{6,4},{7,5},{8,10},{9,11},{10,... | collective-permute-start | bytes 1544 | tf_op jit(solution)/shard_map/ppermute | solution.py:182
  191.2 1.5 copy-start.2
  191.3 1.7 copy-start.3
  194.0 2.2 collective-permute-start.27
  194.1 17.1 %collective-permute-start.26 = (bf16[128,2560]{1,0:T(8,128)(2,1)S(1)}, bf16[128,2560]{1,0:T(8,128)(2,1)S(1)}, u32[]{:S(2)}, u32[]{:S(2)}) collective-permute-start(bf16[128,2560]{1,0:T(8,128)(2,1)S(1)} %fusion.4), channel_id=1, source_target_pairs={{0,2},{1,3},{2,0},{3,1},{4,6},{5,7},{6,4},{7,5},{8,10},{9,11},{10,... | collective-permute-start | bytes 1966088 | tf_op jit(solution)/shard_map/ppermute | solution.py:182
  203.7 12.6 %collective-permute-start.29 = (bf16[2,64,1792]{2,1,0:T(8,128)(2,1)S(1)}, bf16[2,64,1792]{2,1,0:T(8,128)(2,1)S(1)}, u32[]{:S(2)}, u32[]{:S(2)}) collective-permute-start(bf16[2,64,1792]{2,1,0:T(8,128)(2,1)S(1)} %slice_bitcast_fusion.2), channel_id=1, source_target_pairs={{0,4},{4,0},{8,12},{12,8},{1,5},{5,1},{9,13},{13,9},{2,6},{6,2},{1... | collective-permute-start | bytes 1376264 | tf_op jit(solution)/shard_map/ppermute | solution.py:182
  211.2 5.3 %collective-permute-start.28 = (bf16[128,2560]{1,0:T(8,128)(2,1)S(1)}, bf16[128,2560]{1,0:T(8,128)(2,1)S(1)}, u32[]{:S(2)}, u32[]{:S(2)}) collective-permute-start(bf16[128,2560]{1,0:T(8,128)(2,1)S(1)} %collective-permute-done.26), channel_id=1, source_target_pairs={{0,1},{1,0},{2,3},{3,2},{4,5},{5,4},{6,7},{7,6},{8,9},{9,8},{10,11... | collective-permute-start | bytes 1966088 | tf_op jit(solution)/shard_map/ppermute | solution.py:182
  224.0 16.7 %collective-permute-start.30 = (bf16[2,64,1792]{2,1,0:T(8,128)(2,1)S(1)}, bf16[2,64,1792]{2,1,0:T(8,128)(2,1)S(1)}, u32[]{:S(2)}, u32[]{:S(2)}) collective-permute-start(bf16[2,64,1792]{2,1,0:T(8,128)(2,1)S(1)} %slice_bitcast_fusion), channel_id=1, source_target_pairs={{0,4},{4,0},{8,12},{12,8},{1,5},{5,1},{9,13},{13,9},{2,6},{6,2},{1... | collective-permute-start | bytes 1376264 | tf_op jit(solution)/shard_map/ppermute | solution.py:182
  225.8 15.4 %collective-permute-start.32 = (bf16[64,1792]{1,0:T(8,128)(2,1)S(1)}, bf16[64,1792]{1,0:T(8,128)(2,1)S(1)}, u32[]{:S(2)}, u32[]{:S(2)}) collective-permute-start(bf16[64,1792]{1,0:T(8,128)(2,1)S(1)} %fusion.18), channel_id=1, source_target_pairs={{0,8},{4,12},{8,0},{12,4},{1,9},{5,13},{9,1},{13,5},{2,10},{6,14},... | collective-permute-start | bytes 688136 | tf_op jit(solution)/shard_map/ppermute | solution.py:182
  240.9 11.5 %collective-permute-start.31 = (bf16[64,1792]{1,0:T(8,128)(2,1)S(1)}, bf16[64,1792]{1,0:T(8,128)(2,1)S(1)}, u32[]{:S(2)}, u32[]{:S(2)}) collective-permute-start(bf16[64,1792]{1,0:T(8,128)(2,1)S(1)} %fusion.19), channel_id=1, source_target_pairs={{0,8},{4,12},{8,0},{12,4},{1,9},{5,13},{9,1},{13,5},{2,10},{6,14},... | collective-permute-start | bytes 688136 | tf_op jit(solution)/shard_map/ppermute | solution.py:182
  252.6 1.0 copy-start.4

commit v7 on v6

--- a/solution.py
+++ b/solution.py
@@ -160,7 +160,7 @@
             pltpu.VMEM((key_count, LAT), jnp.bfloat16),
             pltpu.VMEM((row_count, key_count), jnp.float32),
         ],
-        compiler_params=pltpu.CompilerParams(vmem_limit_bytes=40 * 1024 * 1024),
+        compiler_params=pltpu.CompilerParams(vmem_limit_bytes=(6 + key_count // 64) * 1024 * 1024),
         cost_estimate=pl.CostEstimate(
             flops=2 * row_count * local_heads * (key_count * (deep + LAT) + LAT * VHEAD),
             bytes_accessed=2 * (queries.size + keys.size + value_weight.size),
@@ -190,26 +190,39 @@
     return value.astype(jnp.float32)
 
 
-def streamed_kernel(count, *refs):
-    rows, weights, outs = refs[0], refs[1 : 1 + count], refs[1 + count :]
-    for weight, out in zip(weights, outs):
-        out[...] = jnp.dot(rows[...], weight[...], preferred_element_type=jnp.float32).astype(out.dtype)
-
-
-def matmuls(rows, weights):
-    row_count, depth = rows.shape
-    columns = weights[0].shape[1]
-    block = 256
+def matmul(a, b):
+    return jnp.dot(a, b, preferred_element_type=jnp.float32).astype(jnp.bfloat16)
+
+
+def load_kernel(chunks, weight, out, sems):
+    rows = weight.shape[0] // chunks
+    copies = [
+        pltpu.make_async_copy(
+            weight.at[pl.ds(i * rows, rows)], out.at[pl.ds(i * rows, rows)], sems.at[i]
+        )
+        for i in range(chunks)
+    ]
+    for copy in copies:
+        copy.start()
+    for copy in copies:
+        copy.wait()
+
+
+def load(weight, grant):
+    chunks = 8
     return pl.pallas_call(
-        functools.partial(streamed_kernel, len(weights)),
-        grid=(columns // block,),
-        in_specs=[pl.BlockSpec((row_count, depth), lambda i: (0, 0))]
-        + [pl.BlockSpec((depth, block), lambda i: (0, i)) for _ in weights],
-        out_specs=[pl.BlockSpec((row_count, block), lambda i: (0, i)) for _ in weights],
-        out_shape=[jax.ShapeDtypeStruct((row_count, columns), jnp.bfloat16) for _ in weights],
-        compiler_params=pltpu.CompilerParams(vmem_limit_bytes=50 * 1024 * 1024),
-        cost_estimate=pl.CostEstimate(flops=1024, bytes_accessed=1024, transcendentals=0),
-    )(rows, *weights)
+        functools.partial(load_kernel, chunks),
+        in_specs=[pl.BlockSpec(memory_space=pltpu.HBM)],
+        out_specs=pl.BlockSpec(memory_space=pltpu.VMEM),
+        out_shape=pltpu.VMEM(weight.shape, weight.dtype),
+        scratch_shapes=[pltpu.SemaphoreType.DMA((chunks,))],
+        compiler_params=pltpu.CompilerParams(vmem_limit_bytes=grant * 1024 * 1024),
+        cost_estimate=pl.CostEstimate(flops=0, bytes_accessed=1024, transcendentals=0),
+    )(weight)
+
+
+def after(value, earlier):
+    return lax.optimization_barrier((value, earlier))[0]
 
 
 def gather_keys(rotated_keys, n_ctx):
@@ -246,10 +259,6 @@
     )
 
 
-def after(value, earlier):
-    return lax.optimization_barrier((value, earlier))[0]
-
-
 def paired_tail(
     heads_out, residual, output_weight, norm_gain, gate_weight, up_weight, down_weight, n_ctx, n_tp
 ):
@@ -261,12 +270,14 @@
     core = t & 1
     first_half = (t >> 1) ^ (c >> 1)
     own = spread_heads(heads_out, n_ctx, n_tp)
-    own_all = jnp.stack(own)
+    gate_weight = load(after(gate_weight, heads_out), 44)
+    up_weight = load(after(up_weight, gate_weight), 34)
+    own_all = jnp.stack(after(own, up_weight))
     near = swap(own_all, "tp", 1)
     residual_halves = residual.reshape(2, half, width)
 
     def first_hop(rows):
-        blocks = matmuls(rows, [output_weight])[0].reshape(n_ctx, half, width)
+        blocks = matmul(rows, output_weight).reshape(n_ctx, half, width)
         place = t ^ c
         sent = jnp.stack([pick(blocks, place ^ 1), pick(blocks, place ^ 3)])
         kept = [pick(blocks, place), pick(blocks, place ^ 2)]
@@ -288,7 +299,7 @@
         scaled = (values * norm_gain[None, :]).astype(jnp.bfloat16)
         terms = [
             term.reshape(-1, 2, half, term.shape[1])
-            for term in matmuls(scaled, [gate_weight, up_weight])
+            for term in [matmul(scaled, weight) for weight in (gate_weight, up_weight)]
         ]
         sent = jnp.stack([side(term, 1 - core) for term in terms])
         kept = jnp.stack([side(term, core) for term in terms])
@@ -316,7 +327,9 @@
     attended_b = attend(mine_b, last_b, 1 - first_half)
     sums_q = (wide(kept_q) + wide(swap(sent_q, "tp", 1))).astype(jnp.bfloat16)
     across_q = swap(sums_q, "tp", 2)
-    pair_b = jnp.concatenate([attended_b, swap(attended_b, "ctx", 2)], axis=0)
+    down_weight = load(after(down_weight, attended_b), 24)
+    twin_b = after(swap(attended_b, "ctx", 2), down_weight)
+    pair_b = jnp.concatenate([attended_b, twin_b], axis=0)
     all_b = jnp.concatenate([pair_b, swap(pair_b, "ctx", 1)], axis=0)
     all_b, across_q = lax.optimization_barrier((all_b, across_q))
     kept, sent, squares_b = gate_up(all_b)
@@ -335,7 +348,7 @@
     hidden_far = swap(hidden, "tp", 2)
 
     def down_hop(mine, other):
-        blocks = matmuls(jnp.concatenate([mine, other], axis=0), [down_weight])[0]
+        blocks = matmul(jnp.concatenate([mine, other], axis=0), down_weight)
         blocks = blocks.reshape(2, 2, half, width)
         return blocks[:, 0], swap(blocks[:, 1], "ctx", 1)
 

time: 256 us -> 255 us (level)
  Pallas kernels: 68.3 us -> 14.1 us
  matrix products: 0 us -> 32 us
  local copies, waits for them, and re-layouts: 7.26 us -> 24.8 us
  waiting for transfers between devices: 124 us -> 135 us
  starting transfers between devices: 42.5 us -> 36.7 us
    pallas_call x7 -> x3, Pallas kernels: 61.7 us -> 7.45 us  [load(): pl.pallas_call(functools.partial(load_kernel, chunks), in_specs=[pl.Block...]
    dot_general x0 -> x10, matrix products: none -> 32 us  [matmul(): jnp.dot(a, b, preferred_element_type=jnp.float32).astype(jnp.bfloat16)]
    ppermute x26, waiting for transfers between devices: 105 us -> 127 us  [swap(): return lax.ppermute(value, axis_name, [(i, i ^ bit) for i in range(width)])]
    unnamed x37 -> x83, local copies, waits for them, and re-layouts: 1.87 us -> 15.9 us
    ppermute x4, waiting for transfers between devices: 17.8 us -> 6.54 us  [spread_heads(): lax.ppermute(pieces[s], ('ctx', 'tp'), [(c * n_tp + t, t * n_tp + (c ^ s)...]
    ppermute x26, starting transfers between devices: 25.7 us -> 17.4 us  [swap(): return lax.ppermute(value, axis_name, [(i, i ^ bit) for i in range(width)])]
    dynamic_slice x4 -> x6, local copies, waits for them, and re-layouts: 0.21 us -> 3.51 us  [side(): return lax.dynamic_index_in_dim(value, which, 1, keepdims=False)]
  transfers between devices with their start and end apart: 33 -> 33, of which waited for: 19 -> 20; matrix products, arithmetic and copies ran while one was open for 3% -> 10% of each run, Pallas kernels for 19% -> 3%
where the time goes in v7:
time: 255 us
  waiting for transfers between devices  135 us (53%)
  starting transfers between devices  36.7 us (14%)
  matrix products  32 us (13%)
  local copies, waits for them, and re-layouts  24.8 us (10%)
  Pallas kernels  14.1 us (6%)
  other arithmetic  10.8 us (4%)
    ppermute x26, waiting for transfers between devices, swap(): return lax.ppermute(value, axis_name, [(i, i ^ bit) for i in range(width)])  127 us
    dot_general x10, matrix products, matmul(): jnp.dot(a, b, preferred_element_type=jnp.float32).astype(jnp.bfloat16)  32 us
    ppermute x26, starting transfers between devices, swap(): return lax.ppermute(value, axis_name, [(i, i ^ bit) for i in range(width)])  17.4 us
    unnamed x83, local copies, waits for them, and re-layouts  15.9 us
    ppermute x3, starting transfers between devices, gather_keys(): lax.ppermute(half, 'ctx', [(c, c + d) for c in range(n_ctx - d)])  10.7 us
    ppermute x4, starting transfers between devices, spread_heads(): lax.ppermute(pieces[s], ('ctx', 'tp'), [(c * n_tp + t, t * n_tp + (c ^ s)...  8.6 us
    pallas_call x3, Pallas kernels, load(): pl.pallas_call(functools.partial(load_kernel, chunks), in_specs=[pl.Block...  7.45 us
    pallas_call x1, Pallas kernels, attention(): pl.pallas_call(functools.partial(attention_kernel, group), grid=(local_he...  6.62 us
  transfers between devices with their start and end apart: 33, of which 20 were waited for; matrix products, arithmetic and copies ran while one was open for 10% of the time, Pallas kernels for 3%

profile of v7, /device:TPU:0, one launch (start us, length us, event | category | flops | bytes accessed | tf_op | source)
XLA Modules:
  0.0 254.6 jit_solution(9530937603868043788)
XLA Ops:
  0.6 0.9 convert_element_type.259
  1.6 1.1 slice.104
  2.7 0.8 reduce-window.8
  4.8 7.0 %collective-permute-start = (bf16[288,128]{1,0:T(8,128)(2,1)S(1)}, bf16[288,128]{1,0:T(8,128)(2,1)S(1)}, u32[]{:S(2)}, u32[]{:S(2)}) collective-permute-start(bf16[288,128]{1,0:T(8,128)(2,1)S(1)} %fusion.41), channel_id=1, source_target_pairs={{0,12},{1,13},{2,14},{3,15},{16,28},{17,29},{18,30},{19,31}} | collective-permute-start | bytes 221192 | tf_op jit(solution)/shard_map/ppermute | solution.py:233
  11.8 1.3 collective-permute-start.1
  13.1 2.5 collective-permute-start.2
  16.3 1.2 collective-permute-done.2
  17.7 1.4 collective-permute-done.3
  19.2 6.6 %shard_map.113 = bf16[128,2048]{1,0:T(8,128)(2,1)S(1)} custom-call(f32[4,128,128]{2,1,0:T(8,128)S(1)} %pad_maximum_fusion.11.tables, s32[128,1]{1,0:T(8,128)S(1)} %copy.17.starts, s32[128,1]{1,0:T(8,128)S(1)} %iota_add_fusion.own_index, s32[1,512]{1,0:T(1,128)S(1)} %iota_add_fusion.1.key_index, bf16[576,512]{1,0:T(8,128)(2,1)S(1)} %maximum_maximum_fusion.keys, ...), custom_call_target="tpu_custom_call" | custom-call | flops 2684354560 | bytes 5046272 | tf_op jit(solution)/shard_map/pallas_call | solution.py:143
  26.7 3.9 %collective-permute-start.5 = (bf16[32,2048]{1,0:T(8,128)(2,1)S(1)}, bf16[32,2048]{1,0:T(8,128)(2,1)S(1)}, u32[]{:S(2)}, u32[]{:S(2)}) collective-permute-start(bf16[32,2048]{1,0:T(8,128)(2,1)S(1)} %get-tuple-element.75), channel_id=1, source_target_pairs={{0,1},{1,5},{2,9},{3,13},{4,0},{5,4},{6,8},{7,12},{8,3},{9,7},{10,... | collective-permute-start | bytes 393224 | tf_op jit(solution)/shard_map/ppermute | solution.py:247
  30.7 3.5 %collective-permute-start.6 = (bf16[32,2048]{1,0:T(8,128)(2,1)S(1)}, bf16[32,2048]{1,0:T(8,128)(2,1)S(1)}, u32[]{:S(2)}, u32[]{:S(2)}) collective-permute-start(bf16[32,2048]{1,0:T(8,128)(2,1)S(1)} %get-tuple-element.74), channel_id=1, source_target_pairs={{0,2},{1,6},{2,10},{3,14},{4,3},{5,7},{6,11},{7,15},{8,0},{9,4},{1... | collective-permute-start | bytes 393224 | tf_op jit(solution)/shard_map/ppermute | solution.py:247
  34.5 3.9 %shard_map.114 = bf16[1792,2560]{1,0:T(8,128)(2,1)S(1)} custom-call(bf16[1792,2560]{1,0:T(8,128)(2,1)} %weight), custom_call_target="tpu_custom_call" | custom-call | bytes 1024 | tf_op jit(solution)/shard_map/pallas_call | solution.py:213
  38.5 3.6 %copy-done.1 = bf16[1792,2560]{1,0:T(8,128)(2,1)} copy-done((bf16[1792,2560]{1,0:T(8,128)(2,1)}, bf16[1792,2560]{1,0:T(8,128)(2,1)S(1)}, u32[]{:S(2)}) %copy-start.1) | copy-done | bytes 9175064
  42.1 1.7 shard_map.115
  43.7 3.6 %copy-done = bf16[1792,2560]{1,0:T(8,128)(2,1)} copy-done((bf16[1792,2560]{1,0:T(8,128)(2,1)}, bf16[1792,2560]{1,0:T(8,128)(2,1)S(1)}, u32[]{:S(2)}) %copy-start) | copy-done | bytes 9175064
  47.3 6.5 %collective-permute-done.6 = bf16[32,2048]{1,0:T(8,128)(2,1)S(1)} collective-permute-done((bf16[32,2048]{1,0:T(8,128)(2,1)S(1)}, bf16[32,2048]{1,0:T(8,128)(2,1)S(1)}, u32[]{:S(2)}, u32[]{:S(2)}) %collective-permute-start.6) | collective-permute-done | bytes 131104 | tf_op jit(solution)/shard_map/ppermute | solution.py:247
  53.9 2.7 %collective-permute-start.8 = (bf16[4,32,2048]{2,1,0:T(8,128)(2,1)S(1)}, bf16[4,32,2048]{2,1,0:T(8,128)(2,1)S(1)}, u32[]{:S(2)}, u32[]{:S(2)}) collective-permute-start(bf16[4,32,2048]{2,1,0:T(8,128)(2,1)S(1)} %pad_maximum_fusion.4), channel_id=1, source_target_pairs={{0,1},{1,0},{2,3},{3,2},{4,5},{5,4},{6,7},{7,6},{8,9},{9,8},{10,11... | collective-permute-start | bytes 1572872 | tf_op jit(solution)/shard_map/ppermute | solution.py:182
  56.6 1.5 collective-permute-done.8
  58.3 5.2 %convolution_convert_fusion.7 = bf16[256,1792]{1,0:T(8,128)(2,1)S(1)} fusion(bf16[256,2048]{1,0:T(8,128)(2,1)S(1)} %constant_dynamic-update-slice_fusion.3, bf16[2048,1792]{1,0:T(8,128)(2,1)} %param.15), kind=kOutput, calls=%fused_computation.7 | convolution fusion | flops 1879506944 | bytes 9306112 | tf_op jit(solution)/shard_map/dot_general | solution.py:194
  63.6 0.9 collective-permute-start.9
  64.5 11.9 %collective-permute-done.9 = bf16[2,64,1792]{2,1,0:T(8,128)(2,1)S(1)} collective-permute-done((bf16[2,64,1792]{2,1,0:T(8,128)(2,1)S(1)}, bf16[2,64,1792]{2,1,0:T(8,128)(2,1)S(1)}, u32[]{:S(2)}, u32[]{:S(2)}) %collective-permute-start.9) | collective-permute-done | bytes 458784 | tf_op jit(solution)/shard_map/ppermute | solution.py:182
  76.7 1.7 collective-permute-done.11
  78.4 11.0 %collective-permute-done.10 = bf16[64,1792]{1,0:T(8,128)(2,1)S(1)} collective-permute-done((bf16[64,1792]{1,0:T(8,128)(2,1)S(1)}, bf16[64,1792]{1,0:T(8,128)(2,1)S(1)}, u32[]{:S(2)}, u32[]{:S(2)}) %collective-permute-start.10) | collective-permute-done | bytes 229408 | tf_op jit(solution)/shard_map/ppermute | solution.py:182
  89.8 5.3 %convolution_convert_fusion.6 = bf16[256,1792]{1,0:T(8,128)(2,1)S(1)} fusion(bf16[256,2048]{1,0:T(8,128)(2,1)S(1)} %bitcast_dynamic-update-slice_fusion, bf16[2048,1792]{1,0:T(8,128)(2,1)} %param.15), kind=kOutput, calls=%fused_computation.6 | convolution fusion | flops 1879506944 | bytes 9306112 | tf_op jit(solution)/shard_map/dot_general | solution.py:194
  95.3 5.0 %collective-permute-done.14 = bf16[64,1792]{1,0:T(8,128)(2,1)S(1)} collective-permute-done((bf16[64,1792]{1,0:T(8,128)(2,1)S(1)}, bf16[64,1792]{1,0:T(8,128)(2,1)S(1)}, u32[]{:S(2)}, u32[]{:S(2)}) %collective-permute-start.14) | collective-permute-done | bytes 229408 | tf_op jit(solution)/shard_map/ppermute | solution.py:182
  100.3 1.4 convolution_convert_fusion.5
  101.8 1.4 convolution_convert_fusion.4
  103.6 2.1 collective-permute-start.18
  105.7 11.0 %collective-permute-done.13 = bf16[2,64,1792]{2,1,0:T(8,128)(2,1)S(1)} collective-permute-done((bf16[2,64,1792]{2,1,0:T(8,128)(2,1)S(1)}, bf16[2,64,1792]{2,1,0:T(8,128)(2,1)S(1)}, u32[]{:S(2)}, u32[]{:S(2)}) %collective-permute-start.13) | collective-permute-done | bytes 458784 | tf_op jit(solution)/shard_map/ppermute | solution.py:182
  116.7 1.3 collective-permute-start.17
  118.2 12.2 %collective-permute-done.18 = bf16[128,1792]{1,0:T(8,128)(2,1)S(1)} collective-permute-done((bf16[128,1792]{1,0:T(8,128)(2,1)S(1)}, bf16[128,1792]{1,0:T(8,128)(2,1)S(1)}, u32[]{:S(2)}, u32[]{:S(2)}) %collective-permute-start.18) | collective-permute-done | bytes 458784 | tf_op jit(solution)/shard_map/ppermute | solution.py:182
  130.4 1.4 convolution_convert_fusion.3
  131.8 1.4 convolution_convert_fusion.2
  133.3 1.0 collective-permute-start.16
  134.5 14.7 %collective-permute-done.16 = bf16[2,1,64,2560]{3,2,1,0:T(8,128)(2,1)S(1)} collective-permute-done((bf16[2,1,64,2560]{3,2,1,0:T(8,128)(2,1)S(1)}, bf16[2,1,64,2560]{3,2,1,0:T(8,128)(2,1)S(1)}, u32[]{:S(2)}, u32[]{:S(2)}) %collective-permute-start.16) | collective-permute-done | bytes 655392 | tf_op jit(solution)/shard_map/ppermute | solution.py:182
  150.5 3.6 %copy-done.2 = bf16[2560,1792]{1,0:T(8,128)(2,1)S(1)} copy-done((bf16[2560,1792]{1,0:T(8,128)(2,1)S(1)}, bf16[2560,1792]{1,0:T(8,128)(2,1)}, u32[]{:S(2)}) %copy-start.2) | copy-done | bytes 9175064
  154.1 1.9 shard_map.116
  156.0 3.7 %copy-done.3 = bf16[2560,1792]{1,0:T(8,128)(2,1)} copy-done((bf16[2560,1792]{1,0:T(8,128)(2,1)}, bf16[2560,1792]{1,0:T(8,128)(2,1)S(1)}, u32[]{:S(2)}) %copy-start.3) | copy-done | bytes 9175064
  159.7 2.4 collective-permute-done.19
  162.3 1.2 add_convert_fusion
  163.5 1.2 collective-permute-start.22
  164.8 9.9 %collective-permute-done.20 = bf16[128,1792]{1,0:T(8,128)(2,1)S(1)} collective-permute-done((bf16[128,1792]{1,0:T(8,128)(2,1)S(1)}, bf16[128,1792]{1,0:T(8,128)(2,1)S(1)}, u32[]{:S(2)}, u32[]{:S(2)}) %collective-permute-start.20) | collective-permute-done | bytes 458784 | tf_op jit(solution)/shard_map/ppermute | solution.py:182
  174.8 5.6 %collective-permute-done.22 = bf16[2,1,64,2560]{3,2,1,0:T(8,128)(2,1)} collective-permute-done((bf16[2,1,64,2560]{3,2,1,0:T(8,128)(2,1)S(1)}, bf16[2,1,64,2560]{3,2,1,0:T(8,128)(2,1)}, u32[]{:S(2)}, u32[]{:S(2)}) %collective-permute-start.22) | collective-permute-done | bytes 655392 | tf_op jit(solution)/shard_map/ppermute | solution.py:182
  180.7 3.6 %convolution_convert_fusion.1 = bf16[256,2560]{1,0:T(8,128)(2,1)} fusion(bf16[1792,2560]{1,0:T(8,128)(2,1)S(1)} %bitcast.177, bf16[256,1792]{1,0:T(8,128)(2,1)S(1)} %pad_maximum_fusion.1, f32[1792]{0:T(1024)S(1)} %copy-done.10), kind=kOutput, calls=%fused_computation.1 | convolution fusion | flops 2350841856 | bytes 11410432 | tf_op jit(solution)/shard_map/dot_general | solution.py:194
  184.3 3.6 %convolution_convert_fusion = bf16[256,2560]{1,0:T(8,128)(2,1)} fusion(bf16[1792,2560]{1,0:T(8,128)(2,1)S(1)} %bitcast.173, bf16[256,1792]{1,0:T(8,128)(2,1)S(1)} %pad_maximum_fusion.1, f32[1792]{0:T(1024)S(1)} %copy-done.10), kind=kOutput, calls=%fused_computation | convolution fusion | flops 2350841856 | bytes 11410432 | tf_op jit(solution)/shard_map/dot_general | solution.py:194
  188.1 2.4 constant_dynamic-slice_fusion.3
  190.5 0.9 constant_dynamic-slice_fusion
  191.4 1.2 pad_maximum_fusion
  193.1 1.1 constant_dynamic-update-slice_fusion.7
  194.2 1.2 collective-permute-start.25
  195.5 1.0 fusion.63
  196.4 1.4 collective-permute-done.25
  198.0 1.5 fusion.62
  199.8 1.0 fusion.10
  201.0 1.2 collective-permute-start.26
  202.2 0.8 collective-permute-done.27
  203.1 6.1 %convolution_convert_fusion.9 = bf16[256,1792]{1,0:T(8,128)(2,1)S(1)} fusion(bf16[2560,1792]{1,0:T(8,128)(2,1)} %copy-done.3, bf16[128,2560]{1,0:T(8,128)(2,1)S(1)} %collective-permute-done.27, bf16[128,2560]{1,0:T(8,128)(2,1)S(1)} %fusion.10), kind=kOutput, calls=%fused_computation.9 | convolution fusion | flops 2351890432 | bytes 11403264 | tf_op jit(solution)/shard_map/dot_general | solution.py:194
  209.2 1.8 collective-permute-start.29
  211.0 7.1 %collective-permute-done.26 = bf16[128,2560]{1,0:T(8,128)(2,1)S(1)} collective-permute-done((bf16[128,2560]{1,0:T(8,128)(2,1)S(1)}, bf16[128,2560]{1,0:T(8,128)(2,1)S(1)}, u32[]{:S(2)}, u32[]{:S(2)}) %collective-permute-start.26) | collective-permute-done | bytes 655392 | tf_op jit(solution)/shard_map/ppermute | solution.py:182
  218.1 3.7 %collective-permute-done.29 = bf16[2,64,1792]{2,1,0:T(8,128)(2,1)S(1)} collective-permute-done((bf16[2,64,1792]{2,1,0:T(8,128)(2,1)S(1)}, bf16[2,64,1792]{2,1,0:T(8,128)(2,1)S(1)}, u32[]{:S(2)}, u32[]{:S(2)}) %collective-permute-start.29) | collective-permute-done | bytes 458784 | tf_op jit(solution)/shard_map/ppermute | solution.py:182
  222.1 2.5 convolution_convert_fusion.8
  224.6 1.8 collective-permute-start.30
  227.2 14.1 %collective-permute-done.30 = bf16[2,64,1792]{2,1,0:T(8,128)(2,1)S(1)} collective-permute-done((bf16[2,64,1792]{2,1,0:T(8,128)(2,1)S(1)}, bf16[2,64,1792]{2,1,0:T(8,128)(2,1)S(1)}, u32[]{:S(2)}, u32[]{:S(2)}) %collective-permute-start.30) | collective-permute-done | bytes 458784 | tf_op jit(solution)/shard_map/ppermute | solution.py:182
  241.6 11.2 %collective-permute-done.31 = bf16[64,1792]{1,0:T(8,128)(2,1)S(1)} collective-permute-done((bf16[64,1792]{1,0:T(8,128)(2,1)S(1)}, bf16[64,1792]{1,0:T(8,128)(2,1)S(1)}, u32[]{:S(2)}, u32[]{:S(2)}) %collective-permute-start.31) | collective-permute-done | bytes 229408 | tf_op jit(solution)/shard_map/ppermute | solution.py:182
  (179 shorter events, 11.3 us)
Async XLA Ops:
  1.6 17.6 %copy-start.5 = (bf16[512,2048]{1,0:T(8,128)(2,1)S(1)}, bf16[512,2048]{1,0:T(8,128)(2,1)}, u32[]{:S(2)}) copy-start(bf16[512,2048]{1,0:T(8,128)(2,1)} %value_weight.1) | copy-start | bytes 6291460
  4.8 11.4 %collective-permute-start = (bf16[288,128]{1,0:T(8,128)(2,1)S(1)}, bf16[288,128]{1,0:T(8,128)(2,1)S(1)}, u32[]{:S(2)}, u32[]{:S(2)}) collective-permute-start(bf16[288,128]{1,0:T(8,128)(2,1)S(1)} %fusion.41), channel_id=1, source_target_pairs={{0,12},{1,13},{2,14},{3,15},{16,28},{17,29},{18,30},{19,31}} | collective-permute-start | bytes 221192 | tf_op jit(solution)/shard_map/ppermute | solution.py:233
  11.8 4.5 %collective-permute-start.1 = (bf16[288,128]{1,0:T(8,128)(2,1)S(1)}, bf16[288,128]{1,0:T(8,128)(2,1)S(1)}, u32[]{:S(2)}, u32[]{:S(2)}) collective-permute-start(bf16[288,128]{1,0:T(8,128)(2,1)S(1)} %fusion.41), channel_id=1, source_target_pairs={{0,8},{4,12},{1,9},{5,13},{2,10},{6,14},{3,11},{7,15},{16,24},{20,... | collective-permute-start | bytes 221192 | tf_op jit(solution)/shard_map/ppermute | solution.py:233
  13.1 4.4 %collective-permute-start.2 = (bf16[288,128]{1,0:T(8,128)(2,1)S(1)}, bf16[288,128]{1,0:T(8,128)(2,1)S(1)}, u32[]{:S(2)}, u32[]{:S(2)}) collective-permute-start(bf16[288,128]{1,0:T(8,128)(2,1)S(1)} %fusion.41), channel_id=1, source_target_pairs={{0,4},{4,8},{8,12},{1,5},{5,9},{9,13},{2,6},{6,10},{10,14},{3,7},{... | collective-permute-start | bytes 221192 | tf_op jit(solution)/shard_map/ppermute | solution.py:233
  17.6 1.7 copy-start.4
  17.6 1.5 collective-permute-start.3
  25.9 16.2 %slice-start.12 = ((s8[9175040]{0:T(1024)(128)(4,1)}), s8[4194304]{0:T(1024)(128)(4,1)S(1)}, s32[]{:S(2)}) async-start(s8[9175040]{0:T(1024)(128)(4,1)} %bitcast.178), calls=%async_computation.12 | async-start | bytes 8388608
  25.9 21.4 %collective-permute-start.4 = (bf16[32,2048]{1,0:T(8,128)(2,1)S(1)}, bf16[32,2048]{1,0:T(8,128)(2,1)S(1)}, u32[]{:S(2)}, u32[]{:S(2)}) collective-permute-start(bf16[32,2048]{1,0:T(8,128)(2,1)S(1)} %get-tuple-element.76), channel_id=1, source_target_pairs={{0,0},{1,4},{2,8},{3,12},{4,1},{5,5},{6,9},{7,13},{8,2},{9,6},{10,... | collective-permute-start | bytes 393224 | tf_op jit(solution)/shard_map/ppermute | solution.py:247
  26.7 20.6 %collective-permute-start.5 = (bf16[32,2048]{1,0:T(8,128)(2,1)S(1)}, bf16[32,2048]{1,0:T(8,128)(2,1)S(1)}, u32[]{:S(2)}, u32[]{:S(2)}) collective-permute-start(bf16[32,2048]{1,0:T(8,128)(2,1)S(1)} %get-tuple-element.75), channel_id=1, source_target_pairs={{0,1},{1,5},{2,9},{3,13},{4,0},{5,4},{6,8},{7,12},{8,3},{9,7},{10,... | collective-permute-start | bytes 393224 | tf_op jit(solution)/shard_map/ppermute | solution.py:247
  30.7 23.2 %collective-permute-start.6 = (bf16[32,2048]{1,0:T(8,128)(2,1)S(1)}, bf16[32,2048]{1,0:T(8,128)(2,1)S(1)}, u32[]{:S(2)}, u32[]{:S(2)}) collective-permute-start(bf16[32,2048]{1,0:T(8,128)(2,1)S(1)} %get-tuple-element.74), channel_id=1, source_target_pairs={{0,2},{1,6},{2,10},{3,14},{4,3},{5,7},{6,11},{7,15},{8,0},{9,4},{1... | collective-permute-start | bytes 393224 | tf_op jit(solution)/shard_map/ppermute | solution.py:247
  34.1 7.9 %slice-start.13 = ((s8[9175040]{0:T(1024)(128)(4,1)}), s8[4194304]{0:T(1024)(128)(4,1)S(1)}, s32[]{:S(2)}) async-start(s8[9175040]{0:T(1024)(128)(4,1)} %bitcast.178), calls=%async_computation.13 | async-start | bytes 8388608
  34.1 7.9 %slice-start.14 = ((s8[9175040]{0:T(1024)(128)(4,1)}), s8[786432]{0:T(1024)(128)(4,1)S(1)}, s32[]{:S(2)}) async-start(s8[9175040]{0:T(1024)(128)(4,1)} %bitcast.178), calls=%async_computation.14 | async-start | bytes 1572864
  34.1 19.7 %collective-permute-start.7 = (bf16[32,2048]{1,0:T(8,128)(2,1)S(1)}, bf16[32,2048]{1,0:T(8,128)(2,1)S(1)}, u32[]{:S(2)}, u32[]{:S(2)}) collective-permute-start(bf16[32,2048]{1,0:T(8,128)(2,1)S(1)} %get-tuple-element.73), channel_id=1, source_target_pairs={{0,3},{1,7},{2,11},{3,15},{4,2},{5,6},{6,10},{7,14},{8,1},{9,5},{1... | collective-permute-start | bytes 393224 | tf_op jit(solution)/shard_map/ppermute | solution.py:247
  38.5 3.6 %copy-start.1 = (bf16[1792,2560]{1,0:T(8,128)(2,1)}, bf16[1792,2560]{1,0:T(8,128)(2,1)S(1)}, u32[]{:S(2)}) copy-start(bf16[1792,2560]{1,0:T(8,128)(2,1)S(1)} %shard_map.114) | copy-start | bytes 27525124
  43.7 3.6 %copy-start = (bf16[1792,2560]{1,0:T(8,128)(2,1)}, bf16[1792,2560]{1,0:T(8,128)(2,1)S(1)}, u32[]{:S(2)}) copy-start(bf16[1792,2560]{1,0:T(8,128)(2,1)S(1)} %shard_map.115) | copy-start | bytes 27525124
  53.9 4.2 %collective-permute-start.8 = (bf16[4,32,2048]{2,1,0:T(8,128)(2,1)S(1)}, bf16[4,32,2048]{2,1,0:T(8,128)(2,1)S(1)}, u32[]{:S(2)}, u32[]{:S(2)}) collective-permute-start(bf16[4,32,2048]{2,1,0:T(8,128)(2,1)S(1)} %pad_maximum_fusion.4), channel_id=1, source_target_pairs={{0,1},{1,0},{2,3},{3,2},{4,5},{5,4},{6,7},{7,6},{8,9},{9,8},{10,11... | collective-permute-start | bytes 1572872 | tf_op jit(solution)/shard_map/ppermute | solution.py:182
  63.4 26.0 %copy-start.13 = (bf16[128,1792]{1,0:T(8,128)(2,1)S(1)}, bf16[128,1792]{1,0:T(8,128)(2,1)}, u32[]{:S(2)}) copy-start(bf16[128,1792]{1,0:T(8,128)(2,1)} %param.10) | copy-start | bytes 1376260
  63.6 12.9 %collective-permute-start.9 = (bf16[2,64,1792]{2,1,0:T(8,128)(2,1)S(1)}, bf16[2,64,1792]{2,1,0:T(8,128)(2,1)S(1)}, u32[]{:S(2)}, u32[]{:S(2)}) collective-permute-start(bf16[2,64,1792]{2,1,0:T(8,128)(2,1)S(1)} %pad_maximum_fusion.5), channel_id=1, source_target_pairs={{0,4},{4,0},{8,12},{12,8},{1,5},{5,1},{9,13},{13,9},{2,6},{6,2},{1... | collective-permute-start | bytes 1376264 | tf_op jit(solution)/shard_map/ppermute | solution.py:182
  64.5 13.9 %collective-permute-start.11 = (bf16[4,32,2048]{2,1,0:T(8,128)(2,1)S(1)}, bf16[4,32,2048]{2,1,0:T(8,128)(2,1)S(1)}, u32[]{:S(2)}, u32[]{:S(2)}) collective-permute-start(bf16[4,32,2048]{2,1,0:T(8,128)(2,1)S(1)} %pad_maximum_fusion.4), channel_id=1, source_target_pairs={{0,2},{1,3},{2,0},{3,1},{4,6},{5,7},{6,4},{7,5},{8,10},{9,11},{10,... | collective-permute-start | bytes 1572872 | tf_op jit(solution)/shard_map/ppermute | solution.py:182
  76.5 12.9 %collective-permute-start.10 = (bf16[64,1792]{1,0:T(8,128)(2,1)S(1)}, bf16[64,1792]{1,0:T(8,128)(2,1)S(1)}, u32[]{:S(2)}, u32[]{:S(2)}) collective-permute-start(bf16[64,1792]{1,0:T(8,128)(2,1)S(1)} %fusion.28), channel_id=1, source_target_pairs={{0,8},{4,12},{8,0},{12,4},{1,9},{5,13},{9,1},{13,5},{2,10},{6,14},... | collective-permute-start | bytes 688136 | tf_op jit(solution)/shard_map/ppermute | solution.py:182
  78.4 11.2 %collective-permute-start.12 = (bf16[4,32,2048]{2,1,0:T(8,128)(2,1)S(1)}, bf16[4,32,2048]{2,1,0:T(8,128)(2,1)S(1)}, u32[]{:S(2)}, u32[]{:S(2)}) collective-permute-start(bf16[4,32,2048]{2,1,0:T(8,128)(2,1)S(1)} %collective-permute-done.11), channel_id=1, source_target_pairs={{0,1},{1,0},{2,3},{3,2},{4,5},{5,4},{6,7},{7,6},{8,9},{9,8},{10,11... | collective-permute-start | bytes 1572872 | tf_op jit(solution)/shard_map/ppermute | solution.py:182
  89.6 10.7 %collective-permute-start.14 = (bf16[64,1792]{1,0:T(8,128)(2,1)S(1)}, bf16[64,1792]{1,0:T(8,128)(2,1)S(1)}, u32[]{:S(2)}, u32[]{:S(2)}) collective-permute-start(bf16[64,1792]{1,0:T(8,128)(2,1)S(1)} %fusion.23), channel_id=1, source_target_pairs={{0,8},{4,12},{8,0},{12,4},{1,9},{5,13},{9,1},{13,5},{2,10},{6,14},... | collective-permute-start | bytes 688136 | tf_op jit(solution)/shard_map/ppermute | solution.py:182
  89.7 10.6 %slice-start.6 = ((s8[9175040]{0:T(1024)(128)(4,1)}), s8[4194304]{0:T(1024)(128)(4,1)S(1)}, s32[]{:S(2)}) async-start(s8[9175040]{0:T(1024)(128)(4,1)} %bitcast.174), calls=%async_computation.6 | async-start | bytes 8388608
  89.8 10.5 %slice-start.7 = ((s8[9175040]{0:T(1024)(128)(4,1)}), s8[4194304]{0:T(1024)(128)(4,1)S(1)}, s32[]{:S(2)}) async-start(s8[9175040]{0:T(1024)(128)(4,1)} %bitcast.174), calls=%async_computation.7 | async-start | bytes 8388608
  89.8 10.5 %slice-start.8 = ((s8[9175040]{0:T(1024)(128)(4,1)}), s8[786432]{0:T(1024)(128)(4,1)S(1)}, s32[]{:S(2)}) async-start(s8[9175040]{0:T(1024)(128)(4,1)} %bitcast.174), calls=%async_computation.8 | async-start | bytes 1572864
  95.1 5.2 %copy-start.10 = (f32[1792]{0:T(1024)S(1)}, f32[1792]{0:T(1024)}, u32[]{:S(2)}) copy-start(f32[1792]{0:T(1024)} %param.16) | copy-start | bytes 21508
  95.2 6.6 %slice-start = ((s8[9175040]{0:T(1024)(128)(4,1)}), s8[4194304]{0:T(1024)(128)(4,1)S(1)}, s32[]{:S(2)}) async-start(s8[9175040]{0:T(1024)(128)(4,1)} %bitcast.170), calls=%async_computation | async-start | bytes 8388608
  95.2 6.5 %slice-start.1 = ((s8[9175040]{0:T(1024)(128)(4,1)}), s8[4194304]{0:T(1024)(128)(4,1)S(1)}, s32[]{:S(2)}) async-start(s8[9175040]{0:T(1024)(128)(4,1)} %bitcast.170), calls=%async_computation.1 | async-start | bytes 8388608
  95.2 6.5 %slice-start.2 = ((s8[9175040]{0:T(1024)(128)(4,1)}), s8[786432]{0:T(1024)(128)(4,1)S(1)}, s32[]{:S(2)}) async-start(s8[9175040]{0:T(1024)(128)(4,1)} %bitcast.170), calls=%async_computation.2 | async-start | bytes 1572864
  103.2 13.5 %collective-permute-start.13 = (bf16[2,64,1792]{2,1,0:T(8,128)(2,1)S(1)}, bf16[2,64,1792]{2,1,0:T(8,128)(2,1)S(1)}, u32[]{:S(2)}, u32[]{:S(2)}) collective-permute-start(bf16[2,64,1792]{2,1,0:T(8,128)(2,1)S(1)} %pad_maximum_fusion.6), channel_id=1, source_target_pairs={{0,4},{4,0},{8,12},{12,8},{1,5},{5,1},{9,13},{13,9},{2,6},{6,2},{1... | collective-permute-start | bytes 1376264 | tf_op jit(solution)/shard_map/ppermute | solution.py:182
  103.5 14.6 %collective-permute-start.15 = (bf16[2,1,64,2560]{3,2,1,0:T(8,128)(2,1)S(1)}, bf16[2,1,64,2560]{3,2,1,0:T(8,128)(2,1)S(1)}, u32[]{:S(2)}, u32[]{:S(2)}) collective-permute-start(bf16[2,1,64,2560]{3,2,1,0:T(8,128)(2,1)S(1)} %pad_maximum_fusion.2), channel_id=1, source_target_pairs={{0,1},{1,0},{2,3},{3,2},{4,5},{5,4},{6,7},{7,6},{8,9},{9,8},{10,11... | collective-permute-start | bytes 1966088 | tf_op jit(solution)/shard_map/ppermute | solution.py:182
  103.6 26.8 %collective-permute-start.18 = (bf16[128,1792]{1,0:T(8,128)(2,1)S(1)}, bf16[128,1792]{1,0:T(8,128)(2,1)S(1)}, u32[]{:S(2)}, u32[]{:S(2)}) collective-permute-start(bf16[128,1792]{1,0:T(8,128)(2,1)S(1)} %pad_maximum_fusion.7), channel_id=1, source_target_pairs={{0,4},{4,0},{8,12},{12,8},{1,5},{5,1},{9,13},{13,9},{2,6},{6,2},{1... | collective-permute-start | bytes 1376264 | tf_op jit(solution)/shard_map/ppermute | solution.py:182
  116.7 17.7 %collective-permute-start.17 = (bf16[64,1792]{1,0:T(8,128)(2,1)S(1)}, bf16[64,1792]{1,0:T(8,128)(2,1)S(1)}, u32[]{:S(2)}, u32[]{:S(2)}) collective-permute-start(bf16[64,1792]{1,0:T(8,128)(2,1)S(1)} %fusion.29), channel_id=1, source_target_pairs={{0,8},{4,12},{8,0},{12,4},{1,9},{5,13},{9,1},{13,5},{2,10},{6,14},... | collective-permute-start | bytes 688136 | tf_op jit(solution)/shard_map/ppermute | solution.py:182
  133.3 15.8 %collective-permute-start.16 = (bf16[2,1,64,2560]{3,2,1,0:T(8,128)(2,1)S(1)}, bf16[2,1,64,2560]{3,2,1,0:T(8,128)(2,1)S(1)}, u32[]{:S(2)}, u32[]{:S(2)}) collective-permute-start(bf16[2,1,64,2560]{3,2,1,0:T(8,128)(2,1)S(1)} %add_convert_fusion.1), channel_id=1, source_target_pairs={{0,2},{1,3},{2,0},{3,1},{4,6},{5,7},{6,4},{7,5},{8,10},{9,11},{10,... | collective-permute-start | bytes 1966088 | tf_op jit(solution)/shard_map/ppermute | solution.py:182
  134.3 14.8 %copy-start.14 = (bf16[128,1792]{1,0:T(8,128)(2,1)S(1)}, bf16[128,1792]{1,0:T(8,128)(2,1)}, u32[]{:S(2)}) copy-start(bf16[128,1792]{1,0:T(8,128)(2,1)} %param.10) | copy-start | bytes 1376260
  149.1 13.2 %collective-permute-start.21 = (bf16[2,1,64,2560]{3,2,1,0:T(8,128)(2,1)S(1)}, bf16[2,1,64,2560]{3,2,1,0:T(8,128)(2,1)}, u32[]{:S(2)}, u32[]{:S(2)}) collective-permute-start(bf16[2,1,64,2560]{3,2,1,0:T(8,128)(2,1)S(1)} %pad_maximum_fusion.3), channel_id=1, source_target_pairs={{0,1},{1,0},{2,3},{3,2},{4,5},{5,4},{6,7},{7,6},{8,9},{9,8},{10,11... | collective-permute-start | bytes 1966088 | tf_op jit(solution)/shard_map/ppermute | solution.py:182
  149.1 31.5 %slice-start.9 = ((s8[9175040]{0:T(1024)(128)(4,1)}), s8[786432]{0:T(1024)(128)(4,1)S(1)}, s32[]{:S(2)}) async-start(s8[9175040]{0:T(1024)(128)(4,1)} %bitcast.176), calls=%async_computation.9 | async-start | bytes 1572864
  150.0 12.2 %collective-permute-start.19 = (bf16[64,1792]{1,0:T(8,128)(2,1)S(1)}, bf16[64,1792]{1,0:T(8,128)(2,1)S(1)}, u32[]{:S(2)}, u32[]{:S(2)}) collective-permute-start(bf16[64,1792]{1,0:T(8,128)(2,1)S(1)} %get-tuple-element.52), channel_id=1, source_target_pairs={{0,8},{4,12},{8,0},{12,4},{1,9},{5,13},{9,1},{13,5},{2,10},{6,14},... | collective-permute-start | bytes 688136 | tf_op jit(solution)/shard_map/ppermute | solution.py:182
  150.5 3.6 %copy-start.2 = (bf16[2560,1792]{1,0:T(8,128)(2,1)S(1)}, bf16[2560,1792]{1,0:T(8,128)(2,1)}, u32[]{:S(2)}) copy-start(bf16[2560,1792]{1,0:T(8,128)(2,1)} %weight.2) | copy-start | bytes 27525124
  154.1 26.5 %slice-start.10 = ((s8[9175040]{0:T(1024)(128)(4,1)}), s8[4194304]{0:T(1024)(128)(4,1)S(1)}, s32[]{:S(2)}) async-start(s8[9175040]{0:T(1024)(128)(4,1)} %bitcast.176), calls=%async_computation.10 | async-start | bytes 8388608
  154.1 26.5 %slice-start.11 = ((s8[9175040]{0:T(1024)(128)(4,1)}), s8[4194304]{0:T(1024)(128)(4,1)S(1)}, s32[]{:S(2)}) async-start(s8[9175040]{0:T(1024)(128)(4,1)} %bitcast.176), calls=%async_computation.11 | async-start | bytes 8388608
  156.0 3.7 %copy-start.3 = (bf16[2560,1792]{1,0:T(8,128)(2,1)}, bf16[2560,1792]{1,0:T(8,128)(2,1)S(1)}, u32[]{:S(2)}) copy-start(bf16[2560,1792]{1,0:T(8,128)(2,1)S(1)} %shard_map.116) | copy-start | bytes 27525124
  159.7 5.1 %copy-start.12 = (bf16[2,1,64,2560]{3,2,1,0:T(8,128)(2,1)S(1)}, bf16[2,1,64,2560]{3,2,1,0:T(8,128)(2,1)}, u32[]{:S(2)}) copy-start(bf16[2,1,64,2560]{3,2,1,0:T(8,128)(2,1)} %copy-done.11) | copy-start | bytes 1966084
  162.2 12.5 %collective-permute-start.20 = (bf16[128,1792]{1,0:T(8,128)(2,1)S(1)}, bf16[128,1792]{1,0:T(8,128)(2,1)S(1)}, u32[]{:S(2)}, u32[]{:S(2)}) collective-permute-start(bf16[128,1792]{1,0:T(8,128)(2,1)S(1)} %pad_maximum_fusion.9), channel_id=1, source_target_pairs={{0,4},{4,0},{8,12},{12,8},{1,5},{5,1},{9,13},{13,9},{2,6},{6,2},{1... | collective-permute-start | bytes 1376264 | tf_op jit(solution)/shard_map/ppermute | solution.py:182
  163.5 16.8 %collective-permute-start.22 = (bf16[2,1,64,2560]{3,2,1,0:T(8,128)(2,1)S(1)}, bf16[2,1,64,2560]{3,2,1,0:T(8,128)(2,1)}, u32[]{:S(2)}, u32[]{:S(2)}) collective-permute-start(bf16[2,1,64,2560]{3,2,1,0:T(8,128)(2,1)S(1)} %add_convert_fusion), channel_id=1, source_target_pairs={{0,2},{1,3},{2,0},{3,1},{4,6},{5,7},{6,4},{7,5},{8,10},{9,11},{10,... | collective-permute-start | bytes 1966088 | tf_op jit(solution)/shard_map/ppermute | solution.py:182
  174.7 9.6 %slice-start.3 = ((s8[9175040]{0:T(1024)(128)(4,1)}), s8[4194304]{0:T(1024)(128)(4,1)S(1)}, s32[]{:S(2)}) async-start(s8[9175040]{0:T(1024)(128)(4,1)} %bitcast.172), calls=%async_computation.3 | async-start | bytes 8388608
  180.7 3.6 %slice-start.4 = ((s8[9175040]{0:T(1024)(128)(4,1)}), s8[4194304]{0:T(1024)(128)(4,1)S(1)}, s32[]{:S(2)}) async-start(s8[9175040]{0:T(1024)(128)(4,1)} %bitcast.172), calls=%async_computation.4 | async-start | bytes 8388608
  180.7 3.6 %slice-start.5 = ((s8[9175040]{0:T(1024)(128)(4,1)}), s8[786432]{0:T(1024)(128)(4,1)S(1)}, s32[]{:S(2)}) async-start(s8[9175040]{0:T(1024)(128)(4,1)} %bitcast.172), calls=%async_computation.5 | async-start | bytes 1572864
  188.0 6.2 %collective-permute-start.24 = (f32[2,2,64]{2,1,0:T(2,128)S(1)}, f32[2,2,64]{2,1,0:T(2,128)S(1)}, u32[]{:S(2)}, u32[]{:S(2)}) collective-permute-start(f32[2,2,64]{2,1,0:T(2,128)S(1)} %bitcast.205), channel_id=1, source_target_pairs={{0,1},{1,0},{2,3},{3,2},{4,5},{5,4},{6,7},{7,6},{8,9},{9,8},{10,11... | collective-permute-start | bytes 3080 | tf_op jit(solution)/shard_map/ppermute | solution.py:182
  188.1 2.4 copy-start.9
  192.6 5.4 %collective-permute-start.23 = (bf16[2,2,64,2560]{3,2,1,0:T(8,128)(2,1)}, bf16[2,2,64,2560]{3,2,1,0:T(8,128)(2,1)}, u32[]{:S(2)}, u32[]{:S(2)}) collective-permute-start(bf16[2,2,64,2560]{3,2,1,0:T(8,128)(2,1)} %pad_maximum_fusion), channel_id=1, source_target_pairs={{0,1},{1,0},{2,3},{3,2},{4,5},{5,4},{6,7},{7,6},{8,9},{9,8},{10,11... | collective-permute-start | bytes 3932168 | tf_op jit(solution)/shard_map/ppermute | solution.py:182
  194.2 3.6 %collective-permute-start.25 = (f32[2,64]{1,0:T(2,128)S(1)}, f32[2,64]{1,0:T(2,128)S(1)}, u32[]{:S(2)}, u32[]{:S(2)}) collective-permute-start(f32[2,64]{1,0:T(2,128)S(1)} %slice_bitcast_fusion.12), channel_id=1, source_target_pairs={{0,2},{1,3},{2,0},{3,1},{4,6},{5,7},{6,4},{7,5},{8,10},{9,11},{10,... | collective-permute-start | bytes 1544 | tf_op jit(solution)/shard_map/ppermute | solution.py:182
  198.0 1.7 copy-start.7
  198.0 1.9 copy-start.8
  199.8 22.2 %slice-start.15 = ((s8[9175040]{0:T(1024)(128)(4,1)}), s8[4194304]{0:T(1024)(128)(4,1)S(1)}, s32[]{:S(2)}) async-start(s8[9175040]{0:T(1024)(128)(4,1)} %bitcast.180), calls=%async_computation.15 | async-start | bytes 8388608
  200.9 21.2 %slice-start.16 = ((s8[9175040]{0:T(1024)(128)(4,1)}), s8[4194304]{0:T(1024)(128)(4,1)S(1)}, s32[]{:S(2)}) async-start(s8[9175040]{0:T(1024)(128)(4,1)} %bitcast.180), calls=%async_computation.16 | async-start | bytes 8388608
  200.9 21.1 %slice-start.17 = ((s8[9175040]{0:T(1024)(128)(4,1)}), s8[786432]{0:T(1024)(128)(4,1)S(1)}, s32[]{:S(2)}) async-start(s8[9175040]{0:T(1024)(128)(4,1)} %bitcast.180), calls=%async_computation.17 | async-start | bytes 1572864
  200.9 2.2 collective-permute-start.27
  201.0 17.1 %collective-permute-start.26 = (bf16[128,2560]{1,0:T(8,128)(2,1)S(1)}, bf16[128,2560]{1,0:T(8,128)(2,1)S(1)}, u32[]{:S(2)}, u32[]{:S(2)}) collective-permute-start(bf16[128,2560]{1,0:T(8,128)(2,1)S(1)} %fusion.10), channel_id=1, source_target_pairs={{0,2},{1,3},{2,0},{3,1},{4,6},{5,7},{6,4},{7,5},{8,10},{9,11},{10,... | collective-permute-start | bytes 1966088 | tf_op jit(solution)/shard_map/ppermute | solution.py:182
  209.2 12.6 %collective-permute-start.29 = (bf16[2,64,1792]{2,1,0:T(8,128)(2,1)S(1)}, bf16[2,64,1792]{2,1,0:T(8,128)(2,1)S(1)}, u32[]{:S(2)}, u32[]{:S(2)}) collective-permute-start(bf16[2,64,1792]{2,1,0:T(8,128)(2,1)S(1)} %slice_bitcast_fusion.2), channel_id=1, source_target_pairs={{0,4},{4,0},{8,12},{12,8},{1,5},{5,1},{9,13},{13,9},{2,6},{6,2},{1... | collective-permute-start | bytes 1376264 | tf_op jit(solution)/shard_map/ppermute | solution.py:182
  218.1 3.9 %collective-permute-start.28 = (bf16[128,2560]{1,0:T(8,128)(2,1)S(1)}, bf16[128,2560]{1,0:T(8,128)(2,1)S(1)}, u32[]{:S(2)}, u32[]{:S(2)}) collective-permute-start(bf16[128,2560]{1,0:T(8,128)(2,1)S(1)} %collective-permute-done.26), channel_id=1, source_target_pairs={{0,1},{1,0},{2,3},{3,2},{4,5},{5,4},{6,7},{7,6},{8,9},{9,8},{10,11... | collective-permute-start | bytes 1966088 | tf_op jit(solution)/shard_map/ppermute | solution.py:182
  224.6 16.7 %collective-permute-start.30 = (bf16[2,64,1792]{2,1,0:T(8,128)(2,1)S(1)}, bf16[2,64,1792]{2,1,0:T(8,128)(2,1)S(1)}, u32[]{:S(2)}, u32[]{:S(2)}) collective-permute-start(bf16[2,64,1792]{2,1,0:T(8,128)(2,1)S(1)} %slice_bitcast_fusion), channel_id=1, source_target_pairs={{0,4},{4,0},{8,12},{12,8},{1,5},{5,1},{9,13},{13,9},{2,6},{6,2},{1... | collective-permute-start | bytes 1376264 | tf_op jit(solution)/shard_map/ppermute | solution.py:182
  226.4 15.2 %collective-permute-start.32 = (bf16[64,1792]{1,0:T(8,128)(2,1)S(1)}, bf16[64,1792]{1,0:T(8,128)(2,1)S(1)}, u32[]{:S(2)}, u32[]{:S(2)}) collective-permute-start(bf16[64,1792]{1,0:T(8,128)(2,1)S(1)} %fusion.30), channel_id=1, source_target_pairs={{0,8},{4,12},{8,0},{12,4},{1,9},{5,13},{9,1},{13,5},{2,10},{6,14},... | collective-permute-start | bytes 688136 | tf_op jit(solution)/shard_map/ppermute | solution.py:182
  241.5 11.3 %collective-permute-start.31 = (bf16[64,1792]{1,0:T(8,128)(2,1)S(1)}, bf16[64,1792]{1,0:T(8,128)(2,1)S(1)}, u32[]{:S(2)}, u32[]{:S(2)}) collective-permute-start(bf16[64,1792]{1,0:T(8,128)(2,1)S(1)} %fusion.31), channel_id=1, source_target_pairs={{0,8},{4,12},{8,0},{12,4},{1,9},{5,13},{9,1},{13,5},{2,10},{6,14},... | collective-permute-start | bytes 688136 | tf_op jit(solution)/shard_map/ppermute | solution.py:182
  (2 other events, 2.4 us)

commit v8 on v7

--- a/solution.py
+++ b/solution.py
@@ -290,60 +290,69 @@
     def attend(mine, came, which):
         return (wide(pick(residual_halves, which)) + mine + wide(came)).astype(jnp.bfloat16)
 
-    def side(value, which):
-        return lax.dynamic_index_in_dim(value, which, 1, keepdims=False)
-
     def gate_up(rows):
         values = wide(rows)
-        squares = jnp.sum(values * values, axis=1).reshape(-1, 2, half)
         scaled = (values * norm_gain[None, :]).astype(jnp.bfloat16)
-        terms = [
-            term.reshape(-1, 2, half, term.shape[1])
-            for term in [matmul(scaled, weight) for weight in (gate_weight, up_weight)]
-        ]
-        sent = jnp.stack([side(term, 1 - core) for term in terms])
-        kept = jnp.stack([side(term, core) for term in terms])
-        return kept, sent, squares
+        terms = [matmul(scaled, gate_weight), matmul(scaled, up_weight)]
+
+        def side(which):
+            return jnp.concatenate(
+                [lax.dynamic_slice_in_dim(term, which * half, half, 0) for term in terms], axis=0
+            )
+
+        return side(core), side(1 - core), jnp.sum(values * values, axis=1)
+
+    def chip_sum(kept, sent):
+        return wide(kept) + wide(swap(sent, "tp", 1))
 
     kept_a, sent_a, came_a = first_hop(pair_rows(own_all, near))
     far = swap(after(own_all, sent_a), "tp", 2)
     mine_a, other_a, last_a = second_hop(kept_a, came_a)
     far = after(far, other_a)
     far_near = swap(far, "tp", 1)
-    attended_a = attend(mine_a, last_a, first_half)
-    twin_a = swap(attended_a, "ctx", 2)
     order = [2, 3, 0, 1]
     rows_b = pair_rows([far[i] for i in order], [far_near[i] for i in order])
-    kept_b, sent_b, came_b = first_hop(after(rows_b, attended_a))
-    pair_a = jnp.concatenate([attended_a, after(twin_a, sent_b)], axis=0)
+    kept_b, sent_b, came_b = first_hop(rows_b)
+    attended_a = attend(mine_a, after(last_a, sent_b), first_half)
+    twin_a = swap(attended_a, "ctx", 2)
+    mine_b, other_b, last_b = second_hop(kept_b, after(came_b, attended_a))
+    pair_a = jnp.concatenate([attended_a, after(twin_a, other_b)], axis=0)
     rest_a = swap(pair_a, "ctx", 1)
-    kept_p, sent_p, squares_p = gate_up(pair_a)
-    came_p = swap(sent_p, "tp", 1)
-    mine_b, other_b, last_b = second_hop(kept_b, after(came_b, sent_p))
-    sums_p = (wide(kept_p) + wide(after(came_p, other_b))).astype(jnp.bfloat16)
+    kept, sent, squares_p = gate_up(pair_a)
+    sums_p = chip_sum(kept, sent).astype(jnp.bfloat16)
     across_p = swap(sums_p, "tp", 2)
-    kept_q, sent_q, squares_q = gate_up(after(rest_a, sums_p))
-    across_p, last_b, sent_q = lax.optimization_barrier((across_p, last_b, sent_q))
-    attended_b = attend(mine_b, last_b, 1 - first_half)
-    sums_q = (wide(kept_q) + wide(swap(sent_q, "tp", 1))).astype(jnp.bfloat16)
+    attended_b = attend(mine_b, after(last_b, sums_p), 1 - first_half)
+    twin_b = swap(attended_b, "ctx", 2)
+    rest_a, across_p, _ = lax.optimization_barrier((rest_a, across_p, attended_b))
+    kept, sent, squares_q = gate_up(rest_a)
+    sums_q = chip_sum(kept, sent).astype(jnp.bfloat16)
     across_q = swap(sums_q, "tp", 2)
-    down_weight = load(after(down_weight, attended_b), 24)
-    twin_b = after(swap(attended_b, "ctx", 2), down_weight)
-    pair_b = jnp.concatenate([attended_b, twin_b], axis=0)
-    all_b = jnp.concatenate([pair_b, swap(pair_b, "ctx", 1)], axis=0)
-    all_b, across_q = lax.optimization_barrier((all_b, across_q))
-    kept, sent, squares_b = gate_up(all_b)
-    came = swap(sent, "tp", 1)
-    squares = jnp.stack([jnp.concatenate([squares_p, squares_q], axis=0), squares_b])
-    chip_squares = lax.dynamic_index_in_dim(squares, core, 2, keepdims=False) + swap(
-        lax.dynamic_index_in_dim(squares, 1 - core, 2, keepdims=False), "tp", 1
-    )
-    total_squares = chip_squares[1] + swap(chip_squares[0], "tp", 2)
-    inverse_rms = lax.rsqrt(total_squares / model_width + norm_eps)[:, :, None]
-    across = jnp.concatenate([across_p, across_q], axis=1)
-    gate = (wide(kept[0]) + wide(came[0]) + wide(across[0])) * inverse_rms
-    up = (wide(kept[1]) + wide(came[1]) + wide(across[1])) * inverse_rms
-    hidden = (jax.nn.silu(gate) * up).astype(jnp.bfloat16).reshape(2 * half, -1)
+    squares_a = jnp.concatenate([squares_p, squares_q])
+    across_squares = swap(squares_a + swap(squares_a, "tp", 1), "tp", 2)
+    pair_b = jnp.concatenate([attended_b, after(twin_b, sums_q)], axis=0)
+    rest_b = swap(pair_b, "ctx", 1)
+
+    def hide(chip_terms, squares, across, across_squares):
+        squares = squares + swap(squares, "tp", 1) + across_squares
+        squares = lax.dynamic_slice_in_dim(squares, core * half, half, 0)
+        inverse_rms = lax.rsqrt(squares / model_width + norm_eps)[:, None]
+        gate = (chip_terms[:half] + wide(across[:half])) * inverse_rms
+        up = (chip_terms[half:] + wide(across[half:])) * inverse_rms
+        return (jax.nn.silu(gate) * up).astype(jnp.bfloat16)
+
+    kept, sent, squares_p = gate_up(pair_b)
+    terms_p = chip_sum(kept, sent)
+    down_weight = load(after(down_weight, sums_q), 24)
+    rest_b, across_q, _, _ = lax.optimization_barrier((rest_b, across_q, sent, down_weight))
+    kept, sent, squares_q = gate_up(rest_b)
+    terms_q = chip_sum(kept, sent)
+    hidden = jnp.concatenate(
+        [
+            hide(terms_p, squares_p, across_p, across_squares[: 2 * half]),
+            hide(terms_q, squares_q, across_q, across_squares[2 * half :]),
+        ],
+        axis=0,
+    )
     hidden_near = swap(hidden, "tp", 1)
     hidden_far = swap(hidden, "tp", 2)
 

time: 255 us -> 237 us (0.929)
  waiting for transfers between devices: 135 us -> 120 us
  local copies, waits for them, and re-layouts: 24.8 us -> 12 us
  starting transfers between devices: 36.7 us -> 40.7 us
  matrix products: 32 us -> 34.6 us
    ppermute x26 -> x29, waiting for transfers between devices: 127 us -> 116 us  [swap(): return lax.ppermute(value, axis_name, [(i, i ^ bit) for i in range(width)])]
    ppermute x26 -> x29, starting transfers between devices: 17.4 us -> 24.6 us  [swap(): return lax.ppermute(value, axis_name, [(i, i ^ bit) for i in range(width)])]
    unnamed x83 -> x76, local copies, waits for them, and re-layouts: 15.9 us -> 10.3 us
    ppermute x4, waiting for transfers between devices: 6.54 us -> 2.8 us  [spread_heads(): lax.ppermute(pieces[s], ('ctx', 'tp'), [(c * n_tp + t, t * n_tp + (c ^ s)...]
    dynamic_slice x6 -> x8, local copies, waits for them, and re-layouts: 3.51 us -> 0.41 us  [side(): lax.dynamic_slice_in_dim(term, which * half, half, 0)]
    dot_general x10 -> x12, matrix products: 32 us -> 34.6 us  [matmul(): jnp.dot(a, b, preferred_element_type=jnp.float32).astype(jnp.bfloat16)]
    ppermute x4, starting transfers between devices: 8.6 us -> 6 us  [spread_heads(): lax.ppermute(pieces[s], ('ctx', 'tp'), [(c * n_tp + t, t * n_tp + (c ^ s)...]
  transfers between devices with their start and end apart: 33 -> 36, of which waited for: 20 -> 21; matrix products, arithmetic and copies ran while one was open for 10% -> 9% of each run, Pallas kernels for 3% -> 3%
where the time goes in v8:
time: 237 us; the launch traced here: 236 us
  waiting for transfers between devices  120 us (51%)
  starting transfers between devices  40.7 us (17%)
  matrix products  34.6 us (15%)
  Pallas kernels  14.2 us (6%)
  other arithmetic  13 us (5%)
  local copies, waits for them, and re-layouts  12 us (5%)
    ppermute x29, waiting for transfers between devices, swap(): return lax.ppermute(value, axis_name, [(i, i ^ bit) for i in range(width)])  116 us
    dot_general x12, matrix products, matmul(): jnp.dot(a, b, preferred_element_type=jnp.float32).astype(jnp.bfloat16)  34.6 us
    ppermute x29, starting transfers between devices, swap(): return lax.ppermute(value, axis_name, [(i, i ^ bit) for i in range(width)])  24.6 us
    unnamed x76, local copies, waits for them, and re-layouts  10.3 us
    ppermute x3, starting transfers between devices, gather_keys(): lax.ppermute(half, 'ctx', [(c, c + d) for c in range(n_ctx - d)])  10.1 us
    pallas_call x3, Pallas kernels, load(): pl.pallas_call(functools.partial(load_kernel, chunks), in_specs=[pl.Block...  7.61 us
    pallas_call x1, Pallas kernels, attention(): pl.pallas_call(functools.partial(attention_kernel, group), grid=(local_he...  6.62 us
    ppermute x4, starting transfers between devices, spread_heads(): lax.ppermute(pieces[s], ('ctx', 'tp'), [(c * n_tp + t, t * n_tp + (c ^ s)...  6 us
  transfers between devices with their start and end apart: 36, of which 21 were waited for; matrix products, arithmetic and copies ran while one was open for 9% of the time, Pallas kernels for 3%

profile of v8, /device:TPU:0, one launch (start us, length us, event | category | flops | bytes accessed | tf_op | source)
XLA Modules:
  0.0 236.1 jit_solution(8368851649639244553)
XLA Ops:
  0.6 0.9 slice.116
  1.6 1.1 convert_element_type.239
  2.7 0.8 reduce-window.8
  3.5 0.7 subtract_subtract_fusion
  4.8 5.9 %collective-permute-start.1 = (bf16[288,128]{1,0:T(8,128)(2,1)S(1)}, bf16[288,128]{1,0:T(8,128)(2,1)S(1)}, u32[]{:S(2)}, u32[]{:S(2)}) collective-permute-start(bf16[288,128]{1,0:T(8,128)(2,1)S(1)} %fusion.51), channel_id=1, source_target_pairs={{0,8},{4,12},{1,9},{5,13},{2,10},{6,14},{3,11},{7,15},{16,24},{20,... | collective-permute-start | bytes 221192 | tf_op jit(solution)/shard_map/ppermute | solution.py:233
  10.8 2.3 collective-permute-start
  13.1 1.8 collective-permute-start.2
  15.7 1.2 collective-permute-done.2
  17.1 1.4 collective-permute-done.3
  18.6 6.6 %shard_map.113 = bf16[128,2048]{1,0:T(8,128)(2,1)S(1)} custom-call(f32[4,128,128]{2,1,0:T(8,128)S(1)} %pad_maximum_fusion.12.tables, s32[128,1]{1,0:T(8,128)S(1)} %copy.17.starts, s32[128,1]{1,0:T(8,128)S(1)} %iota_add_fusion.own_index, s32[1,512]{1,0:T(1,128)S(1)} %iota_add_fusion.1.key_index, bf16[576,512]{1,0:T(8,128)(2,1)S(1)} %maximum_maximum_fusion.keys, ...), custom_call_target="tpu_custom_call" | custom-call | flops 2684354560 | bytes 5046272 | tf_op jit(solution)/shard_map/pallas_call | solution.py:143
  25.3 1.3 collective-permute-start.7
  26.6 3.5 %collective-permute-start.6 = (bf16[32,2048]{1,0:T(8,128)(2,1)S(1)}, bf16[32,2048]{1,0:T(8,128)(2,1)S(1)}, u32[]{:S(2)}, u32[]{:S(2)}) collective-permute-start(bf16[32,2048]{1,0:T(8,128)(2,1)S(1)} %get-tuple-element.70), channel_id=1, source_target_pairs={{0,2},{1,6},{2,10},{3,14},{4,3},{5,7},{6,11},{7,15},{8,0},{9,4},{1... | collective-permute-start | bytes 393224 | tf_op jit(solution)/shard_map/ppermute | solution.py:247
  30.5 0.8 collective-permute-start.4
  31.3 4.1 %shard_map.114 = bf16[1792,2560]{1,0:T(8,128)(2,1)S(1)} custom-call(bf16[1792,2560]{1,0:T(8,128)(2,1)} %weight), custom_call_target="tpu_custom_call" | custom-call | bytes 1024 | tf_op jit(solution)/shard_map/pallas_call | solution.py:213
  35.4 3.6 %copy-done = bf16[1792,2560]{1,0:T(8,128)(2,1)} copy-done((bf16[1792,2560]{1,0:T(8,128)(2,1)}, bf16[1792,2560]{1,0:T(8,128)(2,1)S(1)}, u32[]{:S(2)}) %copy-start) | copy-done | bytes 9175064
  39.0 1.8 shard_map.115
  40.9 3.6 %copy-done.1 = bf16[1792,2560]{1,0:T(8,128)(2,1)} copy-done((bf16[1792,2560]{1,0:T(8,128)(2,1)}, bf16[1792,2560]{1,0:T(8,128)(2,1)S(1)}, u32[]{:S(2)}) %copy-start.1) | copy-done | bytes 9175064
  44.4 2.8 %collective-permute-done.6 = bf16[32,2048]{1,0:T(8,128)(2,1)S(1)} collective-permute-done((bf16[32,2048]{1,0:T(8,128)(2,1)S(1)}, bf16[32,2048]{1,0:T(8,128)(2,1)S(1)}, u32[]{:S(2)}, u32[]{:S(2)}) %collective-permute-start.6) | collective-permute-done | bytes 131104 | tf_op jit(solution)/shard_map/ppermute | solution.py:247
  47.4 1.9 collective-permute-done.8
  49.4 5.2 %convolution_convert_fusion.9 = bf16[256,1792]{1,0:T(8,128)(2,1)S(1)} fusion(bf16[256,2048]{1,0:T(8,128)(2,1)S(1)} %constant_dynamic-update-slice_fusion.3, bf16[2048,1792]{1,0:T(8,128)(2,1)} %param.15), kind=kOutput, calls=%fused_computation.9 | convolution fusion | flops 1879506944 | bytes 9306112 | tf_op jit(solution)/shard_map/dot_general | solution.py:194
  54.7 0.6 collective-permute-start.9
  55.3 6.5 %collective-permute-start.11 = (bf16[4,32,2048]{2,1,0:T(8,128)(2,1)S(1)}, bf16[4,32,2048]{2,1,0:T(8,128)(2,1)S(1)}, u32[]{:S(2)}, u32[]{:S(2)}) collective-permute-start(bf16[4,32,2048]{2,1,0:T(8,128)(2,1)S(1)} %pad_maximum_fusion.5), channel_id=1, source_target_pairs={{0,2},{1,3},{2,0},{3,1},{4,6},{5,7},{6,4},{7,5},{8,10},{9,11},{10,... | collective-permute-start | bytes 1572872 | tf_op jit(solution)/shard_map/ppermute | solution.py:182
  61.9 5.5 %collective-permute-done.9 = bf16[2,64,1792]{2,1,0:T(8,128)(2,1)S(1)} collective-permute-done((bf16[2,64,1792]{2,1,0:T(8,128)(2,1)S(1)}, bf16[2,64,1792]{2,1,0:T(8,128)(2,1)S(1)}, u32[]{:S(2)}, u32[]{:S(2)}) %collective-permute-start.9) | collective-permute-done | bytes 458784 | tf_op jit(solution)/shard_map/ppermute | solution.py:182
  67.4 6.6 %collective-permute-done.11 = bf16[4,32,2048]{2,1,0:T(8,128)(2,1)S(1)} collective-permute-done((bf16[4,32,2048]{2,1,0:T(8,128)(2,1)S(1)}, bf16[4,32,2048]{2,1,0:T(8,128)(2,1)S(1)}, u32[]{:S(2)}, u32[]{:S(2)}) %collective-permute-start.11) | collective-permute-done | bytes 524320 | tf_op jit(solution)/shard_map/ppermute | solution.py:182
  74.0 4.2 %collective-permute-start.10 = (bf16[64,1792]{1,0:T(8,128)(2,1)S(1)}, bf16[64,1792]{1,0:T(8,128)(2,1)S(1)}, u32[]{:S(2)}, u32[]{:S(2)}) collective-permute-start(bf16[64,1792]{1,0:T(8,128)(2,1)S(1)} %fusion.38), channel_id=1, source_target_pairs={{0,8},{4,12},{8,0},{12,4},{1,9},{5,13},{9,1},{13,5},{2,10},{6,14},... | collective-permute-start | bytes 688136 | tf_op jit(solution)/shard_map/ppermute | solution.py:182
  78.4 5.3 %convolution_convert_fusion.8 = bf16[256,1792]{1,0:T(8,128)(2,1)S(1)} fusion(bf16[256,2048]{1,0:T(8,128)(2,1)S(1)} %bitcast_dynamic-update-slice_fusion, bf16[2048,1792]{1,0:T(8,128)(2,1)} %param.15), kind=kOutput, calls=%fused_computation.8 | convolution fusion | flops 1879506944 | bytes 9306112 | tf_op jit(solution)/shard_map/dot_general | solution.py:194
  84.3 5.0 %collective-permute-done.10 = bf16[64,1792]{1,0:T(8,128)(2,1)S(1)} collective-permute-done((bf16[64,1792]{1,0:T(8,128)(2,1)S(1)}, bf16[64,1792]{1,0:T(8,128)(2,1)S(1)}, u32[]{:S(2)}, u32[]{:S(2)}) %collective-permute-start.10) | collective-permute-done | bytes 229408 | tf_op jit(solution)/shard_map/ppermute | solution.py:182
  89.6 14.4 %collective-permute-done.13 = bf16[2,64,1792]{2,1,0:T(8,128)(2,1)S(1)} collective-permute-done((bf16[2,64,1792]{2,1,0:T(8,128)(2,1)S(1)}, bf16[2,64,1792]{2,1,0:T(8,128)(2,1)S(1)}, u32[]{:S(2)}, u32[]{:S(2)}) %collective-permute-start.13) | collective-permute-done | bytes 458784 | tf_op jit(solution)/shard_map/ppermute | solution.py:182
  104.1 1.4 convolution_convert_fusion.7
  105.6 0.8 slice-done.6
  106.3 1.3 slice-done.7
  107.7 1.4 convolution_convert_fusion.6
  109.4 0.8 collective-permute-start.14
  110.2 1.4 collective-permute-done.16
  111.6 1.4 add_convert_fusion.1
  113.6 1.0 collective-permute-start.18
  114.5 8.8 %collective-permute-done.14 = bf16[64,1792]{1,0:T(8,128)(2,1)S(1)} collective-permute-done((bf16[64,1792]{1,0:T(8,128)(2,1)S(1)}, bf16[64,1792]{1,0:T(8,128)(2,1)S(1)}, u32[]{:S(2)}, u32[]{:S(2)}) %collective-permute-start.14) | collective-permute-done | bytes 229408 | tf_op jit(solution)/shard_map/ppermute | solution.py:182
  123.5 7.2 %collective-permute-done.18 = bf16[128,1792]{1,0:T(8,128)(2,1)S(1)} collective-permute-done((bf16[128,1792]{1,0:T(8,128)(2,1)S(1)}, bf16[128,1792]{1,0:T(8,128)(2,1)S(1)}, u32[]{:S(2)}, u32[]{:S(2)}) %collective-permute-start.18) | collective-permute-done | bytes 458784 | tf_op jit(solution)/shard_map/ppermute | solution.py:182
  130.7 5.1 %convolution_convert_fusion.4 = bf16[128,2560]{1,0:T(8,128)(2,1)S(1)} fusion(bf16[1792,2560]{1,0:T(8,128)(2,1)} %copy-done.1, bf16[128,1792]{1,0:T(8,128)(2,1)S(1)} %collective-permute-done.18, f32[1792]{0:T(1024)S(1)} %copy-done.5), kind=kOutput, calls=%fused_computation.4 | convolution fusion | flops 1175420928 | bytes 10296320 | tf_op jit(solution)/shard_map/dot_general | solution.py:194
  135.9 1.4 convolution_convert_fusion.5
  139.1 0.6 collective-permute-done.23
  139.7 1.6 collective-permute-start.24
  141.2 1.0 add_convert_fusion
  142.3 9.4 %collective-permute-done.17 = bf16[64,1792]{1,0:T(8,128)(2,1)S(1)} collective-permute-done((bf16[64,1792]{1,0:T(8,128)(2,1)S(1)}, bf16[64,1792]{1,0:T(8,128)(2,1)S(1)}, u32[]{:S(2)}, u32[]{:S(2)}) %collective-permute-start.17) | collective-permute-done | bytes 229408 | tf_op jit(solution)/shard_map/ppermute | solution.py:182
  152.0 1.7 convolution_convert_fusion.3
  154.4 1.4 convolution_convert_fusion.2
  155.8 1.8 collective-permute-start.26
  157.7 0.9 pad_maximum_fusion.2
  159.1 1.7 shard_map.116
  160.8 9.7 %collective-permute-done.25 = bf16[128,1792]{1,0:T(8,128)(2,1)S(1)} collective-permute-done((bf16[128,1792]{1,0:T(8,128)(2,1)S(1)}, bf16[128,1792]{1,0:T(8,128)(2,1)S(1)}, u32[]{:S(2)}, u32[]{:S(2)}) %collective-permute-start.25) | collective-permute-done | bytes 458784 | tf_op jit(solution)/shard_map/ppermute | solution.py:182
  170.5 2.2 collective-permute-done.26
  172.7 1.4 convolution_convert_fusion
  174.1 1.4 convolution_convert_fusion.1
  176.5 1.3 convert_add_fusion.1
  179.2 1.7 collective-permute-start.29
  181.1 2.5 %convolution_convert_fusion.11 = bf16[256,1792]{1,0:T(8,128)(2,1)S(1)} fusion(bf16[2560,1792]{1,0:T(8,128)(2,1)S(1)} %shard_map.116, bf16[128,2560]{1,0:T(8,128)(2,1)S(1)} %collective-permute-done.30, bf16[64,2560]{1,0:T(8,128)(2,1)S(1)} %fusion.18, bf16[64,2560]{1,0:T(8,128)(2,1)S(1)} %fusion.22), kind=kOutput, calls=%fused_computation.11 | convolution fusion | flops 2353201152 | bytes 11403264 | tf_op jit(solution)/shard_map/dot_general | solution.py:194
  183.7 12.5 %collective-permute-done.29 = bf16[128,2560]{1,0:T(8,128)(2,1)} collective-permute-done((bf16[128,2560]{1,0:T(8,128)(2,1)S(1)}, bf16[128,2560]{1,0:T(8,128)(2,1)}, u32[]{:S(2)}, u32[]{:S(2)}) %collective-permute-start.29) | collective-permute-done | bytes 655392 | tf_op jit(solution)/shard_map/ppermute | solution.py:182
  196.5 2.0 collective-permute-done.31
  198.5 6.4 %convolution_convert_fusion.10 = bf16[256,1792]{1,0:T(8,128)(2,1)S(1)} fusion(bf16[2560,1792]{1,0:T(8,128)(2,1)} %copy-done.2, bf16[128,2560]{1,0:T(8,128)(2,1)S(1)} %collective-permute-done.31, bf16[128,2560]{1,0:T(8,128)(2,1)} %collective-permute-done.29), kind=kOutput, calls=%fused_computation.10 | convolution fusion | flops 2351890432 | bytes 11403264 | tf_op jit(solution)/shard_map/dot_general | solution.py:194
  205.0 2.2 collective-permute-start.35
  207.2 15.3 %collective-permute-done.33 = bf16[2,64,1792]{2,1,0:T(8,128)(2,1)S(1)} collective-permute-done((bf16[2,64,1792]{2,1,0:T(8,128)(2,1)S(1)}, bf16[2,64,1792]{2,1,0:T(8,128)(2,1)S(1)}, u32[]{:S(2)}, u32[]{:S(2)}) %collective-permute-start.33) | collective-permute-done | bytes 458784 | tf_op jit(solution)/shard_map/ppermute | solution.py:182
  222.7 11.6 %collective-permute-done.34 = bf16[64,1792]{1,0:T(8,128)(2,1)S(1)} collective-permute-done((bf16[64,1792]{1,0:T(8,128)(2,1)S(1)}, bf16[64,1792]{1,0:T(8,128)(2,1)S(1)}, u32[]{:S(2)}, u32[]{:S(2)}) %collective-permute-start.34) | collective-permute-done | bytes 229408 | tf_op jit(solution)/shard_map/ppermute | solution.py:182
  234.5 0.8 pad_maximum_fusion.11
  235.3 0.8 pad_maximum_fusion.9
  (180 shorter events, 11.1 us)
Async XLA Ops:
  1.6 17.0 %copy-start.4 = (bf16[512,2048]{1,0:T(8,128)(2,1)S(1)}, bf16[512,2048]{1,0:T(8,128)(2,1)}, u32[]{:S(2)}) copy-start(bf16[512,2048]{1,0:T(8,128)(2,1)} %value_weight.1) | copy-start | bytes 6291460
  4.8 10.8 %collective-permute-start.1 = (bf16[288,128]{1,0:T(8,128)(2,1)S(1)}, bf16[288,128]{1,0:T(8,128)(2,1)S(1)}, u32[]{:S(2)}, u32[]{:S(2)}) collective-permute-start(bf16[288,128]{1,0:T(8,128)(2,1)S(1)} %fusion.51), channel_id=1, source_target_pairs={{0,8},{4,12},{1,9},{5,13},{2,10},{6,14},{3,11},{7,15},{16,24},{20,... | collective-permute-start | bytes 221192 | tf_op jit(solution)/shard_map/ppermute | solution.py:233
  10.8 4.9 %collective-permute-start = (bf16[288,128]{1,0:T(8,128)(2,1)S(1)}, bf16[288,128]{1,0:T(8,128)(2,1)S(1)}, u32[]{:S(2)}, u32[]{:S(2)}) collective-permute-start(bf16[288,128]{1,0:T(8,128)(2,1)S(1)} %fusion.51), channel_id=1, source_target_pairs={{0,12},{1,13},{2,14},{3,15},{16,28},{17,29},{18,30},{19,31}} | collective-permute-start | bytes 221192 | tf_op jit(solution)/shard_map/ppermute | solution.py:233
  13.1 3.8 %collective-permute-start.2 = (bf16[288,128]{1,0:T(8,128)(2,1)S(1)}, bf16[288,128]{1,0:T(8,128)(2,1)S(1)}, u32[]{:S(2)}, u32[]{:S(2)}) collective-permute-start(bf16[288,128]{1,0:T(8,128)(2,1)S(1)} %fusion.51), channel_id=1, source_target_pairs={{0,4},{4,8},{8,12},{1,5},{5,9},{9,13},{2,6},{6,10},{10,14},{3,7},{... | collective-permute-start | bytes 221192 | tf_op jit(solution)/shard_map/ppermute | solution.py:233
  16.9 1.5 collective-permute-start.3
  25.2 13.8 %slice-start.12 = ((s8[9175040]{0:T(1024)(128)(4,1)}), s8[4194304]{0:T(1024)(128)(4,1)S(1)}, s32[]{:S(2)}) async-start(s8[9175040]{0:T(1024)(128)(4,1)} %bitcast.136), calls=%async_computation.12 | async-start | bytes 8388608
  25.3 19.1 %collective-permute-start.7 = (bf16[32,2048]{1,0:T(8,128)(2,1)S(1)}, bf16[32,2048]{1,0:T(8,128)(2,1)S(1)}, u32[]{:S(2)}, u32[]{:S(2)}) collective-permute-start(bf16[32,2048]{1,0:T(8,128)(2,1)S(1)} %get-tuple-element.69), channel_id=1, source_target_pairs={{0,3},{1,7},{2,11},{3,15},{4,2},{5,6},{6,10},{7,14},{8,1},{9,5},{1... | collective-permute-start | bytes 393224 | tf_op jit(solution)/shard_map/ppermute | solution.py:247
  26.6 20.6 %collective-permute-start.6 = (bf16[32,2048]{1,0:T(8,128)(2,1)S(1)}, bf16[32,2048]{1,0:T(8,128)(2,1)S(1)}, u32[]{:S(2)}, u32[]{:S(2)}) collective-permute-start(bf16[32,2048]{1,0:T(8,128)(2,1)S(1)} %get-tuple-element.70), channel_id=1, source_target_pairs={{0,2},{1,6},{2,10},{3,14},{4,3},{5,7},{6,11},{7,15},{8,0},{9,4},{1... | collective-permute-start | bytes 393224 | tf_op jit(solution)/shard_map/ppermute | solution.py:247
  30.1 17.1 %collective-permute-start.5 = (bf16[32,2048]{1,0:T(8,128)(2,1)S(1)}, bf16[32,2048]{1,0:T(8,128)(2,1)S(1)}, u32[]{:S(2)}, u32[]{:S(2)}) collective-permute-start(bf16[32,2048]{1,0:T(8,128)(2,1)S(1)} %get-tuple-element.71), channel_id=1, source_target_pairs={{0,1},{1,5},{2,9},{3,13},{4,0},{5,4},{6,8},{7,12},{8,3},{9,7},{10,... | collective-permute-start | bytes 393224 | tf_op jit(solution)/shard_map/ppermute | solution.py:247
  30.5 8.5 %slice-start.13 = ((s8[9175040]{0:T(1024)(128)(4,1)}), s8[4194304]{0:T(1024)(128)(4,1)S(1)}, s32[]{:S(2)}) async-start(s8[9175040]{0:T(1024)(128)(4,1)} %bitcast.136), calls=%async_computation.13 | async-start | bytes 8388608
  30.5 8.5 %slice-start.14 = ((s8[9175040]{0:T(1024)(128)(4,1)}), s8[786432]{0:T(1024)(128)(4,1)S(1)}, s32[]{:S(2)}) async-start(s8[9175040]{0:T(1024)(128)(4,1)} %bitcast.136), calls=%async_computation.14 | async-start | bytes 1572864
  30.5 16.7 %collective-permute-start.4 = (bf16[32,2048]{1,0:T(8,128)(2,1)S(1)}, bf16[32,2048]{1,0:T(8,128)(2,1)S(1)}, u32[]{:S(2)}, u32[]{:S(2)}) collective-permute-start(bf16[32,2048]{1,0:T(8,128)(2,1)S(1)} %get-tuple-element.72), channel_id=1, source_target_pairs={{0,0},{1,4},{2,8},{3,12},{4,1},{5,5},{6,9},{7,13},{8,2},{9,6},{10,... | collective-permute-start | bytes 393224 | tf_op jit(solution)/shard_map/ppermute | solution.py:247
  35.4 3.6 %copy-start = (bf16[1792,2560]{1,0:T(8,128)(2,1)}, bf16[1792,2560]{1,0:T(8,128)(2,1)S(1)}, u32[]{:S(2)}) copy-start(bf16[1792,2560]{1,0:T(8,128)(2,1)S(1)} %shard_map.114) | copy-start | bytes 27525124
  40.9 3.6 %copy-start.1 = (bf16[1792,2560]{1,0:T(8,128)(2,1)}, bf16[1792,2560]{1,0:T(8,128)(2,1)S(1)}, u32[]{:S(2)}) copy-start(bf16[1792,2560]{1,0:T(8,128)(2,1)S(1)} %shard_map.115) | copy-start | bytes 27525124
  47.3 2.0 collective-permute-start.8
  54.7 12.6 %collective-permute-start.9 = (bf16[2,64,1792]{2,1,0:T(8,128)(2,1)S(1)}, bf16[2,64,1792]{2,1,0:T(8,128)(2,1)S(1)}, u32[]{:S(2)}, u32[]{:S(2)}) collective-permute-start(bf16[2,64,1792]{2,1,0:T(8,128)(2,1)S(1)} %pad_maximum_fusion.6), channel_id=1, source_target_pairs={{0,4},{4,0},{8,12},{12,8},{1,5},{5,1},{9,13},{13,9},{2,6},{6,2},{1... | collective-permute-start | bytes 1376264 | tf_op jit(solution)/shard_map/ppermute | solution.py:182
  55.3 18.6 %collective-permute-start.11 = (bf16[4,32,2048]{2,1,0:T(8,128)(2,1)S(1)}, bf16[4,32,2048]{2,1,0:T(8,128)(2,1)S(1)}, u32[]{:S(2)}, u32[]{:S(2)}) collective-permute-start(bf16[4,32,2048]{2,1,0:T(8,128)(2,1)S(1)} %pad_maximum_fusion.5), channel_id=1, source_target_pairs={{0,2},{1,3},{2,0},{3,1},{4,6},{5,7},{6,4},{7,5},{8,10},{9,11},{10,... | collective-permute-start | bytes 1572872 | tf_op jit(solution)/shard_map/ppermute | solution.py:182
  67.3 11.0 %copy-start.10 = (bf16[2,64,1792]{2,1,0:T(8,128)(2,1)}, bf16[2,64,1792]{2,1,0:T(8,128)(2,1)S(1)}, u32[]{:S(2)}) copy-start(bf16[2,64,1792]{2,1,0:T(8,128)(2,1)S(1)} %collective-permute-done.9) | copy-start | bytes 1376260
  74.0 4.2 %collective-permute-start.12 = (bf16[4,32,2048]{2,1,0:T(8,128)(2,1)S(1)}, bf16[4,32,2048]{2,1,0:T(8,128)(2,1)S(1)}, u32[]{:S(2)}, u32[]{:S(2)}) collective-permute-start(bf16[4,32,2048]{2,1,0:T(8,128)(2,1)S(1)} %collective-permute-done.11), channel_id=1, source_target_pairs={{0,1},{1,0},{2,3},{3,2},{4,5},{5,4},{6,7},{7,6},{8,9},{9,8},{10,11... | collective-permute-start | bytes 1572872 | tf_op jit(solution)/shard_map/ppermute | solution.py:182
  74.0 15.4 %collective-permute-start.10 = (bf16[64,1792]{1,0:T(8,128)(2,1)S(1)}, bf16[64,1792]{1,0:T(8,128)(2,1)S(1)}, u32[]{:S(2)}, u32[]{:S(2)}) collective-permute-start(bf16[64,1792]{1,0:T(8,128)(2,1)S(1)} %fusion.38), channel_id=1, source_target_pairs={{0,8},{4,12},{8,0},{12,4},{1,9},{5,13},{9,1},{13,5},{2,10},{6,14},... | collective-permute-start | bytes 688136 | tf_op jit(solution)/shard_map/ppermute | solution.py:182
  78.3 25.8 %slice-start = ((s8[9175040]{0:T(1024)(128)(4,1)}), s8[4194304]{0:T(1024)(128)(4,1)S(1)}, s32[]{:S(2)}) async-start(s8[9175040]{0:T(1024)(128)(4,1)} %bitcast.128), calls=%async_computation | async-start | bytes 8388608
  78.4 25.7 %slice-start.1 = ((s8[9175040]{0:T(1024)(128)(4,1)}), s8[4194304]{0:T(1024)(128)(4,1)S(1)}, s32[]{:S(2)}) async-start(s8[9175040]{0:T(1024)(128)(4,1)} %bitcast.128), calls=%async_computation.1 | async-start | bytes 8388608
  78.4 25.7 %slice-start.2 = ((s8[9175040]{0:T(1024)(128)(4,1)}), s8[786432]{0:T(1024)(128)(4,1)S(1)}, s32[]{:S(2)}) async-start(s8[9175040]{0:T(1024)(128)(4,1)} %bitcast.128), calls=%async_computation.2 | async-start | bytes 1572864
  83.7 5.6 %copy-start.8 = (bf16[128,1792]{1,0:T(8,128)(2,1)S(1)}, bf16[128,1792]{1,0:T(8,128)(2,1)}, u32[]{:S(2)}) copy-start(bf16[128,1792]{1,0:T(8,128)(2,1)} %param.10) | copy-start | bytes 1376260
  83.7 5.6 %copy-start.11 = (bf16[2,64,1792]{2,1,0:T(8,128)(2,1)S(1)}, bf16[2,64,1792]{2,1,0:T(8,128)(2,1)}, u32[]{:S(2)}) copy-start(bf16[2,64,1792]{2,1,0:T(8,128)(2,1)} %copy-done.10) | copy-start | bytes 1376260
  83.8 20.3 %copy-start.5 = (f32[1792]{0:T(1024)S(1)}, f32[1792]{0:T(1024)}, u32[]{:S(2)}) copy-start(f32[1792]{0:T(1024)} %param.16) | copy-start | bytes 21508
  83.8 20.1 %collective-permute-start.13 = (bf16[2,64,1792]{2,1,0:T(8,128)(2,1)S(1)}, bf16[2,64,1792]{2,1,0:T(8,128)(2,1)S(1)}, u32[]{:S(2)}, u32[]{:S(2)}) collective-permute-start(bf16[2,64,1792]{2,1,0:T(8,128)(2,1)S(1)} %pad_maximum_fusion.7), channel_id=1, source_target_pairs={{0,4},{4,0},{8,12},{12,8},{1,5},{5,1},{9,13},{13,9},{2,6},{6,2},{1... | collective-permute-start | bytes 1376264 | tf_op jit(solution)/shard_map/ppermute | solution.py:182
  89.5 14.6 %collective-permute-start.15 = (bf16[64,1792]{1,0:T(8,128)(2,1)S(1)}, bf16[64,1792]{1,0:T(8,128)(2,1)S(1)}, u32[]{:S(2)}, u32[]{:S(2)}) collective-permute-start(bf16[64,1792]{1,0:T(8,128)(2,1)S(1)} %fusion.29), channel_id=1, source_target_pairs={{0,8},{4,12},{8,0},{12,4},{1,9},{5,13},{9,1},{13,5},{2,10},{6,14},... | collective-permute-start | bytes 688136 | tf_op jit(solution)/shard_map/ppermute | solution.py:182
  104.0 2.4 slice-start.6
  104.0 3.6 %slice-start.7 = ((s8[9175040]{0:T(1024)(128)(4,1)}), s8[4194304]{0:T(1024)(128)(4,1)S(1)}, s32[]{:S(2)}) async-start(s8[9175040]{0:T(1024)(128)(4,1)} %bitcast.132), calls=%async_computation.7 | async-start | bytes 8388608
  104.1 3.7 %slice-start.8 = ((s8[9175040]{0:T(1024)(128)(4,1)}), s8[786432]{0:T(1024)(128)(4,1)S(1)}, s32[]{:S(2)}) async-start(s8[9175040]{0:T(1024)(128)(4,1)} %bitcast.132), calls=%async_computation.8 | async-start | bytes 1572864
  109.3 2.3 collective-permute-start.16
  109.4 13.9 %collective-permute-start.14 = (bf16[64,1792]{1,0:T(8,128)(2,1)S(1)}, bf16[64,1792]{1,0:T(8,128)(2,1)S(1)}, u32[]{:S(2)}, u32[]{:S(2)}) collective-permute-start(bf16[64,1792]{1,0:T(8,128)(2,1)S(1)} %fusion.39), channel_id=1, source_target_pairs={{0,8},{4,12},{8,0},{12,4},{1,9},{5,13},{9,1},{13,5},{2,10},{6,14},... | collective-permute-start | bytes 688136 | tf_op jit(solution)/shard_map/ppermute | solution.py:182
  111.6 11.7 %copy-start.7 = (bf16[2,64,1792]{2,1,0:T(8,128)(2,1)S(1)}, bf16[2,64,1792]{2,1,0:T(8,128)(2,1)}, u32[]{:S(2)}) copy-start(bf16[2,64,1792]{2,1,0:T(8,128)(2,1)} %copy-done.6) | copy-start | bytes 1376260
  111.6 11.7 %copy-start.9 = (bf16[128,1792]{1,0:T(8,128)(2,1)S(1)}, bf16[128,1792]{1,0:T(8,128)(2,1)}, u32[]{:S(2)}) copy-start(bf16[128,1792]{1,0:T(8,128)(2,1)} %param.10) | copy-start | bytes 1376260
  113.0 17.7 %collective-permute-start.19 = (bf16[128,2560]{1,0:T(8,128)(2,1)S(1)}, bf16[128,2560]{1,0:T(8,128)(2,1)S(1)}, u32[]{:S(2)}, u32[]{:S(2)}) collective-permute-start(bf16[128,2560]{1,0:T(8,128)(2,1)S(1)} %add_convert_fusion.1), channel_id=1, source_target_pairs={{0,2},{1,3},{2,0},{3,1},{4,6},{5,7},{6,4},{7,5},{8,10},{9,11},{10,... | collective-permute-start | bytes 1966088 | tf_op jit(solution)/shard_map/ppermute | solution.py:182
  113.6 17.2 %collective-permute-start.18 = (bf16[128,1792]{1,0:T(8,128)(2,1)S(1)}, bf16[128,1792]{1,0:T(8,128)(2,1)S(1)}, u32[]{:S(2)}, u32[]{:S(2)}) collective-permute-start(bf16[128,1792]{1,0:T(8,128)(2,1)S(1)} %pad_maximum_fusion.8), channel_id=1, source_target_pairs={{0,4},{4,0},{8,12},{12,8},{1,5},{5,1},{9,13},{13,9},{2,6},{6,2},{1... | collective-permute-start | bytes 1376264 | tf_op jit(solution)/shard_map/ppermute | solution.py:182
  123.3 12.5 %slice-start.3 = ((s8[9175040]{0:T(1024)(128)(4,1)}), s8[4194304]{0:T(1024)(128)(4,1)S(1)}, s32[]{:S(2)}) async-start(s8[9175040]{0:T(1024)(128)(4,1)} %bitcast.130), calls=%async_computation.3 | async-start | bytes 8388608
  130.7 5.2 %slice-start.4 = ((s8[9175040]{0:T(1024)(128)(4,1)}), s8[4194304]{0:T(1024)(128)(4,1)S(1)}, s32[]{:S(2)}) async-start(s8[9175040]{0:T(1024)(128)(4,1)} %bitcast.130), calls=%async_computation.4 | async-start | bytes 8388608
  130.7 5.2 %slice-start.5 = ((s8[9175040]{0:T(1024)(128)(4,1)}), s8[786432]{0:T(1024)(128)(4,1)S(1)}, s32[]{:S(2)}) async-start(s8[9175040]{0:T(1024)(128)(4,1)} %bitcast.130), calls=%async_computation.5 | async-start | bytes 1572864
  137.5 3.8 %collective-permute-start.20 = (bf16[128,2560]{1,0:T(8,128)(2,1)S(1)}, bf16[128,2560]{1,0:T(8,128)(2,1)S(1)}, u32[]{:S(2)}, u32[]{:S(2)}) collective-permute-start(bf16[128,2560]{1,0:T(8,128)(2,1)S(1)} %pad_maximum_fusion.1), channel_id=1, source_target_pairs={{0,1},{1,0},{2,3},{3,2},{4,5},{5,4},{6,7},{7,6},{8,9},{9,8},{10,11... | collective-permute-start | bytes 1966088 | tf_op jit(solution)/shard_map/ppermute | solution.py:182
  137.9 1.7 collective-permute-start.23
  138.5 13.3 %collective-permute-start.17 = (bf16[64,1792]{1,0:T(8,128)(2,1)S(1)}, bf16[64,1792]{1,0:T(8,128)(2,1)S(1)}, u32[]{:S(2)}, u32[]{:S(2)}) collective-permute-start(bf16[64,1792]{1,0:T(8,128)(2,1)S(1)} %get-tuple-element.48), channel_id=1, source_target_pairs={{0,8},{4,12},{8,0},{12,4},{1,9},{5,13},{9,1},{13,5},{2,10},{6,14},... | collective-permute-start | bytes 688136 | tf_op jit(solution)/shard_map/ppermute | solution.py:182
  139.7 38.2 %collective-permute-start.24 = (f32[256]{0:T(256)S(1)}, f32[256]{0:T(256)S(1)}, u32[]{:S(2)}, u32[]{:S(2)}) collective-permute-start(f32[256]{0:T(256)S(1)} %fusion.63), channel_id=1, source_target_pairs={{0,2},{1,3},{2,0},{3,1},{4,6},{5,7},{6,4},{7,5},{8,10},{9,11},{10,... | collective-permute-start | bytes 3080 | tf_op jit(solution)/shard_map/ppermute | solution.py:182
  141.2 12.4 %slice-start.9 = ((s8[9175040]{0:T(1024)(128)(4,1)}), s8[4194304]{0:T(1024)(128)(4,1)S(1)}, s32[]{:S(2)}) async-start(s8[9175040]{0:T(1024)(128)(4,1)} %bitcast.134), calls=%async_computation.9 | async-start | bytes 8388608
  152.0 2.2 slice-start.10
  152.0 2.4 %slice-start.11 = ((s8[9175040]{0:T(1024)(128)(4,1)}), s8[786432]{0:T(1024)(128)(4,1)S(1)}, s32[]{:S(2)}) async-start(s8[9175040]{0:T(1024)(128)(4,1)} %bitcast.134), calls=%async_computation.11 | async-start | bytes 1572864
  152.0 7.1 %slice-start.15 = ((s8[9175040]{0:T(1024)(128)(4,1)}), s8[4194304]{0:T(1024)(128)(4,1)S(1)}, s32[]{:S(2)}) async-start(s8[9175040]{0:T(1024)(128)(4,1)} %bitcast.138), calls=%async_computation.15 | async-start | bytes 8388608
  152.0 7.1 %slice-start.16 = ((s8[9175040]{0:T(1024)(128)(4,1)}), s8[4194304]{0:T(1024)(128)(4,1)S(1)}, s32[]{:S(2)}) async-start(s8[9175040]{0:T(1024)(128)(4,1)} %bitcast.138), calls=%async_computation.16 | async-start | bytes 8388608
  154.3 4.7 %slice-start.17 = ((s8[9175040]{0:T(1024)(128)(4,1)}), s8[786432]{0:T(1024)(128)(4,1)S(1)}, s32[]{:S(2)}) async-start(s8[9175040]{0:T(1024)(128)(4,1)} %bitcast.138), calls=%async_computation.17 | async-start | bytes 1572864
  155.8 16.9 %collective-permute-start.26 = (bf16[128,2560]{1,0:T(8,128)(2,1)}, bf16[128,2560]{1,0:T(8,128)(2,1)S(1)}, u32[]{:S(2)}, u32[]{:S(2)}) collective-permute-start(bf16[128,2560]{1,0:T(8,128)(2,1)} %add_convert_fusion), channel_id=1, source_target_pairs={{0,2},{1,3},{2,0},{3,1},{4,6},{5,7},{6,4},{7,5},{8,10},{9,11},{10,... | collective-permute-start | bytes 1966088 | tf_op jit(solution)/shard_map/ppermute | solution.py:182
  157.6 20.2 %collective-permute-start.22 = (f32[128]{0:T(128)S(1)}, f32[128]{0:T(128)S(1)}, u32[]{:S(2)}, u32[]{:S(2)}) collective-permute-start(f32[128]{0:T(128)S(1)} %fusion.13), channel_id=1, source_target_pairs={{0,1},{1,0},{2,3},{3,2},{4,5},{5,4},{6,7},{7,6},{8,9},{9,8},{10,11... | collective-permute-start | bytes 1544 | tf_op jit(solution)/shard_map/ppermute | solution.py:182
  157.6 12.9 %collective-permute-start.25 = (bf16[128,1792]{1,0:T(8,128)(2,1)S(1)}, bf16[128,1792]{1,0:T(8,128)(2,1)S(1)}, u32[]{:S(2)}, u32[]{:S(2)}) collective-permute-start(bf16[128,1792]{1,0:T(8,128)(2,1)S(1)} %pad_maximum_fusion.10), channel_id=1, source_target_pairs={{0,4},{4,0},{8,12},{12,8},{1,5},{5,1},{9,13},{13,9},{2,6},{6,2},{1... | collective-permute-start | bytes 1376264 | tf_op jit(solution)/shard_map/ppermute | solution.py:182
  158.6 17.9 %collective-permute-start.21 = (bf16[128,2560]{1,0:T(8,128)(2,1)}, bf16[128,2560]{1,0:T(8,128)(2,1)}, u32[]{:S(2)}, u32[]{:S(2)}) collective-permute-start(bf16[128,2560]{1,0:T(8,128)(2,1)} %pad_maximum_fusion.2), channel_id=1, source_target_pairs={{0,1},{1,0},{2,3},{3,2},{4,5},{5,4},{6,7},{7,6},{8,9},{9,8},{10,11... | collective-permute-start | bytes 1966088 | tf_op jit(solution)/shard_map/ppermute | solution.py:182
  160.8 20.3 %copy-start.2 = (bf16[2560,1792]{1,0:T(8,128)(2,1)}, bf16[2560,1792]{1,0:T(8,128)(2,1)S(1)}, u32[]{:S(2)}) copy-start(bf16[2560,1792]{1,0:T(8,128)(2,1)S(1)} %shard_map.116) | copy-start | bytes 27525124
  175.8 2.1 collective-permute-start.28
  176.0 2.4 %collective-permute-start.27 = (bf16[128,2560]{1,0:T(8,128)(2,1)S(1)}, bf16[128,2560]{1,0:T(8,128)(2,1)S(1)}, u32[]{:S(2)}, u32[]{:S(2)}) collective-permute-start(bf16[128,2560]{1,0:T(8,128)(2,1)S(1)} %pad_maximum_fusion.3), channel_id=1, source_target_pairs={{0,1},{1,0},{2,3},{3,2},{4,5},{5,4},{6,7},{7,6},{8,9},{9,8},{10,11... | collective-permute-start | bytes 1966088 | tf_op jit(solution)/shard_map/ppermute | solution.py:182
  178.9 2.2 collective-permute-start.30
  179.2 17.0 %collective-permute-start.29 = (bf16[128,2560]{1,0:T(8,128)(2,1)S(1)}, bf16[128,2560]{1,0:T(8,128)(2,1)}, u32[]{:S(2)}, u32[]{:S(2)}) collective-permute-start(bf16[128,2560]{1,0:T(8,128)(2,1)S(1)} %pad_maximum_fusion.4), channel_id=1, source_target_pairs={{0,2},{1,3},{2,0},{3,1},{4,6},{5,7},{6,4},{7,5},{8,10},{9,11},{10,... | collective-permute-start | bytes 1966088 | tf_op jit(solution)/shard_map/ppermute | solution.py:182
  183.7 12.7 %collective-permute-start.32 = (bf16[2,64,1792]{2,1,0:T(8,128)(2,1)S(1)}, bf16[2,64,1792]{2,1,0:T(8,128)(2,1)S(1)}, u32[]{:S(2)}, u32[]{:S(2)}) collective-permute-start(bf16[2,64,1792]{2,1,0:T(8,128)(2,1)S(1)} %slice_bitcast_fusion.2), channel_id=1, source_target_pairs={{0,4},{4,0},{8,12},{12,8},{1,5},{5,1},{9,13},{13,9},{2,6},{6,2},{1... | collective-permute-start | bytes 1376264 | tf_op jit(solution)/shard_map/ppermute | solution.py:182
  196.2 2.3 collective-permute-start.31
  205.0 17.5 %collective-permute-start.33 = (bf16[2,64,1792]{2,1,0:T(8,128)(2,1)S(1)}, bf16[2,64,1792]{2,1,0:T(8,128)(2,1)S(1)}, u32[]{:S(2)}, u32[]{:S(2)}) collective-permute-start(bf16[2,64,1792]{2,1,0:T(8,128)(2,1)S(1)} %slice_bitcast_fusion), channel_id=1, source_target_pairs={{0,4},{4,0},{8,12},{12,8},{1,5},{5,1},{9,13},{13,9},{2,6},{6,2},{1... | collective-permute-start | bytes 1376264 | tf_op jit(solution)/shard_map/ppermute | solution.py:182
  205.0 17.7 %collective-permute-start.35 = (bf16[64,1792]{1,0:T(8,128)(2,1)S(1)}, bf16[64,1792]{1,0:T(8,128)(2,1)S(1)}, u32[]{:S(2)}, u32[]{:S(2)}) collective-permute-start(bf16[64,1792]{1,0:T(8,128)(2,1)S(1)} %fusion.40), channel_id=1, source_target_pairs={{0,8},{4,12},{8,0},{12,4},{1,9},{5,13},{9,1},{13,5},{2,10},{6,14},... | collective-permute-start | bytes 688136 | tf_op jit(solution)/shard_map/ppermute | solution.py:182
  222.6 11.7 %collective-permute-start.34 = (bf16[64,1792]{1,0:T(8,128)(2,1)S(1)}, bf16[64,1792]{1,0:T(8,128)(2,1)S(1)}, u32[]{:S(2)}, u32[]{:S(2)}) collective-permute-start(bf16[64,1792]{1,0:T(8,128)(2,1)S(1)} %fusion.41), channel_id=1, source_target_pairs={{0,8},{4,12},{8,0},{12,4},{1,9},{5,13},{9,1},{13,5},{2,10},{6,14},... | collective-permute-start | bytes 688136 | tf_op jit(solution)/shard_map/ppermute | solution.py:182
  (2 other events, 3.2 us)

commit v9 on v8

--- a/solution.py
+++ b/solution.py
@@ -310,12 +310,13 @@
     mine_a, other_a, last_a = second_hop(kept_a, came_a)
     far = after(far, other_a)
     far_near = swap(far, "tp", 1)
+    attended_a = attend(mine_a, after(last_a, far), first_half)
+    twin_a = swap(attended_a, "ctx", 2)
+    far_near = after(far_near, attended_a)
     order = [2, 3, 0, 1]
     rows_b = pair_rows([far[i] for i in order], [far_near[i] for i in order])
     kept_b, sent_b, came_b = first_hop(rows_b)
-    attended_a = attend(mine_a, after(last_a, sent_b), first_half)
-    twin_a = swap(attended_a, "ctx", 2)
-    mine_b, other_b, last_b = second_hop(kept_b, after(came_b, attended_a))
+    mine_b, other_b, last_b = second_hop(kept_b, came_b)
     pair_a = jnp.concatenate([attended_a, after(twin_a, other_b)], axis=0)
     rest_a = swap(pair_a, "ctx", 1)
     kept, sent, squares_p = gate_up(pair_a)
@@ -323,13 +324,13 @@
     across_p = swap(sums_p, "tp", 2)
     attended_b = attend(mine_b, after(last_b, sums_p), 1 - first_half)
     twin_b = swap(attended_b, "ctx", 2)
-    rest_a, across_p, _ = lax.optimization_barrier((rest_a, across_p, attended_b))
+    rest_a, across_p, twin_b = lax.optimization_barrier((rest_a, across_p, twin_b))
     kept, sent, squares_q = gate_up(rest_a)
     sums_q = chip_sum(kept, sent).astype(jnp.bfloat16)
     across_q = swap(sums_q, "tp", 2)
     squares_a = jnp.concatenate([squares_p, squares_q])
     across_squares = swap(squares_a + swap(squares_a, "tp", 1), "tp", 2)
-    pair_b = jnp.concatenate([attended_b, after(twin_b, sums_q)], axis=0)
+    pair_b = jnp.concatenate([attended_b, twin_b], axis=0)
     rest_b = swap(pair_b, "ctx", 1)
 
     def hide(chip_terms, squares, across, across_squares):
@@ -340,7 +341,7 @@
         up = (chip_terms[half:] + wide(across[half:])) * inverse_rms
         return (jax.nn.silu(gate) * up).astype(jnp.bfloat16)
 
-    kept, sent, squares_p = gate_up(pair_b)
+    kept, sent, squares_p = gate_up(after(pair_b, sums_q))
     terms_p = chip_sum(kept, sent)
     down_weight = load(after(down_weight, sums_q), 24)
     rest_b, across_q, _, _ = lax.optimization_barrier((rest_b, across_q, sent, down_weight))

time: 237 us -> 242 us (1.021)
  starting transfers between devices: 40.7 us -> 54.2 us
  waiting for transfers between devices: 120 us -> 107 us
  matrix products: 34.6 us -> 38.6 us
  other arithmetic: 13 us -> 16.3 us
  local copies, waits for them, and re-layouts: 12 us -> 9.33 us
    ppermute x29, starting transfers between devices: 24.6 us -> 38.1 us  [swap(): return lax.ppermute(value, axis_name, [(i, i ^ bit) for i in range(width)])]
    ppermute x29, waiting for transfers between devices: 116 us -> 103 us  [swap(): return lax.ppermute(value, axis_name, [(i, i ^ bit) for i in range(width)])]
    dot_general x12, matrix products: 34.6 us -> 38.6 us  [matmul(): jnp.dot(a, b, preferred_element_type=jnp.float32).astype(jnp.bfloat16)]
    unnamed x76 -> x66, local copies, waits for them, and re-layouts: 10.3 us -> 7.58 us
  transfers between devices with their start and end apart: 36 -> 36, of which waited for: 21 -> 19; matrix products, arithmetic and copies ran while one was open for 9% -> 8% of each run, Pallas kernels for 3% -> 3%
where the time goes in v9:
time: 242 us
  waiting for transfers between devices  107 us (44%)
  starting transfers between devices  54.2 us (22%)
  matrix products  38.6 us (16%)
  other arithmetic  16.3 us (7%)
  Pallas kernels  14.2 us (6%)
  local copies, waits for them, and re-layouts  9.33 us (4%)
    ppermute x29, waiting for transfers between devices, swap(): return lax.ppermute(value, axis_name, [(i, i ^ bit) for i in range(width)])  103 us
    dot_general x12, matrix products, matmul(): jnp.dot(a, b, preferred_element_type=jnp.float32).astype(jnp.bfloat16)  38.6 us
    ppermute x29, starting transfers between devices, swap(): return lax.ppermute(value, axis_name, [(i, i ^ bit) for i in range(width)])  38.1 us
    ppermute x3, starting transfers between devices, gather_keys(): lax.ppermute(half, 'ctx', [(c, c + d) for c in range(n_ctx - d)])  10.1 us
    pallas_call x3, Pallas kernels, load(): pl.pallas_call(functools.partial(load_kernel, chunks), in_specs=[pl.Block...  7.61 us
    unnamed x66, local copies, waits for them, and re-layouts  7.58 us
    pallas_call x1, Pallas kernels, attention(): pl.pallas_call(functools.partial(attention_kernel, group), grid=(local_he...  6.62 us
    ppermute x4, starting transfers between devices, spread_heads(): lax.ppermute(pieces[s], ('ctx', 'tp'), [(c * n_tp + t, t * n_tp + (c ^ s)...  6 us
  transfers between devices with their start and end apart: 36, of which 19 were waited for; matrix products, arithmetic and copies ran while one was open for 8% of the time, Pallas kernels for 3%

profile of v9, /device:TPU:0, one launch (start us, length us, event | category | flops | bytes accessed | tf_op | source)
XLA Modules:
  0.0 241.8 jit_solution(18420251836198177948)
XLA Ops:
  0.6 0.9 slice.116
  1.6 1.1 convert_element_type.239
  2.7 0.8 reduce-window.8
  4.8 5.9 %collective-permute-start.1 = (bf16[288,128]{1,0:T(8,128)(2,1)S(1)}, bf16[288,128]{1,0:T(8,128)(2,1)S(1)}, u32[]{:S(2)}, u32[]{:S(2)}) collective-permute-start(bf16[288,128]{1,0:T(8,128)(2,1)S(1)} %fusion.47), channel_id=1, source_target_pairs={{0,8},{4,12},{1,9},{5,13},{2,10},{6,14},{3,11},{7,15},{16,24},{20,... | collective-permute-start | bytes 221192 | tf_op jit(solution)/shard_map/ppermute | solution.py:233
  10.8 2.3 collective-permute-start
  13.1 1.8 collective-permute-start.2
  15.7 1.2 collective-permute-done.2
  17.1 1.4 collective-permute-done.3
  18.6 6.6 %shard_map.113 = bf16[128,2048]{1,0:T(8,128)(2,1)S(1)} custom-call(f32[4,128,128]{2,1,0:T(8,128)S(1)} %pad_maximum_fusion.12.tables, s32[128,1]{1,0:T(8,128)S(1)} %copy.17.starts, s32[128,1]{1,0:T(8,128)S(1)} %iota_add_fusion.own_index, s32[1,512]{1,0:T(1,128)S(1)} %iota_add_fusion.1.key_index, bf16[576,512]{1,0:T(8,128)(2,1)S(1)} %maximum_maximum_fusion.keys, ...), custom_call_target="tpu_custom_call" | custom-call | flops 2684354560 | bytes 5046272 | tf_op jit(solution)/shard_map/pallas_call | solution.py:143
  25.3 1.3 collective-permute-start.7
  26.6 3.5 %collective-permute-start.6 = (bf16[32,2048]{1,0:T(8,128)(2,1)S(1)}, bf16[32,2048]{1,0:T(8,128)(2,1)S(1)}, u32[]{:S(2)}, u32[]{:S(2)}) collective-permute-start(bf16[32,2048]{1,0:T(8,128)(2,1)S(1)} %get-tuple-element.72), channel_id=1, source_target_pairs={{0,2},{1,6},{2,10},{3,14},{4,3},{5,7},{6,11},{7,15},{8,0},{9,4},{1... | collective-permute-start | bytes 393224 | tf_op jit(solution)/shard_map/ppermute | solution.py:247
  30.5 0.8 collective-permute-start.4
  31.3 4.1 %shard_map.114 = bf16[1792,2560]{1,0:T(8,128)(2,1)S(1)} custom-call(bf16[1792,2560]{1,0:T(8,128)(2,1)} %weight), custom_call_target="tpu_custom_call" | custom-call | bytes 1024 | tf_op jit(solution)/shard_map/pallas_call | solution.py:213
  35.4 3.5 %copy-done = bf16[1792,2560]{1,0:T(8,128)(2,1)} copy-done((bf16[1792,2560]{1,0:T(8,128)(2,1)}, bf16[1792,2560]{1,0:T(8,128)(2,1)S(1)}, u32[]{:S(2)}) %copy-start) | copy-done | bytes 9175064
  39.0 1.8 shard_map.115
  40.8 3.6 %copy-done.1 = bf16[1792,2560]{1,0:T(8,128)(2,1)} copy-done((bf16[1792,2560]{1,0:T(8,128)(2,1)}, bf16[1792,2560]{1,0:T(8,128)(2,1)S(1)}, u32[]{:S(2)}) %copy-start.1) | copy-done | bytes 9175064
  44.4 2.8 %collective-permute-done.6 = bf16[32,2048]{1,0:T(8,128)(2,1)S(1)} collective-permute-done((bf16[32,2048]{1,0:T(8,128)(2,1)S(1)}, bf16[32,2048]{1,0:T(8,128)(2,1)S(1)}, u32[]{:S(2)}, u32[]{:S(2)}) %collective-permute-start.6) | collective-permute-done | bytes 131104 | tf_op jit(solution)/shard_map/ppermute | solution.py:247
  47.4 1.9 collective-permute-done.8
  49.4 5.2 %convolution_convert_fusion.9 = bf16[256,1792]{1,0:T(8,128)(2,1)S(1)} fusion(bf16[256,2048]{1,0:T(8,128)(2,1)S(1)} %constant_dynamic-update-slice_fusion.3, bf16[2048,1792]{1,0:T(8,128)(2,1)} %param.15), kind=kOutput, calls=%fused_computation.9 | convolution fusion | flops 1879506944 | bytes 9306112 | tf_op jit(solution)/shard_map/dot_general | solution.py:194
  55.3 6.6 %collective-permute-start.11 = (bf16[4,32,2048]{2,1,0:T(8,128)(2,1)S(1)}, bf16[4,32,2048]{2,1,0:T(8,128)(2,1)S(1)}, u32[]{:S(2)}, u32[]{:S(2)}) collective-permute-start(bf16[4,32,2048]{2,1,0:T(8,128)(2,1)S(1)} %pad_maximum_fusion.5), channel_id=1, source_target_pairs={{0,2},{1,3},{2,0},{3,1},{4,6},{5,7},{6,4},{7,5},{8,10},{9,11},{10,... | collective-permute-start | bytes 1572872 | tf_op jit(solution)/shard_map/ppermute | solution.py:182
  61.9 5.6 %collective-permute-done.9 = bf16[2,64,1792]{2,1,0:T(8,128)(2,1)} collective-permute-done((bf16[2,64,1792]{2,1,0:T(8,128)(2,1)S(1)}, bf16[2,64,1792]{2,1,0:T(8,128)(2,1)}, u32[]{:S(2)}, u32[]{:S(2)}) %collective-permute-start.9) | collective-permute-done | bytes 458784 | tf_op jit(solution)/shard_map/ppermute | solution.py:182
  67.4 1.0 fusion.38
  68.4 8.2 %collective-permute-start.10 = (bf16[64,1792]{1,0:T(8,128)(2,1)S(1)}, bf16[64,1792]{1,0:T(8,128)(2,1)S(1)}, u32[]{:S(2)}, u32[]{:S(2)}) collective-permute-start(bf16[64,1792]{1,0:T(8,128)(2,1)S(1)} %fusion.38), channel_id=1, source_target_pairs={{0,8},{4,12},{8,0},{12,4},{1,9},{5,13},{9,1},{13,5},{2,10},{6,14},... | collective-permute-start | bytes 688136 | tf_op jit(solution)/shard_map/ppermute | solution.py:182
  76.7 10.2 %collective-permute-done.10 = bf16[64,1792]{1,0:T(8,128)(2,1)S(1)} collective-permute-done((bf16[64,1792]{1,0:T(8,128)(2,1)S(1)}, bf16[64,1792]{1,0:T(8,128)(2,1)S(1)}, u32[]{:S(2)}, u32[]{:S(2)}) %collective-permute-start.10) | collective-permute-done | bytes 229408 | tf_op jit(solution)/shard_map/ppermute | solution.py:182
  86.9 1.1 fusion.29
  88.1 5.2 %convolution_convert_fusion.8 = bf16[256,1792]{1,0:T(8,128)(2,1)S(1)} fusion(bf16[256,2048]{1,0:T(8,128)(2,1)S(1)} %bitcast_dynamic-update-slice_fusion, bf16[2048,1792]{1,0:T(8,128)(2,1)} %param.15), kind=kOutput, calls=%fused_computation.8 | convolution fusion | flops 1879506944 | bytes 9306112 | tf_op jit(solution)/shard_map/dot_general | solution.py:194
  93.4 0.8 collective-permute-start.13
  94.1 3.4 %collective-permute-start.15 = (bf16[64,1792]{1,0:T(8,128)(2,1)S(1)}, bf16[64,1792]{1,0:T(8,128)(2,1)S(1)}, u32[]{:S(2)}, u32[]{:S(2)}) collective-permute-start(bf16[64,1792]{1,0:T(8,128)(2,1)S(1)} %fusion.29), channel_id=1, source_target_pairs={{0,8},{4,12},{8,0},{12,4},{1,9},{5,13},{9,1},{13,5},{2,10},{6,14},... | collective-permute-start | bytes 688136 | tf_op jit(solution)/shard_map/ppermute | solution.py:182
  97.5 12.2 %collective-permute-done.13 = bf16[2,64,1792]{2,1,0:T(8,128)(2,1)S(1)} collective-permute-done((bf16[2,64,1792]{2,1,0:T(8,128)(2,1)S(1)}, bf16[2,64,1792]{2,1,0:T(8,128)(2,1)S(1)}, u32[]{:S(2)}, u32[]{:S(2)}) %collective-permute-start.13) | collective-permute-done | bytes 458784 | tf_op jit(solution)/shard_map/ppermute | solution.py:182
  110.5 5.6 %convolution_convert_fusion.7 = bf16[128,2560]{1,0:T(8,128)(2,1)S(1)} fusion(bf16[1792,2560]{1,0:T(8,128)(2,1)} %copy-done, f32[1792]{0:T(1024)S(1)} %copy-done.5, bf16[64,1792]{1,0:T(8,128)(2,1)S(1)} %collective-permute-done.15, bf16[64,1792]{1,0:T(8,128)(2,1)S(1)} %fusion.29), kind=kOutput, calls=%fused_computation.7 | convolution fusion | flops 1176109056 | bytes 10296320 | tf_op jit(solution)/shard_map/dot_general | solution.py:194
  116.3 1.4 convolution_convert_fusion.6
  118.0 2.7 %collective-permute-start.14 = (bf16[64,1792]{1,0:T(8,128)(2,1)}, bf16[64,1792]{1,0:T(8,128)(2,1)S(1)}, u32[]{:S(2)}, u32[]{:S(2)}) collective-permute-start(bf16[64,1792]{1,0:T(8,128)(2,1)} %fusion.39), channel_id=1, source_target_pairs={{0,8},{4,12},{8,0},{12,4},{1,9},{5,13},{9,1},{13,5},{2,10},{6,14},... | collective-permute-start | bytes 688136 | tf_op jit(solution)/shard_map/ppermute | solution.py:182
  120.8 2.5 %collective-permute-start.17 = (bf16[128,1792]{1,0:T(8,128)(2,1)S(1)}, bf16[128,1792]{1,0:T(8,128)(2,1)S(1)}, u32[]{:S(2)}, u32[]{:S(2)}) collective-permute-start(bf16[128,1792]{1,0:T(8,128)(2,1)S(1)} %pad_maximum_fusion.8), channel_id=1, source_target_pairs={{0,4},{4,0},{8,12},{12,8},{1,5},{5,1},{9,13},{13,9},{2,6},{6,2},{1... | collective-permute-start | bytes 1376264 | tf_op jit(solution)/shard_map/ppermute | solution.py:182
  123.6 8.6 %collective-permute-done.14 = bf16[64,1792]{1,0:T(8,128)(2,1)S(1)} collective-permute-done((bf16[64,1792]{1,0:T(8,128)(2,1)}, bf16[64,1792]{1,0:T(8,128)(2,1)S(1)}, u32[]{:S(2)}, u32[]{:S(2)}) %collective-permute-start.14) | collective-permute-done | bytes 229408 | tf_op jit(solution)/shard_map/ppermute | solution.py:182
  132.6 7.9 %collective-permute-done.17 = bf16[128,1792]{1,0:T(8,128)(2,1)S(1)} collective-permute-done((bf16[128,1792]{1,0:T(8,128)(2,1)S(1)}, bf16[128,1792]{1,0:T(8,128)(2,1)S(1)}, u32[]{:S(2)}, u32[]{:S(2)}) %collective-permute-start.17) | collective-permute-done | bytes 458784 | tf_op jit(solution)/shard_map/ppermute | solution.py:182
  140.6 4.8 %collective-permute-done.19 = bf16[64,1792]{1,0:T(8,128)(2,1)S(1)} collective-permute-done((bf16[64,1792]{1,0:T(8,128)(2,1)S(1)}, bf16[64,1792]{1,0:T(8,128)(2,1)S(1)}, u32[]{:S(2)}, u32[]{:S(2)}) %collective-permute-start.19) | collective-permute-done | bytes 229408 | tf_op jit(solution)/shard_map/ppermute | solution.py:182
  145.4 5.1 %convolution_convert_fusion.4 = bf16[128,2560]{1,0:T(8,128)(2,1)S(1)} fusion(bf16[1792,2560]{1,0:T(8,128)(2,1)} %copy-done.1, bf16[128,1792]{1,0:T(8,128)(2,1)S(1)} %collective-permute-done.17, f32[1792]{0:T(1024)S(1)} %copy-done.5), kind=kOutput, calls=%fused_computation.4 | convolution fusion | flops 1175420928 | bytes 10296320 | tf_op jit(solution)/shard_map/dot_general | solution.py:194
  150.6 1.4 convolution_convert_fusion.5
  153.0 1.2 collective-permute-start.25
  154.3 0.8 collective-permute-start.24
  155.1 1.0 add_convert_fusion
  156.4 1.7 convolution_convert_fusion.2
  158.0 1.4 convolution_convert_fusion.3
  159.5 1.3 collective-permute-start.26
  160.9 0.9 pad_maximum_fusion.2
  162.3 1.7 shard_map.116
  164.0 1.5 collective-permute-done.25
  165.5 10.8 %collective-permute-done.26 = bf16[128,2560]{1,0:T(8,128)(2,1)} collective-permute-done((bf16[128,2560]{1,0:T(8,128)(2,1)}, bf16[128,2560]{1,0:T(8,128)(2,1)}, u32[]{:S(2)}, u32[]{:S(2)}) %collective-permute-start.26) | collective-permute-done | bytes 655392 | tf_op jit(solution)/shard_map/ppermute | solution.py:182
  176.3 1.4 convolution_convert_fusion
  177.7 1.4 convolution_convert_fusion.1
  180.1 1.2 convert_add_fusion.1
  182.1 1.4 fusion.18
  183.9 1.2 collective-permute-start.29
  185.7 2.5 %convolution_convert_fusion.11 = bf16[256,1792]{1,0:T(8,128)(2,1)S(1)} fusion(bf16[2560,1792]{1,0:T(8,128)(2,1)S(1)} %shard_map.116, bf16[128,2560]{1,0:T(8,128)(2,1)S(1)} %collective-permute-done.30, bf16[64,2560]{1,0:T(8,128)(2,1)S(1)} %fusion.18, bf16[64,2560]{1,0:T(8,128)(2,1)S(1)} %fusion.22), kind=kOutput, calls=%fused_computation.11 | convolution fusion | flops 2353201152 | bytes 11403264 | tf_op jit(solution)/shard_map/dot_general | solution.py:194
  189.0 11.9 %collective-permute-done.29 = bf16[128,2560]{1,0:T(8,128)(2,1)} collective-permute-done((bf16[128,2560]{1,0:T(8,128)(2,1)S(1)}, bf16[128,2560]{1,0:T(8,128)(2,1)}, u32[]{:S(2)}, u32[]{:S(2)}) %collective-permute-start.29) | collective-permute-done | bytes 655392 | tf_op jit(solution)/shard_map/ppermute | solution.py:182
  201.2 1.1 convert_add_fusion.3
  202.3 0.9 collective-permute-done.31
  203.2 6.4 %convolution_convert_fusion.10 = bf16[256,1792]{1,0:T(8,128)(2,1)S(1)} fusion(bf16[2560,1792]{1,0:T(8,128)(2,1)} %copy-done.2, bf16[128,2560]{1,0:T(8,128)(2,1)S(1)} %collective-permute-done.31, bf16[128,2560]{1,0:T(8,128)(2,1)} %collective-permute-done.29), kind=kOutput, calls=%fused_computation.10 | convolution fusion | flops 2351890432 | bytes 11403264 | tf_op jit(solution)/shard_map/dot_general | solution.py:194
  210.3 3.4 %collective-permute-start.35 = (bf16[64,1792]{1,0:T(8,128)(2,1)S(1)}, bf16[64,1792]{1,0:T(8,128)(2,1)S(1)}, u32[]{:S(2)}, u32[]{:S(2)}) collective-permute-start(bf16[64,1792]{1,0:T(8,128)(2,1)S(1)} %fusion.40), channel_id=1, source_target_pairs={{0,8},{4,12},{8,0},{12,4},{1,9},{5,13},{9,1},{13,5},{2,10},{6,14},... | collective-permute-start | bytes 688136 | tf_op jit(solution)/shard_map/ppermute | solution.py:182
  213.7 13.5 %collective-permute-done.33 = bf16[2,64,1792]{2,1,0:T(8,128)(2,1)S(1)} collective-permute-done((bf16[2,64,1792]{2,1,0:T(8,128)(2,1)S(1)}, bf16[2,64,1792]{2,1,0:T(8,128)(2,1)S(1)}, u32[]{:S(2)}, u32[]{:S(2)}) %collective-permute-start.33) | collective-permute-done | bytes 458784 | tf_op jit(solution)/shard_map/ppermute | solution.py:182
  227.3 1.6 collective-permute-start.34
  228.9 11.1 %collective-permute-done.34 = bf16[64,1792]{1,0:T(8,128)(2,1)S(1)} collective-permute-done((bf16[64,1792]{1,0:T(8,128)(2,1)S(1)}, bf16[64,1792]{1,0:T(8,128)(2,1)S(1)}, u32[]{:S(2)}, u32[]{:S(2)}) %collective-permute-start.34) | collective-permute-done | bytes 229408 | tf_op jit(solution)/shard_map/ppermute | solution.py:182
  240.2 0.8 pad_maximum_fusion.11
  241.0 0.8 pad_maximum_fusion.9
  (169 shorter events, 12.3 us)
Async XLA Ops:
  1.6 17.0 %copy-start.4 = (bf16[512,2048]{1,0:T(8,128)(2,1)S(1)}, bf16[512,2048]{1,0:T(8,128)(2,1)}, u32[]{:S(2)}) copy-start(bf16[512,2048]{1,0:T(8,128)(2,1)} %value_weight.1) | copy-start | bytes 6291460
  4.8 10.8 %collective-permute-start.1 = (bf16[288,128]{1,0:T(8,128)(2,1)S(1)}, bf16[288,128]{1,0:T(8,128)(2,1)S(1)}, u32[]{:S(2)}, u32[]{:S(2)}) collective-permute-start(bf16[288,128]{1,0:T(8,128)(2,1)S(1)} %fusion.47), channel_id=1, source_target_pairs={{0,8},{4,12},{1,9},{5,13},{2,10},{6,14},{3,11},{7,15},{16,24},{20,... | collective-permute-start | bytes 221192 | tf_op jit(solution)/shard_map/ppermute | solution.py:233
  10.8 4.9 %collective-permute-start = (bf16[288,128]{1,0:T(8,128)(2,1)S(1)}, bf16[288,128]{1,0:T(8,128)(2,1)S(1)}, u32[]{:S(2)}, u32[]{:S(2)}) collective-permute-start(bf16[288,128]{1,0:T(8,128)(2,1)S(1)} %fusion.47), channel_id=1, source_target_pairs={{0,12},{1,13},{2,14},{3,15},{16,28},{17,29},{18,30},{19,31}} | collective-permute-start | bytes 221192 | tf_op jit(solution)/shard_map/ppermute | solution.py:233
  13.1 3.8 %collective-permute-start.2 = (bf16[288,128]{1,0:T(8,128)(2,1)S(1)}, bf16[288,128]{1,0:T(8,128)(2,1)S(1)}, u32[]{:S(2)}, u32[]{:S(2)}) collective-permute-start(bf16[288,128]{1,0:T(8,128)(2,1)S(1)} %fusion.47), channel_id=1, source_target_pairs={{0,4},{4,8},{8,12},{1,5},{5,9},{9,13},{2,6},{6,10},{10,14},{3,7},{... | collective-permute-start | bytes 221192 | tf_op jit(solution)/shard_map/ppermute | solution.py:233
  16.9 1.7 copy-start.3
  16.9 1.5 collective-permute-start.3
  25.2 13.7 %slice-start.9 = ((s8[9175040]{0:T(1024)(128)(4,1)}), s8[4194304]{0:T(1024)(128)(4,1)S(1)}, s32[]{:S(2)}) async-start(s8[9175040]{0:T(1024)(128)(4,1)} %bitcast.126), calls=%async_computation.9 | async-start | bytes 8388608
  25.3 19.1 %collective-permute-start.7 = (bf16[32,2048]{1,0:T(8,128)(2,1)S(1)}, bf16[32,2048]{1,0:T(8,128)(2,1)S(1)}, u32[]{:S(2)}, u32[]{:S(2)}) collective-permute-start(bf16[32,2048]{1,0:T(8,128)(2,1)S(1)} %get-tuple-element.71), channel_id=1, source_target_pairs={{0,3},{1,7},{2,11},{3,15},{4,2},{5,6},{6,10},{7,14},{8,1},{9,5},{1... | collective-permute-start | bytes 393224 | tf_op jit(solution)/shard_map/ppermute | solution.py:247
  26.6 20.6 %collective-permute-start.6 = (bf16[32,2048]{1,0:T(8,128)(2,1)S(1)}, bf16[32,2048]{1,0:T(8,128)(2,1)S(1)}, u32[]{:S(2)}, u32[]{:S(2)}) collective-permute-start(bf16[32,2048]{1,0:T(8,128)(2,1)S(1)} %get-tuple-element.72), channel_id=1, source_target_pairs={{0,2},{1,6},{2,10},{3,14},{4,3},{5,7},{6,11},{7,15},{8,0},{9,4},{1... | collective-permute-start | bytes 393224 | tf_op jit(solution)/shard_map/ppermute | solution.py:247
  30.1 17.1 %collective-permute-start.5 = (bf16[32,2048]{1,0:T(8,128)(2,1)S(1)}, bf16[32,2048]{1,0:T(8,128)(2,1)S(1)}, u32[]{:S(2)}, u32[]{:S(2)}) collective-permute-start(bf16[32,2048]{1,0:T(8,128)(2,1)S(1)} %get-tuple-element.73), channel_id=1, source_target_pairs={{0,1},{1,5},{2,9},{3,13},{4,0},{5,4},{6,8},{7,12},{8,3},{9,7},{10,... | collective-permute-start | bytes 393224 | tf_op jit(solution)/shard_map/ppermute | solution.py:247
  30.5 8.4 %slice-start.10 = ((s8[9175040]{0:T(1024)(128)(4,1)}), s8[4194304]{0:T(1024)(128)(4,1)S(1)}, s32[]{:S(2)}) async-start(s8[9175040]{0:T(1024)(128)(4,1)} %bitcast.126), calls=%async_computation.10 | async-start | bytes 8388608
  30.5 8.4 %slice-start.11 = ((s8[9175040]{0:T(1024)(128)(4,1)}), s8[786432]{0:T(1024)(128)(4,1)S(1)}, s32[]{:S(2)}) async-start(s8[9175040]{0:T(1024)(128)(4,1)} %bitcast.126), calls=%async_computation.11 | async-start | bytes 1572864
  30.5 16.7 %collective-permute-start.4 = (bf16[32,2048]{1,0:T(8,128)(2,1)S(1)}, bf16[32,2048]{1,0:T(8,128)(2,1)S(1)}, u32[]{:S(2)}, u32[]{:S(2)}) collective-permute-start(bf16[32,2048]{1,0:T(8,128)(2,1)S(1)} %get-tuple-element.74), channel_id=1, source_target_pairs={{0,0},{1,4},{2,8},{3,12},{4,1},{5,5},{6,9},{7,13},{8,2},{9,6},{10,... | collective-permute-start | bytes 393224 | tf_op jit(solution)/shard_map/ppermute | solution.py:247
  35.4 3.5 %copy-start = (bf16[1792,2560]{1,0:T(8,128)(2,1)}, bf16[1792,2560]{1,0:T(8,128)(2,1)S(1)}, u32[]{:S(2)}) copy-start(bf16[1792,2560]{1,0:T(8,128)(2,1)S(1)} %shard_map.114) | copy-start | bytes 27525124
  40.8 3.6 %copy-start.1 = (bf16[1792,2560]{1,0:T(8,128)(2,1)}, bf16[1792,2560]{1,0:T(8,128)(2,1)S(1)}, u32[]{:S(2)}) copy-start(bf16[1792,2560]{1,0:T(8,128)(2,1)S(1)} %shard_map.115) | copy-start | bytes 27525124
  47.3 2.0 collective-permute-start.8
  54.6 32.3 %copy-start.8 = (bf16[128,1792]{1,0:T(8,128)(2,1)S(1)}, bf16[128,1792]{1,0:T(8,128)(2,1)}, u32[]{:S(2)}) copy-start(bf16[128,1792]{1,0:T(8,128)(2,1)} %param.10) | copy-start | bytes 1376260
  54.7 12.7 %collective-permute-start.9 = (bf16[2,64,1792]{2,1,0:T(8,128)(2,1)S(1)}, bf16[2,64,1792]{2,1,0:T(8,128)(2,1)}, u32[]{:S(2)}, u32[]{:S(2)}) collective-permute-start(bf16[2,64,1792]{2,1,0:T(8,128)(2,1)S(1)} %pad_maximum_fusion.6), channel_id=1, source_target_pairs={{0,4},{4,0},{8,12},{12,8},{1,5},{5,1},{9,13},{13,9},{2,6},{6,2},{1... | collective-permute-start | bytes 1376264 | tf_op jit(solution)/shard_map/ppermute | solution.py:182
  55.3 21.3 %collective-permute-start.11 = (bf16[4,32,2048]{2,1,0:T(8,128)(2,1)S(1)}, bf16[4,32,2048]{2,1,0:T(8,128)(2,1)S(1)}, u32[]{:S(2)}, u32[]{:S(2)}) collective-permute-start(bf16[4,32,2048]{2,1,0:T(8,128)(2,1)S(1)} %pad_maximum_fusion.5), channel_id=1, source_target_pairs={{0,2},{1,3},{2,0},{3,1},{4,6},{5,7},{6,4},{7,5},{8,10},{9,11},{10,... | collective-permute-start | bytes 1572872 | tf_op jit(solution)/shard_map/ppermute | solution.py:182
  68.4 18.4 %collective-permute-start.10 = (bf16[64,1792]{1,0:T(8,128)(2,1)S(1)}, bf16[64,1792]{1,0:T(8,128)(2,1)S(1)}, u32[]{:S(2)}, u32[]{:S(2)}) collective-permute-start(bf16[64,1792]{1,0:T(8,128)(2,1)S(1)} %fusion.38), channel_id=1, source_target_pairs={{0,8},{4,12},{8,0},{12,4},{1,9},{5,13},{9,1},{13,5},{2,10},{6,14},... | collective-permute-start | bytes 688136 | tf_op jit(solution)/shard_map/ppermute | solution.py:182
  76.6 11.3 %collective-permute-start.12 = (bf16[4,32,2048]{2,1,0:T(8,128)(2,1)S(1)}, bf16[4,32,2048]{2,1,0:T(8,128)(2,1)S(1)}, u32[]{:S(2)}, u32[]{:S(2)}) collective-permute-start(bf16[4,32,2048]{2,1,0:T(8,128)(2,1)S(1)} %collective-permute-done.11), channel_id=1, source_target_pairs={{0,1},{1,0},{2,3},{3,2},{4,5},{5,4},{6,7},{7,6},{8,9},{9,8},{10,11... | collective-permute-start | bytes 1572872 | tf_op jit(solution)/shard_map/ppermute | solution.py:182
  93.2 17.3 %copy-start.5 = (f32[1792]{0:T(1024)S(1)}, f32[1792]{0:T(1024)}, u32[]{:S(2)}) copy-start(f32[1792]{0:T(1024)} %param.16) | copy-start | bytes 21508
  93.4 16.4 %collective-permute-start.13 = (bf16[2,64,1792]{2,1,0:T(8,128)(2,1)S(1)}, bf16[2,64,1792]{2,1,0:T(8,128)(2,1)S(1)}, u32[]{:S(2)}, u32[]{:S(2)}) collective-permute-start(bf16[2,64,1792]{2,1,0:T(8,128)(2,1)S(1)} %pad_maximum_fusion.7), channel_id=1, source_target_pairs={{0,4},{4,0},{8,12},{12,8},{1,5},{5,1},{9,13},{13,9},{2,6},{6,2},{1... | collective-permute-start | bytes 1376264 | tf_op jit(solution)/shard_map/ppermute | solution.py:182
  94.1 16.4 %collective-permute-start.15 = (bf16[64,1792]{1,0:T(8,128)(2,1)S(1)}, bf16[64,1792]{1,0:T(8,128)(2,1)S(1)}, u32[]{:S(2)}, u32[]{:S(2)}) collective-permute-start(bf16[64,1792]{1,0:T(8,128)(2,1)S(1)} %fusion.29), channel_id=1, source_target_pairs={{0,8},{4,12},{8,0},{12,4},{1,9},{5,13},{9,1},{13,5},{2,10},{6,14},... | collective-permute-start | bytes 688136 | tf_op jit(solution)/shard_map/ppermute | solution.py:182
  109.8 6.4 %copy-start.6 = (bf16[2,64,1792]{2,1,0:T(8,128)(2,1)}, bf16[2,64,1792]{2,1,0:T(8,128)(2,1)S(1)}, u32[]{:S(2)}) copy-start(bf16[2,64,1792]{2,1,0:T(8,128)(2,1)S(1)} %collective-permute-done.13) | copy-start | bytes 1376260
  109.8 6.4 %slice-start.3 = ((s8[9175040]{0:T(1024)(128)(4,1)}), s8[4194304]{0:T(1024)(128)(4,1)S(1)}, s32[]{:S(2)}) async-start(s8[9175040]{0:T(1024)(128)(4,1)} %bitcast.122), calls=%async_computation.3 | async-start | bytes 8388608
  110.5 5.7 %slice-start.4 = ((s8[9175040]{0:T(1024)(128)(4,1)}), s8[4194304]{0:T(1024)(128)(4,1)S(1)}, s32[]{:S(2)}) async-start(s8[9175040]{0:T(1024)(128)(4,1)} %bitcast.122), calls=%async_computation.4 | async-start | bytes 8388608
  110.5 5.8 %slice-start.5 = ((s8[9175040]{0:T(1024)(128)(4,1)}), s8[786432]{0:T(1024)(128)(4,1)S(1)}, s32[]{:S(2)}) async-start(s8[9175040]{0:T(1024)(128)(4,1)} %bitcast.122), calls=%async_computation.5 | async-start | bytes 1572864
  117.9 5.4 %collective-permute-start.16 = (bf16[128,2560]{1,0:T(8,128)(2,1)S(1)}, bf16[128,2560]{1,0:T(8,128)(2,1)S(1)}, u32[]{:S(2)}, u32[]{:S(2)}) collective-permute-start(bf16[128,2560]{1,0:T(8,128)(2,1)S(1)} %pad_maximum_fusion), channel_id=1, source_target_pairs={{0,1},{1,0},{2,3},{3,2},{4,5},{5,4},{6,7},{7,6},{8,9},{9,8},{10,11... | collective-permute-start | bytes 1966088 | tf_op jit(solution)/shard_map/ppermute | solution.py:182
  118.0 14.2 %copy-start.7 = (bf16[2,64,1792]{2,1,0:T(8,128)(2,1)S(1)}, bf16[2,64,1792]{2,1,0:T(8,128)(2,1)}, u32[]{:S(2)}) copy-start(bf16[2,64,1792]{2,1,0:T(8,128)(2,1)} %copy-done.6) | copy-start | bytes 1376260
  118.0 14.2 %copy-start.9 = (bf16[128,1792]{1,0:T(8,128)(2,1)S(1)}, bf16[128,1792]{1,0:T(8,128)(2,1)}, u32[]{:S(2)}) copy-start(bf16[128,1792]{1,0:T(8,128)(2,1)} %param.10) | copy-start | bytes 1376260
  118.0 14.1 %collective-permute-start.14 = (bf16[64,1792]{1,0:T(8,128)(2,1)}, bf16[64,1792]{1,0:T(8,128)(2,1)S(1)}, u32[]{:S(2)}, u32[]{:S(2)}) collective-permute-start(bf16[64,1792]{1,0:T(8,128)(2,1)} %fusion.39), channel_id=1, source_target_pairs={{0,8},{4,12},{8,0},{12,4},{1,9},{5,13},{9,1},{13,5},{2,10},{6,14},... | collective-permute-start | bytes 688136 | tf_op jit(solution)/shard_map/ppermute | solution.py:182
  120.8 19.8 %collective-permute-start.17 = (bf16[128,1792]{1,0:T(8,128)(2,1)S(1)}, bf16[128,1792]{1,0:T(8,128)(2,1)S(1)}, u32[]{:S(2)}, u32[]{:S(2)}) collective-permute-start(bf16[128,1792]{1,0:T(8,128)(2,1)S(1)} %pad_maximum_fusion.8), channel_id=1, source_target_pairs={{0,4},{4,0},{8,12},{12,8},{1,5},{5,1},{9,13},{13,9},{2,6},{6,2},{1... | collective-permute-start | bytes 1376264 | tf_op jit(solution)/shard_map/ppermute | solution.py:182
  123.5 21.9 %collective-permute-start.18 = (bf16[128,2560]{1,0:T(8,128)(2,1)S(1)}, bf16[128,2560]{1,0:T(8,128)(2,1)S(1)}, u32[]{:S(2)}, u32[]{:S(2)}) collective-permute-start(bf16[128,2560]{1,0:T(8,128)(2,1)S(1)} %add_convert_fusion.1), channel_id=1, source_target_pairs={{0,2},{1,3},{2,0},{3,1},{4,6},{5,7},{6,4},{7,5},{8,10},{9,11},{10,... | collective-permute-start | bytes 1966088 | tf_op jit(solution)/shard_map/ppermute | solution.py:182
  132.3 13.0 %collective-permute-start.19 = (bf16[64,1792]{1,0:T(8,128)(2,1)S(1)}, bf16[64,1792]{1,0:T(8,128)(2,1)S(1)}, u32[]{:S(2)}, u32[]{:S(2)}) collective-permute-start(bf16[64,1792]{1,0:T(8,128)(2,1)S(1)} %get-tuple-element.50), channel_id=1, source_target_pairs={{0,8},{4,12},{8,0},{12,4},{1,9},{5,13},{9,1},{13,5},{2,10},{6,14},... | collective-permute-start | bytes 688136 | tf_op jit(solution)/shard_map/ppermute | solution.py:182
  132.4 18.1 %slice-start = ((s8[9175040]{0:T(1024)(128)(4,1)}), s8[4194304]{0:T(1024)(128)(4,1)S(1)}, s32[]{:S(2)}) async-start(s8[9175040]{0:T(1024)(128)(4,1)} %bitcast.120), calls=%async_computation | async-start | bytes 8388608
  132.6 17.9 %slice-start.1 = ((s8[9175040]{0:T(1024)(128)(4,1)}), s8[4194304]{0:T(1024)(128)(4,1)S(1)}, s32[]{:S(2)}) async-start(s8[9175040]{0:T(1024)(128)(4,1)} %bitcast.120), calls=%async_computation.1 | async-start | bytes 8388608
  132.6 17.9 %slice-start.2 = ((s8[9175040]{0:T(1024)(128)(4,1)}), s8[786432]{0:T(1024)(128)(4,1)S(1)}, s32[]{:S(2)}) async-start(s8[9175040]{0:T(1024)(128)(4,1)} %bitcast.120), calls=%async_computation.2 | async-start | bytes 1572864
  145.4 10.9 %slice-start.6 = ((s8[9175040]{0:T(1024)(128)(4,1)}), s8[4194304]{0:T(1024)(128)(4,1)S(1)}, s32[]{:S(2)}) async-start(s8[9175040]{0:T(1024)(128)(4,1)} %bitcast.124), calls=%async_computation.6 | async-start | bytes 8388608
  145.4 10.9 %slice-start.7 = ((s8[9175040]{0:T(1024)(128)(4,1)}), s8[4194304]{0:T(1024)(128)(4,1)S(1)}, s32[]{:S(2)}) async-start(s8[9175040]{0:T(1024)(128)(4,1)} %bitcast.124), calls=%async_computation.7 | async-start | bytes 8388608
  150.5 5.8 %slice-start.8 = ((s8[9175040]{0:T(1024)(128)(4,1)}), s8[786432]{0:T(1024)(128)(4,1)S(1)}, s32[]{:S(2)}) async-start(s8[9175040]{0:T(1024)(128)(4,1)} %bitcast.124), calls=%async_computation.8 | async-start | bytes 1572864
  152.1 3.0 %collective-permute-start.20 = (bf16[128,2560]{1,0:T(8,128)(2,1)S(1)}, bf16[128,2560]{1,0:T(8,128)(2,1)S(1)}, u32[]{:S(2)}, u32[]{:S(2)}) collective-permute-start(bf16[128,2560]{1,0:T(8,128)(2,1)S(1)} %pad_maximum_fusion.1), channel_id=1, source_target_pairs={{0,1},{1,0},{2,3},{3,2},{4,5},{5,4},{6,7},{7,6},{8,9},{9,8},{10,11... | collective-permute-start | bytes 1966088 | tf_op jit(solution)/shard_map/ppermute | solution.py:182
  152.4 1.9 collective-permute-start.23
  153.0 12.5 %collective-permute-start.25 = (bf16[128,1792]{1,0:T(8,128)(2,1)S(1)}, bf16[128,1792]{1,0:T(8,128)(2,1)S(1)}, u32[]{:S(2)}, u32[]{:S(2)}) collective-permute-start(bf16[128,1792]{1,0:T(8,128)(2,1)S(1)} %pad_maximum_fusion.10), channel_id=1, source_target_pairs={{0,4},{4,0},{8,12},{12,8},{1,5},{5,1},{9,13},{13,9},{2,6},{6,2},{1... | collective-permute-start | bytes 1376264 | tf_op jit(solution)/shard_map/ppermute | solution.py:182
  154.3 27.1 %collective-permute-start.24 = (f32[256]{0:T(256)S(1)}, f32[256]{0:T(256)S(1)}, u32[]{:S(2)}, u32[]{:S(2)}) collective-permute-start(f32[256]{0:T(256)S(1)} %fusion.59), channel_id=1, source_target_pairs={{0,2},{1,3},{2,0},{3,1},{4,6},{5,7},{6,4},{7,5},{8,10},{9,11},{10,... | collective-permute-start | bytes 3080 | tf_op jit(solution)/shard_map/ppermute | solution.py:182
  156.3 5.9 %slice-start.12 = ((s8[9175040]{0:T(1024)(128)(4,1)}), s8[4194304]{0:T(1024)(128)(4,1)S(1)}, s32[]{:S(2)}) async-start(s8[9175040]{0:T(1024)(128)(4,1)} %bitcast.128), calls=%async_computation.12 | async-start | bytes 8388608
  156.3 5.9 %slice-start.13 = ((s8[9175040]{0:T(1024)(128)(4,1)}), s8[4194304]{0:T(1024)(128)(4,1)S(1)}, s32[]{:S(2)}) async-start(s8[9175040]{0:T(1024)(128)(4,1)} %bitcast.128), calls=%async_computation.13 | async-start | bytes 8388608
  158.0 4.3 %slice-start.14 = ((s8[9175040]{0:T(1024)(128)(4,1)}), s8[786432]{0:T(1024)(128)(4,1)S(1)}, s32[]{:S(2)}) async-start(s8[9175040]{0:T(1024)(128)(4,1)} %bitcast.128), calls=%async_computation.14 | async-start | bytes 1572864
  159.5 16.9 %collective-permute-start.26 = (bf16[128,2560]{1,0:T(8,128)(2,1)}, bf16[128,2560]{1,0:T(8,128)(2,1)}, u32[]{:S(2)}, u32[]{:S(2)}) collective-permute-start(bf16[128,2560]{1,0:T(8,128)(2,1)} %add_convert_fusion), channel_id=1, source_target_pairs={{0,2},{1,3},{2,0},{3,1},{4,6},{5,7},{6,4},{7,5},{8,10},{9,11},{10,... | collective-permute-start | bytes 1966088 | tf_op jit(solution)/shard_map/ppermute | solution.py:182
  160.8 20.6 %collective-permute-start.22 = (f32[128]{0:T(128)S(1)}, f32[128]{0:T(128)S(1)}, u32[]{:S(2)}, u32[]{:S(2)}) collective-permute-start(f32[128]{0:T(128)S(1)} %fusion.13), channel_id=1, source_target_pairs={{0,1},{1,0},{2,3},{3,2},{4,5},{5,4},{6,7},{7,6},{8,9},{9,8},{10,11... | collective-permute-start | bytes 1544 | tf_op jit(solution)/shard_map/ppermute | solution.py:182
  161.8 18.4 %collective-permute-start.21 = (bf16[128,2560]{1,0:T(8,128)(2,1)}, bf16[128,2560]{1,0:T(8,128)(2,1)}, u32[]{:S(2)}, u32[]{:S(2)}) collective-permute-start(bf16[128,2560]{1,0:T(8,128)(2,1)} %pad_maximum_fusion.2), channel_id=1, source_target_pairs={{0,1},{1,0},{2,3},{3,2},{4,5},{5,4},{6,7},{7,6},{8,9},{9,8},{10,11... | collective-permute-start | bytes 1966088 | tf_op jit(solution)/shard_map/ppermute | solution.py:182
  164.0 21.8 %copy-start.2 = (bf16[2560,1792]{1,0:T(8,128)(2,1)}, bf16[2560,1792]{1,0:T(8,128)(2,1)S(1)}, u32[]{:S(2)}) copy-start(bf16[2560,1792]{1,0:T(8,128)(2,1)S(1)} %shard_map.116) | copy-start | bytes 27525124
  179.4 2.0 collective-permute-start.28
  179.6 2.4 collective-permute-start.27
  183.6 2.2 collective-permute-start.30
  183.9 17.0 %collective-permute-start.29 = (bf16[128,2560]{1,0:T(8,128)(2,1)S(1)}, bf16[128,2560]{1,0:T(8,128)(2,1)}, u32[]{:S(2)}, u32[]{:S(2)}) collective-permute-start(bf16[128,2560]{1,0:T(8,128)(2,1)S(1)} %pad_maximum_fusion.4), channel_id=1, source_target_pairs={{0,2},{1,3},{2,0},{3,1},{4,6},{5,7},{6,4},{7,5},{8,10},{9,11},{10,... | collective-permute-start | bytes 1966088 | tf_op jit(solution)/shard_map/ppermute | solution.py:182
  188.3 12.9 %collective-permute-start.32 = (bf16[2,64,1792]{2,1,0:T(8,128)(2,1)S(1)}, bf16[2,64,1792]{2,1,0:T(8,128)(2,1)}, u32[]{:S(2)}, u32[]{:S(2)}) collective-permute-start(bf16[2,64,1792]{2,1,0:T(8,128)(2,1)S(1)} %slice_bitcast_fusion.2), channel_id=1, source_target_pairs={{0,4},{4,0},{8,12},{12,8},{1,5},{5,1},{9,13},{13,9},{2,6},{6,2},{1... | collective-permute-start | bytes 1376264 | tf_op jit(solution)/shard_map/ppermute | solution.py:182
  200.9 2.3 collective-permute-start.31
  209.6 17.5 %collective-permute-start.33 = (bf16[2,64,1792]{2,1,0:T(8,128)(2,1)S(1)}, bf16[2,64,1792]{2,1,0:T(8,128)(2,1)S(1)}, u32[]{:S(2)}, u32[]{:S(2)}) collective-permute-start(bf16[2,64,1792]{2,1,0:T(8,128)(2,1)S(1)} %slice_bitcast_fusion), channel_id=1, source_target_pairs={{0,4},{4,0},{8,12},{12,8},{1,5},{5,1},{9,13},{13,9},{2,6},{6,2},{1... | collective-permute-start | bytes 1376264 | tf_op jit(solution)/shard_map/ppermute | solution.py:182
  210.3 18.6 %collective-permute-start.35 = (bf16[64,1792]{1,0:T(8,128)(2,1)S(1)}, bf16[64,1792]{1,0:T(8,128)(2,1)S(1)}, u32[]{:S(2)}, u32[]{:S(2)}) collective-permute-start(bf16[64,1792]{1,0:T(8,128)(2,1)S(1)} %fusion.40), channel_id=1, source_target_pairs={{0,8},{4,12},{8,0},{12,4},{1,9},{5,13},{9,1},{13,5},{2,10},{6,14},... | collective-permute-start | bytes 688136 | tf_op jit(solution)/shard_map/ppermute | solution.py:182
  227.3 12.7 %collective-permute-start.34 = (bf16[64,1792]{1,0:T(8,128)(2,1)S(1)}, bf16[64,1792]{1,0:T(8,128)(2,1)S(1)}, u32[]{:S(2)}, u32[]{:S(2)}) collective-permute-start(bf16[64,1792]{1,0:T(8,128)(2,1)S(1)} %fusion.41), channel_id=1, source_target_pairs={{0,8},{4,12},{8,0},{12,4},{1,9},{5,13},{9,1},{13,5},{2,10},{6,14},... | collective-permute-start | bytes 688136 | tf_op jit(solution)/shard_map/ppermute | solution.py:182

commit v10 on v9

--- a/solution.py
+++ b/solution.py
@@ -194,31 +194,53 @@
     return jnp.dot(a, b, preferred_element_type=jnp.float32).astype(jnp.bfloat16)
 
 
-def load_kernel(chunks, weight, out, sems):
-    rows = weight.shape[0] // chunks
+def streamed_kernel(depth, rows, weight, out, held, total, sems):
+    steps = weight.shape[0] // depth
     copies = [
         pltpu.make_async_copy(
-            weight.at[pl.ds(i * rows, rows)], out.at[pl.ds(i * rows, rows)], sems.at[i]
+            weight.at[pl.ds(i * depth, depth)], held.at[pl.ds(i * depth, depth)], sems.at[i]
         )
-        for i in range(chunks)
+        for i in range(steps)
     ]
     for copy in copies:
         copy.start()
-    for copy in copies:
+    block = 256
+    for i, copy in enumerate(copies):
         copy.wait()
-
-
-def load(weight, grant):
-    chunks = 8
+        part = rows[:, i * depth : (i + 1) * depth]
+        for start in range(0, weight.shape[1], block):
+            columns = slice(start, start + block)
+            term = jnp.dot(
+                part,
+                held[i * depth : (i + 1) * depth, columns],
+                preferred_element_type=jnp.float32,
+            )
+            if i > 0:
+                term = term + total[:, columns]
+            if i < steps - 1:
+                total[:, columns] = term
+            else:
+                out[:, columns] = term.astype(out.dtype)
+
+
+def streamed_matmul(rows, weight):
+    steps = weight.shape[0] // 512
     return pl.pallas_call(
-        functools.partial(load_kernel, chunks),
-        in_specs=[pl.BlockSpec(memory_space=pltpu.HBM)],
+        functools.partial(streamed_kernel, 512),
+        in_specs=[
+            pl.BlockSpec(memory_space=pltpu.VMEM),
+            pl.BlockSpec(memory_space=pl.ANY),
+        ],
         out_specs=pl.BlockSpec(memory_space=pltpu.VMEM),
-        out_shape=pltpu.VMEM(weight.shape, weight.dtype),
-        scratch_shapes=[pltpu.SemaphoreType.DMA((chunks,))],
-        compiler_params=pltpu.CompilerParams(vmem_limit_bytes=grant * 1024 * 1024),
-        cost_estimate=pl.CostEstimate(flops=0, bytes_accessed=1024, transcendentals=0),
-    )(weight)
+        out_shape=jax.ShapeDtypeStruct((rows.shape[0], weight.shape[1]), jnp.bfloat16),
+        scratch_shapes=[
+            pltpu.VMEM(weight.shape, weight.dtype),
+            pltpu.VMEM((rows.shape[0], weight.shape[1]), jnp.float32),
+            pltpu.SemaphoreType.DMA((steps,)),
+        ],
+        compiler_params=pltpu.CompilerParams(vmem_limit_bytes=50 * 1024 * 1024),
+        cost_estimate=pl.CostEstimate(flops=1024, bytes_accessed=1024, transcendentals=0),
+    )(rows, weight)
 
 
 def after(value, earlier):
@@ -242,21 +264,20 @@
 
 
 def spread_heads(heads_out, n_ctx, n_tp):
-    pieces = heads_out.reshape(n_ctx, heads_out.shape[0] // n_ctx, heads_out.shape[1])
-    return [
-        lax.ppermute(
-            pieces[s],
-            ("ctx", "tp"),
-            [(c * n_tp + t, t * n_tp + (c ^ s)) for c in range(n_ctx) for t in range(n_tp)],
-        )
-        for s in range(n_ctx)
-    ]
-
-
-def pair_rows(first, second):
-    return jnp.concatenate(
-        [first[0], second[1], second[0], first[1], first[2], second[3], second[2], first[3]], axis=0
-    )
+    c, t = lax.axis_index("ctx"), lax.axis_index("tp")
+    quarters = heads_out.reshape(n_tp, heads_out.shape[0] // n_tp, heads_out.shape[1])
+    groups = jnp.stack(
+        [pick(quarters, t)] + [swap(pick(quarters, t ^ m), "tp", m) for m in range(1, n_tp)]
+    )
+    return jnp.stack(
+        [pick(groups, t ^ c)] + [swap(pick(groups, t ^ c ^ j), "ctx", j) for j in range(1, n_ctx)]
+    )
+
+
+def core_rows(mine, other):
+    first = lax.axis_index("tp") & 1 == 0
+    both = jnp.stack([jnp.where(first, mine, other), jnp.where(first, other, mine)], axis=1)
+    return both.reshape(-1, mine.shape[-1])
 
 
 def paired_tail(
@@ -265,23 +286,18 @@
     row_count, width = residual.shape
     half = row_count // 2
     model_width = width * n_tp
-    c = lax.axis_index("ctx")
     t = lax.axis_index("tp")
     core = t & 1
-    first_half = (t >> 1) ^ (c >> 1)
+    first_half = t >> 1
     own = spread_heads(heads_out, n_ctx, n_tp)
-    gate_weight = load(after(gate_weight, heads_out), 44)
-    up_weight = load(after(up_weight, gate_weight), 34)
-    own_all = jnp.stack(after(own, up_weight))
-    near = swap(own_all, "tp", 1)
+    near = swap(own, "tp", 1)
+    far = swap(own, "tp", 2)
     residual_halves = residual.reshape(2, half, width)
 
     def first_hop(rows):
-        blocks = matmul(rows, output_weight).reshape(n_ctx, half, width)
-        place = t ^ c
-        sent = jnp.stack([pick(blocks, place ^ 1), pick(blocks, place ^ 3)])
-        kept = [pick(blocks, place), pick(blocks, place ^ 2)]
-        return kept, sent, swap(sent, "ctx", 1)
+        blocks = streamed_matmul(rows, output_weight).reshape(2, 2, half, width)
+        sent = blocks[:, 1]
+        return blocks[:, 0], sent, swap(sent, "ctx", 1)
 
     def second_hop(kept, came):
         other = (wide(kept[1]) + wide(came[1])).astype(jnp.bfloat16)
@@ -305,18 +321,14 @@
     def chip_sum(kept, sent):
         return wide(kept) + wide(swap(sent, "tp", 1))
 
-    kept_a, sent_a, came_a = first_hop(pair_rows(own_all, near))
-    far = swap(after(own_all, sent_a), "tp", 2)
+    kept_a, sent_a, came_a = first_hop(core_rows(own, near))
+    far = after(far, sent_a)
+    far_near = swap(far, "tp", 1)
     mine_a, other_a, last_a = second_hop(kept_a, came_a)
-    far = after(far, other_a)
-    far_near = swap(far, "tp", 1)
-    attended_a = attend(mine_a, after(last_a, far), first_half)
+    kept_b, sent_b, came_b = first_hop(core_rows(far, after(far_near, other_a)))
+    attended_a = attend(mine_a, after(last_a, sent_b), first_half)
     twin_a = swap(attended_a, "ctx", 2)
-    far_near = after(far_near, attended_a)
-    order = [2, 3, 0, 1]
-    rows_b = pair_rows([far[i] for i in order], [far_near[i] for i in order])
-    kept_b, sent_b, came_b = first_hop(rows_b)
-    mine_b, other_b, last_b = second_hop(kept_b, came_b)
+    mine_b, other_b, last_b = second_hop(kept_b, after(came_b, attended_a))
     pair_a = jnp.concatenate([attended_a, after(twin_a, other_b)], axis=0)
     rest_a = swap(pair_a, "ctx", 1)
     kept, sent, squares_p = gate_up(pair_a)
@@ -343,8 +355,7 @@
 
     kept, sent, squares_p = gate_up(after(pair_b, sums_q))
     terms_p = chip_sum(kept, sent)
-    down_weight = load(after(down_weight, sums_q), 24)
-    rest_b, across_q, _, _ = lax.optimization_barrier((rest_b, across_q, sent, down_weight))
+    rest_b, across_q, _ = lax.optimization_barrier((rest_b, across_q, sent))
     kept, sent, squares_q = gate_up(rest_b)
     terms_q = chip_sum(kept, sent)
     hidden = jnp.concatenate(
@@ -358,7 +369,7 @@
     hidden_far = swap(hidden, "tp", 2)
 
     def down_hop(mine, other):
-        blocks = matmul(jnp.concatenate([mine, other], axis=0), down_weight)
+        blocks = streamed_matmul(jnp.concatenate([mine, other], axis=0), down_weight)
         blocks = blocks.reshape(2, 2, half, width)
         return blocks[:, 0], swap(blocks[:, 1], "ctx", 1)
 
@@ -397,7 +408,14 @@
     row_count = residual.shape[0]
     ctx_place = lax.axis_index("ctx")
     n_ctx, n_tp = lax.axis_size("ctx"), lax.axis_size("tp")
-    paired = n_ctx == 4 and n_tp == 4 and row_count % 64 == 0 and residual.shape[1] % 256 == 0
+    paired = (
+        n_ctx == 4
+        and n_tp == 4
+        and row_count % 64 == 0
+        and residual.shape[1] % 256 == 0
+        and output_weight.shape[0] % 512 == 0
+        and down_weight.shape[0] % 512 == 0
+    )
     own_index = ctx_place * row_count + jnp.arange(row_count, dtype=jnp.int32)
     _, own_position = trace_info(own_index, lengths)
     rotated_keys = rope_keys(latent, own_position, LAT)

time: 242 us -> 226 us (0.934)
  waiting for transfers between devices: 107 us -> 135 us
  starting transfers between devices: 54.2 us -> 31.1 us
  matrix products: 38.6 us -> 19.2 us
  Pallas kernels: 14.2 us -> 24.7 us
  local copies, waits for them, and re-layouts: 9.33 us -> 3.81 us
  other arithmetic: 16.3 us -> 11.1 us
    ppermute x29 -> x35, waiting for transfers between devices: 103 us -> 133 us  [swap(): return lax.ppermute(value, axis_name, [(i, i ^ bit) for i in range(width)])]
    dot_general x12 -> x8, matrix products: 38.6 us -> 19.2 us  [matmul(): jnp.dot(a, b, preferred_element_type=jnp.float32).astype(jnp.bfloat16)]
    ppermute x29 -> x35, starting transfers between devices: 38.1 us -> 21 us  [swap(): return lax.ppermute(value, axis_name, [(i, i ^ bit) for i in range(width)])]
    pallas_call x3 -> x4, Pallas kernels: 7.61 us -> 17.9 us  [streamed_matmul(): pl.pallas_call(functools.partial(streamed_kernel, 512), in_specs=[pl.Bloc...]
    unnamed x66 -> x34, local copies, waits for them, and re-layouts: 7.58 us -> 0.3 us
    ppermute x4 -> x0, starting transfers between devices: 6 us -> none  [spread_heads(): lax.ppermute(pieces[s], ('ctx', 'tp'), [(c * n_tp + t, t * n_tp + (c ^ s)...]
    ppermute x4 -> x0, waiting for transfers between devices: 2.85 us -> none  [spread_heads(): lax.ppermute(pieces[s], ('ctx', 'tp'), [(c * n_tp + t, t * n_tp + (c ^ s)...]
  transfers between devices with their start and end apart: 36 -> 38, of which waited for: 19 -> 25; matrix products, arithmetic and copies ran while one was open for 8% -> 6% of each run, Pallas kernels for 3% -> 6%
where the time goes in v10:
time: 226 us
  waiting for transfers between devices  135 us (60%)
  starting transfers between devices  31.1 us (14%)
  Pallas kernels  24.7 us (11%)
  matrix products  19.2 us (8%)
  other arithmetic  11.1 us (5%)
  local copies, waits for them, and re-layouts  3.81 us (2%)
    ppermute x35, waiting for transfers between devices, swap(): return lax.ppermute(value, axis_name, [(i, i ^ bit) for i in range(width)])  133 us
    ppermute x35, starting transfers between devices, swap(): return lax.ppermute(value, axis_name, [(i, i ^ bit) for i in range(width)])  21 us
    dot_general x8, matrix products, matmul(): jnp.dot(a, b, preferred_element_type=jnp.float32).astype(jnp.bfloat16)  19.2 us
    pallas_call x4, Pallas kernels, streamed_matmul(): pl.pallas_call(functools.partial(streamed_kernel, 512), in_specs=[pl.Bloc...  17.9 us
    ppermute x3, starting transfers between devices, gather_keys(): lax.ppermute(half, 'ctx', [(c, c + d) for c in range(n_ctx - d)])  10.1 us
    pallas_call x1, Pallas kernels, attention(): pl.pallas_call(functools.partial(attention_kernel, group), grid=(local_he...  6.8 us
  transfers between devices with their start and end apart: 38, of which 25 were waited for; matrix products, arithmetic and copies ran while one was open for 6% of the time, Pallas kernels for 6%

profile of v10, /device:TPU:0, one launch (start us, length us, event | category | flops | bytes accessed | tf_op | source)
XLA Modules:
  0.0 225.9 jit_solution(4899964723429914033)
XLA Ops:
  0.6 0.9 slice.92
  1.6 1.1 convert_element_type.242
  2.7 0.8 reduce-window.8
  3.5 0.7 subtract_subtract_fusion
  4.8 5.9 %collective-permute-start.1 = (bf16[288,128]{1,0:T(8,128)(2,1)S(1)}, bf16[288,128]{1,0:T(8,128)(2,1)S(1)}, u32[]{:S(2)}, u32[]{:S(2)}) collective-permute-start(bf16[288,128]{1,0:T(8,128)(2,1)S(1)} %fusion.39), channel_id=1, source_target_pairs={{0,8},{4,12},{1,9},{5,13},{2,10},{6,14},{3,11},{7,15},{16,24},{20,... | collective-permute-start | bytes 221192 | tf_op jit(solution)/shard_map/ppermute | solution.py:255
  10.8 2.3 %collective-permute-start = (bf16[288,128]{1,0:T(8,128)(2,1)S(1)}, bf16[288,128]{1,0:T(8,128)(2,1)S(1)}, u32[]{:S(2)}, u32[]{:S(2)}) collective-permute-start(bf16[288,128]{1,0:T(8,128)(2,1)S(1)} %fusion.39), channel_id=1, source_target_pairs={{0,12},{1,13},{2,14},{3,15},{16,28},{17,29},{18,30},{19,31}} | collective-permute-start | bytes 221192 | tf_op jit(solution)/shard_map/ppermute | solution.py:255
  13.1 1.8 collective-permute-start.2
  15.7 1.2 collective-permute-done.2
  17.1 1.4 collective-permute-done.3
  18.6 6.8 %shard_map.113 = bf16[128,2048]{1,0:T(8,128)(2,1)S(1)} custom-call(f32[4,128,128]{2,1,0:T(8,128)S(1)} %pad_maximum_fusion.15.tables, s32[128,1]{1,0:T(8,128)S(1)} %copy.19.starts, s32[128,1]{1,0:T(8,128)S(1)} %iota_add_fusion.own_index, s32[1,512]{1,0:T(1,128)S(1)} %iota_add_fusion.1.key_index, bf16[576,512]{1,0:T(8,128)(2,1)S(1)} %maximum_maximum_fusion.keys, ...), custom_call_target="tpu_custom_call" | custom-call | flops 2684354560 | bytes 5046272 | tf_op jit(solution)/shard_map/pallas_call | solution.py:143
  25.5 1.3 collective-permute-start.6
  26.8 0.6 collective-permute-start.5
  27.4 3.6 %collective-permute-done.6 = bf16[32,2048]{1,0:T(8,128)(2,1)S(1)} collective-permute-done((bf16[32,2048]{1,0:T(8,128)(2,1)S(1)}, bf16[32,2048]{1,0:T(8,128)(2,1)S(1)}, u32[]{:S(2)}, u32[]{:S(2)}) %collective-permute-start.6) | collective-permute-done | bytes 131104 | tf_op jit(solution)/shard_map/ppermute | solution.py:182
  31.0 3.1 %collective-permute-done.5 = bf16[32,2048]{1,0:T(8,128)(2,1)S(1)} collective-permute-done((bf16[32,2048]{1,0:T(8,128)(2,1)S(1)}, bf16[32,2048]{1,0:T(8,128)(2,1)S(1)}, u32[]{:S(2)}, u32[]{:S(2)}) %collective-permute-start.5) | collective-permute-done | bytes 131104 | tf_op jit(solution)/shard_map/ppermute | solution.py:182
  34.3 4.4 %collective-permute-start.9 = (bf16[32,2048]{1,0:T(8,128)(2,1)S(1)}, bf16[32,2048]{1,0:T(8,128)(2,1)S(1)}, u32[]{:S(2)}, u32[]{:S(2)}) collective-permute-start(bf16[32,2048]{1,0:T(8,128)(2,1)S(1)} %get-tuple-element.58), channel_id=1, source_target_pairs={{0,12},{4,8},{8,4},{12,0},{1,13},{5,9},{9,5},{13,1},{2,14},{6,10},... | collective-permute-start | bytes 393224 | tf_op jit(solution)/shard_map/ppermute | solution.py:182
  38.6 0.6 collective-permute-start.7
  39.3 3.8 %collective-permute-done.9 = bf16[32,2048]{1,0:T(8,128)(2,1)S(1)} collective-permute-done((bf16[32,2048]{1,0:T(8,128)(2,1)S(1)}, bf16[32,2048]{1,0:T(8,128)(2,1)S(1)}, u32[]{:S(2)}, u32[]{:S(2)}) %collective-permute-start.9) | collective-permute-done | bytes 131104 | tf_op jit(solution)/shard_map/ppermute | solution.py:182
  43.1 6.7 %collective-permute-done.8 = bf16[32,2048]{1,0:T(8,128)(2,1)S(1)} collective-permute-done((bf16[32,2048]{1,0:T(8,128)(2,1)S(1)}, bf16[32,2048]{1,0:T(8,128)(2,1)S(1)}, u32[]{:S(2)}, u32[]{:S(2)}) %collective-permute-start.8) | collective-permute-done | bytes 131104 | tf_op jit(solution)/shard_map/ppermute | solution.py:182
  49.9 1.6 collective-permute-start.13
  52.1 4.1 %shard_map.114 = bf16[256,1792]{1,0:T(8,128)(2,1)S(1)} custom-call(bf16[256,2048]{1,0:T(8,128)(2,1)S(1)} %bitcast.146, bf16[2048,1792]{1,0:T(8,128)(2,1)} %weight.5), custom_call_target="tpu_custom_call" | custom-call | flops 1024 | bytes 1024 | tf_op jit(solution)/shard_map/pallas_call | solution.py:228
  56.4 7.9 %collective-permute-done.13 = bf16[4,32,2048]{2,1,0:T(8,128)(2,1)S(1)} collective-permute-done((bf16[4,32,2048]{2,1,0:T(8,128)(2,1)S(1)}, bf16[4,32,2048]{2,1,0:T(8,128)(2,1)S(1)}, u32[]{:S(2)}, u32[]{:S(2)}) %collective-permute-start.13) | collective-permute-done | bytes 524320 | tf_op jit(solution)/shard_map/ppermute | solution.py:182
  64.3 4.6 %collective-permute-done.11 = bf16[2,64,1792]{2,1,0:T(8,128)(2,1)S(1)} collective-permute-done((bf16[2,64,1792]{2,1,0:T(8,128)(2,1)S(1)}, bf16[2,64,1792]{2,1,0:T(8,128)(2,1)S(1)}, u32[]{:S(2)}, u32[]{:S(2)}) %collective-permute-start.11) | collective-permute-done | bytes 458784 | tf_op jit(solution)/shard_map/ppermute | solution.py:182
  69.0 1.5 collective-permute-start.12
  70.7 4.2 %shard_map.115 = bf16[256,1792]{1,0:T(8,128)(2,1)S(1)} custom-call(bf16[256,2048]{1,0:T(8,128)(2,1)S(1)} %bitcast.145, bf16[2048,1792]{1,0:T(8,128)(2,1)} %weight.5), custom_call_target="tpu_custom_call" | custom-call | flops 1024 | bytes 1024 | tf_op jit(solution)/shard_map/pallas_call | solution.py:228
  74.9 1.8 collective-permute-start.15
  76.8 5.0 %collective-permute-done.12 = bf16[64,1792]{1,0:T(8,128)(2,1)S(1)} collective-permute-done((bf16[64,1792]{1,0:T(8,128)(2,1)S(1)}, bf16[64,1792]{1,0:T(8,128)(2,1)S(1)}, u32[]{:S(2)}, u32[]{:S(2)}) %collective-permute-start.12) | collective-permute-done | bytes 229408 | tf_op jit(solution)/shard_map/ppermute | solution.py:182
  82.0 14.4 %collective-permute-done.15 = bf16[2,64,1792]{2,1,0:T(8,128)(2,1)S(1)} collective-permute-done((bf16[2,64,1792]{2,1,0:T(8,128)(2,1)S(1)}, bf16[2,64,1792]{2,1,0:T(8,128)(2,1)S(1)}, u32[]{:S(2)}, u32[]{:S(2)}) %collective-permute-start.15) | collective-permute-done | bytes 458784 | tf_op jit(solution)/shard_map/ppermute | solution.py:182
  96.4 0.7 fusion.16
  97.2 5.6 %convolution_convert_fusion.7 = bf16[128,2560]{1,0:T(8,128)(2,1)S(1)} fusion(bf16[1792,2560]{1,0:T(8,128)(2,1)} %param.17, f32[1792]{0:T(1024)S(1)} %copy-done.2, bf16[64,1792]{1,0:T(8,128)(2,1)S(1)} %collective-permute-done.17, bf16[64,1792]{1,0:T(8,128)(2,1)S(1)} %fusion.23), kind=kOutput, calls=%fused_computation.7 | convolution fusion | flops 1176109056 | bytes 10296320 | tf_op jit(solution)/shard_map/dot_general | solution.py:194
  103.0 1.4 convolution_convert_fusion.6
  105.3 1.5 collective-permute-done.18
  106.9 1.6 collective-permute-start.20
  108.5 9.3 %collective-permute-done.16 = bf16[64,1792]{1,0:T(8,128)(2,1)S(1)} collective-permute-done((bf16[64,1792]{1,0:T(8,128)(2,1)}, bf16[64,1792]{1,0:T(8,128)(2,1)S(1)}, u32[]{:S(2)}, u32[]{:S(2)}) %collective-permute-start.16) | collective-permute-done | bytes 229408 | tf_op jit(solution)/shard_map/ppermute | solution.py:182
  118.3 5.6 %collective-permute-done.19 = bf16[128,1792]{1,0:T(8,128)(2,1)S(1)} collective-permute-done((bf16[128,1792]{1,0:T(8,128)(2,1)S(1)}, bf16[128,1792]{1,0:T(8,128)(2,1)S(1)}, u32[]{:S(2)}, u32[]{:S(2)}) %collective-permute-start.19) | collective-permute-done | bytes 458784 | tf_op jit(solution)/shard_map/ppermute | solution.py:182
  123.8 7.5 %collective-permute-done.21 = bf16[64,1792]{1,0:T(8,128)(2,1)S(1)} collective-permute-done((bf16[64,1792]{1,0:T(8,128)(2,1)S(1)}, bf16[64,1792]{1,0:T(8,128)(2,1)S(1)}, u32[]{:S(2)}, u32[]{:S(2)}) %collective-permute-start.21) | collective-permute-done | bytes 229408 | tf_op jit(solution)/shard_map/ppermute | solution.py:182
  131.4 5.1 %convolution_convert_fusion.4 = bf16[128,2560]{1,0:T(8,128)(2,1)S(1)} fusion(bf16[1792,2560]{1,0:T(8,128)(2,1)} %param.18, bf16[128,1792]{1,0:T(8,128)(2,1)S(1)} %collective-permute-done.19, f32[1792]{0:T(1024)S(1)} %copy-done.2), kind=kOutput, calls=%fused_computation.4 | convolution fusion | flops 1175420928 | bytes 10296320 | tf_op jit(solution)/shard_map/dot_general | solution.py:194
  136.6 1.4 convolution_convert_fusion.5
  138.7 0.6 collective-permute-start.25
  139.3 1.2 collective-permute-done.25
  140.6 1.5 collective-permute-start.26
  142.4 1.4 convolution_convert_fusion.2
  143.8 1.4 convolution_convert_fusion.3
  145.3 0.6 collective-permute-start.28
  146.0 0.6 collective-permute-start.23
  146.6 5.2 %collective-permute-done.27 = bf16[128,1792]{1,0:T(8,128)(2,1)S(1)} collective-permute-done((bf16[128,1792]{1,0:T(8,128)(2,1)S(1)}, bf16[128,1792]{1,0:T(8,128)(2,1)S(1)}, u32[]{:S(2)}, u32[]{:S(2)}) %collective-permute-start.27) | collective-permute-done | bytes 458784 | tf_op jit(solution)/shard_map/ppermute | solution.py:182
  151.8 10.1 %collective-permute-done.28 = bf16[128,2560]{1,0:T(8,128)(2,1)S(1)} collective-permute-done((bf16[128,2560]{1,0:T(8,128)(2,1)S(1)}, bf16[128,2560]{1,0:T(8,128)(2,1)S(1)}, u32[]{:S(2)}, u32[]{:S(2)}) %collective-permute-start.28) | collective-permute-done | bytes 655392 | tf_op jit(solution)/shard_map/ppermute | solution.py:182
  162.0 1.4 convolution_convert_fusion
  163.4 1.4 convolution_convert_fusion.1
  165.1 0.5 collective-permute-start.29
  166.5 0.8 collective-permute-done.29
  168.3 0.5 collective-permute-start.31
  168.9 1.2 collective-permute-done.32
  170.2 4.8 %shard_map.116 = bf16[256,1792]{1,0:T(8,128)(2,1)S(1)} custom-call(bf16[256,2560]{1,0:T(8,128)(2,1)S(1)} %pad_maximum_fusion.rows, bf16[2560,1792]{1,0:T(8,128)(2,1)} %weight.7), custom_call_target="tpu_custom_call" | custom-call | flops 1024 | bytes 1024 | tf_op jit(solution)/shard_map/pallas_call | solution.py:228
  174.9 0.8 slice_bitcast_fusion.2
  176.2 8.9 %collective-permute-done.31 = bf16[128,2560]{1,0:T(8,128)(2,1)S(1)} collective-permute-done((bf16[128,2560]{1,0:T(8,128)(2,1)S(1)}, bf16[128,2560]{1,0:T(8,128)(2,1)S(1)}, u32[]{:S(2)}, u32[]{:S(2)}) %collective-permute-start.31) | collective-permute-done | bytes 655392 | tf_op jit(solution)/shard_map/ppermute | solution.py:182
  185.1 3.7 %collective-permute-done.34 = bf16[2,64,1792]{2,1,0:T(8,128)(2,1)} collective-permute-done((bf16[2,64,1792]{2,1,0:T(8,128)(2,1)}, bf16[2,64,1792]{2,1,0:T(8,128)(2,1)}, u32[]{:S(2)}, u32[]{:S(2)}) %collective-permute-start.34) | collective-permute-done | bytes 458784 | tf_op jit(solution)/shard_map/ppermute | solution.py:182
  188.8 1.1 convert_add_fusion.3
  190.1 4.8 %shard_map.117 = bf16[256,1792]{1,0:T(8,128)(2,1)S(1)} custom-call(bf16[256,2560]{1,0:T(8,128)(2,1)S(1)} %pad_maximum_fusion.1.rows, bf16[2560,1792]{1,0:T(8,128)(2,1)} %weight.7), custom_call_target="tpu_custom_call" | custom-call | flops 1024 | bytes 1024 | tf_op jit(solution)/shard_map/pallas_call | solution.py:228
  195.5 0.6 collective-permute-start.37
  196.1 15.8 %collective-permute-done.35 = bf16[2,64,1792]{2,1,0:T(8,128)(2,1)S(1)} collective-permute-done((bf16[2,64,1792]{2,1,0:T(8,128)(2,1)S(1)}, bf16[2,64,1792]{2,1,0:T(8,128)(2,1)S(1)}, u32[]{:S(2)}, u32[]{:S(2)}) %collective-permute-start.35) | collective-permute-done | bytes 458784 | tf_op jit(solution)/shard_map/ppermute | solution.py:182
  212.0 0.7 fusion.37
  212.7 11.4 %collective-permute-done.36 = bf16[64,1792]{1,0:T(8,128)(2,1)S(1)} collective-permute-done((bf16[64,1792]{1,0:T(8,128)(2,1)}, bf16[64,1792]{1,0:T(8,128)(2,1)S(1)}, u32[]{:S(2)}, u32[]{:S(2)}) %collective-permute-start.36) | collective-permute-done | bytes 229408 | tf_op jit(solution)/shard_map/ppermute | solution.py:182
  224.3 0.8 pad_maximum_fusion.14
  225.1 0.8 pad_maximum_fusion.12
  (141 shorter events, 9.7 us)
Async XLA Ops:
  1.6 17.0 %copy-start.1 = (bf16[512,2048]{1,0:T(8,128)(2,1)S(1)}, bf16[512,2048]{1,0:T(8,128)(2,1)}, u32[]{:S(2)}) copy-start(bf16[512,2048]{1,0:T(8,128)(2,1)} %value_weight.1) | copy-start | bytes 6291460
  4.8 10.9 %collective-permute-start.1 = (bf16[288,128]{1,0:T(8,128)(2,1)S(1)}, bf16[288,128]{1,0:T(8,128)(2,1)S(1)}, u32[]{:S(2)}, u32[]{:S(2)}) collective-permute-start(bf16[288,128]{1,0:T(8,128)(2,1)S(1)} %fusion.39), channel_id=1, source_target_pairs={{0,8},{4,12},{1,9},{5,13},{2,10},{6,14},{3,11},{7,15},{16,24},{20,... | collective-permute-start | bytes 221192 | tf_op jit(solution)/shard_map/ppermute | solution.py:255
  10.8 4.9 %collective-permute-start = (bf16[288,128]{1,0:T(8,128)(2,1)S(1)}, bf16[288,128]{1,0:T(8,128)(2,1)S(1)}, u32[]{:S(2)}, u32[]{:S(2)}) collective-permute-start(bf16[288,128]{1,0:T(8,128)(2,1)S(1)} %fusion.39), channel_id=1, source_target_pairs={{0,12},{1,13},{2,14},{3,15},{16,28},{17,29},{18,30},{19,31}} | collective-permute-start | bytes 221192 | tf_op jit(solution)/shard_map/ppermute | solution.py:255
  13.1 3.8 %collective-permute-start.2 = (bf16[288,128]{1,0:T(8,128)(2,1)S(1)}, bf16[288,128]{1,0:T(8,128)(2,1)S(1)}, u32[]{:S(2)}, u32[]{:S(2)}) collective-permute-start(bf16[288,128]{1,0:T(8,128)(2,1)S(1)} %fusion.39), channel_id=1, source_target_pairs={{0,4},{4,8},{8,12},{1,5},{5,9},{9,13},{2,6},{6,10},{10,14},{3,7},{... | collective-permute-start | bytes 221192 | tf_op jit(solution)/shard_map/ppermute | solution.py:255
  16.9 1.7 copy-start
  16.9 1.5 collective-permute-start.3
  25.5 5.5 %collective-permute-start.6 = (bf16[32,2048]{1,0:T(8,128)(2,1)S(1)}, bf16[32,2048]{1,0:T(8,128)(2,1)S(1)}, u32[]{:S(2)}, u32[]{:S(2)}) collective-permute-start(bf16[32,2048]{1,0:T(8,128)(2,1)S(1)} %get-tuple-element.62), channel_id=1, source_target_pairs={{0,3},{1,2},{2,1},{3,0},{4,7},{5,6},{6,5},{7,4},{8,11},{9,10},{10,... | collective-permute-start | bytes 393224 | tf_op jit(solution)/shard_map/ppermute | solution.py:182
  26.8 7.4 %collective-permute-start.5 = (bf16[32,2048]{1,0:T(8,128)(2,1)S(1)}, bf16[32,2048]{1,0:T(8,128)(2,1)S(1)}, u32[]{:S(2)}, u32[]{:S(2)}) collective-permute-start(bf16[32,2048]{1,0:T(8,128)(2,1)S(1)} %get-tuple-element.63), channel_id=1, source_target_pairs={{0,2},{1,3},{2,0},{3,1},{4,6},{5,7},{6,4},{7,5},{8,10},{9,11},{10,... | collective-permute-start | bytes 393224 | tf_op jit(solution)/shard_map/ppermute | solution.py:182
  27.3 6.8 %collective-permute-start.4 = (bf16[32,2048]{1,0:T(8,128)(2,1)S(1)}, bf16[32,2048]{1,0:T(8,128)(2,1)S(1)}, u32[]{:S(2)}, u32[]{:S(2)}) collective-permute-start(bf16[32,2048]{1,0:T(8,128)(2,1)S(1)} %get-tuple-element.64), channel_id=1, source_target_pairs={{0,1},{1,0},{2,3},{3,2},{4,5},{5,4},{6,7},{7,6},{8,9},{9,8},{10,11... | collective-permute-start | bytes 393224 | tf_op jit(solution)/shard_map/ppermute | solution.py:182
  34.3 8.8 %collective-permute-start.9 = (bf16[32,2048]{1,0:T(8,128)(2,1)S(1)}, bf16[32,2048]{1,0:T(8,128)(2,1)S(1)}, u32[]{:S(2)}, u32[]{:S(2)}) collective-permute-start(bf16[32,2048]{1,0:T(8,128)(2,1)S(1)} %get-tuple-element.58), channel_id=1, source_target_pairs={{0,12},{4,8},{8,4},{12,0},{1,13},{5,9},{9,5},{13,1},{2,14},{6,10},... | collective-permute-start | bytes 393224 | tf_op jit(solution)/shard_map/ppermute | solution.py:182
  38.6 11.2 %collective-permute-start.8 = (bf16[32,2048]{1,0:T(8,128)(2,1)S(1)}, bf16[32,2048]{1,0:T(8,128)(2,1)S(1)}, u32[]{:S(2)}, u32[]{:S(2)}) collective-permute-start(bf16[32,2048]{1,0:T(8,128)(2,1)S(1)} %get-tuple-element.59), channel_id=1, source_target_pairs={{0,8},{4,12},{8,0},{12,4},{1,9},{5,13},{9,1},{13,5},{2,10},{6,14},... | collective-permute-start | bytes 393224 | tf_op jit(solution)/shard_map/ppermute | solution.py:182
  38.6 11.2 %collective-permute-start.7 = (bf16[32,2048]{1,0:T(8,128)(2,1)S(1)}, bf16[32,2048]{1,0:T(8,128)(2,1)S(1)}, u32[]{:S(2)}, u32[]{:S(2)}) collective-permute-start(bf16[32,2048]{1,0:T(8,128)(2,1)S(1)} %get-tuple-element.60), channel_id=1, source_target_pairs={{0,4},{4,0},{8,12},{12,8},{1,5},{5,1},{9,13},{13,9},{2,6},{6,2},{1... | collective-permute-start | bytes 393224 | tf_op jit(solution)/shard_map/ppermute | solution.py:182
  49.9 2.0 collective-permute-start.10
  49.9 14.3 %collective-permute-start.13 = (bf16[4,32,2048]{2,1,0:T(8,128)(2,1)S(1)}, bf16[4,32,2048]{2,1,0:T(8,128)(2,1)S(1)}, u32[]{:S(2)}, u32[]{:S(2)}) collective-permute-start(bf16[4,32,2048]{2,1,0:T(8,128)(2,1)S(1)} %pad_maximum_fusion.10), channel_id=1, source_target_pairs={{0,2},{1,3},{2,0},{3,1},{4,6},{5,7},{6,4},{7,5},{8,10},{9,11},{10,... | collective-permute-start | bytes 1572872 | tf_op jit(solution)/shard_map/ppermute | solution.py:182
  56.3 12.6 %collective-permute-start.11 = (bf16[2,64,1792]{2,1,0:T(8,128)(2,1)S(1)}, bf16[2,64,1792]{2,1,0:T(8,128)(2,1)S(1)}, u32[]{:S(2)}, u32[]{:S(2)}) collective-permute-start(bf16[2,64,1792]{2,1,0:T(8,128)(2,1)S(1)} %slice_bitcast_fusion.5), channel_id=1, source_target_pairs={{0,4},{4,0},{8,12},{12,8},{1,5},{5,1},{9,13},{13,9},{2,6},{6,2},{1... | collective-permute-start | bytes 1376264 | tf_op jit(solution)/shard_map/ppermute | solution.py:182
  64.3 6.2 %collective-permute-start.14 = (bf16[4,32,2048]{2,1,0:T(8,128)(2,1)S(1)}, bf16[4,32,2048]{2,1,0:T(8,128)(2,1)S(1)}, u32[]{:S(2)}, u32[]{:S(2)}) collective-permute-start(bf16[4,32,2048]{2,1,0:T(8,128)(2,1)S(1)} %collective-permute-done.13), channel_id=1, source_target_pairs={{0,1},{1,0},{2,3},{3,2},{4,5},{5,4},{6,7},{7,6},{8,9},{9,8},{10,11... | collective-permute-start | bytes 1572872 | tf_op jit(solution)/shard_map/ppermute | solution.py:182
  69.0 12.8 %collective-permute-start.12 = (bf16[64,1792]{1,0:T(8,128)(2,1)S(1)}, bf16[64,1792]{1,0:T(8,128)(2,1)S(1)}, u32[]{:S(2)}, u32[]{:S(2)}) collective-permute-start(bf16[64,1792]{1,0:T(8,128)(2,1)S(1)} %fusion.20), channel_id=1, source_target_pairs={{0,8},{4,12},{8,0},{12,4},{1,9},{5,13},{9,1},{13,5},{2,10},{6,14},... | collective-permute-start | bytes 688136 | tf_op jit(solution)/shard_map/ppermute | solution.py:182
  70.7 11.1 %copy-start.3 = (bf16[128,1792]{1,0:T(8,128)(2,1)S(1)}, bf16[128,1792]{1,0:T(8,128)(2,1)}, u32[]{:S(2)}) copy-start(bf16[128,1792]{1,0:T(8,128)(2,1)} %param.10) | copy-start | bytes 1376260
  74.9 22.3 %copy-start.2 = (f32[1792]{0:T(1024)S(1)}, f32[1792]{0:T(1024)}, u32[]{:S(2)}) copy-start(f32[1792]{0:T(1024)} %param.16) | copy-start | bytes 21508
  74.9 21.5 %collective-permute-start.15 = (bf16[2,64,1792]{2,1,0:T(8,128)(2,1)S(1)}, bf16[2,64,1792]{2,1,0:T(8,128)(2,1)S(1)}, u32[]{:S(2)}, u32[]{:S(2)}) collective-permute-start(bf16[2,64,1792]{2,1,0:T(8,128)(2,1)S(1)} %slice_bitcast_fusion.4), channel_id=1, source_target_pairs={{0,4},{4,0},{8,12},{12,8},{1,5},{5,1},{9,13},{13,9},{2,6},{6,2},{1... | collective-permute-start | bytes 1376264 | tf_op jit(solution)/shard_map/ppermute | solution.py:182
  81.9 15.3 %collective-permute-start.17 = (bf16[64,1792]{1,0:T(8,128)(2,1)S(1)}, bf16[64,1792]{1,0:T(8,128)(2,1)S(1)}, u32[]{:S(2)}, u32[]{:S(2)}) collective-permute-start(bf16[64,1792]{1,0:T(8,128)(2,1)S(1)} %fusion.23), channel_id=1, source_target_pairs={{0,8},{4,12},{8,0},{12,4},{1,9},{5,13},{9,1},{13,5},{2,10},{6,14},... | collective-permute-start | bytes 688136 | tf_op jit(solution)/shard_map/ppermute | solution.py:182
  96.4 6.4 %copy-start.5 = (bf16[2,64,1792]{2,1,0:T(8,128)(2,1)}, bf16[2,64,1792]{2,1,0:T(8,128)(2,1)S(1)}, u32[]{:S(2)}) copy-start(bf16[2,64,1792]{2,1,0:T(8,128)(2,1)S(1)} %collective-permute-done.15) | copy-start | bytes 1376260
  96.4 6.4 %slice-start = ((s8[9175040]{0:T(1024)(128)(4,1)}), s8[4194304]{0:T(1024)(128)(4,1)S(1)}, s32[]{:S(2)}) async-start(s8[9175040]{0:T(1024)(128)(4,1)} %bitcast.158), calls=%async_computation | async-start | bytes 8388608
  97.2 5.7 %slice-start.1 = ((s8[9175040]{0:T(1024)(128)(4,1)}), s8[4194304]{0:T(1024)(128)(4,1)S(1)}, s32[]{:S(2)}) async-start(s8[9175040]{0:T(1024)(128)(4,1)} %bitcast.158), calls=%async_computation.1 | async-start | bytes 8388608
  97.2 5.8 %slice-start.2 = ((s8[9175040]{0:T(1024)(128)(4,1)}), s8[786432]{0:T(1024)(128)(4,1)S(1)}, s32[]{:S(2)}) async-start(s8[9175040]{0:T(1024)(128)(4,1)} %bitcast.158), calls=%async_computation.2 | async-start | bytes 1572864
  104.6 2.2 collective-permute-start.18
  104.7 13.1 %copy-start.4 = (bf16[128,1792]{1,0:T(8,128)(2,1)S(1)}, bf16[128,1792]{1,0:T(8,128)(2,1)}, u32[]{:S(2)}) copy-start(bf16[128,1792]{1,0:T(8,128)(2,1)} %param.10) | copy-start | bytes 1376260
  104.7 13.1 %copy-start.6 = (bf16[2,64,1792]{2,1,0:T(8,128)(2,1)S(1)}, bf16[2,64,1792]{2,1,0:T(8,128)(2,1)}, u32[]{:S(2)}) copy-start(bf16[2,64,1792]{2,1,0:T(8,128)(2,1)} %copy-done.5) | copy-start | bytes 1376260
  104.7 13.1 %collective-permute-start.16 = (bf16[64,1792]{1,0:T(8,128)(2,1)}, bf16[64,1792]{1,0:T(8,128)(2,1)S(1)}, u32[]{:S(2)}, u32[]{:S(2)}) collective-permute-start(bf16[64,1792]{1,0:T(8,128)(2,1)} %fusion.16), channel_id=1, source_target_pairs={{0,8},{4,12},{8,0},{12,4},{1,9},{5,13},{9,1},{13,5},{2,10},{6,14},... | collective-permute-start | bytes 688136 | tf_op jit(solution)/shard_map/ppermute | solution.py:182
  104.8 19.0 %collective-permute-start.19 = (bf16[128,1792]{1,0:T(8,128)(2,1)S(1)}, bf16[128,1792]{1,0:T(8,128)(2,1)S(1)}, u32[]{:S(2)}, u32[]{:S(2)}) collective-permute-start(bf16[128,1792]{1,0:T(8,128)(2,1)S(1)} %pad_maximum_fusion.11), channel_id=1, source_target_pairs={{0,4},{4,0},{8,12},{12,8},{1,5},{5,1},{9,13},{13,9},{2,6},{6,2},{1... | collective-permute-start | bytes 1376264 | tf_op jit(solution)/shard_map/ppermute | solution.py:182
  106.9 24.5 %collective-permute-start.20 = (bf16[128,2560]{1,0:T(8,128)(2,1)S(1)}, bf16[128,2560]{1,0:T(8,128)(2,1)S(1)}, u32[]{:S(2)}, u32[]{:S(2)}) collective-permute-start(bf16[128,2560]{1,0:T(8,128)(2,1)S(1)} %add_convert_fusion.1), channel_id=1, source_target_pairs={{0,2},{1,3},{2,0},{3,1},{4,6},{5,7},{6,4},{7,5},{8,10},{9,11},{10,... | collective-permute-start | bytes 1966088 | tf_op jit(solution)/shard_map/ppermute | solution.py:182
  118.0 13.4 %collective-permute-start.21 = (bf16[64,1792]{1,0:T(8,128)(2,1)S(1)}, bf16[64,1792]{1,0:T(8,128)(2,1)S(1)}, u32[]{:S(2)}, u32[]{:S(2)}) collective-permute-start(bf16[64,1792]{1,0:T(8,128)(2,1)S(1)} %get-tuple-element.36), channel_id=1, source_target_pairs={{0,8},{4,12},{8,0},{12,4},{1,9},{5,13},{9,1},{13,5},{2,10},{6,14},... | collective-permute-start | bytes 688136 | tf_op jit(solution)/shard_map/ppermute | solution.py:182
  118.1 18.5 %slice-start.6 = ((s8[9175040]{0:T(1024)(128)(4,1)}), s8[4194304]{0:T(1024)(128)(4,1)S(1)}, s32[]{:S(2)}) async-start(s8[9175040]{0:T(1024)(128)(4,1)} %bitcast.162), calls=%async_computation.6 | async-start | bytes 8388608
  118.3 18.3 %slice-start.7 = ((s8[9175040]{0:T(1024)(128)(4,1)}), s8[4194304]{0:T(1024)(128)(4,1)S(1)}, s32[]{:S(2)}) async-start(s8[9175040]{0:T(1024)(128)(4,1)} %bitcast.162), calls=%async_computation.7 | async-start | bytes 8388608
  118.3 18.3 %slice-start.8 = ((s8[9175040]{0:T(1024)(128)(4,1)}), s8[786432]{0:T(1024)(128)(4,1)S(1)}, s32[]{:S(2)}) async-start(s8[9175040]{0:T(1024)(128)(4,1)} %bitcast.162), calls=%async_computation.8 | async-start | bytes 1572864
  131.4 11.0 %slice-start.3 = ((s8[9175040]{0:T(1024)(128)(4,1)}), s8[4194304]{0:T(1024)(128)(4,1)S(1)}, s32[]{:S(2)}) async-start(s8[9175040]{0:T(1024)(128)(4,1)} %bitcast.160), calls=%async_computation.3 | async-start | bytes 8388608
  131.4 11.0 %slice-start.4 = ((s8[9175040]{0:T(1024)(128)(4,1)}), s8[4194304]{0:T(1024)(128)(4,1)S(1)}, s32[]{:S(2)}) async-start(s8[9175040]{0:T(1024)(128)(4,1)} %bitcast.160), calls=%async_computation.4 | async-start | bytes 8388608
  136.6 5.9 %slice-start.5 = ((s8[9175040]{0:T(1024)(128)(4,1)}), s8[786432]{0:T(1024)(128)(4,1)S(1)}, s32[]{:S(2)}) async-start(s8[9175040]{0:T(1024)(128)(4,1)} %bitcast.160), calls=%async_computation.5 | async-start | bytes 1572864
  138.4 3.7 %collective-permute-start.22 = (bf16[128,2560]{1,0:T(8,128)(2,1)S(1)}, bf16[128,2560]{1,0:T(8,128)(2,1)S(1)}, u32[]{:S(2)}, u32[]{:S(2)}) collective-permute-start(bf16[128,2560]{1,0:T(8,128)(2,1)S(1)} %pad_maximum_fusion.5), channel_id=1, source_target_pairs={{0,1},{1,0},{2,3},{3,2},{4,5},{5,4},{6,7},{7,6},{8,9},{9,8},{10,11... | collective-permute-start | bytes 1966088 | tf_op jit(solution)/shard_map/ppermute | solution.py:182
  138.7 1.9 collective-permute-start.25
  139.2 12.5 %collective-permute-start.27 = (bf16[128,1792]{1,0:T(8,128)(2,1)S(1)}, bf16[128,1792]{1,0:T(8,128)(2,1)S(1)}, u32[]{:S(2)}, u32[]{:S(2)}) collective-permute-start(bf16[128,1792]{1,0:T(8,128)(2,1)S(1)} %pad_maximum_fusion.13), channel_id=1, source_target_pairs={{0,4},{4,0},{8,12},{12,8},{1,5},{5,1},{9,13},{13,9},{2,6},{6,2},{1... | collective-permute-start | bytes 1376264 | tf_op jit(solution)/shard_map/ppermute | solution.py:182
  140.6 25.2 %collective-permute-start.26 = (f32[256]{0:T(256)S(1)}, f32[256]{0:T(256)S(1)}, u32[]{:S(2)}, u32[]{:S(2)}) collective-permute-start(f32[256]{0:T(256)S(1)} %fusion.49), channel_id=1, source_target_pairs={{0,2},{1,3},{2,0},{3,1},{4,6},{5,7},{6,4},{7,5},{8,10},{9,11},{10,... | collective-permute-start | bytes 3080 | tf_op jit(solution)/shard_map/ppermute | solution.py:182
  145.3 16.6 %collective-permute-start.28 = (bf16[128,2560]{1,0:T(8,128)(2,1)S(1)}, bf16[128,2560]{1,0:T(8,128)(2,1)S(1)}, u32[]{:S(2)}, u32[]{:S(2)}) collective-permute-start(bf16[128,2560]{1,0:T(8,128)(2,1)S(1)} %add_convert_fusion), channel_id=1, source_target_pairs={{0,2},{1,3},{2,0},{3,1},{4,6},{5,7},{6,4},{7,5},{8,10},{9,11},{10,... | collective-permute-start | bytes 1966088 | tf_op jit(solution)/shard_map/ppermute | solution.py:182
  145.9 20.0 %collective-permute-start.24 = (f32[128]{0:T(128)S(1)}, f32[128]{0:T(128)S(1)}, u32[]{:S(2)}, u32[]{:S(2)}) collective-permute-start(f32[128]{0:T(128)S(1)} %fusion.5), channel_id=1, source_target_pairs={{0,1},{1,0},{2,3},{3,2},{4,5},{5,4},{6,7},{7,6},{8,9},{9,8},{10,11... | collective-permute-start | bytes 1544 | tf_op jit(solution)/shard_map/ppermute | solution.py:182
  146.0 19.6 %collective-permute-start.23 = (bf16[128,2560]{1,0:T(8,128)(2,1)S(1)}, bf16[128,2560]{1,0:T(8,128)(2,1)S(1)}, u32[]{:S(2)}, u32[]{:S(2)}) collective-permute-start(bf16[128,2560]{1,0:T(8,128)(2,1)S(1)} %pad_maximum_fusion.6), channel_id=1, source_target_pairs={{0,1},{1,0},{2,3},{3,2},{4,5},{5,4},{6,7},{7,6},{8,9},{9,8},{10,11... | collective-permute-start | bytes 1966088 | tf_op jit(solution)/shard_map/ppermute | solution.py:182
  164.8 1.2 collective-permute-start.30
  165.1 2.3 %collective-permute-start.29 = (bf16[128,2560]{1,0:T(8,128)(2,1)S(1)}, bf16[128,2560]{1,0:T(8,128)(2,1)S(1)}, u32[]{:S(2)}, u32[]{:S(2)}) collective-permute-start(bf16[128,2560]{1,0:T(8,128)(2,1)S(1)} %pad_maximum_fusion.7), channel_id=1, source_target_pairs={{0,1},{1,0},{2,3},{3,2},{4,5},{5,4},{6,7},{7,6},{8,9},{9,8},{10,11... | collective-permute-start | bytes 1966088 | tf_op jit(solution)/shard_map/ppermute | solution.py:182
  167.9 2.2 collective-permute-start.32
  168.3 16.8 %collective-permute-start.31 = (bf16[128,2560]{1,0:T(8,128)(2,1)S(1)}, bf16[128,2560]{1,0:T(8,128)(2,1)S(1)}, u32[]{:S(2)}, u32[]{:S(2)}) collective-permute-start(bf16[128,2560]{1,0:T(8,128)(2,1)S(1)} %pad_maximum_fusion.8), channel_id=1, source_target_pairs={{0,2},{1,3},{2,0},{3,1},{4,6},{5,7},{6,4},{7,5},{8,10},{9,11},{10,... | collective-permute-start | bytes 1966088 | tf_op jit(solution)/shard_map/ppermute | solution.py:182
  175.7 13.1 %collective-permute-start.34 = (bf16[2,64,1792]{2,1,0:T(8,128)(2,1)}, bf16[2,64,1792]{2,1,0:T(8,128)(2,1)}, u32[]{:S(2)}, u32[]{:S(2)}) collective-permute-start(bf16[2,64,1792]{2,1,0:T(8,128)(2,1)} %slice_bitcast_fusion.2), channel_id=1, source_target_pairs={{0,4},{4,0},{8,12},{12,8},{1,5},{5,1},{9,13},{13,9},{2,6},{6,2},{1... | collective-permute-start | bytes 1376264 | tf_op jit(solution)/shard_map/ppermute | solution.py:182
  185.1 4.9 %collective-permute-start.33 = (bf16[128,2560]{1,0:T(8,128)(2,1)S(1)}, bf16[128,2560]{1,0:T(8,128)(2,1)S(1)}, u32[]{:S(2)}, u32[]{:S(2)}) collective-permute-start(bf16[128,2560]{1,0:T(8,128)(2,1)S(1)} %collective-permute-done.31), channel_id=1, source_target_pairs={{0,1},{1,0},{2,3},{3,2},{4,5},{5,4},{6,7},{7,6},{8,9},{9,8},{10,11... | collective-permute-start | bytes 1966088 | tf_op jit(solution)/shard_map/ppermute | solution.py:182
  194.9 17.0 %collective-permute-start.35 = (bf16[2,64,1792]{2,1,0:T(8,128)(2,1)S(1)}, bf16[2,64,1792]{2,1,0:T(8,128)(2,1)S(1)}, u32[]{:S(2)}, u32[]{:S(2)}) collective-permute-start(bf16[2,64,1792]{2,1,0:T(8,128)(2,1)S(1)} %slice_bitcast_fusion), channel_id=1, source_target_pairs={{0,4},{4,0},{8,12},{12,8},{1,5},{5,1},{9,13},{13,9},{2,6},{6,2},{1... | collective-permute-start | bytes 1376264 | tf_op jit(solution)/shard_map/ppermute | solution.py:182
  195.5 17.2 %collective-permute-start.37 = (bf16[64,1792]{1,0:T(8,128)(2,1)S(1)}, bf16[64,1792]{1,0:T(8,128)(2,1)S(1)}, u32[]{:S(2)}, u32[]{:S(2)}) collective-permute-start(bf16[64,1792]{1,0:T(8,128)(2,1)S(1)} %fusion.36), channel_id=1, source_target_pairs={{0,8},{4,12},{8,0},{12,4},{1,9},{5,13},{9,1},{13,5},{2,10},{6,14},... | collective-permute-start | bytes 688136 | tf_op jit(solution)/shard_map/ppermute | solution.py:182
  212.7 11.4 %collective-permute-start.36 = (bf16[64,1792]{1,0:T(8,128)(2,1)}, bf16[64,1792]{1,0:T(8,128)(2,1)S(1)}, u32[]{:S(2)}, u32[]{:S(2)}) collective-permute-start(bf16[64,1792]{1,0:T(8,128)(2,1)} %fusion.37), channel_id=1, source_target_pairs={{0,8},{4,12},{8,0},{12,4},{1,9},{5,13},{9,1},{13,5},{2,10},{6,14},... | collective-permute-start | bytes 688136 | tf_op jit(solution)/shard_map/ppermute | solution.py:182

commit v11 on v10

--- a/solution.py
+++ b/solution.py
@@ -247,10 +247,10 @@
     return lax.optimization_barrier((value, earlier))[0]
 
 
-def gather_keys(rotated_keys, n_ctx):
-    rows = rotated_keys.shape[0] // 2
+def gather_keys(latent, n_ctx):
+    rows = latent.shape[0] // 2
     core = lax.axis_index("tp") & 1
-    half = lax.dynamic_slice_in_dim(rotated_keys, core * rows, rows, 0)
+    half = lax.dynamic_slice_in_dim(latent, core * rows, rows, 0)
     came = [
         lax.ppermute(half, "ctx", [(c, c + d) for c in range(n_ctx - d)])
         for d in range(n_ctx - 1, 0, -1)
@@ -260,7 +260,7 @@
     before = jnp.concatenate(
         [jnp.where(core == 0, mine, other), jnp.where(core == 0, other, mine)], axis=0
     )
-    return jnp.concatenate([before, rotated_keys], axis=1)
+    return jnp.concatenate([before, latent], axis=1)
 
 
 def spread_heads(heads_out, n_ctx, n_tp):
@@ -306,9 +306,13 @@
     def attend(mine, came, which):
         return (wide(pick(residual_halves, which)) + mine + wide(came)).astype(jnp.bfloat16)
 
-    def gate_up(rows):
+    def scale(rows):
         values = wide(rows)
         scaled = (values * norm_gain[None, :]).astype(jnp.bfloat16)
+        return jnp.sum(values * values, axis=1), scaled
+
+    def gate_up(rows):
+        squares, scaled = scale(rows)
         terms = [matmul(scaled, gate_weight), matmul(scaled, up_weight)]
 
         def side(which):
@@ -316,7 +320,7 @@
                 [lax.dynamic_slice_in_dim(term, which * half, half, 0) for term in terms], axis=0
             )
 
-        return side(core), side(1 - core), jnp.sum(values * values, axis=1)
+        return side(core), side(1 - core), squares
 
     def chip_sum(kept, sent):
         return wide(kept) + wide(swap(sent, "tp", 1))
@@ -328,43 +332,55 @@
     kept_b, sent_b, came_b = first_hop(core_rows(far, after(far_near, other_a)))
     attended_a = attend(mine_a, after(last_a, sent_b), first_half)
     twin_a = swap(attended_a, "ctx", 2)
-    mine_b, other_b, last_b = second_hop(kept_b, after(came_b, attended_a))
-    pair_a = jnp.concatenate([attended_a, after(twin_a, other_b)], axis=0)
+    pair_a = jnp.concatenate([attended_a, twin_a], axis=0)
     rest_a = swap(pair_a, "ctx", 1)
-    kept, sent, squares_p = gate_up(pair_a)
-    sums_p = chip_sum(kept, sent).astype(jnp.bfloat16)
-    across_p = swap(sums_p, "tp", 2)
-    attended_b = attend(mine_b, after(last_b, sums_p), 1 - first_half)
+    mine_b, other_b, last_b = second_hop(kept_b, after(came_b, pair_a))
+    rest_a, last_b = lax.optimization_barrier((rest_a, last_b))
+    attended_b = attend(mine_b, last_b, 1 - first_half)
     twin_b = swap(attended_b, "ctx", 2)
-    rest_a, across_p, twin_b = lax.optimization_barrier((rest_a, across_p, twin_b))
-    kept, sent, squares_q = gate_up(rest_a)
-    sums_q = chip_sum(kept, sent).astype(jnp.bfloat16)
-    across_q = swap(sums_q, "tp", 2)
-    squares_a = jnp.concatenate([squares_p, squares_q])
+    all_a = jnp.concatenate([pair_a, rest_a], axis=0)
+    squares_a, scaled = scale(all_a)
+
+    def cross(rows, weight):
+        term = matmul(rows, weight).reshape(2, 2, half, -1)
+
+        def side(which):
+            return lax.dynamic_index_in_dim(term, which, 1, keepdims=False).reshape(2 * half, -1)
+
+        sent = side(1 - core)
+        total = chip_sum(side(core), sent).astype(jnp.bfloat16)
+        return sent, total, swap(total, "tp", 2)
+
+    sent_gate, _, across_gate = cross(scaled, gate_weight)
+    _, sums_up, across_up = cross(after(scaled, sent_gate), up_weight)
     across_squares = swap(squares_a + swap(squares_a, "tp", 1), "tp", 2)
-    pair_b = jnp.concatenate([attended_b, twin_b], axis=0)
+    pair_b = jnp.concatenate([attended_b, after(twin_b, across_gate)], axis=0)
     rest_b = swap(pair_b, "ctx", 1)
 
-    def hide(chip_terms, squares, across, across_squares):
+    def hide(chip_terms, squares, across_gate, across_up, across_squares):
         squares = squares + swap(squares, "tp", 1) + across_squares
         squares = lax.dynamic_slice_in_dim(squares, core * half, half, 0)
         inverse_rms = lax.rsqrt(squares / model_width + norm_eps)[:, None]
-        gate = (chip_terms[:half] + wide(across[:half])) * inverse_rms
-        up = (chip_terms[half:] + wide(across[half:])) * inverse_rms
+        gate = (chip_terms[:half] + wide(across_gate)) * inverse_rms
+        up = (chip_terms[half:] + wide(across_up)) * inverse_rms
         return (jax.nn.silu(gate) * up).astype(jnp.bfloat16)
 
-    kept, sent, squares_p = gate_up(after(pair_b, sums_q))
+    kept, sent, squares_p = gate_up(after(pair_b, sums_up))
     terms_p = chip_sum(kept, sent)
-    rest_b, across_q, _ = lax.optimization_barrier((rest_b, across_q, sent))
+    rest_b, across_up, _ = lax.optimization_barrier((rest_b, across_up, sent))
     kept, sent, squares_q = gate_up(rest_b)
     terms_q = chip_sum(kept, sent)
-    hidden = jnp.concatenate(
-        [
-            hide(terms_p, squares_p, across_p, across_squares[: 2 * half]),
-            hide(terms_q, squares_q, across_q, across_squares[2 * half :]),
-        ],
-        axis=0,
-    )
+    parts = [
+        hide(
+            terms,
+            squares,
+            across_gate[i * half : (i + 1) * half],
+            across_up[i * half : (i + 1) * half],
+            across_squares[2 * i * half : 2 * (i + 1) * half],
+        )
+        for i, (terms, squares) in enumerate(((terms_p, squares_p), (terms_q, squares_q)))
+    ]
+    hidden = jnp.concatenate(parts, axis=0)
     hidden_near = swap(hidden, "tp", 1)
     hidden_far = swap(hidden, "tp", 2)
 
@@ -378,19 +394,20 @@
         other = pick(pair, 1 - core).astype(jnp.bfloat16)
         return pick(pair, core), other, swap(other, "ctx", 2)
 
+    def in_order(a, b):
+        first = first_half == 0
+        return jnp.concatenate([jnp.where(first, a, b), jnp.where(first, b, a)], axis=0)
+
+    attended = in_order(attended_a, attended_b)
     kept_b, came_b = down_hop(hidden, hidden_near)
-    hidden_far = after(hidden_far, kept_b)
+    hidden_far = after(hidden_far, (kept_b, attended))
     hidden_far_near = swap(hidden_far, "tp", 1)
     down_b, other_b, last_b = down_second(kept_b, after(came_b, hidden_far))
     down_a, _, last_a = down_second(*down_hop(hidden_far, after(hidden_far_near, other_b)))
     out_b = (wide(attended_b) + down_b + wide(last_b)).astype(jnp.bfloat16)
     out_a = (wide(attended_a) + down_a + wide(last_a)).astype(jnp.bfloat16)
 
-    def in_order(a, b):
-        first = first_half == 0
-        return jnp.concatenate([jnp.where(first, a, b), jnp.where(first, b, a)], axis=0)
-
-    return in_order(attended_a, attended_b), in_order(out_a, out_b)
+    return attended, in_order(out_a, out_b)
 
 
 def on_device(
@@ -418,12 +435,13 @@
     )
     own_index = ctx_place * row_count + jnp.arange(row_count, dtype=jnp.int32)
     _, own_position = trace_info(own_index, lengths)
-    rotated_keys = rope_keys(latent, own_position, LAT)
     key_order = jnp.arange(n_ctx * row_count, dtype=jnp.int32)
     if paired:
-        keys = gather_keys(rotated_keys, n_ctx)
         key_index = key_order + (ctx_place - (n_ctx - 1)) * row_count
+        _, key_position = trace_info(key_index, lengths)
+        keys = rope_keys(gather_keys(latent, n_ctx), key_position, LAT)
     else:
+        rotated_keys = rope_keys(latent, own_position, LAT)
         keys = lax.all_gather(rotated_keys, "ctx", axis=1, tiled=True)
         key_index = key_order
     heads_out = attention(queries, keys, key_index, own_index, own_position, value_weight)

time: 226 us -> 219 us (0.969)
  waiting for transfers between devices: 135 us -> 125 us
  starting transfers between devices: 31.1 us -> 39 us
  matrix products: 19.2 us -> 14.6 us
    ppermute x35, waiting for transfers between devices: 133 us -> 125 us  [swap(): return lax.ppermute(value, axis_name, [(i, i ^ bit) for i in range(width)])]
    ppermute x35, starting transfers between devices: 21 us -> 28.3 us  [swap(): return lax.ppermute(value, axis_name, [(i, i ^ bit) for i in range(width)])]
    dot_general x8 -> x6, matrix products: 19.2 us -> 14.6 us  [matmul(): jnp.dot(a, b, preferred_element_type=jnp.float32).astype(jnp.bfloat16)]
    unnamed x34 -> x28, local copies, waits for them, and re-layouts: 0.3 us -> 3.31 us
  transfers between devices with their start and end apart: 38 -> 38, of which waited for: 25 -> 23; matrix products, arithmetic and copies ran while one was open for 6% -> 7% of each run, Pallas kernels for 6% -> 6%
where the time goes in v11:
time: 219 us
  waiting for transfers between devices  125 us (57%)
  starting transfers between devices  39 us (18%)
  Pallas kernels  24.6 us (11%)
  matrix products  14.6 us (7%)
  other arithmetic  9.11 us (4%)
  local copies, waits for them, and re-layouts  5.16 us (2%)
    ppermute x35, waiting for transfers between devices, swap(): return lax.ppermute(value, axis_name, [(i, i ^ bit) for i in range(width)])  125 us
    ppermute x35, starting transfers between devices, swap(): return lax.ppermute(value, axis_name, [(i, i ^ bit) for i in range(width)])  28.3 us
    pallas_call x4, Pallas kernels, streamed_matmul(): pl.pallas_call(functools.partial(streamed_kernel, 512), in_specs=[pl.Bloc...  17.8 us
    dot_general x6, matrix products, matmul(): jnp.dot(a, b, preferred_element_type=jnp.float32).astype(jnp.bfloat16)  14.6 us
    ppermute x3, starting transfers between devices, gather_keys(): lax.ppermute(half, 'ctx', [(c, c + d) for c in range(n_ctx - d)])  10.7 us
    pallas_call x1, Pallas kernels, attention(): pl.pallas_call(functools.partial(attention_kernel, group), grid=(local_he...  6.79 us
  transfers between devices with their start and end apart: 38, of which 23 were waited for; matrix products, arithmetic and copies ran while one was open for 7% of the time, Pallas kernels for 6%

profile of v11, /device:TPU:0, one launch (start us, length us, event | category | flops | bytes accessed | tf_op | source)
XLA Modules:
  0.0 218.8 jit_solution(11508889255719681934)
XLA Ops:
  0.6 0.9 constant_dynamic-slice_fusion.14
  1.5 4.9 %collective-permute-start.2 = (bf16[288,128]{1,0:T(8,128)(2,1)S(1)}, bf16[288,128]{1,0:T(8,128)(2,1)S(1)}, u32[]{:S(2)}, u32[]{:S(2)}) collective-permute-start(bf16[288,128]{1,0:T(8,128)(2,1)S(1)} %constant_dynamic-slice_fusion.14), channel_id=1, source_target_pairs={{0,4},{4,8},{8,12},{1,5},{5,9},{9,13},{2,6},{6,10},{10,14},{3,7},{... | collective-permute-start | bytes 221192 | tf_op jit(solution)/shard_map/ppermute | solution.py:255
  6.5 4.5 %collective-permute-start.1 = (bf16[288,128]{1,0:T(8,128)(2,1)S(1)}, bf16[288,128]{1,0:T(8,128)(2,1)S(1)}, u32[]{:S(2)}, u32[]{:S(2)}) collective-permute-start(bf16[288,128]{1,0:T(8,128)(2,1)S(1)} %constant_dynamic-slice_fusion.14), channel_id=1, source_target_pairs={{0,8},{4,12},{1,9},{5,13},{2,10},{6,14},{3,11},{7,15},{16,24},{20,... | collective-permute-start | bytes 221192 | tf_op jit(solution)/shard_map/ppermute | solution.py:255
  11.0 1.3 collective-permute-start
  12.3 0.8 reduce-window.8
  13.2 0.7 subtract_subtract_fusion
  15.1 1.5 collective-permute-done.3
  17.2 1.0 copy-done.1
  18.2 0.7 copy-done
  19.0 6.8 %shard_map.113 = bf16[128,2048]{1,0:T(8,128)(2,1)S(1)} custom-call(f32[4,128,128]{2,1,0:T(8,128)S(1)} %pad_maximum_fusion.16.tables, s32[128,1]{1,0:T(8,128)S(1)} %copy.23.starts, s32[128,1]{1,0:T(8,128)S(1)} %iota_add_fusion.own_index, s32[1,512]{1,0:T(1,128)S(1)} %iota_add_fusion.2.key_index, bf16[576,512]{1,0:T(8,128)(2,1)S(1)} %pad_maximum_fusion.9.keys, ...), custom_call_target="tpu_custom_call" | custom-call | flops 2684354560 | bytes 5046272 | tf_op jit(solution)/shard_map/pallas_call | solution.py:143
  25.8 1.3 collective-permute-start.6
  27.1 0.5 collective-permute-start.5
  27.7 3.6 %collective-permute-done.6 = bf16[32,2048]{1,0:T(8,128)(2,1)S(1)} collective-permute-done((bf16[32,2048]{1,0:T(8,128)(2,1)S(1)}, bf16[32,2048]{1,0:T(8,128)(2,1)S(1)}, u32[]{:S(2)}, u32[]{:S(2)}) %collective-permute-start.6) | collective-permute-done | bytes 131104 | tf_op jit(solution)/shard_map/ppermute | solution.py:182
  31.4 3.1 %collective-permute-done.5 = bf16[32,2048]{1,0:T(8,128)(2,1)S(1)} collective-permute-done((bf16[32,2048]{1,0:T(8,128)(2,1)S(1)}, bf16[32,2048]{1,0:T(8,128)(2,1)S(1)}, u32[]{:S(2)}, u32[]{:S(2)}) %collective-permute-start.5) | collective-permute-done | bytes 131104 | tf_op jit(solution)/shard_map/ppermute | solution.py:182
  34.6 3.7 %collective-permute-start.9 = (bf16[32,2048]{1,0:T(8,128)(2,1)S(1)}, bf16[32,2048]{1,0:T(8,128)(2,1)S(1)}, u32[]{:S(2)}, u32[]{:S(2)}) collective-permute-start(bf16[32,2048]{1,0:T(8,128)(2,1)S(1)} %get-tuple-element.60), channel_id=1, source_target_pairs={{0,12},{4,8},{8,4},{12,0},{1,13},{5,9},{9,5},{13,1},{2,14},{6,10},... | collective-permute-start | bytes 393224 | tf_op jit(solution)/shard_map/ppermute | solution.py:182
  38.3 0.8 collective-permute-start.7
  39.1 3.8 %collective-permute-done.9 = bf16[32,2048]{1,0:T(8,128)(2,1)S(1)} collective-permute-done((bf16[32,2048]{1,0:T(8,128)(2,1)S(1)}, bf16[32,2048]{1,0:T(8,128)(2,1)S(1)}, u32[]{:S(2)}, u32[]{:S(2)}) %collective-permute-start.9) | collective-permute-done | bytes 131104 | tf_op jit(solution)/shard_map/ppermute | solution.py:182
  42.9 5.6 %collective-permute-done.8 = bf16[32,2048]{1,0:T(8,128)(2,1)S(1)} collective-permute-done((bf16[32,2048]{1,0:T(8,128)(2,1)S(1)}, bf16[32,2048]{1,0:T(8,128)(2,1)S(1)}, u32[]{:S(2)}, u32[]{:S(2)}) %collective-permute-start.8) | collective-permute-done | bytes 131104 | tf_op jit(solution)/shard_map/ppermute | solution.py:182
  48.6 1.6 collective-permute-start.13
  50.8 4.1 %shard_map.114 = bf16[256,1792]{1,0:T(8,128)(2,1)S(1)} custom-call(bf16[256,2048]{1,0:T(8,128)(2,1)S(1)} %bitcast.164, bf16[2048,1792]{1,0:T(8,128)(2,1)} %weight.5), custom_call_target="tpu_custom_call" | custom-call | flops 1024 | bytes 1024 | tf_op jit(solution)/shard_map/pallas_call | solution.py:228
  55.0 0.8 collective-permute-start.11
  55.7 7.2 %collective-permute-done.13 = bf16[4,32,2048]{2,1,0:T(8,128)(2,1)S(1)} collective-permute-done((bf16[4,32,2048]{2,1,0:T(8,128)(2,1)S(1)}, bf16[4,32,2048]{2,1,0:T(8,128)(2,1)S(1)}, u32[]{:S(2)}, u32[]{:S(2)}) %collective-permute-start.13) | collective-permute-done | bytes 524320 | tf_op jit(solution)/shard_map/ppermute | solution.py:182
  63.0 4.6 %collective-permute-done.11 = bf16[2,64,1792]{2,1,0:T(8,128)(2,1)S(1)} collective-permute-done((bf16[2,64,1792]{2,1,0:T(8,128)(2,1)S(1)}, bf16[2,64,1792]{2,1,0:T(8,128)(2,1)S(1)}, u32[]{:S(2)}, u32[]{:S(2)}) %collective-permute-start.11) | collective-permute-done | bytes 458784 | tf_op jit(solution)/shard_map/ppermute | solution.py:182
  67.7 1.5 collective-permute-start.12
  69.4 4.2 %shard_map.115 = bf16[256,1792]{1,0:T(8,128)(2,1)S(1)} custom-call(bf16[256,2048]{1,0:T(8,128)(2,1)S(1)} %bitcast.163, bf16[2048,1792]{1,0:T(8,128)(2,1)} %weight.5), custom_call_target="tpu_custom_call" | custom-call | flops 1024 | bytes 1024 | tf_op jit(solution)/shard_map/pallas_call | solution.py:228
  73.6 6.7 %collective-permute-done.12 = bf16[64,1792]{1,0:T(8,128)(2,1)S(1)} collective-permute-done((bf16[64,1792]{1,0:T(8,128)(2,1)S(1)}, bf16[64,1792]{1,0:T(8,128)(2,1)S(1)}, u32[]{:S(2)}, u32[]{:S(2)}) %collective-permute-start.12) | collective-permute-done | bytes 229408 | tf_op jit(solution)/shard_map/ppermute | solution.py:182
  80.6 3.2 %collective-permute-start.15 = (bf16[2,64,1792]{2,1,0:T(8,128)(2,1)S(1)}, bf16[2,64,1792]{2,1,0:T(8,128)(2,1)S(1)}, u32[]{:S(2)}, u32[]{:S(2)}) collective-permute-start(bf16[2,64,1792]{2,1,0:T(8,128)(2,1)S(1)} %slice_bitcast_fusion.4), channel_id=1, source_target_pairs={{0,4},{4,0},{8,12},{12,8},{1,5},{5,1},{9,13},{13,9},{2,6},{6,2},{1... | collective-permute-start | bytes 1376264 | tf_op jit(solution)/shard_map/ppermute | solution.py:182
  83.8 10.1 %collective-permute-done.16 = bf16[64,1792]{1,0:T(8,128)(2,1)S(1)} collective-permute-done((bf16[64,1792]{1,0:T(8,128)(2,1)S(1)}, bf16[64,1792]{1,0:T(8,128)(2,1)S(1)}, u32[]{:S(2)}, u32[]{:S(2)}) %collective-permute-start.16) | collective-permute-done | bytes 229408 | tf_op jit(solution)/shard_map/ppermute | solution.py:182
  94.0 5.9 %collective-permute-done.15 = bf16[2,64,1792]{2,1,0:T(8,128)(2,1)S(1)} collective-permute-done((bf16[2,64,1792]{2,1,0:T(8,128)(2,1)S(1)}, bf16[2,64,1792]{2,1,0:T(8,128)(2,1)S(1)}, u32[]{:S(2)}, u32[]{:S(2)}) %collective-permute-start.15) | collective-permute-done | bytes 458784 | tf_op jit(solution)/shard_map/ppermute | solution.py:182
  99.9 0.7 fusion.16
  100.8 9.7 %collective-permute-done.18 = bf16[64,1792]{1,0:T(8,128)(2,1)S(1)} collective-permute-done((bf16[64,1792]{1,0:T(8,128)(2,1)}, bf16[64,1792]{1,0:T(8,128)(2,1)S(1)}, u32[]{:S(2)}, u32[]{:S(2)}) %collective-permute-start.18) | collective-permute-done | bytes 229408 | tf_op jit(solution)/shard_map/ppermute | solution.py:182
  110.5 3.1 %collective-permute-done.17 = bf16[128,1792]{1,0:T(8,128)(2,1)S(1)} collective-permute-done((bf16[128,1792]{1,0:T(8,128)(2,1)S(1)}, bf16[128,1792]{1,0:T(8,128)(2,1)S(1)}, u32[]{:S(2)}, u32[]{:S(2)}) %collective-permute-start.17) | collective-permute-done | bytes 458784 | tf_op jit(solution)/shard_map/ppermute | solution.py:182
  114.0 6.3 %convolution_convert_fusion.1 = bf16[256,2560]{1,0:T(8,128)(2,1)S(1)} fusion(bf16[256,1792]{1,0:T(8,128)(2,1)S(1)} %get-tuple-element.23, bf16[1792,2560]{1,0:T(8,128)(2,1)} %param.17), kind=kOutput, calls=%fused_computation.1 | convolution fusion | flops 2349465600 | bytes 11403264 | tf_op jit(solution)/shard_map/dot_general | solution.py:194
  120.5 0.7 copy-done.6
  121.8 2.5 %convolution_convert_fusion = bf16[256,2560]{1,0:T(8,128)(2,1)S(1)} fusion(bf16[256,1792]{1,0:T(8,128)(2,1)S(1)} %get-tuple-element.23, bf16[1792,2560]{1,0:T(8,128)(2,1)S(1)} %bitcast.177), kind=kOutput, calls=%fused_computation | convolution fusion | flops 2349465600 | bytes 11403264 | tf_op jit(solution)/shard_map/dot_general | solution.py:194
  124.4 0.6 collective-permute-start.22
  125.0 1.5 collective-permute-start.26
  126.7 0.6 collective-permute-start.21
  127.5 1.6 collective-permute-start.28
  129.0 5.6 %collective-permute-done.19 = bf16[64,1792]{1,0:T(8,128)(2,1)S(1)} collective-permute-done((bf16[64,1792]{1,0:T(8,128)(2,1)S(1)}, bf16[64,1792]{1,0:T(8,128)(2,1)S(1)}, u32[]{:S(2)}, u32[]{:S(2)}) %collective-permute-start.19) | collective-permute-done | bytes 229408 | tf_op jit(solution)/shard_map/ppermute | solution.py:182
  134.6 9.8 %collective-permute-done.21 = bf16[128,2560]{1,0:T(8,128)(2,1)S(1)} collective-permute-done((bf16[128,2560]{1,0:T(8,128)(2,1)S(1)}, bf16[128,2560]{1,0:T(8,128)(2,1)S(1)}, u32[]{:S(2)}, u32[]{:S(2)}) %collective-permute-start.21) | collective-permute-done | bytes 655392 | tf_op jit(solution)/shard_map/ppermute | solution.py:182
  144.4 2.1 collective-permute-start.27
  146.7 1.6 convolution_convert_fusion.4
  149.1 1.4 convolution_convert_fusion.5
  150.7 0.5 collective-permute-start.23
  151.3 6.0 %collective-permute-done.28 = bf16[128,2560]{1,0:T(8,128)(2,1)S(1)} collective-permute-done((bf16[128,2560]{1,0:T(8,128)(2,1)S(1)}, bf16[128,2560]{1,0:T(8,128)(2,1)S(1)}, u32[]{:S(2)}, u32[]{:S(2)}) %collective-permute-start.28) | collective-permute-done | bytes 655392 | tf_op jit(solution)/shard_map/ppermute | solution.py:182
  157.4 1.4 convolution_convert_fusion.2
  158.8 1.4 convolution_convert_fusion.3
  160.4 0.5 collective-permute-start.29
  161.7 1.0 collective-permute-done.29
  162.9 0.6 fusion.14
  164.0 0.5 collective-permute-start.31
  164.5 1.2 collective-permute-done.32
  165.8 4.8 %shard_map.116 = bf16[256,1792]{1,0:T(8,128)(2,1)S(1)} custom-call(bf16[256,2560]{1,0:T(8,128)(2,1)S(1)} %pad_maximum_fusion.rows, bf16[2560,1792]{1,0:T(8,128)(2,1)} %weight.7), custom_call_target="tpu_custom_call" | custom-call | flops 1024 | bytes 1024 | tf_op jit(solution)/shard_map/pallas_call | solution.py:228
  170.6 2.1 collective-permute-start.34
  172.8 0.8 pad_maximum_fusion.13
  173.6 7.2 %collective-permute-done.31 = bf16[128,2560]{1,0:T(8,128)(2,1)S(1)} collective-permute-done((bf16[128,2560]{1,0:T(8,128)(2,1)S(1)}, bf16[128,2560]{1,0:T(8,128)(2,1)S(1)}, u32[]{:S(2)}, u32[]{:S(2)}) %collective-permute-start.31) | collective-permute-done | bytes 655392 | tf_op jit(solution)/shard_map/ppermute | solution.py:182
  180.8 3.0 %collective-permute-done.34 = bf16[2,64,1792]{2,1,0:T(8,128)(2,1)S(1)} collective-permute-done((bf16[2,64,1792]{2,1,0:T(8,128)(2,1)S(1)}, bf16[2,64,1792]{2,1,0:T(8,128)(2,1)S(1)}, u32[]{:S(2)}, u32[]{:S(2)}) %collective-permute-start.34) | collective-permute-done | bytes 458784 | tf_op jit(solution)/shard_map/ppermute | solution.py:182
  184.0 4.8 %shard_map.117 = bf16[256,1792]{1,0:T(8,128)(2,1)S(1)} custom-call(bf16[256,2560]{1,0:T(8,128)(2,1)S(1)} %pad_maximum_fusion.1.rows, bf16[2560,1792]{1,0:T(8,128)(2,1)} %weight.7), custom_call_target="tpu_custom_call" | custom-call | flops 1024 | bytes 1024 | tf_op jit(solution)/shard_map/pallas_call | solution.py:228
  188.8 1.8 collective-permute-start.35
  190.7 1.3 collective-permute-start.37
  191.9 14.1 %collective-permute-done.35 = bf16[2,64,1792]{2,1,0:T(8,128)(2,1)S(1)} collective-permute-done((bf16[2,64,1792]{2,1,0:T(8,128)(2,1)S(1)}, bf16[2,64,1792]{2,1,0:T(8,128)(2,1)S(1)}, u32[]{:S(2)}, u32[]{:S(2)}) %collective-permute-start.35) | collective-permute-done | bytes 458784 | tf_op jit(solution)/shard_map/ppermute | solution.py:182
  206.5 11.2 %collective-permute-done.36 = bf16[64,1792]{1,0:T(8,128)(2,1)S(1)} collective-permute-done((bf16[64,1792]{1,0:T(8,128)(2,1)S(1)}, bf16[64,1792]{1,0:T(8,128)(2,1)S(1)}, u32[]{:S(2)}, u32[]{:S(2)}) %collective-permute-start.36) | collective-permute-done | bytes 229408 | tf_op jit(solution)/shard_map/ppermute | solution.py:182
  218.0 0.8 pad_maximum_fusion.15
  (130 shorter events, 9.1 us)
Async XLA Ops:
  1.5 13.5 %collective-permute-start.2 = (bf16[288,128]{1,0:T(8,128)(2,1)S(1)}, bf16[288,128]{1,0:T(8,128)(2,1)S(1)}, u32[]{:S(2)}, u32[]{:S(2)}) collective-permute-start(bf16[288,128]{1,0:T(8,128)(2,1)S(1)} %constant_dynamic-slice_fusion.14), channel_id=1, source_target_pairs={{0,4},{4,8},{8,12},{1,5},{5,9},{9,13},{2,6},{6,10},{10,14},{3,7},{... | collective-permute-start | bytes 221192 | tf_op jit(solution)/shard_map/ppermute | solution.py:255
  6.5 8.5 %collective-permute-start.1 = (bf16[288,128]{1,0:T(8,128)(2,1)S(1)}, bf16[288,128]{1,0:T(8,128)(2,1)S(1)}, u32[]{:S(2)}, u32[]{:S(2)}) collective-permute-start(bf16[288,128]{1,0:T(8,128)(2,1)S(1)} %constant_dynamic-slice_fusion.14), channel_id=1, source_target_pairs={{0,8},{4,12},{1,9},{5,13},{2,10},{6,14},{3,11},{7,15},{16,24},{20,... | collective-permute-start | bytes 221192 | tf_op jit(solution)/shard_map/ppermute | solution.py:255
  11.0 4.0 %collective-permute-start = (bf16[288,128]{1,0:T(8,128)(2,1)S(1)}, bf16[288,128]{1,0:T(8,128)(2,1)S(1)}, u32[]{:S(2)}, u32[]{:S(2)}) collective-permute-start(bf16[288,128]{1,0:T(8,128)(2,1)S(1)} %constant_dynamic-slice_fusion.14), channel_id=1, source_target_pairs={{0,12},{1,13},{2,14},{3,15},{16,28},{17,29},{18,30},{19,31}} | collective-permute-start | bytes 221192 | tf_op jit(solution)/shard_map/ppermute | solution.py:255
  14.6 2.0 copy-start.4
  15.0 1.5 collective-permute-start.3
  16.6 1.6 copy-start.1
  16.8 2.2 copy-start
  25.8 5.5 %collective-permute-start.6 = (bf16[32,2048]{1,0:T(8,128)(2,1)S(1)}, bf16[32,2048]{1,0:T(8,128)(2,1)S(1)}, u32[]{:S(2)}, u32[]{:S(2)}) collective-permute-start(bf16[32,2048]{1,0:T(8,128)(2,1)S(1)} %get-tuple-element.64), channel_id=1, source_target_pairs={{0,3},{1,2},{2,1},{3,0},{4,7},{5,6},{6,5},{7,4},{8,11},{9,10},{10,... | collective-permute-start | bytes 393224 | tf_op jit(solution)/shard_map/ppermute | solution.py:182
  27.1 7.4 %collective-permute-start.5 = (bf16[32,2048]{1,0:T(8,128)(2,1)S(1)}, bf16[32,2048]{1,0:T(8,128)(2,1)S(1)}, u32[]{:S(2)}, u32[]{:S(2)}) collective-permute-start(bf16[32,2048]{1,0:T(8,128)(2,1)S(1)} %get-tuple-element.65), channel_id=1, source_target_pairs={{0,2},{1,3},{2,0},{3,1},{4,6},{5,7},{6,4},{7,5},{8,10},{9,11},{10,... | collective-permute-start | bytes 393224 | tf_op jit(solution)/shard_map/ppermute | solution.py:182
  27.7 6.8 %collective-permute-start.4 = (bf16[32,2048]{1,0:T(8,128)(2,1)S(1)}, bf16[32,2048]{1,0:T(8,128)(2,1)S(1)}, u32[]{:S(2)}, u32[]{:S(2)}) collective-permute-start(bf16[32,2048]{1,0:T(8,128)(2,1)S(1)} %get-tuple-element.66), channel_id=1, source_target_pairs={{0,1},{1,0},{2,3},{3,2},{4,5},{5,4},{6,7},{7,6},{8,9},{9,8},{10,11... | collective-permute-start | bytes 393224 | tf_op jit(solution)/shard_map/ppermute | solution.py:182
  34.6 8.3 %collective-permute-start.9 = (bf16[32,2048]{1,0:T(8,128)(2,1)S(1)}, bf16[32,2048]{1,0:T(8,128)(2,1)S(1)}, u32[]{:S(2)}, u32[]{:S(2)}) collective-permute-start(bf16[32,2048]{1,0:T(8,128)(2,1)S(1)} %get-tuple-element.60), channel_id=1, source_target_pairs={{0,12},{4,8},{8,4},{12,0},{1,13},{5,9},{9,5},{13,1},{2,14},{6,10},... | collective-permute-start | bytes 393224 | tf_op jit(solution)/shard_map/ppermute | solution.py:182
  38.3 10.2 %collective-permute-start.8 = (bf16[32,2048]{1,0:T(8,128)(2,1)S(1)}, bf16[32,2048]{1,0:T(8,128)(2,1)S(1)}, u32[]{:S(2)}, u32[]{:S(2)}) collective-permute-start(bf16[32,2048]{1,0:T(8,128)(2,1)S(1)} %get-tuple-element.61), channel_id=1, source_target_pairs={{0,8},{4,12},{8,0},{12,4},{1,9},{5,13},{9,1},{13,5},{2,10},{6,14},... | collective-permute-start | bytes 393224 | tf_op jit(solution)/shard_map/ppermute | solution.py:182
  38.3 10.2 %collective-permute-start.7 = (bf16[32,2048]{1,0:T(8,128)(2,1)S(1)}, bf16[32,2048]{1,0:T(8,128)(2,1)S(1)}, u32[]{:S(2)}, u32[]{:S(2)}) collective-permute-start(bf16[32,2048]{1,0:T(8,128)(2,1)S(1)} %get-tuple-element.62), channel_id=1, source_target_pairs={{0,4},{4,0},{8,12},{12,8},{1,5},{5,1},{9,13},{13,9},{2,6},{6,2},{1... | collective-permute-start | bytes 393224 | tf_op jit(solution)/shard_map/ppermute | solution.py:182
  48.6 2.0 collective-permute-start.10
  48.6 14.3 %collective-permute-start.13 = (bf16[4,32,2048]{2,1,0:T(8,128)(2,1)S(1)}, bf16[4,32,2048]{2,1,0:T(8,128)(2,1)S(1)}, u32[]{:S(2)}, u32[]{:S(2)}) collective-permute-start(bf16[4,32,2048]{2,1,0:T(8,128)(2,1)S(1)} %pad_maximum_fusion.11), channel_id=1, source_target_pairs={{0,2},{1,3},{2,0},{3,1},{4,6},{5,7},{6,4},{7,5},{8,10},{9,11},{10,... | collective-permute-start | bytes 1572872 | tf_op jit(solution)/shard_map/ppermute | solution.py:182
  55.0 12.6 %collective-permute-start.11 = (bf16[2,64,1792]{2,1,0:T(8,128)(2,1)S(1)}, bf16[2,64,1792]{2,1,0:T(8,128)(2,1)S(1)}, u32[]{:S(2)}, u32[]{:S(2)}) collective-permute-start(bf16[2,64,1792]{2,1,0:T(8,128)(2,1)S(1)} %slice_bitcast_fusion.5), channel_id=1, source_target_pairs={{0,4},{4,0},{8,12},{12,8},{1,5},{5,1},{9,13},{13,9},{2,6},{6,2},{1... | collective-permute-start | bytes 1376264 | tf_op jit(solution)/shard_map/ppermute | solution.py:182
  63.0 6.2 %collective-permute-start.14 = (bf16[4,32,2048]{2,1,0:T(8,128)(2,1)S(1)}, bf16[4,32,2048]{2,1,0:T(8,128)(2,1)S(1)}, u32[]{:S(2)}, u32[]{:S(2)}) collective-permute-start(bf16[4,32,2048]{2,1,0:T(8,128)(2,1)S(1)} %collective-permute-done.13), channel_id=1, source_target_pairs={{0,1},{1,0},{2,3},{3,2},{4,5},{5,4},{6,7},{7,6},{8,9},{9,8},{10,11... | collective-permute-start | bytes 1572872 | tf_op jit(solution)/shard_map/ppermute | solution.py:182
  67.7 12.7 %collective-permute-start.12 = (bf16[64,1792]{1,0:T(8,128)(2,1)S(1)}, bf16[64,1792]{1,0:T(8,128)(2,1)S(1)}, u32[]{:S(2)}, u32[]{:S(2)}) collective-permute-start(bf16[64,1792]{1,0:T(8,128)(2,1)S(1)} %fusion.20), channel_id=1, source_target_pairs={{0,8},{4,12},{8,0},{12,4},{1,9},{5,13},{9,1},{13,5},{2,10},{6,14},... | collective-permute-start | bytes 688136 | tf_op jit(solution)/shard_map/ppermute | solution.py:182
  69.4 11.0 %copy-start.3 = (bf16[128,1792]{1,0:T(8,128)(2,1)S(1)}, bf16[128,1792]{1,0:T(8,128)(2,1)}, u32[]{:S(2)}) copy-start(bf16[128,1792]{1,0:T(8,128)(2,1)} %param.10) | copy-start | bytes 1376260
  80.4 33.2 %copy-start.2 = (f32[1792]{0:T(1024)S(1)}, f32[1792]{0:T(1024)}, u32[]{:S(2)}) copy-start(f32[1792]{0:T(1024)} %param.16) | copy-start | bytes 21508
  80.5 13.4 %collective-permute-start.16 = (bf16[64,1792]{1,0:T(8,128)(2,1)S(1)}, bf16[64,1792]{1,0:T(8,128)(2,1)S(1)}, u32[]{:S(2)}, u32[]{:S(2)}) collective-permute-start(bf16[64,1792]{1,0:T(8,128)(2,1)S(1)} %fusion.23), channel_id=1, source_target_pairs={{0,8},{4,12},{8,0},{12,4},{1,9},{5,13},{9,1},{13,5},{2,10},{6,14},... | collective-permute-start | bytes 688136 | tf_op jit(solution)/shard_map/ppermute | solution.py:182
  80.6 19.3 %collective-permute-start.15 = (bf16[2,64,1792]{2,1,0:T(8,128)(2,1)S(1)}, bf16[2,64,1792]{2,1,0:T(8,128)(2,1)S(1)}, u32[]{:S(2)}, u32[]{:S(2)}) collective-permute-start(bf16[2,64,1792]{2,1,0:T(8,128)(2,1)S(1)} %slice_bitcast_fusion.4), channel_id=1, source_target_pairs={{0,4},{4,0},{8,12},{12,8},{1,5},{5,1},{9,13},{13,9},{2,6},{6,2},{1... | collective-permute-start | bytes 1376264 | tf_op jit(solution)/shard_map/ppermute | solution.py:182
  93.9 19.7 %collective-permute-start.17 = (bf16[128,1792]{1,0:T(8,128)(2,1)S(1)}, bf16[128,1792]{1,0:T(8,128)(2,1)S(1)}, u32[]{:S(2)}, u32[]{:S(2)}) collective-permute-start(bf16[128,1792]{1,0:T(8,128)(2,1)S(1)} %pad_maximum_fusion.12), channel_id=1, source_target_pairs={{0,4},{4,0},{8,12},{12,8},{1,5},{5,1},{9,13},{13,9},{2,6},{6,2},{1... | collective-permute-start | bytes 1376264 | tf_op jit(solution)/shard_map/ppermute | solution.py:182
  100.6 9.9 %collective-permute-start.18 = (bf16[64,1792]{1,0:T(8,128)(2,1)}, bf16[64,1792]{1,0:T(8,128)(2,1)S(1)}, u32[]{:S(2)}, u32[]{:S(2)}) collective-permute-start(bf16[64,1792]{1,0:T(8,128)(2,1)} %fusion.16), channel_id=1, source_target_pairs={{0,8},{4,12},{8,0},{12,4},{1,9},{5,13},{9,1},{13,5},{2,10},{6,14},... | collective-permute-start | bytes 688136 | tf_op jit(solution)/shard_map/ppermute | solution.py:182
  110.5 9.8 %copy-start.5 = (bf16[64,1792]{1,0:T(8,128)(2,1)}, bf16[64,1792]{1,0:T(8,128)(2,1)S(1)}, u32[]{:S(2)}) copy-start(bf16[64,1792]{1,0:T(8,128)(2,1)S(1)} %collective-permute-done.18) | copy-start | bytes 688132
  113.6 8.1 %slice-start = ((s8[9175040]{0:T(1024)(128)(4,1)}), s8[4194304]{0:T(1024)(128)(4,1)S(1)}, s32[]{:S(2)}) async-start(s8[9175040]{0:T(1024)(128)(4,1)} %bitcast.176), calls=%async_computation | async-start | bytes 8388608
  114.0 7.8 %slice-start.1 = ((s8[9175040]{0:T(1024)(128)(4,1)}), s8[4194304]{0:T(1024)(128)(4,1)S(1)}, s32[]{:S(2)}) async-start(s8[9175040]{0:T(1024)(128)(4,1)} %bitcast.176), calls=%async_computation.1 | async-start | bytes 8388608
  114.0 7.8 %slice-start.2 = ((s8[9175040]{0:T(1024)(128)(4,1)}), s8[786432]{0:T(1024)(128)(4,1)S(1)}, s32[]{:S(2)}) async-start(s8[9175040]{0:T(1024)(128)(4,1)} %bitcast.176), calls=%async_computation.2 | async-start | bytes 1572864
  120.3 0.9 copy-start.6
  120.5 6.0 %collective-permute-start.20 = (bf16[128,2560]{1,0:T(8,128)(2,1)S(1)}, bf16[128,2560]{1,0:T(8,128)(2,1)S(1)}, u32[]{:S(2)}, u32[]{:S(2)}) collective-permute-start(bf16[128,2560]{1,0:T(8,128)(2,1)S(1)} %bitcast.182), channel_id=1, source_target_pairs={{0,1},{1,0},{2,3},{3,2},{4,5},{5,4},{6,7},{7,6},{8,9},{9,8},{10,11... | collective-permute-start | bytes 1966088 | tf_op jit(solution)/shard_map/ppermute | solution.py:182
  121.4 13.2 %collective-permute-start.19 = (bf16[64,1792]{1,0:T(8,128)(2,1)S(1)}, bf16[64,1792]{1,0:T(8,128)(2,1)S(1)}, u32[]{:S(2)}, u32[]{:S(2)}) collective-permute-start(bf16[64,1792]{1,0:T(8,128)(2,1)S(1)} %get-tuple-element.34), channel_id=1, source_target_pairs={{0,8},{4,12},{8,0},{12,4},{1,9},{5,13},{9,1},{13,5},{2,10},{6,14},... | collective-permute-start | bytes 688136 | tf_op jit(solution)/shard_map/ppermute | solution.py:182
  121.8 3.2 %collective-permute-start.25 = (f32[256]{0:T(256)S(1)}, f32[256]{0:T(256)S(1)}, u32[]{:S(2)}, u32[]{:S(2)}) collective-permute-start(f32[256]{0:T(256)S(1)} %get-tuple-element.47), channel_id=1, source_target_pairs={{0,1},{1,0},{2,3},{3,2},{4,5},{5,4},{6,7},{7,6},{8,9},{9,8},{10,11... | collective-permute-start | bytes 3080 | tf_op jit(solution)/shard_map/ppermute | solution.py:182
  124.4 2.9 %collective-permute-start.22 = (bf16[128,2560]{1,0:T(8,128)(2,1)S(1)}, bf16[128,2560]{1,0:T(8,128)(2,1)S(1)}, u32[]{:S(2)}, u32[]{:S(2)}) collective-permute-start(bf16[128,2560]{1,0:T(8,128)(2,1)S(1)} %bitcast.183), channel_id=1, source_target_pairs={{0,1},{1,0},{2,3},{3,2},{4,5},{5,4},{6,7},{7,6},{8,9},{9,8},{10,11... | collective-permute-start | bytes 1966088 | tf_op jit(solution)/shard_map/ppermute | solution.py:182
  125.0 36.0 %collective-permute-start.26 = (f32[256]{0:T(256)S(1)}, f32[256]{0:T(256)S(1)}, u32[]{:S(2)}, u32[]{:S(2)}) collective-permute-start(f32[256]{0:T(256)S(1)} %add.261), channel_id=1, source_target_pairs={{0,2},{1,3},{2,0},{3,1},{4,6},{5,7},{6,4},{7,5},{8,10},{9,11},{10,... | collective-permute-start | bytes 3080 | tf_op jit(solution)/shard_map/ppermute | solution.py:182
  126.7 17.7 %collective-permute-start.21 = (bf16[128,2560]{1,0:T(8,128)(2,1)S(1)}, bf16[128,2560]{1,0:T(8,128)(2,1)S(1)}, u32[]{:S(2)}, u32[]{:S(2)}) collective-permute-start(bf16[128,2560]{1,0:T(8,128)(2,1)S(1)} %fusion.3), channel_id=1, source_target_pairs={{0,2},{1,3},{2,0},{3,1},{4,6},{5,7},{6,4},{7,5},{8,10},{9,11},{10,... | collective-permute-start | bytes 1966088 | tf_op jit(solution)/shard_map/ppermute | solution.py:182
  127.5 29.8 %collective-permute-start.28 = (bf16[128,2560]{1,0:T(8,128)(2,1)S(1)}, bf16[128,2560]{1,0:T(8,128)(2,1)S(1)}, u32[]{:S(2)}, u32[]{:S(2)}) collective-permute-start(bf16[128,2560]{1,0:T(8,128)(2,1)S(1)} %fusion.2), channel_id=1, source_target_pairs={{0,2},{1,3},{2,0},{3,1},{4,6},{5,7},{6,4},{7,5},{8,10},{9,11},{10,... | collective-permute-start | bytes 1966088 | tf_op jit(solution)/shard_map/ppermute | solution.py:182
  144.4 3.9 %slice-start.3 = ((s8[9175040]{0:T(1024)(128)(4,1)}), s8[4194304]{0:T(1024)(128)(4,1)S(1)}, s32[]{:S(2)}) async-start(s8[9175040]{0:T(1024)(128)(4,1)} %bitcast.178), calls=%async_computation.3 | async-start | bytes 8388608
  144.4 12.8 %collective-permute-start.27 = (bf16[128,1792]{1,0:T(8,128)(2,1)S(1)}, bf16[128,1792]{1,0:T(8,128)(2,1)S(1)}, u32[]{:S(2)}, u32[]{:S(2)}) collective-permute-start(bf16[128,1792]{1,0:T(8,128)(2,1)S(1)} %pad_maximum_fusion.14), channel_id=1, source_target_pairs={{0,4},{4,0},{8,12},{12,8},{1,5},{5,1},{9,13},{13,9},{2,6},{6,2},{1... | collective-permute-start | bytes 1376264 | tf_op jit(solution)/shard_map/ppermute | solution.py:182
  146.7 2.2 %slice-start.4 = ((s8[9175040]{0:T(1024)(128)(4,1)}), s8[4194304]{0:T(1024)(128)(4,1)S(1)}, s32[]{:S(2)}) async-start(s8[9175040]{0:T(1024)(128)(4,1)} %bitcast.178), calls=%async_computation.4 | async-start | bytes 8388608
  146.7 2.4 %slice-start.5 = ((s8[9175040]{0:T(1024)(128)(4,1)}), s8[786432]{0:T(1024)(128)(4,1)S(1)}, s32[]{:S(2)}) async-start(s8[9175040]{0:T(1024)(128)(4,1)} %bitcast.178), calls=%async_computation.5 | async-start | bytes 1572864
  150.5 10.5 %collective-permute-start.24 = (f32[128]{0:T(128)S(1)}, f32[128]{0:T(128)S(1)}, u32[]{:S(2)}, u32[]{:S(2)}) collective-permute-start(f32[128]{0:T(128)S(1)} %fusion.5), channel_id=1, source_target_pairs={{0,1},{1,0},{2,3},{3,2},{4,5},{5,4},{6,7},{7,6},{8,9},{9,8},{10,11... | collective-permute-start | bytes 1544 | tf_op jit(solution)/shard_map/ppermute | solution.py:182
  150.7 10.8 %collective-permute-start.23 = (bf16[128,2560]{1,0:T(8,128)(2,1)S(1)}, bf16[128,2560]{1,0:T(8,128)(2,1)S(1)}, u32[]{:S(2)}, u32[]{:S(2)}) collective-permute-start(bf16[128,2560]{1,0:T(8,128)(2,1)S(1)} %pad_maximum_fusion.5), channel_id=1, source_target_pairs={{0,1},{1,0},{2,3},{3,2},{4,5},{5,4},{6,7},{7,6},{8,9},{9,8},{10,11... | collective-permute-start | bytes 1966088 | tf_op jit(solution)/shard_map/ppermute | solution.py:182
  160.2 1.2 collective-permute-start.30
  160.4 2.3 %collective-permute-start.29 = (bf16[128,2560]{1,0:T(8,128)(2,1)S(1)}, bf16[128,2560]{1,0:T(8,128)(2,1)S(1)}, u32[]{:S(2)}, u32[]{:S(2)}) collective-permute-start(bf16[128,2560]{1,0:T(8,128)(2,1)S(1)} %pad_maximum_fusion.6), channel_id=1, source_target_pairs={{0,1},{1,0},{2,3},{3,2},{4,5},{5,4},{6,7},{7,6},{8,9},{9,8},{10,11... | collective-permute-start | bytes 1966088 | tf_op jit(solution)/shard_map/ppermute | solution.py:182
  163.5 2.2 collective-permute-start.32
  164.0 16.8 %collective-permute-start.31 = (bf16[128,2560]{1,0:T(8,128)(2,1)S(1)}, bf16[128,2560]{1,0:T(8,128)(2,1)S(1)}, u32[]{:S(2)}, u32[]{:S(2)}) collective-permute-start(bf16[128,2560]{1,0:T(8,128)(2,1)S(1)} %pad_maximum_fusion.7), channel_id=1, source_target_pairs={{0,2},{1,3},{2,0},{3,1},{4,6},{5,7},{6,4},{7,5},{8,10},{9,11},{10,... | collective-permute-start | bytes 1966088 | tf_op jit(solution)/shard_map/ppermute | solution.py:182
  170.6 13.2 %collective-permute-start.34 = (bf16[2,64,1792]{2,1,0:T(8,128)(2,1)S(1)}, bf16[2,64,1792]{2,1,0:T(8,128)(2,1)S(1)}, u32[]{:S(2)}, u32[]{:S(2)}) collective-permute-start(bf16[2,64,1792]{2,1,0:T(8,128)(2,1)S(1)} %slice_bitcast_fusion.2), channel_id=1, source_target_pairs={{0,4},{4,0},{8,12},{12,8},{1,5},{5,1},{9,13},{13,9},{2,6},{6,2},{1... | collective-permute-start | bytes 1376264 | tf_op jit(solution)/shard_map/ppermute | solution.py:182
  180.8 3.2 %collective-permute-start.33 = (bf16[128,2560]{1,0:T(8,128)(2,1)S(1)}, bf16[128,2560]{1,0:T(8,128)(2,1)S(1)}, u32[]{:S(2)}, u32[]{:S(2)}) collective-permute-start(bf16[128,2560]{1,0:T(8,128)(2,1)S(1)} %collective-permute-done.31), channel_id=1, source_target_pairs={{0,1},{1,0},{2,3},{3,2},{4,5},{5,4},{6,7},{7,6},{8,9},{9,8},{10,11... | collective-permute-start | bytes 1966088 | tf_op jit(solution)/shard_map/ppermute | solution.py:182
  188.8 17.2 %collective-permute-start.35 = (bf16[2,64,1792]{2,1,0:T(8,128)(2,1)S(1)}, bf16[2,64,1792]{2,1,0:T(8,128)(2,1)S(1)}, u32[]{:S(2)}, u32[]{:S(2)}) collective-permute-start(bf16[2,64,1792]{2,1,0:T(8,128)(2,1)S(1)} %slice_bitcast_fusion), channel_id=1, source_target_pairs={{0,4},{4,0},{8,12},{12,8},{1,5},{5,1},{9,13},{13,9},{2,6},{6,2},{1... | collective-permute-start | bytes 1376264 | tf_op jit(solution)/shard_map/ppermute | solution.py:182
  190.7 15.9 %collective-permute-start.37 = (bf16[64,1792]{1,0:T(8,128)(2,1)S(1)}, bf16[64,1792]{1,0:T(8,128)(2,1)S(1)}, u32[]{:S(2)}, u32[]{:S(2)}) collective-permute-start(bf16[64,1792]{1,0:T(8,128)(2,1)S(1)} %fusion.32), channel_id=1, source_target_pairs={{0,8},{4,12},{8,0},{12,4},{1,9},{5,13},{9,1},{13,5},{2,10},{6,14},... | collective-permute-start | bytes 688136 | tf_op jit(solution)/shard_map/ppermute | solution.py:182
  206.2 11.6 %collective-permute-start.36 = (bf16[64,1792]{1,0:T(8,128)(2,1)S(1)}, bf16[64,1792]{1,0:T(8,128)(2,1)S(1)}, u32[]{:S(2)}, u32[]{:S(2)}) collective-permute-start(bf16[64,1792]{1,0:T(8,128)(2,1)S(1)} %fusion.33), channel_id=1, source_target_pairs={{0,8},{4,12},{8,0},{12,4},{1,9},{5,13},{9,1},{13,5},{2,10},{6,14},... | collective-permute-start | bytes 688136 | tf_op jit(solution)/shard_map/ppermute | solution.py:182

commit v12 on v11

--- a/solution.py
+++ b/solution.py
@@ -243,6 +243,33 @@
     )(rows, weight)
 
 
+def load_kernel(chunks, weight, out, sems):
+    rows = weight.shape[0] // chunks
+    copies = [
+        pltpu.make_async_copy(
+            weight.at[pl.ds(i * rows, rows)], out.at[pl.ds(i * rows, rows)], sems.at[i]
+        )
+        for i in range(chunks)
+    ]
+    for copy in copies:
+        copy.start()
+    for copy in copies:
+        copy.wait()
+
+
+def load(weight, grant):
+    chunks = 8
+    return pl.pallas_call(
+        functools.partial(load_kernel, chunks),
+        in_specs=[pl.BlockSpec(memory_space=pl.ANY)],
+        out_specs=pl.BlockSpec(memory_space=pltpu.VMEM),
+        out_shape=pltpu.VMEM(weight.shape, weight.dtype),
+        scratch_shapes=[pltpu.SemaphoreType.DMA((chunks,))],
+        compiler_params=pltpu.CompilerParams(vmem_limit_bytes=grant * 1024 * 1024),
+        cost_estimate=pl.CostEstimate(flops=0, bytes_accessed=1024, transcendentals=0),
+    )(weight)
+
+
 def after(value, earlier):
     return lax.optimization_barrier((value, earlier))[0]
 
@@ -332,6 +359,8 @@
     kept_b, sent_b, came_b = first_hop(core_rows(far, after(far_near, other_a)))
     attended_a = attend(mine_a, after(last_a, sent_b), first_half)
     twin_a = swap(attended_a, "ctx", 2)
+    gate_weight = load(after(gate_weight, attended_a), 44)
+    twin_a, came_b, gate_weight = lax.optimization_barrier((twin_a, came_b, gate_weight))
     pair_a = jnp.concatenate([attended_a, twin_a], axis=0)
     rest_a = swap(pair_a, "ctx", 1)
     mine_b, other_b, last_b = second_hop(kept_b, after(came_b, pair_a))
@@ -341,18 +370,20 @@
     all_a = jnp.concatenate([pair_a, rest_a], axis=0)
     squares_a, scaled = scale(all_a)
 
-    def cross(rows, weight):
+    def cross(rows, weight, earlier):
         term = matmul(rows, weight).reshape(2, 2, half, -1)
 
         def side(which):
             return lax.dynamic_index_in_dim(term, which, 1, keepdims=False).reshape(2 * half, -1)
 
-        sent = side(1 - core)
-        total = chip_sum(side(core), sent).astype(jnp.bfloat16)
-        return sent, total, swap(total, "tp", 2)
-
-    sent_gate, _, across_gate = cross(scaled, gate_weight)
-    _, sums_up, across_up = cross(after(scaled, sent_gate), up_weight)
+        came = swap(side(1 - core), "tp", 1)
+        if earlier is not None:
+            came = after(came, earlier)
+        total = (wide(side(core)) + wide(came)).astype(jnp.bfloat16)
+        return total, swap(total, "tp", 2)
+
+    sums_gate, across_gate = cross(scaled, gate_weight, None)
+    sums_up, across_up = cross(after(scaled, sums_gate), up_weight, across_gate)
     across_squares = swap(squares_a + swap(squares_a, "tp", 1), "tp", 2)
     pair_b = jnp.concatenate([attended_b, after(twin_b, across_gate)], axis=0)
     rest_b = swap(pair_b, "ctx", 1)
@@ -367,7 +398,8 @@
 
     kept, sent, squares_p = gate_up(after(pair_b, sums_up))
     terms_p = chip_sum(kept, sent)
-    rest_b, across_up, _ = lax.optimization_barrier((rest_b, across_up, sent))
+    down_loaded = load(after(down_weight, sent), 24)
+    rest_b, across_up, down_loaded = lax.optimization_barrier((rest_b, across_up, down_loaded))
     kept, sent, squares_q = gate_up(rest_b)
     terms_q = chip_sum(kept, sent)
     parts = [
@@ -384,8 +416,8 @@
     hidden_near = swap(hidden, "tp", 1)
     hidden_far = swap(hidden, "tp", 2)
 
-    def down_hop(mine, other):
-        blocks = streamed_matmul(jnp.concatenate([mine, other], axis=0), down_weight)
+    def down_hop(mine, other, product, weight):
+        blocks = product(jnp.concatenate([mine, other], axis=0), weight)
         blocks = blocks.reshape(2, 2, half, width)
         return blocks[:, 0], swap(blocks[:, 1], "ctx", 1)
 
@@ -399,11 +431,13 @@
         return jnp.concatenate([jnp.where(first, a, b), jnp.where(first, b, a)], axis=0)
 
     attended = in_order(attended_a, attended_b)
-    kept_b, came_b = down_hop(hidden, hidden_near)
+    kept_b, came_b = down_hop(hidden, hidden_near, matmul, down_loaded)
     hidden_far = after(hidden_far, (kept_b, attended))
     hidden_far_near = swap(hidden_far, "tp", 1)
     down_b, other_b, last_b = down_second(kept_b, after(came_b, hidden_far))
-    down_a, _, last_a = down_second(*down_hop(hidden_far, after(hidden_far_near, other_b)))
+    down_a, _, last_a = down_second(
+        *down_hop(hidden_far, after(hidden_far_near, other_b), streamed_matmul, down_weight)
+    )
     out_b = (wide(attended_b) + down_b + wide(last_b)).astype(jnp.bfloat16)
     out_a = (wide(attended_a) + down_a + wide(last_a)).astype(jnp.bfloat16)
 

time: 219 us -> 234 us (1.068)
  matrix products: 14.6 us -> 24.3 us
  local copies, waits for them, and re-layouts: 5.16 us -> 10.6 us
  starting transfers between devices: 39 us -> 35.6 us
    dot_general x6 -> x7, matrix products: 14.6 us -> 24.3 us  [matmul(): jnp.dot(a, b, preferred_element_type=jnp.float32).astype(jnp.bfloat16)]
    pallas_call x0 -> x2, Pallas kernels: none -> 5.37 us  [load(): pl.pallas_call(functools.partial(load_kernel, chunks), in_specs=[pl.Block...]
    pallas_call x4 -> x3, Pallas kernels: 17.8 us -> 13.1 us  [streamed_matmul(): pl.pallas_call(functools.partial(streamed_kernel, 512), in_specs=[pl.Bloc...]
    unnamed x28 -> x42, local copies, waits for them, and re-layouts: 3.31 us -> 7.01 us
    ppermute x35, starting transfers between devices: 28.3 us -> 24.9 us  [swap(): return lax.ppermute(value, axis_name, [(i, i ^ bit) for i in range(width)])]
  transfers between devices with their start and end apart: 38 -> 38, of which waited for: 23 -> 27; matrix products, arithmetic and copies ran while one was open for 7% -> 11% of each run, Pallas kernels for 6% -> 6%
where the time goes in v12:
time: 234 us
  waiting for transfers between devices  125 us (53%)
  starting transfers between devices  35.6 us (15%)
  Pallas kernels  25.2 us (11%)
  matrix products  24.3 us (10%)
  other arithmetic  11.3 us (5%)
  local copies, waits for them, and re-layouts  10.6 us (5%)
    ppermute x35, waiting for transfers between devices, swap(): return lax.ppermute(value, axis_name, [(i, i ^ bit) for i in range(width)])  125 us
    ppermute x35, starting transfers between devices, swap(): return lax.ppermute(value, axis_name, [(i, i ^ bit) for i in range(width)])  24.9 us
    dot_general x7, matrix products, matmul(): jnp.dot(a, b, preferred_element_type=jnp.float32).astype(jnp.bfloat16)  24.3 us
    pallas_call x3, Pallas kernels, streamed_matmul(): pl.pallas_call(functools.partial(streamed_kernel, 512), in_specs=[pl.Bloc...  13.1 us
    ppermute x3, starting transfers between devices, gather_keys(): lax.ppermute(half, 'ctx', [(c, c + d) for c in range(n_ctx - d)])  10.7 us
    unnamed x42, local copies, waits for them, and re-layouts  7.01 us
    pallas_call x1, Pallas kernels, attention(): pl.pallas_call(functools.partial(attention_kernel, group), grid=(local_he...  6.79 us
    pallas_call x2, Pallas kernels, load(): pl.pallas_call(functools.partial(load_kernel, chunks), in_specs=[pl.Block...  5.37 us
  transfers between devices with their start and end apart: 38, of which 27 were waited for; matrix products, arithmetic and copies ran while one was open for 11% of the time, Pallas kernels for 6%

profile of v12, /device:TPU:0, one launch (start us, length us, event | category | flops | bytes accessed | tf_op | source)
XLA Modules:
  0.0 233.6 jit_solution(6781529480143304821)
XLA Ops:
  0.6 0.9 constant_dynamic-slice_fusion.14
  1.5 4.9 %collective-permute-start.2 = (bf16[288,128]{1,0:T(8,128)(2,1)S(1)}, bf16[288,128]{1,0:T(8,128)(2,1)S(1)}, u32[]{:S(2)}, u32[]{:S(2)}) collective-permute-start(bf16[288,128]{1,0:T(8,128)(2,1)S(1)} %constant_dynamic-slice_fusion.14), channel_id=1, source_target_pairs={{0,4},{4,8},{8,12},{1,5},{5,9},{9,13},{2,6},{6,10},{10,14},{3,7},{... | collective-permute-start | bytes 221192 | tf_op jit(solution)/shard_map/ppermute | solution.py:282
  6.5 4.5 %collective-permute-start.1 = (bf16[288,128]{1,0:T(8,128)(2,1)S(1)}, bf16[288,128]{1,0:T(8,128)(2,1)S(1)}, u32[]{:S(2)}, u32[]{:S(2)}) collective-permute-start(bf16[288,128]{1,0:T(8,128)(2,1)S(1)} %constant_dynamic-slice_fusion.14), channel_id=1, source_target_pairs={{0,8},{4,12},{1,9},{5,13},{2,10},{6,14},{3,11},{7,15},{16,24},{20,... | collective-permute-start | bytes 221192 | tf_op jit(solution)/shard_map/ppermute | solution.py:282
  11.0 1.3 collective-permute-start
  12.3 0.8 reduce-window.8
  15.1 1.5 collective-permute-done.3
  17.2 1.0 copy-done.2
  18.2 0.7 copy-done.1
  19.0 6.8 %shard_map.113 = bf16[128,2048]{1,0:T(8,128)(2,1)S(1)} custom-call(f32[4,128,128]{2,1,0:T(8,128)S(1)} %pad_maximum_fusion.15.tables, s32[128,1]{1,0:T(8,128)S(1)} %copy.23.starts, s32[128,1]{1,0:T(8,128)S(1)} %iota_add_fusion.own_index, s32[1,512]{1,0:T(1,128)S(1)} %iota_add_fusion.2.key_index, bf16[576,512]{1,0:T(8,128)(2,1)S(1)} %pad_maximum_fusion.8.keys, ...), custom_call_target="tpu_custom_call" | custom-call | flops 2684354560 | bytes 5046272 | tf_op jit(solution)/shard_map/pallas_call | solution.py:143
  25.8 1.3 collective-permute-start.6
  27.7 3.6 %collective-permute-done.6 = bf16[32,2048]{1,0:T(8,128)(2,1)S(1)} collective-permute-done((bf16[32,2048]{1,0:T(8,128)(2,1)S(1)}, bf16[32,2048]{1,0:T(8,128)(2,1)S(1)}, u32[]{:S(2)}, u32[]{:S(2)}) %collective-permute-start.6) | collective-permute-done | bytes 131104 | tf_op jit(solution)/shard_map/ppermute | solution.py:182
  31.4 3.1 %collective-permute-done.5 = bf16[32,2048]{1,0:T(8,128)(2,1)S(1)} collective-permute-done((bf16[32,2048]{1,0:T(8,128)(2,1)S(1)}, bf16[32,2048]{1,0:T(8,128)(2,1)S(1)}, u32[]{:S(2)}, u32[]{:S(2)}) %collective-permute-start.5) | collective-permute-done | bytes 131104 | tf_op jit(solution)/shard_map/ppermute | solution.py:182
  34.6 3.7 %collective-permute-start.9 = (bf16[32,2048]{1,0:T(8,128)(2,1)S(1)}, bf16[32,2048]{1,0:T(8,128)(2,1)S(1)}, u32[]{:S(2)}, u32[]{:S(2)}) collective-permute-start(bf16[32,2048]{1,0:T(8,128)(2,1)S(1)} %get-tuple-element.74), channel_id=1, source_target_pairs={{0,12},{4,8},{8,4},{12,0},{1,13},{5,9},{9,5},{13,1},{2,14},{6,10},... | collective-permute-start | bytes 393224 | tf_op jit(solution)/shard_map/ppermute | solution.py:182
  38.3 0.8 collective-permute-start.7
  39.1 3.8 %collective-permute-done.9 = bf16[32,2048]{1,0:T(8,128)(2,1)S(1)} collective-permute-done((bf16[32,2048]{1,0:T(8,128)(2,1)S(1)}, bf16[32,2048]{1,0:T(8,128)(2,1)S(1)}, u32[]{:S(2)}, u32[]{:S(2)}) %collective-permute-start.9) | collective-permute-done | bytes 131104 | tf_op jit(solution)/shard_map/ppermute | solution.py:182
  42.9 5.6 %collective-permute-done.8 = bf16[32,2048]{1,0:T(8,128)(2,1)S(1)} collective-permute-done((bf16[32,2048]{1,0:T(8,128)(2,1)S(1)}, bf16[32,2048]{1,0:T(8,128)(2,1)S(1)}, u32[]{:S(2)}, u32[]{:S(2)}) %collective-permute-start.8) | collective-permute-done | bytes 131104 | tf_op jit(solution)/shard_map/ppermute | solution.py:182
  48.6 1.6 collective-permute-start.13
  50.8 4.1 %shard_map.114 = bf16[256,1792]{1,0:T(8,128)(2,1)S(1)} custom-call(bf16[256,2048]{1,0:T(8,128)(2,1)S(1)} %bitcast.169, bf16[2048,1792]{1,0:T(8,128)(2,1)} %weight.4), custom_call_target="tpu_custom_call" | custom-call | flops 1024 | bytes 1024 | tf_op jit(solution)/shard_map/pallas_call | solution.py:228
  55.0 0.8 collective-permute-start.11
  55.7 7.2 %collective-permute-done.13 = bf16[4,32,2048]{2,1,0:T(8,128)(2,1)S(1)} collective-permute-done((bf16[4,32,2048]{2,1,0:T(8,128)(2,1)S(1)}, bf16[4,32,2048]{2,1,0:T(8,128)(2,1)S(1)}, u32[]{:S(2)}, u32[]{:S(2)}) %collective-permute-start.13) | collective-permute-done | bytes 524320 | tf_op jit(solution)/shard_map/ppermute | solution.py:182
  63.0 4.6 %collective-permute-done.11 = bf16[2,64,1792]{2,1,0:T(8,128)(2,1)S(1)} collective-permute-done((bf16[2,64,1792]{2,1,0:T(8,128)(2,1)S(1)}, bf16[2,64,1792]{2,1,0:T(8,128)(2,1)S(1)}, u32[]{:S(2)}, u32[]{:S(2)}) %collective-permute-start.11) | collective-permute-done | bytes 458784 | tf_op jit(solution)/shard_map/ppermute | solution.py:182
  67.7 1.5 collective-permute-start.12
  69.4 4.2 %shard_map.115 = bf16[256,1792]{1,0:T(8,128)(2,1)S(1)} custom-call(bf16[256,2048]{1,0:T(8,128)(2,1)S(1)} %bitcast.168, bf16[2048,1792]{1,0:T(8,128)(2,1)} %weight.4), custom_call_target="tpu_custom_call" | custom-call | flops 1024 | bytes 1024 | tf_op jit(solution)/shard_map/pallas_call | solution.py:228
  73.6 1.8 collective-permute-start.16
  75.4 5.0 %collective-permute-done.12 = bf16[64,1792]{1,0:T(8,128)(2,1)S(1)} collective-permute-done((bf16[64,1792]{1,0:T(8,128)(2,1)S(1)}, bf16[64,1792]{1,0:T(8,128)(2,1)S(1)}, u32[]{:S(2)}, u32[]{:S(2)}) %collective-permute-start.12) | collective-permute-done | bytes 229408 | tf_op jit(solution)/shard_map/ppermute | solution.py:182
  80.7 3.7 %shard_map.116 = bf16[1792,2560]{1,0:T(8,128)(2,1)S(1)} custom-call(bf16[1792,2560]{1,0:T(8,128)(2,1)} %weight.5), custom_call_target="tpu_custom_call" | custom-call | bytes 1024 | tf_op jit(solution)/shard_map/pallas_call | solution.py:262
  84.4 3.6 %copy-done = bf16[1792,2560]{1,0:T(8,128)(2,1)} copy-done((bf16[1792,2560]{1,0:T(8,128)(2,1)}, bf16[1792,2560]{1,0:T(8,128)(2,1)S(1)}, u32[]{:S(2)}) %copy-start) | copy-done | bytes 9175064
  88.0 5.9 %collective-permute-done.15 = bf16[64,1792]{1,0:T(8,128)(2,1)S(1)} collective-permute-done((bf16[64,1792]{1,0:T(8,128)(2,1)S(1)}, bf16[64,1792]{1,0:T(8,128)(2,1)S(1)}, u32[]{:S(2)}, u32[]{:S(2)}) %collective-permute-start.15) | collective-permute-done | bytes 229408 | tf_op jit(solution)/shard_map/ppermute | solution.py:182
  93.9 1.1 collective-permute-done.16
  95.2 2.1 collective-permute-start.18
  97.3 12.9 %collective-permute-done.18 = bf16[64,1792]{1,0:T(8,128)(2,1)S(1)} collective-permute-done((bf16[64,1792]{1,0:T(8,128)(2,1)S(1)}, bf16[64,1792]{1,0:T(8,128)(2,1)S(1)}, u32[]{:S(2)}, u32[]{:S(2)}) %collective-permute-start.18) | collective-permute-done | bytes 229408 | tf_op jit(solution)/shard_map/ppermute | solution.py:182
  110.3 0.7 copy-done.9
  111.0 1.5 collective-permute-done.17
  112.8 6.1 %convolution_convert_fusion.1 = bf16[256,2560]{1,0:T(8,128)(2,1)S(1)} fusion(bf16[256,1792]{1,0:T(8,128)(2,1)S(1)} %get-tuple-element.34, bf16[1792,2560]{1,0:T(8,128)(2,1)} %copy-done), kind=kOutput, calls=%fused_computation.1 | convolution fusion | flops 2349465600 | bytes 11403264 | tf_op jit(solution)/shard_map/dot_general | solution.py:194
  119.0 1.0 constant_dynamic-slice_fusion.11
  119.9 2.4 %collective-permute-done.20 = bf16[128,2560]{1,0:T(8,128)(2,1)} collective-permute-done((bf16[128,2560]{1,0:T(8,128)(2,1)}, bf16[128,2560]{1,0:T(8,128)(2,1)}, u32[]{:S(2)}, u32[]{:S(2)}) %collective-permute-start.20) | collective-permute-done | bytes 655392 | tf_op jit(solution)/shard_map/ppermute | solution.py:182
  122.4 2.1 fusion.8
  124.5 1.5 collective-permute-start.21
  126.0 6.1 %convolution_convert_fusion = bf16[256,2560]{1,0:T(8,128)(2,1)S(1)} fusion(bf16[256,1792]{1,0:T(8,128)(2,1)S(1)} %get-tuple-element.34, bf16[1792,2560]{1,0:T(8,128)(2,1)} %param.18), kind=kOutput, calls=%fused_computation | convolution fusion | flops 2349465600 | bytes 11403264 | tf_op jit(solution)/shard_map/dot_general | solution.py:194
  132.1 1.0 constant_dynamic-slice_fusion.9
  133.7 1.9 collective-permute-start.19
  135.7 1.1 collective-permute-done.25
  137.3 4.2 %collective-permute-done.21 = bf16[128,2560]{1,0:T(8,128)(2,1)} collective-permute-done((bf16[128,2560]{1,0:T(8,128)(2,1)}, bf16[128,2560]{1,0:T(8,128)(2,1)}, u32[]{:S(2)}, u32[]{:S(2)}) %collective-permute-start.21) | collective-permute-done | bytes 655392 | tf_op jit(solution)/shard_map/ppermute | solution.py:182
  141.6 5.6 %collective-permute-done.19 = bf16[64,1792]{1,0:T(8,128)(2,1)S(1)} collective-permute-done((bf16[64,1792]{1,0:T(8,128)(2,1)S(1)}, bf16[64,1792]{1,0:T(8,128)(2,1)S(1)}, u32[]{:S(2)}, u32[]{:S(2)}) %collective-permute-start.19) | collective-permute-done | bytes 229408 | tf_op jit(solution)/shard_map/ppermute | solution.py:182
  147.7 5.4 %convolution_convert_fusion.4 = bf16[128,2560]{1,0:T(8,128)(2,1)S(1)} fusion(bf16[1792,2560]{1,0:T(8,128)(2,1)} %param.18, bf16[128,1792]{1,0:T(8,128)(2,1)S(1)} %pad_maximum_fusion.13, f32[1792]{0:T(1024)S(1)} %copy-done.3), kind=kOutput, calls=%fused_computation.4 | convolution fusion | flops 1175420928 | bytes 10296320 | tf_op jit(solution)/shard_map/dot_general | solution.py:194
  153.6 1.4 convolution_convert_fusion.5
  156.3 1.7 shard_map.117
  158.0 1.6 collective-permute-done.27
  159.6 12.0 %collective-permute-done.28 = bf16[128,2560]{1,0:T(8,128)(2,1)S(1)} collective-permute-done((bf16[128,2560]{1,0:T(8,128)(2,1)S(1)}, bf16[128,2560]{1,0:T(8,128)(2,1)S(1)}, u32[]{:S(2)}, u32[]{:S(2)}) %collective-permute-start.28) | collective-permute-done | bytes 655392 | tf_op jit(solution)/shard_map/ppermute | solution.py:182
  171.6 1.4 convolution_convert_fusion.3
  173.2 1.4 convolution_convert_fusion.2
  176.0 1.1 collective-permute-done.29
  177.3 1.7 fusion.19
  180.0 1.2 collective-permute-done.32
  181.2 2.5 %convolution_convert_fusion.6 = bf16[256,1792]{1,0:T(8,128)(2,1)S(1)} fusion(bf16[2560,1792]{1,0:T(8,128)(2,1)S(1)} %shard_map.117, bf16[128,2560]{1,0:T(8,128)(2,1)S(1)} %collective-permute-done.32, bf16[64,2560]{1,0:T(8,128)(2,1)S(1)} %get-tuple-element.50, bf16[64,2560]{1,0:T(8,128)(2,1)S(1)} %get-tuple-element.49), kind=kOutput, calls=%fused_computation.6 | convolution fusion | flops 2353201152 | bytes 11403264 | tf_op jit(solution)/shard_map/dot_general | solution.py:194
  183.7 1.8 collective-permute-start.34
  185.6 0.8 pad_maximum_fusion.12
  186.4 9.8 %collective-permute-done.31 = bf16[128,2560]{1,0:T(8,128)(2,1)S(1)} collective-permute-done((bf16[128,2560]{1,0:T(8,128)(2,1)S(1)}, bf16[128,2560]{1,0:T(8,128)(2,1)S(1)}, u32[]{:S(2)}, u32[]{:S(2)}) %collective-permute-start.31) | collective-permute-done | bytes 655392 | tf_op jit(solution)/shard_map/ppermute | solution.py:182
  196.7 1.6 collective-permute-done.33
  198.4 4.8 %shard_map.118 = bf16[256,1792]{1,0:T(8,128)(2,1)S(1)} custom-call(bf16[256,2560]{1,0:T(8,128)(2,1)S(1)} %pad_maximum_fusion.rows, bf16[2560,1792]{1,0:T(8,128)(2,1)} %weight.7), custom_call_target="tpu_custom_call" | custom-call | flops 1024 | bytes 1024 | tf_op jit(solution)/shard_map/pallas_call | solution.py:228
  203.2 1.8 collective-permute-start.35
  205.0 15.7 %collective-permute-done.35 = bf16[2,64,1792]{2,1,0:T(8,128)(2,1)S(1)} collective-permute-done((bf16[2,64,1792]{2,1,0:T(8,128)(2,1)S(1)}, bf16[2,64,1792]{2,1,0:T(8,128)(2,1)S(1)}, u32[]{:S(2)}, u32[]{:S(2)}) %collective-permute-start.35) | collective-permute-done | bytes 458784 | tf_op jit(solution)/shard_map/ppermute | solution.py:182
  221.0 11.6 %collective-permute-done.36 = bf16[64,1792]{1,0:T(8,128)(2,1)S(1)} collective-permute-done((bf16[64,1792]{1,0:T(8,128)(2,1)S(1)}, bf16[64,1792]{1,0:T(8,128)(2,1)S(1)}, u32[]{:S(2)}, u32[]{:S(2)}) %collective-permute-start.36) | collective-permute-done | bytes 229408 | tf_op jit(solution)/shard_map/ppermute | solution.py:182
  232.8 0.8 pad_maximum_fusion.14
  (146 shorter events, 12.2 us)
Async XLA Ops:
  1.5 13.5 %collective-permute-start.2 = (bf16[288,128]{1,0:T(8,128)(2,1)S(1)}, bf16[288,128]{1,0:T(8,128)(2,1)S(1)}, u32[]{:S(2)}, u32[]{:S(2)}) collective-permute-start(bf16[288,128]{1,0:T(8,128)(2,1)S(1)} %constant_dynamic-slice_fusion.14), channel_id=1, source_target_pairs={{0,4},{4,8},{8,12},{1,5},{5,9},{9,13},{2,6},{6,10},{10,14},{3,7},{... | collective-permute-start | bytes 221192 | tf_op jit(solution)/shard_map/ppermute | solution.py:282
  6.5 8.5 %collective-permute-start.1 = (bf16[288,128]{1,0:T(8,128)(2,1)S(1)}, bf16[288,128]{1,0:T(8,128)(2,1)S(1)}, u32[]{:S(2)}, u32[]{:S(2)}) collective-permute-start(bf16[288,128]{1,0:T(8,128)(2,1)S(1)} %constant_dynamic-slice_fusion.14), channel_id=1, source_target_pairs={{0,8},{4,12},{1,9},{5,13},{2,10},{6,14},{3,11},{7,15},{16,24},{20,... | collective-permute-start | bytes 221192 | tf_op jit(solution)/shard_map/ppermute | solution.py:282
  11.0 4.0 %collective-permute-start = (bf16[288,128]{1,0:T(8,128)(2,1)S(1)}, bf16[288,128]{1,0:T(8,128)(2,1)S(1)}, u32[]{:S(2)}, u32[]{:S(2)}) collective-permute-start(bf16[288,128]{1,0:T(8,128)(2,1)S(1)} %constant_dynamic-slice_fusion.14), channel_id=1, source_target_pairs={{0,12},{1,13},{2,14},{3,15},{16,28},{17,29},{18,30},{19,31}} | collective-permute-start | bytes 221192 | tf_op jit(solution)/shard_map/ppermute | solution.py:282
  14.6 2.0 copy-start.8
  15.0 1.5 collective-permute-start.3
  16.6 1.6 copy-start.2
  16.8 2.2 copy-start.1
  25.8 5.5 %collective-permute-start.6 = (bf16[32,2048]{1,0:T(8,128)(2,1)S(1)}, bf16[32,2048]{1,0:T(8,128)(2,1)S(1)}, u32[]{:S(2)}, u32[]{:S(2)}) collective-permute-start(bf16[32,2048]{1,0:T(8,128)(2,1)S(1)} %get-tuple-element.78), channel_id=1, source_target_pairs={{0,3},{1,2},{2,1},{3,0},{4,7},{5,6},{6,5},{7,4},{8,11},{9,10},{10,... | collective-permute-start | bytes 393224 | tf_op jit(solution)/shard_map/ppermute | solution.py:182
  27.1 7.4 %collective-permute-start.5 = (bf16[32,2048]{1,0:T(8,128)(2,1)S(1)}, bf16[32,2048]{1,0:T(8,128)(2,1)S(1)}, u32[]{:S(2)}, u32[]{:S(2)}) collective-permute-start(bf16[32,2048]{1,0:T(8,128)(2,1)S(1)} %get-tuple-element.79), channel_id=1, source_target_pairs={{0,2},{1,3},{2,0},{3,1},{4,6},{5,7},{6,4},{7,5},{8,10},{9,11},{10,... | collective-permute-start | bytes 393224 | tf_op jit(solution)/shard_map/ppermute | solution.py:182
  27.7 6.8 %collective-permute-start.4 = (bf16[32,2048]{1,0:T(8,128)(2,1)S(1)}, bf16[32,2048]{1,0:T(8,128)(2,1)S(1)}, u32[]{:S(2)}, u32[]{:S(2)}) collective-permute-start(bf16[32,2048]{1,0:T(8,128)(2,1)S(1)} %get-tuple-element.80), channel_id=1, source_target_pairs={{0,1},{1,0},{2,3},{3,2},{4,5},{5,4},{6,7},{7,6},{8,9},{9,8},{10,11... | collective-permute-start | bytes 393224 | tf_op jit(solution)/shard_map/ppermute | solution.py:182
  34.6 8.3 %collective-permute-start.9 = (bf16[32,2048]{1,0:T(8,128)(2,1)S(1)}, bf16[32,2048]{1,0:T(8,128)(2,1)S(1)}, u32[]{:S(2)}, u32[]{:S(2)}) collective-permute-start(bf16[32,2048]{1,0:T(8,128)(2,1)S(1)} %get-tuple-element.74), channel_id=1, source_target_pairs={{0,12},{4,8},{8,4},{12,0},{1,13},{5,9},{9,5},{13,1},{2,14},{6,10},... | collective-permute-start | bytes 393224 | tf_op jit(solution)/shard_map/ppermute | solution.py:182
  38.3 10.2 %collective-permute-start.8 = (bf16[32,2048]{1,0:T(8,128)(2,1)S(1)}, bf16[32,2048]{1,0:T(8,128)(2,1)S(1)}, u32[]{:S(2)}, u32[]{:S(2)}) collective-permute-start(bf16[32,2048]{1,0:T(8,128)(2,1)S(1)} %get-tuple-element.75), channel_id=1, source_target_pairs={{0,8},{4,12},{8,0},{12,4},{1,9},{5,13},{9,1},{13,5},{2,10},{6,14},... | collective-permute-start | bytes 393224 | tf_op jit(solution)/shard_map/ppermute | solution.py:182
  38.3 10.2 %collective-permute-start.7 = (bf16[32,2048]{1,0:T(8,128)(2,1)S(1)}, bf16[32,2048]{1,0:T(8,128)(2,1)S(1)}, u32[]{:S(2)}, u32[]{:S(2)}) collective-permute-start(bf16[32,2048]{1,0:T(8,128)(2,1)S(1)} %get-tuple-element.76), channel_id=1, source_target_pairs={{0,4},{4,0},{8,12},{12,8},{1,5},{5,1},{9,13},{13,9},{2,6},{6,2},{1... | collective-permute-start | bytes 393224 | tf_op jit(solution)/shard_map/ppermute | solution.py:182
  48.6 2.0 collective-permute-start.10
  48.6 14.3 %collective-permute-start.13 = (bf16[4,32,2048]{2,1,0:T(8,128)(2,1)S(1)}, bf16[4,32,2048]{2,1,0:T(8,128)(2,1)S(1)}, u32[]{:S(2)}, u32[]{:S(2)}) collective-permute-start(bf16[4,32,2048]{2,1,0:T(8,128)(2,1)S(1)} %pad_maximum_fusion.10), channel_id=1, source_target_pairs={{0,2},{1,3},{2,0},{3,1},{4,6},{5,7},{6,4},{7,5},{8,10},{9,11},{10,... | collective-permute-start | bytes 1572872 | tf_op jit(solution)/shard_map/ppermute | solution.py:182
  55.0 12.6 %collective-permute-start.11 = (bf16[2,64,1792]{2,1,0:T(8,128)(2,1)S(1)}, bf16[2,64,1792]{2,1,0:T(8,128)(2,1)S(1)}, u32[]{:S(2)}, u32[]{:S(2)}) collective-permute-start(bf16[2,64,1792]{2,1,0:T(8,128)(2,1)S(1)} %slice_bitcast_fusion.5), channel_id=1, source_target_pairs={{0,4},{4,0},{8,12},{12,8},{1,5},{5,1},{9,13},{13,9},{2,6},{6,2},{1... | collective-permute-start | bytes 1376264 | tf_op jit(solution)/shard_map/ppermute | solution.py:182
  63.0 6.2 %collective-permute-start.14 = (bf16[4,32,2048]{2,1,0:T(8,128)(2,1)S(1)}, bf16[4,32,2048]{2,1,0:T(8,128)(2,1)S(1)}, u32[]{:S(2)}, u32[]{:S(2)}) collective-permute-start(bf16[4,32,2048]{2,1,0:T(8,128)(2,1)S(1)} %collective-permute-done.13), channel_id=1, source_target_pairs={{0,1},{1,0},{2,3},{3,2},{4,5},{5,4},{6,7},{7,6},{8,9},{9,8},{10,11... | collective-permute-start | bytes 1572872 | tf_op jit(solution)/shard_map/ppermute | solution.py:182
  67.7 12.8 %collective-permute-start.12 = (bf16[64,1792]{1,0:T(8,128)(2,1)S(1)}, bf16[64,1792]{1,0:T(8,128)(2,1)S(1)}, u32[]{:S(2)}, u32[]{:S(2)}) collective-permute-start(bf16[64,1792]{1,0:T(8,128)(2,1)S(1)} %fusion.25), channel_id=1, source_target_pairs={{0,8},{4,12},{8,0},{12,4},{1,9},{5,13},{9,1},{13,5},{2,10},{6,14},... | collective-permute-start | bytes 688136 | tf_op jit(solution)/shard_map/ppermute | solution.py:182
  69.4 11.1 %copy-start.4 = (bf16[128,1792]{1,0:T(8,128)(2,1)S(1)}, bf16[128,1792]{1,0:T(8,128)(2,1)}, u32[]{:S(2)}) copy-start(bf16[128,1792]{1,0:T(8,128)(2,1)} %param.10) | copy-start | bytes 1376260
  73.6 21.4 %collective-permute-start.16 = (bf16[2,64,1792]{2,1,0:T(8,128)(2,1)S(1)}, bf16[2,64,1792]{2,1,0:T(8,128)(2,1)S(1)}, u32[]{:S(2)}, u32[]{:S(2)}) collective-permute-start(bf16[2,64,1792]{2,1,0:T(8,128)(2,1)S(1)} %slice_bitcast_fusion.4), channel_id=1, source_target_pairs={{0,4},{4,0},{8,12},{12,8},{1,5},{5,1},{9,13},{13,9},{2,6},{6,2},{1... | collective-permute-start | bytes 1376264 | tf_op jit(solution)/shard_map/ppermute | solution.py:182
  80.6 13.3 %collective-permute-start.15 = (bf16[64,1792]{1,0:T(8,128)(2,1)S(1)}, bf16[64,1792]{1,0:T(8,128)(2,1)S(1)}, u32[]{:S(2)}, u32[]{:S(2)}) collective-permute-start(bf16[64,1792]{1,0:T(8,128)(2,1)S(1)} %fusion.28), channel_id=1, source_target_pairs={{0,8},{4,12},{8,0},{12,4},{1,9},{5,13},{9,1},{13,5},{2,10},{6,14},... | collective-permute-start | bytes 688136 | tf_op jit(solution)/shard_map/ppermute | solution.py:182
  84.4 3.6 %copy-start = (bf16[1792,2560]{1,0:T(8,128)(2,1)}, bf16[1792,2560]{1,0:T(8,128)(2,1)S(1)}, u32[]{:S(2)}) copy-start(bf16[1792,2560]{1,0:T(8,128)(2,1)S(1)} %shard_map.116) | copy-start | bytes 27525124
  88.0 24.5 %copy-start.3 = (f32[1792]{0:T(1024)S(1)}, f32[1792]{0:T(1024)}, u32[]{:S(2)}) copy-start(f32[1792]{0:T(1024)} %param.16) | copy-start | bytes 21508
  95.1 15.2 %copy-start.6 = (bf16[2,64,1792]{2,1,0:T(8,128)(2,1)}, bf16[2,64,1792]{2,1,0:T(8,128)(2,1)S(1)}, u32[]{:S(2)}) copy-start(bf16[2,64,1792]{2,1,0:T(8,128)(2,1)S(1)} %collective-permute-done.16) | copy-start | bytes 1376260
  95.1 17.4 %collective-permute-start.17 = (bf16[128,1792]{1,0:T(8,128)(2,1)S(1)}, bf16[128,1792]{1,0:T(8,128)(2,1)S(1)}, u32[]{:S(2)}, u32[]{:S(2)}) collective-permute-start(bf16[128,1792]{1,0:T(8,128)(2,1)S(1)} %pad_maximum_fusion.11), channel_id=1, source_target_pairs={{0,4},{4,0},{8,12},{12,8},{1,5},{5,1},{9,13},{13,9},{2,6},{6,2},{1... | collective-permute-start | bytes 1376264 | tf_op jit(solution)/shard_map/ppermute | solution.py:182
  95.2 15.0 %collective-permute-start.18 = (bf16[64,1792]{1,0:T(8,128)(2,1)S(1)}, bf16[64,1792]{1,0:T(8,128)(2,1)S(1)}, u32[]{:S(2)}, u32[]{:S(2)}) collective-permute-start(bf16[64,1792]{1,0:T(8,128)(2,1)S(1)} %fusion.21), channel_id=1, source_target_pairs={{0,8},{4,12},{8,0},{12,4},{1,9},{5,13},{9,1},{13,5},{2,10},{6,14},... | collective-permute-start | bytes 688136 | tf_op jit(solution)/shard_map/ppermute | solution.py:182
  110.3 0.7 copy-start.9
  119.9 2.4 %collective-permute-start.20 = (bf16[128,2560]{1,0:T(8,128)(2,1)}, bf16[128,2560]{1,0:T(8,128)(2,1)}, u32[]{:S(2)}, u32[]{:S(2)}) collective-permute-start(bf16[128,2560]{1,0:T(8,128)(2,1)} %bitcast.44), channel_id=1, source_target_pairs={{0,1},{1,0},{2,3},{3,2},{4,5},{5,4},{6,7},{7,6},{8,9},{9,8},{10,11... | collective-permute-start | bytes 1966088 | tf_op jit(solution)/shard_map/ppermute | solution.py:182
  124.5 17.1 %collective-permute-start.21 = (bf16[128,2560]{1,0:T(8,128)(2,1)}, bf16[128,2560]{1,0:T(8,128)(2,1)}, u32[]{:S(2)}, u32[]{:S(2)}) collective-permute-start(bf16[128,2560]{1,0:T(8,128)(2,1)} %fusion.8), channel_id=1, source_target_pairs={{0,2},{1,3},{2,0},{3,1},{4,6},{5,7},{6,4},{7,5},{8,10},{9,11},{10,... | collective-permute-start | bytes 1966088 | tf_op jit(solution)/shard_map/ppermute | solution.py:182
  132.1 1.0 copy-start.5
  132.1 1.4 copy-start.7
  132.1 1.4 copy-start.10
  133.1 4.3 %collective-permute-start.22 = (bf16[128,2560]{1,0:T(8,128)(2,1)}, bf16[128,2560]{1,0:T(8,128)(2,1)S(1)}, u32[]{:S(2)}, u32[]{:S(2)}) collective-permute-start(bf16[128,2560]{1,0:T(8,128)(2,1)} %bitcast.47), channel_id=1, source_target_pairs={{0,1},{1,0},{2,3},{3,2},{4,5},{5,4},{6,7},{7,6},{8,9},{9,8},{10,11... | collective-permute-start | bytes 1966088 | tf_op jit(solution)/shard_map/ppermute | solution.py:182
  133.7 13.4 %collective-permute-start.19 = (bf16[64,1792]{1,0:T(8,128)(2,1)S(1)}, bf16[64,1792]{1,0:T(8,128)(2,1)S(1)}, u32[]{:S(2)}, u32[]{:S(2)}) collective-permute-start(bf16[64,1792]{1,0:T(8,128)(2,1)S(1)} %get-tuple-element.48), channel_id=1, source_target_pairs={{0,8},{4,12},{8,0},{12,4},{1,9},{5,13},{9,1},{13,5},{2,10},{6,14},... | collective-permute-start | bytes 688136 | tf_op jit(solution)/shard_map/ppermute | solution.py:182
  135.7 1.1 collective-permute-start.25
  136.8 38.8 %collective-permute-start.26 = (f32[256]{0:T(256)S(1)}, f32[256]{0:T(256)S(1)}, u32[]{:S(2)}, u32[]{:S(2)}) collective-permute-start(f32[256]{0:T(256)S(1)} %add.261), channel_id=1, source_target_pairs={{0,2},{1,3},{2,0},{3,1},{4,6},{5,7},{6,4},{7,5},{8,10},{9,11},{10,... | collective-permute-start | bytes 3080 | tf_op jit(solution)/shard_map/ppermute | solution.py:182
  147.2 12.5 %collective-permute-start.27 = (bf16[128,1792]{1,0:T(8,128)(2,1)S(1)}, bf16[128,1792]{1,0:T(8,128)(2,1)S(1)}, u32[]{:S(2)}, u32[]{:S(2)}) collective-permute-start(bf16[128,1792]{1,0:T(8,128)(2,1)S(1)} %pad_maximum_fusion.13), channel_id=1, source_target_pairs={{0,4},{4,0},{8,12},{12,8},{1,5},{5,1},{9,13},{13,9},{2,6},{6,2},{1... | collective-permute-start | bytes 1376264 | tf_op jit(solution)/shard_map/ppermute | solution.py:182
  147.3 5.9 %slice-start = ((s8[9175040]{0:T(1024)(128)(4,1)}), s8[4194304]{0:T(1024)(128)(4,1)S(1)}, s32[]{:S(2)}) async-start(s8[9175040]{0:T(1024)(128)(4,1)} %bitcast.164), calls=%async_computation | async-start | bytes 8388608
  147.7 5.8 %slice-start.1 = ((s8[9175040]{0:T(1024)(128)(4,1)}), s8[4194304]{0:T(1024)(128)(4,1)S(1)}, s32[]{:S(2)}) async-start(s8[9175040]{0:T(1024)(128)(4,1)} %bitcast.164), calls=%async_computation.1 | async-start | bytes 8388608
  147.7 5.9 %slice-start.2 = ((s8[9175040]{0:T(1024)(128)(4,1)}), s8[786432]{0:T(1024)(128)(4,1)S(1)}, s32[]{:S(2)}) async-start(s8[9175040]{0:T(1024)(128)(4,1)} %bitcast.164), calls=%async_computation.2 | async-start | bytes 1572864
  147.7 8.6 %slice-start.3 = ((s8[9175040]{0:T(1024)(128)(4,1)}), s8[4194304]{0:T(1024)(128)(4,1)S(1)}, s32[]{:S(2)}) async-start(s8[9175040]{0:T(1024)(128)(4,1)} %bitcast.166), calls=%async_computation.3 | async-start | bytes 8388608
  147.7 8.6 %slice-start.4 = ((s8[9175040]{0:T(1024)(128)(4,1)}), s8[4194304]{0:T(1024)(128)(4,1)S(1)}, s32[]{:S(2)}) async-start(s8[9175040]{0:T(1024)(128)(4,1)} %bitcast.166), calls=%async_computation.4 | async-start | bytes 8388608
  153.6 2.7 %slice-start.5 = ((s8[9175040]{0:T(1024)(128)(4,1)}), s8[786432]{0:T(1024)(128)(4,1)S(1)}, s32[]{:S(2)}) async-start(s8[9175040]{0:T(1024)(128)(4,1)} %bitcast.166), calls=%async_computation.5 | async-start | bytes 1572864
  154.9 16.7 %collective-permute-start.28 = (bf16[128,2560]{1,0:T(8,128)(2,1)S(1)}, bf16[128,2560]{1,0:T(8,128)(2,1)S(1)}, u32[]{:S(2)}, u32[]{:S(2)}) collective-permute-start(bf16[128,2560]{1,0:T(8,128)(2,1)S(1)} %fusion.7), channel_id=1, source_target_pairs={{0,2},{1,3},{2,0},{3,1},{4,6},{5,7},{6,4},{7,5},{8,10},{9,11},{10,... | collective-permute-start | bytes 1966088 | tf_op jit(solution)/shard_map/ppermute | solution.py:182
  155.5 20.0 %collective-permute-start.24 = (f32[128]{0:T(128)S(1)}, f32[128]{0:T(128)S(1)}, u32[]{:S(2)}, u32[]{:S(2)}) collective-permute-start(f32[128]{0:T(128)S(1)} %fusion.10), channel_id=1, source_target_pairs={{0,1},{1,0},{2,3},{3,2},{4,5},{5,4},{6,7},{7,6},{8,9},{9,8},{10,11... | collective-permute-start | bytes 1544 | tf_op jit(solution)/shard_map/ppermute | solution.py:182
  155.7 19.7 %collective-permute-start.23 = (bf16[128,2560]{1,0:T(8,128)(2,1)S(1)}, bf16[128,2560]{1,0:T(8,128)(2,1)S(1)}, u32[]{:S(2)}, u32[]{:S(2)}) collective-permute-start(bf16[128,2560]{1,0:T(8,128)(2,1)S(1)} %pad_maximum_fusion.4), channel_id=1, source_target_pairs={{0,1},{1,0},{2,3},{3,2},{4,5},{5,4},{6,7},{7,6},{8,9},{9,8},{10,11... | collective-permute-start | bytes 1966088 | tf_op jit(solution)/shard_map/ppermute | solution.py:182
  156.3 16.9 %slice-start.6 = ((s8[9175040]{0:T(1024)(128)(4,1)}), s8[786432]{0:T(1024)(128)(4,1)S(1)}, s32[]{:S(2)}) async-start(s8[9175040]{0:T(1024)(128)(4,1)} %bitcast.179), calls=%async_computation.6 | async-start | bytes 1572864
  156.3 16.9 %slice-start.7 = ((s8[9175040]{0:T(1024)(128)(4,1)}), s8[4194304]{0:T(1024)(128)(4,1)S(1)}, s32[]{:S(2)}) async-start(s8[9175040]{0:T(1024)(128)(4,1)} %bitcast.179), calls=%async_computation.7 | async-start | bytes 8388608
  158.0 15.2 %slice-start.8 = ((s8[9175040]{0:T(1024)(128)(4,1)}), s8[4194304]{0:T(1024)(128)(4,1)S(1)}, s32[]{:S(2)}) async-start(s8[9175040]{0:T(1024)(128)(4,1)} %bitcast.179), calls=%async_computation.8 | async-start | bytes 8388608
  174.6 1.2 collective-permute-start.30
  174.8 2.3 collective-permute-start.29
  179.0 2.2 collective-permute-start.32
  179.4 16.8 %collective-permute-start.31 = (bf16[128,2560]{1,0:T(8,128)(2,1)S(1)}, bf16[128,2560]{1,0:T(8,128)(2,1)S(1)}, u32[]{:S(2)}, u32[]{:S(2)}) collective-permute-start(bf16[128,2560]{1,0:T(8,128)(2,1)S(1)} %pad_maximum_fusion.6), channel_id=1, source_target_pairs={{0,2},{1,3},{2,0},{3,1},{4,6},{5,7},{6,4},{7,5},{8,10},{9,11},{10,... | collective-permute-start | bytes 1966088 | tf_op jit(solution)/shard_map/ppermute | solution.py:182
  183.7 12.9 %collective-permute-start.34 = (bf16[2,64,1792]{2,1,0:T(8,128)(2,1)S(1)}, bf16[2,64,1792]{2,1,0:T(8,128)(2,1)S(1)}, u32[]{:S(2)}, u32[]{:S(2)}) collective-permute-start(bf16[2,64,1792]{2,1,0:T(8,128)(2,1)S(1)} %slice_bitcast_fusion.2), channel_id=1, source_target_pairs={{0,4},{4,0},{8,12},{12,8},{1,5},{5,1},{9,13},{13,9},{2,6},{6,2},{1... | collective-permute-start | bytes 1376264 | tf_op jit(solution)/shard_map/ppermute | solution.py:182
  196.2 2.1 collective-permute-start.33
  203.2 17.5 %collective-permute-start.35 = (bf16[2,64,1792]{2,1,0:T(8,128)(2,1)S(1)}, bf16[2,64,1792]{2,1,0:T(8,128)(2,1)S(1)}, u32[]{:S(2)}, u32[]{:S(2)}) collective-permute-start(bf16[2,64,1792]{2,1,0:T(8,128)(2,1)S(1)} %slice_bitcast_fusion), channel_id=1, source_target_pairs={{0,4},{4,0},{8,12},{12,8},{1,5},{5,1},{9,13},{13,9},{2,6},{6,2},{1... | collective-permute-start | bytes 1376264 | tf_op jit(solution)/shard_map/ppermute | solution.py:182
  205.0 16.0 %collective-permute-start.37 = (bf16[64,1792]{1,0:T(8,128)(2,1)S(1)}, bf16[64,1792]{1,0:T(8,128)(2,1)S(1)}, u32[]{:S(2)}, u32[]{:S(2)}) collective-permute-start(bf16[64,1792]{1,0:T(8,128)(2,1)S(1)} %fusion.37), channel_id=1, source_target_pairs={{0,8},{4,12},{8,0},{12,4},{1,9},{5,13},{9,1},{13,5},{2,10},{6,14},... | collective-permute-start | bytes 688136 | tf_op jit(solution)/shard_map/ppermute | solution.py:182
  220.9 11.7 %collective-permute-start.36 = (bf16[64,1792]{1,0:T(8,128)(2,1)S(1)}, bf16[64,1792]{1,0:T(8,128)(2,1)S(1)}, u32[]{:S(2)}, u32[]{:S(2)}) collective-permute-start(bf16[64,1792]{1,0:T(8,128)(2,1)S(1)} %fusion.38), channel_id=1, source_target_pairs={{0,8},{4,12},{8,0},{12,4},{1,9},{5,13},{9,1},{13,5},{2,10},{6,14},... | collective-permute-start | bytes 688136 | tf_op jit(solution)/shard_map/ppermute | solution.py:182

commit v13 on v12

--- a/solution.py
+++ b/solution.py
@@ -160,7 +160,7 @@
             pltpu.VMEM((key_count, LAT), jnp.bfloat16),
             pltpu.VMEM((row_count, key_count), jnp.float32),
         ],
-        compiler_params=pltpu.CompilerParams(vmem_limit_bytes=(6 + key_count // 64) * 1024 * 1024),
+        compiler_params=pltpu.CompilerParams(vmem_limit_bytes=min(40 + key_count // 64, 56) * 1024 * 1024),
         cost_estimate=pl.CostEstimate(
             flops=2 * row_count * local_heads * (key_count * (deep + LAT) + LAT * VHEAD),
             bytes_accessed=2 * (queries.size + keys.size + value_weight.size),
@@ -224,9 +224,10 @@
 
 
 def streamed_matmul(rows, weight):
-    steps = weight.shape[0] // 512
+    depth = 512 if weight.shape[0] % 512 == 0 else 256
+    steps = weight.shape[0] // depth
     return pl.pallas_call(
-        functools.partial(streamed_kernel, 512),
+        functools.partial(streamed_kernel, depth),
         in_specs=[
             pl.BlockSpec(memory_space=pltpu.VMEM),
             pl.BlockSpec(memory_space=pl.ANY),
@@ -359,8 +360,6 @@
     kept_b, sent_b, came_b = first_hop(core_rows(far, after(far_near, other_a)))
     attended_a = attend(mine_a, after(last_a, sent_b), first_half)
     twin_a = swap(attended_a, "ctx", 2)
-    gate_weight = load(after(gate_weight, attended_a), 44)
-    twin_a, came_b, gate_weight = lax.optimization_barrier((twin_a, came_b, gate_weight))
     pair_a = jnp.concatenate([attended_a, twin_a], axis=0)
     rest_a = swap(pair_a, "ctx", 1)
     mine_b, other_b, last_b = second_hop(kept_b, after(came_b, pair_a))
@@ -370,20 +369,19 @@
     all_a = jnp.concatenate([pair_a, rest_a], axis=0)
     squares_a, scaled = scale(all_a)
 
-    def cross(rows, weight, earlier):
+    def cross(rows, weight):
         term = matmul(rows, weight).reshape(2, 2, half, -1)
 
         def side(which):
             return lax.dynamic_index_in_dim(term, which, 1, keepdims=False).reshape(2 * half, -1)
 
-        came = swap(side(1 - core), "tp", 1)
-        if earlier is not None:
-            came = after(came, earlier)
-        total = (wide(side(core)) + wide(came)).astype(jnp.bfloat16)
-        return total, swap(total, "tp", 2)
-
-    sums_gate, across_gate = cross(scaled, gate_weight, None)
-    sums_up, across_up = cross(after(scaled, sums_gate), up_weight, across_gate)
+        sent = side(1 - core)
+        total = chip_sum(side(core), sent).astype(jnp.bfloat16)
+        return sent, total, swap(total, "tp", 2)
+
+    sent_gate, _, across_gate = cross(scaled, gate_weight)
+    _, sums_up, across_up = cross(after(scaled, sent_gate), up_weight)
+    squares_a = after(squares_a, sums_up)
     across_squares = swap(squares_a + swap(squares_a, "tp", 1), "tp", 2)
     pair_b = jnp.concatenate([attended_b, after(twin_b, across_gate)], axis=0)
     rest_b = swap(pair_b, "ctx", 1)
@@ -466,6 +464,8 @@
         and residual.shape[1] % 256 == 0
         and output_weight.shape[0] % 512 == 0
         and down_weight.shape[0] % 512 == 0
+        and gate_weight.shape[0] % 256 == 0
+        and gate_weight.shape[1] % 256 == 0
     )
     own_index = ctx_place * row_count + jnp.arange(row_count, dtype=jnp.int32)
     _, own_position = trace_info(own_index, lengths)

time: 234 us -> 224 us (0.957)
  waiting for transfers between devices: 125 us -> 119 us
  Pallas kernels: 25.2 us -> 21.5 us
  local copies, waits for them, and re-layouts: 10.6 us -> 7.4 us
    ppermute x35, waiting for transfers between devices: 125 us -> 119 us  [swap(): return lax.ppermute(value, axis_name, [(i, i ^ bit) for i in range(width)])]
    pallas_call x2 -> x1, Pallas kernels: 5.37 us -> 1.67 us  [load(): pl.pallas_call(functools.partial(load_kernel, chunks), in_specs=[pl.Block...]
    unnamed x42 -> x44, local copies, waits for them, and re-layouts: 7.01 us -> 5.56 us
  transfers between devices with their start and end apart: 38 -> 38, of which waited for: 27 -> 24; matrix products, arithmetic and copies ran while one was open for 11% -> 12% of each run, Pallas kernels for 6% -> 4%
where the time goes in v13:
time: 224 us; the launch traced here: 223 us
  waiting for transfers between devices  119 us (53%)
  starting transfers between devices  37.3 us (17%)
  matrix products  24.5 us (11%)
  Pallas kernels  21.5 us (10%)
  other arithmetic  11.8 us (5%)
  local copies, waits for them, and re-layouts  7.4 us (3%)
    ppermute x35, waiting for transfers between devices, swap(): return lax.ppermute(value, axis_name, [(i, i ^ bit) for i in range(width)])  119 us
    ppermute x35, starting transfers between devices, swap(): return lax.ppermute(value, axis_name, [(i, i ^ bit) for i in range(width)])  26.6 us
    dot_general x7, matrix products, matmul(): jnp.dot(a, b, preferred_element_type=jnp.float32).astype(jnp.bfloat16)  24.5 us
    pallas_call x3, Pallas kernels, streamed_matmul(): pl.pallas_call(functools.partial(streamed_kernel, depth), in_specs=[pl.Bl...  13.1 us
    ppermute x3, starting transfers between devices, gather_keys(): lax.ppermute(half, 'ctx', [(c, c + d) for c in range(n_ctx - d)])  10.7 us
    pallas_call x1, Pallas kernels, attention(): pl.pallas_call(functools.partial(attention_kernel, group), grid=(local_he...  6.79 us
    unnamed x44, local copies, waits for them, and re-layouts  5.56 us
  transfers between devices with their start and end apart: 38, of which 24 were waited for; matrix products, arithmetic and copies ran while one was open for 12% of the time, Pallas kernels for 4%

profile of v13, /device:TPU:0, one launch (start us, length us, event | category | flops | bytes accessed | tf_op | source)
XLA Modules:
  0.0 223.1 jit_solution(16731435261990057260)
XLA Ops:
  0.6 0.9 constant_dynamic-slice_fusion.14
  1.5 4.9 %collective-permute-start.2 = (bf16[288,128]{1,0:T(8,128)(2,1)S(1)}, bf16[288,128]{1,0:T(8,128)(2,1)S(1)}, u32[]{:S(2)}, u32[]{:S(2)}) collective-permute-start(bf16[288,128]{1,0:T(8,128)(2,1)S(1)} %constant_dynamic-slice_fusion.14), channel_id=1, source_target_pairs={{0,4},{4,8},{8,12},{1,5},{5,9},{9,13},{2,6},{6,10},{10,14},{3,7},{... | collective-permute-start | bytes 221192 | tf_op jit(solution)/shard_map/ppermute | solution.py:283
  6.5 4.5 %collective-permute-start.1 = (bf16[288,128]{1,0:T(8,128)(2,1)S(1)}, bf16[288,128]{1,0:T(8,128)(2,1)S(1)}, u32[]{:S(2)}, u32[]{:S(2)}) collective-permute-start(bf16[288,128]{1,0:T(8,128)(2,1)S(1)} %constant_dynamic-slice_fusion.14), channel_id=1, source_target_pairs={{0,8},{4,12},{1,9},{5,13},{2,10},{6,14},{3,11},{7,15},{16,24},{20,... | collective-permute-start | bytes 221192 | tf_op jit(solution)/shard_map/ppermute | solution.py:283
  11.0 1.3 collective-permute-start
  12.3 0.8 reduce-window.8
  13.2 0.7 subtract_subtract_fusion
  15.1 1.5 collective-permute-done.3
  17.2 1.0 copy-done.1
  18.2 0.7 copy-done
  19.0 6.8 %shard_map.113 = bf16[128,2048]{1,0:T(8,128)(2,1)S(1)} custom-call(f32[4,128,128]{2,1,0:T(8,128)S(1)} %pad_maximum_fusion.15.tables, s32[128,1]{1,0:T(8,128)S(1)} %copy.23.starts, s32[128,1]{1,0:T(8,128)S(1)} %iota_add_fusion.own_index, s32[1,512]{1,0:T(1,128)S(1)} %iota_add_fusion.2.key_index, bf16[576,512]{1,0:T(8,128)(2,1)S(1)} %pad_maximum_fusion.8.keys, ...), custom_call_target="tpu_custom_call" | custom-call | flops 2684354560 | bytes 5046272 | tf_op jit(solution)/shard_map/pallas_call | solution.py:143
  25.8 1.3 collective-permute-start.6
  27.7 3.6 %collective-permute-done.6 = bf16[32,2048]{1,0:T(8,128)(2,1)S(1)} collective-permute-done((bf16[32,2048]{1,0:T(8,128)(2,1)S(1)}, bf16[32,2048]{1,0:T(8,128)(2,1)S(1)}, u32[]{:S(2)}, u32[]{:S(2)}) %collective-permute-start.6) | collective-permute-done | bytes 131104 | tf_op jit(solution)/shard_map/ppermute | solution.py:182
  31.4 3.1 %collective-permute-done.5 = bf16[32,2048]{1,0:T(8,128)(2,1)S(1)} collective-permute-done((bf16[32,2048]{1,0:T(8,128)(2,1)S(1)}, bf16[32,2048]{1,0:T(8,128)(2,1)S(1)}, u32[]{:S(2)}, u32[]{:S(2)}) %collective-permute-start.5) | collective-permute-done | bytes 131104 | tf_op jit(solution)/shard_map/ppermute | solution.py:182
  34.6 3.7 %collective-permute-start.9 = (bf16[32,2048]{1,0:T(8,128)(2,1)S(1)}, bf16[32,2048]{1,0:T(8,128)(2,1)S(1)}, u32[]{:S(2)}, u32[]{:S(2)}) collective-permute-start(bf16[32,2048]{1,0:T(8,128)(2,1)S(1)} %get-tuple-element.66), channel_id=1, source_target_pairs={{0,12},{4,8},{8,4},{12,0},{1,13},{5,9},{9,5},{13,1},{2,14},{6,10},... | collective-permute-start | bytes 393224 | tf_op jit(solution)/shard_map/ppermute | solution.py:182
  38.3 0.8 collective-permute-start.7
  39.1 3.8 %collective-permute-done.9 = bf16[32,2048]{1,0:T(8,128)(2,1)S(1)} collective-permute-done((bf16[32,2048]{1,0:T(8,128)(2,1)S(1)}, bf16[32,2048]{1,0:T(8,128)(2,1)S(1)}, u32[]{:S(2)}, u32[]{:S(2)}) %collective-permute-start.9) | collective-permute-done | bytes 131104 | tf_op jit(solution)/shard_map/ppermute | solution.py:182
  42.9 5.6 %collective-permute-done.8 = bf16[32,2048]{1,0:T(8,128)(2,1)S(1)} collective-permute-done((bf16[32,2048]{1,0:T(8,128)(2,1)S(1)}, bf16[32,2048]{1,0:T(8,128)(2,1)S(1)}, u32[]{:S(2)}, u32[]{:S(2)}) %collective-permute-start.8) | collective-permute-done | bytes 131104 | tf_op jit(solution)/shard_map/ppermute | solution.py:182
  48.6 1.5 collective-permute-start.13
  50.8 4.1 %shard_map.114 = bf16[256,1792]{1,0:T(8,128)(2,1)S(1)} custom-call(bf16[256,2048]{1,0:T(8,128)(2,1)S(1)} %bitcast.167, bf16[2048,1792]{1,0:T(8,128)(2,1)} %weight.4), custom_call_target="tpu_custom_call" | custom-call | flops 1024 | bytes 1024 | tf_op jit(solution)/shard_map/pallas_call | solution.py:229
  55.0 0.8 collective-permute-start.11
  55.7 7.2 %collective-permute-done.13 = bf16[4,32,2048]{2,1,0:T(8,128)(2,1)S(1)} collective-permute-done((bf16[4,32,2048]{2,1,0:T(8,128)(2,1)S(1)}, bf16[4,32,2048]{2,1,0:T(8,128)(2,1)S(1)}, u32[]{:S(2)}, u32[]{:S(2)}) %collective-permute-start.13) | collective-permute-done | bytes 524320 | tf_op jit(solution)/shard_map/ppermute | solution.py:182
  63.0 4.6 %collective-permute-done.11 = bf16[2,64,1792]{2,1,0:T(8,128)(2,1)S(1)} collective-permute-done((bf16[2,64,1792]{2,1,0:T(8,128)(2,1)S(1)}, bf16[2,64,1792]{2,1,0:T(8,128)(2,1)S(1)}, u32[]{:S(2)}, u32[]{:S(2)}) %collective-permute-start.11) | collective-permute-done | bytes 458784 | tf_op jit(solution)/shard_map/ppermute | solution.py:182
  67.7 1.5 collective-permute-start.12
  69.4 4.2 %shard_map.115 = bf16[256,1792]{1,0:T(8,128)(2,1)S(1)} custom-call(bf16[256,2048]{1,0:T(8,128)(2,1)S(1)} %bitcast.166, bf16[2048,1792]{1,0:T(8,128)(2,1)} %weight.4), custom_call_target="tpu_custom_call" | custom-call | flops 1024 | bytes 1024 | tf_op jit(solution)/shard_map/pallas_call | solution.py:229
  73.6 6.7 %collective-permute-done.12 = bf16[64,1792]{1,0:T(8,128)(2,1)S(1)} collective-permute-done((bf16[64,1792]{1,0:T(8,128)(2,1)S(1)}, bf16[64,1792]{1,0:T(8,128)(2,1)S(1)}, u32[]{:S(2)}, u32[]{:S(2)}) %collective-permute-start.12) | collective-permute-done | bytes 229408 | tf_op jit(solution)/shard_map/ppermute | solution.py:182
  80.6 3.2 %collective-permute-start.15 = (bf16[2,64,1792]{2,1,0:T(8,128)(2,1)S(1)}, bf16[2,64,1792]{2,1,0:T(8,128)(2,1)S(1)}, u32[]{:S(2)}, u32[]{:S(2)}) collective-permute-start(bf16[2,64,1792]{2,1,0:T(8,128)(2,1)S(1)} %slice_bitcast_fusion.4), channel_id=1, source_target_pairs={{0,4},{4,0},{8,12},{12,8},{1,5},{5,1},{9,13},{13,9},{2,6},{6,2},{1... | collective-permute-start | bytes 1376264 | tf_op jit(solution)/shard_map/ppermute | solution.py:182
  83.8 10.1 %collective-permute-done.16 = bf16[64,1792]{1,0:T(8,128)(2,1)S(1)} collective-permute-done((bf16[64,1792]{1,0:T(8,128)(2,1)S(1)}, bf16[64,1792]{1,0:T(8,128)(2,1)S(1)}, u32[]{:S(2)}, u32[]{:S(2)}) %collective-permute-start.16) | collective-permute-done | bytes 229408 | tf_op jit(solution)/shard_map/ppermute | solution.py:182
  94.0 5.9 %collective-permute-done.15 = bf16[2,64,1792]{2,1,0:T(8,128)(2,1)S(1)} collective-permute-done((bf16[2,64,1792]{2,1,0:T(8,128)(2,1)S(1)}, bf16[2,64,1792]{2,1,0:T(8,128)(2,1)S(1)}, u32[]{:S(2)}, u32[]{:S(2)}) %collective-permute-start.15) | collective-permute-done | bytes 458784 | tf_op jit(solution)/shard_map/ppermute | solution.py:182
  99.9 0.7 fusion.21
  100.8 9.7 %collective-permute-done.18 = bf16[64,1792]{1,0:T(8,128)(2,1)S(1)} collective-permute-done((bf16[64,1792]{1,0:T(8,128)(2,1)}, bf16[64,1792]{1,0:T(8,128)(2,1)S(1)}, u32[]{:S(2)}, u32[]{:S(2)}) %collective-permute-start.18) | collective-permute-done | bytes 229408 | tf_op jit(solution)/shard_map/ppermute | solution.py:182
  110.5 3.1 %collective-permute-done.17 = bf16[128,1792]{1,0:T(8,128)(2,1)S(1)} collective-permute-done((bf16[128,1792]{1,0:T(8,128)(2,1)S(1)}, bf16[128,1792]{1,0:T(8,128)(2,1)S(1)}, u32[]{:S(2)}, u32[]{:S(2)}) %collective-permute-start.17) | collective-permute-done | bytes 458784 | tf_op jit(solution)/shard_map/ppermute | solution.py:182
  114.0 6.3 %convolution_convert_fusion.1 = bf16[256,2560]{1,0:T(8,128)(2,1)S(1)} fusion(bf16[256,1792]{1,0:T(8,128)(2,1)S(1)} %get-tuple-element.26, bf16[1792,2560]{1,0:T(8,128)(2,1)} %param.17), kind=kOutput, calls=%fused_computation.1 | convolution fusion | flops 2349465600 | bytes 11403264 | tf_op jit(solution)/shard_map/dot_general | solution.py:194
  120.5 0.7 copy-done.8
  121.8 2.5 %convolution_convert_fusion = bf16[256,2560]{1,0:T(8,128)(2,1)S(1)} fusion(bf16[256,1792]{1,0:T(8,128)(2,1)S(1)} %get-tuple-element.26, bf16[1792,2560]{1,0:T(8,128)(2,1)S(1)} %bitcast.178), kind=kOutput, calls=%fused_computation | convolution fusion | flops 2349465600 | bytes 11403264 | tf_op jit(solution)/shard_map/dot_general | solution.py:194
  124.7 1.5 collective-permute-start.21
  126.6 1.0 fusion.7
  127.7 1.5 collective-permute-start.28
  129.2 1.0 collective-permute-start.26
  130.2 4.4 %collective-permute-done.19 = bf16[64,1792]{1,0:T(8,128)(2,1)S(1)} collective-permute-done((bf16[64,1792]{1,0:T(8,128)(2,1)S(1)}, bf16[64,1792]{1,0:T(8,128)(2,1)S(1)}, u32[]{:S(2)}, u32[]{:S(2)}) %collective-permute-start.19) | collective-permute-done | bytes 229408 | tf_op jit(solution)/shard_map/ppermute | solution.py:182
  134.6 7.7 %collective-permute-done.21 = bf16[128,2560]{1,0:T(8,128)(2,1)S(1)} collective-permute-done((bf16[128,2560]{1,0:T(8,128)(2,1)S(1)}, bf16[128,2560]{1,0:T(8,128)(2,1)S(1)}, u32[]{:S(2)}, u32[]{:S(2)}) %collective-permute-start.21) | collective-permute-done | bytes 655392 | tf_op jit(solution)/shard_map/ppermute | solution.py:182
  142.3 2.1 collective-permute-start.27
  144.6 5.4 %convolution_convert_fusion.4 = bf16[128,2560]{1,0:T(8,128)(2,1)S(1)} fusion(bf16[1792,2560]{1,0:T(8,128)(2,1)} %param.18, bf16[128,1792]{1,0:T(8,128)(2,1)S(1)} %pad_maximum_fusion.13, f32[1792]{0:T(1024)S(1)} %copy-done.2), kind=kOutput, calls=%fused_computation.4 | convolution fusion | flops 1175420928 | bytes 10296320 | tf_op jit(solution)/shard_map/dot_general | solution.py:194
  150.0 5.1 %convolution_convert_fusion.5 = bf16[128,2560]{1,0:T(8,128)(2,1)S(1)} fusion(bf16[1792,2560]{1,0:T(8,128)(2,1)} %param.17, bf16[128,1792]{1,0:T(8,128)(2,1)S(1)} %pad_maximum_fusion.13, f32[1792]{0:T(1024)S(1)} %copy-done.2), kind=kOutput, calls=%fused_computation.5 | convolution fusion | flops 1175420928 | bytes 10296320 | tf_op jit(solution)/shard_map/dot_general | solution.py:194
  155.3 0.9 pad_maximum_fusion.4
  156.7 1.7 shard_map.116
  158.4 0.8 copy-done.3
  159.5 1.4 convolution_convert_fusion.2
  160.9 1.1 slice-done.10
  162.1 1.4 convolution_convert_fusion.3
  163.4 0.6 collective-permute-start.30
  164.3 0.6 collective-permute-done.30
  165.0 1.3 convert_add_fusion.3
  166.5 0.9 copy-done.4
  167.4 0.6 fusion.19
  168.4 1.5 collective-permute-start.31
  170.2 2.5 %convolution_convert_fusion.6 = bf16[256,1792]{1,0:T(8,128)(2,1)S(1)} fusion(bf16[2560,1792]{1,0:T(8,128)(2,1)S(1)} %shard_map.116, bf16[128,2560]{1,0:T(8,128)(2,1)S(1)} %collective-permute-done.32, bf16[64,2560]{1,0:T(8,128)(2,1)S(1)} %get-tuple-element.42, bf16[64,2560]{1,0:T(8,128)(2,1)S(1)} %get-tuple-element.41), kind=kOutput, calls=%fused_computation.6 | convolution fusion | flops 2353201152 | bytes 11403264 | tf_op jit(solution)/shard_map/dot_general | solution.py:194
  172.9 0.8 pad_maximum_fusion.12
  173.7 11.6 %collective-permute-done.31 = bf16[128,2560]{1,0:T(8,128)(2,1)S(1)} collective-permute-done((bf16[128,2560]{1,0:T(8,128)(2,1)S(1)}, bf16[128,2560]{1,0:T(8,128)(2,1)S(1)}, u32[]{:S(2)}, u32[]{:S(2)}) %collective-permute-start.31) | collective-permute-done | bytes 655392 | tf_op jit(solution)/shard_map/ppermute | solution.py:182
  185.7 1.7 collective-permute-done.33
  187.5 4.8 %shard_map.117 = bf16[256,1792]{1,0:T(8,128)(2,1)S(1)} custom-call(bf16[256,2560]{1,0:T(8,128)(2,1)S(1)} %pad_maximum_fusion.rows, bf16[2560,1792]{1,0:T(8,128)(2,1)} %weight.6), custom_call_target="tpu_custom_call" | custom-call | flops 1024 | bytes 1024 | tf_op jit(solution)/shard_map/pallas_call | solution.py:229
  192.4 2.6 %collective-permute-start.37 = (bf16[64,1792]{1,0:T(8,128)(2,1)S(1)}, bf16[64,1792]{1,0:T(8,128)(2,1)S(1)}, u32[]{:S(2)}, u32[]{:S(2)}) collective-permute-start(bf16[64,1792]{1,0:T(8,128)(2,1)S(1)} %fusion.37), channel_id=1, source_target_pairs={{0,8},{4,12},{8,0},{12,4},{1,9},{5,13},{9,1},{13,5},{2,10},{6,14},... | collective-permute-start | bytes 688136 | tf_op jit(solution)/shard_map/ppermute | solution.py:182
  195.0 14.8 %collective-permute-done.35 = bf16[2,64,1792]{2,1,0:T(8,128)(2,1)S(1)} collective-permute-done((bf16[2,64,1792]{2,1,0:T(8,128)(2,1)S(1)}, bf16[2,64,1792]{2,1,0:T(8,128)(2,1)S(1)}, u32[]{:S(2)}, u32[]{:S(2)}) %collective-permute-start.35) | collective-permute-done | bytes 458784 | tf_op jit(solution)/shard_map/ppermute | solution.py:182
  210.2 11.9 %collective-permute-done.36 = bf16[64,1792]{1,0:T(8,128)(2,1)S(1)} collective-permute-done((bf16[64,1792]{1,0:T(8,128)(2,1)S(1)}, bf16[64,1792]{1,0:T(8,128)(2,1)S(1)}, u32[]{:S(2)}, u32[]{:S(2)}) %collective-permute-start.36) | collective-permute-done | bytes 229408 | tf_op jit(solution)/shard_map/ppermute | solution.py:182
  222.3 0.8 pad_maximum_fusion.14
  (148 shorter events, 9.8 us)
Async XLA Ops:
  1.5 13.5 %collective-permute-start.2 = (bf16[288,128]{1,0:T(8,128)(2,1)S(1)}, bf16[288,128]{1,0:T(8,128)(2,1)S(1)}, u32[]{:S(2)}, u32[]{:S(2)}) collective-permute-start(bf16[288,128]{1,0:T(8,128)(2,1)S(1)} %constant_dynamic-slice_fusion.14), channel_id=1, source_target_pairs={{0,4},{4,8},{8,12},{1,5},{5,9},{9,13},{2,6},{6,10},{10,14},{3,7},{... | collective-permute-start | bytes 221192 | tf_op jit(solution)/shard_map/ppermute | solution.py:283
  6.5 8.5 %collective-permute-start.1 = (bf16[288,128]{1,0:T(8,128)(2,1)S(1)}, bf16[288,128]{1,0:T(8,128)(2,1)S(1)}, u32[]{:S(2)}, u32[]{:S(2)}) collective-permute-start(bf16[288,128]{1,0:T(8,128)(2,1)S(1)} %constant_dynamic-slice_fusion.14), channel_id=1, source_target_pairs={{0,8},{4,12},{1,9},{5,13},{2,10},{6,14},{3,11},{7,15},{16,24},{20,... | collective-permute-start | bytes 221192 | tf_op jit(solution)/shard_map/ppermute | solution.py:283
  11.0 4.0 %collective-permute-start = (bf16[288,128]{1,0:T(8,128)(2,1)S(1)}, bf16[288,128]{1,0:T(8,128)(2,1)S(1)}, u32[]{:S(2)}, u32[]{:S(2)}) collective-permute-start(bf16[288,128]{1,0:T(8,128)(2,1)S(1)} %constant_dynamic-slice_fusion.14), channel_id=1, source_target_pairs={{0,12},{1,13},{2,14},{3,15},{16,28},{17,29},{18,30},{19,31}} | collective-permute-start | bytes 221192 | tf_op jit(solution)/shard_map/ppermute | solution.py:283
  14.6 2.0 copy-start.6
  15.0 1.5 collective-permute-start.3
  16.6 1.6 copy-start.1
  16.8 2.2 copy-start
  25.8 5.5 %collective-permute-start.6 = (bf16[32,2048]{1,0:T(8,128)(2,1)S(1)}, bf16[32,2048]{1,0:T(8,128)(2,1)S(1)}, u32[]{:S(2)}, u32[]{:S(2)}) collective-permute-start(bf16[32,2048]{1,0:T(8,128)(2,1)S(1)} %get-tuple-element.70), channel_id=1, source_target_pairs={{0,3},{1,2},{2,1},{3,0},{4,7},{5,6},{6,5},{7,4},{8,11},{9,10},{10,... | collective-permute-start | bytes 393224 | tf_op jit(solution)/shard_map/ppermute | solution.py:182
  27.1 7.4 %collective-permute-start.5 = (bf16[32,2048]{1,0:T(8,128)(2,1)S(1)}, bf16[32,2048]{1,0:T(8,128)(2,1)S(1)}, u32[]{:S(2)}, u32[]{:S(2)}) collective-permute-start(bf16[32,2048]{1,0:T(8,128)(2,1)S(1)} %get-tuple-element.71), channel_id=1, source_target_pairs={{0,2},{1,3},{2,0},{3,1},{4,6},{5,7},{6,4},{7,5},{8,10},{9,11},{10,... | collective-permute-start | bytes 393224 | tf_op jit(solution)/shard_map/ppermute | solution.py:182
  27.7 6.8 %collective-permute-start.4 = (bf16[32,2048]{1,0:T(8,128)(2,1)S(1)}, bf16[32,2048]{1,0:T(8,128)(2,1)S(1)}, u32[]{:S(2)}, u32[]{:S(2)}) collective-permute-start(bf16[32,2048]{1,0:T(8,128)(2,1)S(1)} %get-tuple-element.72), channel_id=1, source_target_pairs={{0,1},{1,0},{2,3},{3,2},{4,5},{5,4},{6,7},{7,6},{8,9},{9,8},{10,11... | collective-permute-start | bytes 393224 | tf_op jit(solution)/shard_map/ppermute | solution.py:182
  34.6 8.3 %collective-permute-start.9 = (bf16[32,2048]{1,0:T(8,128)(2,1)S(1)}, bf16[32,2048]{1,0:T(8,128)(2,1)S(1)}, u32[]{:S(2)}, u32[]{:S(2)}) collective-permute-start(bf16[32,2048]{1,0:T(8,128)(2,1)S(1)} %get-tuple-element.66), channel_id=1, source_target_pairs={{0,12},{4,8},{8,4},{12,0},{1,13},{5,9},{9,5},{13,1},{2,14},{6,10},... | collective-permute-start | bytes 393224 | tf_op jit(solution)/shard_map/ppermute | solution.py:182
  38.3 10.2 %collective-permute-start.8 = (bf16[32,2048]{1,0:T(8,128)(2,1)S(1)}, bf16[32,2048]{1,0:T(8,128)(2,1)S(1)}, u32[]{:S(2)}, u32[]{:S(2)}) collective-permute-start(bf16[32,2048]{1,0:T(8,128)(2,1)S(1)} %get-tuple-element.67), channel_id=1, source_target_pairs={{0,8},{4,12},{8,0},{12,4},{1,9},{5,13},{9,1},{13,5},{2,10},{6,14},... | collective-permute-start | bytes 393224 | tf_op jit(solution)/shard_map/ppermute | solution.py:182
  38.3 10.2 %collective-permute-start.7 = (bf16[32,2048]{1,0:T(8,128)(2,1)S(1)}, bf16[32,2048]{1,0:T(8,128)(2,1)S(1)}, u32[]{:S(2)}, u32[]{:S(2)}) collective-permute-start(bf16[32,2048]{1,0:T(8,128)(2,1)S(1)} %get-tuple-element.68), channel_id=1, source_target_pairs={{0,4},{4,0},{8,12},{12,8},{1,5},{5,1},{9,13},{13,9},{2,6},{6,2},{1... | collective-permute-start | bytes 393224 | tf_op jit(solution)/shard_map/ppermute | solution.py:182
  48.6 2.0 collective-permute-start.10
  48.6 14.3 %collective-permute-start.13 = (bf16[4,32,2048]{2,1,0:T(8,128)(2,1)S(1)}, bf16[4,32,2048]{2,1,0:T(8,128)(2,1)S(1)}, u32[]{:S(2)}, u32[]{:S(2)}) collective-permute-start(bf16[4,32,2048]{2,1,0:T(8,128)(2,1)S(1)} %pad_maximum_fusion.10), channel_id=1, source_target_pairs={{0,2},{1,3},{2,0},{3,1},{4,6},{5,7},{6,4},{7,5},{8,10},{9,11},{10,... | collective-permute-start | bytes 1572872 | tf_op jit(solution)/shard_map/ppermute | solution.py:182
  55.0 12.6 %collective-permute-start.11 = (bf16[2,64,1792]{2,1,0:T(8,128)(2,1)S(1)}, bf16[2,64,1792]{2,1,0:T(8,128)(2,1)S(1)}, u32[]{:S(2)}, u32[]{:S(2)}) collective-permute-start(bf16[2,64,1792]{2,1,0:T(8,128)(2,1)S(1)} %slice_bitcast_fusion.5), channel_id=1, source_target_pairs={{0,4},{4,0},{8,12},{12,8},{1,5},{5,1},{9,13},{13,9},{2,6},{6,2},{1... | collective-permute-start | bytes 1376264 | tf_op jit(solution)/shard_map/ppermute | solution.py:182
  63.0 6.2 %collective-permute-start.14 = (bf16[4,32,2048]{2,1,0:T(8,128)(2,1)S(1)}, bf16[4,32,2048]{2,1,0:T(8,128)(2,1)S(1)}, u32[]{:S(2)}, u32[]{:S(2)}) collective-permute-start(bf16[4,32,2048]{2,1,0:T(8,128)(2,1)S(1)} %collective-permute-done.13), channel_id=1, source_target_pairs={{0,1},{1,0},{2,3},{3,2},{4,5},{5,4},{6,7},{7,6},{8,9},{9,8},{10,11... | collective-permute-start | bytes 1572872 | tf_op jit(solution)/shard_map/ppermute | solution.py:182
  67.7 12.7 %collective-permute-start.12 = (bf16[64,1792]{1,0:T(8,128)(2,1)S(1)}, bf16[64,1792]{1,0:T(8,128)(2,1)S(1)}, u32[]{:S(2)}, u32[]{:S(2)}) collective-permute-start(bf16[64,1792]{1,0:T(8,128)(2,1)S(1)} %fusion.25), channel_id=1, source_target_pairs={{0,8},{4,12},{8,0},{12,4},{1,9},{5,13},{9,1},{13,5},{2,10},{6,14},... | collective-permute-start | bytes 688136 | tf_op jit(solution)/shard_map/ppermute | solution.py:182
  69.4 11.0 %copy-start.5 = (bf16[128,1792]{1,0:T(8,128)(2,1)S(1)}, bf16[128,1792]{1,0:T(8,128)(2,1)}, u32[]{:S(2)}) copy-start(bf16[128,1792]{1,0:T(8,128)(2,1)} %param.10) | copy-start | bytes 1376260
  80.4 33.2 %copy-start.2 = (f32[1792]{0:T(1024)S(1)}, f32[1792]{0:T(1024)}, u32[]{:S(2)}) copy-start(f32[1792]{0:T(1024)} %param.16) | copy-start | bytes 21508
  80.5 13.4 %collective-permute-start.16 = (bf16[64,1792]{1,0:T(8,128)(2,1)S(1)}, bf16[64,1792]{1,0:T(8,128)(2,1)S(1)}, u32[]{:S(2)}, u32[]{:S(2)}) collective-permute-start(bf16[64,1792]{1,0:T(8,128)(2,1)S(1)} %fusion.28), channel_id=1, source_target_pairs={{0,8},{4,12},{8,0},{12,4},{1,9},{5,13},{9,1},{13,5},{2,10},{6,14},... | collective-permute-start | bytes 688136 | tf_op jit(solution)/shard_map/ppermute | solution.py:182
  80.6 19.3 %collective-permute-start.15 = (bf16[2,64,1792]{2,1,0:T(8,128)(2,1)S(1)}, bf16[2,64,1792]{2,1,0:T(8,128)(2,1)S(1)}, u32[]{:S(2)}, u32[]{:S(2)}) collective-permute-start(bf16[2,64,1792]{2,1,0:T(8,128)(2,1)S(1)} %slice_bitcast_fusion.4), channel_id=1, source_target_pairs={{0,4},{4,0},{8,12},{12,8},{1,5},{5,1},{9,13},{13,9},{2,6},{6,2},{1... | collective-permute-start | bytes 1376264 | tf_op jit(solution)/shard_map/ppermute | solution.py:182
  93.9 19.7 %collective-permute-start.17 = (bf16[128,1792]{1,0:T(8,128)(2,1)S(1)}, bf16[128,1792]{1,0:T(8,128)(2,1)S(1)}, u32[]{:S(2)}, u32[]{:S(2)}) collective-permute-start(bf16[128,1792]{1,0:T(8,128)(2,1)S(1)} %pad_maximum_fusion.11), channel_id=1, source_target_pairs={{0,4},{4,0},{8,12},{12,8},{1,5},{5,1},{9,13},{13,9},{2,6},{6,2},{1... | collective-permute-start | bytes 1376264 | tf_op jit(solution)/shard_map/ppermute | solution.py:182
  100.6 9.9 %collective-permute-start.18 = (bf16[64,1792]{1,0:T(8,128)(2,1)}, bf16[64,1792]{1,0:T(8,128)(2,1)S(1)}, u32[]{:S(2)}, u32[]{:S(2)}) collective-permute-start(bf16[64,1792]{1,0:T(8,128)(2,1)} %fusion.21), channel_id=1, source_target_pairs={{0,8},{4,12},{8,0},{12,4},{1,9},{5,13},{9,1},{13,5},{2,10},{6,14},... | collective-permute-start | bytes 688136 | tf_op jit(solution)/shard_map/ppermute | solution.py:182
  110.5 9.8 %copy-start.7 = (bf16[64,1792]{1,0:T(8,128)(2,1)}, bf16[64,1792]{1,0:T(8,128)(2,1)S(1)}, u32[]{:S(2)}) copy-start(bf16[64,1792]{1,0:T(8,128)(2,1)S(1)} %collective-permute-done.18) | copy-start | bytes 688132
  113.6 8.1 %slice-start.3 = ((s8[9175040]{0:T(1024)(128)(4,1)}), s8[4194304]{0:T(1024)(128)(4,1)S(1)}, s32[]{:S(2)}) async-start(s8[9175040]{0:T(1024)(128)(4,1)} %bitcast.177), calls=%async_computation.3 | async-start | bytes 8388608
  114.0 7.8 %slice-start.4 = ((s8[9175040]{0:T(1024)(128)(4,1)}), s8[4194304]{0:T(1024)(128)(4,1)S(1)}, s32[]{:S(2)}) async-start(s8[9175040]{0:T(1024)(128)(4,1)} %bitcast.177), calls=%async_computation.4 | async-start | bytes 8388608
  114.0 7.8 %slice-start.5 = ((s8[9175040]{0:T(1024)(128)(4,1)}), s8[786432]{0:T(1024)(128)(4,1)S(1)}, s32[]{:S(2)}) async-start(s8[9175040]{0:T(1024)(128)(4,1)} %bitcast.177), calls=%async_computation.5 | async-start | bytes 1572864
  120.3 0.9 copy-start.8
  120.4 4.0 %collective-permute-start.20 = (bf16[128,2560]{1,0:T(8,128)(2,1)S(1)}, bf16[128,2560]{1,0:T(8,128)(2,1)S(1)}, u32[]{:S(2)}, u32[]{:S(2)}) collective-permute-start(bf16[128,2560]{1,0:T(8,128)(2,1)S(1)} %bitcast.187), channel_id=1, source_target_pairs={{0,1},{1,0},{2,3},{3,2},{4,5},{5,4},{6,7},{7,6},{8,9},{9,8},{10,11... | collective-permute-start | bytes 1966088 | tf_op jit(solution)/shard_map/ppermute | solution.py:182
  121.4 13.2 %collective-permute-start.19 = (bf16[64,1792]{1,0:T(8,128)(2,1)S(1)}, bf16[64,1792]{1,0:T(8,128)(2,1)S(1)}, u32[]{:S(2)}, u32[]{:S(2)}) collective-permute-start(bf16[64,1792]{1,0:T(8,128)(2,1)S(1)} %get-tuple-element.40), channel_id=1, source_target_pairs={{0,8},{4,12},{8,0},{12,4},{1,9},{5,13},{9,1},{13,5},{2,10},{6,14},... | collective-permute-start | bytes 688136 | tf_op jit(solution)/shard_map/ppermute | solution.py:182
  124.4 2.2 collective-permute-start.22
  124.7 17.6 %collective-permute-start.21 = (bf16[128,2560]{1,0:T(8,128)(2,1)S(1)}, bf16[128,2560]{1,0:T(8,128)(2,1)S(1)}, u32[]{:S(2)}, u32[]{:S(2)}) collective-permute-start(bf16[128,2560]{1,0:T(8,128)(2,1)S(1)} %fusion.8), channel_id=1, source_target_pairs={{0,2},{1,3},{2,0},{3,1},{4,6},{5,7},{6,4},{7,5},{8,10},{9,11},{10,... | collective-permute-start | bytes 1966088 | tf_op jit(solution)/shard_map/ppermute | solution.py:182
  127.6 1.6 collective-permute-start.25
  127.7 30.6 %collective-permute-start.28 = (bf16[128,2560]{1,0:T(8,128)(2,1)}, bf16[128,2560]{1,0:T(8,128)(2,1)S(1)}, u32[]{:S(2)}, u32[]{:S(2)}) collective-permute-start(bf16[128,2560]{1,0:T(8,128)(2,1)} %fusion.7), channel_id=1, source_target_pairs={{0,2},{1,3},{2,0},{3,1},{4,6},{5,7},{6,4},{7,5},{8,10},{9,11},{10,... | collective-permute-start | bytes 1966088 | tf_op jit(solution)/shard_map/ppermute | solution.py:182
  129.2 35.0 %collective-permute-start.26 = (f32[256]{0:T(256)S(1)}, f32[256]{0:T(256)S(1)}, u32[]{:S(2)}, u32[]{:S(2)}) collective-permute-start(f32[256]{0:T(256)S(1)} %add.261), channel_id=1, source_target_pairs={{0,2},{1,3},{2,0},{3,1},{4,6},{5,7},{6,4},{7,5},{8,10},{9,11},{10,... | collective-permute-start | bytes 3080 | tf_op jit(solution)/shard_map/ppermute | solution.py:182
  142.3 16.1 %collective-permute-start.27 = (bf16[128,1792]{1,0:T(8,128)(2,1)S(1)}, bf16[128,1792]{1,0:T(8,128)(2,1)S(1)}, u32[]{:S(2)}, u32[]{:S(2)}) collective-permute-start(bf16[128,1792]{1,0:T(8,128)(2,1)S(1)} %pad_maximum_fusion.13), channel_id=1, source_target_pairs={{0,4},{4,0},{8,12},{12,8},{1,5},{5,1},{9,13},{13,9},{2,6},{6,2},{1... | collective-permute-start | bytes 1376264 | tf_op jit(solution)/shard_map/ppermute | solution.py:182
  144.6 12.1 %slice-start = ((s8[9175040]{0:T(1024)(128)(4,1)}), s8[4194304]{0:T(1024)(128)(4,1)S(1)}, s32[]{:S(2)}) async-start(s8[9175040]{0:T(1024)(128)(4,1)} %bitcast.164), calls=%async_computation | async-start | bytes 8388608
  144.6 12.1 %slice-start.1 = ((s8[9175040]{0:T(1024)(128)(4,1)}), s8[4194304]{0:T(1024)(128)(4,1)S(1)}, s32[]{:S(2)}) async-start(s8[9175040]{0:T(1024)(128)(4,1)} %bitcast.164), calls=%async_computation.1 | async-start | bytes 8388608
  150.0 6.7 %slice-start.2 = ((s8[9175040]{0:T(1024)(128)(4,1)}), s8[786432]{0:T(1024)(128)(4,1)S(1)}, s32[]{:S(2)}) async-start(s8[9175040]{0:T(1024)(128)(4,1)} %bitcast.164), calls=%async_computation.2 | async-start | bytes 1572864
  155.1 9.2 %collective-permute-start.24 = (f32[128]{0:T(128)S(1)}, f32[128]{0:T(128)S(1)}, u32[]{:S(2)}, u32[]{:S(2)}) collective-permute-start(f32[128]{0:T(128)S(1)} %fusion.10), channel_id=1, source_target_pairs={{0,1},{1,0},{2,3},{3,2},{4,5},{5,4},{6,7},{7,6},{8,9},{9,8},{10,11... | collective-permute-start | bytes 1544 | tf_op jit(solution)/shard_map/ppermute | solution.py:182
  155.2 4.2 %slice-start.6 = ((s8[9175040]{0:T(1024)(128)(4,1)}), s8[4194304]{0:T(1024)(128)(4,1)S(1)}, s32[]{:S(2)}) async-start(s8[9175040]{0:T(1024)(128)(4,1)} %bitcast.179), calls=%async_computation.6 | async-start | bytes 8388608
  156.2 3.2 %slice-start.7 = ((s8[9175040]{0:T(1024)(128)(4,1)}), s8[4194304]{0:T(1024)(128)(4,1)S(1)}, s32[]{:S(2)}) async-start(s8[9175040]{0:T(1024)(128)(4,1)} %bitcast.179), calls=%async_computation.7 | async-start | bytes 8388608
  156.2 3.2 %slice-start.8 = ((s8[9175040]{0:T(1024)(128)(4,1)}), s8[786432]{0:T(1024)(128)(4,1)S(1)}, s32[]{:S(2)}) async-start(s8[9175040]{0:T(1024)(128)(4,1)} %bitcast.179), calls=%async_computation.8 | async-start | bytes 1572864
  156.2 8.8 %collective-permute-start.23 = (bf16[128,2560]{1,0:T(8,128)(2,1)}, bf16[128,2560]{1,0:T(8,128)(2,1)}, u32[]{:S(2)}, u32[]{:S(2)}) collective-permute-start(bf16[128,2560]{1,0:T(8,128)(2,1)} %pad_maximum_fusion.4), channel_id=1, source_target_pairs={{0,1},{1,0},{2,3},{3,2},{4,5},{5,4},{6,7},{7,6},{8,9},{9,8},{10,11... | collective-permute-start | bytes 1966088 | tf_op jit(solution)/shard_map/ppermute | solution.py:182
  156.7 4.2 %slice-start.9 = ((s8[9175040]{0:T(1024)(128)(4,1)}), s8[4194304]{0:T(1024)(128)(4,1)S(1)}, s32[]{:S(2)}) async-start(s8[9175040]{0:T(1024)(128)(4,1)} %bitcast.181), calls=%async_computation.9 | async-start | bytes 8388608
  156.7 5.3 %slice-start.10 = ((s8[9175040]{0:T(1024)(128)(4,1)}), s8[4194304]{0:T(1024)(128)(4,1)S(1)}, s32[]{:S(2)}) async-start(s8[9175040]{0:T(1024)(128)(4,1)} %bitcast.181), calls=%async_computation.10 | async-start | bytes 8388608
  158.4 0.8 copy-start.3
  159.4 2.6 %slice-start.11 = ((s8[9175040]{0:T(1024)(128)(4,1)}), s8[786432]{0:T(1024)(128)(4,1)S(1)}, s32[]{:S(2)}) async-start(s8[9175040]{0:T(1024)(128)(4,1)} %bitcast.181), calls=%async_computation.11 | async-start | bytes 1572864
  163.4 1.4 collective-permute-start.30
  164.2 2.2 collective-permute-start.29
  166.3 1.1 copy-start.4
  168.1 2.2 collective-permute-start.32
  168.4 16.9 %collective-permute-start.31 = (bf16[128,2560]{1,0:T(8,128)(2,1)S(1)}, bf16[128,2560]{1,0:T(8,128)(2,1)S(1)}, u32[]{:S(2)}, u32[]{:S(2)}) collective-permute-start(bf16[128,2560]{1,0:T(8,128)(2,1)S(1)} %pad_maximum_fusion.6), channel_id=1, source_target_pairs={{0,2},{1,3},{2,0},{3,1},{4,6},{5,7},{6,4},{7,5},{8,10},{9,11},{10,... | collective-permute-start | bytes 1966088 | tf_op jit(solution)/shard_map/ppermute | solution.py:182
  172.8 12.7 %collective-permute-start.34 = (bf16[2,64,1792]{2,1,0:T(8,128)(2,1)S(1)}, bf16[2,64,1792]{2,1,0:T(8,128)(2,1)S(1)}, u32[]{:S(2)}, u32[]{:S(2)}) collective-permute-start(bf16[2,64,1792]{2,1,0:T(8,128)(2,1)S(1)} %slice_bitcast_fusion.2), channel_id=1, source_target_pairs={{0,4},{4,0},{8,12},{12,8},{1,5},{5,1},{9,13},{13,9},{2,6},{6,2},{1... | collective-permute-start | bytes 1376264 | tf_op jit(solution)/shard_map/ppermute | solution.py:182
  185.3 2.1 collective-permute-start.33
  192.3 17.5 %collective-permute-start.35 = (bf16[2,64,1792]{2,1,0:T(8,128)(2,1)S(1)}, bf16[2,64,1792]{2,1,0:T(8,128)(2,1)S(1)}, u32[]{:S(2)}, u32[]{:S(2)}) collective-permute-start(bf16[2,64,1792]{2,1,0:T(8,128)(2,1)S(1)} %slice_bitcast_fusion), channel_id=1, source_target_pairs={{0,4},{4,0},{8,12},{12,8},{1,5},{5,1},{9,13},{13,9},{2,6},{6,2},{1... | collective-permute-start | bytes 1376264 | tf_op jit(solution)/shard_map/ppermute | solution.py:182
  192.4 17.9 %collective-permute-start.37 = (bf16[64,1792]{1,0:T(8,128)(2,1)S(1)}, bf16[64,1792]{1,0:T(8,128)(2,1)S(1)}, u32[]{:S(2)}, u32[]{:S(2)}) collective-permute-start(bf16[64,1792]{1,0:T(8,128)(2,1)S(1)} %fusion.37), channel_id=1, source_target_pairs={{0,8},{4,12},{8,0},{12,4},{1,9},{5,13},{9,1},{13,5},{2,10},{6,14},... | collective-permute-start | bytes 688136 | tf_op jit(solution)/shard_map/ppermute | solution.py:182
  210.0 12.2 %collective-permute-start.36 = (bf16[64,1792]{1,0:T(8,128)(2,1)S(1)}, bf16[64,1792]{1,0:T(8,128)(2,1)S(1)}, u32[]{:S(2)}, u32[]{:S(2)}) collective-permute-start(bf16[64,1792]{1,0:T(8,128)(2,1)S(1)} %fusion.38), channel_id=1, source_target_pairs={{0,8},{4,12},{8,0},{12,4},{1,9},{5,13},{9,1},{13,5},{2,10},{6,14},... | collective-permute-start | bytes 688136 | tf_op jit(solution)/shard_map/ppermute | solution.py:182

commit v14 on v11

--- a/solution.py
+++ b/solution.py
@@ -196,17 +196,19 @@
 
 def streamed_kernel(depth, rows, weight, out, held, total, sems):
     steps = weight.shape[0] // depth
+    each = depth // 2
     copies = [
         pltpu.make_async_copy(
-            weight.at[pl.ds(i * depth, depth)], held.at[pl.ds(i * depth, depth)], sems.at[i]
+            weight.at[pl.ds(i * each, each)], held.at[pl.ds(i * each, each)], sems.at[i]
         )
-        for i in range(steps)
+        for i in range(2 * steps)
     ]
     for copy in copies:
         copy.start()
     block = 256
-    for i, copy in enumerate(copies):
-        copy.wait()
+    for i in range(steps):
+        copies[2 * i].wait()
+        copies[2 * i + 1].wait()
         part = rows[:, i * depth : (i + 1) * depth]
         for start in range(0, weight.shape[1], block):
             columns = slice(start, start + block)
@@ -236,7 +238,7 @@
         scratch_shapes=[
             pltpu.VMEM(weight.shape, weight.dtype),
             pltpu.VMEM((rows.shape[0], weight.shape[1]), jnp.float32),
-            pltpu.SemaphoreType.DMA((steps,)),
+            pltpu.SemaphoreType.DMA((2 * steps,)),
         ],
         compiler_params=pltpu.CompilerParams(vmem_limit_bytes=50 * 1024 * 1024),
         cost_estimate=pl.CostEstimate(flops=1024, bytes_accessed=1024, transcendentals=0),
@@ -353,6 +355,7 @@
 
     sent_gate, _, across_gate = cross(scaled, gate_weight)
     _, sums_up, across_up = cross(after(scaled, sent_gate), up_weight)
+    squares_a = after(squares_a, sums_up)
     across_squares = swap(squares_a + swap(squares_a, "tp", 1), "tp", 2)
     pair_b = jnp.concatenate([attended_b, after(twin_b, across_gate)], axis=0)
     rest_b = swap(pair_b, "ctx", 1)

time: 219 us -> 220 us (level)
  waiting for transfers between devices: 125 us -> 117 us
  matrix products: 14.6 us -> 22.1 us
    ppermute x35, waiting for transfers between devices: 125 us -> 117 us  [swap(): return lax.ppermute(value, axis_name, [(i, i ^ bit) for i in range(width)])]
    dot_general x6, matrix products: 14.6 us -> 22.1 us  [matmul(): jnp.dot(a, b, preferred_element_type=jnp.float32).astype(jnp.bfloat16)]
  transfers between devices with their start and end apart: 38 -> 38, of which waited for: 23 -> 23; matrix products, arithmetic and copies ran while one was open for 7% -> 11% of each run, Pallas kernels for 6% -> 6%
where the time goes in v14:
time: 220 us; the launch traced here: 219 us
  waiting for transfers between devices  117 us (53%)
  starting transfers between devices  38.5 us (18%)
  Pallas kernels  24.6 us (11%)
  matrix products  22.1 us (10%)
  other arithmetic  9.97 us (5%)
  local copies, waits for them, and re-layouts  5.91 us (3%)
    ppermute x35, waiting for transfers between devices, swap(): return lax.ppermute(value, axis_name, [(i, i ^ bit) for i in range(width)])  117 us
    ppermute x35, starting transfers between devices, swap(): return lax.ppermute(value, axis_name, [(i, i ^ bit) for i in range(width)])  27.8 us
    dot_general x6, matrix products, matmul(): jnp.dot(a, b, preferred_element_type=jnp.float32).astype(jnp.bfloat16)  22.1 us
    pallas_call x4, Pallas kernels, streamed_matmul(): pl.pallas_call(functools.partial(streamed_kernel, 512), in_specs=[pl.Bloc...  17.9 us
    ppermute x3, starting transfers between devices, gather_keys(): lax.ppermute(half, 'ctx', [(c, c + d) for c in range(n_ctx - d)])  10.7 us
    pallas_call x1, Pallas kernels, attention(): pl.pallas_call(functools.partial(attention_kernel, group), grid=(local_he...  6.79 us
  transfers between devices with their start and end apart: 38, of which 23 were waited for; matrix products, arithmetic and copies ran while one was open for 11% of the time, Pallas kernels for 6%

profile of v14, /device:TPU:0, one launch (start us, length us, event | category | flops | bytes accessed | tf_op | source)
XLA Modules:
  0.0 219.5 jit_solution(4750315644810692548)
XLA Ops:
  0.6 0.9 constant_dynamic-slice_fusion.14
  1.5 4.9 %collective-permute-start.2 = (bf16[288,128]{1,0:T(8,128)(2,1)S(1)}, bf16[288,128]{1,0:T(8,128)(2,1)S(1)}, u32[]{:S(2)}, u32[]{:S(2)}) collective-permute-start(bf16[288,128]{1,0:T(8,128)(2,1)S(1)} %constant_dynamic-slice_fusion.14), channel_id=1, source_target_pairs={{0,4},{4,8},{8,12},{1,5},{5,9},{9,13},{2,6},{6,10},{10,14},{3,7},{... | collective-permute-start | bytes 221192 | tf_op jit(solution)/shard_map/ppermute | solution.py:257
  6.5 4.5 %collective-permute-start.1 = (bf16[288,128]{1,0:T(8,128)(2,1)S(1)}, bf16[288,128]{1,0:T(8,128)(2,1)S(1)}, u32[]{:S(2)}, u32[]{:S(2)}) collective-permute-start(bf16[288,128]{1,0:T(8,128)(2,1)S(1)} %constant_dynamic-slice_fusion.14), channel_id=1, source_target_pairs={{0,8},{4,12},{1,9},{5,13},{2,10},{6,14},{3,11},{7,15},{16,24},{20,... | collective-permute-start | bytes 221192 | tf_op jit(solution)/shard_map/ppermute | solution.py:257
  11.0 1.3 collective-permute-start
  12.3 0.8 reduce-window.8
  13.2 0.7 subtract_subtract_fusion
  15.1 1.5 collective-permute-done.3
  17.2 1.0 copy-done.1
  18.2 0.7 copy-done
  19.0 6.8 %shard_map.113 = bf16[128,2048]{1,0:T(8,128)(2,1)S(1)} custom-call(f32[4,128,128]{2,1,0:T(8,128)S(1)} %pad_maximum_fusion.16.tables, s32[128,1]{1,0:T(8,128)S(1)} %copy.23.starts, s32[128,1]{1,0:T(8,128)S(1)} %iota_add_fusion.own_index, s32[1,512]{1,0:T(1,128)S(1)} %iota_add_fusion.2.key_index, bf16[576,512]{1,0:T(8,128)(2,1)S(1)} %pad_maximum_fusion.9.keys, ...), custom_call_target="tpu_custom_call" | custom-call | flops 2684354560 | bytes 5046272 | tf_op jit(solution)/shard_map/pallas_call | solution.py:143
  25.8 1.3 collective-permute-start.6
  27.1 0.5 collective-permute-start.5
  27.7 3.6 %collective-permute-done.6 = bf16[32,2048]{1,0:T(8,128)(2,1)S(1)} collective-permute-done((bf16[32,2048]{1,0:T(8,128)(2,1)S(1)}, bf16[32,2048]{1,0:T(8,128)(2,1)S(1)}, u32[]{:S(2)}, u32[]{:S(2)}) %collective-permute-start.6) | collective-permute-done | bytes 131104 | tf_op jit(solution)/shard_map/ppermute | solution.py:182
  31.4 3.1 %collective-permute-done.5 = bf16[32,2048]{1,0:T(8,128)(2,1)S(1)} collective-permute-done((bf16[32,2048]{1,0:T(8,128)(2,1)S(1)}, bf16[32,2048]{1,0:T(8,128)(2,1)S(1)}, u32[]{:S(2)}, u32[]{:S(2)}) %collective-permute-start.5) | collective-permute-done | bytes 131104 | tf_op jit(solution)/shard_map/ppermute | solution.py:182
  34.6 3.7 %collective-permute-start.9 = (bf16[32,2048]{1,0:T(8,128)(2,1)S(1)}, bf16[32,2048]{1,0:T(8,128)(2,1)S(1)}, u32[]{:S(2)}, u32[]{:S(2)}) collective-permute-start(bf16[32,2048]{1,0:T(8,128)(2,1)S(1)} %get-tuple-element.62), channel_id=1, source_target_pairs={{0,12},{4,8},{8,4},{12,0},{1,13},{5,9},{9,5},{13,1},{2,14},{6,10},... | collective-permute-start | bytes 393224 | tf_op jit(solution)/shard_map/ppermute | solution.py:182
  38.3 0.8 collective-permute-start.7
  39.1 3.8 %collective-permute-done.9 = bf16[32,2048]{1,0:T(8,128)(2,1)S(1)} collective-permute-done((bf16[32,2048]{1,0:T(8,128)(2,1)S(1)}, bf16[32,2048]{1,0:T(8,128)(2,1)S(1)}, u32[]{:S(2)}, u32[]{:S(2)}) %collective-permute-start.9) | collective-permute-done | bytes 131104 | tf_op jit(solution)/shard_map/ppermute | solution.py:182
  42.9 5.6 %collective-permute-done.8 = bf16[32,2048]{1,0:T(8,128)(2,1)S(1)} collective-permute-done((bf16[32,2048]{1,0:T(8,128)(2,1)S(1)}, bf16[32,2048]{1,0:T(8,128)(2,1)S(1)}, u32[]{:S(2)}, u32[]{:S(2)}) %collective-permute-start.8) | collective-permute-done | bytes 131104 | tf_op jit(solution)/shard_map/ppermute | solution.py:182
  48.6 1.6 collective-permute-start.13
  50.8 4.1 %shard_map.114 = bf16[256,1792]{1,0:T(8,128)(2,1)S(1)} custom-call(bf16[256,2048]{1,0:T(8,128)(2,1)S(1)} %bitcast.164, bf16[2048,1792]{1,0:T(8,128)(2,1)} %weight.5), custom_call_target="tpu_custom_call" | custom-call | flops 1024 | bytes 1024 | tf_op jit(solution)/shard_map/pallas_call | solution.py:230
  55.0 0.8 collective-permute-start.11
  55.7 7.2 %collective-permute-done.13 = bf16[4,32,2048]{2,1,0:T(8,128)(2,1)S(1)} collective-permute-done((bf16[4,32,2048]{2,1,0:T(8,128)(2,1)S(1)}, bf16[4,32,2048]{2,1,0:T(8,128)(2,1)S(1)}, u32[]{:S(2)}, u32[]{:S(2)}) %collective-permute-start.13) | collective-permute-done | bytes 524320 | tf_op jit(solution)/shard_map/ppermute | solution.py:182
  63.0 4.6 %collective-permute-done.11 = bf16[2,64,1792]{2,1,0:T(8,128)(2,1)S(1)} collective-permute-done((bf16[2,64,1792]{2,1,0:T(8,128)(2,1)S(1)}, bf16[2,64,1792]{2,1,0:T(8,128)(2,1)S(1)}, u32[]{:S(2)}, u32[]{:S(2)}) %collective-permute-start.11) | collective-permute-done | bytes 458784 | tf_op jit(solution)/shard_map/ppermute | solution.py:182
  67.7 1.5 collective-permute-start.12
  69.4 4.2 %shard_map.115 = bf16[256,1792]{1,0:T(8,128)(2,1)S(1)} custom-call(bf16[256,2048]{1,0:T(8,128)(2,1)S(1)} %bitcast.163, bf16[2048,1792]{1,0:T(8,128)(2,1)} %weight.5), custom_call_target="tpu_custom_call" | custom-call | flops 1024 | bytes 1024 | tf_op jit(solution)/shard_map/pallas_call | solution.py:230
  73.6 6.8 %collective-permute-done.12 = bf16[64,1792]{1,0:T(8,128)(2,1)S(1)} collective-permute-done((bf16[64,1792]{1,0:T(8,128)(2,1)S(1)}, bf16[64,1792]{1,0:T(8,128)(2,1)S(1)}, u32[]{:S(2)}, u32[]{:S(2)}) %collective-permute-start.12) | collective-permute-done | bytes 229408 | tf_op jit(solution)/shard_map/ppermute | solution.py:182
  80.6 3.2 %collective-permute-start.15 = (bf16[2,64,1792]{2,1,0:T(8,128)(2,1)S(1)}, bf16[2,64,1792]{2,1,0:T(8,128)(2,1)S(1)}, u32[]{:S(2)}, u32[]{:S(2)}) collective-permute-start(bf16[2,64,1792]{2,1,0:T(8,128)(2,1)S(1)} %slice_bitcast_fusion.4), channel_id=1, source_target_pairs={{0,4},{4,0},{8,12},{12,8},{1,5},{5,1},{9,13},{13,9},{2,6},{6,2},{1... | collective-permute-start | bytes 1376264 | tf_op jit(solution)/shard_map/ppermute | solution.py:182
  83.8 10.1 %collective-permute-done.16 = bf16[64,1792]{1,0:T(8,128)(2,1)S(1)} collective-permute-done((bf16[64,1792]{1,0:T(8,128)(2,1)S(1)}, bf16[64,1792]{1,0:T(8,128)(2,1)S(1)}, u32[]{:S(2)}, u32[]{:S(2)}) %collective-permute-start.16) | collective-permute-done | bytes 229408 | tf_op jit(solution)/shard_map/ppermute | solution.py:182
  94.0 5.9 %collective-permute-done.15 = bf16[2,64,1792]{2,1,0:T(8,128)(2,1)S(1)} collective-permute-done((bf16[2,64,1792]{2,1,0:T(8,128)(2,1)S(1)}, bf16[2,64,1792]{2,1,0:T(8,128)(2,1)S(1)}, u32[]{:S(2)}, u32[]{:S(2)}) %collective-permute-start.15) | collective-permute-done | bytes 458784 | tf_op jit(solution)/shard_map/ppermute | solution.py:182
  99.9 0.7 fusion.16
  100.8 9.7 %collective-permute-done.18 = bf16[64,1792]{1,0:T(8,128)(2,1)S(1)} collective-permute-done((bf16[64,1792]{1,0:T(8,128)(2,1)}, bf16[64,1792]{1,0:T(8,128)(2,1)S(1)}, u32[]{:S(2)}, u32[]{:S(2)}) %collective-permute-start.18) | collective-permute-done | bytes 229408 | tf_op jit(solution)/shard_map/ppermute | solution.py:182
  110.5 3.1 %collective-permute-done.17 = bf16[128,1792]{1,0:T(8,128)(2,1)S(1)} collective-permute-done((bf16[128,1792]{1,0:T(8,128)(2,1)S(1)}, bf16[128,1792]{1,0:T(8,128)(2,1)S(1)}, u32[]{:S(2)}, u32[]{:S(2)}) %collective-permute-start.17) | collective-permute-done | bytes 458784 | tf_op jit(solution)/shard_map/ppermute | solution.py:182
  114.0 6.3 %convolution_convert_fusion.1 = bf16[256,2560]{1,0:T(8,128)(2,1)S(1)} fusion(bf16[256,1792]{1,0:T(8,128)(2,1)S(1)} %get-tuple-element.24, bf16[1792,2560]{1,0:T(8,128)(2,1)} %param.17), kind=kOutput, calls=%fused_computation.1 | convolution fusion | flops 2349465600 | bytes 11403264 | tf_op jit(solution)/shard_map/dot_general | solution.py:194
  120.5 0.7 copy-done.6
  121.8 2.5 %convolution_convert_fusion = bf16[256,2560]{1,0:T(8,128)(2,1)S(1)} fusion(bf16[256,1792]{1,0:T(8,128)(2,1)S(1)} %get-tuple-element.24, bf16[1792,2560]{1,0:T(8,128)(2,1)S(1)} %bitcast.177), kind=kOutput, calls=%fused_computation | convolution fusion | flops 2349465600 | bytes 11403264 | tf_op jit(solution)/shard_map/dot_general | solution.py:194
  124.5 1.0 fusion.3
  125.5 1.5 collective-permute-start.21
  127.5 1.0 collective-permute-start.28
  128.5 1.1 collective-permute-start.26
  129.5 5.0 %collective-permute-done.19 = bf16[64,1792]{1,0:T(8,128)(2,1)S(1)} collective-permute-done((bf16[64,1792]{1,0:T(8,128)(2,1)S(1)}, bf16[64,1792]{1,0:T(8,128)(2,1)S(1)}, u32[]{:S(2)}, u32[]{:S(2)}) %collective-permute-start.19) | collective-permute-done | bytes 229408 | tf_op jit(solution)/shard_map/ppermute | solution.py:182
  134.6 8.7 %collective-permute-done.21 = bf16[128,2560]{1,0:T(8,128)(2,1)S(1)} collective-permute-done((bf16[128,2560]{1,0:T(8,128)(2,1)}, bf16[128,2560]{1,0:T(8,128)(2,1)S(1)}, u32[]{:S(2)}, u32[]{:S(2)}) %collective-permute-start.21) | collective-permute-done | bytes 655392 | tf_op jit(solution)/shard_map/ppermute | solution.py:182
  143.3 2.1 collective-permute-start.27
  145.6 5.4 %convolution_convert_fusion.4 = bf16[128,2560]{1,0:T(8,128)(2,1)S(1)} fusion(bf16[1792,2560]{1,0:T(8,128)(2,1)} %param.18, bf16[128,1792]{1,0:T(8,128)(2,1)S(1)} %pad_maximum_fusion.14, f32[1792]{0:T(1024)S(1)} %copy-done.2), kind=kOutput, calls=%fused_computation.4 | convolution fusion | flops 1175420928 | bytes 10296320 | tf_op jit(solution)/shard_map/dot_general | solution.py:194
  151.0 5.1 %convolution_convert_fusion.5 = bf16[128,2560]{1,0:T(8,128)(2,1)S(1)} fusion(bf16[1792,2560]{1,0:T(8,128)(2,1)} %param.17, bf16[128,1792]{1,0:T(8,128)(2,1)S(1)} %pad_maximum_fusion.14, f32[1792]{0:T(1024)S(1)} %copy-done.2), kind=kOutput, calls=%fused_computation.5 | convolution fusion | flops 1175420928 | bytes 10296320 | tf_op jit(solution)/shard_map/dot_general | solution.py:194
  156.3 0.5 collective-permute-start.23
  157.2 1.4 convolution_convert_fusion.2
  158.6 1.4 slice-done.7
  160.1 1.4 convolution_convert_fusion.3
  162.3 0.4 collective-permute-done.30
  163.1 1.2 collective-permute-done.29
  164.4 0.6 fusion.14
  165.3 1.5 collective-permute-start.31
  166.8 0.4 collective-permute-done.32
  167.3 4.8 %shard_map.116 = bf16[256,1792]{1,0:T(8,128)(2,1)S(1)} custom-call(bf16[256,2560]{1,0:T(8,128)(2,1)S(1)} %pad_maximum_fusion.rows, bf16[2560,1792]{1,0:T(8,128)(2,1)} %weight.7), custom_call_target="tpu_custom_call" | custom-call | flops 1024 | bytes 1024 | tf_op jit(solution)/shard_map/pallas_call | solution.py:230
  172.2 1.4 collective-permute-start.34
  173.5 0.8 pad_maximum_fusion.13
  174.3 7.9 %collective-permute-done.31 = bf16[128,2560]{1,0:T(8,128)(2,1)S(1)} collective-permute-done((bf16[128,2560]{1,0:T(8,128)(2,1)S(1)}, bf16[128,2560]{1,0:T(8,128)(2,1)S(1)}, u32[]{:S(2)}, u32[]{:S(2)}) %collective-permute-start.31) | collective-permute-done | bytes 655392 | tf_op jit(solution)/shard_map/ppermute | solution.py:182
  182.3 2.5 %collective-permute-done.34 = bf16[2,64,1792]{2,1,0:T(8,128)(2,1)S(1)} collective-permute-done((bf16[2,64,1792]{2,1,0:T(8,128)(2,1)S(1)}, bf16[2,64,1792]{2,1,0:T(8,128)(2,1)S(1)}, u32[]{:S(2)}, u32[]{:S(2)}) %collective-permute-start.34) | collective-permute-done | bytes 458784 | tf_op jit(solution)/shard_map/ppermute | solution.py:182
  185.0 4.8 %shard_map.117 = bf16[256,1792]{1,0:T(8,128)(2,1)S(1)} custom-call(bf16[256,2560]{1,0:T(8,128)(2,1)S(1)} %pad_maximum_fusion.1.rows, bf16[2560,1792]{1,0:T(8,128)(2,1)} %weight.7), custom_call_target="tpu_custom_call" | custom-call | flops 1024 | bytes 1024 | tf_op jit(solution)/shard_map/pallas_call | solution.py:230
  189.9 1.6 collective-permute-start.35
  191.4 1.4 collective-permute-start.37
  192.8 14.1 %collective-permute-done.35 = bf16[2,64,1792]{2,1,0:T(8,128)(2,1)S(1)} collective-permute-done((bf16[2,64,1792]{2,1,0:T(8,128)(2,1)S(1)}, bf16[2,64,1792]{2,1,0:T(8,128)(2,1)S(1)}, u32[]{:S(2)}, u32[]{:S(2)}) %collective-permute-start.35) | collective-permute-done | bytes 458784 | tf_op jit(solution)/shard_map/ppermute | solution.py:182
  207.3 11.1 %collective-permute-done.36 = bf16[64,1792]{1,0:T(8,128)(2,1)S(1)} collective-permute-done((bf16[64,1792]{1,0:T(8,128)(2,1)S(1)}, bf16[64,1792]{1,0:T(8,128)(2,1)S(1)}, u32[]{:S(2)}, u32[]{:S(2)}) %collective-permute-start.36) | collective-permute-done | bytes 229408 | tf_op jit(solution)/shard_map/ppermute | solution.py:182
  218.7 0.8 pad_maximum_fusion.15
  (137 shorter events, 8.7 us)
Async XLA Ops:
  1.5 13.5 %collective-permute-start.2 = (bf16[288,128]{1,0:T(8,128)(2,1)S(1)}, bf16[288,128]{1,0:T(8,128)(2,1)S(1)}, u32[]{:S(2)}, u32[]{:S(2)}) collective-permute-start(bf16[288,128]{1,0:T(8,128)(2,1)S(1)} %constant_dynamic-slice_fusion.14), channel_id=1, source_target_pairs={{0,4},{4,8},{8,12},{1,5},{5,9},{9,13},{2,6},{6,10},{10,14},{3,7},{... | collective-permute-start | bytes 221192 | tf_op jit(solution)/shard_map/ppermute | solution.py:257
  6.5 8.5 %collective-permute-start.1 = (bf16[288,128]{1,0:T(8,128)(2,1)S(1)}, bf16[288,128]{1,0:T(8,128)(2,1)S(1)}, u32[]{:S(2)}, u32[]{:S(2)}) collective-permute-start(bf16[288,128]{1,0:T(8,128)(2,1)S(1)} %constant_dynamic-slice_fusion.14), channel_id=1, source_target_pairs={{0,8},{4,12},{1,9},{5,13},{2,10},{6,14},{3,11},{7,15},{16,24},{20,... | collective-permute-start | bytes 221192 | tf_op jit(solution)/shard_map/ppermute | solution.py:257
  11.0 4.0 %collective-permute-start = (bf16[288,128]{1,0:T(8,128)(2,1)S(1)}, bf16[288,128]{1,0:T(8,128)(2,1)S(1)}, u32[]{:S(2)}, u32[]{:S(2)}) collective-permute-start(bf16[288,128]{1,0:T(8,128)(2,1)S(1)} %constant_dynamic-slice_fusion.14), channel_id=1, source_target_pairs={{0,12},{1,13},{2,14},{3,15},{16,28},{17,29},{18,30},{19,31}} | collective-permute-start | bytes 221192 | tf_op jit(solution)/shard_map/ppermute | solution.py:257
  14.6 2.0 copy-start.4
  15.0 1.5 collective-permute-start.3
  16.6 1.6 copy-start.1
  16.8 2.2 copy-start
  25.8 5.5 %collective-permute-start.6 = (bf16[32,2048]{1,0:T(8,128)(2,1)S(1)}, bf16[32,2048]{1,0:T(8,128)(2,1)S(1)}, u32[]{:S(2)}, u32[]{:S(2)}) collective-permute-start(bf16[32,2048]{1,0:T(8,128)(2,1)S(1)} %get-tuple-element.66), channel_id=1, source_target_pairs={{0,3},{1,2},{2,1},{3,0},{4,7},{5,6},{6,5},{7,4},{8,11},{9,10},{10,... | collective-permute-start | bytes 393224 | tf_op jit(solution)/shard_map/ppermute | solution.py:182
  27.1 7.4 %collective-permute-start.5 = (bf16[32,2048]{1,0:T(8,128)(2,1)S(1)}, bf16[32,2048]{1,0:T(8,128)(2,1)S(1)}, u32[]{:S(2)}, u32[]{:S(2)}) collective-permute-start(bf16[32,2048]{1,0:T(8,128)(2,1)S(1)} %get-tuple-element.67), channel_id=1, source_target_pairs={{0,2},{1,3},{2,0},{3,1},{4,6},{5,7},{6,4},{7,5},{8,10},{9,11},{10,... | collective-permute-start | bytes 393224 | tf_op jit(solution)/shard_map/ppermute | solution.py:182
  27.7 6.8 %collective-permute-start.4 = (bf16[32,2048]{1,0:T(8,128)(2,1)S(1)}, bf16[32,2048]{1,0:T(8,128)(2,1)S(1)}, u32[]{:S(2)}, u32[]{:S(2)}) collective-permute-start(bf16[32,2048]{1,0:T(8,128)(2,1)S(1)} %get-tuple-element.68), channel_id=1, source_target_pairs={{0,1},{1,0},{2,3},{3,2},{4,5},{5,4},{6,7},{7,6},{8,9},{9,8},{10,11... | collective-permute-start | bytes 393224 | tf_op jit(solution)/shard_map/ppermute | solution.py:182
  34.6 8.3 %collective-permute-start.9 = (bf16[32,2048]{1,0:T(8,128)(2,1)S(1)}, bf16[32,2048]{1,0:T(8,128)(2,1)S(1)}, u32[]{:S(2)}, u32[]{:S(2)}) collective-permute-start(bf16[32,2048]{1,0:T(8,128)(2,1)S(1)} %get-tuple-element.62), channel_id=1, source_target_pairs={{0,12},{4,8},{8,4},{12,0},{1,13},{5,9},{9,5},{13,1},{2,14},{6,10},... | collective-permute-start | bytes 393224 | tf_op jit(solution)/shard_map/ppermute | solution.py:182
  38.3 10.2 %collective-permute-start.8 = (bf16[32,2048]{1,0:T(8,128)(2,1)S(1)}, bf16[32,2048]{1,0:T(8,128)(2,1)S(1)}, u32[]{:S(2)}, u32[]{:S(2)}) collective-permute-start(bf16[32,2048]{1,0:T(8,128)(2,1)S(1)} %get-tuple-element.63), channel_id=1, source_target_pairs={{0,8},{4,12},{8,0},{12,4},{1,9},{5,13},{9,1},{13,5},{2,10},{6,14},... | collective-permute-start | bytes 393224 | tf_op jit(solution)/shard_map/ppermute | solution.py:182
  38.3 10.2 %collective-permute-start.7 = (bf16[32,2048]{1,0:T(8,128)(2,1)S(1)}, bf16[32,2048]{1,0:T(8,128)(2,1)S(1)}, u32[]{:S(2)}, u32[]{:S(2)}) collective-permute-start(bf16[32,2048]{1,0:T(8,128)(2,1)S(1)} %get-tuple-element.64), channel_id=1, source_target_pairs={{0,4},{4,0},{8,12},{12,8},{1,5},{5,1},{9,13},{13,9},{2,6},{6,2},{1... | collective-permute-start | bytes 393224 | tf_op jit(solution)/shard_map/ppermute | solution.py:182
  48.6 2.0 collective-permute-start.10
  48.6 14.3 %collective-permute-start.13 = (bf16[4,32,2048]{2,1,0:T(8,128)(2,1)S(1)}, bf16[4,32,2048]{2,1,0:T(8,128)(2,1)S(1)}, u32[]{:S(2)}, u32[]{:S(2)}) collective-permute-start(bf16[4,32,2048]{2,1,0:T(8,128)(2,1)S(1)} %pad_maximum_fusion.11), channel_id=1, source_target_pairs={{0,2},{1,3},{2,0},{3,1},{4,6},{5,7},{6,4},{7,5},{8,10},{9,11},{10,... | collective-permute-start | bytes 1572872 | tf_op jit(solution)/shard_map/ppermute | solution.py:182
  55.0 12.6 %collective-permute-start.11 = (bf16[2,64,1792]{2,1,0:T(8,128)(2,1)S(1)}, bf16[2,64,1792]{2,1,0:T(8,128)(2,1)S(1)}, u32[]{:S(2)}, u32[]{:S(2)}) collective-permute-start(bf16[2,64,1792]{2,1,0:T(8,128)(2,1)S(1)} %slice_bitcast_fusion.5), channel_id=1, source_target_pairs={{0,4},{4,0},{8,12},{12,8},{1,5},{5,1},{9,13},{13,9},{2,6},{6,2},{1... | collective-permute-start | bytes 1376264 | tf_op jit(solution)/shard_map/ppermute | solution.py:182
  63.0 6.2 %collective-permute-start.14 = (bf16[4,32,2048]{2,1,0:T(8,128)(2,1)S(1)}, bf16[4,32,2048]{2,1,0:T(8,128)(2,1)S(1)}, u32[]{:S(2)}, u32[]{:S(2)}) collective-permute-start(bf16[4,32,2048]{2,1,0:T(8,128)(2,1)S(1)} %collective-permute-done.13), channel_id=1, source_target_pairs={{0,1},{1,0},{2,3},{3,2},{4,5},{5,4},{6,7},{7,6},{8,9},{9,8},{10,11... | collective-permute-start | bytes 1572872 | tf_op jit(solution)/shard_map/ppermute | solution.py:182
  67.7 12.7 %collective-permute-start.12 = (bf16[64,1792]{1,0:T(8,128)(2,1)S(1)}, bf16[64,1792]{1,0:T(8,128)(2,1)S(1)}, u32[]{:S(2)}, u32[]{:S(2)}) collective-permute-start(bf16[64,1792]{1,0:T(8,128)(2,1)S(1)} %fusion.20), channel_id=1, source_target_pairs={{0,8},{4,12},{8,0},{12,4},{1,9},{5,13},{9,1},{13,5},{2,10},{6,14},... | collective-permute-start | bytes 688136 | tf_op jit(solution)/shard_map/ppermute | solution.py:182
  69.4 11.0 %copy-start.3 = (bf16[128,1792]{1,0:T(8,128)(2,1)S(1)}, bf16[128,1792]{1,0:T(8,128)(2,1)}, u32[]{:S(2)}) copy-start(bf16[128,1792]{1,0:T(8,128)(2,1)} %param.10) | copy-start | bytes 1376260
  80.4 33.2 %copy-start.2 = (f32[1792]{0:T(1024)S(1)}, f32[1792]{0:T(1024)}, u32[]{:S(2)}) copy-start(f32[1792]{0:T(1024)} %param.16) | copy-start | bytes 21508
  80.5 13.4 %collective-permute-start.16 = (bf16[64,1792]{1,0:T(8,128)(2,1)S(1)}, bf16[64,1792]{1,0:T(8,128)(2,1)S(1)}, u32[]{:S(2)}, u32[]{:S(2)}) collective-permute-start(bf16[64,1792]{1,0:T(8,128)(2,1)S(1)} %fusion.23), channel_id=1, source_target_pairs={{0,8},{4,12},{8,0},{12,4},{1,9},{5,13},{9,1},{13,5},{2,10},{6,14},... | collective-permute-start | bytes 688136 | tf_op jit(solution)/shard_map/ppermute | solution.py:182
  80.6 19.3 %collective-permute-start.15 = (bf16[2,64,1792]{2,1,0:T(8,128)(2,1)S(1)}, bf16[2,64,1792]{2,1,0:T(8,128)(2,1)S(1)}, u32[]{:S(2)}, u32[]{:S(2)}) collective-permute-start(bf16[2,64,1792]{2,1,0:T(8,128)(2,1)S(1)} %slice_bitcast_fusion.4), channel_id=1, source_target_pairs={{0,4},{4,0},{8,12},{12,8},{1,5},{5,1},{9,13},{13,9},{2,6},{6,2},{1... | collective-permute-start | bytes 1376264 | tf_op jit(solution)/shard_map/ppermute | solution.py:182
  93.9 19.7 %collective-permute-start.17 = (bf16[128,1792]{1,0:T(8,128)(2,1)S(1)}, bf16[128,1792]{1,0:T(8,128)(2,1)S(1)}, u32[]{:S(2)}, u32[]{:S(2)}) collective-permute-start(bf16[128,1792]{1,0:T(8,128)(2,1)S(1)} %pad_maximum_fusion.12), channel_id=1, source_target_pairs={{0,4},{4,0},{8,12},{12,8},{1,5},{5,1},{9,13},{13,9},{2,6},{6,2},{1... | collective-permute-start | bytes 1376264 | tf_op jit(solution)/shard_map/ppermute | solution.py:182
  100.6 9.9 %collective-permute-start.18 = (bf16[64,1792]{1,0:T(8,128)(2,1)}, bf16[64,1792]{1,0:T(8,128)(2,1)S(1)}, u32[]{:S(2)}, u32[]{:S(2)}) collective-permute-start(bf16[64,1792]{1,0:T(8,128)(2,1)} %fusion.16), channel_id=1, source_target_pairs={{0,8},{4,12},{8,0},{12,4},{1,9},{5,13},{9,1},{13,5},{2,10},{6,14},... | collective-permute-start | bytes 688136 | tf_op jit(solution)/shard_map/ppermute | solution.py:182
  110.5 9.8 %copy-start.5 = (bf16[64,1792]{1,0:T(8,128)(2,1)}, bf16[64,1792]{1,0:T(8,128)(2,1)S(1)}, u32[]{:S(2)}) copy-start(bf16[64,1792]{1,0:T(8,128)(2,1)S(1)} %collective-permute-done.18) | copy-start | bytes 688132
  113.6 8.1 %slice-start = ((s8[9175040]{0:T(1024)(128)(4,1)}), s8[4194304]{0:T(1024)(128)(4,1)S(1)}, s32[]{:S(2)}) async-start(s8[9175040]{0:T(1024)(128)(4,1)} %bitcast.176), calls=%async_computation | async-start | bytes 8388608
  114.0 7.8 %slice-start.1 = ((s8[9175040]{0:T(1024)(128)(4,1)}), s8[4194304]{0:T(1024)(128)(4,1)S(1)}, s32[]{:S(2)}) async-start(s8[9175040]{0:T(1024)(128)(4,1)} %bitcast.176), calls=%async_computation.1 | async-start | bytes 8388608
  114.0 7.8 %slice-start.2 = ((s8[9175040]{0:T(1024)(128)(4,1)}), s8[786432]{0:T(1024)(128)(4,1)S(1)}, s32[]{:S(2)}) async-start(s8[9175040]{0:T(1024)(128)(4,1)} %bitcast.176), calls=%async_computation.2 | async-start | bytes 1572864
  120.3 0.9 copy-start.6
  120.5 4.0 %collective-permute-start.20 = (bf16[128,2560]{1,0:T(8,128)(2,1)S(1)}, bf16[128,2560]{1,0:T(8,128)(2,1)S(1)}, u32[]{:S(2)}, u32[]{:S(2)}) collective-permute-start(bf16[128,2560]{1,0:T(8,128)(2,1)S(1)} %bitcast.184), channel_id=1, source_target_pairs={{0,1},{1,0},{2,3},{3,2},{4,5},{5,4},{6,7},{7,6},{8,9},{9,8},{10,11... | collective-permute-start | bytes 1966088 | tf_op jit(solution)/shard_map/ppermute | solution.py:182
  121.4 13.2 %collective-permute-start.19 = (bf16[64,1792]{1,0:T(8,128)(2,1)S(1)}, bf16[64,1792]{1,0:T(8,128)(2,1)S(1)}, u32[]{:S(2)}, u32[]{:S(2)}) collective-permute-start(bf16[64,1792]{1,0:T(8,128)(2,1)S(1)} %get-tuple-element.36), channel_id=1, source_target_pairs={{0,8},{4,12},{8,0},{12,4},{1,9},{5,13},{9,1},{13,5},{2,10},{6,14},... | collective-permute-start | bytes 688136 | tf_op jit(solution)/shard_map/ppermute | solution.py:182
  124.4 2.6 %collective-permute-start.22 = (bf16[128,2560]{1,0:T(8,128)(2,1)S(1)}, bf16[128,2560]{1,0:T(8,128)(2,1)S(1)}, u32[]{:S(2)}, u32[]{:S(2)}) collective-permute-start(bf16[128,2560]{1,0:T(8,128)(2,1)S(1)} %bitcast.185), channel_id=1, source_target_pairs={{0,1},{1,0},{2,3},{3,2},{4,5},{5,4},{6,7},{7,6},{8,9},{9,8},{10,11... | collective-permute-start | bytes 1966088 | tf_op jit(solution)/shard_map/ppermute | solution.py:182
  125.5 17.7 %collective-permute-start.21 = (bf16[128,2560]{1,0:T(8,128)(2,1)}, bf16[128,2560]{1,0:T(8,128)(2,1)S(1)}, u32[]{:S(2)}, u32[]{:S(2)}) collective-permute-start(bf16[128,2560]{1,0:T(8,128)(2,1)} %fusion.3), channel_id=1, source_target_pairs={{0,2},{1,3},{2,0},{3,1},{4,6},{5,7},{6,4},{7,5},{8,10},{9,11},{10,... | collective-permute-start | bytes 1966088 | tf_op jit(solution)/shard_map/ppermute | solution.py:182
  127.2 1.2 collective-permute-start.25
  127.5 29.4 %collective-permute-start.28 = (bf16[128,2560]{1,0:T(8,128)(2,1)S(1)}, bf16[128,2560]{1,0:T(8,128)(2,1)S(1)}, u32[]{:S(2)}, u32[]{:S(2)}) collective-permute-start(bf16[128,2560]{1,0:T(8,128)(2,1)S(1)} %fusion.2), channel_id=1, source_target_pairs={{0,2},{1,3},{2,0},{3,1},{4,6},{5,7},{6,4},{7,5},{8,10},{9,11},{10,... | collective-permute-start | bytes 1966088 | tf_op jit(solution)/shard_map/ppermute | solution.py:182
  128.5 33.8 %collective-permute-start.26 = (f32[256]{0:T(256)S(1)}, f32[256]{0:T(256)S(1)}, u32[]{:S(2)}, u32[]{:S(2)}) collective-permute-start(f32[256]{0:T(256)S(1)} %add.261), channel_id=1, source_target_pairs={{0,2},{1,3},{2,0},{3,1},{4,6},{5,7},{6,4},{7,5},{8,10},{9,11},{10,... | collective-permute-start | bytes 3080 | tf_op jit(solution)/shard_map/ppermute | solution.py:182
  143.3 13.6 %collective-permute-start.27 = (bf16[128,1792]{1,0:T(8,128)(2,1)S(1)}, bf16[128,1792]{1,0:T(8,128)(2,1)S(1)}, u32[]{:S(2)}, u32[]{:S(2)}) collective-permute-start(bf16[128,1792]{1,0:T(8,128)(2,1)S(1)} %pad_maximum_fusion.14), channel_id=1, source_target_pairs={{0,4},{4,0},{8,12},{12,8},{1,5},{5,1},{9,13},{13,9},{2,6},{6,2},{1... | collective-permute-start | bytes 1376264 | tf_op jit(solution)/shard_map/ppermute | solution.py:182
  145.6 11.5 %slice-start.3 = ((s8[9175040]{0:T(1024)(128)(4,1)}), s8[4194304]{0:T(1024)(128)(4,1)S(1)}, s32[]{:S(2)}) async-start(s8[9175040]{0:T(1024)(128)(4,1)} %bitcast.178), calls=%async_computation.3 | async-start | bytes 8388608
  145.6 11.5 %slice-start.4 = ((s8[9175040]{0:T(1024)(128)(4,1)}), s8[4194304]{0:T(1024)(128)(4,1)S(1)}, s32[]{:S(2)}) async-start(s8[9175040]{0:T(1024)(128)(4,1)} %bitcast.178), calls=%async_computation.4 | async-start | bytes 8388608
  151.0 6.1 %slice-start.5 = ((s8[9175040]{0:T(1024)(128)(4,1)}), s8[786432]{0:T(1024)(128)(4,1)S(1)}, s32[]{:S(2)}) async-start(s8[9175040]{0:T(1024)(128)(4,1)} %bitcast.178), calls=%async_computation.5 | async-start | bytes 1572864
  156.1 6.2 %collective-permute-start.24 = (f32[128]{0:T(128)S(1)}, f32[128]{0:T(128)S(1)}, u32[]{:S(2)}, u32[]{:S(2)}) collective-permute-start(f32[128]{0:T(128)S(1)} %fusion.5), channel_id=1, source_target_pairs={{0,1},{1,0},{2,3},{3,2},{4,5},{5,4},{6,7},{7,6},{8,9},{9,8},{10,11... | collective-permute-start | bytes 1544 | tf_op jit(solution)/shard_map/ppermute | solution.py:182
  156.3 2.3 %slice-start.6 = ((s8[9175040]{0:T(1024)(128)(4,1)}), s8[4194304]{0:T(1024)(128)(4,1)S(1)}, s32[]{:S(2)}) async-start(s8[9175040]{0:T(1024)(128)(4,1)} %bitcast.180), calls=%async_computation.6 | async-start | bytes 8388608
  156.3 6.6 %collective-permute-start.23 = (bf16[128,2560]{1,0:T(8,128)(2,1)S(1)}, bf16[128,2560]{1,0:T(8,128)(2,1)S(1)}, u32[]{:S(2)}, u32[]{:S(2)}) collective-permute-start(bf16[128,2560]{1,0:T(8,128)(2,1)S(1)} %pad_maximum_fusion.5), channel_id=1, source_target_pairs={{0,1},{1,0},{2,3},{3,2},{4,5},{5,4},{6,7},{7,6},{8,9},{9,8},{10,11... | collective-permute-start | bytes 1966088 | tf_op jit(solution)/shard_map/ppermute | solution.py:182
  157.1 2.8 %slice-start.7 = ((s8[9175040]{0:T(1024)(128)(4,1)}), s8[4194304]{0:T(1024)(128)(4,1)S(1)}, s32[]{:S(2)}) async-start(s8[9175040]{0:T(1024)(128)(4,1)} %bitcast.180), calls=%async_computation.7 | async-start | bytes 8388608
  157.1 2.9 %slice-start.8 = ((s8[9175040]{0:T(1024)(128)(4,1)}), s8[786432]{0:T(1024)(128)(4,1)S(1)}, s32[]{:S(2)}) async-start(s8[9175040]{0:T(1024)(128)(4,1)} %bitcast.180), calls=%async_computation.8 | async-start | bytes 1572864
  161.5 1.2 collective-permute-start.30
  162.1 2.2 collective-permute-start.29
  165.1 2.2 collective-permute-start.32
  165.3 17.0 %collective-permute-start.31 = (bf16[128,2560]{1,0:T(8,128)(2,1)S(1)}, bf16[128,2560]{1,0:T(8,128)(2,1)S(1)}, u32[]{:S(2)}, u32[]{:S(2)}) collective-permute-start(bf16[128,2560]{1,0:T(8,128)(2,1)S(1)} %pad_maximum_fusion.7), channel_id=1, source_target_pairs={{0,2},{1,3},{2,0},{3,1},{4,6},{5,7},{6,4},{7,5},{8,10},{9,11},{10,... | collective-permute-start | bytes 1966088 | tf_op jit(solution)/shard_map/ppermute | solution.py:182
  172.2 12.6 %collective-permute-start.34 = (bf16[2,64,1792]{2,1,0:T(8,128)(2,1)S(1)}, bf16[2,64,1792]{2,1,0:T(8,128)(2,1)S(1)}, u32[]{:S(2)}, u32[]{:S(2)}) collective-permute-start(bf16[2,64,1792]{2,1,0:T(8,128)(2,1)S(1)} %slice_bitcast_fusion.2), channel_id=1, source_target_pairs={{0,4},{4,0},{8,12},{12,8},{1,5},{5,1},{9,13},{13,9},{2,6},{6,2},{1... | collective-permute-start | bytes 1376264 | tf_op jit(solution)/shard_map/ppermute | solution.py:182
  182.3 2.7 %collective-permute-start.33 = (bf16[128,2560]{1,0:T(8,128)(2,1)S(1)}, bf16[128,2560]{1,0:T(8,128)(2,1)S(1)}, u32[]{:S(2)}, u32[]{:S(2)}) collective-permute-start(bf16[128,2560]{1,0:T(8,128)(2,1)S(1)} %collective-permute-done.31), channel_id=1, source_target_pairs={{0,1},{1,0},{2,3},{3,2},{4,5},{5,4},{6,7},{7,6},{8,9},{9,8},{10,11... | collective-permute-start | bytes 1966088 | tf_op jit(solution)/shard_map/ppermute | solution.py:182
  189.9 17.0 %collective-permute-start.35 = (bf16[2,64,1792]{2,1,0:T(8,128)(2,1)S(1)}, bf16[2,64,1792]{2,1,0:T(8,128)(2,1)S(1)}, u32[]{:S(2)}, u32[]{:S(2)}) collective-permute-start(bf16[2,64,1792]{2,1,0:T(8,128)(2,1)S(1)} %slice_bitcast_fusion), channel_id=1, source_target_pairs={{0,4},{4,0},{8,12},{12,8},{1,5},{5,1},{9,13},{13,9},{2,6},{6,2},{1... | collective-permute-start | bytes 1376264 | tf_op jit(solution)/shard_map/ppermute | solution.py:182
  191.4 15.9 %collective-permute-start.37 = (bf16[64,1792]{1,0:T(8,128)(2,1)S(1)}, bf16[64,1792]{1,0:T(8,128)(2,1)S(1)}, u32[]{:S(2)}, u32[]{:S(2)}) collective-permute-start(bf16[64,1792]{1,0:T(8,128)(2,1)S(1)} %fusion.32), channel_id=1, source_target_pairs={{0,8},{4,12},{8,0},{12,4},{1,9},{5,13},{9,1},{13,5},{2,10},{6,14},... | collective-permute-start | bytes 688136 | tf_op jit(solution)/shard_map/ppermute | solution.py:182
  207.0 11.5 %collective-permute-start.36 = (bf16[64,1792]{1,0:T(8,128)(2,1)S(1)}, bf16[64,1792]{1,0:T(8,128)(2,1)S(1)}, u32[]{:S(2)}, u32[]{:S(2)}) collective-permute-start(bf16[64,1792]{1,0:T(8,128)(2,1)S(1)} %fusion.33), channel_id=1, source_target_pairs={{0,8},{4,12},{8,0},{12,4},{1,9},{5,13},{9,1},{13,5},{2,10},{6,14},... | collective-permute-start | bytes 688136 | tf_op jit(solution)/shard_map/ppermute | solution.py:182

commit v15 on v14

--- a/solution.py
+++ b/solution.py
@@ -245,6 +245,23 @@
     )(rows, weight)
 
 
+def add_kernel(mine, came, out):
+    out[...] = (mine[...].astype(jnp.float32) + came[...].astype(jnp.float32)).astype(out.dtype)
+
+
+def add_rows(mine, came):
+    whole = pl.BlockSpec(memory_space=pltpu.VMEM)
+    return pl.pallas_call(
+        add_kernel,
+        in_specs=[whole, whole],
+        out_specs=whole,
+        out_shape=jax.ShapeDtypeStruct(mine.shape, jnp.bfloat16),
+        cost_estimate=pl.CostEstimate(
+            flops=8 * 10**9, bytes_accessed=6 * mine.size, transcendentals=0
+        ),
+    )(mine, came)
+
+
 def after(value, earlier):
     return lax.optimization_barrier((value, earlier))[0]
 
@@ -301,8 +318,8 @@
         sent = blocks[:, 1]
         return blocks[:, 0], sent, swap(sent, "ctx", 1)
 
-    def second_hop(kept, came):
-        other = (wide(kept[1]) + wide(came[1])).astype(jnp.bfloat16)
+    def second_hop(kept, came, add=lambda a, b: (wide(a) + wide(b)).astype(jnp.bfloat16)):
+        other = add(kept[1], came[1])
         return wide(kept[0]) + wide(came[0]), other, swap(other, "ctx", 2)
 
     def attend(mine, came, which):
@@ -336,7 +353,7 @@
     twin_a = swap(attended_a, "ctx", 2)
     pair_a = jnp.concatenate([attended_a, twin_a], axis=0)
     rest_a = swap(pair_a, "ctx", 1)
-    mine_b, other_b, last_b = second_hop(kept_b, after(came_b, pair_a))
+    mine_b, other_b, last_b = second_hop(kept_b, after(came_b, pair_a), add_rows)
     rest_a, last_b = lax.optimization_barrier((rest_a, last_b))
     attended_b = attend(mine_b, last_b, 1 - first_half)
     twin_b = swap(attended_b, "ctx", 2)

time: 220 us -> 218 us (level)
  waiting for transfers between devices: 117 us -> 111 us
    ppermute x35, waiting for transfers between devices: 117 us -> 111 us  [swap(): return lax.ppermute(value, axis_name, [(i, i ^ bit) for i in range(width)])]
  transfers between devices with their start and end apart: 38 -> 38, of which waited for: 23 -> 22; matrix products, arithmetic and copies ran while one was open for 11% -> 11% of each run, Pallas kernels for 6% -> 7%
where the time goes in v15:
time: 218 us
  waiting for transfers between devices  111 us (51%)
  starting transfers between devices  40.1 us (18%)
  Pallas kernels  26.4 us (12%)
  matrix products  22 us (10%)
  other arithmetic  9.23 us (4%)
  local copies, waits for them, and re-layouts  7.45 us (3%)
    ppermute x35, waiting for transfers between devices, swap(): return lax.ppermute(value, axis_name, [(i, i ^ bit) for i in range(width)])  111 us
    ppermute x35, starting transfers between devices, swap(): return lax.ppermute(value, axis_name, [(i, i ^ bit) for i in range(width)])  29.4 us
    dot_general x6, matrix products, matmul(): jnp.dot(a, b, preferred_element_type=jnp.float32).astype(jnp.bfloat16)  22 us
    pallas_call x4, Pallas kernels, streamed_matmul(): pl.pallas_call(functools.partial(streamed_kernel, 512), in_specs=[pl.Bloc...  17.9 us
    ppermute x3, starting transfers between devices, gather_keys(): lax.ppermute(half, 'ctx', [(c, c + d) for c in range(n_ctx - d)])  10.7 us
    pallas_call x1, Pallas kernels, attention(): pl.pallas_call(functools.partial(attention_kernel, group), grid=(local_he...  6.79 us
  transfers between devices with their start and end apart: 38, of which 22 were waited for; matrix products, arithmetic and copies ran while one was open for 11% of the time, Pallas kernels for 7%

profile of v15, /device:TPU:0, one launch (start us, length us, event | category | flops | bytes accessed | tf_op | source)
XLA Modules:
  0.0 218.0 jit_solution(11274145924639899227)
XLA Ops:
  0.6 0.9 constant_dynamic-slice_fusion.14
  1.5 4.9 %collective-permute-start.2 = (bf16[288,128]{1,0:T(8,128)(2,1)S(1)}, bf16[288,128]{1,0:T(8,128)(2,1)S(1)}, u32[]{:S(2)}, u32[]{:S(2)}) collective-permute-start(bf16[288,128]{1,0:T(8,128)(2,1)S(1)} %constant_dynamic-slice_fusion.14), channel_id=1, source_target_pairs={{0,4},{4,8},{8,12},{1,5},{5,9},{9,13},{2,6},{6,10},{10,14},{3,7},{... | collective-permute-start | bytes 221192 | tf_op jit(solution)/shard_map/ppermute | solution.py:274
  6.5 4.5 %collective-permute-start.1 = (bf16[288,128]{1,0:T(8,128)(2,1)S(1)}, bf16[288,128]{1,0:T(8,128)(2,1)S(1)}, u32[]{:S(2)}, u32[]{:S(2)}) collective-permute-start(bf16[288,128]{1,0:T(8,128)(2,1)S(1)} %constant_dynamic-slice_fusion.14), channel_id=1, source_target_pairs={{0,8},{4,12},{1,9},{5,13},{2,10},{6,14},{3,11},{7,15},{16,24},{20,... | collective-permute-start | bytes 221192 | tf_op jit(solution)/shard_map/ppermute | solution.py:274
  11.0 1.3 collective-permute-start
  12.3 0.8 reduce-window.8
  13.2 0.7 subtract_subtract_fusion
  15.1 1.5 collective-permute-done.3
  17.2 1.0 copy-done.1
  18.2 0.7 copy-done
  19.0 6.8 %shard_map.113 = bf16[128,2048]{1,0:T(8,128)(2,1)S(1)} custom-call(f32[4,128,128]{2,1,0:T(8,128)S(1)} %pad_maximum_fusion.16.tables, s32[128,1]{1,0:T(8,128)S(1)} %copy.23.starts, s32[128,1]{1,0:T(8,128)S(1)} %iota_add_fusion.own_index, s32[1,512]{1,0:T(1,128)S(1)} %iota_add_fusion.2.key_index, bf16[576,512]{1,0:T(8,128)(2,1)S(1)} %pad_maximum_fusion.9.keys, ...), custom_call_target="tpu_custom_call" | custom-call | flops 2684354560 | bytes 5046272 | tf_op jit(solution)/shard_map/pallas_call | solution.py:143
  25.8 1.3 collective-permute-start.6
  27.7 3.6 %collective-permute-done.6 = bf16[32,2048]{1,0:T(8,128)(2,1)S(1)} collective-permute-done((bf16[32,2048]{1,0:T(8,128)(2,1)S(1)}, bf16[32,2048]{1,0:T(8,128)(2,1)S(1)}, u32[]{:S(2)}, u32[]{:S(2)}) %collective-permute-start.6) | collective-permute-done | bytes 131104 | tf_op jit(solution)/shard_map/ppermute | solution.py:182
  31.4 3.1 %collective-permute-done.5 = bf16[32,2048]{1,0:T(8,128)(2,1)S(1)} collective-permute-done((bf16[32,2048]{1,0:T(8,128)(2,1)S(1)}, bf16[32,2048]{1,0:T(8,128)(2,1)S(1)}, u32[]{:S(2)}, u32[]{:S(2)}) %collective-permute-start.5) | collective-permute-done | bytes 131104 | tf_op jit(solution)/shard_map/ppermute | solution.py:182
  34.6 3.7 %collective-permute-start.9 = (bf16[32,2048]{1,0:T(8,128)(2,1)S(1)}, bf16[32,2048]{1,0:T(8,128)(2,1)S(1)}, u32[]{:S(2)}, u32[]{:S(2)}) collective-permute-start(bf16[32,2048]{1,0:T(8,128)(2,1)S(1)} %get-tuple-element.62), channel_id=1, source_target_pairs={{0,12},{4,8},{8,4},{12,0},{1,13},{5,9},{9,5},{13,1},{2,14},{6,10},... | collective-permute-start | bytes 393224 | tf_op jit(solution)/shard_map/ppermute | solution.py:182
  38.3 0.8 collective-permute-start.7
  39.1 3.8 %collective-permute-done.9 = bf16[32,2048]{1,0:T(8,128)(2,1)S(1)} collective-permute-done((bf16[32,2048]{1,0:T(8,128)(2,1)S(1)}, bf16[32,2048]{1,0:T(8,128)(2,1)S(1)}, u32[]{:S(2)}, u32[]{:S(2)}) %collective-permute-start.9) | collective-permute-done | bytes 131104 | tf_op jit(solution)/shard_map/ppermute | solution.py:182
  42.9 5.6 %collective-permute-done.8 = bf16[32,2048]{1,0:T(8,128)(2,1)S(1)} collective-permute-done((bf16[32,2048]{1,0:T(8,128)(2,1)S(1)}, bf16[32,2048]{1,0:T(8,128)(2,1)S(1)}, u32[]{:S(2)}, u32[]{:S(2)}) %collective-permute-start.8) | collective-permute-done | bytes 131104 | tf_op jit(solution)/shard_map/ppermute | solution.py:182
  48.6 1.5 collective-permute-start.13
  50.9 4.1 %shard_map.114 = bf16[256,1792]{1,0:T(8,128)(2,1)S(1)} custom-call(bf16[256,2048]{1,0:T(8,128)(2,1)S(1)} %bitcast.160, bf16[2048,1792]{1,0:T(8,128)(2,1)} %weight.5), custom_call_target="tpu_custom_call" | custom-call | flops 1024 | bytes 1024 | tf_op jit(solution)/shard_map/pallas_call | solution.py:230
  55.0 0.8 collective-permute-start.11
  55.8 7.2 %collective-permute-done.13 = bf16[4,32,2048]{2,1,0:T(8,128)(2,1)S(1)} collective-permute-done((bf16[4,32,2048]{2,1,0:T(8,128)(2,1)S(1)}, bf16[4,32,2048]{2,1,0:T(8,128)(2,1)S(1)}, u32[]{:S(2)}, u32[]{:S(2)}) %collective-permute-start.13) | collective-permute-done | bytes 524320 | tf_op jit(solution)/shard_map/ppermute | solution.py:182
  63.0 4.7 %collective-permute-done.11 = bf16[2,64,1792]{2,1,0:T(8,128)(2,1)S(1)} collective-permute-done((bf16[2,64,1792]{2,1,0:T(8,128)(2,1)S(1)}, bf16[2,64,1792]{2,1,0:T(8,128)(2,1)S(1)}, u32[]{:S(2)}, u32[]{:S(2)}) %collective-permute-start.11) | collective-permute-done | bytes 458784 | tf_op jit(solution)/shard_map/ppermute | solution.py:182
  67.7 1.5 collective-permute-start.12
  69.4 4.2 %shard_map.115 = bf16[256,1792]{1,0:T(8,128)(2,1)S(1)} custom-call(bf16[256,2048]{1,0:T(8,128)(2,1)S(1)} %bitcast.159, bf16[2048,1792]{1,0:T(8,128)(2,1)} %weight.5), custom_call_target="tpu_custom_call" | custom-call | flops 1024 | bytes 1024 | tf_op jit(solution)/shard_map/pallas_call | solution.py:230
  73.6 1.8 collective-permute-start.15
  75.5 5.1 %collective-permute-done.12 = bf16[64,1792]{1,0:T(8,128)(2,1)S(1)} collective-permute-done((bf16[64,1792]{1,0:T(8,128)(2,1)S(1)}, bf16[64,1792]{1,0:T(8,128)(2,1)S(1)}, u32[]{:S(2)}, u32[]{:S(2)}) %collective-permute-start.12) | collective-permute-done | bytes 229408 | tf_op jit(solution)/shard_map/ppermute | solution.py:182
  80.7 0.7 slice_bitcast_fusion.6.mine
  81.4 12.5 %collective-permute-done.16 = bf16[64,1792]{1,0:T(8,128)(2,1)S(1)} collective-permute-done((bf16[64,1792]{1,0:T(8,128)(2,1)S(1)}, bf16[64,1792]{1,0:T(8,128)(2,1)S(1)}, u32[]{:S(2)}, u32[]{:S(2)}) %collective-permute-start.16) | collective-permute-done | bytes 229408 | tf_op jit(solution)/shard_map/ppermute | solution.py:182
  94.1 1.0 collective-permute-done.15
  95.1 0.7 slice_bitcast_fusion.12.came
  95.8 1.8 shard_map.116
  97.6 2.1 collective-permute-start.18
  99.7 9.0 %collective-permute-done.18 = bf16[64,1792]{1,0:T(8,128)(2,1)S(1)} collective-permute-done((bf16[64,1792]{1,0:T(8,128)(2,1)}, bf16[64,1792]{1,0:T(8,128)(2,1)S(1)}, u32[]{:S(2)}, u32[]{:S(2)}) %collective-permute-start.18) | collective-permute-done | bytes 229408 | tf_op jit(solution)/shard_map/ppermute | solution.py:182
  108.7 2.1 collective-permute-done.17
  111.2 6.3 %convolution_convert_fusion.1 = bf16[256,2560]{1,0:T(8,128)(2,1)S(1)} fusion(bf16[256,1792]{1,0:T(8,128)(2,1)S(1)} %get-tuple-element.24, bf16[1792,2560]{1,0:T(8,128)(2,1)} %param.17), kind=kOutput, calls=%fused_computation.1 | convolution fusion | flops 2349465600 | bytes 11403264 | tf_op jit(solution)/shard_map/dot_general | solution.py:194
  117.7 0.8 copy-done.4
  118.7 1.3 collective-permute-start.19
  119.9 2.5 %convolution_convert_fusion = bf16[256,2560]{1,0:T(8,128)(2,1)S(1)} fusion(bf16[256,1792]{1,0:T(8,128)(2,1)S(1)} %get-tuple-element.24, bf16[1792,2560]{1,0:T(8,128)(2,1)S(1)} %bitcast.173), kind=kOutput, calls=%fused_computation | convolution fusion | flops 2349465600 | bytes 11403264 | tf_op jit(solution)/shard_map/dot_general | solution.py:194
  122.7 1.0 fusion.3
  123.7 1.5 collective-permute-start.21
  125.7 1.0 collective-permute-start.28
  126.6 1.1 collective-permute-start.26
  127.7 4.0 %collective-permute-done.19 = bf16[64,1792]{1,0:T(8,128)(2,1)S(1)} collective-permute-done((bf16[64,1792]{1,0:T(8,128)(2,1)S(1)}, bf16[64,1792]{1,0:T(8,128)(2,1)S(1)}, u32[]{:S(2)}, u32[]{:S(2)}) %collective-permute-start.19) | collective-permute-done | bytes 229408 | tf_op jit(solution)/shard_map/ppermute | solution.py:182
  131.7 9.7 %collective-permute-done.21 = bf16[128,2560]{1,0:T(8,128)(2,1)S(1)} collective-permute-done((bf16[128,2560]{1,0:T(8,128)(2,1)}, bf16[128,2560]{1,0:T(8,128)(2,1)S(1)}, u32[]{:S(2)}, u32[]{:S(2)}) %collective-permute-start.21) | collective-permute-done | bytes 655392 | tf_op jit(solution)/shard_map/ppermute | solution.py:182
  141.5 2.2 %collective-permute-start.27 = (bf16[128,1792]{1,0:T(8,128)(2,1)S(1)}, bf16[128,1792]{1,0:T(8,128)(2,1)S(1)}, u32[]{:S(2)}, u32[]{:S(2)}) collective-permute-start(bf16[128,1792]{1,0:T(8,128)(2,1)S(1)} %pad_maximum_fusion.14), channel_id=1, source_target_pairs={{0,4},{4,0},{8,12},{12,8},{1,5},{5,1},{9,13},{13,9},{2,6},{6,2},{1... | collective-permute-start | bytes 1376264 | tf_op jit(solution)/shard_map/ppermute | solution.py:182
  143.9 5.4 %convolution_convert_fusion.4 = bf16[128,2560]{1,0:T(8,128)(2,1)S(1)} fusion(bf16[1792,2560]{1,0:T(8,128)(2,1)} %param.18, bf16[128,1792]{1,0:T(8,128)(2,1)S(1)} %pad_maximum_fusion.14, f32[1792]{0:T(1024)S(1)} %copy-done.2), kind=kOutput, calls=%fused_computation.4 | convolution fusion | flops 1175420928 | bytes 10296320 | tf_op jit(solution)/shard_map/dot_general | solution.py:194
  149.3 5.1 %convolution_convert_fusion.5 = bf16[128,2560]{1,0:T(8,128)(2,1)S(1)} fusion(bf16[1792,2560]{1,0:T(8,128)(2,1)} %param.17, bf16[128,1792]{1,0:T(8,128)(2,1)S(1)} %pad_maximum_fusion.14, f32[1792]{0:T(1024)S(1)} %copy-done.2), kind=kOutput, calls=%fused_computation.5 | convolution fusion | flops 1175420928 | bytes 10296320 | tf_op jit(solution)/shard_map/dot_general | solution.py:194
  155.4 1.4 convolution_convert_fusion.2
  156.8 1.4 slice-done.7
  158.3 1.4 convolution_convert_fusion.3
  161.3 1.2 collective-permute-done.29
  162.6 0.6 fusion.14
  163.5 1.5 collective-permute-start.31
  165.6 4.8 %shard_map.117 = bf16[256,1792]{1,0:T(8,128)(2,1)S(1)} custom-call(bf16[256,2560]{1,0:T(8,128)(2,1)S(1)} %pad_maximum_fusion.rows, bf16[2560,1792]{1,0:T(8,128)(2,1)} %weight.7), custom_call_target="tpu_custom_call" | custom-call | flops 1024 | bytes 1024 | tf_op jit(solution)/shard_map/pallas_call | solution.py:230
  170.4 1.4 collective-permute-start.34
  171.8 0.8 pad_maximum_fusion.13
  172.6 7.9 %collective-permute-done.31 = bf16[128,2560]{1,0:T(8,128)(2,1)S(1)} collective-permute-done((bf16[128,2560]{1,0:T(8,128)(2,1)S(1)}, bf16[128,2560]{1,0:T(8,128)(2,1)S(1)}, u32[]{:S(2)}, u32[]{:S(2)}) %collective-permute-start.31) | collective-permute-done | bytes 655392 | tf_op jit(solution)/shard_map/ppermute | solution.py:182
  180.5 2.5 %collective-permute-done.34 = bf16[2,64,1792]{2,1,0:T(8,128)(2,1)S(1)} collective-permute-done((bf16[2,64,1792]{2,1,0:T(8,128)(2,1)S(1)}, bf16[2,64,1792]{2,1,0:T(8,128)(2,1)S(1)}, u32[]{:S(2)}, u32[]{:S(2)}) %collective-permute-start.34) | collective-permute-done | bytes 458784 | tf_op jit(solution)/shard_map/ppermute | solution.py:182
  183.3 4.8 %shard_map.118 = bf16[256,1792]{1,0:T(8,128)(2,1)S(1)} custom-call(bf16[256,2560]{1,0:T(8,128)(2,1)S(1)} %pad_maximum_fusion.1.rows, bf16[2560,1792]{1,0:T(8,128)(2,1)} %weight.7), custom_call_target="tpu_custom_call" | custom-call | flops 1024 | bytes 1024 | tf_op jit(solution)/shard_map/pallas_call | solution.py:230
  188.1 1.6 collective-permute-start.35
  189.7 1.2 collective-permute-start.37
  190.9 14.2 %collective-permute-done.35 = bf16[2,64,1792]{2,1,0:T(8,128)(2,1)S(1)} collective-permute-done((bf16[2,64,1792]{2,1,0:T(8,128)(2,1)S(1)}, bf16[2,64,1792]{2,1,0:T(8,128)(2,1)S(1)}, u32[]{:S(2)}, u32[]{:S(2)}) %collective-permute-start.35) | collective-permute-done | bytes 458784 | tf_op jit(solution)/shard_map/ppermute | solution.py:182
  205.5 11.4 %collective-permute-done.36 = bf16[64,1792]{1,0:T(8,128)(2,1)S(1)} collective-permute-done((bf16[64,1792]{1,0:T(8,128)(2,1)S(1)}, bf16[64,1792]{1,0:T(8,128)(2,1)S(1)}, u32[]{:S(2)}, u32[]{:S(2)}) %collective-permute-start.36) | collective-permute-done | bytes 229408 | tf_op jit(solution)/shard_map/ppermute | solution.py:182
  217.2 0.8 pad_maximum_fusion.15
  (137 shorter events, 10.1 us)
Async XLA Ops:
  1.5 13.5 %collective-permute-start.2 = (bf16[288,128]{1,0:T(8,128)(2,1)S(1)}, bf16[288,128]{1,0:T(8,128)(2,1)S(1)}, u32[]{:S(2)}, u32[]{:S(2)}) collective-permute-start(bf16[288,128]{1,0:T(8,128)(2,1)S(1)} %constant_dynamic-slice_fusion.14), channel_id=1, source_target_pairs={{0,4},{4,8},{8,12},{1,5},{5,9},{9,13},{2,6},{6,10},{10,14},{3,7},{... | collective-permute-start | bytes 221192 | tf_op jit(solution)/shard_map/ppermute | solution.py:274
  6.5 8.5 %collective-permute-start.1 = (bf16[288,128]{1,0:T(8,128)(2,1)S(1)}, bf16[288,128]{1,0:T(8,128)(2,1)S(1)}, u32[]{:S(2)}, u32[]{:S(2)}) collective-permute-start(bf16[288,128]{1,0:T(8,128)(2,1)S(1)} %constant_dynamic-slice_fusion.14), channel_id=1, source_target_pairs={{0,8},{4,12},{1,9},{5,13},{2,10},{6,14},{3,11},{7,15},{16,24},{20,... | collective-permute-start | bytes 221192 | tf_op jit(solution)/shard_map/ppermute | solution.py:274
  11.0 4.0 %collective-permute-start = (bf16[288,128]{1,0:T(8,128)(2,1)S(1)}, bf16[288,128]{1,0:T(8,128)(2,1)S(1)}, u32[]{:S(2)}, u32[]{:S(2)}) collective-permute-start(bf16[288,128]{1,0:T(8,128)(2,1)S(1)} %constant_dynamic-slice_fusion.14), channel_id=1, source_target_pairs={{0,12},{1,13},{2,14},{3,15},{16,28},{17,29},{18,30},{19,31}} | collective-permute-start | bytes 221192 | tf_op jit(solution)/shard_map/ppermute | solution.py:274
  14.6 2.0 copy-start.5
  15.0 1.5 collective-permute-start.3
  16.6 1.6 copy-start.1
  16.8 2.2 copy-start
  25.8 5.5 %collective-permute-start.6 = (bf16[32,2048]{1,0:T(8,128)(2,1)S(1)}, bf16[32,2048]{1,0:T(8,128)(2,1)S(1)}, u32[]{:S(2)}, u32[]{:S(2)}) collective-permute-start(bf16[32,2048]{1,0:T(8,128)(2,1)S(1)} %get-tuple-element.66), channel_id=1, source_target_pairs={{0,3},{1,2},{2,1},{3,0},{4,7},{5,6},{6,5},{7,4},{8,11},{9,10},{10,... | collective-permute-start | bytes 393224 | tf_op jit(solution)/shard_map/ppermute | solution.py:182
  27.1 7.4 %collective-permute-start.5 = (bf16[32,2048]{1,0:T(8,128)(2,1)S(1)}, bf16[32,2048]{1,0:T(8,128)(2,1)S(1)}, u32[]{:S(2)}, u32[]{:S(2)}) collective-permute-start(bf16[32,2048]{1,0:T(8,128)(2,1)S(1)} %get-tuple-element.67), channel_id=1, source_target_pairs={{0,2},{1,3},{2,0},{3,1},{4,6},{5,7},{6,4},{7,5},{8,10},{9,11},{10,... | collective-permute-start | bytes 393224 | tf_op jit(solution)/shard_map/ppermute | solution.py:182
  27.7 6.8 %collective-permute-start.4 = (bf16[32,2048]{1,0:T(8,128)(2,1)S(1)}, bf16[32,2048]{1,0:T(8,128)(2,1)S(1)}, u32[]{:S(2)}, u32[]{:S(2)}) collective-permute-start(bf16[32,2048]{1,0:T(8,128)(2,1)S(1)} %get-tuple-element.68), channel_id=1, source_target_pairs={{0,1},{1,0},{2,3},{3,2},{4,5},{5,4},{6,7},{7,6},{8,9},{9,8},{10,11... | collective-permute-start | bytes 393224 | tf_op jit(solution)/shard_map/ppermute | solution.py:182
  34.6 8.3 %collective-permute-start.9 = (bf16[32,2048]{1,0:T(8,128)(2,1)S(1)}, bf16[32,2048]{1,0:T(8,128)(2,1)S(1)}, u32[]{:S(2)}, u32[]{:S(2)}) collective-permute-start(bf16[32,2048]{1,0:T(8,128)(2,1)S(1)} %get-tuple-element.62), channel_id=1, source_target_pairs={{0,12},{4,8},{8,4},{12,0},{1,13},{5,9},{9,5},{13,1},{2,14},{6,10},... | collective-permute-start | bytes 393224 | tf_op jit(solution)/shard_map/ppermute | solution.py:182
  38.3 10.2 %collective-permute-start.8 = (bf16[32,2048]{1,0:T(8,128)(2,1)S(1)}, bf16[32,2048]{1,0:T(8,128)(2,1)S(1)}, u32[]{:S(2)}, u32[]{:S(2)}) collective-permute-start(bf16[32,2048]{1,0:T(8,128)(2,1)S(1)} %get-tuple-element.63), channel_id=1, source_target_pairs={{0,8},{4,12},{8,0},{12,4},{1,9},{5,13},{9,1},{13,5},{2,10},{6,14},... | collective-permute-start | bytes 393224 | tf_op jit(solution)/shard_map/ppermute | solution.py:182
  38.3 10.2 %collective-permute-start.7 = (bf16[32,2048]{1,0:T(8,128)(2,1)S(1)}, bf16[32,2048]{1,0:T(8,128)(2,1)S(1)}, u32[]{:S(2)}, u32[]{:S(2)}) collective-permute-start(bf16[32,2048]{1,0:T(8,128)(2,1)S(1)} %get-tuple-element.64), channel_id=1, source_target_pairs={{0,4},{4,0},{8,12},{12,8},{1,5},{5,1},{9,13},{13,9},{2,6},{6,2},{1... | collective-permute-start | bytes 393224 | tf_op jit(solution)/shard_map/ppermute | solution.py:182
  48.6 2.0 collective-permute-start.10
  48.6 14.3 %collective-permute-start.13 = (bf16[4,32,2048]{2,1,0:T(8,128)(2,1)S(1)}, bf16[4,32,2048]{2,1,0:T(8,128)(2,1)S(1)}, u32[]{:S(2)}, u32[]{:S(2)}) collective-permute-start(bf16[4,32,2048]{2,1,0:T(8,128)(2,1)S(1)} %pad_maximum_fusion.11), channel_id=1, source_target_pairs={{0,2},{1,3},{2,0},{3,1},{4,6},{5,7},{6,4},{7,5},{8,10},{9,11},{10,... | collective-permute-start | bytes 1572872 | tf_op jit(solution)/shard_map/ppermute | solution.py:182
  55.0 12.6 %collective-permute-start.11 = (bf16[2,64,1792]{2,1,0:T(8,128)(2,1)S(1)}, bf16[2,64,1792]{2,1,0:T(8,128)(2,1)S(1)}, u32[]{:S(2)}, u32[]{:S(2)}) collective-permute-start(bf16[2,64,1792]{2,1,0:T(8,128)(2,1)S(1)} %slice_bitcast_fusion.5), channel_id=1, source_target_pairs={{0,4},{4,0},{8,12},{12,8},{1,5},{5,1},{9,13},{13,9},{2,6},{6,2},{1... | collective-permute-start | bytes 1376264 | tf_op jit(solution)/shard_map/ppermute | solution.py:182
  63.0 6.3 %collective-permute-start.14 = (bf16[4,32,2048]{2,1,0:T(8,128)(2,1)S(1)}, bf16[4,32,2048]{2,1,0:T(8,128)(2,1)S(1)}, u32[]{:S(2)}, u32[]{:S(2)}) collective-permute-start(bf16[4,32,2048]{2,1,0:T(8,128)(2,1)S(1)} %collective-permute-done.13), channel_id=1, source_target_pairs={{0,1},{1,0},{2,3},{3,2},{4,5},{5,4},{6,7},{7,6},{8,9},{9,8},{10,11... | collective-permute-start | bytes 1572872 | tf_op jit(solution)/shard_map/ppermute | solution.py:182
  67.7 12.8 %collective-permute-start.12 = (bf16[64,1792]{1,0:T(8,128)(2,1)S(1)}, bf16[64,1792]{1,0:T(8,128)(2,1)S(1)}, u32[]{:S(2)}, u32[]{:S(2)}) collective-permute-start(bf16[64,1792]{1,0:T(8,128)(2,1)S(1)} %fusion.19), channel_id=1, source_target_pairs={{0,8},{4,12},{8,0},{12,4},{1,9},{5,13},{9,1},{13,5},{2,10},{6,14},... | collective-permute-start | bytes 688136 | tf_op jit(solution)/shard_map/ppermute | solution.py:182
  69.4 11.1 %copy-start.3 = (bf16[128,1792]{1,0:T(8,128)(2,1)S(1)}, bf16[128,1792]{1,0:T(8,128)(2,1)}, u32[]{:S(2)}) copy-start(bf16[128,1792]{1,0:T(8,128)(2,1)} %param.10) | copy-start | bytes 1376260
  73.6 21.4 %collective-permute-start.15 = (bf16[2,64,1792]{2,1,0:T(8,128)(2,1)S(1)}, bf16[2,64,1792]{2,1,0:T(8,128)(2,1)S(1)}, u32[]{:S(2)}, u32[]{:S(2)}) collective-permute-start(bf16[2,64,1792]{2,1,0:T(8,128)(2,1)S(1)} %slice_bitcast_fusion.4), channel_id=1, source_target_pairs={{0,4},{4,0},{8,12},{12,8},{1,5},{5,1},{9,13},{13,9},{2,6},{6,2},{1... | collective-permute-start | bytes 1376264 | tf_op jit(solution)/shard_map/ppermute | solution.py:182
  80.6 13.3 %collective-permute-start.16 = (bf16[64,1792]{1,0:T(8,128)(2,1)S(1)}, bf16[64,1792]{1,0:T(8,128)(2,1)S(1)}, u32[]{:S(2)}, u32[]{:S(2)}) collective-permute-start(bf16[64,1792]{1,0:T(8,128)(2,1)S(1)} %fusion.22), channel_id=1, source_target_pairs={{0,8},{4,12},{8,0},{12,4},{1,9},{5,13},{9,1},{13,5},{2,10},{6,14},... | collective-permute-start | bytes 688136 | tf_op jit(solution)/shard_map/ppermute | solution.py:182
  94.0 16.8 %collective-permute-start.17 = (bf16[128,1792]{1,0:T(8,128)(2,1)S(1)}, bf16[128,1792]{1,0:T(8,128)(2,1)S(1)}, u32[]{:S(2)}, u32[]{:S(2)}) collective-permute-start(bf16[128,1792]{1,0:T(8,128)(2,1)S(1)} %pad_maximum_fusion.12), channel_id=1, source_target_pairs={{0,4},{4,0},{8,12},{12,8},{1,5},{5,1},{9,13},{13,9},{2,6},{6,2},{1... | collective-permute-start | bytes 1376264 | tf_op jit(solution)/shard_map/ppermute | solution.py:182
  95.8 15.0 %copy-start.2 = (f32[1792]{0:T(1024)S(1)}, f32[1792]{0:T(1024)}, u32[]{:S(2)}) copy-start(f32[1792]{0:T(1024)} %param.16) | copy-start | bytes 21508
  97.6 11.1 %collective-permute-start.18 = (bf16[64,1792]{1,0:T(8,128)(2,1)}, bf16[64,1792]{1,0:T(8,128)(2,1)S(1)}, u32[]{:S(2)}, u32[]{:S(2)}) collective-permute-start(bf16[64,1792]{1,0:T(8,128)(2,1)} %shard_map.116), channel_id=1, source_target_pairs={{0,8},{4,12},{8,0},{12,4},{1,9},{5,13},{9,1},{13,5},{2,10},{6,14},... | collective-permute-start | bytes 688136 | tf_op jit(solution)/shard_map/ppermute | solution.py:182
  110.8 9.1 %slice-start = ((s8[9175040]{0:T(1024)(128)(4,1)}), s8[4194304]{0:T(1024)(128)(4,1)S(1)}, s32[]{:S(2)}) async-start(s8[9175040]{0:T(1024)(128)(4,1)} %bitcast.172), calls=%async_computation | async-start | bytes 8388608
  111.1 8.8 %slice-start.1 = ((s8[9175040]{0:T(1024)(128)(4,1)}), s8[4194304]{0:T(1024)(128)(4,1)S(1)}, s32[]{:S(2)}) async-start(s8[9175040]{0:T(1024)(128)(4,1)} %bitcast.172), calls=%async_computation.1 | async-start | bytes 8388608
  111.1 8.8 %slice-start.2 = ((s8[9175040]{0:T(1024)(128)(4,1)}), s8[786432]{0:T(1024)(128)(4,1)S(1)}, s32[]{:S(2)}) async-start(s8[9175040]{0:T(1024)(128)(4,1)} %bitcast.172), calls=%async_computation.2 | async-start | bytes 1572864
  117.5 1.0 copy-start.4
  117.6 5.0 %collective-permute-start.20 = (bf16[128,2560]{1,0:T(8,128)(2,1)S(1)}, bf16[128,2560]{1,0:T(8,128)(2,1)S(1)}, u32[]{:S(2)}, u32[]{:S(2)}) collective-permute-start(bf16[128,2560]{1,0:T(8,128)(2,1)S(1)} %bitcast.180), channel_id=1, source_target_pairs={{0,1},{1,0},{2,3},{3,2},{4,5},{5,4},{6,7},{7,6},{8,9},{9,8},{10,11... | collective-permute-start | bytes 1966088 | tf_op jit(solution)/shard_map/ppermute | solution.py:182
  118.7 13.1 %collective-permute-start.19 = (bf16[64,1792]{1,0:T(8,128)(2,1)S(1)}, bf16[64,1792]{1,0:T(8,128)(2,1)S(1)}, u32[]{:S(2)}, u32[]{:S(2)}) collective-permute-start(bf16[64,1792]{1,0:T(8,128)(2,1)S(1)} %get-tuple-element.36), channel_id=1, source_target_pairs={{0,8},{4,12},{8,0},{12,4},{1,9},{5,13},{9,1},{13,5},{2,10},{6,14},... | collective-permute-start | bytes 688136 | tf_op jit(solution)/shard_map/ppermute | solution.py:182
  122.6 2.6 %collective-permute-start.22 = (bf16[128,2560]{1,0:T(8,128)(2,1)S(1)}, bf16[128,2560]{1,0:T(8,128)(2,1)S(1)}, u32[]{:S(2)}, u32[]{:S(2)}) collective-permute-start(bf16[128,2560]{1,0:T(8,128)(2,1)S(1)} %bitcast.181), channel_id=1, source_target_pairs={{0,1},{1,0},{2,3},{3,2},{4,5},{5,4},{6,7},{7,6},{8,9},{9,8},{10,11... | collective-permute-start | bytes 1966088 | tf_op jit(solution)/shard_map/ppermute | solution.py:182
  123.7 17.7 %collective-permute-start.21 = (bf16[128,2560]{1,0:T(8,128)(2,1)}, bf16[128,2560]{1,0:T(8,128)(2,1)S(1)}, u32[]{:S(2)}, u32[]{:S(2)}) collective-permute-start(bf16[128,2560]{1,0:T(8,128)(2,1)} %fusion.3), channel_id=1, source_target_pairs={{0,2},{1,3},{2,0},{3,1},{4,6},{5,7},{6,4},{7,5},{8,10},{9,11},{10,... | collective-permute-start | bytes 1966088 | tf_op jit(solution)/shard_map/ppermute | solution.py:182
  125.4 1.2 collective-permute-start.25
  125.7 29.5 %collective-permute-start.28 = (bf16[128,2560]{1,0:T(8,128)(2,1)S(1)}, bf16[128,2560]{1,0:T(8,128)(2,1)S(1)}, u32[]{:S(2)}, u32[]{:S(2)}) collective-permute-start(bf16[128,2560]{1,0:T(8,128)(2,1)S(1)} %fusion.2), channel_id=1, source_target_pairs={{0,2},{1,3},{2,0},{3,1},{4,6},{5,7},{6,4},{7,5},{8,10},{9,11},{10,... | collective-permute-start | bytes 1966088 | tf_op jit(solution)/shard_map/ppermute | solution.py:182
  126.6 33.9 %collective-permute-start.26 = (f32[256]{0:T(256)S(1)}, f32[256]{0:T(256)S(1)}, u32[]{:S(2)}, u32[]{:S(2)}) collective-permute-start(f32[256]{0:T(256)S(1)} %add.257), channel_id=1, source_target_pairs={{0,2},{1,3},{2,0},{3,1},{4,6},{5,7},{6,4},{7,5},{8,10},{9,11},{10,... | collective-permute-start | bytes 3080 | tf_op jit(solution)/shard_map/ppermute | solution.py:182
  141.5 13.7 %collective-permute-start.27 = (bf16[128,1792]{1,0:T(8,128)(2,1)S(1)}, bf16[128,1792]{1,0:T(8,128)(2,1)S(1)}, u32[]{:S(2)}, u32[]{:S(2)}) collective-permute-start(bf16[128,1792]{1,0:T(8,128)(2,1)S(1)} %pad_maximum_fusion.14), channel_id=1, source_target_pairs={{0,4},{4,0},{8,12},{12,8},{1,5},{5,1},{9,13},{13,9},{2,6},{6,2},{1... | collective-permute-start | bytes 1376264 | tf_op jit(solution)/shard_map/ppermute | solution.py:182
  143.9 11.5 %slice-start.3 = ((s8[9175040]{0:T(1024)(128)(4,1)}), s8[4194304]{0:T(1024)(128)(4,1)S(1)}, s32[]{:S(2)}) async-start(s8[9175040]{0:T(1024)(128)(4,1)} %bitcast.174), calls=%async_computation.3 | async-start | bytes 8388608
  143.9 11.5 %slice-start.4 = ((s8[9175040]{0:T(1024)(128)(4,1)}), s8[4194304]{0:T(1024)(128)(4,1)S(1)}, s32[]{:S(2)}) async-start(s8[9175040]{0:T(1024)(128)(4,1)} %bitcast.174), calls=%async_computation.4 | async-start | bytes 8388608
  149.3 6.1 %slice-start.5 = ((s8[9175040]{0:T(1024)(128)(4,1)}), s8[786432]{0:T(1024)(128)(4,1)S(1)}, s32[]{:S(2)}) async-start(s8[9175040]{0:T(1024)(128)(4,1)} %bitcast.174), calls=%async_computation.5 | async-start | bytes 1572864
  154.4 6.1 %collective-permute-start.24 = (f32[128]{0:T(128)S(1)}, f32[128]{0:T(128)S(1)}, u32[]{:S(2)}, u32[]{:S(2)}) collective-permute-start(f32[128]{0:T(128)S(1)} %fusion.5), channel_id=1, source_target_pairs={{0,1},{1,0},{2,3},{3,2},{4,5},{5,4},{6,7},{7,6},{8,9},{9,8},{10,11... | collective-permute-start | bytes 1544 | tf_op jit(solution)/shard_map/ppermute | solution.py:182
  154.5 2.3 %slice-start.6 = ((s8[9175040]{0:T(1024)(128)(4,1)}), s8[4194304]{0:T(1024)(128)(4,1)S(1)}, s32[]{:S(2)}) async-start(s8[9175040]{0:T(1024)(128)(4,1)} %bitcast.176), calls=%async_computation.6 | async-start | bytes 8388608
  154.6 6.5 %collective-permute-start.23 = (bf16[128,2560]{1,0:T(8,128)(2,1)S(1)}, bf16[128,2560]{1,0:T(8,128)(2,1)S(1)}, u32[]{:S(2)}, u32[]{:S(2)}) collective-permute-start(bf16[128,2560]{1,0:T(8,128)(2,1)S(1)} %pad_maximum_fusion.5), channel_id=1, source_target_pairs={{0,1},{1,0},{2,3},{3,2},{4,5},{5,4},{6,7},{7,6},{8,9},{9,8},{10,11... | collective-permute-start | bytes 1966088 | tf_op jit(solution)/shard_map/ppermute | solution.py:182
  155.4 2.8 %slice-start.7 = ((s8[9175040]{0:T(1024)(128)(4,1)}), s8[4194304]{0:T(1024)(128)(4,1)S(1)}, s32[]{:S(2)}) async-start(s8[9175040]{0:T(1024)(128)(4,1)} %bitcast.176), calls=%async_computation.7 | async-start | bytes 8388608
  155.4 2.9 %slice-start.8 = ((s8[9175040]{0:T(1024)(128)(4,1)}), s8[786432]{0:T(1024)(128)(4,1)S(1)}, s32[]{:S(2)}) async-start(s8[9175040]{0:T(1024)(128)(4,1)} %bitcast.176), calls=%async_computation.8 | async-start | bytes 1572864
  159.7 1.3 collective-permute-start.30
  160.3 2.2 collective-permute-start.29
  163.3 2.2 collective-permute-start.32
  163.5 17.0 %collective-permute-start.31 = (bf16[128,2560]{1,0:T(8,128)(2,1)S(1)}, bf16[128,2560]{1,0:T(8,128)(2,1)S(1)}, u32[]{:S(2)}, u32[]{:S(2)}) collective-permute-start(bf16[128,2560]{1,0:T(8,128)(2,1)S(1)} %pad_maximum_fusion.7), channel_id=1, source_target_pairs={{0,2},{1,3},{2,0},{3,1},{4,6},{5,7},{6,4},{7,5},{8,10},{9,11},{10,... | collective-permute-start | bytes 1966088 | tf_op jit(solution)/shard_map/ppermute | solution.py:182
  170.4 12.6 %collective-permute-start.34 = (bf16[2,64,1792]{2,1,0:T(8,128)(2,1)S(1)}, bf16[2,64,1792]{2,1,0:T(8,128)(2,1)S(1)}, u32[]{:S(2)}, u32[]{:S(2)}) collective-permute-start(bf16[2,64,1792]{2,1,0:T(8,128)(2,1)S(1)} %slice_bitcast_fusion.2), channel_id=1, source_target_pairs={{0,4},{4,0},{8,12},{12,8},{1,5},{5,1},{9,13},{13,9},{2,6},{6,2},{1... | collective-permute-start | bytes 1376264 | tf_op jit(solution)/shard_map/ppermute | solution.py:182
  180.5 2.6 %collective-permute-start.33 = (bf16[128,2560]{1,0:T(8,128)(2,1)S(1)}, bf16[128,2560]{1,0:T(8,128)(2,1)S(1)}, u32[]{:S(2)}, u32[]{:S(2)}) collective-permute-start(bf16[128,2560]{1,0:T(8,128)(2,1)S(1)} %collective-permute-done.31), channel_id=1, source_target_pairs={{0,1},{1,0},{2,3},{3,2},{4,5},{5,4},{6,7},{7,6},{8,9},{9,8},{10,11... | collective-permute-start | bytes 1966088 | tf_op jit(solution)/shard_map/ppermute | solution.py:182
  188.1 17.0 %collective-permute-start.35 = (bf16[2,64,1792]{2,1,0:T(8,128)(2,1)S(1)}, bf16[2,64,1792]{2,1,0:T(8,128)(2,1)S(1)}, u32[]{:S(2)}, u32[]{:S(2)}) collective-permute-start(bf16[2,64,1792]{2,1,0:T(8,128)(2,1)S(1)} %slice_bitcast_fusion), channel_id=1, source_target_pairs={{0,4},{4,0},{8,12},{12,8},{1,5},{5,1},{9,13},{13,9},{2,6},{6,2},{1... | collective-permute-start | bytes 1376264 | tf_op jit(solution)/shard_map/ppermute | solution.py:182
  189.7 15.8 %collective-permute-start.37 = (bf16[64,1792]{1,0:T(8,128)(2,1)S(1)}, bf16[64,1792]{1,0:T(8,128)(2,1)S(1)}, u32[]{:S(2)}, u32[]{:S(2)}) collective-permute-start(bf16[64,1792]{1,0:T(8,128)(2,1)S(1)} %fusion.31), channel_id=1, source_target_pairs={{0,8},{4,12},{8,0},{12,4},{1,9},{5,13},{9,1},{13,5},{2,10},{6,14},... | collective-permute-start | bytes 688136 | tf_op jit(solution)/shard_map/ppermute | solution.py:182
  205.2 11.7 %collective-permute-start.36 = (bf16[64,1792]{1,0:T(8,128)(2,1)S(1)}, bf16[64,1792]{1,0:T(8,128)(2,1)S(1)}, u32[]{:S(2)}, u32[]{:S(2)}) collective-permute-start(bf16[64,1792]{1,0:T(8,128)(2,1)S(1)} %fusion.32), channel_id=1, source_target_pairs={{0,8},{4,12},{8,0},{12,4},{1,9},{5,13},{9,1},{13,5},{2,10},{6,14},... | collective-permute-start | bytes 688136 | tf_op jit(solution)/shard_map/ppermute | solution.py:182

commit v16 on v15

--- a/solution.py
+++ b/solution.py
@@ -256,6 +256,7 @@
         in_specs=[whole, whole],
         out_specs=whole,
         out_shape=jax.ShapeDtypeStruct(mine.shape, jnp.bfloat16),
+        compiler_params=pltpu.CompilerParams(vmem_limit_bytes=4 * 1024 * 1024),
         cost_estimate=pl.CostEstimate(
             flops=8 * 10**9, bytes_accessed=6 * mine.size, transcendentals=0
         ),

time: 218 us -> 218 us (level)
  waiting for transfers between devices: 111 us -> 114 us
    ppermute x35, waiting for transfers between devices: 111 us -> 114 us  [swap(): return lax.ppermute(value, axis_name, [(i, i ^ bit) for i in range(width)])]
  transfers between devices with their start and end apart: 38 -> 38, of which waited for: 22 -> 22; matrix products, arithmetic and copies ran while one was open for 11% -> 10% of each run, Pallas kernels for 7% -> 6%
where the time goes in v16:
time: 218 us
  waiting for transfers between devices  114 us (52%)
  starting transfers between devices  40.4 us (19%)
  Pallas kernels  24.7 us (11%)
  matrix products  22.1 us (10%)
  other arithmetic  9.22 us (4%)
  local copies, waits for them, and re-layouts  6.04 us (3%)
    ppermute x35, waiting for transfers between devices, swap(): return lax.ppermute(value, axis_name, [(i, i ^ bit) for i in range(width)])  114 us
    ppermute x35, starting transfers between devices, swap(): return lax.ppermute(value, axis_name, [(i, i ^ bit) for i in range(width)])  29.7 us
    dot_general x6, matrix products, matmul(): jnp.dot(a, b, preferred_element_type=jnp.float32).astype(jnp.bfloat16)  22.1 us
    pallas_call x4, Pallas kernels, streamed_matmul(): pl.pallas_call(functools.partial(streamed_kernel, 512), in_specs=[pl.Bloc...  17.9 us
    ppermute x3, starting transfers between devices, gather_keys(): lax.ppermute(half, 'ctx', [(c, c + d) for c in range(n_ctx - d)])  10.7 us
    pallas_call x1, Pallas kernels, attention(): pl.pallas_call(functools.partial(attention_kernel, group), grid=(local_he...  6.79 us
  transfers between devices with their start and end apart: 38, of which 22 were waited for; matrix products, arithmetic and copies ran while one was open for 10% of the time, Pallas kernels for 6%

profile of v16, /device:TPU:0, one launch (start us, length us, event | category | flops | bytes accessed | tf_op | source)
XLA Modules:
  0.0 218.1 jit_solution(108546361642533919)
XLA Ops:
  0.6 0.9 constant_dynamic-slice_fusion.14
  1.5 4.9 %collective-permute-start.2 = (bf16[288,128]{1,0:T(8,128)(2,1)S(1)}, bf16[288,128]{1,0:T(8,128)(2,1)S(1)}, u32[]{:S(2)}, u32[]{:S(2)}) collective-permute-start(bf16[288,128]{1,0:T(8,128)(2,1)S(1)} %constant_dynamic-slice_fusion.14), channel_id=1, source_target_pairs={{0,4},{4,8},{8,12},{1,5},{5,9},{9,13},{2,6},{6,10},{10,14},{3,7},{... | collective-permute-start | bytes 221192 | tf_op jit(solution)/shard_map/ppermute | solution.py:275
  6.5 4.5 %collective-permute-start.1 = (bf16[288,128]{1,0:T(8,128)(2,1)S(1)}, bf16[288,128]{1,0:T(8,128)(2,1)S(1)}, u32[]{:S(2)}, u32[]{:S(2)}) collective-permute-start(bf16[288,128]{1,0:T(8,128)(2,1)S(1)} %constant_dynamic-slice_fusion.14), channel_id=1, source_target_pairs={{0,8},{4,12},{1,9},{5,13},{2,10},{6,14},{3,11},{7,15},{16,24},{20,... | collective-permute-start | bytes 221192 | tf_op jit(solution)/shard_map/ppermute | solution.py:275
  11.0 1.3 collective-permute-start
  12.3 0.8 reduce-window.8
  13.2 0.7 subtract_subtract_fusion
  15.1 1.5 collective-permute-done.3
  17.2 1.0 copy-done.1
  18.2 0.7 copy-done
  19.0 6.8 %shard_map.113 = bf16[128,2048]{1,0:T(8,128)(2,1)S(1)} custom-call(f32[4,128,128]{2,1,0:T(8,128)S(1)} %pad_maximum_fusion.16.tables, s32[128,1]{1,0:T(8,128)S(1)} %copy.23.starts, s32[128,1]{1,0:T(8,128)S(1)} %iota_add_fusion.own_index, s32[1,512]{1,0:T(1,128)S(1)} %iota_add_fusion.2.key_index, bf16[576,512]{1,0:T(8,128)(2,1)S(1)} %pad_maximum_fusion.9.keys, ...), custom_call_target="tpu_custom_call" | custom-call | flops 2684354560 | bytes 5046272 | tf_op jit(solution)/shard_map/pallas_call | solution.py:143
  25.8 1.3 collective-permute-start.6
  27.1 0.5 collective-permute-start.5
  27.7 3.6 %collective-permute-done.6 = bf16[32,2048]{1,0:T(8,128)(2,1)S(1)} collective-permute-done((bf16[32,2048]{1,0:T(8,128)(2,1)S(1)}, bf16[32,2048]{1,0:T(8,128)(2,1)S(1)}, u32[]{:S(2)}, u32[]{:S(2)}) %collective-permute-start.6) | collective-permute-done | bytes 131104 | tf_op jit(solution)/shard_map/ppermute | solution.py:182
  31.4 3.1 %collective-permute-done.5 = bf16[32,2048]{1,0:T(8,128)(2,1)S(1)} collective-permute-done((bf16[32,2048]{1,0:T(8,128)(2,1)S(1)}, bf16[32,2048]{1,0:T(8,128)(2,1)S(1)}, u32[]{:S(2)}, u32[]{:S(2)}) %collective-permute-start.5) | collective-permute-done | bytes 131104 | tf_op jit(solution)/shard_map/ppermute | solution.py:182
  34.6 3.7 %collective-permute-start.9 = (bf16[32,2048]{1,0:T(8,128)(2,1)S(1)}, bf16[32,2048]{1,0:T(8,128)(2,1)S(1)}, u32[]{:S(2)}, u32[]{:S(2)}) collective-permute-start(bf16[32,2048]{1,0:T(8,128)(2,1)S(1)} %get-tuple-element.62), channel_id=1, source_target_pairs={{0,12},{4,8},{8,4},{12,0},{1,13},{5,9},{9,5},{13,1},{2,14},{6,10},... | collective-permute-start | bytes 393224 | tf_op jit(solution)/shard_map/ppermute | solution.py:182
  38.3 0.8 collective-permute-start.7
  39.1 3.8 %collective-permute-done.9 = bf16[32,2048]{1,0:T(8,128)(2,1)S(1)} collective-permute-done((bf16[32,2048]{1,0:T(8,128)(2,1)S(1)}, bf16[32,2048]{1,0:T(8,128)(2,1)S(1)}, u32[]{:S(2)}, u32[]{:S(2)}) %collective-permute-start.9) | collective-permute-done | bytes 131104 | tf_op jit(solution)/shard_map/ppermute | solution.py:182
  42.9 5.6 %collective-permute-done.8 = bf16[32,2048]{1,0:T(8,128)(2,1)S(1)} collective-permute-done((bf16[32,2048]{1,0:T(8,128)(2,1)S(1)}, bf16[32,2048]{1,0:T(8,128)(2,1)S(1)}, u32[]{:S(2)}, u32[]{:S(2)}) %collective-permute-start.8) | collective-permute-done | bytes 131104 | tf_op jit(solution)/shard_map/ppermute | solution.py:182
  48.6 1.6 collective-permute-start.13
  50.8 4.1 %shard_map.114 = bf16[256,1792]{1,0:T(8,128)(2,1)S(1)} custom-call(bf16[256,2048]{1,0:T(8,128)(2,1)S(1)} %bitcast.160, bf16[2048,1792]{1,0:T(8,128)(2,1)} %weight.5), custom_call_target="tpu_custom_call" | custom-call | flops 1024 | bytes 1024 | tf_op jit(solution)/shard_map/pallas_call | solution.py:230
  55.0 0.8 collective-permute-start.11
  55.7 7.2 %collective-permute-done.13 = bf16[4,32,2048]{2,1,0:T(8,128)(2,1)S(1)} collective-permute-done((bf16[4,32,2048]{2,1,0:T(8,128)(2,1)S(1)}, bf16[4,32,2048]{2,1,0:T(8,128)(2,1)S(1)}, u32[]{:S(2)}, u32[]{:S(2)}) %collective-permute-start.13) | collective-permute-done | bytes 524320 | tf_op jit(solution)/shard_map/ppermute | solution.py:182
  63.0 4.6 %collective-permute-done.11 = bf16[2,64,1792]{2,1,0:T(8,128)(2,1)S(1)} collective-permute-done((bf16[2,64,1792]{2,1,0:T(8,128)(2,1)S(1)}, bf16[2,64,1792]{2,1,0:T(8,128)(2,1)S(1)}, u32[]{:S(2)}, u32[]{:S(2)}) %collective-permute-start.11) | collective-permute-done | bytes 458784 | tf_op jit(solution)/shard_map/ppermute | solution.py:182
  67.7 1.5 collective-permute-start.12
  69.4 4.2 %shard_map.115 = bf16[256,1792]{1,0:T(8,128)(2,1)S(1)} custom-call(bf16[256,2048]{1,0:T(8,128)(2,1)S(1)} %bitcast.159, bf16[2048,1792]{1,0:T(8,128)(2,1)} %weight.5), custom_call_target="tpu_custom_call" | custom-call | flops 1024 | bytes 1024 | tf_op jit(solution)/shard_map/pallas_call | solution.py:230
  73.6 1.8 collective-permute-start.15
  75.4 5.1 %collective-permute-done.12 = bf16[64,1792]{1,0:T(8,128)(2,1)S(1)} collective-permute-done((bf16[64,1792]{1,0:T(8,128)(2,1)S(1)}, bf16[64,1792]{1,0:T(8,128)(2,1)S(1)}, u32[]{:S(2)}, u32[]{:S(2)}) %collective-permute-start.12) | collective-permute-done | bytes 229408 | tf_op jit(solution)/shard_map/ppermute | solution.py:182
  80.7 13.2 %collective-permute-done.16 = bf16[64,1792]{1,0:T(8,128)(2,1)S(1)} collective-permute-done((bf16[64,1792]{1,0:T(8,128)(2,1)S(1)}, bf16[64,1792]{1,0:T(8,128)(2,1)S(1)}, u32[]{:S(2)}, u32[]{:S(2)}) %collective-permute-start.16) | collective-permute-done | bytes 229408 | tf_op jit(solution)/shard_map/ppermute | solution.py:182
  94.0 1.0 collective-permute-done.15
  95.2 2.2 %collective-permute-start.18 = (bf16[64,1792]{1,0:T(8,128)(2,1)S(1)}, bf16[64,1792]{1,0:T(8,128)(2,1)S(1)}, u32[]{:S(2)}, u32[]{:S(2)}) collective-permute-start(bf16[64,1792]{1,0:T(8,128)(2,1)S(1)} %shard_map.116), channel_id=1, source_target_pairs={{0,8},{4,12},{8,0},{12,4},{1,9},{5,13},{9,1},{13,5},{2,10},{6,14},... | collective-permute-start | bytes 688136 | tf_op jit(solution)/shard_map/ppermute | solution.py:182
  97.3 11.2 %collective-permute-done.18 = bf16[64,1792]{1,0:T(8,128)(2,1)S(1)} collective-permute-done((bf16[64,1792]{1,0:T(8,128)(2,1)S(1)}, bf16[64,1792]{1,0:T(8,128)(2,1)S(1)}, u32[]{:S(2)}, u32[]{:S(2)}) %collective-permute-start.18) | collective-permute-done | bytes 229408 | tf_op jit(solution)/shard_map/ppermute | solution.py:182
  108.5 2.2 %collective-permute-done.17 = bf16[128,1792]{1,0:T(8,128)(2,1)S(1)} collective-permute-done((bf16[128,1792]{1,0:T(8,128)(2,1)S(1)}, bf16[128,1792]{1,0:T(8,128)(2,1)S(1)}, u32[]{:S(2)}, u32[]{:S(2)}) %collective-permute-start.17) | collective-permute-done | bytes 458784 | tf_op jit(solution)/shard_map/ppermute | solution.py:182
  111.1 6.3 %convolution_convert_fusion.1 = bf16[256,2560]{1,0:T(8,128)(2,1)S(1)} fusion(bf16[256,1792]{1,0:T(8,128)(2,1)S(1)} %get-tuple-element.24, bf16[1792,2560]{1,0:T(8,128)(2,1)} %param.17), kind=kOutput, calls=%fused_computation.1 | convolution fusion | flops 2349465600 | bytes 11403264 | tf_op jit(solution)/shard_map/dot_general | solution.py:194
  117.7 0.8 copy-done.4
  118.7 1.4 collective-permute-start.19
  120.1 2.5 %convolution_convert_fusion = bf16[256,2560]{1,0:T(8,128)(2,1)S(1)} fusion(bf16[256,1792]{1,0:T(8,128)(2,1)S(1)} %get-tuple-element.24, bf16[1792,2560]{1,0:T(8,128)(2,1)S(1)} %bitcast.173), kind=kOutput, calls=%fused_computation | convolution fusion | flops 2349465600 | bytes 11403264 | tf_op jit(solution)/shard_map/dot_general | solution.py:194
  122.8 1.0 fusion.3
  123.8 1.5 collective-permute-start.21
  125.8 1.0 collective-permute-start.28
  126.8 1.1 collective-permute-start.26
  127.8 3.9 %collective-permute-done.19 = bf16[64,1792]{1,0:T(8,128)(2,1)S(1)} collective-permute-done((bf16[64,1792]{1,0:T(8,128)(2,1)S(1)}, bf16[64,1792]{1,0:T(8,128)(2,1)S(1)}, u32[]{:S(2)}, u32[]{:S(2)}) %collective-permute-start.19) | collective-permute-done | bytes 229408 | tf_op jit(solution)/shard_map/ppermute | solution.py:182
  131.7 9.8 %collective-permute-done.21 = bf16[128,2560]{1,0:T(8,128)(2,1)S(1)} collective-permute-done((bf16[128,2560]{1,0:T(8,128)(2,1)}, bf16[128,2560]{1,0:T(8,128)(2,1)S(1)}, u32[]{:S(2)}, u32[]{:S(2)}) %collective-permute-start.21) | collective-permute-done | bytes 655392 | tf_op jit(solution)/shard_map/ppermute | solution.py:182
  141.6 2.1 collective-permute-start.27
  143.9 5.4 %convolution_convert_fusion.4 = bf16[128,2560]{1,0:T(8,128)(2,1)S(1)} fusion(bf16[1792,2560]{1,0:T(8,128)(2,1)} %param.18, bf16[128,1792]{1,0:T(8,128)(2,1)S(1)} %pad_maximum_fusion.14, f32[1792]{0:T(1024)S(1)} %copy-done.2), kind=kOutput, calls=%fused_computation.4 | convolution fusion | flops 1175420928 | bytes 10296320 | tf_op jit(solution)/shard_map/dot_general | solution.py:194
  149.3 5.1 %convolution_convert_fusion.5 = bf16[128,2560]{1,0:T(8,128)(2,1)S(1)} fusion(bf16[1792,2560]{1,0:T(8,128)(2,1)} %param.17, bf16[128,1792]{1,0:T(8,128)(2,1)S(1)} %pad_maximum_fusion.14, f32[1792]{0:T(1024)S(1)} %copy-done.2), kind=kOutput, calls=%fused_computation.5 | convolution fusion | flops 1175420928 | bytes 10296320 | tf_op jit(solution)/shard_map/dot_general | solution.py:194
  154.6 0.5 collective-permute-start.23
  155.5 1.4 convolution_convert_fusion.2
  156.9 1.3 slice-done.7
  158.3 1.4 convolution_convert_fusion.3
  161.3 1.2 collective-permute-done.29
  162.7 0.6 fusion.14
  163.6 1.5 collective-permute-start.31
  165.1 0.4 collective-permute-done.32
  165.6 4.8 %shard_map.117 = bf16[256,1792]{1,0:T(8,128)(2,1)S(1)} custom-call(bf16[256,2560]{1,0:T(8,128)(2,1)S(1)} %pad_maximum_fusion.rows, bf16[2560,1792]{1,0:T(8,128)(2,1)} %weight.7), custom_call_target="tpu_custom_call" | custom-call | flops 1024 | bytes 1024 | tf_op jit(solution)/shard_map/pallas_call | solution.py:230
  170.4 1.4 collective-permute-start.34
  171.9 0.8 pad_maximum_fusion.13
  172.7 7.9 %collective-permute-done.31 = bf16[128,2560]{1,0:T(8,128)(2,1)S(1)} collective-permute-done((bf16[128,2560]{1,0:T(8,128)(2,1)S(1)}, bf16[128,2560]{1,0:T(8,128)(2,1)S(1)}, u32[]{:S(2)}, u32[]{:S(2)}) %collective-permute-start.31) | collective-permute-done | bytes 655392 | tf_op jit(solution)/shard_map/ppermute | solution.py:182
  180.6 2.5 %collective-permute-done.34 = bf16[2,64,1792]{2,1,0:T(8,128)(2,1)S(1)} collective-permute-done((bf16[2,64,1792]{2,1,0:T(8,128)(2,1)S(1)}, bf16[2,64,1792]{2,1,0:T(8,128)(2,1)S(1)}, u32[]{:S(2)}, u32[]{:S(2)}) %collective-permute-start.34) | collective-permute-done | bytes 458784 | tf_op jit(solution)/shard_map/ppermute | solution.py:182
  183.3 4.8 %shard_map.118 = bf16[256,1792]{1,0:T(8,128)(2,1)S(1)} custom-call(bf16[256,2560]{1,0:T(8,128)(2,1)S(1)} %pad_maximum_fusion.1.rows, bf16[2560,1792]{1,0:T(8,128)(2,1)} %weight.7), custom_call_target="tpu_custom_call" | custom-call | flops 1024 | bytes 1024 | tf_op jit(solution)/shard_map/pallas_call | solution.py:230
  188.1 1.6 collective-permute-start.35
  189.8 1.3 collective-permute-start.37
  191.1 14.1 %collective-permute-done.35 = bf16[2,64,1792]{2,1,0:T(8,128)(2,1)S(1)} collective-permute-done((bf16[2,64,1792]{2,1,0:T(8,128)(2,1)S(1)}, bf16[2,64,1792]{2,1,0:T(8,128)(2,1)S(1)}, u32[]{:S(2)}, u32[]{:S(2)}) %collective-permute-start.35) | collective-permute-done | bytes 458784 | tf_op jit(solution)/shard_map/ppermute | solution.py:182
  205.7 11.4 %collective-permute-done.36 = bf16[64,1792]{1,0:T(8,128)(2,1)S(1)} collective-permute-done((bf16[64,1792]{1,0:T(8,128)(2,1)S(1)}, bf16[64,1792]{1,0:T(8,128)(2,1)S(1)}, u32[]{:S(2)}, u32[]{:S(2)}) %collective-permute-start.36) | collective-permute-done | bytes 229408 | tf_op jit(solution)/shard_map/ppermute | solution.py:182
  217.3 0.8 pad_maximum_fusion.15
  (141 shorter events, 8.8 us)
Async XLA Ops:
  1.5 13.5 %collective-permute-start.2 = (bf16[288,128]{1,0:T(8,128)(2,1)S(1)}, bf16[288,128]{1,0:T(8,128)(2,1)S(1)}, u32[]{:S(2)}, u32[]{:S(2)}) collective-permute-start(bf16[288,128]{1,0:T(8,128)(2,1)S(1)} %constant_dynamic-slice_fusion.14), channel_id=1, source_target_pairs={{0,4},{4,8},{8,12},{1,5},{5,9},{9,13},{2,6},{6,10},{10,14},{3,7},{... | collective-permute-start | bytes 221192 | tf_op jit(solution)/shard_map/ppermute | solution.py:275
  6.5 8.5 %collective-permute-start.1 = (bf16[288,128]{1,0:T(8,128)(2,1)S(1)}, bf16[288,128]{1,0:T(8,128)(2,1)S(1)}, u32[]{:S(2)}, u32[]{:S(2)}) collective-permute-start(bf16[288,128]{1,0:T(8,128)(2,1)S(1)} %constant_dynamic-slice_fusion.14), channel_id=1, source_target_pairs={{0,8},{4,12},{1,9},{5,13},{2,10},{6,14},{3,11},{7,15},{16,24},{20,... | collective-permute-start | bytes 221192 | tf_op jit(solution)/shard_map/ppermute | solution.py:275
  11.0 4.0 %collective-permute-start = (bf16[288,128]{1,0:T(8,128)(2,1)S(1)}, bf16[288,128]{1,0:T(8,128)(2,1)S(1)}, u32[]{:S(2)}, u32[]{:S(2)}) collective-permute-start(bf16[288,128]{1,0:T(8,128)(2,1)S(1)} %constant_dynamic-slice_fusion.14), channel_id=1, source_target_pairs={{0,12},{1,13},{2,14},{3,15},{16,28},{17,29},{18,30},{19,31}} | collective-permute-start | bytes 221192 | tf_op jit(solution)/shard_map/ppermute | solution.py:275
  14.6 2.0 copy-start.5
  15.0 1.5 collective-permute-start.3
  16.6 1.6 copy-start.1
  16.8 2.2 copy-start
  25.8 5.5 %collective-permute-start.6 = (bf16[32,2048]{1,0:T(8,128)(2,1)S(1)}, bf16[32,2048]{1,0:T(8,128)(2,1)S(1)}, u32[]{:S(2)}, u32[]{:S(2)}) collective-permute-start(bf16[32,2048]{1,0:T(8,128)(2,1)S(1)} %get-tuple-element.66), channel_id=1, source_target_pairs={{0,3},{1,2},{2,1},{3,0},{4,7},{5,6},{6,5},{7,4},{8,11},{9,10},{10,... | collective-permute-start | bytes 393224 | tf_op jit(solution)/shard_map/ppermute | solution.py:182
  27.1 7.4 %collective-permute-start.5 = (bf16[32,2048]{1,0:T(8,128)(2,1)S(1)}, bf16[32,2048]{1,0:T(8,128)(2,1)S(1)}, u32[]{:S(2)}, u32[]{:S(2)}) collective-permute-start(bf16[32,2048]{1,0:T(8,128)(2,1)S(1)} %get-tuple-element.67), channel_id=1, source_target_pairs={{0,2},{1,3},{2,0},{3,1},{4,6},{5,7},{6,4},{7,5},{8,10},{9,11},{10,... | collective-permute-start | bytes 393224 | tf_op jit(solution)/shard_map/ppermute | solution.py:182
  27.7 6.8 %collective-permute-start.4 = (bf16[32,2048]{1,0:T(8,128)(2,1)S(1)}, bf16[32,2048]{1,0:T(8,128)(2,1)S(1)}, u32[]{:S(2)}, u32[]{:S(2)}) collective-permute-start(bf16[32,2048]{1,0:T(8,128)(2,1)S(1)} %get-tuple-element.68), channel_id=1, source_target_pairs={{0,1},{1,0},{2,3},{3,2},{4,5},{5,4},{6,7},{7,6},{8,9},{9,8},{10,11... | collective-permute-start | bytes 393224 | tf_op jit(solution)/shard_map/ppermute | solution.py:182
  34.6 8.3 %collective-permute-start.9 = (bf16[32,2048]{1,0:T(8,128)(2,1)S(1)}, bf16[32,2048]{1,0:T(8,128)(2,1)S(1)}, u32[]{:S(2)}, u32[]{:S(2)}) collective-permute-start(bf16[32,2048]{1,0:T(8,128)(2,1)S(1)} %get-tuple-element.62), channel_id=1, source_target_pairs={{0,12},{4,8},{8,4},{12,0},{1,13},{5,9},{9,5},{13,1},{2,14},{6,10},... | collective-permute-start | bytes 393224 | tf_op jit(solution)/shard_map/ppermute | solution.py:182
  38.3 10.2 %collective-permute-start.8 = (bf16[32,2048]{1,0:T(8,128)(2,1)S(1)}, bf16[32,2048]{1,0:T(8,128)(2,1)S(1)}, u32[]{:S(2)}, u32[]{:S(2)}) collective-permute-start(bf16[32,2048]{1,0:T(8,128)(2,1)S(1)} %get-tuple-element.63), channel_id=1, source_target_pairs={{0,8},{4,12},{8,0},{12,4},{1,9},{5,13},{9,1},{13,5},{2,10},{6,14},... | collective-permute-start | bytes 393224 | tf_op jit(solution)/shard_map/ppermute | solution.py:182
  38.3 10.2 %collective-permute-start.7 = (bf16[32,2048]{1,0:T(8,128)(2,1)S(1)}, bf16[32,2048]{1,0:T(8,128)(2,1)S(1)}, u32[]{:S(2)}, u32[]{:S(2)}) collective-permute-start(bf16[32,2048]{1,0:T(8,128)(2,1)S(1)} %get-tuple-element.64), channel_id=1, source_target_pairs={{0,4},{4,0},{8,12},{12,8},{1,5},{5,1},{9,13},{13,9},{2,6},{6,2},{1... | collective-permute-start | bytes 393224 | tf_op jit(solution)/shard_map/ppermute | solution.py:182
  48.6 2.0 collective-permute-start.10
  48.6 14.3 %collective-permute-start.13 = (bf16[4,32,2048]{2,1,0:T(8,128)(2,1)S(1)}, bf16[4,32,2048]{2,1,0:T(8,128)(2,1)S(1)}, u32[]{:S(2)}, u32[]{:S(2)}) collective-permute-start(bf16[4,32,2048]{2,1,0:T(8,128)(2,1)S(1)} %pad_maximum_fusion.11), channel_id=1, source_target_pairs={{0,2},{1,3},{2,0},{3,1},{4,6},{5,7},{6,4},{7,5},{8,10},{9,11},{10,... | collective-permute-start | bytes 1572872 | tf_op jit(solution)/shard_map/ppermute | solution.py:182
  55.0 12.6 %collective-permute-start.11 = (bf16[2,64,1792]{2,1,0:T(8,128)(2,1)S(1)}, bf16[2,64,1792]{2,1,0:T(8,128)(2,1)S(1)}, u32[]{:S(2)}, u32[]{:S(2)}) collective-permute-start(bf16[2,64,1792]{2,1,0:T(8,128)(2,1)S(1)} %slice_bitcast_fusion.5), channel_id=1, source_target_pairs={{0,4},{4,0},{8,12},{12,8},{1,5},{5,1},{9,13},{13,9},{2,6},{6,2},{1... | collective-permute-start | bytes 1376264 | tf_op jit(solution)/shard_map/ppermute | solution.py:182
  63.0 6.2 %collective-permute-start.14 = (bf16[4,32,2048]{2,1,0:T(8,128)(2,1)S(1)}, bf16[4,32,2048]{2,1,0:T(8,128)(2,1)S(1)}, u32[]{:S(2)}, u32[]{:S(2)}) collective-permute-start(bf16[4,32,2048]{2,1,0:T(8,128)(2,1)S(1)} %collective-permute-done.13), channel_id=1, source_target_pairs={{0,1},{1,0},{2,3},{3,2},{4,5},{5,4},{6,7},{7,6},{8,9},{9,8},{10,11... | collective-permute-start | bytes 1572872 | tf_op jit(solution)/shard_map/ppermute | solution.py:182
  67.7 12.8 %collective-permute-start.12 = (bf16[64,1792]{1,0:T(8,128)(2,1)S(1)}, bf16[64,1792]{1,0:T(8,128)(2,1)S(1)}, u32[]{:S(2)}, u32[]{:S(2)}) collective-permute-start(bf16[64,1792]{1,0:T(8,128)(2,1)S(1)} %fusion.19), channel_id=1, source_target_pairs={{0,8},{4,12},{8,0},{12,4},{1,9},{5,13},{9,1},{13,5},{2,10},{6,14},... | collective-permute-start | bytes 688136 | tf_op jit(solution)/shard_map/ppermute | solution.py:182
  69.4 11.1 %copy-start.3 = (bf16[128,1792]{1,0:T(8,128)(2,1)S(1)}, bf16[128,1792]{1,0:T(8,128)(2,1)}, u32[]{:S(2)}) copy-start(bf16[128,1792]{1,0:T(8,128)(2,1)} %param.10) | copy-start | bytes 1376260
  73.6 21.4 %collective-permute-start.15 = (bf16[2,64,1792]{2,1,0:T(8,128)(2,1)S(1)}, bf16[2,64,1792]{2,1,0:T(8,128)(2,1)S(1)}, u32[]{:S(2)}, u32[]{:S(2)}) collective-permute-start(bf16[2,64,1792]{2,1,0:T(8,128)(2,1)S(1)} %slice_bitcast_fusion.4), channel_id=1, source_target_pairs={{0,4},{4,0},{8,12},{12,8},{1,5},{5,1},{9,13},{13,9},{2,6},{6,2},{1... | collective-permute-start | bytes 1376264 | tf_op jit(solution)/shard_map/ppermute | solution.py:182
  80.6 13.3 %collective-permute-start.16 = (bf16[64,1792]{1,0:T(8,128)(2,1)S(1)}, bf16[64,1792]{1,0:T(8,128)(2,1)S(1)}, u32[]{:S(2)}, u32[]{:S(2)}) collective-permute-start(bf16[64,1792]{1,0:T(8,128)(2,1)S(1)} %fusion.22), channel_id=1, source_target_pairs={{0,8},{4,12},{8,0},{12,4},{1,9},{5,13},{9,1},{13,5},{2,10},{6,14},... | collective-permute-start | bytes 688136 | tf_op jit(solution)/shard_map/ppermute | solution.py:182
  94.0 16.8 %collective-permute-start.17 = (bf16[128,1792]{1,0:T(8,128)(2,1)S(1)}, bf16[128,1792]{1,0:T(8,128)(2,1)S(1)}, u32[]{:S(2)}, u32[]{:S(2)}) collective-permute-start(bf16[128,1792]{1,0:T(8,128)(2,1)S(1)} %pad_maximum_fusion.12), channel_id=1, source_target_pairs={{0,4},{4,0},{8,12},{12,8},{1,5},{5,1},{9,13},{13,9},{2,6},{6,2},{1... | collective-permute-start | bytes 1376264 | tf_op jit(solution)/shard_map/ppermute | solution.py:182
  95.1 15.7 %copy-start.2 = (f32[1792]{0:T(1024)S(1)}, f32[1792]{0:T(1024)}, u32[]{:S(2)}) copy-start(f32[1792]{0:T(1024)} %param.16) | copy-start | bytes 21508
  95.2 13.4 %collective-permute-start.18 = (bf16[64,1792]{1,0:T(8,128)(2,1)S(1)}, bf16[64,1792]{1,0:T(8,128)(2,1)S(1)}, u32[]{:S(2)}, u32[]{:S(2)}) collective-permute-start(bf16[64,1792]{1,0:T(8,128)(2,1)S(1)} %shard_map.116), channel_id=1, source_target_pairs={{0,8},{4,12},{8,0},{12,4},{1,9},{5,13},{9,1},{13,5},{2,10},{6,14},... | collective-permute-start | bytes 688136 | tf_op jit(solution)/shard_map/ppermute | solution.py:182
  108.5 8.9 %copy-start.6 = (bf16[64,1792]{1,0:T(8,128)(2,1)}, bf16[64,1792]{1,0:T(8,128)(2,1)S(1)}, u32[]{:S(2)}) copy-start(bf16[64,1792]{1,0:T(8,128)(2,1)S(1)} %collective-permute-done.18) | copy-start | bytes 688132
  110.7 9.3 %slice-start = ((s8[9175040]{0:T(1024)(128)(4,1)}), s8[4194304]{0:T(1024)(128)(4,1)S(1)}, s32[]{:S(2)}) async-start(s8[9175040]{0:T(1024)(128)(4,1)} %bitcast.172), calls=%async_computation | async-start | bytes 8388608
  111.1 9.0 %slice-start.1 = ((s8[9175040]{0:T(1024)(128)(4,1)}), s8[4194304]{0:T(1024)(128)(4,1)S(1)}, s32[]{:S(2)}) async-start(s8[9175040]{0:T(1024)(128)(4,1)} %bitcast.172), calls=%async_computation.1 | async-start | bytes 8388608
  111.1 9.0 %slice-start.2 = ((s8[9175040]{0:T(1024)(128)(4,1)}), s8[786432]{0:T(1024)(128)(4,1)S(1)}, s32[]{:S(2)}) async-start(s8[9175040]{0:T(1024)(128)(4,1)} %bitcast.172), calls=%async_computation.2 | async-start | bytes 1572864
  117.4 1.0 copy-start.4
  117.5 1.1 copy-start.7
  117.6 5.2 %collective-permute-start.20 = (bf16[128,2560]{1,0:T(8,128)(2,1)S(1)}, bf16[128,2560]{1,0:T(8,128)(2,1)S(1)}, u32[]{:S(2)}, u32[]{:S(2)}) collective-permute-start(bf16[128,2560]{1,0:T(8,128)(2,1)S(1)} %bitcast.180), channel_id=1, source_target_pairs={{0,1},{1,0},{2,3},{3,2},{4,5},{5,4},{6,7},{7,6},{8,9},{9,8},{10,11... | collective-permute-start | bytes 1966088 | tf_op jit(solution)/shard_map/ppermute | solution.py:182
  118.7 13.0 %collective-permute-start.19 = (bf16[64,1792]{1,0:T(8,128)(2,1)S(1)}, bf16[64,1792]{1,0:T(8,128)(2,1)S(1)}, u32[]{:S(2)}, u32[]{:S(2)}) collective-permute-start(bf16[64,1792]{1,0:T(8,128)(2,1)S(1)} %get-tuple-element.36), channel_id=1, source_target_pairs={{0,8},{4,12},{8,0},{12,4},{1,9},{5,13},{9,1},{13,5},{2,10},{6,14},... | collective-permute-start | bytes 688136 | tf_op jit(solution)/shard_map/ppermute | solution.py:182
  122.7 2.6 %collective-permute-start.22 = (bf16[128,2560]{1,0:T(8,128)(2,1)S(1)}, bf16[128,2560]{1,0:T(8,128)(2,1)S(1)}, u32[]{:S(2)}, u32[]{:S(2)}) collective-permute-start(bf16[128,2560]{1,0:T(8,128)(2,1)S(1)} %bitcast.181), channel_id=1, source_target_pairs={{0,1},{1,0},{2,3},{3,2},{4,5},{5,4},{6,7},{7,6},{8,9},{9,8},{10,11... | collective-permute-start | bytes 1966088 | tf_op jit(solution)/shard_map/ppermute | solution.py:182
  123.8 17.7 %collective-permute-start.21 = (bf16[128,2560]{1,0:T(8,128)(2,1)}, bf16[128,2560]{1,0:T(8,128)(2,1)S(1)}, u32[]{:S(2)}, u32[]{:S(2)}) collective-permute-start(bf16[128,2560]{1,0:T(8,128)(2,1)} %fusion.3), channel_id=1, source_target_pairs={{0,2},{1,3},{2,0},{3,1},{4,6},{5,7},{6,4},{7,5},{8,10},{9,11},{10,... | collective-permute-start | bytes 1966088 | tf_op jit(solution)/shard_map/ppermute | solution.py:182
  125.5 1.2 collective-permute-start.25
  125.8 29.4 %collective-permute-start.28 = (bf16[128,2560]{1,0:T(8,128)(2,1)S(1)}, bf16[128,2560]{1,0:T(8,128)(2,1)S(1)}, u32[]{:S(2)}, u32[]{:S(2)}) collective-permute-start(bf16[128,2560]{1,0:T(8,128)(2,1)S(1)} %fusion.2), channel_id=1, source_target_pairs={{0,2},{1,3},{2,0},{3,1},{4,6},{5,7},{6,4},{7,5},{8,10},{9,11},{10,... | collective-permute-start | bytes 1966088 | tf_op jit(solution)/shard_map/ppermute | solution.py:182
  126.8 33.8 %collective-permute-start.26 = (f32[256]{0:T(256)S(1)}, f32[256]{0:T(256)S(1)}, u32[]{:S(2)}, u32[]{:S(2)}) collective-permute-start(f32[256]{0:T(256)S(1)} %add.257), channel_id=1, source_target_pairs={{0,2},{1,3},{2,0},{3,1},{4,6},{5,7},{6,4},{7,5},{8,10},{9,11},{10,... | collective-permute-start | bytes 3080 | tf_op jit(solution)/shard_map/ppermute | solution.py:182
  141.6 13.6 %collective-permute-start.27 = (bf16[128,1792]{1,0:T(8,128)(2,1)S(1)}, bf16[128,1792]{1,0:T(8,128)(2,1)S(1)}, u32[]{:S(2)}, u32[]{:S(2)}) collective-permute-start(bf16[128,1792]{1,0:T(8,128)(2,1)S(1)} %pad_maximum_fusion.14), channel_id=1, source_target_pairs={{0,4},{4,0},{8,12},{12,8},{1,5},{5,1},{9,13},{13,9},{2,6},{6,2},{1... | collective-permute-start | bytes 1376264 | tf_op jit(solution)/shard_map/ppermute | solution.py:182
  143.9 11.5 %slice-start.3 = ((s8[9175040]{0:T(1024)(128)(4,1)}), s8[4194304]{0:T(1024)(128)(4,1)S(1)}, s32[]{:S(2)}) async-start(s8[9175040]{0:T(1024)(128)(4,1)} %bitcast.174), calls=%async_computation.3 | async-start | bytes 8388608
  143.9 11.5 %slice-start.4 = ((s8[9175040]{0:T(1024)(128)(4,1)}), s8[4194304]{0:T(1024)(128)(4,1)S(1)}, s32[]{:S(2)}) async-start(s8[9175040]{0:T(1024)(128)(4,1)} %bitcast.174), calls=%async_computation.4 | async-start | bytes 8388608
  149.3 6.1 %slice-start.5 = ((s8[9175040]{0:T(1024)(128)(4,1)}), s8[786432]{0:T(1024)(128)(4,1)S(1)}, s32[]{:S(2)}) async-start(s8[9175040]{0:T(1024)(128)(4,1)} %bitcast.174), calls=%async_computation.5 | async-start | bytes 1572864
  154.4 6.2 %collective-permute-start.24 = (f32[128]{0:T(128)S(1)}, f32[128]{0:T(128)S(1)}, u32[]{:S(2)}, u32[]{:S(2)}) collective-permute-start(f32[128]{0:T(128)S(1)} %fusion.5), channel_id=1, source_target_pairs={{0,1},{1,0},{2,3},{3,2},{4,5},{5,4},{6,7},{7,6},{8,9},{9,8},{10,11... | collective-permute-start | bytes 1544 | tf_op jit(solution)/shard_map/ppermute | solution.py:182
  154.5 2.4 %slice-start.6 = ((s8[9175040]{0:T(1024)(128)(4,1)}), s8[4194304]{0:T(1024)(128)(4,1)S(1)}, s32[]{:S(2)}) async-start(s8[9175040]{0:T(1024)(128)(4,1)} %bitcast.176), calls=%async_computation.6 | async-start | bytes 8388608
  154.6 6.5 %collective-permute-start.23 = (bf16[128,2560]{1,0:T(8,128)(2,1)S(1)}, bf16[128,2560]{1,0:T(8,128)(2,1)S(1)}, u32[]{:S(2)}, u32[]{:S(2)}) collective-permute-start(bf16[128,2560]{1,0:T(8,128)(2,1)S(1)} %pad_maximum_fusion.5), channel_id=1, source_target_pairs={{0,1},{1,0},{2,3},{3,2},{4,5},{5,4},{6,7},{7,6},{8,9},{9,8},{10,11... | collective-permute-start | bytes 1966088 | tf_op jit(solution)/shard_map/ppermute | solution.py:182
  155.4 2.8 %slice-start.7 = ((s8[9175040]{0:T(1024)(128)(4,1)}), s8[4194304]{0:T(1024)(128)(4,1)S(1)}, s32[]{:S(2)}) async-start(s8[9175040]{0:T(1024)(128)(4,1)} %bitcast.176), calls=%async_computation.7 | async-start | bytes 8388608
  155.4 2.9 %slice-start.8 = ((s8[9175040]{0:T(1024)(128)(4,1)}), s8[786432]{0:T(1024)(128)(4,1)S(1)}, s32[]{:S(2)}) async-start(s8[9175040]{0:T(1024)(128)(4,1)} %bitcast.176), calls=%async_computation.8 | async-start | bytes 1572864
  159.8 1.2 collective-permute-start.30
  160.3 2.2 collective-permute-start.29
  163.3 2.2 collective-permute-start.32
  163.6 17.0 %collective-permute-start.31 = (bf16[128,2560]{1,0:T(8,128)(2,1)S(1)}, bf16[128,2560]{1,0:T(8,128)(2,1)S(1)}, u32[]{:S(2)}, u32[]{:S(2)}) collective-permute-start(bf16[128,2560]{1,0:T(8,128)(2,1)S(1)} %pad_maximum_fusion.7), channel_id=1, source_target_pairs={{0,2},{1,3},{2,0},{3,1},{4,6},{5,7},{6,4},{7,5},{8,10},{9,11},{10,... | collective-permute-start | bytes 1966088 | tf_op jit(solution)/shard_map/ppermute | solution.py:182
  170.4 12.6 %collective-permute-start.34 = (bf16[2,64,1792]{2,1,0:T(8,128)(2,1)S(1)}, bf16[2,64,1792]{2,1,0:T(8,128)(2,1)S(1)}, u32[]{:S(2)}, u32[]{:S(2)}) collective-permute-start(bf16[2,64,1792]{2,1,0:T(8,128)(2,1)S(1)} %slice_bitcast_fusion.2), channel_id=1, source_target_pairs={{0,4},{4,0},{8,12},{12,8},{1,5},{5,1},{9,13},{13,9},{2,6},{6,2},{1... | collective-permute-start | bytes 1376264 | tf_op jit(solution)/shard_map/ppermute | solution.py:182
  180.6 2.7 %collective-permute-start.33 = (bf16[128,2560]{1,0:T(8,128)(2,1)S(1)}, bf16[128,2560]{1,0:T(8,128)(2,1)S(1)}, u32[]{:S(2)}, u32[]{:S(2)}) collective-permute-start(bf16[128,2560]{1,0:T(8,128)(2,1)S(1)} %collective-permute-done.31), channel_id=1, source_target_pairs={{0,1},{1,0},{2,3},{3,2},{4,5},{5,4},{6,7},{7,6},{8,9},{9,8},{10,11... | collective-permute-start | bytes 1966088 | tf_op jit(solution)/shard_map/ppermute | solution.py:182
  188.1 17.0 %collective-permute-start.35 = (bf16[2,64,1792]{2,1,0:T(8,128)(2,1)S(1)}, bf16[2,64,1792]{2,1,0:T(8,128)(2,1)S(1)}, u32[]{:S(2)}, u32[]{:S(2)}) collective-permute-start(bf16[2,64,1792]{2,1,0:T(8,128)(2,1)S(1)} %slice_bitcast_fusion), channel_id=1, source_target_pairs={{0,4},{4,0},{8,12},{12,8},{1,5},{5,1},{9,13},{13,9},{2,6},{6,2},{1... | collective-permute-start | bytes 1376264 | tf_op jit(solution)/shard_map/ppermute | solution.py:182
  189.8 15.9 %collective-permute-start.37 = (bf16[64,1792]{1,0:T(8,128)(2,1)S(1)}, bf16[64,1792]{1,0:T(8,128)(2,1)S(1)}, u32[]{:S(2)}, u32[]{:S(2)}) collective-permute-start(bf16[64,1792]{1,0:T(8,128)(2,1)S(1)} %fusion.31), channel_id=1, source_target_pairs={{0,8},{4,12},{8,0},{12,4},{1,9},{5,13},{9,1},{13,5},{2,10},{6,14},... | collective-permute-start | bytes 688136 | tf_op jit(solution)/shard_map/ppermute | solution.py:182
  205.3 11.9 %collective-permute-start.36 = (bf16[64,1792]{1,0:T(8,128)(2,1)S(1)}, bf16[64,1792]{1,0:T(8,128)(2,1)S(1)}, u32[]{:S(2)}, u32[]{:S(2)}) collective-permute-start(bf16[64,1792]{1,0:T(8,128)(2,1)S(1)} %fusion.32), channel_id=1, source_target_pairs={{0,8},{4,12},{8,0},{12,4},{1,9},{5,13},{9,1},{13,5},{2,10},{6,14},... | collective-permute-start | bytes 688136 | tf_op jit(solution)/shard_map/ppermute | solution.py:182

commit v17 on v16

--- a/solution.py
+++ b/solution.py
@@ -225,10 +225,11 @@
                 out[:, columns] = term.astype(out.dtype)
 
 
-def streamed_matmul(rows, weight):
-    steps = weight.shape[0] // 512
+def streamed_matmul(rows, weight, grant=50, flops=1024):
+    depth = 512 if weight.shape[0] % 512 == 0 else 256
+    steps = weight.shape[0] // depth
     return pl.pallas_call(
-        functools.partial(streamed_kernel, 512),
+        functools.partial(streamed_kernel, depth),
         in_specs=[
             pl.BlockSpec(memory_space=pltpu.VMEM),
             pl.BlockSpec(memory_space=pl.ANY),
@@ -240,8 +241,8 @@
             pltpu.VMEM((rows.shape[0], weight.shape[1]), jnp.float32),
             pltpu.SemaphoreType.DMA((2 * steps,)),
         ],
-        compiler_params=pltpu.CompilerParams(vmem_limit_bytes=50 * 1024 * 1024),
-        cost_estimate=pl.CostEstimate(flops=1024, bytes_accessed=1024, transcendentals=0),
+        compiler_params=pltpu.CompilerParams(vmem_limit_bytes=grant * 1024 * 1024),
+        cost_estimate=pl.CostEstimate(flops=flops, bytes_accessed=1024, transcendentals=0),
     )(rows, weight)
 
 
@@ -361,8 +362,8 @@
     all_a = jnp.concatenate([pair_a, rest_a], axis=0)
     squares_a, scaled = scale(all_a)
 
-    def cross(rows, weight):
-        term = matmul(rows, weight).reshape(2, 2, half, -1)
+    def cross(rows, weight, product):
+        term = product(rows, weight).reshape(2, 2, half, -1)
 
         def side(which):
             return lax.dynamic_index_in_dim(term, which, 1, keepdims=False).reshape(2 * half, -1)
@@ -371,8 +372,9 @@
         total = chip_sum(side(core), sent).astype(jnp.bfloat16)
         return sent, total, swap(total, "tp", 2)
 
-    sent_gate, _, across_gate = cross(scaled, gate_weight)
-    _, sums_up, across_up = cross(after(scaled, sent_gate), up_weight)
+    streamed = functools.partial(streamed_matmul, grant=24, flops=6 * 10**9)
+    sent_gate, _, across_gate = cross(scaled, gate_weight, streamed)
+    _, sums_up, across_up = cross(after(scaled, sent_gate), up_weight, matmul)
     squares_a = after(squares_a, sums_up)
     across_squares = swap(squares_a + swap(squares_a, "tp", 1), "tp", 2)
     pair_b = jnp.concatenate([attended_b, after(twin_b, across_gate)], axis=0)
@@ -453,6 +455,8 @@
         and residual.shape[1] % 256 == 0
         and output_weight.shape[0] % 512 == 0
         and down_weight.shape[0] % 512 == 0
+        and gate_weight.shape[0] % 256 == 0
+        and gate_weight.shape[1] % 256 == 0
     )
     own_index = ctx_place * row_count + jnp.arange(row_count, dtype=jnp.int32)
     _, own_position = trace_info(own_index, lengths)

time: 218 us -> 225 us (1.032)
  matrix products: 22.1 us -> 15.4 us
  Pallas kernels: 24.7 us -> 30.9 us
  local copies, waits for them, and re-layouts: 6.04 us -> 9.07 us
    dot_general x6 -> x5, matrix products: 22.1 us -> 15.4 us  [matmul(): jnp.dot(a, b, preferred_element_type=jnp.float32).astype(jnp.bfloat16)]
    pallas_call x4 -> x5, Pallas kernels: 17.9 us -> 24.2 us  [streamed_matmul(): pl.pallas_call(functools.partial(streamed_kernel, depth), in_specs=[pl.Bl...]
    unnamed x36 -> x32, local copies, waits for them, and re-layouts: 4.17 us -> 7.19 us
where the time goes in v17:
time: 225 us; the launch traced here: 224 us
  waiting for transfers between devices  116 us (52%)
  starting transfers between devices  41.3 us (18%)
  Pallas kernels  30.9 us (14%)
  matrix products  15.4 us (7%)
  other arithmetic  10.3 us (5%)
  local copies, waits for them, and re-layouts  9.07 us (4%)
    ppermute x35, waiting for transfers between devices, swap(): return lax.ppermute(value, axis_name, [(i, i ^ bit) for i in range(width)])  116 us
    ppermute x35, starting transfers between devices, swap(): return lax.ppermute(value, axis_name, [(i, i ^ bit) for i in range(width)])  30.6 us
    pallas_call x5, Pallas kernels, streamed_matmul(): pl.pallas_call(functools.partial(streamed_kernel, depth), in_specs=[pl.Bl...  24.2 us
    dot_general x5, matrix products, matmul(): jnp.dot(a, b, preferred_element_type=jnp.float32).astype(jnp.bfloat16)  15.4 us
    ppermute x3, starting transfers between devices, gather_keys(): lax.ppermute(half, 'ctx', [(c, c + d) for c in range(n_ctx - d)])  10.7 us
    unnamed x32, local copies, waits for them, and re-layouts  7.19 us
    pallas_call x1, Pallas kernels, attention(): pl.pallas_call(functools.partial(attention_kernel, group), grid=(local_he...  6.61 us
  transfers between devices with their start and end apart: 38, of which 22 were waited for; matrix products, arithmetic and copies ran while one was open for 10% of the time, Pallas kernels for 6%

profile of v17, /device:TPU:0, one launch (start us, length us, event | category | flops | bytes accessed | tf_op | source)
XLA Modules:
  0.0 224.4 jit_solution(12411530333772130614)
XLA Ops:
  0.6 0.9 constant_dynamic-slice_fusion.14
  1.5 4.9 %collective-permute-start.2 = (bf16[288,128]{1,0:T(8,128)(2,1)S(1)}, bf16[288,128]{1,0:T(8,128)(2,1)S(1)}, u32[]{:S(2)}, u32[]{:S(2)}) collective-permute-start(bf16[288,128]{1,0:T(8,128)(2,1)S(1)} %constant_dynamic-slice_fusion.14), channel_id=1, source_target_pairs={{0,4},{4,8},{8,12},{1,5},{5,9},{9,13},{2,6},{6,10},{10,14},{3,7},{... | collective-permute-start | bytes 221192 | tf_op jit(solution)/shard_map/ppermute | solution.py:276
  6.5 4.5 %collective-permute-start.1 = (bf16[288,128]{1,0:T(8,128)(2,1)S(1)}, bf16[288,128]{1,0:T(8,128)(2,1)S(1)}, u32[]{:S(2)}, u32[]{:S(2)}) collective-permute-start(bf16[288,128]{1,0:T(8,128)(2,1)S(1)} %constant_dynamic-slice_fusion.14), channel_id=1, source_target_pairs={{0,8},{4,12},{1,9},{5,13},{2,10},{6,14},{3,11},{7,15},{16,24},{20,... | collective-permute-start | bytes 221192 | tf_op jit(solution)/shard_map/ppermute | solution.py:276
  11.0 1.3 collective-permute-start
  12.3 0.8 reduce-window.8
  13.2 0.7 subtract_subtract_fusion
  15.1 1.5 collective-permute-done.3
  17.2 1.0 copy-done.2
  18.2 0.7 copy-done.1
  19.0 6.6 %shard_map.113 = bf16[128,2048]{1,0:T(8,128)(2,1)S(1)} custom-call(f32[4,128,128]{2,1,0:T(8,128)S(1)} %pad_maximum_fusion.16.tables, s32[128,1]{1,0:T(8,128)S(1)} %copy.35.starts, s32[128,1]{1,0:T(8,128)S(1)} %iota_add_fusion.own_index, s32[1,512]{1,0:T(1,128)S(1)} %iota_add_fusion.2.key_index, bf16[576,512]{1,0:T(8,128)(2,1)S(1)} %pad_maximum_fusion.9.keys, ...), custom_call_target="tpu_custom_call" | custom-call | flops 2684354560 | bytes 5046272 | tf_op jit(solution)/shard_map/pallas_call | solution.py:143
  25.6 1.3 collective-permute-start.6
  26.9 0.5 collective-permute-start.5
  27.6 3.6 %collective-permute-done.6 = bf16[32,2048]{1,0:T(8,128)(2,1)S(1)} collective-permute-done((bf16[32,2048]{1,0:T(8,128)(2,1)S(1)}, bf16[32,2048]{1,0:T(8,128)(2,1)S(1)}, u32[]{:S(2)}, u32[]{:S(2)}) %collective-permute-start.6) | collective-permute-done | bytes 131104 | tf_op jit(solution)/shard_map/ppermute | solution.py:182
  31.2 3.1 %collective-permute-done.5 = bf16[32,2048]{1,0:T(8,128)(2,1)S(1)} collective-permute-done((bf16[32,2048]{1,0:T(8,128)(2,1)S(1)}, bf16[32,2048]{1,0:T(8,128)(2,1)S(1)}, u32[]{:S(2)}, u32[]{:S(2)}) %collective-permute-start.5) | collective-permute-done | bytes 131104 | tf_op jit(solution)/shard_map/ppermute | solution.py:182
  34.4 3.7 %collective-permute-start.9 = (bf16[32,2048]{1,0:T(8,128)(2,1)S(1)}, bf16[32,2048]{1,0:T(8,128)(2,1)S(1)}, u32[]{:S(2)}, u32[]{:S(2)}) collective-permute-start(bf16[32,2048]{1,0:T(8,128)(2,1)S(1)} %get-tuple-element.62), channel_id=1, source_target_pairs={{0,12},{4,8},{8,4},{12,0},{1,13},{5,9},{9,5},{13,1},{2,14},{6,10},... | collective-permute-start | bytes 393224 | tf_op jit(solution)/shard_map/ppermute | solution.py:182
  38.1 0.8 collective-permute-start.7
  38.9 3.8 %collective-permute-done.9 = bf16[32,2048]{1,0:T(8,128)(2,1)S(1)} collective-permute-done((bf16[32,2048]{1,0:T(8,128)(2,1)S(1)}, bf16[32,2048]{1,0:T(8,128)(2,1)S(1)}, u32[]{:S(2)}, u32[]{:S(2)}) %collective-permute-start.9) | collective-permute-done | bytes 131104 | tf_op jit(solution)/shard_map/ppermute | solution.py:182
  42.7 5.6 %collective-permute-done.8 = bf16[32,2048]{1,0:T(8,128)(2,1)S(1)} collective-permute-done((bf16[32,2048]{1,0:T(8,128)(2,1)S(1)}, bf16[32,2048]{1,0:T(8,128)(2,1)S(1)}, u32[]{:S(2)}, u32[]{:S(2)}) %collective-permute-start.8) | collective-permute-done | bytes 131104 | tf_op jit(solution)/shard_map/ppermute | solution.py:182
  48.5 1.6 collective-permute-start.13
  50.6 4.1 %shard_map.114 = bf16[256,1792]{1,0:T(8,128)(2,1)S(1)} custom-call(bf16[256,2048]{1,0:T(8,128)(2,1)S(1)} %bitcast.162, bf16[2048,1792]{1,0:T(8,128)(2,1)} %weight.6), custom_call_target="tpu_custom_call" | custom-call | flops 1024 | bytes 1024 | tf_op jit(solution)/shard_map/pallas_call | solution.py:231
  54.8 0.8 collective-permute-start.11
  55.6 7.2 %collective-permute-done.13 = bf16[4,32,2048]{2,1,0:T(8,128)(2,1)S(1)} collective-permute-done((bf16[4,32,2048]{2,1,0:T(8,128)(2,1)S(1)}, bf16[4,32,2048]{2,1,0:T(8,128)(2,1)S(1)}, u32[]{:S(2)}, u32[]{:S(2)}) %collective-permute-start.13) | collective-permute-done | bytes 524320 | tf_op jit(solution)/shard_map/ppermute | solution.py:182
  62.8 4.6 %collective-permute-done.11 = bf16[2,64,1792]{2,1,0:T(8,128)(2,1)S(1)} collective-permute-done((bf16[2,64,1792]{2,1,0:T(8,128)(2,1)S(1)}, bf16[2,64,1792]{2,1,0:T(8,128)(2,1)S(1)}, u32[]{:S(2)}, u32[]{:S(2)}) %collective-permute-start.11) | collective-permute-done | bytes 458784 | tf_op jit(solution)/shard_map/ppermute | solution.py:182
  67.5 1.5 collective-permute-start.12
  69.2 4.2 %shard_map.115 = bf16[256,1792]{1,0:T(8,128)(2,1)S(1)} custom-call(bf16[256,2048]{1,0:T(8,128)(2,1)S(1)} %bitcast.161, bf16[2048,1792]{1,0:T(8,128)(2,1)} %weight.6), custom_call_target="tpu_custom_call" | custom-call | flops 1024 | bytes 1024 | tf_op jit(solution)/shard_map/pallas_call | solution.py:231
  73.4 1.8 collective-permute-start.15
  75.2 5.0 %collective-permute-done.12 = bf16[64,1792]{1,0:T(8,128)(2,1)S(1)} collective-permute-done((bf16[64,1792]{1,0:T(8,128)(2,1)S(1)}, bf16[64,1792]{1,0:T(8,128)(2,1)S(1)}, u32[]{:S(2)}, u32[]{:S(2)}) %collective-permute-start.12) | collective-permute-done | bytes 229408 | tf_op jit(solution)/shard_map/ppermute | solution.py:182
  80.5 13.2 %collective-permute-done.16 = bf16[64,1792]{1,0:T(8,128)(2,1)S(1)} collective-permute-done((bf16[64,1792]{1,0:T(8,128)(2,1)S(1)}, bf16[64,1792]{1,0:T(8,128)(2,1)S(1)}, u32[]{:S(2)}, u32[]{:S(2)}) %collective-permute-start.16) | collective-permute-done | bytes 229408 | tf_op jit(solution)/shard_map/ppermute | solution.py:182
  93.8 1.0 collective-permute-done.15
  95.0 2.2 collective-permute-start.18
  97.2 11.2 %collective-permute-done.18 = bf16[64,1792]{1,0:T(8,128)(2,1)S(1)} collective-permute-done((bf16[64,1792]{1,0:T(8,128)(2,1)S(1)}, bf16[64,1792]{1,0:T(8,128)(2,1)S(1)}, u32[]{:S(2)}, u32[]{:S(2)}) %collective-permute-start.18) | collective-permute-done | bytes 229408 | tf_op jit(solution)/shard_map/ppermute | solution.py:182
  108.4 2.2 collective-permute-done.17
  110.9 3.6 %copy-done = bf16[1792,2560]{1,0:T(8,128)(2,1)S(1)} copy-done((bf16[1792,2560]{1,0:T(8,128)(2,1)S(1)}, bf16[1792,2560]{1,0:T(8,128)(2,1)}, u32[]{:S(2)}) %copy-start) | copy-done | bytes 9175064
  114.5 6.4 %shard_map.117 = bf16[256,2560]{1,0:T(8,128)(2,1)S(1)} custom-call(bf16[256,1792]{1,0:T(8,128)(2,1)S(1)} %get-tuple-element.24.rows, bf16[1792,2560]{1,0:T(8,128)(2,1)S(1)} %copy-done), custom_call_target="tpu_custom_call" | custom-call | flops 6000000000 | bytes 1024 | tf_op jit(solution)/shard_map/pallas_call | solution.py:231
  121.1 0.8 copy-done.5
  122.1 1.3 collective-permute-start.19
  123.4 6.1 %convolution_convert_fusion = bf16[256,2560]{1,0:T(8,128)(2,1)S(1)} fusion(bf16[256,1792]{1,0:T(8,128)(2,1)S(1)} %get-tuple-element.24.rows, bf16[1792,2560]{1,0:T(8,128)(2,1)} %param.18), kind=kOutput, calls=%fused_computation | convolution fusion | flops 2349465600 | bytes 11403264 | tf_op jit(solution)/shard_map/dot_general | solution.py:194
  129.7 1.1 fusion.3
  130.8 1.5 collective-permute-start.21
  132.3 1.0 fusion.2
  133.5 1.0 collective-permute-start.28
  134.5 1.1 collective-permute-start.26
  135.6 13.0 %collective-permute-done.21 = bf16[128,2560]{1,0:T(8,128)(2,1)S(1)} collective-permute-done((bf16[128,2560]{1,0:T(8,128)(2,1)}, bf16[128,2560]{1,0:T(8,128)(2,1)S(1)}, u32[]{:S(2)}, u32[]{:S(2)}) %collective-permute-start.21) | collective-permute-done | bytes 655392 | tf_op jit(solution)/shard_map/ppermute | solution.py:182
  148.5 2.2 collective-permute-start.27
  151.0 5.1 %convolution_convert_fusion.3 = bf16[128,2560]{1,0:T(8,128)(2,1)S(1)} fusion(bf16[1792,2560]{1,0:T(8,128)(2,1)} %param.18, bf16[128,1792]{1,0:T(8,128)(2,1)S(1)} %pad_maximum_fusion.14, f32[1792]{0:T(1024)S(1)} %copy-done.3), kind=kOutput, calls=%fused_computation.3 | convolution fusion | flops 1175420928 | bytes 10296320 | tf_op jit(solution)/shard_map/dot_general | solution.py:194
  156.2 0.9 slice-done.2
  157.0 1.4 convolution_convert_fusion.4
  159.2 2.9 %collective-permute-done.28 = bf16[128,2560]{1,0:T(8,128)(2,1)S(1)} collective-permute-done((bf16[128,2560]{1,0:T(8,128)(2,1)}, bf16[128,2560]{1,0:T(8,128)(2,1)S(1)}, u32[]{:S(2)}, u32[]{:S(2)}) %collective-permute-start.28) | collective-permute-done | bytes 655392 | tf_op jit(solution)/shard_map/ppermute | solution.py:182
  162.4 1.4 convolution_convert_fusion.1
  163.8 1.4 convolution_convert_fusion.2
  166.7 1.0 collective-permute-done.29
  167.9 0.6 fusion.14
  169.0 1.5 collective-permute-start.31
  171.0 4.8 %shard_map.118 = bf16[256,1792]{1,0:T(8,128)(2,1)S(1)} custom-call(bf16[256,2560]{1,0:T(8,128)(2,1)S(1)} %pad_maximum_fusion.rows, bf16[2560,1792]{1,0:T(8,128)(2,1)} %weight.9), custom_call_target="tpu_custom_call" | custom-call | flops 1024 | bytes 1024 | tf_op jit(solution)/shard_map/pallas_call | solution.py:231
  175.8 2.3 %collective-permute-start.34 = (bf16[2,64,1792]{2,1,0:T(8,128)(2,1)S(1)}, bf16[2,64,1792]{2,1,0:T(8,128)(2,1)S(1)}, u32[]{:S(2)}, u32[]{:S(2)}) collective-permute-start(bf16[2,64,1792]{2,1,0:T(8,128)(2,1)S(1)} %slice_bitcast_fusion.2), channel_id=1, source_target_pairs={{0,4},{4,0},{8,12},{12,8},{1,5},{5,1},{9,13},{13,9},{2,6},{6,2},{1... | collective-permute-start | bytes 1376264 | tf_op jit(solution)/shard_map/ppermute | solution.py:182
  178.1 0.8 pad_maximum_fusion.13
  178.9 6.8 %collective-permute-done.31 = bf16[128,2560]{1,0:T(8,128)(2,1)S(1)} collective-permute-done((bf16[128,2560]{1,0:T(8,128)(2,1)S(1)}, bf16[128,2560]{1,0:T(8,128)(2,1)S(1)}, u32[]{:S(2)}, u32[]{:S(2)}) %collective-permute-start.31) | collective-permute-done | bytes 655392 | tf_op jit(solution)/shard_map/ppermute | solution.py:182
  185.8 3.4 %collective-permute-done.34 = bf16[2,64,1792]{2,1,0:T(8,128)(2,1)S(1)} collective-permute-done((bf16[2,64,1792]{2,1,0:T(8,128)(2,1)S(1)}, bf16[2,64,1792]{2,1,0:T(8,128)(2,1)S(1)}, u32[]{:S(2)}, u32[]{:S(2)}) %collective-permute-start.34) | collective-permute-done | bytes 458784 | tf_op jit(solution)/shard_map/ppermute | solution.py:182
  189.4 4.8 %shard_map.119 = bf16[256,1792]{1,0:T(8,128)(2,1)S(1)} custom-call(bf16[256,2560]{1,0:T(8,128)(2,1)S(1)} %pad_maximum_fusion.1.rows, bf16[2560,1792]{1,0:T(8,128)(2,1)} %weight.9), custom_call_target="tpu_custom_call" | custom-call | flops 1024 | bytes 1024 | tf_op jit(solution)/shard_map/pallas_call | solution.py:231
  194.2 1.8 collective-permute-start.35
  196.0 1.2 collective-permute-start.37
  197.2 14.2 %collective-permute-done.35 = bf16[2,64,1792]{2,1,0:T(8,128)(2,1)S(1)} collective-permute-done((bf16[2,64,1792]{2,1,0:T(8,128)(2,1)S(1)}, bf16[2,64,1792]{2,1,0:T(8,128)(2,1)S(1)}, u32[]{:S(2)}, u32[]{:S(2)}) %collective-permute-start.35) | collective-permute-done | bytes 458784 | tf_op jit(solution)/shard_map/ppermute | solution.py:182
  211.9 11.6 %collective-permute-done.36 = bf16[64,1792]{1,0:T(8,128)(2,1)S(1)} collective-permute-done((bf16[64,1792]{1,0:T(8,128)(2,1)S(1)}, bf16[64,1792]{1,0:T(8,128)(2,1)S(1)}, u32[]{:S(2)}, u32[]{:S(2)}) %collective-permute-start.36) | collective-permute-done | bytes 229408 | tf_op jit(solution)/shard_map/ppermute | solution.py:182
  223.6 0.8 pad_maximum_fusion.15
  (136 shorter events, 9.4 us)
Async XLA Ops:
  1.5 13.5 %collective-permute-start.2 = (bf16[288,128]{1,0:T(8,128)(2,1)S(1)}, bf16[288,128]{1,0:T(8,128)(2,1)S(1)}, u32[]{:S(2)}, u32[]{:S(2)}) collective-permute-start(bf16[288,128]{1,0:T(8,128)(2,1)S(1)} %constant_dynamic-slice_fusion.14), channel_id=1, source_target_pairs={{0,4},{4,8},{8,12},{1,5},{5,9},{9,13},{2,6},{6,10},{10,14},{3,7},{... | collective-permute-start | bytes 221192 | tf_op jit(solution)/shard_map/ppermute | solution.py:276
  6.5 8.5 %collective-permute-start.1 = (bf16[288,128]{1,0:T(8,128)(2,1)S(1)}, bf16[288,128]{1,0:T(8,128)(2,1)S(1)}, u32[]{:S(2)}, u32[]{:S(2)}) collective-permute-start(bf16[288,128]{1,0:T(8,128)(2,1)S(1)} %constant_dynamic-slice_fusion.14), channel_id=1, source_target_pairs={{0,8},{4,12},{1,9},{5,13},{2,10},{6,14},{3,11},{7,15},{16,24},{20,... | collective-permute-start | bytes 221192 | tf_op jit(solution)/shard_map/ppermute | solution.py:276
  11.0 4.0 %collective-permute-start = (bf16[288,128]{1,0:T(8,128)(2,1)S(1)}, bf16[288,128]{1,0:T(8,128)(2,1)S(1)}, u32[]{:S(2)}, u32[]{:S(2)}) collective-permute-start(bf16[288,128]{1,0:T(8,128)(2,1)S(1)} %constant_dynamic-slice_fusion.14), channel_id=1, source_target_pairs={{0,12},{1,13},{2,14},{3,15},{16,28},{17,29},{18,30},{19,31}} | collective-permute-start | bytes 221192 | tf_op jit(solution)/shard_map/ppermute | solution.py:276
  14.6 2.0 copy-start.6
  15.0 1.5 collective-permute-start.3
  16.6 1.6 copy-start.2
  16.8 2.2 copy-start.1
  25.6 5.5 %collective-permute-start.6 = (bf16[32,2048]{1,0:T(8,128)(2,1)S(1)}, bf16[32,2048]{1,0:T(8,128)(2,1)S(1)}, u32[]{:S(2)}, u32[]{:S(2)}) collective-permute-start(bf16[32,2048]{1,0:T(8,128)(2,1)S(1)} %get-tuple-element.66), channel_id=1, source_target_pairs={{0,3},{1,2},{2,1},{3,0},{4,7},{5,6},{6,5},{7,4},{8,11},{9,10},{10,... | collective-permute-start | bytes 393224 | tf_op jit(solution)/shard_map/ppermute | solution.py:182
  26.9 7.4 %collective-permute-start.5 = (bf16[32,2048]{1,0:T(8,128)(2,1)S(1)}, bf16[32,2048]{1,0:T(8,128)(2,1)S(1)}, u32[]{:S(2)}, u32[]{:S(2)}) collective-permute-start(bf16[32,2048]{1,0:T(8,128)(2,1)S(1)} %get-tuple-element.67), channel_id=1, source_target_pairs={{0,2},{1,3},{2,0},{3,1},{4,6},{5,7},{6,4},{7,5},{8,10},{9,11},{10,... | collective-permute-start | bytes 393224 | tf_op jit(solution)/shard_map/ppermute | solution.py:182
  27.5 6.8 %collective-permute-start.4 = (bf16[32,2048]{1,0:T(8,128)(2,1)S(1)}, bf16[32,2048]{1,0:T(8,128)(2,1)S(1)}, u32[]{:S(2)}, u32[]{:S(2)}) collective-permute-start(bf16[32,2048]{1,0:T(8,128)(2,1)S(1)} %get-tuple-element.68), channel_id=1, source_target_pairs={{0,1},{1,0},{2,3},{3,2},{4,5},{5,4},{6,7},{7,6},{8,9},{9,8},{10,11... | collective-permute-start | bytes 393224 | tf_op jit(solution)/shard_map/ppermute | solution.py:182
  34.4 8.3 %collective-permute-start.9 = (bf16[32,2048]{1,0:T(8,128)(2,1)S(1)}, bf16[32,2048]{1,0:T(8,128)(2,1)S(1)}, u32[]{:S(2)}, u32[]{:S(2)}) collective-permute-start(bf16[32,2048]{1,0:T(8,128)(2,1)S(1)} %get-tuple-element.62), channel_id=1, source_target_pairs={{0,12},{4,8},{8,4},{12,0},{1,13},{5,9},{9,5},{13,1},{2,14},{6,10},... | collective-permute-start | bytes 393224 | tf_op jit(solution)/shard_map/ppermute | solution.py:182
  38.1 10.2 %collective-permute-start.8 = (bf16[32,2048]{1,0:T(8,128)(2,1)S(1)}, bf16[32,2048]{1,0:T(8,128)(2,1)S(1)}, u32[]{:S(2)}, u32[]{:S(2)}) collective-permute-start(bf16[32,2048]{1,0:T(8,128)(2,1)S(1)} %get-tuple-element.63), channel_id=1, source_target_pairs={{0,8},{4,12},{8,0},{12,4},{1,9},{5,13},{9,1},{13,5},{2,10},{6,14},... | collective-permute-start | bytes 393224 | tf_op jit(solution)/shard_map/ppermute | solution.py:182
  38.1 10.2 %collective-permute-start.7 = (bf16[32,2048]{1,0:T(8,128)(2,1)S(1)}, bf16[32,2048]{1,0:T(8,128)(2,1)S(1)}, u32[]{:S(2)}, u32[]{:S(2)}) collective-permute-start(bf16[32,2048]{1,0:T(8,128)(2,1)S(1)} %get-tuple-element.64), channel_id=1, source_target_pairs={{0,4},{4,0},{8,12},{12,8},{1,5},{5,1},{9,13},{13,9},{2,6},{6,2},{1... | collective-permute-start | bytes 393224 | tf_op jit(solution)/shard_map/ppermute | solution.py:182
  48.4 2.0 collective-permute-start.10
  48.5 14.3 %collective-permute-start.13 = (bf16[4,32,2048]{2,1,0:T(8,128)(2,1)S(1)}, bf16[4,32,2048]{2,1,0:T(8,128)(2,1)S(1)}, u32[]{:S(2)}, u32[]{:S(2)}) collective-permute-start(bf16[4,32,2048]{2,1,0:T(8,128)(2,1)S(1)} %pad_maximum_fusion.11), channel_id=1, source_target_pairs={{0,2},{1,3},{2,0},{3,1},{4,6},{5,7},{6,4},{7,5},{8,10},{9,11},{10,... | collective-permute-start | bytes 1572872 | tf_op jit(solution)/shard_map/ppermute | solution.py:182
  54.8 12.6 %collective-permute-start.11 = (bf16[2,64,1792]{2,1,0:T(8,128)(2,1)S(1)}, bf16[2,64,1792]{2,1,0:T(8,128)(2,1)S(1)}, u32[]{:S(2)}, u32[]{:S(2)}) collective-permute-start(bf16[2,64,1792]{2,1,0:T(8,128)(2,1)S(1)} %slice_bitcast_fusion.5), channel_id=1, source_target_pairs={{0,4},{4,0},{8,12},{12,8},{1,5},{5,1},{9,13},{13,9},{2,6},{6,2},{1... | collective-permute-start | bytes 1376264 | tf_op jit(solution)/shard_map/ppermute | solution.py:182
  62.8 6.2 %collective-permute-start.14 = (bf16[4,32,2048]{2,1,0:T(8,128)(2,1)S(1)}, bf16[4,32,2048]{2,1,0:T(8,128)(2,1)S(1)}, u32[]{:S(2)}, u32[]{:S(2)}) collective-permute-start(bf16[4,32,2048]{2,1,0:T(8,128)(2,1)S(1)} %collective-permute-done.13), channel_id=1, source_target_pairs={{0,1},{1,0},{2,3},{3,2},{4,5},{5,4},{6,7},{7,6},{8,9},{9,8},{10,11... | collective-permute-start | bytes 1572872 | tf_op jit(solution)/shard_map/ppermute | solution.py:182
  67.5 12.8 %collective-permute-start.12 = (bf16[64,1792]{1,0:T(8,128)(2,1)S(1)}, bf16[64,1792]{1,0:T(8,128)(2,1)S(1)}, u32[]{:S(2)}, u32[]{:S(2)}) collective-permute-start(bf16[64,1792]{1,0:T(8,128)(2,1)S(1)} %fusion.19), channel_id=1, source_target_pairs={{0,8},{4,12},{8,0},{12,4},{1,9},{5,13},{9,1},{13,5},{2,10},{6,14},... | collective-permute-start | bytes 688136 | tf_op jit(solution)/shard_map/ppermute | solution.py:182
  69.2 11.1 %copy-start.4 = (bf16[128,1792]{1,0:T(8,128)(2,1)S(1)}, bf16[128,1792]{1,0:T(8,128)(2,1)}, u32[]{:S(2)}) copy-start(bf16[128,1792]{1,0:T(8,128)(2,1)} %param.10) | copy-start | bytes 1376260
  73.4 21.4 %collective-permute-start.15 = (bf16[2,64,1792]{2,1,0:T(8,128)(2,1)S(1)}, bf16[2,64,1792]{2,1,0:T(8,128)(2,1)S(1)}, u32[]{:S(2)}, u32[]{:S(2)}) collective-permute-start(bf16[2,64,1792]{2,1,0:T(8,128)(2,1)S(1)} %slice_bitcast_fusion.4), channel_id=1, source_target_pairs={{0,4},{4,0},{8,12},{12,8},{1,5},{5,1},{9,13},{13,9},{2,6},{6,2},{1... | collective-permute-start | bytes 1376264 | tf_op jit(solution)/shard_map/ppermute | solution.py:182
  80.4 13.3 %collective-permute-start.16 = (bf16[64,1792]{1,0:T(8,128)(2,1)S(1)}, bf16[64,1792]{1,0:T(8,128)(2,1)S(1)}, u32[]{:S(2)}, u32[]{:S(2)}) collective-permute-start(bf16[64,1792]{1,0:T(8,128)(2,1)S(1)} %fusion.22), channel_id=1, source_target_pairs={{0,8},{4,12},{8,0},{12,4},{1,9},{5,13},{9,1},{13,5},{2,10},{6,14},... | collective-permute-start | bytes 688136 | tf_op jit(solution)/shard_map/ppermute | solution.py:182
  93.8 16.8 %collective-permute-start.17 = (bf16[128,1792]{1,0:T(8,128)(2,1)S(1)}, bf16[128,1792]{1,0:T(8,128)(2,1)S(1)}, u32[]{:S(2)}, u32[]{:S(2)}) collective-permute-start(bf16[128,1792]{1,0:T(8,128)(2,1)S(1)} %pad_maximum_fusion.12), channel_id=1, source_target_pairs={{0,4},{4,0},{8,12},{12,8},{1,5},{5,1},{9,13},{13,9},{2,6},{6,2},{1... | collective-permute-start | bytes 1376264 | tf_op jit(solution)/shard_map/ppermute | solution.py:182
  94.9 15.7 %copy-start.3 = (f32[1792]{0:T(1024)S(1)}, f32[1792]{0:T(1024)}, u32[]{:S(2)}) copy-start(f32[1792]{0:T(1024)} %param.16) | copy-start | bytes 21508
  95.0 13.4 %collective-permute-start.18 = (bf16[64,1792]{1,0:T(8,128)(2,1)S(1)}, bf16[64,1792]{1,0:T(8,128)(2,1)S(1)}, u32[]{:S(2)}, u32[]{:S(2)}) collective-permute-start(bf16[64,1792]{1,0:T(8,128)(2,1)S(1)} %shard_map.116), channel_id=1, source_target_pairs={{0,8},{4,12},{8,0},{12,4},{1,9},{5,13},{9,1},{13,5},{2,10},{6,14},... | collective-permute-start | bytes 688136 | tf_op jit(solution)/shard_map/ppermute | solution.py:182
  108.4 12.5 %copy-start.7 = (bf16[64,1792]{1,0:T(8,128)(2,1)}, bf16[64,1792]{1,0:T(8,128)(2,1)S(1)}, u32[]{:S(2)}) copy-start(bf16[64,1792]{1,0:T(8,128)(2,1)S(1)} %collective-permute-done.18) | copy-start | bytes 688132
  110.9 3.6 %copy-start = (bf16[1792,2560]{1,0:T(8,128)(2,1)S(1)}, bf16[1792,2560]{1,0:T(8,128)(2,1)}, u32[]{:S(2)}) copy-start(bf16[1792,2560]{1,0:T(8,128)(2,1)} %weight.7) | copy-start | bytes 27525124
  120.9 1.0 copy-start.5
  120.9 1.1 copy-start.8
  121.0 8.7 %collective-permute-start.20 = (bf16[128,2560]{1,0:T(8,128)(2,1)S(1)}, bf16[128,2560]{1,0:T(8,128)(2,1)S(1)}, u32[]{:S(2)}, u32[]{:S(2)}) collective-permute-start(bf16[128,2560]{1,0:T(8,128)(2,1)S(1)} %bitcast.178), channel_id=1, source_target_pairs={{0,1},{1,0},{2,3},{3,2},{4,5},{5,4},{6,7},{7,6},{8,9},{9,8},{10,11... | collective-permute-start | bytes 1966088 | tf_op jit(solution)/shard_map/ppermute | solution.py:182
  122.1 13.4 %collective-permute-start.19 = (bf16[64,1792]{1,0:T(8,128)(2,1)S(1)}, bf16[64,1792]{1,0:T(8,128)(2,1)S(1)}, u32[]{:S(2)}, u32[]{:S(2)}) collective-permute-start(bf16[64,1792]{1,0:T(8,128)(2,1)S(1)} %get-tuple-element.36), channel_id=1, source_target_pairs={{0,8},{4,12},{8,0},{12,4},{1,9},{5,13},{9,1},{13,5},{2,10},{6,14},... | collective-permute-start | bytes 688136 | tf_op jit(solution)/shard_map/ppermute | solution.py:182
  129.6 2.6 %collective-permute-start.22 = (bf16[128,2560]{1,0:T(8,128)(2,1)S(1)}, bf16[128,2560]{1,0:T(8,128)(2,1)S(1)}, u32[]{:S(2)}, u32[]{:S(2)}) collective-permute-start(bf16[128,2560]{1,0:T(8,128)(2,1)S(1)} %bitcast.179), channel_id=1, source_target_pairs={{0,1},{1,0},{2,3},{3,2},{4,5},{5,4},{6,7},{7,6},{8,9},{9,8},{10,11... | collective-permute-start | bytes 1966088 | tf_op jit(solution)/shard_map/ppermute | solution.py:182
  130.8 17.7 %collective-permute-start.21 = (bf16[128,2560]{1,0:T(8,128)(2,1)}, bf16[128,2560]{1,0:T(8,128)(2,1)S(1)}, u32[]{:S(2)}, u32[]{:S(2)}) collective-permute-start(bf16[128,2560]{1,0:T(8,128)(2,1)} %fusion.3), channel_id=1, source_target_pairs={{0,2},{1,3},{2,0},{3,1},{4,6},{5,7},{6,4},{7,5},{8,10},{9,11},{10,... | collective-permute-start | bytes 1966088 | tf_op jit(solution)/shard_map/ppermute | solution.py:182
  132.3 23.9 %slice-start = ((s8[9175040]{0:T(1024)(128)(4,1)}), s8[786432]{0:T(1024)(128)(4,1)S(1)}, s32[]{:S(2)}) async-start(s8[9175040]{0:T(1024)(128)(4,1)} %bitcast.159), calls=%async_computation | async-start | bytes 1572864
  133.3 1.2 collective-permute-start.25
  133.5 28.7 %collective-permute-start.28 = (bf16[128,2560]{1,0:T(8,128)(2,1)}, bf16[128,2560]{1,0:T(8,128)(2,1)S(1)}, u32[]{:S(2)}, u32[]{:S(2)}) collective-permute-start(bf16[128,2560]{1,0:T(8,128)(2,1)} %fusion.2), channel_id=1, source_target_pairs={{0,2},{1,3},{2,0},{3,1},{4,6},{5,7},{6,4},{7,5},{8,10},{9,11},{10,... | collective-permute-start | bytes 1966088 | tf_op jit(solution)/shard_map/ppermute | solution.py:182
  134.5 31.5 %collective-permute-start.26 = (f32[256]{0:T(256)S(1)}, f32[256]{0:T(256)S(1)}, u32[]{:S(2)}, u32[]{:S(2)}) collective-permute-start(f32[256]{0:T(256)S(1)} %add.257), channel_id=1, source_target_pairs={{0,2},{1,3},{2,0},{3,1},{4,6},{5,7},{6,4},{7,5},{8,10},{9,11},{10,... | collective-permute-start | bytes 3080 | tf_op jit(solution)/shard_map/ppermute | solution.py:182
  148.5 13.6 %collective-permute-start.27 = (bf16[128,1792]{1,0:T(8,128)(2,1)S(1)}, bf16[128,1792]{1,0:T(8,128)(2,1)S(1)}, u32[]{:S(2)}, u32[]{:S(2)}) collective-permute-start(bf16[128,1792]{1,0:T(8,128)(2,1)S(1)} %pad_maximum_fusion.14), channel_id=1, source_target_pairs={{0,4},{4,0},{8,12},{12,8},{1,5},{5,1},{9,13},{13,9},{2,6},{6,2},{1... | collective-permute-start | bytes 1376264 | tf_op jit(solution)/shard_map/ppermute | solution.py:182
  151.0 5.2 %slice-start.1 = ((s8[9175040]{0:T(1024)(128)(4,1)}), s8[4194304]{0:T(1024)(128)(4,1)S(1)}, s32[]{:S(2)}) async-start(s8[9175040]{0:T(1024)(128)(4,1)} %bitcast.159), calls=%async_computation.1 | async-start | bytes 8388608
  151.0 6.1 %slice-start.2 = ((s8[9175040]{0:T(1024)(128)(4,1)}), s8[4194304]{0:T(1024)(128)(4,1)S(1)}, s32[]{:S(2)}) async-start(s8[9175040]{0:T(1024)(128)(4,1)} %bitcast.159), calls=%async_computation.2 | async-start | bytes 8388608
  151.0 11.4 %slice-start.3 = ((s8[9175040]{0:T(1024)(128)(4,1)}), s8[4194304]{0:T(1024)(128)(4,1)S(1)}, s32[]{:S(2)}) async-start(s8[9175040]{0:T(1024)(128)(4,1)} %bitcast.175), calls=%async_computation.3 | async-start | bytes 8388608
  151.0 11.4 %slice-start.4 = ((s8[9175040]{0:T(1024)(128)(4,1)}), s8[4194304]{0:T(1024)(128)(4,1)S(1)}, s32[]{:S(2)}) async-start(s8[9175040]{0:T(1024)(128)(4,1)} %bitcast.175), calls=%async_computation.4 | async-start | bytes 8388608
  157.0 5.3 %slice-start.5 = ((s8[9175040]{0:T(1024)(128)(4,1)}), s8[786432]{0:T(1024)(128)(4,1)S(1)}, s32[]{:S(2)}) async-start(s8[9175040]{0:T(1024)(128)(4,1)} %bitcast.175), calls=%async_computation.5 | async-start | bytes 1572864
  158.4 7.6 %collective-permute-start.24 = (f32[128]{0:T(128)S(1)}, f32[128]{0:T(128)S(1)}, u32[]{:S(2)}, u32[]{:S(2)}) collective-permute-start(f32[128]{0:T(128)S(1)} %fusion.5), channel_id=1, source_target_pairs={{0,1},{1,0},{2,3},{3,2},{4,5},{5,4},{6,7},{7,6},{8,9},{9,8},{10,11... | collective-permute-start | bytes 1544 | tf_op jit(solution)/shard_map/ppermute | solution.py:182
  158.7 7.9 %collective-permute-start.23 = (bf16[128,2560]{1,0:T(8,128)(2,1)S(1)}, bf16[128,2560]{1,0:T(8,128)(2,1)S(1)}, u32[]{:S(2)}, u32[]{:S(2)}) collective-permute-start(bf16[128,2560]{1,0:T(8,128)(2,1)S(1)} %pad_maximum_fusion.5), channel_id=1, source_target_pairs={{0,1},{1,0},{2,3},{3,2},{4,5},{5,4},{6,7},{7,6},{8,9},{9,8},{10,11... | collective-permute-start | bytes 1966088 | tf_op jit(solution)/shard_map/ppermute | solution.py:182
  165.2 1.2 collective-permute-start.30
  165.4 2.3 %collective-permute-start.29 = (bf16[128,2560]{1,0:T(8,128)(2,1)S(1)}, bf16[128,2560]{1,0:T(8,128)(2,1)S(1)}, u32[]{:S(2)}, u32[]{:S(2)}) collective-permute-start(bf16[128,2560]{1,0:T(8,128)(2,1)S(1)} %pad_maximum_fusion.6), channel_id=1, source_target_pairs={{0,1},{1,0},{2,3},{3,2},{4,5},{5,4},{6,7},{7,6},{8,9},{9,8},{10,11... | collective-permute-start | bytes 1966088 | tf_op jit(solution)/shard_map/ppermute | solution.py:182
  168.5 2.2 collective-permute-start.32
  169.0 16.8 %collective-permute-start.31 = (bf16[128,2560]{1,0:T(8,128)(2,1)S(1)}, bf16[128,2560]{1,0:T(8,128)(2,1)S(1)}, u32[]{:S(2)}, u32[]{:S(2)}) collective-permute-start(bf16[128,2560]{1,0:T(8,128)(2,1)S(1)} %pad_maximum_fusion.7), channel_id=1, source_target_pairs={{0,2},{1,3},{2,0},{3,1},{4,6},{5,7},{6,4},{7,5},{8,10},{9,11},{10,... | collective-permute-start | bytes 1966088 | tf_op jit(solution)/shard_map/ppermute | solution.py:182
  175.8 13.3 %collective-permute-start.34 = (bf16[2,64,1792]{2,1,0:T(8,128)(2,1)S(1)}, bf16[2,64,1792]{2,1,0:T(8,128)(2,1)S(1)}, u32[]{:S(2)}, u32[]{:S(2)}) collective-permute-start(bf16[2,64,1792]{2,1,0:T(8,128)(2,1)S(1)} %slice_bitcast_fusion.2), channel_id=1, source_target_pairs={{0,4},{4,0},{8,12},{12,8},{1,5},{5,1},{9,13},{13,9},{2,6},{6,2},{1... | collective-permute-start | bytes 1376264 | tf_op jit(solution)/shard_map/ppermute | solution.py:182
  185.8 3.5 %collective-permute-start.33 = (bf16[128,2560]{1,0:T(8,128)(2,1)S(1)}, bf16[128,2560]{1,0:T(8,128)(2,1)S(1)}, u32[]{:S(2)}, u32[]{:S(2)}) collective-permute-start(bf16[128,2560]{1,0:T(8,128)(2,1)S(1)} %collective-permute-done.31), channel_id=1, source_target_pairs={{0,1},{1,0},{2,3},{3,2},{4,5},{5,4},{6,7},{7,6},{8,9},{9,8},{10,11... | collective-permute-start | bytes 1966088 | tf_op jit(solution)/shard_map/ppermute | solution.py:182
  194.2 17.2 %collective-permute-start.35 = (bf16[2,64,1792]{2,1,0:T(8,128)(2,1)S(1)}, bf16[2,64,1792]{2,1,0:T(8,128)(2,1)S(1)}, u32[]{:S(2)}, u32[]{:S(2)}) collective-permute-start(bf16[2,64,1792]{2,1,0:T(8,128)(2,1)S(1)} %slice_bitcast_fusion), channel_id=1, source_target_pairs={{0,4},{4,0},{8,12},{12,8},{1,5},{5,1},{9,13},{13,9},{2,6},{6,2},{1... | collective-permute-start | bytes 1376264 | tf_op jit(solution)/shard_map/ppermute | solution.py:182
  196.0 15.8 %collective-permute-start.37 = (bf16[64,1792]{1,0:T(8,128)(2,1)S(1)}, bf16[64,1792]{1,0:T(8,128)(2,1)S(1)}, u32[]{:S(2)}, u32[]{:S(2)}) collective-permute-start(bf16[64,1792]{1,0:T(8,128)(2,1)S(1)} %fusion.31), channel_id=1, source_target_pairs={{0,8},{4,12},{8,0},{12,4},{1,9},{5,13},{9,1},{13,5},{2,10},{6,14},... | collective-permute-start | bytes 688136 | tf_op jit(solution)/shard_map/ppermute | solution.py:182
  211.6 11.8 %collective-permute-start.36 = (bf16[64,1792]{1,0:T(8,128)(2,1)S(1)}, bf16[64,1792]{1,0:T(8,128)(2,1)S(1)}, u32[]{:S(2)}, u32[]{:S(2)}) collective-permute-start(bf16[64,1792]{1,0:T(8,128)(2,1)S(1)} %fusion.32), channel_id=1, source_target_pairs={{0,8},{4,12},{8,0},{12,4},{1,9},{5,13},{9,1},{13,5},{2,10},{6,14},... | collective-permute-start | bytes 688136 | tf_op jit(solution)/shard_map/ppermute | solution.py:182
